TPU v7x, 32 devices: a whole 2x2x4 slice. The times are simulated.
32 devices in a mesh: parts: 2 (over y), tensor: 4 (over z), dp: 2 (over x), pipe: 2 (over core).
Axes of the slice: x: 2, y: 2, z: 4, core: 2. Of those that a mesh axis runs over, the one named last changes fastest.
Arguments:
- tokens: bfloat16 [32, 3, 16384], P(('parts', 'tensor'), None, ('dp', 'pipe')), parts along dimension 0, may hold values from -6 to 6
- w_query: bfloat16 [16384, 8192], P(('dp', 'pipe'), 'tensor'), may hold values from -0.046875 to 0.046875
- w_key: bfloat16 [16384, 512], P(('dp', 'pipe'), 'tensor'), may hold values from -0.046875 to 0.046875
- w_value: bfloat16 [16384, 512], P(('dp', 'pipe'), 'tensor'), may hold values from -0.046875 to 0.046875
- w_out: bfloat16 [8192, 16384], P('tensor', ('dp', 'pipe')), may hold values from -0.0625 to 0.0625
- shrink_qkv: bfloat16 [16, 16384, 96], P('tensor', ('dp', 'pipe')), may hold values from -0.046875 to 0.046875
- grow_query: bfloat16 [16, 32, 8192], P(('dp', 'pipe'), None, 'tensor'), may hold values from -1 to 1
- grow_key: bfloat16 [16, 32, 512], P(('dp', 'pipe'), None, 'tensor'), may hold values from -1 to 1
- grow_value: bfloat16 [16, 32, 512], P(('dp', 'pipe'), None, 'tensor'), may hold values from -1 to 1
- shrink_out: bfloat16 [16, 8192, 32], P(('dp', 'pipe'), 'tensor'), may hold values from -0.0625 to 0.0625
- grow_out: bfloat16 [16, 32, 16384], P('tensor', None, ('dp', 'pipe')), may hold values from -1 to 1
- cache_keys: bfloat16 [32, 4, 512, 128], P(('parts', 'tensor', 'dp', 'pipe')), parts along dimension 0, may hold values from -64 to 64
- cache_values: bfloat16 [32, 4, 512, 128], P(('parts', 'tensor', 'dp', 'pipe')), parts along dimension 0, may hold values from -6 to 6
- cache_lengths: int32 [32], P(('parts', 'tensor', 'dp', 'pipe')), parts along dimension 0, may hold values from 1 to 512, 4096 in all
- adapter_ids: int32 [16], replicated, may hold values from 0 to 15, as said below
- adapter_slots: int32 [16], replicated, may hold values from 0 to 15, as said below
Outputs:
- attended: bfloat16 [32, 3, 16384], P(('parts', 'tensor'), None, ('dp', 'pipe')), parts along dimension 0
There are 2 independent parts, one for each index of `parts`. A program takes and returns all parts, laid end to end along the dimension named above; an argument that names none is the same for every part. Nothing has to cross between parts.
Inputs may be any that keep to these rules, and one draw needn't show every extreme that they name: `adapter_ids`: take the blocks of requests r with the same r // 4, and those with the same r % 4. The owner of adapter a is adapter_slots[a] // 4. In every block at most 2 requests name adapters of one owner, and in every block some owner is named by exactly 2 requests. `adapter_slots`: A permutation of the pool slots.
All inputs are finite; a program needn't handle non-finite values. No bound on the sum of `cache_lengths` on one device may be relied on, other than what follows from the above.
Results may differ from a plain program's by a relative error of at most 0.03.
Values may be sent and summed in bfloat16 or wider, within the bound.
No kernel may reach another device: no remote copies, remote signals or barrier semaphores. Data moves between devices by JAX's collectives and lax.ppermute only.
A program may use at most 128 MiB of HBM per device.

v0:
```python
import math

import jax
import jax.numpy as jnp
from jax import lax
from jax.sharding import PartitionSpec as P

rope_base = 500000.0
EVERY = ("tensor", "dp", "pipe")


def rotate(vectors, positions):
    half_size = vectors.shape[-1] // 2
    frequency = rope_base ** (-2.0 * jnp.arange(half_size, dtype=jnp.float32) / vectors.shape[-1])
    angles = positions[:, None, None] * frequency
    cosine = jnp.cos(angles)
    sine_value = jnp.sin(angles)
    first_half = vectors[..., :half_size]
    second = vectors[..., half_size:]
    return jnp.concatenate(
        [first_half * cosine - second * sine_value, second * cosine + first_half * sine_value], -1
    )


def slot_table(adapter_ids, adapter_slots):
    matches = adapter_ids[:, None] == jnp.arange(adapter_slots.shape[0], dtype=jnp.int32)[None, :]
    return jnp.sum(jnp.where(matches, adapter_slots[None, :], 0), axis=1)


def attend(query_heads, key_new, value_new, cache_keys, cache_values, length):
    drafts, head_count, head_size = query_heads.shape
    kv_heads, cache_size, _ = cache_keys.shape
    positions = (length + jnp.arange(drafts, dtype=jnp.int32)).astype(jnp.float32)
    query_rot = rotate(query_heads.astype(jnp.float32), positions).astype(jnp.bfloat16)
    key_rot = rotate(key_new.astype(jnp.float32), positions).astype(jnp.bfloat16)
    grouped = query_rot.reshape(drafts, kv_heads, head_count // kv_heads, head_size)
    score_scale = 1.0 / math.sqrt(head_size)
    cached = (
        jnp.einsum("skgd,kld->skgl", grouped, cache_keys, preferred_element_type=jnp.float32)
        * score_scale
    )
    fresh_scores = (
        jnp.einsum("skgd,tkd->skgt", grouped, key_rot, preferred_element_type=jnp.float32)
        * score_scale
    )
    cache_mask = jnp.arange(cache_size, dtype=jnp.int32) < length
    draft_mask = jnp.arange(drafts)[None, :] <= jnp.arange(drafts)[:, None]
    cached = jnp.where(cache_mask[None, None, None, :], cached, -jnp.inf)
    fresh_scores = jnp.where(draft_mask[:, None, None, :], fresh_scores, -jnp.inf)
    row_peak = jnp.maximum(jnp.max(cached, -1), jnp.max(fresh_scores, -1))
    cached_exp = jnp.exp(cached - row_peak[..., None])
    fresh_exp = jnp.exp(fresh_scores - row_peak[..., None])
    denominator = jnp.sum(cached_exp, -1) + jnp.sum(fresh_exp, -1)
    cached_prob = (cached_exp / denominator[..., None]).astype(jnp.bfloat16)
    fresh_prob = (fresh_exp / denominator[..., None]).astype(jnp.bfloat16)
    mixed = jnp.einsum(
        "skgl,kld->skgd", cached_prob, cache_values, preferred_element_type=jnp.float32
    )
    mixed = mixed + jnp.einsum(
        "skgt,tkd->skgd", fresh_prob, value_new, preferred_element_type=jnp.float32
    )
    return mixed.astype(jnp.bfloat16)


def local(
    tokens,
    w_query,
    w_key,
    w_value,
    w_out,
    shrink_qkv,
    grow_query,
    grow_key,
    grow_value,
    shrink_out,
    grow_out,
    cache_keys,
    cache_values,
    cache_lengths,
    adapter_ids,
    adapter_slots,
):
    splits = lax.axis_size("tensor")
    groups = lax.axis_size(("dp", "pipe"))
    tensor_index = lax.axis_index("tensor")
    group_index = lax.axis_index(("dp", "pipe"))
    local_rows, drafts, feature_width = tokens.shape
    per_owner = shrink_qkv.shape[0]
    rank_size = grow_out.shape[1]
    query_cols = w_query.shape[1]
    key_cols = w_key.shape[1]
    kv_heads = cache_keys.shape[1]
    head_size = cache_keys.shape[3]
    rows = splits * groups
    row_slots = jnp.repeat(slot_table(adapter_ids, adapter_slots), drafts)
    within = jnp.arange(per_owner, dtype=jnp.int32)[None, :]
    width_hot = (row_slots[:, None] == within + tensor_index * per_owner)[:, :, None]
    column_hot = (row_slots[:, None] == within + group_index * per_owner)[:, :, None]

    def spread_ranks(ranks, hot):
        return jnp.where(hot, ranks[:, None, :], 0.0).reshape(rows * drafts, -1).astype(jnp.bfloat16)

    flat_tokens = lax.all_gather(tokens, "tensor", axis=0, tiled=True).reshape(
        rows * drafts, feature_width
    )
    rank_part = jnp.einsum(
        "nd,adr->nar", flat_tokens, shrink_qkv, preferred_element_type=jnp.float32
    )
    rank_part = jnp.sum(jnp.where(width_hot, rank_part, 0.0), 1)
    rank_all = lax.psum(rank_part, EVERY)

    def grown(index, grow):
        ranks = spread_ranks(rank_all[:, index * rank_size : (index + 1) * rank_size], column_hot)
        return jnp.dot(
            ranks, grow.reshape(per_owner * rank_size, -1), preferred_element_type=jnp.float32
        )

    def product(index, weight, grow):
        base = jnp.dot(flat_tokens, weight, preferred_element_type=jnp.float32)
        return (base + grown(index, grow)).astype(jnp.bfloat16).reshape(rows, drafts, -1)

    partial = jnp.concatenate(
        [
            product(0, w_query, grow_query),
            product(1, w_key, grow_key),
            product(2, w_value, grow_value),
        ],
        2,
    )
    arrived = lax.all_to_all(partial, EVERY, split_axis=0, concat_axis=0, tiled=True)
    joined = jnp.sum(
        arrived.reshape(splits, groups, drafts, -1).astype(jnp.float32), 1
    ).astype(jnp.bfloat16)
    joined = jnp.transpose(joined, (1, 0, 2))
    query_heads = joined[:, :, :query_cols].reshape(drafts, -1, head_size)
    key_new = joined[:, :, query_cols : query_cols + key_cols].reshape(drafts, kv_heads, head_size)
    value_new = joined[:, :, query_cols + key_cols :].reshape(drafts, kv_heads, head_size)
    mixed = attend(
        query_heads, key_new, value_new, cache_keys[0], cache_values[0], cache_lengths[0]
    )
    mixed = jnp.transpose(mixed.reshape(drafts, splits, -1), (1, 0, 2))
    outgoing = jnp.repeat(mixed, groups, axis=0)
    flat_heads = lax.all_to_all(
        outgoing, EVERY, split_axis=0, concat_axis=0, tiled=True
    ).reshape(rows * drafts, -1)
    out_part = jnp.einsum(
        "nw,awr->nar", flat_heads, shrink_out, preferred_element_type=jnp.float32
    )
    out_part = jnp.sum(jnp.where(column_hot, out_part, 0.0), 1)
    out_rank = lax.psum(out_part, EVERY)
    out = jnp.dot(flat_heads, w_out, preferred_element_type=jnp.float32)
    out = out + jnp.dot(
        spread_ranks(out_rank, width_hot),
        grow_out.reshape(per_owner * rank_size, -1),
        preferred_element_type=jnp.float32,
    )
    blocks = lax.all_to_all(
        out.astype(jnp.bfloat16).reshape(splits, local_rows, drafts, feature_width),
        "tensor",
        split_axis=0,
        concat_axis=0,
        tiled=True,
    )
    return jnp.sum(blocks.astype(jnp.float32), 0).astype(jnp.bfloat16)


def solution(mesh):
    placed = (
        P(("parts", "tensor"), None, ("dp", "pipe")),
        P(("dp", "pipe"), "tensor"),
        P(("dp", "pipe"), "tensor"),
        P(("dp", "pipe"), "tensor"),
        P("tensor", ("dp", "pipe")),
        P("tensor", ("dp", "pipe"), None),
        P(("dp", "pipe"), None, "tensor"),
        P(("dp", "pipe"), None, "tensor"),
        P(("dp", "pipe"), None, "tensor"),
        P(("dp", "pipe"), "tensor", None),
        P("tensor", None, ("dp", "pipe")),
        P(("parts", "tensor", "dp", "pipe"), None, None, None),
        P(("parts", "tensor", "dp", "pipe"), None, None, None),
        P(("parts", "tensor", "dp", "pipe")),
        P(),
        P(),
    )
    return jax.shard_map(
        local,
        mesh=mesh,
        in_specs=placed,
        out_specs=P(("parts", "tensor"), None, ("dp", "pipe")),
        check_vma=False,
    )
```

profile of v0, /device:TPU:0, one launch (start us, length us, event | category | flops | bytes accessed | tf_op | source)
XLA Modules:
  0.0 229.4 jit_solution(14919999344499351738)
XLA Ops:
  0.0 1.1 copy.61
  1.1 18.0 %all_gather.3 = bf16[16,3,4096]{2,1,0:T(4,128)(2,1)} all-gather(bf16[4,3,4096]{2,1,0:T(4,128)(2,1)S(1)} %copy.61), channel_id=1, replica_groups=mesh['parts'=2,'tensor'=4,'dp'=2,'pipe'=2] {'tensor'}, dimensions={0}, use_global_device_ids=true | all-gather | bytes 491520 | tf_op jit(solution)/shard_map/all_gather | solution.py:103
  19.1 2.1 reshape.235
  21.3 1.4 reshape.225
  22.6 0.9 select_reduce_fusion.1
  23.5 0.1 broadcast_in_dim.136
  23.6 0.1 eq.50
  23.7 0.1 broadcast_compare_fusion.1
  23.8 0.5 copy-done.4
  24.3 2.8 %fusion.7 = f32[48,96]{1,0:T(8,128)} fusion(bf16[48,4096,1]{1,0,2:T(8,128)(2,1)} %reshape.235, bf16[4,4096,96]{1,2,0:T(8,128)(2,1)S(1)} %copy-done, pred[48,4]{0,1:T(4,128)(4,1)S(1)} %get-tuple-element.17), kind=kOutput, calls=%fused_computation.14 | convolution fusion | flops 151027200 | bytes 3557568 | tf_op jit(solution)/shard_map/nd,adr->nar/dot_general | solution.py:106
  27.1 58.4 %psum.14 = bf16[48,96]{1,0:T(8,128)(2,1)S(1)} all-reduce(f32[48,96]{1,0:T(8,128)} %fusion.7), channel_id=1, replica_groups=mesh['parts'=2,'tensor'=4,'dp'=2,'pipe'=2] {'tensor','dp','pipe'}, use_global_device_ids=true, to_apply=%region_2.3 | all-reduce | flops 4608 | bytes 27648 | tf_op jit(solution)/shard_map/psum | solution.py:110
  85.5 0.7 fusion.40
  86.2 0.8 copy.64
  87.0 0.9 convolution_bitcast_fusion.4
  88.0 2.1 fusion.11
  90.1 0.7 reshape.228
  90.8 1.4 copy.63
  92.2 0.9 convolution_bitcast_fusion.5
  93.1 2.1 fusion.10
  95.3 1.3 reshape.227
  96.6 1.4 copy.62
  98.0 1.3 convolution_bitcast_fusion.1
  99.3 9.5 %fusion.2 = bf16[48,2048]{1,0:T(8,128)(2,1)} fusion(f32[48,2048]{1,0:T(8,128)S(1)} %convolution_bitcast_fusion.1, bf16[48,4096]{1,0:T(8,128)(2,1)S(1)} %reshape.225, bf16[4096,2048]{1,0:T(8,128)(2,1)} %param.17), kind=kOutput, calls=%fused_computation.5 | convolution fusion | flops 805502976 | bytes 17760256 | tf_op jit(solution)/shard_map/dot_general | solution.py:119
  108.8 1.1 reshape.226
  109.8 1.6 pad_maximum_fusion
  111.4 3.5 %all-to-all-start = ((bf16[16,3,2304]{2,1,0:T(4,128)(2,1)}), bf16[16,3,2304]{2,1,0:T(4,128)(2,1)S(1)}, u32[]{:S(2)}, u32[]{:S(2)}) async-start(bf16[16,3,2304]{2,1,0:T(4,128)(2,1)} %pad_maximum_fusion), calls=%async_computation | async-start | bytes 589824 | tf_op jit(solution)/shard_map/all_to_all | solution.py:130
  115.6 0.1 multiply_cosine_fusion
  115.7 9.7 %all-to-all-done = bf16[16,3,2304]{2,1,0:T(4,128)(2,1)S(1)} async-done(((bf16[16,3,2304]{2,1,0:T(4,128)(2,1)}), bf16[16,3,2304]{2,1,0:T(4,128)(2,1)S(1)}, u32[]{:S(2)}, u32[]{:S(2)}) %all-to-all-start) | async-done | bytes 221216 | tf_op jit(solution)/shard_map/all_to_all | solution.py:130
  125.5 0.2 bitcast_reduce_fusion
  125.7 0.1 subtract_convert_fusion
  125.9 0.1 subtract_convert_fusion.1
  125.9 0.1 maximum_bitcast_fusion
  126.0 1.4 fusion.41
  127.5 0.3 fusion.42
  127.8 0.2 fusion.14
  128.1 1.3 convolution_bitcast_fusion.3
  129.4 0.2 fusion.6
  129.7 0.1 broadcast_in_dim.147
  129.8 13.3 %all_to_all.15 = bf16[16,3,2048]{2,1,0:T(4,128)(2,1)} all-to-all(bf16[16,3,2048]{2,1,0:T(4,128)(2,1)S(1)} %bitcast.78), channel_id=1, replica_groups=mesh['parts'=2,'tensor'=4,'dp'=2,'pipe'=2] {'tensor','dp','pipe'}, dimensions={0} | all-to-all | bytes 393216 | tf_op jit(solution)/shard_map/all_to_all | solution.py:143
  143.1 1.1 reshape.232
  144.2 9.7 %fusion.43 = f32[48,4096]{1,0:T(8,128)} fusion(bf16[48,2048]{1,0:T(8,128)(2,1)S(1)} %reshape.232, bf16[2048,4096]{1,0:T(8,128)(2,1)} %param.20), kind=kOutput, calls=%fused_computation.88 | convolution fusion | flops 805306368 | bytes 17760256 | tf_op jit(solution)/shard_map/dot_general | solution.py:151
  154.0 0.3 fusion.44
  154.3 58.8 %psum.15 = bf16[48,32]{0,1:T(8,128)(2,1)S(1)} all-reduce(f32[48,32]{0,1:T(8,128)S(1)} %select_reduce_fusion), channel_id=1, replica_groups=mesh['parts'=2,'tensor'=4,'dp'=2,'pipe'=2] {'tensor','dp','pipe'}, use_global_device_ids=true, to_apply=%region_9.10 | all-reduce | flops 1536 | bytes 9216 | tf_op jit(solution)/shard_map/psum | solution.py:150
  213.1 1.8 fusion.1
  214.9 1.0 reshape.233
  215.9 1.4 copy.72
  217.3 11.3 %all_to_all.16 = bf16[4,4,3,4096]{3,1,2,0:T(4,128)(2,1)S(1)} all-to-all(bf16[4,4,3,4096]{3,1,2,0:T(4,128)(2,1)S(1)} %copy.72), channel_id=1, replica_groups=mesh['parts'=2,'tensor'=4,'dp'=2,'pipe'=2] {'tensor'}, dimensions={0} | all-to-all | bytes 786432 | tf_op jit(solution)/shard_map/all_to_all | solution.py:157
  228.6 0.9 reduce_sum.75
  (25 shorter events, 0.3 us)
Async XLA Ops:
  0.0 24.3 %copy-start = (bf16[4,4096,96]{1,2,0:T(8,128)(2,1)S(1)}, bf16[4,4096,96]{1,2,0:T(8,128)(2,1)}, u32[]{:S(2)}) copy-start(bf16[4,4096,96]{1,2,0:T(8,128)(2,1)} %param.21) | copy-start | bytes 9437188
  23.7 0.5 copy-start.4
  23.8 64.2 %copy-start.2 = (pred[48,4]{0,1:T(4,128)(4,1)}, pred[48,4]{0,1:T(4,128)(4,1)S(1)}, u32[]{:S(2)}) copy-start(pred[48,4]{0,1:T(4,128)(4,1)S(1)} %get-tuple-element.16) | copy-start | bytes 580
  108.8 45.5 %copy-start.3 = (pred[48,4]{0,1:T(4,128)(4,1)S(1)}, pred[48,4]{0,1:T(4,128)(4,1)}, u32[]{:S(2)}) copy-start(pred[48,4]{0,1:T(4,128)(4,1)} %copy-done.2) | copy-start | bytes 580
  111.4 14.1 %all-to-all-start = ((bf16[16,3,2304]{2,1,0:T(4,128)(2,1)}), bf16[16,3,2304]{2,1,0:T(4,128)(2,1)S(1)}, u32[]{:S(2)}, u32[]{:S(2)}) async-start(bf16[16,3,2304]{2,1,0:T(4,128)(2,1)} %pad_maximum_fusion), calls=%async_computation | async-start | bytes 589824 | tf_op jit(solution)/shard_map/all_to_all | solution.py:130
  144.2 9.7 %copy-start.1 = (bf16[4,2048,32]{1,2,0:T(8,128)(2,1)S(1)}, bf16[4,2048,32]{1,2,0:T(8,128)(2,1)}, u32[]{:S(2)}) copy-start(bf16[4,2048,32]{1,2,0:T(8,128)(2,1)} %param.25) | copy-start | bytes 1572868
where the time goes:
time: 231 us; the launch traced here: 229 us
  blocking collectives  160 us (69%)
  matrix products  34.9 us (15%)
  local copies, waits for them, and re-layouts  16.5 us (7%)
  waiting for transfers between devices  9.72 us (4%)
  other arithmetic  4.19 us (2%)
  starting transfers between devices  3.54 us (2%)
    psum x1, blocking collectives, local(): out_rank = lax.psum(out_part, EVERY)  58.8 us
    psum x1, blocking collectives, local(): rank_all = lax.psum(rank_part, EVERY)  58.4 us
    all_gather x1, blocking collectives, local(): lax.all_gather(tokens, 'tensor', axis=0, tiled=True)  18 us
    dot_general x3, matrix products, product(): base = jnp.dot(flat_tokens, weight, preferred_element_type=jnp.float32)  13.8 us
    all_to_all x1, blocking collectives, local(): lax.all_to_all(outgoing, EVERY, split_axis=0, concat_axis=0, tiled=True)  13.3 us
    all_to_all x1, blocking collectives, local(): lax.all_to_all(out.astype(jnp.bfloat16).reshape(splits, local_rows, draft...  11.3 us
    dot_general x1, matrix products, local(): out = jnp.dot(flat_heads, w_out, preferred_element_type=jnp.float32)  9.73 us
    all_to_all x1, waiting for transfers between devices, local(): lax.all_to_all(partial, EVERY, split_axis=0, concat_axis=0, tiled=True)  9.72 us
  transfers between devices with their start and end apart: 1, of which 1 were waited for; matrix products, arithmetic and copies ran while one was open for 0% of the time, Pallas kernels for 0%

commit v1 on v0

--- a/solution.py
+++ b/solution.py
@@ -20,6 +20,32 @@
     return jnp.concatenate(
         [first_half * cosine - second * sine_value, second * cosine + first_half * sine_value], -1
     )
+
+
+def to_growers(partial, splits):
+    total = None
+    for shift in range(splits):
+        route = [
+            (t * splits + g, ((g + shift) % splits) * splits + t)
+            for t in range(splits)
+            for g in range(splits)
+        ]
+        got = lax.ppermute(partial, EVERY, route).astype(jnp.float32)
+        total = got if total is None else total + got
+    return total
+
+
+def to_out_growers(partial, splits):
+    total = None
+    for shift in range(splits):
+        route = [
+            (t * splits + g, g * splits + (t + shift) % splits)
+            for t in range(splits)
+            for g in range(splits)
+        ]
+        got = lax.ppermute(partial, EVERY, route).astype(jnp.float32)
+        total = got if total is None else total + got
+    return total
 
 
 def slot_table(adapter_ids, adapter_slots):
@@ -107,7 +133,7 @@
         "nd,adr->nar", flat_tokens, shrink_qkv, preferred_element_type=jnp.float32
     )
     rank_part = jnp.sum(jnp.where(width_hot, rank_part, 0.0), 1)
-    rank_all = lax.psum(rank_part, EVERY)
+    rank_all = to_growers(rank_part.astype(jnp.bfloat16), splits)
 
     def grown(index, grow):
         ranks = spread_ranks(rank_all[:, index * rank_size : (index + 1) * rank_size], column_hot)
@@ -115,15 +141,19 @@
             ranks, grow.reshape(per_owner * rank_size, -1), preferred_element_type=jnp.float32
         )
 
-    def product(index, weight, grow):
-        base = jnp.dot(flat_tokens, weight, preferred_element_type=jnp.float32)
-        return (base + grown(index, grow)).astype(jnp.bfloat16).reshape(rows, drafts, -1)
+    bases = [
+        jnp.dot(flat_tokens, weight, preferred_element_type=jnp.float32)
+        for weight in (w_query, w_key, w_value)
+    ]
+
+    def product(index, grow):
+        return (bases[index] + grown(index, grow)).astype(jnp.bfloat16).reshape(rows, drafts, -1)
 
     partial = jnp.concatenate(
         [
-            product(0, w_query, grow_query),
-            product(1, w_key, grow_key),
-            product(2, w_value, grow_value),
+            product(0, grow_query),
+            product(1, grow_key),
+            product(2, grow_value),
         ],
         2,
     )
@@ -147,7 +177,7 @@
         "nw,awr->nar", flat_heads, shrink_out, preferred_element_type=jnp.float32
     )
     out_part = jnp.sum(jnp.where(column_hot, out_part, 0.0), 1)
-    out_rank = lax.psum(out_part, EVERY)
+    out_rank = to_out_growers(out_part.astype(jnp.bfloat16), splits)
     out = jnp.dot(flat_heads, w_out, preferred_element_type=jnp.float32)
     out = out + jnp.dot(
         spread_ranks(out_rank, width_hot),

time: 231 us -> 135 us (0.58)
  blocking collectives: 160 us -> 49.5 us
  starting transfers between devices: 3.54 us -> 17.4 us
  other arithmetic: 4.19 us -> 7.31 us
    psum x2 -> x0, blocking collectives: 117 us -> none  [the longest x1 58.8 us: local(): out_rank = lax.psum(out_part, EVERY)]
    ppermute x0 -> x8, starting transfers between devices: none -> 10.3 us  [the longest x4 7.01 us: to_growers(): got = lax.ppermute(partial, EVERY, route).astype(jnp.float32)]
    all_to_all x1, blocking collectives: 11.3 us -> 18.2 us  [local(): lax.all_to_all(out.astype(jnp.bfloat16).reshape(splits, local_rows, draft...]
    all_to_all x1, starting transfers between devices: 3.54 us -> 7.05 us  [local(): lax.all_to_all(partial, EVERY, split_axis=0, concat_axis=0, tiled=True)]
  transfers between devices with their start and end apart: 1 -> 9, of which waited for: 1 -> 1; matrix products, arithmetic and copies ran while one was open for 0% -> 9% of each run, Pallas kernels for 0% -> 0%
where the time goes in v1:
time: 135 us; the launch traced here: 133 us
  blocking collectives  49.5 us (37%)
  matrix products  33.2 us (25%)
  starting transfers between devices  17.4 us (13%)
  local copies, waits for them, and re-layouts  15 us (11%)
  waiting for transfers between devices  9.87 us (7%)
  other arithmetic  7.31 us (5%)
    all_to_all x1, blocking collectives, local(): lax.all_to_all(out.astype(jnp.bfloat16).reshape(splits, local_rows, draft...  18.2 us
    all_gather x1, blocking collectives, local(): lax.all_gather(tokens, 'tensor', axis=0, tiled=True)  18 us
    dot_general x3, matrix products, local(): jnp.dot(flat_tokens, weight, preferred_element_type=jnp.float32)  13.8 us
    all_to_all x1, blocking collectives, local(): lax.all_to_all(outgoing, EVERY, split_axis=0, concat_axis=0, tiled=True)  13.3 us
    all_to_all x1, waiting for transfers between devices, local(): lax.all_to_all(partial, EVERY, split_axis=0, concat_axis=0, tiled=True)  9.85 us
    dot_general x1, matrix products, local(): out = jnp.dot(flat_heads, w_out, preferred_element_type=jnp.float32)  8.79 us
    all_to_all x1, starting transfers between devices, local(): lax.all_to_all(partial, EVERY, split_axis=0, concat_axis=0, tiled=True)  7.05 us
    ppermute x4, starting transfers between devices, to_growers(): got = lax.ppermute(partial, EVERY, route).astype(jnp.float32)  7.01 us
  transfers between devices with their start and end apart: 9, of which 1 were waited for; matrix products, arithmetic and copies ran while one was open for 9% of the time, Pallas kernels for 0%

profile of v1, /device:TPU:0, one launch (start us, length us, event | category | flops | bytes accessed | tf_op | source)
XLA Modules:
  0.0 133.3 jit_solution(996438114537036669)
XLA Ops:
  0.0 1.1 copy.61
  1.1 18.0 %all_gather.3 = bf16[16,3,4096]{2,1,0:T(4,128)(2,1)} all-gather(bf16[4,3,4096]{2,1,0:T(4,128)(2,1)S(1)} %copy.61), channel_id=1, replica_groups=mesh['parts'=2,'tensor'=4,'dp'=2,'pipe'=2] {'tensor'}, dimensions={0}, use_global_device_ids=true | all-gather | bytes 491520 | tf_op jit(solution)/shard_map/all_gather | solution.py:129
  19.1 1.4 %reshape.235 = bf16[48,4096,1]{1,0,2:T(8,128)(2,1)S(1)} reshape(bf16[16,3,4096]{2,1,0:T(4,128)(2,1)} %all_gather.3) | data formatting | bytes 786432 | tf_op jit(solution)/shard_map/reshape | solution.py:129
  20.5 0.9 select_reduce_fusion.1
  21.6 1.2 fusion.7
  22.9 4.3 %collective-permute-start.3 = (bf16[48,96]{1,0:T(8,128)(2,1)S(1)}, bf16[48,96]{1,0:T(8,128)(2,1)}, u32[]{:S(2)}, u32[]{:S(2)}) collective-permute-start(bf16[48,96]{1,0:T(8,128)(2,1)S(1)} %fusion.7), channel_id=1, source_target_pairs={{0,12},{1,0},{2,4},{3,8},{4,13},{5,1},{6,5},{7,9},{8,14},{9,2},{10... | collective-permute-start | bytes 27656 | tf_op jit(solution)/shard_map/ppermute | solution.py:33
  27.2 1.5 %collective-permute-start.2 = (bf16[48,96]{1,0:T(8,128)(2,1)S(1)}, bf16[48,96]{1,0:T(8,128)(2,1)}, u32[]{:S(2)}, u32[]{:S(2)}) collective-permute-start(bf16[48,96]{1,0:T(8,128)(2,1)S(1)} %fusion.7), channel_id=1, source_target_pairs={{0,8},{1,12},{2,0},{3,4},{4,9},{5,13},{6,1},{7,5},{8,10},{9,14},{1... | collective-permute-start | bytes 27656 | tf_op jit(solution)/shard_map/ppermute | solution.py:33
  28.7 1.2 collective-permute-start
  29.9 0.5 multiply_power_fusion
  30.4 0.6 iota_compare_fusion.1
  31.0 1.4 %reshape.225 = bf16[48,4096]{1,0:T(8,128)(2,1)S(1)} reshape(bf16[16,3,4096]{2,1,0:T(4,128)(2,1)} %all_gather.3) | data formatting | bytes 786432 | tf_op jit(solution)/shard_map/reshape | solution.py:129
  33.1 0.8 convert_add_fusion
  33.8 0.7 fusion.40
  34.5 0.7 copy.64
  35.2 0.9 convolution_bitcast_fusion.4
  36.1 2.1 %fusion.11 = bf16[48,128]{1,0:T(8,128)(2,1)} fusion(f32[48,128]{1,0:T(8,128)S(1)} %convolution_bitcast_fusion.4, bf16[48,4096]{1,0:T(8,128)(2,1)S(1)} %reshape.225, bf16[4096,128]{1,0:T(8,128)(2,1)} %param.19), kind=kOutput, calls=%fused_computation.23 | convolution fusion | flops 50343936 | bytes 1478656 | tf_op jit(solution)/shard_map/dot_general | solution.py:145
  38.3 0.7 reshape.228
  39.0 1.4 %copy.63 = bf16[48,32]{0,1:T(8,128)(2,1)} copy(bf16[48,32]{1,0:T(8,128)(2,1)} %get-tuple-element.11) | data formatting | bytes 6144 | tf_op jit(solution)/shard_map/slice | solution.py:139
  40.4 0.9 convolution_bitcast_fusion.5
  41.3 2.1 %fusion.10 = bf16[48,128]{1,0:T(8,128)(2,1)} fusion(f32[48,128]{1,0:T(8,128)S(1)} %convolution_bitcast_fusion.5, bf16[48,4096]{1,0:T(8,128)(2,1)S(1)} %reshape.225, bf16[4096,128]{1,0:T(8,128)(2,1)} %param.18), kind=kOutput, calls=%fused_computation.22 | convolution fusion | flops 50343936 | bytes 1478656 | tf_op jit(solution)/shard_map/dot_general | solution.py:145
  43.5 1.3 reshape.227
  44.8 1.4 %copy.62 = bf16[48,32]{0,1:T(8,128)(2,1)} copy(bf16[48,32]{1,0:T(8,128)(2,1)} %get-tuple-element.9) | data formatting | bytes 6144 | tf_op jit(solution)/shard_map/slice | solution.py:139
  46.1 1.3 convolution_bitcast_fusion.1
  47.5 9.5 %fusion.2 = bf16[48,2048]{1,0:T(8,128)(2,1)} fusion(f32[48,2048]{1,0:T(8,128)S(1)} %convolution_bitcast_fusion.1, bf16[48,4096]{1,0:T(8,128)(2,1)S(1)} %reshape.225, bf16[4096,2048]{1,0:T(8,128)(2,1)} %param.17), kind=kOutput, calls=%fused_computation.5 | convolution fusion | flops 805502976 | bytes 17760256 | tf_op jit(solution)/shard_map/dot_general | solution.py:145
  56.9 1.1 reshape.226
  58.0 1.6 %pad_maximum_fusion = bf16[16,3,2304]{2,1,0:T(4,128)(2,1)} fusion(bf16[16,3,128]{2,1,0:T(4,128)(2,1)S(1)} %reshape.228, bf16[16,3,128]{2,1,0:T(4,128)(2,1)} %reshape.227, bf16[16,3,2048]{2,1,0:T(4,128)(2,1)S(1)} %reshape.226), kind=kLoop, calls=%fused_computation.29 | loop fusion | flops 663552 | bytes 442368 | tf_op jit(solution)/shard_map/concatenate | solution.py:152
  59.6 7.0 %all-to-all-start = ((bf16[16,3,2304]{2,1,0:T(4,128)(2,1)}), bf16[16,3,2304]{2,1,0:T(4,128)(2,1)S(1)}, u32[]{:S(2)}, u32[]{:S(2)}) async-start(bf16[16,3,2304]{2,1,0:T(4,128)(2,1)} %pad_maximum_fusion), calls=%async_computation | async-start | bytes 589824 | tf_op jit(solution)/shard_map/all_to_all | solution.py:160
  66.6 0.7 multiply_cosine_fusion
  67.3 9.8 %all-to-all-done = bf16[16,3,2304]{2,1,0:T(4,128)(2,1)S(1)} async-done(((bf16[16,3,2304]{2,1,0:T(4,128)(2,1)}), bf16[16,3,2304]{2,1,0:T(4,128)(2,1)S(1)}, u32[]{:S(2)}, u32[]{:S(2)}) %all-to-all-start) | async-done | bytes 221216 | tf_op jit(solution)/shard_map/all_to_all | solution.py:160
  77.7 1.4 %fusion.41 = (f32[3,4,16]{2,0,1:T(4,128)S(1)}, f32[3,4,16,512]{3,2,0,1:T(8,128)S(1)}) fusion(bf16[1,4,512,128]{3,2,1,0:T(8,128)(2,1)} %param.27, pred[512]{0:T(512)(128)(4,1)S(1)} %iota_compare_fusion.2, bf16[3,4,16,64]{3,2,1,0:T(8,128)(2,1)S(1)} %bitcast.85, bf16[3,4,16,64]{3,2,1,0:T(8,128)(2,1)S(1)} %bitcast.83), kind=kOutput, calls=%fused_computation.88 | convolution fusion | flops 25558848 | bytes 967936 | tf_op jit(solution)/shard_map/skgd,kld->skgl/dot_general | solution.py:65
  79.2 1.0 fusion.42
  80.2 0.2 fusion.14
  80.4 1.3 convolution_bitcast_fusion.3
  81.8 0.2 fusion.6
  82.2 13.3 %all_to_all.15 = bf16[16,3,2048]{2,1,0:T(4,128)(2,1)} all-to-all(bf16[16,3,2048]{2,1,0:T(4,128)(2,1)S(1)} %bitcast.78), channel_id=1, replica_groups=mesh['parts'=2,'tensor'=4,'dp'=2,'pipe'=2] {'tensor','dp','pipe'}, dimensions={0} | all-to-all | bytes 393216 | tf_op jit(solution)/shard_map/all_to_all | solution.py:173
  95.5 1.1 reshape.232
  96.6 1.4 %fusion.44 = f32[48,128]{0,1:S(1)} fusion(bf16[48,2048]{1,0:T(8,128)(2,1)S(1)} %reshape.232, bf16[2048,128]{0,1:T(8,128)(2,1)} %bitcast.79), kind=kOutput, calls=%fused_computation.91 | convolution fusion | flops 25165824 | bytes 745472
  98.0 0.7 select_reduce_fusion
  98.7 0.2 collective-permute-start.7
  98.9 0.5 collective-permute-start.6
  99.4 1.9 %collective-permute-start.5 = (bf16[48,32]{0,1:T(8,128)(2,1)S(1)}, bf16[48,32]{0,1:T(8,128)(2,1)S(1)}, u32[]{:S(2)}, u32[]{:S(2)}) collective-permute-start(bf16[48,32]{0,1:T(8,128)(2,1)S(1)} %select_reduce_fusion), channel_id=1, source_target_pairs={{0,1},{1,5},{2,9},{3,13},{4,2},{5,6},{6,10},{7,14},{8,3},{9,7},{10... | collective-permute-start | bytes 9224 | tf_op jit(solution)/shard_map/ppermute | solution.py:46
  101.4 0.6 collective-permute-start.4
  102.0 8.8 %fusion.43 = f32[48,4096]{1,0:T(8,128)S(1)} fusion(bf16[48,2048]{1,0:T(8,128)(2,1)S(1)} %reshape.232, bf16[2048,4096]{1,0:T(8,128)(2,1)} %param.20), kind=kOutput, calls=%fused_computation.90 | convolution fusion | flops 805306368 | bytes 17760256 | tf_op jit(solution)/shard_map/dot_general | solution.py:181
  110.9 0.9 fusion.1
  111.8 1.0 reshape.233
  112.8 1.4 %copy.72 = bf16[4,4,3,4096]{3,1,2,0:T(4,128)(2,1)S(1)} copy(bf16[4,4,3,4096]{3,2,1,0:T(4,128)(2,1)} %reshape.233) | data formatting | bytes 786432 | tf_op jit(solution)/shard_map/reshape | solution.py:188
  114.3 18.2 %all_to_all.16 = bf16[4,4,3,4096]{3,1,2,0:T(4,128)(2,1)S(1)} all-to-all(bf16[4,4,3,4096]{3,1,2,0:T(4,128)(2,1)S(1)} %copy.72), channel_id=1, replica_groups=mesh['parts'=2,'tensor'=4,'dp'=2,'pipe'=2] {'tensor'}, dimensions={0} | all-to-all | bytes 786432 | tf_op jit(solution)/shard_map/all_to_all | solution.py:187
  132.4 0.9 reduce_sum.75
  (39 shorter events, 1.0 us)
Async XLA Ops:
  0.0 21.6 %copy-start = (bf16[4,4096,96]{1,2,0:T(8,128)(2,1)S(1)}, bf16[4,4096,96]{1,2,0:T(8,128)(2,1)}, u32[]{:S(2)}) copy-start(bf16[4,4096,96]{1,2,0:T(8,128)(2,1)} %param.21) | copy-start | bytes 9437188
  21.6 8.8 %copy-start.2 = (pred[48,4]{0,1:T(4,128)(4,1)}, pred[48,4]{0,1:T(4,128)(4,1)S(1)}, u32[]{:S(2)}) copy-start(pred[48,4]{0,1:T(4,128)(4,1)S(1)} %get-tuple-element.17) | copy-start | bytes 580
  21.6 14.5 %copy-start.3 = (pred[48,4]{0,1:T(4,128)(4,1)}, pred[48,4]{0,1:T(4,128)(4,1)S(1)}, u32[]{:S(2)}) copy-start(pred[48,4]{0,1:T(4,128)(4,1)S(1)} %get-tuple-element.16) | copy-start | bytes 580
  22.9 10.1 %collective-permute-start.3 = (bf16[48,96]{1,0:T(8,128)(2,1)S(1)}, bf16[48,96]{1,0:T(8,128)(2,1)}, u32[]{:S(2)}, u32[]{:S(2)}) collective-permute-start(bf16[48,96]{1,0:T(8,128)(2,1)S(1)} %fusion.7), channel_id=1, source_target_pairs={{0,12},{1,0},{2,4},{3,8},{4,13},{5,1},{6,5},{7,9},{8,14},{9,2},{10... | collective-permute-start | bytes 27656 | tf_op jit(solution)/shard_map/ppermute | solution.py:33
  27.2 5.9 %collective-permute-start.2 = (bf16[48,96]{1,0:T(8,128)(2,1)S(1)}, bf16[48,96]{1,0:T(8,128)(2,1)}, u32[]{:S(2)}, u32[]{:S(2)}) collective-permute-start(bf16[48,96]{1,0:T(8,128)(2,1)S(1)} %fusion.7), channel_id=1, source_target_pairs={{0,8},{1,12},{2,0},{3,4},{4,9},{5,13},{6,1},{7,5},{8,10},{9,14},{1... | collective-permute-start | bytes 27656 | tf_op jit(solution)/shard_map/ppermute | solution.py:33
  28.7 4.4 %collective-permute-start.1 = (bf16[48,96]{1,0:T(8,128)(2,1)S(1)}, bf16[48,96]{1,0:T(8,128)(2,1)}, u32[]{:S(2)}, u32[]{:S(2)}) collective-permute-start(bf16[48,96]{1,0:T(8,128)(2,1)S(1)} %fusion.7), channel_id=1, source_target_pairs={{0,4},{1,8},{2,12},{3,0},{4,5},{5,9},{6,13},{7,1},{8,6},{9,10},{10... | collective-permute-start | bytes 27656 | tf_op jit(solution)/shard_map/ppermute | solution.py:33
  28.7 4.4 %collective-permute-start = (bf16[48,96]{1,0:T(8,128)(2,1)S(1)}, bf16[48,96]{1,0:T(8,128)(2,1)}, u32[]{:S(2)}, u32[]{:S(2)}) collective-permute-start(bf16[48,96]{1,0:T(8,128)(2,1)S(1)} %fusion.7), channel_id=1, source_target_pairs={{0,0},{1,4},{2,8},{3,12},{4,1},{5,5},{6,9},{7,13},{8,2},{9,6},{10,... | collective-permute-start | bytes 27656 | tf_op jit(solution)/shard_map/ppermute | solution.py:33
  59.6 17.6 %all-to-all-start = ((bf16[16,3,2304]{2,1,0:T(4,128)(2,1)}), bf16[16,3,2304]{2,1,0:T(4,128)(2,1)S(1)}, u32[]{:S(2)}, u32[]{:S(2)}) async-start(bf16[16,3,2304]{2,1,0:T(4,128)(2,1)} %pad_maximum_fusion), calls=%async_computation | async-start | bytes 589824 | tf_op jit(solution)/shard_map/all_to_all | solution.py:160
  96.6 14.3 %copy-start.1 = (bf16[4,32,4096]{2,1,0:T(8,128)(2,1)S(1)}, bf16[4,32,4096]{2,1,0:T(8,128)(2,1)}, u32[]{:S(2)}) copy-start(bf16[4,32,4096]{2,1,0:T(8,128)(2,1)} %param.26) | copy-start | bytes 3145732
  98.7 12.1 %collective-permute-start.7 = (bf16[48,32]{0,1:T(8,128)(2,1)S(1)}, bf16[48,32]{0,1:T(8,128)(2,1)S(1)}, u32[]{:S(2)}, u32[]{:S(2)}) collective-permute-start(bf16[48,32]{0,1:T(8,128)(2,1)S(1)} %select_reduce_fusion), channel_id=1, source_target_pairs={{0,3},{1,7},{2,11},{3,15},{4,0},{5,4},{6,8},{7,12},{8,1},{9,5},{10... | collective-permute-start | bytes 9224 | tf_op jit(solution)/shard_map/ppermute | solution.py:46
  98.9 11.9 %collective-permute-start.6 = (bf16[48,32]{0,1:T(8,128)(2,1)S(1)}, bf16[48,32]{0,1:T(8,128)(2,1)S(1)}, u32[]{:S(2)}, u32[]{:S(2)}) collective-permute-start(bf16[48,32]{0,1:T(8,128)(2,1)S(1)} %select_reduce_fusion), channel_id=1, source_target_pairs={{0,2},{1,6},{2,10},{3,14},{4,3},{5,7},{6,11},{7,15},{8,0},{9,4},{1... | collective-permute-start | bytes 9224 | tf_op jit(solution)/shard_map/ppermute | solution.py:46
  99.4 11.4 %collective-permute-start.5 = (bf16[48,32]{0,1:T(8,128)(2,1)S(1)}, bf16[48,32]{0,1:T(8,128)(2,1)S(1)}, u32[]{:S(2)}, u32[]{:S(2)}) collective-permute-start(bf16[48,32]{0,1:T(8,128)(2,1)S(1)} %select_reduce_fusion), channel_id=1, source_target_pairs={{0,1},{1,5},{2,9},{3,13},{4,2},{5,6},{6,10},{7,14},{8,3},{9,7},{10... | collective-permute-start | bytes 9224 | tf_op jit(solution)/shard_map/ppermute | solution.py:46
  101.4 9.5 %collective-permute-start.4 = (bf16[48,32]{0,1:T(8,128)(2,1)S(1)}, bf16[48,32]{0,1:T(8,128)(2,1)S(1)}, u32[]{:S(2)}, u32[]{:S(2)}) collective-permute-start(bf16[48,32]{0,1:T(8,128)(2,1)S(1)} %select_reduce_fusion), channel_id=1, source_target_pairs={{0,0},{1,4},{2,8},{3,12},{4,1},{5,5},{6,9},{7,13},{8,2},{9,6},{10,... | collective-permute-start | bytes 9224 | tf_op jit(solution)/shard_map/ppermute | solution.py:46

commit v2 on v1

--- a/solution.py
+++ b/solution.py
@@ -1,12 +1,497 @@
+import functools
 import math
 
 import jax
 import jax.numpy as jnp
 from jax import lax
+from jax.experimental import pallas as pl
+from jax.experimental.pallas import tpu as pltpu
 from jax.sharding import PartitionSpec as P
 
 rope_base = 500000.0
 EVERY = ("tensor", "dp", "pipe")
+GROUP = ("dp", "pipe")
+VMEM = pl.BlockSpec(memory_space=pltpu.VMEM)
+HBM = pl.BlockSpec(memory_space=pltpu.HBM)
+MIB = 1 << 20
+
+
+def dot(left, right):
+    return jnp.dot(left, right, preferred_element_type=jnp.float32)
+
+
+def dot_nt(left, right):
+    return lax.dot_general(
+        left, right, (((1,), (1,)), ((), ())), preferred_element_type=jnp.float32
+    )
+
+
+def iota(shape, axis):
+    return lax.broadcasted_iota(jnp.int32, shape, axis)
+
+
+def call(kernel, outs, ins, scratch=(), flops=0, moved=0, limit=24 * MIB):
+    return pl.pallas_call(
+        kernel,
+        out_shape=outs,
+        in_specs=ins,
+        out_specs=jax.tree.map(lambda _: VMEM, outs),
+        scratch_shapes=list(scratch),
+        cost_estimate=pl.CostEstimate(flops=flops, bytes_accessed=moved, transcendentals=0),
+        compiler_params=pltpu.CompilerParams(vmem_limit_bytes=limit),
+    )
+
+
+def shape(dims, kind=jnp.bfloat16):
+    return jax.ShapeDtypeStruct(tuple(dims), kind)
+
+
+def over(value, size):
+    return value >> (size.bit_length() - 1) if size & (size - 1) == 0 else lax.div(value, size)
+
+
+def rest_of(value, size):
+    return value & (size - 1) if size & (size - 1) == 0 else lax.rem(value, size)
+
+
+def block_first(sizes, group, block, draft):
+    groups, blocks, drafts = sizes
+    return (block * drafts + draft) * groups + group
+
+
+def group_first(sizes, group, block, draft):
+    groups, blocks, drafts = sizes
+    return (group * blocks + block) * drafts + draft
+
+
+def parts_of(order, sizes, index):
+    groups, blocks, drafts = sizes
+    if order is block_first:
+        return (
+            rest_of(index, groups),
+            over(index, groups * drafts),
+            rest_of(over(index, groups), drafts),
+        )
+    return over(index, blocks * drafts), rest_of(over(index, drafts), blocks), rest_of(index, drafts)
+
+
+def reorder(sizes, after, before, turn_block, turn_group=0):
+    groups, blocks, drafts = sizes
+    rows = groups * blocks * drafts
+    group, block, draft = parts_of(after, sizes, iota((rows, rows), 0))
+    wanted = before(
+        sizes, rest_of(group + turn_group, groups), rest_of(block + turn_block, blocks), draft
+    )
+    return jnp.where(wanted == iota((rows, rows), 1), 1.0, 0.0).astype(jnp.bfloat16)
+
+
+def rank_kernel(blocks, drafts, groups, *refs):
+    pieces = refs[:blocks]
+    shrink_ref, place_ref, rows_ref, rank_ref, wide = refs[blocks:]
+    for block in range(blocks):
+        for draft in range(drafts):
+            start = (block * drafts + draft) * groups
+            wide[start : start + groups, :] = pieces[block][draft].astype(jnp.float32)
+    rows = wide[...].astype(jnp.bfloat16)
+    rows_ref[...] = rows
+    rank_ref[...] = owned_ranks(rows, shrink_ref[...], place_ref[...], rank_ref.shape[1])
+
+
+def owned_ranks(rows, shrink, place, width):
+    ranks = dot_nt(rows, shrink)
+    columns = iota(ranks.shape, 1)
+    kept = jnp.where(over(columns, width) == place, ranks, 0.0).astype(jnp.bfloat16)
+    fold = rest_of(iota((ranks.shape[1], width), 0), width) == iota((ranks.shape[1], width), 1)
+    return dot(kept, jnp.where(fold, 1.0, 0.0).astype(jnp.bfloat16)).astype(jnp.bfloat16)
+
+
+def spread_ranks(ranks, place, width, owned):
+    parts = ranks.shape[1] // width
+    span = owned * width
+    row = iota((ranks.shape[1], parts * span), 0)
+    column = iota((ranks.shape[1], parts * span), 1)
+    tile = (over(row, width) == over(column, span)) & (
+        rest_of(row, width) == rest_of(column, width)
+    )
+    wide = dot(ranks, jnp.where(tile, 1.0, 0.0).astype(jnp.bfloat16))
+    slot = over(rest_of(iota(wide.shape, 1), span), width)
+    return jnp.where(slot == place, wide, 0.0).astype(jnp.bfloat16)
+
+
+def stream_kernel(weights, chunks, rows_ref, *refs):
+    sources = refs[:weights]
+    total_ref, buffer, sems = refs[weights:]
+    depth = rows_ref.shape[1] // chunks
+
+    def copy(chunk, index):
+        part = pl.ds(chunk * depth, depth)
+        start = sum(source.shape[1] for source in sources[:index])
+        return pltpu.make_async_copy(
+            sources[index].at[part],
+            buffer.at[part, pl.ds(start, sources[index].shape[1])],
+            sems.at[chunk, index],
+        )
+
+    for chunk in range(chunks):
+        for index in range(weights):
+            copy(chunk, index).start()
+    for chunk in range(chunks):
+        for index in range(weights):
+            copy(chunk, index).wait()
+        product = dot(
+            rows_ref[:, chunk * depth : (chunk + 1) * depth],
+            buffer[chunk * depth : (chunk + 1) * depth, :],
+        )
+        if chunk == 0:
+            total_ref[...] = product
+        else:
+            total_ref[...] += product
+
+
+def stream(rows, weights, chunks):
+    width = sum(w.shape[1] for w in weights)
+    return call(
+        functools.partial(stream_kernel, len(weights), chunks),
+        shape((rows.shape[0], width), jnp.float32),
+        [VMEM] + [HBM] * len(weights),
+        [
+            pltpu.VMEM((rows.shape[1], width), jnp.bfloat16),
+            pltpu.SemaphoreType.DMA((chunks, len(weights))),
+        ],
+        2 * rows.shape[0] * rows.shape[1] * width,
+        2 * rows.shape[1] * width,
+        40 * MIB,
+    )(rows, *weights)
+
+
+def pack_kernel(blocks, keys_ref, values_ref, extra_ref, *refs):
+    outs = refs[:blocks]
+    sems = refs[blocks]
+    size = keys_ref.shape[2]
+    me = lax.axis_index("tensor")
+    copies = []
+    for shift in range(blocks):
+        head = lax.rem(me + shift, blocks)
+        copies += [
+            pltpu.make_async_copy(
+                keys_ref.at[0, head], outs[shift].at[pl.ds(0, size)], sems.at[shift, 0]
+            ),
+            pltpu.make_async_copy(
+                values_ref.at[0, head], outs[shift].at[pl.ds(size, size)], sems.at[shift, 1]
+            ),
+            pltpu.make_async_copy(
+                extra_ref,
+                outs[shift].at[pl.ds(2 * size, extra_ref.shape[0])],
+                sems.at[shift, 2],
+            ),
+        ]
+    for copy in copies:
+        copy.start()
+    for copy in copies:
+        copy.wait()
+
+
+def pack(blocks, keys, values, extra):
+    rows = 2 * keys.shape[2] + extra.shape[0]
+    outs = [shape((rows, keys.shape[3]))] * blocks
+    return pl.pallas_call(
+        functools.partial(pack_kernel, blocks),
+        out_shape=outs,
+        in_specs=[HBM, HBM, VMEM],
+        out_specs=[HBM] * blocks,
+        scratch_shapes=[pltpu.SemaphoreType.DMA((blocks, 3))],
+        cost_estimate=pl.CostEstimate(flops=0, bytes_accessed=8 * keys.size, transcendentals=0),
+        compiler_params=pltpu.CompilerParams(vmem_limit_bytes=24 * MIB),
+    )(keys, values, extra)
+
+
+def grow_kernel(blocks, drafts, groups, width, *refs):
+    total_ref, place_ref, turn_ref, *rest = refs
+    ranks_in = rest[:blocks]
+    grows = rest[blocks : blocks + 3]
+    outs = rest[blocks + 3 :]
+    sizes = (groups, blocks, drafts)
+    ranks = ranks_in[0][...].astype(jnp.float32)
+    for other in ranks_in[1:]:
+        ranks = ranks + other[...].astype(jnp.float32)
+    ranks = dot(
+        reorder(sizes, block_first, block_first, turn_ref[0]), ranks.astype(jnp.bfloat16)
+    )
+    wide = spread_ranks(
+        ranks.astype(jnp.bfloat16), place_ref[...], width, grows[0].shape[0] // width
+    )
+    by_group = reorder(sizes, group_first, block_first, 0, turn_ref[1])
+    start = 0
+    for index, grow in enumerate(grows):
+        deep, cols = grow.shape
+        full = total_ref[:, start : start + cols] + dot(
+            wide[:, index * deep : (index + 1) * deep], grow[...]
+        )
+        full = dot(by_group, full.astype(jnp.bfloat16)).astype(jnp.bfloat16)
+        for step in range(groups):
+            for block in range(blocks):
+                row = (step * blocks + block) * drafts
+                outs[step][block, :, start : start + cols] = full[row : row + drafts]
+        start += cols
+
+
+def attend_kernel(blocks, drafts, groups, cache_size, *refs):
+    parts = refs[:groups]
+    caches = refs[groups : groups + blocks]
+    mixed_ref, query_s, fresh_s, out_s = refs[groups + blocks :]
+    head_size = caches[0].shape[1]
+    cols = parts[0].shape[2]
+    heads = cols // head_size - 2
+    count = heads * drafts
+    scale = 1.0 / math.sqrt(head_size)
+    fresh_s[...] = jnp.zeros(fresh_s.shape, jnp.float32)
+    pad = fresh_s.shape[1]
+    for block in range(blocks):
+        joined = parts[0][block].astype(jnp.float32)
+        for other in parts[1:]:
+            joined = joined + other[block].astype(jnp.float32)
+        joined = joined.astype(jnp.bfloat16).astype(jnp.float32)
+        extra = caches[block][2 * cache_size :, :].astype(jnp.float32)
+        cosine = extra[0:drafts] + extra[drafts : 2 * drafts]
+        sine = extra[2 * drafts : 3 * drafts] + extra[3 * drafts : 4 * drafts]
+        length = extra[4 * drafts : 4 * drafts + 1, 0:1] * 16.0 + extra[
+            4 * drafts + 1 : 4 * drafts + 2, 0:1
+        ]
+
+        def rotated(head):
+            value = joined[:, head * head_size : (head + 1) * head_size]
+            return value * cosine + pltpu.roll(value, head_size // 2, 1) * sine
+
+        for head in range(heads):
+            query_s[block, head * drafts : (head + 1) * drafts, :] = rotated(head)
+        fresh_s[2 * block, 0:drafts, :] = rotated(heads)
+        fresh_s[2 * block + 1, 0:drafts, :] = joined[:, (heads + 1) * head_size :]
+        query = query_s[block].astype(jnp.bfloat16)
+        old = dot_nt(query, caches[block][0:cache_size, :]) * scale
+        new = dot_nt(query, fresh_s[2 * block].astype(jnp.bfloat16)) * scale
+        old_seen = iota(old.shape, 1).astype(jnp.float32) < length
+        new_seen = iota(new.shape, 1) <= lax.rem(iota(new.shape, 0), drafts)
+        old = jnp.where(old_seen, old, -jnp.inf)
+        new = jnp.where(new_seen, new, -jnp.inf)
+        peak = jnp.maximum(
+            jnp.max(old, 1, keepdims=True), jnp.max(new, 1, keepdims=True)
+        )
+        old = jnp.exp(old - peak)
+        new = jnp.exp(new - peak)
+        below = jnp.sum(old, 1, keepdims=True) + jnp.sum(new, 1, keepdims=True)
+        mixed = dot(
+            (old / below).astype(jnp.bfloat16), caches[block][cache_size : 2 * cache_size, :]
+        ) + dot((new / below).astype(jnp.bfloat16), fresh_s[2 * block + 1].astype(jnp.bfloat16))
+        for head in range(heads):
+            out_s[
+                block * drafts : (block + 1) * drafts, head * head_size : (head + 1) * head_size
+            ] = mixed[head * drafts : (head + 1) * drafts]
+    mixed_ref[...] = out_s[...].astype(jnp.bfloat16)
+
+
+def out_rank_kernel(span, got_ref, shrink_ref, place_ref, rows_ref, rank_ref, wide):
+    for group in range(got_ref.shape[0]):
+        wide[group * span : (group + 1) * span, :] = got_ref[group].astype(jnp.float32)
+    rows = wide[...].astype(jnp.bfloat16)
+    rows_ref[...] = rows
+    rank_ref[...] = owned_ranks(rows, shrink_ref[...], place_ref[...], rank_ref.shape[1])
+
+
+def out_grow_kernel(blocks, drafts, groups, *refs):
+    total_ref, place_ref, turn_ref, *rest = refs
+    ranks_in = rest[:blocks]
+    grow_ref = rest[blocks]
+    outs = rest[blocks + 1 :]
+    sizes = (groups, blocks, drafts)
+    width = ranks_in[0].shape[1]
+    ranks = None
+    for index, part in enumerate(ranks_in):
+        moved = dot(reorder(sizes, group_first, group_first, turn_ref[index]), part[...])
+        ranks = moved if ranks is None else ranks + moved
+    wide = spread_ranks(
+        ranks.astype(jnp.bfloat16), place_ref[...], width, grow_ref.shape[0] // width
+    )
+    full = (total_ref[...] + dot(wide, grow_ref[...])).astype(jnp.bfloat16)
+    full = dot(reorder(sizes, block_first, group_first, 0), full).astype(jnp.bfloat16)
+    for block in range(blocks):
+        for draft in range(drafts):
+            start = (block * drafts + draft) * groups
+            outs[block][draft] = full[start : start + groups]
+
+
+def halves(value):
+    high = value.astype(jnp.bfloat16)
+    return high, (value - high.astype(jnp.float32)).astype(jnp.bfloat16)
+
+
+def by_head(
+    tokens,
+    w_query,
+    w_key,
+    w_value,
+    w_out,
+    shrink_qkv,
+    grow_query,
+    grow_key,
+    grow_value,
+    shrink_out,
+    grow_out,
+    cache_keys,
+    cache_values,
+    cache_lengths,
+    adapter_ids,
+    adapter_slots,
+):
+    blocks = lax.axis_size("tensor")
+    groups = lax.axis_size(GROUP)
+    tensor_index = lax.axis_index("tensor")
+    group_index = lax.axis_index(GROUP)
+    _, drafts, features = tokens.shape
+    owned = shrink_qkv.shape[0]
+    width = grow_out.shape[1]
+    cache_size, head_size = cache_keys.shape[2:]
+    span = blocks * drafts
+    count = groups * span
+
+    def over_tensor(value, shift):
+        route = [(t, (t + shift) % blocks) for t in range(blocks)]
+        return lax.ppermute(value, "tensor", route)
+
+    def over_group(value, shift):
+        route = [(g, (g + shift) % groups) for g in range(groups)]
+        return lax.ppermute(value, GROUP, route)
+
+    def to_growers(value, shift):
+        route = [
+            (t * groups + g, ((g + shift) % blocks) * groups + t)
+            for t in range(blocks)
+            for g in range(groups)
+        ]
+        return lax.ppermute(value, EVERY, route)
+
+    def to_out_growers(value, shift):
+        route = [
+            (t * groups + g, g * groups + (t + shift) % groups)
+            for t in range(blocks)
+            for g in range(groups)
+        ]
+        return lax.ppermute(value, EVERY, route)
+
+    mine = jnp.transpose(tokens, (1, 0, 2))
+    pieces = [mine] + [over_tensor(mine, shift) for shift in range(1, blocks)]
+
+    length = cache_lengths[0]
+    positions = (length + jnp.arange(drafts, dtype=jnp.int32)).astype(jnp.float32)
+    half_size = head_size // 2
+    frequency = rope_base ** (-2.0 * jnp.arange(half_size, dtype=jnp.float32) / head_size)
+    angles = positions[:, None] * frequency
+    cosine = jnp.cos(angles)
+    sine = jnp.sin(angles)
+    cos_high, cos_low = halves(jnp.concatenate([cosine, cosine], 1))
+    sin_high, sin_low = halves(jnp.concatenate([-sine, sine], 1))
+    spell = jnp.stack([length // 16, length % 16]).astype(jnp.bfloat16)
+    used = 4 * drafts + 2
+    extra = jnp.concatenate(
+        [
+            cos_high,
+            cos_low,
+            sin_high,
+            sin_low,
+            jnp.broadcast_to(spell[:, None], (2, head_size)),
+            jnp.zeros((-used % 16, head_size), jnp.bfloat16),
+        ],
+        0,
+    )
+
+    messages = pack(blocks, cache_keys, cache_values, extra)
+    caches = [messages[0]] + [over_tensor(messages[shift], shift) for shift in range(1, blocks)]
+
+    matches = adapter_ids[:, None] == jnp.arange(adapter_slots.shape[0], dtype=jnp.int32)[None, :]
+    row_slots = jnp.sum(jnp.where(matches, adapter_slots[None, :], 0), axis=1)
+    turned = (tensor_index - jnp.arange(blocks, dtype=jnp.int32)) % blocks
+    places = turned[None, :] * groups + jnp.arange(groups, dtype=jnp.int32)[:, None]
+    slots = jnp.sum(
+        jnp.where(
+            places[:, :, None] == jnp.arange(blocks * groups, dtype=jnp.int32), row_slots, 0
+        ),
+        -1,
+    )
+    group_slots = jnp.broadcast_to(slots[:, :, None], (groups, blocks, drafts)).reshape(count, 1)
+    block_slots = jnp.broadcast_to(slots.T[:, None, :], (blocks, drafts, groups)).reshape(count, 1)
+    first_width = block_slots - tensor_index * owned
+    first_column = block_slots - group_index * owned
+    last_width = group_slots - tensor_index * owned
+    last_column = group_slots - group_index * owned
+
+    shrink_in = jnp.transpose(shrink_qkv, (0, 2, 1)).reshape(-1, features)
+    rows, rank_part = call(
+        functools.partial(rank_kernel, blocks, drafts, groups),
+        [shape((count, features)), shape((count, shrink_qkv.shape[2]))],
+        [VMEM] * (blocks + 2),
+        [pltpu.VMEM((count, features), jnp.float32)],
+        2 * count * shrink_qkv.size,
+        2 * shrink_qkv.size + 4 * count * features,
+    )(*pieces, shrink_in, first_width)
+    ranks = [to_growers(rank_part, shift) for shift in range(blocks)]
+    weights_in = (w_query, w_key, w_value)
+    total = stream(rows, weights_in, 8)
+    cols = total.shape[1]
+    turn = jnp.stack([(group_index - tensor_index) % blocks, group_index]).astype(jnp.int32)
+    sent = call(
+        functools.partial(grow_kernel, blocks, drafts, groups, width),
+        [shape((blocks, drafts, cols))] * groups,
+        [VMEM, VMEM, pl.BlockSpec(memory_space=pltpu.SMEM)] + [VMEM] * (blocks + 3),
+        [],
+        2 * count * owned * width * cols,
+        8 * count * cols + 2 * owned * width * cols,
+    )(
+        total,
+        first_column,
+        turn,
+        *ranks,
+        *[grow.reshape(owned * width, -1) for grow in (grow_query, grow_key, grow_value)],
+    )
+    parts = [sent[0]] + [over_group(sent[shift], shift) for shift in range(1, groups)]
+    head_cols = cols - 2 * head_size
+    mixed = call(
+        functools.partial(attend_kernel, blocks, drafts, groups, cache_size),
+        shape((span, head_cols)),
+        [VMEM] * (groups + blocks),
+        [
+            pltpu.VMEM((blocks, head_cols // head_size * drafts, head_size), jnp.float32),
+            pltpu.VMEM((2 * blocks, 128, head_size), jnp.float32),
+            pltpu.VMEM((span, head_cols), jnp.float32),
+        ],
+        4 * span * head_cols * cache_size,
+        4 * blocks * cache_size * head_size,
+    )(*parts, *caches)
+    gathered = lax.all_gather(mixed, GROUP, axis=0, tiled=False)
+    out_rows, out_part = call(
+        functools.partial(out_rank_kernel, span),
+        [shape((count, head_cols)), shape((count, width))],
+        [VMEM] * 3,
+        [pltpu.VMEM((count, head_cols), jnp.float32)],
+        2 * count * shrink_out.size,
+        2 * shrink_out.size + 4 * count * head_cols,
+    )(gathered, jnp.transpose(shrink_out, (0, 2, 1)).reshape(-1, head_cols), last_column)
+    out_ranks = [to_out_growers(out_part, shift) for shift in range(groups)]
+    out_total = stream(out_rows, (w_out,), 8)
+    out_cols = out_total.shape[1]
+    out_turn = (
+        (group_index - tensor_index - jnp.arange(groups, dtype=jnp.int32)) % blocks
+    ).astype(jnp.int32)
+    leaving = call(
+        functools.partial(out_grow_kernel, blocks, drafts, groups),
+        [shape((drafts, groups, out_cols))] * blocks,
+        [VMEM, VMEM, pl.BlockSpec(memory_space=pltpu.SMEM)] + [VMEM] * (groups + 1),
+        [],
+        2 * count * owned * width * out_cols,
+        8 * count * out_cols + 2 * owned * width * out_cols,
+    )(out_total, last_width, out_turn, *out_ranks, grow_out.reshape(owned * width, -1))
+    result = leaving[0].astype(jnp.float32)
+    for shift in range(1, blocks):
+        result = result + over_tensor(leaving[shift], -shift).astype(jnp.float32)
+    return jnp.transpose(result.astype(jnp.bfloat16), (1, 0, 2))
 
 
 def rotate(vectors, positions):
@@ -88,7 +573,7 @@
     return mixed.astype(jnp.bfloat16)
 
 
-def local(
+def by_row(
     tokens,
     w_query,
     w_key,
@@ -194,6 +679,13 @@
     return jnp.sum(blocks.astype(jnp.float32), 0).astype(jnp.bfloat16)
 
 
+def local(*arrays):
+    heads = arrays[11].shape[1]
+    if heads == lax.axis_size("tensor") == lax.axis_size(GROUP):
+        return by_head(*arrays)
+    return by_row(*arrays)
+
+
 def solution(mesh):
     placed = (
         P(("parts", "tensor"), None, ("dp", "pipe")),

time: 135 us -> 94.4 us (0.70)
  blocking collectives: 49.5 us -> 6.84 us
  matrix products: 33.2 us -> 0 us
  starting transfers between devices: 17.4 us -> 39.5 us
  Pallas kernels: 0 us -> 21.8 us
  other arithmetic: 7.31 us -> 2.82 us
  local copies, waits for them, and re-layouts: 15 us -> 11.3 us
    dot_general x13 -> x0, matrix products: 31.8 us -> none  [the longest x3 13.8 us: local(): jnp.dot(flat_tokens, weight, preferred_element_type=jnp.float32)]
    all_to_all x2 -> x0, blocking collectives: 31.5 us -> none  [the longest x1 18.2 us: local(): lax.all_to_all(out.astype(jnp.bfloat16).reshape(splits, local_rows, draft...]
    ppermute x8 -> x20, starting transfers between devices: 10.3 us -> 39.5 us  [the longest x4 14.4 us: to_growers(): return lax.ppermute(value, EVERY, route)]
    pallas_call x0 -> x8, Pallas kernels: none -> 21.8 us  [the longest x2 13.2 us: stream(): call(functools.partial(stream_kernel, len(weights), chunks), shape((rows....]
    all_gather x1, blocking collectives: 18 us -> 6.84 us  [by_head(): gathered = lax.all_gather(mixed, GROUP, axis=0, tiled=False)]
    ppermute x8 -> x20, waiting for transfers between devices: 0.02 us -> 10.7 us  [the longest x9 8.73 us: over_tensor(): return lax.ppermute(value, 'tensor', route)]
    all_to_all x1 -> x0, waiting for transfers between devices: 9.85 us -> none  [local(): lax.all_to_all(partial, EVERY, split_axis=0, concat_axis=0, tiled=True)]
    reshape x9 -> x0, local copies, waits for them, and re-layouts: 9.41 us -> none  [the longest x3 3.09 us: product(): (bases[index] + grown(index, grow)).astype(jnp.bfloat16)]
  transfers between devices with their start and end apart: 9 -> 20, of which waited for: 1 -> 5; matrix products, arithmetic and copies ran while one was open for 9% -> 5% of each run, Pallas kernels for 0% -> 20%
where the time goes in v2:
time: 94.4 us; the launch traced here: 93.9 us
  starting transfers between devices  39.5 us (42%)
  Pallas kernels  21.8 us (23%)
  local copies, waits for them, and re-layouts  11.3 us (12%)
  waiting for transfers between devices  10.7 us (11%)
  blocking collectives  6.84 us (7%)
  other arithmetic  2.82 us (3%)
  between operations  0.95 us (1%)
    ppermute x4, starting transfers between devices, to_growers(): return lax.ppermute(value, EVERY, route)  14.4 us
    pallas_call x2, Pallas kernels, stream(): call(functools.partial(stream_kernel, len(weights), chunks), shape((rows....  13.2 us
    ppermute x9, starting transfers between devices, over_tensor(): return lax.ppermute(value, 'tensor', route)  12.9 us
    unnamed x40, local copies, waits for them, and re-layouts  9.1 us
    ppermute x9, waiting for transfers between devices, over_tensor(): return lax.ppermute(value, 'tensor', route)  8.73 us
    ppermute x4, starting transfers between devices, to_out_growers(): return lax.ppermute(value, EVERY, route)  8.3 us
    all_gather x1, blocking collectives, by_head(): gathered = lax.all_gather(mixed, GROUP, axis=0, tiled=False)  6.84 us
    ppermute x3, starting transfers between devices, over_group(): return lax.ppermute(value, GROUP, route)  3.88 us
  transfers between devices with their start and end apart: 20, of which 5 were waited for; matrix products, arithmetic and copies ran while one was open for 5% of the time, Pallas kernels for 20%

profile of v2, /device:TPU:0, one launch (start us, length us, event | category | flops | bytes accessed | tf_op | source)
XLA Modules:
  0.0 93.9 jit_solution(16173353775175664823)
XLA Ops:
  0.0 3.0 %collective-permute-start = (bf16[3,4,4096]{2,1,0:T(4,128)(2,1)}, bf16[3,4,4096]{2,1,0:T(4,128)(2,1)S(1)}, u32[]{:S(2)}, u32[]{:S(2)}) collective-permute-start(bf16[3,4,4096]{2,1,0:T(4,128)(2,1)} %bitcast.31), channel_id=1, source_target_pairs={{0,4},{4,8},{8,12},{12,0},{1,5},{5,9},{9,13},{13,1},{2,6},{6,10},{... | collective-permute-start | bytes 294920 | tf_op jit(solution)/shard_map/ppermute | solution.py:358
  3.0 2.6 %collective-permute-start.1 = (bf16[3,4,4096]{2,1,0:T(4,128)(2,1)}, bf16[3,4,4096]{2,1,0:T(4,128)(2,1)S(1)}, u32[]{:S(2)}, u32[]{:S(2)}) collective-permute-start(bf16[3,4,4096]{2,1,0:T(4,128)(2,1)} %bitcast.32), channel_id=1, source_target_pairs={{0,8},{4,12},{8,0},{12,4},{1,9},{5,13},{9,1},{13,5},{2,10},{6,14},... | collective-permute-start | bytes 294920 | tf_op jit(solution)/shard_map/ppermute | solution.py:358
  5.6 1.3 %collective-permute-start.2 = (bf16[3,4,4096]{2,1,0:T(4,128)(2,1)}, bf16[3,4,4096]{2,1,0:T(4,128)(2,1)S(1)}, u32[]{:S(2)}, u32[]{:S(2)}) collective-permute-start(bf16[3,4,4096]{2,1,0:T(4,128)(2,1)} %bitcast.33), channel_id=1, source_target_pairs={{0,12},{4,0},{8,4},{12,8},{1,13},{5,1},{9,5},{13,9},{2,14},{6,2},{... | collective-permute-start | bytes 294920 | tf_op jit(solution)/shard_map/ppermute | solution.py:358
  8.2 1.0 %copy-done.4 = bf16[1,4,512,128]{3,2,1,0:T(8,128)(2,1)S(1)} copy-done((bf16[1,4,512,128]{3,2,1,0:T(8,128)(2,1)S(1)}, bf16[1,4,512,128]{3,2,1,0:T(8,128)(2,1)}, u32[]{:S(2)}) %copy-start.4) | copy-done | bytes 524312
  9.3 1.0 %copy-done.5 = bf16[1,4,512,128]{3,2,1,0:T(8,128)(2,1)S(1)} copy-done((bf16[1,4,512,128]{3,2,1,0:T(8,128)(2,1)S(1)}, bf16[1,4,512,128]{3,2,1,0:T(8,128)(2,1)}, u32[]{:S(2)}) %copy-start.5) | copy-done | bytes 524312
  10.3 1.3 %shard_map.157 = (bf16[1040,128]{1,0:T(8,128)(2,1)S(1)}, bf16[1040,128]{1,0:T(8,128)(2,1)}, bf16[1040,128]{1,0:T(8,128)(2,1)}, bf16[1040,128]{1,0:T(8,128)(2,1)}) custom-call(bf16[1,4,512,128]{3,2,1,0:T(8,128)(2,1)S(1)} %copy-done.4, bf16[1,4,512,128]{3,2,1,0:T(8,128)(2,1)S(1)} %copy-done.5, bf16[16,128]{1,0:T(8,128)(2,1)S(1)} %concatenate.16.extra_ref), custom_call_target="tpu_custom_call" | custom-call | bytes 2097152 | tf_op jit(solution)/shard_map/pallas_call | solution.py:197
  11.6 0.7 collective-permute-start.10
  12.4 0.3 collective-permute-start.11
  12.7 0.9 select_reduce_fusion.1
  13.6 0.2 select_reduce_fusion
  13.9 0.5 copy-done.17
  14.6 2.8 %collective-permute-start.12 = (bf16[1040,128]{1,0:T(8,128)(2,1)}, bf16[1040,128]{1,0:T(8,128)(2,1)S(1)}, u32[]{:S(2)}, u32[]{:S(2)}) collective-permute-start(bf16[1040,128]{1,0:T(8,128)(2,1)} %get-tuple-element.30), channel_id=1, source_target_pairs={{0,12},{4,0},{8,4},{12,8},{1,13},{5,1},{9,5},{13,9},{2,14},{6,2},{... | collective-permute-start | bytes 798728 | tf_op jit(solution)/shard_map/ppermute | solution.py:358
  17.4 1.9 %copy-done = bf16[4,4096,96]{1,2,0:T(8,128)(2,1)S(1)} copy-done((bf16[4,4096,96]{1,2,0:T(8,128)(2,1)S(1)}, bf16[4,4096,96]{1,2,0:T(8,128)(2,1)}, u32[]{:S(2)}) %copy-start) | copy-done | bytes 3145752
  19.3 0.9 copy-done.8
  20.2 1.9 %shard_map.154 = (bf16[48,4096]{1,0:T(8,128)(2,1)S(1)}, bf16[48,96]{1,0:T(8,128)(2,1)}) custom-call(bf16[3,4,4096]{2,1,0:T(4,128)(2,1)S(1)} %bitcast.34, bf16[3,4,4096]{2,1,0:T(4,128)(2,1)S(1)} %collective-permute-done.refs_1_, bf16[3,4,4096]{2,1,0:T(4,128)(2,1)S(1)} %collective-permute-done.1.refs_2_, ...), custom_call_target="tpu_custom_call" | custom-call | flops 150994944 | bytes 3932160 | tf_op jit(solution)/shard_map/pallas_call | solution.py:427
  22.1 1.4 %collective-permute-start.3 = (bf16[48,96]{1,0:T(8,128)(2,1)}, bf16[48,96]{1,0:T(8,128)(2,1)S(1)}, u32[]{:S(2)}, u32[]{:S(2)}) collective-permute-start(bf16[48,96]{1,0:T(8,128)(2,1)} %get-tuple-element.22), channel_id=1, source_target_pairs={{0,0},{1,4},{2,8},{3,12},{4,1},{5,5},{6,9},{7,13},{8,2},{9,6},{10,... | collective-permute-start | bytes 27656 | tf_op jit(solution)/shard_map/ppermute | solution.py:370
  23.4 1.2 %collective-permute-start.4 = (bf16[48,96]{1,0:T(8,128)(2,1)}, bf16[48,96]{1,0:T(8,128)(2,1)S(1)}, u32[]{:S(2)}, u32[]{:S(2)}) collective-permute-start(bf16[48,96]{1,0:T(8,128)(2,1)} %get-tuple-element.22), channel_id=1, source_target_pairs={{0,4},{1,8},{2,12},{3,0},{4,5},{5,9},{6,13},{7,1},{8,6},{9,10},{10... | collective-permute-start | bytes 27656 | tf_op jit(solution)/shard_map/ppermute | solution.py:370
  24.6 0.6 pad_add_fusion.refs_2_
  25.3 0.7 sub.77.refs_1_
  26.0 0.6 copy-done.12
  26.6 11.9 %collective-permute-start.5 = (bf16[48,96]{1,0:T(8,128)(2,1)}, bf16[48,96]{1,0:T(8,128)(2,1)S(1)}, u32[]{:S(2)}, u32[]{:S(2)}) collective-permute-start(bf16[48,96]{1,0:T(8,128)(2,1)} %get-tuple-element.22), channel_id=1, source_target_pairs={{0,8},{1,12},{2,0},{3,4},{4,9},{5,13},{6,1},{7,5},{8,10},{9,14},{1... | collective-permute-start | bytes 27656 | tf_op jit(solution)/shard_map/ppermute | solution.py:370
  38.5 0.6 copy-done.14
  39.1 1.2 %copy-done.1 = bf16[4096,128]{1,0:T(8,128)(2,1)S(1)} copy-done((bf16[4096,128]{1,0:T(8,128)(2,1)S(1)}, bf16[4096,128]{1,0:T(8,128)(2,1)}, u32[]{:S(2)}) %copy-start.1) | copy-done | bytes 1048600
  40.3 1.2 %copy-done.2 = bf16[4096,128]{1,0:T(8,128)(2,1)S(1)} copy-done((bf16[4096,128]{1,0:T(8,128)(2,1)S(1)}, bf16[4096,128]{1,0:T(8,128)(2,1)}, u32[]{:S(2)}) %copy-start.2) | copy-done | bytes 1048600
  41.6 6.8 %shard_map.155.refs_0_ = f32[48,2304]{1,0:T(8,128)S(1)} custom-call(bf16[48,4096]{1,0:T(8,128)(2,1)S(1)} %get-tuple-element.21.rows_ref, bf16[4096,2048]{1,0:T(8,128)(2,1)} %refs_0_.2, bf16[4096,128]{1,0:T(8,128)(2,1)S(1)} %copy-done.1, bf16[4096,128]{1,0:T(8,128)(2,1)S(1)} %copy-done.2), custom_call_target="tpu_custom_call" | custom-call | flops 905969664 | bytes 18874368 | tf_op jit(solution)/shard_map/pallas_call | solution.py:153
  48.4 2.0 %shard_map.156 = (bf16[4,3,2304]{2,1,0:T(4,128)(2,1)S(1)}, bf16[4,3,2304]{2,1,0:T(4,128)(2,1)S(1)}, bf16[4,3,2304]{2,1,0:T(4,128)(2,1)}, bf16[4,3,2304]{2,1,0:T(4,128)(2,1)}) custom-call(f32[48,2304]{1,0:T(8,128)S(1)} %shard_map.155.refs_0_, s32[48,1]{1,0:T(8,128)S(1)} %copy-done.9, s32[2]{0:T(128)S(1)} %copy-done.16, bf16[48,96]{1,0:T(8,128)(2,1)S(1)} %copy-done.13, ...), custom_call_target="tpu_custom_call" | custom-call | flops 28311552 | bytes 1474560 | tf_op jit(solution)/shard_map/pallas_call | solution.py:440
  50.4 0.5 collective-permute-start.7
  50.9 2.6 %collective-permute-start.8 = (bf16[4,3,2304]{2,1,0:T(4,128)(2,1)}, bf16[4,3,2304]{2,1,0:T(4,128)(2,1)S(1)}, u32[]{:S(2)}, u32[]{:S(2)}) collective-permute-start(bf16[4,3,2304]{2,1,0:T(4,128)(2,1)} %get-tuple-element.25), channel_id=1, source_target_pairs={{0,2},{1,3},{2,0},{3,1},{4,6},{5,7},{6,4},{7,5},{8,10},{9,11},{10,... | collective-permute-start | bytes 165896 | tf_op jit(solution)/shard_map/ppermute | solution.py:362
  53.5 0.7 collective-permute-done.7.refs_1_
  54.2 0.8 collective-permute-start.9
  55.1 0.7 broadcast_in_dim.63
  56.0 0.5 collective-permute-done.8.refs_2_
  56.5 0.8 collective-permute-done.9.refs_3_
  57.3 1.8 %shard_map.158 = bf16[12,2048]{1,0:T(8,128)(2,1)S(1)} custom-call(bf16[4,3,2304]{2,1,0:T(4,128)(2,1)S(1)} %get-tuple-element.23.refs_0_, bf16[4,3,2304]{2,1,0:T(4,128)(2,1)S(1)} %collective-permute-done.7.refs_1_, bf16[4,3,2304]{2,1,0:T(4,128)(2,1)S(1)} %collective-permute-done.8.refs_2_, bf16[4,3,2304]{2,1,0:T(4,128)(2,1)S(1)} %collective-permute-done.9.refs_3_, ...), custom_call_target="tpu_custom_call" | custom-call | flops 50331648 | bytes 1048576 | tf_op jit(solution)/shard_map/pallas_call | solution.py:456
  59.1 6.8 %all-gather.1.got_ref = bf16[4,12,2048]{2,1,0:T(8,128)(2,1)S(1)} all-gather(bf16[1,12,2048]{2,1,0:T(8,128)(2,1)S(1)} %bitcast.30), channel_id=2, replica_groups=mesh['parts'=2,'tensor'=4,'dp'=2,'pipe'=2] {'dp','pipe'}, dimensions={0}, use_global_device_ids=true | all-gather | bytes 245760 | tf_op jit(solution)/shard_map/all_gather | solution.py:468
  65.9 0.4 shard_map.159
  66.3 0.7 collective-permute-start.13
  67.0 2.3 %collective-permute-start.14 = (bf16[48,32]{1,0:T(8,128)(2,1)S(1)}, bf16[48,32]{1,0:T(8,128)(2,1)S(1)}, u32[]{:S(2)}, u32[]{:S(2)}) collective-permute-start(bf16[48,32]{1,0:T(8,128)(2,1)S(1)} %get-tuple-element.32), channel_id=1, source_target_pairs={{0,1},{1,5},{2,9},{3,13},{4,2},{5,6},{6,10},{7,14},{8,3},{9,7},{10... | collective-permute-start | bytes 9224 | tf_op jit(solution)/shard_map/ppermute | solution.py:378
  69.3 3.1 %collective-permute-start.15 = (bf16[48,32]{1,0:T(8,128)(2,1)S(1)}, bf16[48,32]{1,0:T(8,128)(2,1)S(1)}, u32[]{:S(2)}, u32[]{:S(2)}) collective-permute-start(bf16[48,32]{1,0:T(8,128)(2,1)S(1)} %get-tuple-element.32), channel_id=1, source_target_pairs={{0,2},{1,6},{2,10},{3,14},{4,3},{5,7},{6,11},{7,15},{8,0},{9,4},{1... | collective-permute-start | bytes 9224 | tf_op jit(solution)/shard_map/ppermute | solution.py:378
  72.4 2.3 %collective-permute-start.16 = (bf16[48,32]{1,0:T(8,128)(2,1)S(1)}, bf16[48,32]{1,0:T(8,128)(2,1)S(1)}, u32[]{:S(2)}, u32[]{:S(2)}) collective-permute-start(bf16[48,32]{1,0:T(8,128)(2,1)S(1)} %get-tuple-element.32), channel_id=1, source_target_pairs={{0,3},{1,7},{2,11},{3,15},{4,0},{5,4},{6,8},{7,12},{8,1},{9,5},{10... | collective-permute-start | bytes 9224 | tf_op jit(solution)/shard_map/ppermute | solution.py:378
  74.6 6.4 %shard_map.160.refs_0_ = f32[48,4096]{1,0:T(8,128)S(1)} custom-call(bf16[48,2048]{1,0:T(8,128)(2,1)S(1)} %get-tuple-element.31.rows_ref, bf16[2048,4096]{1,0:T(8,128)(2,1)} %refs_0_.3), custom_call_target="tpu_custom_call" | custom-call | flops 805306368 | bytes 16777216 | tf_op jit(solution)/shard_map/pallas_call | solution.py:153
  81.1 1.2 %shard_map.161 = (bf16[3,4,4096]{2,1,0:T(4,128)(2,1)S(1)}, bf16[3,4,4096]{2,1,0:T(4,128)(2,1)S(1)}, bf16[3,4,4096]{2,1,0:T(4,128)(2,1)S(1)}, bf16[3,4,4096]{2,1,0:T(4,128)(2,1)S(1)}) custom-call(f32[48,4096]{1,0:T(8,128)S(1)} %shard_map.160.refs_0_, s32[48,1]{1,0:T(8,128)S(1)} %sub.79.refs_1_, s32[4]{0:T(128)S(1)} %and_select_fusion.refs_2_, ...), custom_call_target="tpu_custom_call" | custom-call | flops 50331648 | bytes 2621440 | tf_op jit(solution)/shard_map/pallas_call | solution.py:483
  82.4 1.1 %collective-permute-start.17 = (bf16[3,4,4096]{2,1,0:T(4,128)(2,1)S(1)}, bf16[3,4,4096]{2,1,0:T(4,128)(2,1)S(1)}, u32[]{:S(2)}, u32[]{:S(2)}) collective-permute-start(bf16[3,4,4096]{2,1,0:T(4,128)(2,1)S(1)} %get-tuple-element.34), channel_id=1, source_target_pairs={{0,12},{4,0},{8,4},{12,8},{1,13},{5,1},{9,5},{13,9},{2,14},{6,2},{... | collective-permute-start | bytes 294920 | tf_op jit(solution)/shard_map/ppermute | solution.py:358
  83.4 0.2 collective-permute-start.18
  83.6 0.8 collective-permute-start.19
  84.4 2.9 %collective-permute-done.17 = bf16[3,4,4096]{2,1,0:T(4,128)(2,1)S(1)} collective-permute-done((bf16[3,4,4096]{2,1,0:T(4,128)(2,1)S(1)}, bf16[3,4,4096]{2,1,0:T(4,128)(2,1)S(1)}, u32[]{:S(2)}, u32[]{:S(2)}) %collective-permute-start.17) | collective-permute-done | bytes 98336 | tf_op jit(solution)/shard_map/ppermute | solution.py:358
  87.3 5.9 %collective-permute-done.18 = bf16[3,4,4096]{2,1,0:T(4,128)(2,1)S(1)} collective-permute-done((bf16[3,4,4096]{2,1,0:T(4,128)(2,1)S(1)}, bf16[3,4,4096]{2,1,0:T(4,128)(2,1)S(1)}, u32[]{:S(2)}, u32[]{:S(2)}) %collective-permute-start.18) | collective-permute-done | bytes 98336 | tf_op jit(solution)/shard_map/ppermute | solution.py:358
  93.2 0.7 fusion
  (68 shorter events, 1.2 us)
Async XLA Ops:
  0.0 14.6 %collective-permute-start = (bf16[3,4,4096]{2,1,0:T(4,128)(2,1)}, bf16[3,4,4096]{2,1,0:T(4,128)(2,1)S(1)}, u32[]{:S(2)}, u32[]{:S(2)}) collective-permute-start(bf16[3,4,4096]{2,1,0:T(4,128)(2,1)} %bitcast.31), channel_id=1, source_target_pairs={{0,4},{4,8},{8,12},{12,0},{1,5},{5,9},{9,13},{13,1},{2,6},{6,10},{... | collective-permute-start | bytes 294920 | tf_op jit(solution)/shard_map/ppermute | solution.py:358
  3.0 14.4 %collective-permute-start.1 = (bf16[3,4,4096]{2,1,0:T(4,128)(2,1)}, bf16[3,4,4096]{2,1,0:T(4,128)(2,1)S(1)}, u32[]{:S(2)}, u32[]{:S(2)}) collective-permute-start(bf16[3,4,4096]{2,1,0:T(4,128)(2,1)} %bitcast.32), channel_id=1, source_target_pairs={{0,8},{4,12},{8,0},{12,4},{1,9},{5,13},{9,1},{13,5},{2,10},{6,14},... | collective-permute-start | bytes 294920 | tf_op jit(solution)/shard_map/ppermute | solution.py:358
  5.6 11.8 %collective-permute-start.2 = (bf16[3,4,4096]{2,1,0:T(4,128)(2,1)}, bf16[3,4,4096]{2,1,0:T(4,128)(2,1)S(1)}, u32[]{:S(2)}, u32[]{:S(2)}) collective-permute-start(bf16[3,4,4096]{2,1,0:T(4,128)(2,1)} %bitcast.33), channel_id=1, source_target_pairs={{0,12},{4,0},{8,4},{12,8},{1,13},{5,1},{9,5},{13,9},{2,14},{6,2},{... | collective-permute-start | bytes 294920 | tf_op jit(solution)/shard_map/ppermute | solution.py:358
  8.2 1.0 %copy-start.4 = (bf16[1,4,512,128]{3,2,1,0:T(8,128)(2,1)S(1)}, bf16[1,4,512,128]{3,2,1,0:T(8,128)(2,1)}, u32[]{:S(2)}) copy-start(bf16[1,4,512,128]{3,2,1,0:T(8,128)(2,1)} %keys_ref.1) | copy-start | bytes 1572868
  9.3 1.0 %copy-start.5 = (bf16[1,4,512,128]{3,2,1,0:T(8,128)(2,1)S(1)}, bf16[1,4,512,128]{3,2,1,0:T(8,128)(2,1)}, u32[]{:S(2)}) copy-start(bf16[1,4,512,128]{3,2,1,0:T(8,128)(2,1)} %values_ref.1) | copy-start | bytes 1572868
  10.3 38.1 %copy-start.6 = (bf16[4,32,2048]{2,1,0:T(8,128)(2,1)S(1)}, bf16[4,32,2048]{2,1,0:T(8,128)(2,1)}, u32[]{:S(2)}) copy-start(bf16[4,32,2048]{2,1,0:T(8,128)(2,1)} %param.22) | copy-start | bytes 1572868
  10.3 55.6 %copy-start.7 = (bf16[4,2048,32]{1,2,0:T(8,128)(2,1)S(1)}, bf16[4,2048,32]{1,2,0:T(8,128)(2,1)}, u32[]{:S(2)}) copy-start(bf16[4,2048,32]{1,2,0:T(8,128)(2,1)} %param.25) | copy-start | bytes 1572868
  11.6 45.6 %collective-permute-start.10 = (bf16[1040,128]{1,0:T(8,128)(2,1)}, bf16[1040,128]{1,0:T(8,128)(2,1)S(1)}, u32[]{:S(2)}, u32[]{:S(2)}) collective-permute-start(bf16[1040,128]{1,0:T(8,128)(2,1)} %get-tuple-element.28), channel_id=1, source_target_pairs={{0,4},{4,8},{8,12},{12,0},{1,5},{5,9},{9,13},{13,1},{2,6},{6,10},{... | collective-permute-start | bytes 798728 | tf_op jit(solution)/shard_map/ppermute | solution.py:358
  12.4 44.9 %collective-permute-start.11 = (bf16[1040,128]{1,0:T(8,128)(2,1)}, bf16[1040,128]{1,0:T(8,128)(2,1)S(1)}, u32[]{:S(2)}, u32[]{:S(2)}) collective-permute-start(bf16[1040,128]{1,0:T(8,128)(2,1)} %get-tuple-element.29), channel_id=1, source_target_pairs={{0,8},{4,12},{8,0},{12,4},{1,9},{5,13},{9,1},{13,5},{2,10},{6,14},... | collective-permute-start | bytes 798728 | tf_op jit(solution)/shard_map/ppermute | solution.py:358
  13.8 0.6 copy-start.17
  13.8 25.3 %copy-start.18 = (s32[4,4]{1,0:T(4,128)}, s32[4,4]{1,0:T(4,128)S(1)}, u32[]{:S(2)}) copy-start(s32[4,4]{1,0:T(4,128)S(1)} %get-tuple-element.37) | copy-start | bytes 196
  14.6 42.7 %collective-permute-start.12 = (bf16[1040,128]{1,0:T(8,128)(2,1)}, bf16[1040,128]{1,0:T(8,128)(2,1)S(1)}, u32[]{:S(2)}, u32[]{:S(2)}) collective-permute-start(bf16[1040,128]{1,0:T(8,128)(2,1)} %get-tuple-element.30), channel_id=1, source_target_pairs={{0,12},{4,0},{8,4},{12,8},{1,13},{5,1},{9,5},{13,9},{2,14},{6,2},{... | collective-permute-start | bytes 798728 | tf_op jit(solution)/shard_map/ppermute | solution.py:358
  17.4 1.9 %copy-start = (bf16[4,4096,96]{1,2,0:T(8,128)(2,1)S(1)}, bf16[4,4096,96]{1,2,0:T(8,128)(2,1)}, u32[]{:S(2)}) copy-start(bf16[4,4096,96]{1,2,0:T(8,128)(2,1)} %param.21) | copy-start | bytes 9437188
  19.3 0.9 copy-start.8
  22.1 4.0 %collective-permute-start.3 = (bf16[48,96]{1,0:T(8,128)(2,1)}, bf16[48,96]{1,0:T(8,128)(2,1)S(1)}, u32[]{:S(2)}, u32[]{:S(2)}) collective-permute-start(bf16[48,96]{1,0:T(8,128)(2,1)} %get-tuple-element.22), channel_id=1, source_target_pairs={{0,0},{1,4},{2,8},{3,12},{4,1},{5,5},{6,9},{7,13},{8,2},{9,6},{10,... | collective-permute-start | bytes 27656 | tf_op jit(solution)/shard_map/ppermute | solution.py:370
  23.4 15.1 %collective-permute-start.4 = (bf16[48,96]{1,0:T(8,128)(2,1)}, bf16[48,96]{1,0:T(8,128)(2,1)S(1)}, u32[]{:S(2)}, u32[]{:S(2)}) collective-permute-start(bf16[48,96]{1,0:T(8,128)(2,1)} %get-tuple-element.22), channel_id=1, source_target_pairs={{0,4},{1,8},{2,12},{3,0},{4,5},{5,9},{6,13},{7,1},{8,6},{9,10},{10... | collective-permute-start | bytes 27656 | tf_op jit(solution)/shard_map/ppermute | solution.py:370
  26.0 22.4 %copy-start.16 = (s32[2]{0:T(128)S(1)}, s32[2]{0:T(128)}, u32[]{:S(2)}) copy-start(s32[2]{0:T(128)} %pad_add_fusion.refs_2_) | copy-start | bytes 28
  26.0 0.6 copy-start.12
  26.6 21.7 %collective-permute-start.5 = (bf16[48,96]{1,0:T(8,128)(2,1)}, bf16[48,96]{1,0:T(8,128)(2,1)S(1)}, u32[]{:S(2)}, u32[]{:S(2)}) collective-permute-start(bf16[48,96]{1,0:T(8,128)(2,1)} %get-tuple-element.22), channel_id=1, source_target_pairs={{0,8},{1,12},{2,0},{3,4},{4,9},{5,13},{6,1},{7,5},{8,10},{9,14},{1... | collective-permute-start | bytes 27656 | tf_op jit(solution)/shard_map/ppermute | solution.py:370
  38.5 0.6 copy-start.14
  39.1 9.3 %collective-permute-start.6 = (bf16[48,96]{1,0:T(8,128)(2,1)}, bf16[48,96]{1,0:T(8,128)(2,1)S(1)}, u32[]{:S(2)}, u32[]{:S(2)}) collective-permute-start(bf16[48,96]{1,0:T(8,128)(2,1)} %get-tuple-element.22), channel_id=1, source_target_pairs={{0,12},{1,0},{2,4},{3,8},{4,13},{5,1},{6,5},{7,9},{8,14},{9,2},{10... | collective-permute-start | bytes 27656 | tf_op jit(solution)/shard_map/ppermute | solution.py:370
  39.1 1.2 %copy-start.1 = (bf16[4096,128]{1,0:T(8,128)(2,1)S(1)}, bf16[4096,128]{1,0:T(8,128)(2,1)}, u32[]{:S(2)}) copy-start(bf16[4096,128]{1,0:T(8,128)(2,1)} %refs_1_.1) | copy-start | bytes 3145732
  40.3 1.2 %copy-start.2 = (bf16[4096,128]{1,0:T(8,128)(2,1)S(1)}, bf16[4096,128]{1,0:T(8,128)(2,1)}, u32[]{:S(2)}) copy-start(bf16[4096,128]{1,0:T(8,128)(2,1)} %refs_2_.1) | copy-start | bytes 3145732
  41.5 6.9 %copy-start.9 = (s32[48,1]{1,0:T(8,128)S(1)}, s32[48,1]{1,0:T(8,128)}, u32[]{:S(2)}) copy-start(s32[48,1]{1,0:T(8,128)} %sub.77.refs_1_) | copy-start | bytes 580
  41.5 6.9 %copy-start.10 = (bf16[4,32,128]{2,1,0:T(8,128)(2,1)S(1)}, bf16[4,32,128]{2,1,0:T(8,128)(2,1)}, u32[]{:S(2)}) copy-start(bf16[4,32,128]{2,1,0:T(8,128)(2,1)} %param.23) | copy-start | bytes 98308
  41.5 6.9 %copy-start.11 = (bf16[4,32,128]{2,1,0:T(8,128)(2,1)S(1)}, bf16[4,32,128]{2,1,0:T(8,128)(2,1)}, u32[]{:S(2)}) copy-start(bf16[4,32,128]{2,1,0:T(8,128)(2,1)} %param.24) | copy-start | bytes 98308
  41.5 6.9 %copy-start.13 = (bf16[48,96]{1,0:T(8,128)(2,1)S(1)}, bf16[48,96]{1,0:T(8,128)(2,1)}, u32[]{:S(2)}) copy-start(bf16[48,96]{1,0:T(8,128)(2,1)} %copy-done.12) | copy-start | bytes 27652
  41.5 6.9 %copy-start.15 = (bf16[48,96]{1,0:T(8,128)(2,1)S(1)}, bf16[48,96]{1,0:T(8,128)(2,1)}, u32[]{:S(2)}) copy-start(bf16[48,96]{1,0:T(8,128)(2,1)} %copy-done.14) | copy-start | bytes 27652
  41.6 13.4 %copy-start.19 = (s32[4,4]{1,0:T(4,128)S(1)}, s32[4,4]{1,0:T(4,128)}, u32[]{:S(2)}) copy-start(s32[4,4]{1,0:T(4,128)} %copy-done.18) | copy-start | bytes 196
  41.6 39.5 %copy-start.3 = (bf16[4,32,4096]{2,1,0:T(8,128)(2,1)S(1)}, bf16[4,32,4096]{2,1,0:T(8,128)(2,1)}, u32[]{:S(2)}) copy-start(bf16[4,32,4096]{2,1,0:T(8,128)(2,1)} %param.26) | copy-start | bytes 3145732
  50.4 3.8 %collective-permute-start.7 = (bf16[4,3,2304]{2,1,0:T(4,128)(2,1)S(1)}, bf16[4,3,2304]{2,1,0:T(4,128)(2,1)S(1)}, u32[]{:S(2)}, u32[]{:S(2)}) collective-permute-start(bf16[4,3,2304]{2,1,0:T(4,128)(2,1)S(1)} %get-tuple-element.24), channel_id=1, source_target_pairs={{0,1},{1,2},{2,3},{3,0},{4,5},{5,6},{6,7},{7,4},{8,9},{9,10},{10,1... | collective-permute-start | bytes 165896 | tf_op jit(solution)/shard_map/ppermute | solution.py:362
  50.9 5.6 %collective-permute-start.8 = (bf16[4,3,2304]{2,1,0:T(4,128)(2,1)}, bf16[4,3,2304]{2,1,0:T(4,128)(2,1)S(1)}, u32[]{:S(2)}, u32[]{:S(2)}) collective-permute-start(bf16[4,3,2304]{2,1,0:T(4,128)(2,1)} %get-tuple-element.25), channel_id=1, source_target_pairs={{0,2},{1,3},{2,0},{3,1},{4,6},{5,7},{6,4},{7,5},{8,10},{9,11},{10,... | collective-permute-start | bytes 165896 | tf_op jit(solution)/shard_map/ppermute | solution.py:362
  54.2 3.1 %collective-permute-start.9 = (bf16[4,3,2304]{2,1,0:T(4,128)(2,1)}, bf16[4,3,2304]{2,1,0:T(4,128)(2,1)S(1)}, u32[]{:S(2)}, u32[]{:S(2)}) collective-permute-start(bf16[4,3,2304]{2,1,0:T(4,128)(2,1)} %get-tuple-element.26), channel_id=1, source_target_pairs={{0,3},{1,0},{2,1},{3,2},{4,7},{5,4},{6,5},{7,6},{8,11},{9,8},{10,9... | collective-permute-start | bytes 165896 | tf_op jit(solution)/shard_map/ppermute | solution.py:362
  66.3 14.7 %collective-permute-start.13 = (bf16[48,32]{1,0:T(8,128)(2,1)S(1)}, bf16[48,32]{1,0:T(8,128)(2,1)S(1)}, u32[]{:S(2)}, u32[]{:S(2)}) collective-permute-start(bf16[48,32]{1,0:T(8,128)(2,1)S(1)} %get-tuple-element.32), channel_id=1, source_target_pairs={{0,0},{1,4},{2,8},{3,12},{4,1},{5,5},{6,9},{7,13},{8,2},{9,6},{10,... | collective-permute-start | bytes 9224 | tf_op jit(solution)/shard_map/ppermute | solution.py:378
  67.0 14.1 %collective-permute-start.14 = (bf16[48,32]{1,0:T(8,128)(2,1)S(1)}, bf16[48,32]{1,0:T(8,128)(2,1)S(1)}, u32[]{:S(2)}, u32[]{:S(2)}) collective-permute-start(bf16[48,32]{1,0:T(8,128)(2,1)S(1)} %get-tuple-element.32), channel_id=1, source_target_pairs={{0,1},{1,5},{2,9},{3,13},{4,2},{5,6},{6,10},{7,14},{8,3},{9,7},{10... | collective-permute-start | bytes 9224 | tf_op jit(solution)/shard_map/ppermute | solution.py:378
  69.3 11.8 %collective-permute-start.15 = (bf16[48,32]{1,0:T(8,128)(2,1)S(1)}, bf16[48,32]{1,0:T(8,128)(2,1)S(1)}, u32[]{:S(2)}, u32[]{:S(2)}) collective-permute-start(bf16[48,32]{1,0:T(8,128)(2,1)S(1)} %get-tuple-element.32), channel_id=1, source_target_pairs={{0,2},{1,6},{2,10},{3,14},{4,3},{5,7},{6,11},{7,15},{8,0},{9,4},{1... | collective-permute-start | bytes 9224 | tf_op jit(solution)/shard_map/ppermute | solution.py:378
  72.4 8.7 %collective-permute-start.16 = (bf16[48,32]{1,0:T(8,128)(2,1)S(1)}, bf16[48,32]{1,0:T(8,128)(2,1)S(1)}, u32[]{:S(2)}, u32[]{:S(2)}) collective-permute-start(bf16[48,32]{1,0:T(8,128)(2,1)S(1)} %get-tuple-element.32), channel_id=1, source_target_pairs={{0,3},{1,7},{2,11},{3,15},{4,0},{5,4},{6,8},{7,12},{8,1},{9,5},{10... | collective-permute-start | bytes 9224 | tf_op jit(solution)/shard_map/ppermute | solution.py:378
  82.4 4.9 %collective-permute-start.17 = (bf16[3,4,4096]{2,1,0:T(4,128)(2,1)S(1)}, bf16[3,4,4096]{2,1,0:T(4,128)(2,1)S(1)}, u32[]{:S(2)}, u32[]{:S(2)}) collective-permute-start(bf16[3,4,4096]{2,1,0:T(4,128)(2,1)S(1)} %get-tuple-element.34), channel_id=1, source_target_pairs={{0,12},{4,0},{8,4},{12,8},{1,13},{5,1},{9,5},{13,9},{2,14},{6,2},{... | collective-permute-start | bytes 294920 | tf_op jit(solution)/shard_map/ppermute | solution.py:358
  83.4 9.7 %collective-permute-start.18 = (bf16[3,4,4096]{2,1,0:T(4,128)(2,1)S(1)}, bf16[3,4,4096]{2,1,0:T(4,128)(2,1)S(1)}, u32[]{:S(2)}, u32[]{:S(2)}) collective-permute-start(bf16[3,4,4096]{2,1,0:T(4,128)(2,1)S(1)} %get-tuple-element.35), channel_id=1, source_target_pairs={{0,8},{4,12},{8,0},{12,4},{1,9},{5,13},{9,1},{13,5},{2,10},{6,14},... | collective-permute-start | bytes 294920 | tf_op jit(solution)/shard_map/ppermute | solution.py:358
  83.6 9.5 %collective-permute-start.19 = (bf16[3,4,4096]{2,1,0:T(4,128)(2,1)S(1)}, bf16[3,4,4096]{2,1,0:T(4,128)(2,1)S(1)}, u32[]{:S(2)}, u32[]{:S(2)}) collective-permute-start(bf16[3,4,4096]{2,1,0:T(4,128)(2,1)S(1)} %get-tuple-element.36), channel_id=1, source_target_pairs={{0,4},{4,8},{8,12},{12,0},{1,5},{5,9},{9,13},{13,1},{2,6},{6,10},{... | collective-permute-start | bytes 294920 | tf_op jit(solution)/shard_map/ppermute | solution.py:358

commit v3 on v2

--- a/solution.py
+++ b/solution.py
@@ -3,6 +3,7 @@
 
 import jax
 import jax.numpy as jnp
+import numpy as np
 from jax import lax
 from jax.experimental import pallas as pl
 from jax.experimental.pallas import tpu as pltpu
@@ -85,28 +86,37 @@
     return jnp.where(wanted == iota((rows, rows), 1), 1.0, 0.0).astype(jnp.bfloat16)
 
 
-def rank_kernel(blocks, drafts, groups, *refs):
+def group_of():
+    return lax.axis_index("dp") * lax.axis_size("pipe") + lax.axis_index("pipe")
+
+
+def rank_kernel(sizes, owned, *refs):
+    groups, blocks, drafts = sizes
     pieces = refs[:blocks]
-    shrink_ref, place_ref, rows_ref, rank_ref, wide = refs[blocks:]
+    shrink_ref, slots_ref, rows_ref, rank_ref, wide = refs[blocks:]
     for block in range(blocks):
         for draft in range(drafts):
             start = (block * drafts + draft) * groups
             wide[start : start + groups, :] = pieces[block][draft].astype(jnp.float32)
     rows = wide[...].astype(jnp.bfloat16)
     rows_ref[...] = rows
-    rank_ref[...] = owned_ranks(rows, shrink_ref[...], place_ref[...], rank_ref.shape[1])
-
-
-def owned_ranks(rows, shrink, place, width):
+    place = slots_ref[:, 0:1] - lax.axis_index("tensor") * owned
+    ranks = owned_ranks(
+        rows, shrink_ref[...], place, shrink_ref.shape[0] // owned, rank_ref.shape[2]
+    )
+    for target in range(rank_ref.shape[0]):
+        rank_ref[target] = ranks
+
+
+def owned_ranks(rows, shrink, place, width, lanes):
     ranks = dot_nt(rows, shrink)
-    columns = iota(ranks.shape, 1)
-    kept = jnp.where(over(columns, width) == place, ranks, 0.0).astype(jnp.bfloat16)
-    fold = rest_of(iota((ranks.shape[1], width), 0), width) == iota((ranks.shape[1], width), 1)
+    kept = jnp.where(over(iota(ranks.shape, 1), width) == place, ranks, 0.0).astype(jnp.bfloat16)
+    fold = (ranks.shape[1], lanes)
+    fold = rest_of(iota(fold, 0), width) == iota(fold, 1)
     return dot(kept, jnp.where(fold, 1.0, 0.0).astype(jnp.bfloat16)).astype(jnp.bfloat16)
 
 
-def spread_ranks(ranks, place, width, owned):
-    parts = ranks.shape[1] // width
+def spread_ranks(ranks, place, width, owned, parts):
     span = owned * width
     row = iota((ranks.shape[1], parts * span), 0)
     column = iota((ranks.shape[1], parts * span), 1)
@@ -118,57 +128,64 @@
     return jnp.where(slot == place, wide, 0.0).astype(jnp.bfloat16)
 
 
-def stream_kernel(weights, chunks, rows_ref, *refs):
-    sources = refs[:weights]
-    total_ref, buffer, sems = refs[weights:]
-    depth = rows_ref.shape[1] // chunks
-
-    def copy(chunk, index):
-        part = pl.ds(chunk * depth, depth)
-        start = sum(source.shape[1] for source in sources[:index])
+def stream_kernel(first, chunks, depth, rows_ref, weight_ref, *refs):
+    *sums, total_ref, buffer, sems = refs
+
+    def copy(chunk):
         return pltpu.make_async_copy(
-            sources[index].at[part],
-            buffer.at[part, pl.ds(start, sources[index].shape[1])],
-            sems.at[chunk, index],
+            weight_ref.at[pl.ds(first + chunk * depth, depth)],
+            buffer.at[pl.ds(chunk * depth, depth)],
+            sems.at[chunk],
         )
 
     for chunk in range(chunks):
-        for index in range(weights):
-            copy(chunk, index).start()
+        copy(chunk).start()
     for chunk in range(chunks):
-        for index in range(weights):
-            copy(chunk, index).wait()
+        start = first + chunk * depth
+        copy(chunk).wait()
         product = dot(
-            rows_ref[:, chunk * depth : (chunk + 1) * depth],
-            buffer[chunk * depth : (chunk + 1) * depth, :],
+            rows_ref[:, start : start + depth], buffer[chunk * depth : (chunk + 1) * depth, :]
         )
-        if chunk == 0:
+        if chunk:
+            total_ref[...] += product
+        elif sums:
+            total_ref[...] = sums[0][...] + product
+        else:
             total_ref[...] = product
-        else:
-            total_ref[...] += product
-
-
-def stream(rows, weights, chunks):
-    width = sum(w.shape[1] for w in weights)
+
+
+def stream(rows, weight, chunks, first, size, *sums):
+    width = weight.shape[1]
     return call(
-        functools.partial(stream_kernel, len(weights), chunks),
+        functools.partial(stream_kernel, first, chunks, size // chunks),
         shape((rows.shape[0], width), jnp.float32),
-        [VMEM] + [HBM] * len(weights),
-        [
-            pltpu.VMEM((rows.shape[1], width), jnp.bfloat16),
-            pltpu.SemaphoreType.DMA((chunks, len(weights))),
-        ],
-        2 * rows.shape[0] * rows.shape[1] * width,
-        2 * rows.shape[1] * width,
+        [VMEM, HBM] + [VMEM] * len(sums),
+        [pltpu.VMEM((size, width), jnp.bfloat16), pltpu.SemaphoreType.DMA((chunks,))],
+        2 * rows.shape[0] * size * width,
+        2 * size * width,
         40 * MIB,
-    )(rows, *weights)
-
-
-def pack_kernel(blocks, keys_ref, values_ref, extra_ref, *refs):
+    )(rows, weight, *sums)
+
+
+def pack_kernel(sizes, ids_ref, pool_ref, length_ref, keys_ref, values_ref, turns_ref, *refs):
+    groups, blocks, drafts = sizes
     outs = refs[:blocks]
-    sems = refs[blocks]
-    size = keys_ref.shape[2]
+    slots_ref, extra_f32, extra_ref, sems = refs[blocks:]
+    size, head_size = keys_ref.shape[2:]
     me = lax.axis_index("tensor")
+    length = length_ref[0]
+    positions = (iota((drafts, head_size), 0) + length).astype(jnp.float32)
+    angles = positions * turns_ref[0:1, :]
+    extra_f32[...] = jnp.zeros(extra_f32.shape, jnp.float32)
+    for index, value in enumerate((jnp.cos(angles), jnp.sin(angles) * turns_ref[1:2, :])):
+        high = value.astype(jnp.bfloat16).astype(jnp.float32)
+        start = 2 * index * drafts
+        extra_f32[start : start + drafts, :] = high
+        extra_f32[start + drafts : start + 2 * drafts, :] = value - high
+    ones = jnp.ones((1, head_size), jnp.float32)
+    extra_f32[4 * drafts : 4 * drafts + 1, :] = ones * (length >> 4).astype(jnp.float32)
+    extra_f32[4 * drafts + 1 : 4 * drafts + 2, :] = ones * (length & 15).astype(jnp.float32)
+    extra_ref[...] = extra_f32[...].astype(jnp.bfloat16)
     copies = []
     for shift in range(blocks):
         head = lax.rem(me + shift, blocks)
@@ -187,46 +204,67 @@
         ]
     for copy in copies:
         copy.start()
+    index = iota(slots_ref.shape, 0)
+    column = iota(slots_ref.shape, 1)
+    near = parts_of(block_first, sizes, index)
+    far = parts_of(group_first, sizes, index)
+    row_group = jnp.where(column == 0, near[0], far[0])
+    row_block = jnp.where(column == 0, near[1], far[1])
+    place = row_block * groups + row_group
+    slots = jnp.zeros(slots_ref.shape, jnp.int32)
+    for block in range(blocks):
+        for group in range(groups):
+            row = lax.rem(me - block + blocks, blocks) * groups + group
+            slots = jnp.where(place == block * groups + group, pool_ref[ids_ref[row]], slots)
+    slots_ref[...] = slots
     for copy in copies:
         copy.wait()
 
 
-def pack(blocks, keys, values, extra):
-    rows = 2 * keys.shape[2] + extra.shape[0]
-    outs = [shape((rows, keys.shape[3]))] * blocks
+def pack(sizes, ids, pool, lengths, keys, values):
+    groups, blocks, drafts = sizes
+    head_size = keys.shape[3]
+    half = np.arange(head_size // 2)
+    frequency = (rope_base ** (-2.0 * half / head_size)).astype(np.float32)
+    signs = np.ones(half.size, np.float32)
+    turns = np.stack([np.tile(frequency, 2), np.concatenate([-signs, signs])])
+    used = -(-(4 * drafts + 2) // 16) * 16
+    outs = [shape((2 * keys.shape[2] + used, head_size))] * blocks
+    smem = pl.BlockSpec(memory_space=pltpu.SMEM)
     return pl.pallas_call(
-        functools.partial(pack_kernel, blocks),
-        out_shape=outs,
-        in_specs=[HBM, HBM, VMEM],
-        out_specs=[HBM] * blocks,
-        scratch_shapes=[pltpu.SemaphoreType.DMA((blocks, 3))],
+        functools.partial(pack_kernel, sizes),
+        out_shape=outs + [shape((groups * blocks * drafts, 128), jnp.int32)],
+        in_specs=[smem, smem, smem, VMEM, VMEM, VMEM],
+        out_specs=[HBM] * blocks + [VMEM],
+        scratch_shapes=[
+            pltpu.VMEM((used, head_size), jnp.float32),
+            pltpu.VMEM((used, head_size), jnp.bfloat16),
+            pltpu.SemaphoreType.DMA((blocks, 3)),
+        ],
         cost_estimate=pl.CostEstimate(flops=0, bytes_accessed=8 * keys.size, transcendentals=0),
         compiler_params=pltpu.CompilerParams(vmem_limit_bytes=24 * MIB),
-    )(keys, values, extra)
-
-
-def grow_kernel(blocks, drafts, groups, width, *refs):
-    total_ref, place_ref, turn_ref, *rest = refs
-    ranks_in = rest[:blocks]
-    grows = rest[blocks : blocks + 3]
-    outs = rest[blocks + 3 :]
-    sizes = (groups, blocks, drafts)
-    ranks = ranks_in[0][...].astype(jnp.float32)
-    for other in ranks_in[1:]:
-        ranks = ranks + other[...].astype(jnp.float32)
-    ranks = dot(
-        reorder(sizes, block_first, block_first, turn_ref[0]), ranks.astype(jnp.bfloat16)
-    )
-    wide = spread_ranks(
-        ranks.astype(jnp.bfloat16), place_ref[...], width, grows[0].shape[0] // width
-    )
-    by_group = reorder(sizes, group_first, block_first, 0, turn_ref[1])
+    )(ids, pool, lengths, keys, values, jnp.asarray(turns))
+
+
+def grow_kernel(sizes, width, total_ref, rows_ref, key_ref, value_ref, slots_ref, ranks_ref, *rest):
+    groups, blocks, drafts = sizes
+    grows = rest[:3]
+    outs = rest[3:]
+    group = group_of()
+    owned = grows[0].shape[0] // width
+    ranks = ranks_ref[group * groups].astype(jnp.float32)
+    for other in range(1, groups):
+        ranks = ranks + ranks_ref[group * groups + other].astype(jnp.float32)
+    turn = rest_of(group - lax.axis_index("tensor") + blocks, blocks)
+    ranks = dot(reorder(sizes, block_first, block_first, turn), ranks.astype(jnp.bfloat16))
+    place = slots_ref[:, 0:1] - group * owned
+    wide = spread_ranks(ranks.astype(jnp.bfloat16), place, width, owned, len(grows))
+    by_group = reorder(sizes, group_first, block_first, 0, group)
     start = 0
     for index, grow in enumerate(grows):
         deep, cols = grow.shape
-        full = total_ref[:, start : start + cols] + dot(
-            wide[:, index * deep : (index + 1) * deep], grow[...]
-        )
+        base = total_ref[...] if index == 0 else dot(rows_ref[...], (key_ref, value_ref)[index - 1][...])
+        full = base + dot(wide[:, index * deep : (index + 1) * deep], grow[...])
         full = dot(by_group, full.astype(jnp.bfloat16)).astype(jnp.bfloat16)
         for step in range(groups):
             for block in range(blocks):
@@ -289,39 +327,39 @@
     mixed_ref[...] = out_s[...].astype(jnp.bfloat16)
 
 
-def out_rank_kernel(span, got_ref, shrink_ref, place_ref, rows_ref, rank_ref, wide):
+def out_rank_kernel(owned, got_ref, shrink_ref, slots_ref, rows_ref, rank_ref, wide):
+    span = got_ref.shape[1]
     for group in range(got_ref.shape[0]):
         wide[group * span : (group + 1) * span, :] = got_ref[group].astype(jnp.float32)
     rows = wide[...].astype(jnp.bfloat16)
     rows_ref[...] = rows
-    rank_ref[...] = owned_ranks(rows, shrink_ref[...], place_ref[...], rank_ref.shape[1])
-
-
-def out_grow_kernel(blocks, drafts, groups, *refs):
-    total_ref, place_ref, turn_ref, *rest = refs
-    ranks_in = rest[:blocks]
-    grow_ref = rest[blocks]
-    outs = rest[blocks + 1 :]
-    sizes = (groups, blocks, drafts)
-    width = ranks_in[0].shape[1]
+    place = slots_ref[:, 1:2] - group_of() * owned
+    ranks = owned_ranks(
+        rows, shrink_ref[...], place, shrink_ref.shape[0] // owned, rank_ref.shape[2]
+    )
+    for target in range(rank_ref.shape[0]):
+        rank_ref[target] = ranks
+
+
+def out_grow_kernel(sizes, width, total_ref, slots_ref, ranks_ref, grow_ref, *outs):
+    groups, blocks, drafts = sizes
+    owned = grow_ref.shape[0] // width
+    me = lax.axis_index("tensor")
     ranks = None
-    for index, part in enumerate(ranks_in):
-        moved = dot(reorder(sizes, group_first, group_first, turn_ref[index]), part[...])
+    for source in range(blocks):
+        turn = rest_of(source - me + blocks, blocks)
+        moved = dot(
+            reorder(sizes, group_first, group_first, turn), ranks_ref[source * groups + me]
+        )
         ranks = moved if ranks is None else ranks + moved
-    wide = spread_ranks(
-        ranks.astype(jnp.bfloat16), place_ref[...], width, grow_ref.shape[0] // width
-    )
+    place = slots_ref[:, 1:2] - me * owned
+    wide = spread_ranks(ranks.astype(jnp.bfloat16), place, width, owned, 1)
     full = (total_ref[...] + dot(wide, grow_ref[...])).astype(jnp.bfloat16)
     full = dot(reorder(sizes, block_first, group_first, 0), full).astype(jnp.bfloat16)
     for block in range(blocks):
         for draft in range(drafts):
             start = (block * drafts + draft) * groups
             outs[block][draft] = full[start : start + groups]
-
-
-def halves(value):
-    high = value.astype(jnp.bfloat16)
-    return high, (value - high.astype(jnp.float32)).astype(jnp.bfloat16)
 
 
 def by_head(
@@ -344,14 +382,14 @@
 ):
     blocks = lax.axis_size("tensor")
     groups = lax.axis_size(GROUP)
-    tensor_index = lax.axis_index("tensor")
-    group_index = lax.axis_index(GROUP)
     _, drafts, features = tokens.shape
+    sizes = (groups, blocks, drafts)
     owned = shrink_qkv.shape[0]
     width = grow_out.shape[1]
     cache_size, head_size = cache_keys.shape[2:]
     span = blocks * drafts
     count = groups * span
+    lanes = -(-shrink_qkv.shape[2] // 128) * 128
 
     def over_tensor(value, shift):
         route = [(t, (t + shift) % blocks) for t in range(blocks)]
@@ -361,94 +399,49 @@
         route = [(g, (g + shift) % groups) for g in range(groups)]
         return lax.ppermute(value, GROUP, route)
 
-    def to_growers(value, shift):
-        route = [
-            (t * groups + g, ((g + shift) % blocks) * groups + t)
-            for t in range(blocks)
-            for g in range(groups)
-        ]
-        return lax.ppermute(value, EVERY, route)
-
-    def to_out_growers(value, shift):
-        route = [
-            (t * groups + g, g * groups + (t + shift) % groups)
-            for t in range(blocks)
-            for g in range(groups)
-        ]
-        return lax.ppermute(value, EVERY, route)
+    def exchange(value):
+        return lax.all_to_all(value, EVERY, split_axis=0, concat_axis=0, tiled=True)
 
     mine = jnp.transpose(tokens, (1, 0, 2))
     pieces = [mine] + [over_tensor(mine, shift) for shift in range(1, blocks)]
 
-    length = cache_lengths[0]
-    positions = (length + jnp.arange(drafts, dtype=jnp.int32)).astype(jnp.float32)
-    half_size = head_size // 2
-    frequency = rope_base ** (-2.0 * jnp.arange(half_size, dtype=jnp.float32) / head_size)
-    angles = positions[:, None] * frequency
-    cosine = jnp.cos(angles)
-    sine = jnp.sin(angles)
-    cos_high, cos_low = halves(jnp.concatenate([cosine, cosine], 1))
-    sin_high, sin_low = halves(jnp.concatenate([-sine, sine], 1))
-    spell = jnp.stack([length // 16, length % 16]).astype(jnp.bfloat16)
-    used = 4 * drafts + 2
-    extra = jnp.concatenate(
-        [
-            cos_high,
-            cos_low,
-            sin_high,
-            sin_low,
-            jnp.broadcast_to(spell[:, None], (2, head_size)),
-            jnp.zeros((-used % 16, head_size), jnp.bfloat16),
-        ],
-        0,
-    )
-
-    messages = pack(blocks, cache_keys, cache_values, extra)
-    caches = [messages[0]] + [over_tensor(messages[shift], shift) for shift in range(1, blocks)]
-
-    matches = adapter_ids[:, None] == jnp.arange(adapter_slots.shape[0], dtype=jnp.int32)[None, :]
-    row_slots = jnp.sum(jnp.where(matches, adapter_slots[None, :], 0), axis=1)
-    turned = (tensor_index - jnp.arange(blocks, dtype=jnp.int32)) % blocks
-    places = turned[None, :] * groups + jnp.arange(groups, dtype=jnp.int32)[:, None]
-    slots = jnp.sum(
-        jnp.where(
-            places[:, :, None] == jnp.arange(blocks * groups, dtype=jnp.int32), row_slots, 0
-        ),
-        -1,
-    )
-    group_slots = jnp.broadcast_to(slots[:, :, None], (groups, blocks, drafts)).reshape(count, 1)
-    block_slots = jnp.broadcast_to(slots.T[:, None, :], (blocks, drafts, groups)).reshape(count, 1)
-    first_width = block_slots - tensor_index * owned
-    first_column = block_slots - group_index * owned
-    last_width = group_slots - tensor_index * owned
-    last_column = group_slots - group_index * owned
+    *messages, slots = pack(
+        sizes, adapter_ids, adapter_slots, cache_lengths, cache_keys, cache_values
+    )
+    caches = {shift: over_tensor(messages[shift], shift) for shift in range(1, blocks) if shift != 2}
 
     shrink_in = jnp.transpose(shrink_qkv, (0, 2, 1)).reshape(-1, features)
     rows, rank_part = call(
-        functools.partial(rank_kernel, blocks, drafts, groups),
-        [shape((count, features)), shape((count, shrink_qkv.shape[2]))],
+        functools.partial(rank_kernel, sizes, owned),
+        [shape((count, features)), shape((blocks * groups, count, lanes))],
         [VMEM] * (blocks + 2),
         [pltpu.VMEM((count, features), jnp.float32)],
         2 * count * shrink_qkv.size,
         2 * shrink_qkv.size + 4 * count * features,
-    )(*pieces, shrink_in, first_width)
-    ranks = [to_growers(rank_part, shift) for shift in range(blocks)]
-    weights_in = (w_query, w_key, w_value)
-    total = stream(rows, weights_in, 8)
-    cols = total.shape[1]
-    turn = jnp.stack([(group_index - tensor_index) % blocks, group_index]).astype(jnp.int32)
+    )(*pieces, shrink_in, slots)
+    ranks = exchange(rank_part)
+    half = features // 2
+    total = stream(rows, w_query, 4, 0, half)
+    total, *late = lax.optimization_barrier((total, *messages[2:3]))
+    for message in late:
+        caches[2] = over_tensor(message, 2)
+    total = stream(rows, w_query, 4, half, features - half, total)
+    caches = [messages[0]] + [caches[shift] for shift in range(1, blocks)]
+    cols = total.shape[1] + w_key.shape[1] + w_value.shape[1]
     sent = call(
-        functools.partial(grow_kernel, blocks, drafts, groups, width),
+        functools.partial(grow_kernel, sizes, width),
         [shape((blocks, drafts, cols))] * groups,
-        [VMEM, VMEM, pl.BlockSpec(memory_space=pltpu.SMEM)] + [VMEM] * (blocks + 3),
+        [VMEM] * 9,
         [],
         2 * count * owned * width * cols,
         8 * count * cols + 2 * owned * width * cols,
     )(
         total,
-        first_column,
-        turn,
-        *ranks,
+        rows,
+        w_key,
+        w_value,
+        slots,
+        ranks,
         *[grow.reshape(owned * width, -1) for grow in (grow_query, grow_key, grow_value)],
     )
     parts = [sent[0]] + [over_group(sent[shift], shift) for shift in range(1, groups)]
@@ -467,27 +460,24 @@
     )(*parts, *caches)
     gathered = lax.all_gather(mixed, GROUP, axis=0, tiled=False)
     out_rows, out_part = call(
-        functools.partial(out_rank_kernel, span),
-        [shape((count, head_cols)), shape((count, width))],
+        functools.partial(out_rank_kernel, owned),
+        [shape((count, head_cols)), shape((blocks * groups, count, lanes))],
         [VMEM] * 3,
         [pltpu.VMEM((count, head_cols), jnp.float32)],
         2 * count * shrink_out.size,
         2 * shrink_out.size + 4 * count * head_cols,
-    )(gathered, jnp.transpose(shrink_out, (0, 2, 1)).reshape(-1, head_cols), last_column)
-    out_ranks = [to_out_growers(out_part, shift) for shift in range(groups)]
-    out_total = stream(out_rows, (w_out,), 8)
+    )(gathered, jnp.transpose(shrink_out, (0, 2, 1)).reshape(-1, head_cols), slots)
+    out_ranks = exchange(out_part)
+    out_total = stream(out_rows, w_out, 8, 0, head_cols)
     out_cols = out_total.shape[1]
-    out_turn = (
-        (group_index - tensor_index - jnp.arange(groups, dtype=jnp.int32)) % blocks
-    ).astype(jnp.int32)
     leaving = call(
-        functools.partial(out_grow_kernel, blocks, drafts, groups),
+        functools.partial(out_grow_kernel, sizes, width),
         [shape((drafts, groups, out_cols))] * blocks,
-        [VMEM, VMEM, pl.BlockSpec(memory_space=pltpu.SMEM)] + [VMEM] * (groups + 1),
+        [VMEM] * 4,
         [],
         2 * count * owned * width * out_cols,
         8 * count * out_cols + 2 * owned * width * out_cols,
-    )(out_total, last_width, out_turn, *out_ranks, grow_out.reshape(owned * width, -1))
+    )(out_total, slots, out_ranks, grow_out.reshape(owned * width, -1))
     result = leaving[0].astype(jnp.float32)
     for shift in range(1, blocks):
         result = result + over_tensor(leaving[shift], -shift).astype(jnp.float32)

time: 94.4 us -> 91 us (0.964)
  starting transfers between devices: 39.5 us -> 25.1 us
  waiting for transfers between devices: 10.7 us -> 24.7 us
  Pallas kernels: 21.8 us -> 24.3 us
  local copies, waits for them, and re-layouts: 11.3 us -> 8.95 us
  other arithmetic: 2.82 us -> 0.75 us
  blocking collectives: 6.84 us -> 5.79 us
    ppermute x8 -> x0, starting transfers between devices: 22.7 us -> none  [the longest x4 14.4 us: to_growers(): return lax.ppermute(value, EVERY, route)]
    ppermute x9, waiting for transfers between devices: 8.73 us -> 22.1 us  [over_tensor(): return lax.ppermute(value, 'tensor', route)]
    all_to_all x0 -> x2, starting transfers between devices: none -> 8.32 us  [exchange(): return lax.all_to_all(value, EVERY, split_axis=0, concat_axis=0, tiled=True)]
    all_to_all x0 -> x2, waiting for transfers between devices: none -> 2.58 us  [exchange(): return lax.all_to_all(value, EVERY, split_axis=0, concat_axis=0, tiled=True)]
    ppermute x3, waiting for transfers between devices: 1.97 us -> 0.01 us  [over_group(): return lax.ppermute(value, GROUP, route)]
    pallas_call x7 -> x8, Pallas kernels: 20 us -> 21.4 us  [the longest x3 14.5 us: stream(): call(functools.partial(stream_kernel, first, chunks, size // chunks), sha...]
    sub x6 -> x0, local copies, waits for them, and re-layouts: 1.12 us -> none  [the longest x2 0.78 us: by_head(): first_column = block_slots - group_index * owned]
    pallas_call x1, Pallas kernels: 1.79 us -> 2.9 us  [by_head(): call(functools.partial(attend_kernel, blocks, drafts, groups, cache_size)...]
  transfers between devices with their start and end apart: 20 -> 14, of which waited for: 5 -> 5; matrix products, arithmetic and copies ran while one was open for 5% -> 0% of each run, Pallas kernels for 20% -> 20%
where the time goes in v3:
time: 91 us; the launch traced here: 90.4 us
  starting transfers between devices  25.1 us (28%)
  waiting for transfers between devices  24.7 us (27%)
  Pallas kernels  24.3 us (27%)
  local copies, waits for them, and re-layouts  8.95 us (10%)
  blocking collectives  5.79 us (6%)
    ppermute x9, waiting for transfers between devices, over_tensor(): return lax.ppermute(value, 'tensor', route)  22.1 us
    pallas_call x3, Pallas kernels, stream(): call(functools.partial(stream_kernel, first, chunks, size // chunks), sha...  14.5 us
    ppermute x9, starting transfers between devices, over_tensor(): return lax.ppermute(value, 'tensor', route)  13.8 us
    unnamed x28, local copies, waits for them, and re-layouts  8.95 us
    all_to_all x2, starting transfers between devices, exchange(): return lax.all_to_all(value, EVERY, split_axis=0, concat_axis=0, tiled=True)  8.32 us
    all_gather x1, blocking collectives, by_head(): gathered = lax.all_gather(mixed, GROUP, axis=0, tiled=False)  5.79 us
    ppermute x3, starting transfers between devices, over_group(): return lax.ppermute(value, GROUP, route)  2.97 us
    pallas_call x1, Pallas kernels, by_head(): call(functools.partial(attend_kernel, blocks, drafts, groups, cache_size)...  2.9 us
  transfers between devices with their start and end apart: 14, of which 5 were waited for; matrix products, arithmetic and copies ran while one was open for 0% of the time, Pallas kernels for 20%

profile of v3, /device:TPU:0, one launch (start us, length us, event | category | flops | bytes accessed | tf_op | source)
XLA Modules:
  0.0 90.4 jit_solution(12137952091907252905)
XLA Ops:
  0.0 5.0 %collective-permute-start.2 = (bf16[3,4,4096]{2,1,0:T(4,128)(2,1)}, bf16[3,4,4096]{2,1,0:T(4,128)(2,1)S(1)}, u32[]{:S(2)}, u32[]{:S(2)}) collective-permute-start(bf16[3,4,4096]{2,1,0:T(4,128)(2,1)} %bitcast.19), channel_id=1, source_target_pairs={{0,12},{4,0},{8,4},{12,8},{1,13},{5,1},{9,5},{13,9},{2,14},{6,2},{... | collective-permute-start | bytes 294920 | tf_op jit(solution)/shard_map/ppermute | solution.py:396
  5.0 0.0 collective-permute-start.1
  5.1 1.0 %collective-permute-start = (bf16[3,4,4096]{2,1,0:T(4,128)(2,1)}, bf16[3,4,4096]{2,1,0:T(4,128)(2,1)S(1)}, u32[]{:S(2)}, u32[]{:S(2)}) collective-permute-start(bf16[3,4,4096]{2,1,0:T(4,128)(2,1)} %bitcast.21), channel_id=1, source_target_pairs={{0,4},{4,8},{8,12},{12,0},{1,5},{5,9},{9,13},{13,1},{2,6},{6,10},{... | collective-permute-start | bytes 294920 | tf_op jit(solution)/shard_map/ppermute | solution.py:396
  6.7 1.0 %copy-done.6 = bf16[1,4,512,128]{3,2,1,0:T(8,128)(2,1)S(1)} copy-done((bf16[1,4,512,128]{3,2,1,0:T(8,128)(2,1)S(1)}, bf16[1,4,512,128]{3,2,1,0:T(8,128)(2,1)}, u32[]{:S(2)}) %copy-start.6) | copy-done | bytes 524312
  7.8 1.0 %copy-done.7 = bf16[1,4,512,128]{3,2,1,0:T(8,128)(2,1)S(1)} copy-done((bf16[1,4,512,128]{3,2,1,0:T(8,128)(2,1)S(1)}, bf16[1,4,512,128]{3,2,1,0:T(8,128)(2,1)}, u32[]{:S(2)}) %copy-start.7) | copy-done | bytes 524312
  8.8 0.7 copy-done.11
  9.5 0.7 copy-done.12
  10.1 0.7 copy-done.13
  10.8 1.9 %shard_map.163 = (bf16[1040,128]{1,0:T(8,128)(2,1)S(1)}, bf16[1040,128]{1,0:T(8,128)(2,1)}, bf16[1040,128]{1,0:T(8,128)(2,1)}, bf16[1040,128]{1,0:T(8,128)(2,1)}, s32[48,128]{1,0:T(8,128)S(1)}) custom-call(s32[16]{0:T(128)S(1)} %copy-done.12, s32[16]{0:T(128)S(1)} %copy-done.13, s32[1]{0:T(128)S(6)} %copy.18.length_ref, ...), custom_call_target="tpu_custom_call" | custom-call | bytes 2097152 | tf_op jit(solution)/shard_map/pallas_call | solution.py:234
  12.7 0.0 collective-permute-done.2.refs_3_
  12.8 1.3 %collective-permute-done.1.refs_2_ = bf16[3,4,4096]{2,1,0:T(4,128)(2,1)S(1)} collective-permute-done((bf16[3,4,4096]{2,1,0:T(4,128)(2,1)}, bf16[3,4,4096]{2,1,0:T(4,128)(2,1)S(1)}, u32[]{:S(2)}, u32[]{:S(2)}) %collective-permute-start.1) | collective-permute-done | bytes 98336 | tf_op jit(solution)/shard_map/ppermute | solution.py:396
  14.0 0.0 collective-permute-done.refs_1_
  14.0 1.9 %copy-done = bf16[4,4096,96]{1,2,0:T(8,128)(2,1)S(1)} copy-done((bf16[4,4096,96]{1,2,0:T(8,128)(2,1)S(1)}, bf16[4,4096,96]{1,2,0:T(8,128)(2,1)}, u32[]{:S(2)}) %copy-start) | copy-done | bytes 3145752
  15.9 0.9 copy-done.8
  16.8 1.9 %shard_map.164 = (bf16[48,4096]{1,0:T(8,128)(2,1)S(1)}, bf16[16,48,128]{2,1,0:T(8,128)(2,1)}) custom-call(bf16[3,4,4096]{2,1,0:T(4,128)(2,1)S(1)} %bitcast.22, bf16[3,4,4096]{2,1,0:T(4,128)(2,1)S(1)} %collective-permute-done.refs_1_, bf16[3,4,4096]{2,1,0:T(4,128)(2,1)S(1)} %collective-permute-done.1.refs_2_, ...), custom_call_target="tpu_custom_call" | custom-call | flops 150994944 | bytes 3932160 | tf_op jit(solution)/shard_map/pallas_call | solution.py:414
  18.7 4.6 %all-to-all-start = ((bf16[16,48,128]{2,1,0:T(8,128)(2,1)}), bf16[16,48,128]{2,1,0:T(8,128)(2,1)S(1)}, u32[]{:S(2)}, u32[]{:S(2)}) async-start(bf16[16,48,128]{2,1,0:T(8,128)(2,1)} %get-tuple-element.28), calls=%async_computation | async-start | bytes 393216 | tf_op jit(solution)/shard_map/all_to_all | solution.py:403
  23.3 1.9 %collective-permute-start.6 = (bf16[1040,128]{1,0:T(8,128)(2,1)}, bf16[1040,128]{1,0:T(8,128)(2,1)}, u32[]{:S(2)}, u32[]{:S(2)}) collective-permute-start(bf16[1040,128]{1,0:T(8,128)(2,1)} %get-tuple-element.34), channel_id=1, source_target_pairs={{0,4},{4,8},{8,12},{12,0},{1,5},{5,9},{9,13},{13,1},{2,6},{6,10},{... | collective-permute-start | bytes 798728 | tf_op jit(solution)/shard_map/ppermute | solution.py:396
  25.3 2.0 %collective-permute-start.8 = (bf16[1040,128]{1,0:T(8,128)(2,1)}, bf16[1040,128]{1,0:T(8,128)(2,1)}, u32[]{:S(2)}, u32[]{:S(2)}) collective-permute-start(bf16[1040,128]{1,0:T(8,128)(2,1)} %get-tuple-element.36), channel_id=1, source_target_pairs={{0,12},{4,0},{8,4},{12,8},{1,13},{5,1},{9,5},{13,9},{2,14},{6,2},{... | collective-permute-start | bytes 798728 | tf_op jit(solution)/shard_map/ppermute | solution.py:396
  27.2 4.1 %shard_map.165.refs_0_ = f32[48,2048]{1,0:T(8,128)S(1)} custom-call(bf16[48,4096]{1,0:T(8,128)(2,1)S(1)} %get-tuple-element.25.rows_ref, bf16[4096,2048]{1,0:T(8,128)(2,1)} %weight_ref.4), custom_call_target="tpu_custom_call" | custom-call | flops 402653184 | bytes 8388608 | tf_op jit(solution)/shard_map/pallas_call | solution.py:159
  31.4 1.0 %collective-permute-start.7 = (bf16[1040,128]{1,0:T(8,128)(2,1)}, bf16[1040,128]{1,0:T(8,128)(2,1)}, u32[]{:S(2)}, u32[]{:S(2)}) collective-permute-start(bf16[1040,128]{1,0:T(8,128)(2,1)} %get-tuple-element.35), channel_id=1, source_target_pairs={{0,8},{4,12},{8,0},{12,4},{1,9},{5,13},{9,1},{13,5},{2,10},{6,14},... | collective-permute-start | bytes 798728 | tf_op jit(solution)/shard_map/ppermute | solution.py:396
  32.4 4.0 %shard_map.166.total_ref = f32[48,2048]{1,0:T(8,128)S(1)} custom-call(bf16[48,4096]{1,0:T(8,128)(2,1)S(1)} %get-tuple-element.25.rows_ref, bf16[4096,2048]{1,0:T(8,128)(2,1)} %weight_ref.4, f32[48,2048]{1,0:T(8,128)S(1)} %shard_map.165.refs_0_), custom_call_target="tpu_custom_call" | custom-call | flops 402653184 | bytes 8388608 | tf_op jit(solution)/shard_map/pallas_call | solution.py:159
  36.4 0.0 all-to-all-done.ranks_ref
  36.4 0.0 copy-start.4
  36.4 1.0 %copy-done.4 = bf16[4,32,2048]{2,1,0:T(8,128)(2,1)S(1)} copy-done((bf16[4,32,2048]{2,1,0:T(8,128)(2,1)S(1)}, bf16[4,32,2048]{2,1,0:T(8,128)(2,1)}, u32[]{:S(2)}) %copy-start.4) | copy-done | bytes 524312
  37.5 1.2 %shard_map.167 = (bf16[4,3,2304]{2,1,0:T(4,128)(2,1)S(1)}, bf16[4,3,2304]{2,1,0:T(4,128)(2,1)S(1)}, bf16[4,3,2304]{2,1,0:T(4,128)(2,1)S(1)}, bf16[4,3,2304]{2,1,0:T(4,128)(2,1)S(1)}) custom-call(f32[48,2048]{1,0:T(8,128)S(1)} %shard_map.166.total_ref, bf16[48,4096]{1,0:T(8,128)(2,1)S(1)} %get-tuple-element.25.rows_ref, bf16[4096,128]{1,0:T(8,128)(2,1)S(1)} %copy-done.1, ...), custom_call_target="tpu_custom_call" | custom-call | flops 28311552 | bytes 1474560 | tf_op jit(solution)/shard_map/pallas_call | solution.py:431
  38.7 0.0 copy-start.3
  38.7 0.1 collective-permute-start.3
  38.8 2.1 %collective-permute-start.4 = (bf16[4,3,2304]{2,1,0:T(4,128)(2,1)S(1)}, bf16[4,3,2304]{2,1,0:T(4,128)(2,1)S(1)}, u32[]{:S(2)}, u32[]{:S(2)}) collective-permute-start(bf16[4,3,2304]{2,1,0:T(4,128)(2,1)S(1)} %get-tuple-element.31), channel_id=1, source_target_pairs={{0,2},{1,3},{2,0},{3,1},{4,6},{5,7},{6,4},{7,5},{8,10},{9,11},{10,... | collective-permute-start | bytes 165896 | tf_op jit(solution)/shard_map/ppermute | solution.py:400
  40.9 0.0 collective-permute-done.6.refs_5_
  40.9 0.8 collective-permute-start.5
  41.7 0.0 collective-permute-done.8.refs_7_
  41.7 12.8 %collective-permute-done.7.refs_6_ = bf16[1040,128]{1,0:T(8,128)(2,1)} collective-permute-done((bf16[1040,128]{1,0:T(8,128)(2,1)}, bf16[1040,128]{1,0:T(8,128)(2,1)}, u32[]{:S(2)}, u32[]{:S(2)}) %collective-permute-start.7) | collective-permute-done | bytes 266272 | tf_op jit(solution)/shard_map/ppermute | solution.py:396
  54.5 0.0 collective-permute-done.3.refs_1_
  54.5 0.0 collective-permute-done.4.refs_2_
  54.5 0.0 collective-permute-done.5.refs_3_
  54.5 2.9 %shard_map.168 = bf16[12,2048]{1,0:T(8,128)(2,1)S(1)} custom-call(bf16[4,3,2304]{2,1,0:T(4,128)(2,1)S(1)} %get-tuple-element.29.refs_0_, bf16[4,3,2304]{2,1,0:T(4,128)(2,1)S(1)} %collective-permute-done.3.refs_1_, bf16[4,3,2304]{2,1,0:T(4,128)(2,1)S(1)} %collective-permute-done.4.refs_2_, bf16[4,3,2304]{2,1,0:T(4,128)(2,1)S(1)} %collective-permute-done.5.refs_3_, ...), custom_call_target="tpu_custom_call" | custom-call | flops 50331648 | bytes 1048576 | tf_op jit(solution)/shard_map/pallas_call | solution.py:449
  57.4 5.8 %all-gather.1.got_ref = bf16[4,12,2048]{2,1,0:T(8,128)(2,1)S(1)} all-gather(bf16[1,12,2048]{2,1,0:T(8,128)(2,1)S(1)} %bitcast.18), channel_id=2, replica_groups=mesh['parts'=2,'tensor'=4,'dp'=2,'pipe'=2] {'dp','pipe'}, dimensions={0}, use_global_device_ids=true | all-gather | bytes 245760 | tf_op jit(solution)/shard_map/all_gather | solution.py:461
  63.2 1.0 %copy-done.5 = bf16[4,2048,32]{1,2,0:T(8,128)(2,1)S(1)} copy-done((bf16[4,2048,32]{1,2,0:T(8,128)(2,1)S(1)}, bf16[4,2048,32]{1,2,0:T(8,128)(2,1)}, u32[]{:S(2)}) %copy-start.5) | copy-done | bytes 524312
  64.3 1.1 %shard_map.169 = (bf16[48,2048]{1,0:T(8,128)(2,1)S(1)}, bf16[16,48,128]{2,1,0:T(8,128)(2,1)}) custom-call(bf16[4,12,2048]{2,1,0:T(8,128)(2,1)S(1)} %all-gather.1.got_ref, bf16[128,2048]{1,0:T(8,128)(2,1)S(1)} %bitcast.17, s32[48,128]{1,0:T(8,128)S(1)} %get-tuple-element.24.refs_5_.slots_ref), custom_call_target="tpu_custom_call" | custom-call | flops 25165824 | bytes 917504 | tf_op jit(solution)/shard_map/pallas_call | solution.py:462
  65.4 3.7 %all-to-all-start.1 = ((bf16[16,48,128]{2,1,0:T(8,128)(2,1)}), bf16[16,48,128]{2,1,0:T(8,128)(2,1)S(1)}, u32[]{:S(2)}, u32[]{:S(2)}) async-start(bf16[16,48,128]{2,1,0:T(8,128)(2,1)} %get-tuple-element.38), calls=%async_computation.1 | async-start | bytes 393216 | tf_op jit(solution)/shard_map/all_to_all | solution.py:403
  69.1 6.4 %shard_map.170.total_ref = f32[48,4096]{1,0:T(8,128)S(1)} custom-call(bf16[48,2048]{1,0:T(8,128)(2,1)S(1)} %get-tuple-element.37.rows_ref, bf16[2048,4096]{1,0:T(8,128)(2,1)} %weight_ref.5), custom_call_target="tpu_custom_call" | custom-call | flops 805306368 | bytes 16777216 | tf_op jit(solution)/shard_map/pallas_call | solution.py:159
  75.5 2.6 %all-to-all-done.1.ranks_ref = bf16[16,48,128]{2,1,0:T(8,128)(2,1)S(1)} async-done(((bf16[16,48,128]{2,1,0:T(8,128)(2,1)}), bf16[16,48,128]{2,1,0:T(8,128)(2,1)S(1)}, u32[]{:S(2)}, u32[]{:S(2)}) %all-to-all-start.1) | async-done | bytes 196640 | tf_op jit(solution)/shard_map/all_to_all | solution.py:403
  78.1 0.7 shard_map.171
  78.8 1.2 %collective-permute-start.9 = (bf16[3,4,4096]{2,1,0:T(4,128)(2,1)S(1)}, bf16[3,4,4096]{2,1,0:T(4,128)(2,1)S(1)}, u32[]{:S(2)}, u32[]{:S(2)}) collective-permute-start(bf16[3,4,4096]{2,1,0:T(4,128)(2,1)S(1)} %get-tuple-element.40), channel_id=1, source_target_pairs={{0,12},{4,0},{8,4},{12,8},{1,13},{5,1},{9,5},{13,9},{2,14},{6,2},{... | collective-permute-start | bytes 294920 | tf_op jit(solution)/shard_map/ppermute | solution.py:396
  80.0 1.6 %collective-permute-start.11 = (bf16[3,4,4096]{2,1,0:T(4,128)(2,1)S(1)}, bf16[3,4,4096]{2,1,0:T(4,128)(2,1)S(1)}, u32[]{:S(2)}, u32[]{:S(2)}) collective-permute-start(bf16[3,4,4096]{2,1,0:T(4,128)(2,1)S(1)} %get-tuple-element.42), channel_id=1, source_target_pairs={{0,4},{4,8},{8,12},{12,0},{1,5},{5,9},{9,13},{13,1},{2,6},{6,10},{... | collective-permute-start | bytes 294920 | tf_op jit(solution)/shard_map/ppermute | solution.py:396
  81.6 1.9 %collective-permute-done.9 = bf16[3,4,4096]{2,1,0:T(4,128)(2,1)S(1)} collective-permute-done((bf16[3,4,4096]{2,1,0:T(4,128)(2,1)S(1)}, bf16[3,4,4096]{2,1,0:T(4,128)(2,1)S(1)}, u32[]{:S(2)}, u32[]{:S(2)}) %collective-permute-start.9) | collective-permute-done | bytes 98336 | tf_op jit(solution)/shard_map/ppermute | solution.py:396
  83.5 6.1 %collective-permute-done.10 = bf16[3,4,4096]{2,1,0:T(4,128)(2,1)S(1)} collective-permute-done((bf16[3,4,4096]{2,1,0:T(4,128)(2,1)S(1)}, bf16[3,4,4096]{2,1,0:T(4,128)(2,1)S(1)}, u32[]{:S(2)}, u32[]{:S(2)}) %collective-permute-start.10) | collective-permute-done | bytes 98336 | tf_op jit(solution)/shard_map/ppermute | solution.py:396
  89.7 0.7 fusion
  (19 shorter events, 0.0 us)
Async XLA Ops:
  0.0 12.7 %collective-permute-start.2 = (bf16[3,4,4096]{2,1,0:T(4,128)(2,1)}, bf16[3,4,4096]{2,1,0:T(4,128)(2,1)S(1)}, u32[]{:S(2)}, u32[]{:S(2)}) collective-permute-start(bf16[3,4,4096]{2,1,0:T(4,128)(2,1)} %bitcast.19), channel_id=1, source_target_pairs={{0,12},{4,0},{8,4},{12,8},{1,13},{5,1},{9,5},{13,9},{2,14},{6,2},{... | collective-permute-start | bytes 294920 | tf_op jit(solution)/shard_map/ppermute | solution.py:396
  5.0 9.0 %collective-permute-start.1 = (bf16[3,4,4096]{2,1,0:T(4,128)(2,1)}, bf16[3,4,4096]{2,1,0:T(4,128)(2,1)S(1)}, u32[]{:S(2)}, u32[]{:S(2)}) collective-permute-start(bf16[3,4,4096]{2,1,0:T(4,128)(2,1)} %bitcast.20), channel_id=1, source_target_pairs={{0,8},{4,12},{8,0},{12,4},{1,9},{5,13},{9,1},{13,5},{2,10},{6,14},... | collective-permute-start | bytes 294920 | tf_op jit(solution)/shard_map/ppermute | solution.py:396
  5.1 9.0 %collective-permute-start = (bf16[3,4,4096]{2,1,0:T(4,128)(2,1)}, bf16[3,4,4096]{2,1,0:T(4,128)(2,1)S(1)}, u32[]{:S(2)}, u32[]{:S(2)}) collective-permute-start(bf16[3,4,4096]{2,1,0:T(4,128)(2,1)} %bitcast.21), channel_id=1, source_target_pairs={{0,4},{4,8},{8,12},{12,0},{1,5},{5,9},{9,13},{13,1},{2,6},{6,10},{... | collective-permute-start | bytes 294920 | tf_op jit(solution)/shard_map/ppermute | solution.py:396
  6.7 1.0 %copy-start.6 = (bf16[1,4,512,128]{3,2,1,0:T(8,128)(2,1)S(1)}, bf16[1,4,512,128]{3,2,1,0:T(8,128)(2,1)}, u32[]{:S(2)}) copy-start(bf16[1,4,512,128]{3,2,1,0:T(8,128)(2,1)} %keys_ref.1) | copy-start | bytes 1572868
  7.8 1.0 %copy-start.7 = (bf16[1,4,512,128]{3,2,1,0:T(8,128)(2,1)S(1)}, bf16[1,4,512,128]{3,2,1,0:T(8,128)(2,1)}, u32[]{:S(2)}) copy-start(bf16[1,4,512,128]{3,2,1,0:T(8,128)(2,1)} %values_ref.1) | copy-start | bytes 1572868
  8.8 0.7 copy-start.11
  9.5 0.7 copy-start.12
  10.1 0.7 copy-start.13
  14.0 1.9 %copy-start = (bf16[4,4096,96]{1,2,0:T(8,128)(2,1)S(1)}, bf16[4,4096,96]{1,2,0:T(8,128)(2,1)}, u32[]{:S(2)}) copy-start(bf16[4,4096,96]{1,2,0:T(8,128)(2,1)} %param.22) | copy-start | bytes 9437188
  15.9 0.9 copy-start.8
  18.7 17.6 %all-to-all-start = ((bf16[16,48,128]{2,1,0:T(8,128)(2,1)}), bf16[16,48,128]{2,1,0:T(8,128)(2,1)S(1)}, u32[]{:S(2)}, u32[]{:S(2)}) async-start(bf16[16,48,128]{2,1,0:T(8,128)(2,1)} %get-tuple-element.28), calls=%async_computation | async-start | bytes 393216 | tf_op jit(solution)/shard_map/all_to_all | solution.py:403
  23.3 17.5 %collective-permute-start.6 = (bf16[1040,128]{1,0:T(8,128)(2,1)}, bf16[1040,128]{1,0:T(8,128)(2,1)}, u32[]{:S(2)}, u32[]{:S(2)}) collective-permute-start(bf16[1040,128]{1,0:T(8,128)(2,1)} %get-tuple-element.34), channel_id=1, source_target_pairs={{0,4},{4,8},{8,12},{12,0},{1,5},{5,9},{9,13},{13,1},{2,6},{6,10},{... | collective-permute-start | bytes 798728 | tf_op jit(solution)/shard_map/ppermute | solution.py:396
  25.3 16.4 %collective-permute-start.8 = (bf16[1040,128]{1,0:T(8,128)(2,1)}, bf16[1040,128]{1,0:T(8,128)(2,1)}, u32[]{:S(2)}, u32[]{:S(2)}) collective-permute-start(bf16[1040,128]{1,0:T(8,128)(2,1)} %get-tuple-element.36), channel_id=1, source_target_pairs={{0,12},{4,0},{8,4},{12,8},{1,13},{5,1},{9,5},{13,9},{2,14},{6,2},{... | collective-permute-start | bytes 798728 | tf_op jit(solution)/shard_map/ppermute | solution.py:396
  27.2 9.2 %copy-start.1 = (bf16[4096,128]{1,0:T(8,128)(2,1)S(1)}, bf16[4096,128]{1,0:T(8,128)(2,1)}, u32[]{:S(2)}) copy-start(bf16[4096,128]{1,0:T(8,128)(2,1)} %key_ref.1) | copy-start | bytes 3145732
  27.2 9.2 %copy-start.2 = (bf16[4096,128]{1,0:T(8,128)(2,1)S(1)}, bf16[4096,128]{1,0:T(8,128)(2,1)}, u32[]{:S(2)}) copy-start(bf16[4096,128]{1,0:T(8,128)(2,1)} %value_ref.1) | copy-start | bytes 3145732
  27.2 9.2 %copy-start.9 = (bf16[4,32,128]{2,1,0:T(8,128)(2,1)S(1)}, bf16[4,32,128]{2,1,0:T(8,128)(2,1)}, u32[]{:S(2)}) copy-start(bf16[4,32,128]{2,1,0:T(8,128)(2,1)} %param.24) | copy-start | bytes 98308
  27.2 9.2 %copy-start.10 = (bf16[4,32,128]{2,1,0:T(8,128)(2,1)S(1)}, bf16[4,32,128]{2,1,0:T(8,128)(2,1)}, u32[]{:S(2)}) copy-start(bf16[4,32,128]{2,1,0:T(8,128)(2,1)} %param.25) | copy-start | bytes 98308
  31.4 23.1 %collective-permute-start.7 = (bf16[1040,128]{1,0:T(8,128)(2,1)}, bf16[1040,128]{1,0:T(8,128)(2,1)}, u32[]{:S(2)}, u32[]{:S(2)}) collective-permute-start(bf16[1040,128]{1,0:T(8,128)(2,1)} %get-tuple-element.35), channel_id=1, source_target_pairs={{0,8},{4,12},{8,0},{12,4},{1,9},{5,13},{9,1},{13,5},{2,10},{6,14},... | collective-permute-start | bytes 798728 | tf_op jit(solution)/shard_map/ppermute | solution.py:396
  36.4 1.0 %copy-start.4 = (bf16[4,32,2048]{2,1,0:T(8,128)(2,1)S(1)}, bf16[4,32,2048]{2,1,0:T(8,128)(2,1)}, u32[]{:S(2)}) copy-start(bf16[4,32,2048]{2,1,0:T(8,128)(2,1)} %param.23) | copy-start | bytes 1572868
  38.7 39.4 %copy-start.3 = (bf16[4,32,4096]{2,1,0:T(8,128)(2,1)S(1)}, bf16[4,32,4096]{2,1,0:T(8,128)(2,1)}, u32[]{:S(2)}) copy-start(bf16[4,32,4096]{2,1,0:T(8,128)(2,1)} %param.27) | copy-start | bytes 3145732
  38.7 15.8 %collective-permute-start.3 = (bf16[4,3,2304]{2,1,0:T(4,128)(2,1)S(1)}, bf16[4,3,2304]{2,1,0:T(4,128)(2,1)S(1)}, u32[]{:S(2)}, u32[]{:S(2)}) collective-permute-start(bf16[4,3,2304]{2,1,0:T(4,128)(2,1)S(1)} %get-tuple-element.30), channel_id=1, source_target_pairs={{0,1},{1,2},{2,3},{3,0},{4,5},{5,6},{6,7},{7,4},{8,9},{9,10},{10,1... | collective-permute-start | bytes 165896 | tf_op jit(solution)/shard_map/ppermute | solution.py:400
  38.8 15.7 %collective-permute-start.4 = (bf16[4,3,2304]{2,1,0:T(4,128)(2,1)S(1)}, bf16[4,3,2304]{2,1,0:T(4,128)(2,1)S(1)}, u32[]{:S(2)}, u32[]{:S(2)}) collective-permute-start(bf16[4,3,2304]{2,1,0:T(4,128)(2,1)S(1)} %get-tuple-element.31), channel_id=1, source_target_pairs={{0,2},{1,3},{2,0},{3,1},{4,6},{5,7},{6,4},{7,5},{8,10},{9,11},{10,... | collective-permute-start | bytes 165896 | tf_op jit(solution)/shard_map/ppermute | solution.py:400
  40.9 13.6 %collective-permute-start.5 = (bf16[4,3,2304]{2,1,0:T(4,128)(2,1)S(1)}, bf16[4,3,2304]{2,1,0:T(4,128)(2,1)S(1)}, u32[]{:S(2)}, u32[]{:S(2)}) collective-permute-start(bf16[4,3,2304]{2,1,0:T(4,128)(2,1)S(1)} %get-tuple-element.32), channel_id=1, source_target_pairs={{0,3},{1,0},{2,1},{3,2},{4,7},{5,4},{6,5},{7,6},{8,11},{9,8},{10,9... | collective-permute-start | bytes 165896 | tf_op jit(solution)/shard_map/ppermute | solution.py:400
  63.2 1.0 %copy-start.5 = (bf16[4,2048,32]{1,2,0:T(8,128)(2,1)S(1)}, bf16[4,2048,32]{1,2,0:T(8,128)(2,1)}, u32[]{:S(2)}) copy-start(bf16[4,2048,32]{1,2,0:T(8,128)(2,1)} %param.26) | copy-start | bytes 1572868
  65.4 12.7 %all-to-all-start.1 = ((bf16[16,48,128]{2,1,0:T(8,128)(2,1)}), bf16[16,48,128]{2,1,0:T(8,128)(2,1)S(1)}, u32[]{:S(2)}, u32[]{:S(2)}) async-start(bf16[16,48,128]{2,1,0:T(8,128)(2,1)} %get-tuple-element.38), calls=%async_computation.1 | async-start | bytes 393216 | tf_op jit(solution)/shard_map/all_to_all | solution.py:403
  78.8 4.7 %collective-permute-start.9 = (bf16[3,4,4096]{2,1,0:T(4,128)(2,1)S(1)}, bf16[3,4,4096]{2,1,0:T(4,128)(2,1)S(1)}, u32[]{:S(2)}, u32[]{:S(2)}) collective-permute-start(bf16[3,4,4096]{2,1,0:T(4,128)(2,1)S(1)} %get-tuple-element.40), channel_id=1, source_target_pairs={{0,12},{4,0},{8,4},{12,8},{1,13},{5,1},{9,5},{13,9},{2,14},{6,2},{... | collective-permute-start | bytes 294920 | tf_op jit(solution)/shard_map/ppermute | solution.py:396
  80.0 9.6 %collective-permute-start.10 = (bf16[3,4,4096]{2,1,0:T(4,128)(2,1)S(1)}, bf16[3,4,4096]{2,1,0:T(4,128)(2,1)S(1)}, u32[]{:S(2)}, u32[]{:S(2)}) collective-permute-start(bf16[3,4,4096]{2,1,0:T(4,128)(2,1)S(1)} %get-tuple-element.41), channel_id=1, source_target_pairs={{0,8},{4,12},{8,0},{12,4},{1,9},{5,13},{9,1},{13,5},{2,10},{6,14},... | collective-permute-start | bytes 294920 | tf_op jit(solution)/shard_map/ppermute | solution.py:396
  80.0 9.6 %collective-permute-start.11 = (bf16[3,4,4096]{2,1,0:T(4,128)(2,1)S(1)}, bf16[3,4,4096]{2,1,0:T(4,128)(2,1)S(1)}, u32[]{:S(2)}, u32[]{:S(2)}) collective-permute-start(bf16[3,4,4096]{2,1,0:T(4,128)(2,1)S(1)} %get-tuple-element.42), channel_id=1, source_target_pairs={{0,4},{4,8},{8,12},{12,0},{1,5},{5,9},{9,13},{13,1},{2,6},{6,10},{... | collective-permute-start | bytes 294920 | tf_op jit(solution)/shard_map/ppermute | solution.py:396

commit v4 on v3

--- a/solution.py
+++ b/solution.py
@@ -3,7 +3,6 @@
 
 import jax
 import jax.numpy as jnp
-import numpy as np
 from jax import lax
 from jax.experimental import pallas as pl
 from jax.experimental.pallas import tpu as pltpu
@@ -161,13 +160,26 @@
         shape((rows.shape[0], width), jnp.float32),
         [VMEM, HBM] + [VMEM] * len(sums),
         [pltpu.VMEM((size, width), jnp.bfloat16), pltpu.SemaphoreType.DMA((chunks,))],
-        2 * rows.shape[0] * size * width,
-        2 * size * width,
-        40 * MIB,
+        limit=50 * MIB,
     )(rows, weight, *sums)
 
 
-def pack_kernel(sizes, ids_ref, pool_ref, length_ref, keys_ref, values_ref, turns_ref, *refs):
+def product_kernel(rows_ref, weight_ref, total_ref):
+    width = total_ref.shape[1]
+    step = width if width % 1024 else 1024
+    for start in range(0, width, step):
+        total_ref[:, start : start + step] = dot(
+            rows_ref[...], weight_ref[:, start : start + step]
+        )
+
+
+def product(rows, weight):
+    return call(
+        product_kernel, shape((rows.shape[0], weight.shape[1]), jnp.float32), [VMEM] * 2
+    )(rows, weight)
+
+
+def pack_kernel(sizes, ids_ref, pool_ref, length_ref, keys_ref, values_ref, *refs):
     groups, blocks, drafts = sizes
     outs = refs[:blocks]
     slots_ref, extra_f32, extra_ref, sems = refs[blocks:]
@@ -175,9 +187,12 @@
     me = lax.axis_index("tensor")
     length = length_ref[0]
     positions = (iota((drafts, head_size), 0) + length).astype(jnp.float32)
-    angles = positions * turns_ref[0:1, :]
+    lane = iota((drafts, head_size), 1)
+    half = (lane & (head_size // 2 - 1)).astype(jnp.float32)
+    angles = positions * jnp.exp(half * (-2.0 * math.log(rope_base) / head_size))
+    signs = jnp.where(lane < head_size // 2, -1.0, 1.0)
     extra_f32[...] = jnp.zeros(extra_f32.shape, jnp.float32)
-    for index, value in enumerate((jnp.cos(angles), jnp.sin(angles) * turns_ref[1:2, :])):
+    for index, value in enumerate((jnp.cos(angles), jnp.sin(angles) * signs)):
         high = value.astype(jnp.bfloat16).astype(jnp.float32)
         start = 2 * index * drafts
         extra_f32[start : start + drafts, :] = high
@@ -224,26 +239,22 @@
 def pack(sizes, ids, pool, lengths, keys, values):
     groups, blocks, drafts = sizes
     head_size = keys.shape[3]
-    half = np.arange(head_size // 2)
-    frequency = (rope_base ** (-2.0 * half / head_size)).astype(np.float32)
-    signs = np.ones(half.size, np.float32)
-    turns = np.stack([np.tile(frequency, 2), np.concatenate([-signs, signs])])
     used = -(-(4 * drafts + 2) // 16) * 16
     outs = [shape((2 * keys.shape[2] + used, head_size))] * blocks
     smem = pl.BlockSpec(memory_space=pltpu.SMEM)
     return pl.pallas_call(
         functools.partial(pack_kernel, sizes),
         out_shape=outs + [shape((groups * blocks * drafts, 128), jnp.int32)],
-        in_specs=[smem, smem, smem, VMEM, VMEM, VMEM],
+        in_specs=[smem, smem, smem, VMEM, VMEM],
         out_specs=[HBM] * blocks + [VMEM],
         scratch_shapes=[
             pltpu.VMEM((used, head_size), jnp.float32),
             pltpu.VMEM((used, head_size), jnp.bfloat16),
             pltpu.SemaphoreType.DMA((blocks, 3)),
         ],
-        cost_estimate=pl.CostEstimate(flops=0, bytes_accessed=8 * keys.size, transcendentals=0),
+        cost_estimate=pl.CostEstimate(flops=0, bytes_accessed=320 * keys.size, transcendentals=0),
         compiler_params=pltpu.CompilerParams(vmem_limit_bytes=24 * MIB),
-    )(ids, pool, lengths, keys, values, jnp.asarray(turns))
+    )(ids, pool, lengths, keys, values)
 
 
 def grow_kernel(sizes, width, total_ref, rows_ref, key_ref, value_ref, slots_ref, ranks_ref, *rest):
@@ -416,8 +427,6 @@
         [shape((count, features)), shape((blocks * groups, count, lanes))],
         [VMEM] * (blocks + 2),
         [pltpu.VMEM((count, features), jnp.float32)],
-        2 * count * shrink_qkv.size,
-        2 * shrink_qkv.size + 4 * count * features,
     )(*pieces, shrink_in, slots)
     ranks = exchange(rank_part)
     half = features // 2
@@ -433,8 +442,6 @@
         [shape((blocks, drafts, cols))] * groups,
         [VMEM] * 9,
         [],
-        2 * count * owned * width * cols,
-        8 * count * cols + 2 * owned * width * cols,
     )(
         total,
         rows,
@@ -456,7 +463,7 @@
             pltpu.VMEM((span, head_cols), jnp.float32),
         ],
         4 * span * head_cols * cache_size,
-        4 * blocks * cache_size * head_size,
+        320 * blocks * cache_size * head_size,
     )(*parts, *caches)
     gathered = lax.all_gather(mixed, GROUP, axis=0, tiled=False)
     out_rows, out_part = call(
@@ -468,8 +475,8 @@
         2 * shrink_out.size + 4 * count * head_cols,
     )(gathered, jnp.transpose(shrink_out, (0, 2, 1)).reshape(-1, head_cols), slots)
     out_ranks = exchange(out_part)
-    out_total = stream(out_rows, w_out, 8, 0, head_cols)
-    out_cols = out_total.shape[1]
+    out_cols = w_out.shape[1]
+    out_total = product(out_rows, w_out)
     leaving = call(
         functools.partial(out_grow_kernel, sizes, width),
         [shape((drafts, groups, out_cols))] * blocks,

time: 91 us -> 93.1 us (1.023)
  local copies, waits for them, and re-layouts: 8.95 us -> 14 us
  Pallas kernels: 24.3 us -> 20.9 us
  starting transfers between devices: 25.1 us -> 27 us
  waiting for transfers between devices: 24.7 us -> 23.2 us
    pallas_call x3 -> x2, Pallas kernels: 14.5 us -> 8.1 us  [stream(): call(functools.partial(stream_kernel, first, chunks, size // chunks), sha...]
    unnamed x28, local copies, waits for them, and re-layouts: 8.95 us -> 14 us
    pallas_call x0 -> x1, Pallas kernels: none -> 2.99 us  [product(): call(product_kernel, shape((rows.shape[0], weight.shape[1]), jnp.float32)...]
    all_to_all x2, waiting for transfers between devices: 2.58 us -> 0.24 us  [exchange(): return lax.all_to_all(value, EVERY, split_axis=0, concat_axis=0, tiled=True)]
    ppermute x9, starting transfers between devices: 13.8 us -> 15.7 us  [over_tensor(): return lax.ppermute(value, 'tensor', route)]
  transfers between devices with their start and end apart: 14 -> 14, of which waited for: 5 -> 5; matrix products, arithmetic and copies ran while one was open for 0% -> 0% of each run, Pallas kernels for 20% -> 15%
where the time goes in v4:
time: 93.1 us; the launch traced here: 92.4 us
  starting transfers between devices  27 us (29%)
  waiting for transfers between devices  23.2 us (25%)
  Pallas kernels  20.9 us (22%)
  local copies, waits for them, and re-layouts  14 us (15%)
  blocking collectives  5.79 us (6%)
    ppermute x9, waiting for transfers between devices, over_tensor(): return lax.ppermute(value, 'tensor', route)  22.9 us
    ppermute x9, starting transfers between devices, over_tensor(): return lax.ppermute(value, 'tensor', route)  15.7 us
    unnamed x28, local copies, waits for them, and re-layouts  14 us
    all_to_all x2, starting transfers between devices, exchange(): return lax.all_to_all(value, EVERY, split_axis=0, concat_axis=0, tiled=True)  8.32 us
    pallas_call x2, Pallas kernels, stream(): call(functools.partial(stream_kernel, first, chunks, size // chunks), sha...  8.1 us
    all_gather x1, blocking collectives, by_head(): gathered = lax.all_gather(mixed, GROUP, axis=0, tiled=False)  5.79 us
    pallas_call x1, Pallas kernels, product(): call(product_kernel, shape((rows.shape[0], weight.shape[1]), jnp.float32)...  2.99 us
    ppermute x3, starting transfers between devices, over_group(): return lax.ppermute(value, GROUP, route)  2.97 us
  transfers between devices with their start and end apart: 14, of which 5 were waited for; matrix products, arithmetic and copies ran while one was open for 0% of the time, Pallas kernels for 15%

profile of v4, /device:TPU:0, one launch (start us, length us, event | category | flops | bytes accessed | tf_op | source)
XLA Modules:
  0.0 92.4 jit_solution(2049630309903633898)
XLA Ops:
  0.0 5.0 %collective-permute-start.2 = (bf16[3,4,4096]{2,1,0:T(4,128)(2,1)}, bf16[3,4,4096]{2,1,0:T(4,128)(2,1)S(1)}, u32[]{:S(2)}, u32[]{:S(2)}) collective-permute-start(bf16[3,4,4096]{2,1,0:T(4,128)(2,1)} %bitcast.19), channel_id=1, source_target_pairs={{0,12},{4,0},{8,4},{12,8},{1,13},{5,1},{9,5},{13,9},{2,14},{6,2},{... | collective-permute-start | bytes 294920 | tf_op jit(solution)/shard_map/ppermute | solution.py:407
  5.0 0.0 collective-permute-start.1
  5.1 1.0 %collective-permute-start = (bf16[3,4,4096]{2,1,0:T(4,128)(2,1)}, bf16[3,4,4096]{2,1,0:T(4,128)(2,1)S(1)}, u32[]{:S(2)}, u32[]{:S(2)}) collective-permute-start(bf16[3,4,4096]{2,1,0:T(4,128)(2,1)} %bitcast.21), channel_id=1, source_target_pairs={{0,4},{4,8},{8,12},{12,0},{1,5},{5,9},{9,13},{13,1},{2,6},{6,10},{... | collective-permute-start | bytes 294920 | tf_op jit(solution)/shard_map/ppermute | solution.py:407
  6.7 1.0 %copy-done.6 = bf16[1,4,512,128]{3,2,1,0:T(8,128)(2,1)S(1)} copy-done((bf16[1,4,512,128]{3,2,1,0:T(8,128)(2,1)S(1)}, bf16[1,4,512,128]{3,2,1,0:T(8,128)(2,1)}, u32[]{:S(2)}) %copy-start.6) | copy-done | bytes 524312
  7.8 1.0 %copy-done.7 = bf16[1,4,512,128]{3,2,1,0:T(8,128)(2,1)S(1)} copy-done((bf16[1,4,512,128]{3,2,1,0:T(8,128)(2,1)S(1)}, bf16[1,4,512,128]{3,2,1,0:T(8,128)(2,1)}, u32[]{:S(2)}) %copy-start.7) | copy-done | bytes 524312
  8.8 0.7 copy-done.12
  9.5 0.7 copy-done.13
  10.1 1.9 %shard_map.154 = (bf16[1040,128]{1,0:T(8,128)(2,1)S(1)}, bf16[1040,128]{1,0:T(8,128)(2,1)}, bf16[1040,128]{1,0:T(8,128)(2,1)}, bf16[1040,128]{1,0:T(8,128)(2,1)}, s32[48,128]{1,0:T(8,128)S(1)}) custom-call(s32[16]{0:T(128)S(1)} %copy-done.12, s32[16]{0:T(128)S(1)} %copy-done.13, s32[1]{0:T(128)S(6)} %copy.17.length_ref, ...), custom_call_target="tpu_custom_call" | custom-call | bytes 83886080 | tf_op jit(solution)/shard_map/pallas_call | solution.py:245
  12.1 0.0 collective-permute-done.2.refs_3_
  12.1 1.9 %collective-permute-done.1.refs_2_ = bf16[3,4,4096]{2,1,0:T(4,128)(2,1)S(1)} collective-permute-done((bf16[3,4,4096]{2,1,0:T(4,128)(2,1)}, bf16[3,4,4096]{2,1,0:T(4,128)(2,1)S(1)}, u32[]{:S(2)}, u32[]{:S(2)}) %collective-permute-start.1) | collective-permute-done | bytes 98336 | tf_op jit(solution)/shard_map/ppermute | solution.py:407
  14.0 0.0 collective-permute-done.refs_1_
  14.0 1.9 %copy-done.1 = bf16[4,4096,96]{1,2,0:T(8,128)(2,1)S(1)} copy-done((bf16[4,4096,96]{1,2,0:T(8,128)(2,1)S(1)}, bf16[4,4096,96]{1,2,0:T(8,128)(2,1)}, u32[]{:S(2)}) %copy-start.1) | copy-done | bytes 3145752
  15.9 0.9 copy-done.9
  16.8 1.9 %shard_map.155 = (bf16[48,4096]{1,0:T(8,128)(2,1)S(1)}, bf16[16,48,128]{2,1,0:T(8,128)(2,1)}) custom-call(bf16[3,4,4096]{2,1,0:T(4,128)(2,1)S(1)} %bitcast.22, bf16[3,4,4096]{2,1,0:T(4,128)(2,1)S(1)} %collective-permute-done.refs_1_, bf16[3,4,4096]{2,1,0:T(4,128)(2,1)S(1)} %collective-permute-done.1.refs_2_, ...), custom_call_target="tpu_custom_call" | custom-call | tf_op jit(solution)/shard_map/pallas_call | solution.py:425
  18.7 4.6 %all-to-all-start = ((bf16[16,48,128]{2,1,0:T(8,128)(2,1)}), bf16[16,48,128]{2,1,0:T(8,128)(2,1)S(1)}, u32[]{:S(2)}, u32[]{:S(2)}) async-start(bf16[16,48,128]{2,1,0:T(8,128)(2,1)} %get-tuple-element.28), calls=%async_computation | async-start | bytes 393216 | tf_op jit(solution)/shard_map/all_to_all | solution.py:414
  23.3 1.9 %collective-permute-start.6 = (bf16[1040,128]{1,0:T(8,128)(2,1)}, bf16[1040,128]{1,0:T(8,128)(2,1)}, u32[]{:S(2)}, u32[]{:S(2)}) collective-permute-start(bf16[1040,128]{1,0:T(8,128)(2,1)} %get-tuple-element.34), channel_id=1, source_target_pairs={{0,4},{4,8},{8,12},{12,0},{1,5},{5,9},{9,13},{13,1},{2,6},{6,10},{... | collective-permute-start | bytes 798728 | tf_op jit(solution)/shard_map/ppermute | solution.py:407
  25.3 2.0 %collective-permute-start.8 = (bf16[1040,128]{1,0:T(8,128)(2,1)}, bf16[1040,128]{1,0:T(8,128)(2,1)}, u32[]{:S(2)}, u32[]{:S(2)}) collective-permute-start(bf16[1040,128]{1,0:T(8,128)(2,1)} %get-tuple-element.36), channel_id=1, source_target_pairs={{0,12},{4,0},{8,4},{12,8},{1,13},{5,1},{9,5},{13,9},{2,14},{6,2},{... | collective-permute-start | bytes 798728 | tf_op jit(solution)/shard_map/ppermute | solution.py:407
  27.2 4.1 %shard_map.156.refs_0_ = f32[48,2048]{1,0:T(8,128)S(1)} custom-call(bf16[48,4096]{1,0:T(8,128)(2,1)S(1)} %get-tuple-element.25.rows_ref, bf16[4096,2048]{1,0:T(8,128)(2,1)} %weight_ref.4), custom_call_target="tpu_custom_call" | custom-call | tf_op jit(solution)/shard_map/pallas_call | solution.py:158
  31.4 1.0 %collective-permute-start.7 = (bf16[1040,128]{1,0:T(8,128)(2,1)}, bf16[1040,128]{1,0:T(8,128)(2,1)}, u32[]{:S(2)}, u32[]{:S(2)}) collective-permute-start(bf16[1040,128]{1,0:T(8,128)(2,1)} %get-tuple-element.35), channel_id=1, source_target_pairs={{0,8},{4,12},{8,0},{12,4},{1,9},{5,13},{9,1},{13,5},{2,10},{6,14},... | collective-permute-start | bytes 798728 | tf_op jit(solution)/shard_map/ppermute | solution.py:407
  32.4 4.0 %shard_map.157.total_ref = f32[48,2048]{1,0:T(8,128)S(1)} custom-call(bf16[48,4096]{1,0:T(8,128)(2,1)S(1)} %get-tuple-element.25.rows_ref, bf16[4096,2048]{1,0:T(8,128)(2,1)} %weight_ref.4, f32[48,2048]{1,0:T(8,128)S(1)} %shard_map.156.refs_0_), custom_call_target="tpu_custom_call" | custom-call | tf_op jit(solution)/shard_map/pallas_call | solution.py:158
  36.4 0.0 all-to-all-done.ranks_ref
  36.4 0.0 copy-start.5
  36.4 1.0 %copy-done.5 = bf16[4,32,2048]{2,1,0:T(8,128)(2,1)S(1)} copy-done((bf16[4,32,2048]{2,1,0:T(8,128)(2,1)S(1)}, bf16[4,32,2048]{2,1,0:T(8,128)(2,1)}, u32[]{:S(2)}) %copy-start.5) | copy-done | bytes 524312
  37.5 1.2 %shard_map.158 = (bf16[4,3,2304]{2,1,0:T(4,128)(2,1)S(1)}, bf16[4,3,2304]{2,1,0:T(4,128)(2,1)S(1)}, bf16[4,3,2304]{2,1,0:T(4,128)(2,1)S(1)}, bf16[4,3,2304]{2,1,0:T(4,128)(2,1)S(1)}) custom-call(f32[48,2048]{1,0:T(8,128)S(1)} %shard_map.157.total_ref, bf16[48,4096]{1,0:T(8,128)(2,1)S(1)} %get-tuple-element.25.rows_ref, bf16[4096,128]{1,0:T(8,128)(2,1)S(1)} %copy-done.2, ...), custom_call_target="tpu_custom_call" | custom-call | tf_op jit(solution)/shard_map/pallas_call | solution.py:440
  38.7 0.0 copy-start.4
  38.7 0.1 collective-permute-start.3
  38.8 2.1 %collective-permute-start.4 = (bf16[4,3,2304]{2,1,0:T(4,128)(2,1)S(1)}, bf16[4,3,2304]{2,1,0:T(4,128)(2,1)S(1)}, u32[]{:S(2)}, u32[]{:S(2)}) collective-permute-start(bf16[4,3,2304]{2,1,0:T(4,128)(2,1)S(1)} %get-tuple-element.31), channel_id=1, source_target_pairs={{0,2},{1,3},{2,0},{3,1},{4,6},{5,7},{6,4},{7,5},{8,10},{9,11},{10,... | collective-permute-start | bytes 165896 | tf_op jit(solution)/shard_map/ppermute | solution.py:411
  40.9 0.0 collective-permute-done.6.refs_5_
  40.9 0.8 collective-permute-start.5
  41.7 0.0 collective-permute-done.8.refs_7_
  41.7 12.8 %collective-permute-done.7.refs_6_ = bf16[1040,128]{1,0:T(8,128)(2,1)} collective-permute-done((bf16[1040,128]{1,0:T(8,128)(2,1)}, bf16[1040,128]{1,0:T(8,128)(2,1)}, u32[]{:S(2)}, u32[]{:S(2)}) %collective-permute-start.7) | collective-permute-done | bytes 266272 | tf_op jit(solution)/shard_map/ppermute | solution.py:407
  54.5 0.0 collective-permute-done.4.refs_2_
  54.5 0.0 collective-permute-done.5.refs_3_
  54.5 2.9 %shard_map.159 = bf16[12,2048]{1,0:T(8,128)(2,1)S(1)} custom-call(bf16[4,3,2304]{2,1,0:T(4,128)(2,1)S(1)} %get-tuple-element.29.refs_0_, bf16[4,3,2304]{2,1,0:T(4,128)(2,1)S(1)} %collective-permute-done.3.refs_1_, bf16[4,3,2304]{2,1,0:T(4,128)(2,1)S(1)} %collective-permute-done.4.refs_2_, bf16[4,3,2304]{2,1,0:T(4,128)(2,1)S(1)} %collective-permute-done.5.refs_3_, ...), custom_call_target="tpu_custom_call" | custom-call | flops 50331648 | bytes 83886080 | tf_op jit(solution)/shard_map/pallas_call | solution.py:456
  57.4 5.8 %all-gather.1.got_ref = bf16[4,12,2048]{2,1,0:T(8,128)(2,1)S(1)} all-gather(bf16[1,12,2048]{2,1,0:T(8,128)(2,1)S(1)} %bitcast.18), channel_id=2, replica_groups=mesh['parts'=2,'tensor'=4,'dp'=2,'pipe'=2] {'dp','pipe'}, dimensions={0}, use_global_device_ids=true | all-gather | bytes 245760 | tf_op jit(solution)/shard_map/all_gather | solution.py:468
  63.2 1.0 %copy-done.8 = bf16[4,2048,32]{1,2,0:T(8,128)(2,1)S(1)} copy-done((bf16[4,2048,32]{1,2,0:T(8,128)(2,1)S(1)}, bf16[4,2048,32]{1,2,0:T(8,128)(2,1)}, u32[]{:S(2)}) %copy-start.8) | copy-done | bytes 524312
  64.3 1.1 %shard_map.160 = (bf16[48,2048]{1,0:T(8,128)(2,1)S(1)}, bf16[16,48,128]{2,1,0:T(8,128)(2,1)}) custom-call(bf16[4,12,2048]{2,1,0:T(8,128)(2,1)S(1)} %all-gather.1.got_ref, bf16[128,2048]{1,0:T(8,128)(2,1)S(1)} %bitcast.17, s32[48,128]{1,0:T(8,128)S(1)} %get-tuple-element.24.refs_5_.slots_ref), custom_call_target="tpu_custom_call" | custom-call | flops 25165824 | bytes 917504 | tf_op jit(solution)/shard_map/pallas_call | solution.py:469
  65.4 3.7 %all-to-all-start.1 = ((bf16[16,48,128]{2,1,0:T(8,128)(2,1)}), bf16[16,48,128]{2,1,0:T(8,128)(2,1)S(1)}, u32[]{:S(2)}, u32[]{:S(2)}) async-start(bf16[16,48,128]{2,1,0:T(8,128)(2,1)} %get-tuple-element.38), calls=%async_computation.1 | async-start | bytes 393216 | tf_op jit(solution)/shard_map/all_to_all | solution.py:414
  69.1 0.0 copy-start
  69.1 5.8 %copy-done = bf16[2048,4096]{1,0:T(8,128)(2,1)S(1)} copy-done((bf16[2048,4096]{1,0:T(8,128)(2,1)S(1)}, bf16[2048,4096]{1,0:T(8,128)(2,1)}, u32[]{:S(2)}) %copy-start) | copy-done | bytes 16777240
  74.9 3.0 %shard_map.161.total_ref = f32[48,4096]{1,0:T(8,128)S(1)} custom-call(bf16[48,2048]{1,0:T(8,128)(2,1)S(1)} %get-tuple-element.37.rows_ref, bf16[2048,4096]{1,0:T(8,128)(2,1)S(1)} %copy-done), custom_call_target="tpu_custom_call" | custom-call | tf_op jit(solution)/shard_map/pallas_call | solution.py:177
  77.9 0.2 all-to-all-done.1.ranks_ref
  78.1 0.7 shard_map.162
  78.8 3.6 %collective-permute-start.9 = (bf16[3,4,4096]{2,1,0:T(4,128)(2,1)S(1)}, bf16[3,4,4096]{2,1,0:T(4,128)(2,1)S(1)}, u32[]{:S(2)}, u32[]{:S(2)}) collective-permute-start(bf16[3,4,4096]{2,1,0:T(4,128)(2,1)S(1)} %get-tuple-element.40), channel_id=1, source_target_pairs={{0,12},{4,0},{8,4},{12,8},{1,13},{5,1},{9,5},{13,9},{2,14},{6,2},{... | collective-permute-start | bytes 294920 | tf_op jit(solution)/shard_map/ppermute | solution.py:407
  82.4 1.1 %collective-permute-start.11 = (bf16[3,4,4096]{2,1,0:T(4,128)(2,1)S(1)}, bf16[3,4,4096]{2,1,0:T(4,128)(2,1)S(1)}, u32[]{:S(2)}, u32[]{:S(2)}) collective-permute-start(bf16[3,4,4096]{2,1,0:T(4,128)(2,1)S(1)} %get-tuple-element.42), channel_id=1, source_target_pairs={{0,4},{4,8},{8,12},{12,0},{1,5},{5,9},{9,13},{13,1},{2,6},{6,10},{... | collective-permute-start | bytes 294920 | tf_op jit(solution)/shard_map/ppermute | solution.py:407
  83.5 2.1 %collective-permute-done.9 = bf16[3,4,4096]{2,1,0:T(4,128)(2,1)S(1)} collective-permute-done((bf16[3,4,4096]{2,1,0:T(4,128)(2,1)S(1)}, bf16[3,4,4096]{2,1,0:T(4,128)(2,1)S(1)}, u32[]{:S(2)}, u32[]{:S(2)}) %collective-permute-start.9) | collective-permute-done | bytes 98336 | tf_op jit(solution)/shard_map/ppermute | solution.py:407
  85.6 6.1 %collective-permute-done.10 = bf16[3,4,4096]{2,1,0:T(4,128)(2,1)S(1)} collective-permute-done((bf16[3,4,4096]{2,1,0:T(4,128)(2,1)S(1)}, bf16[3,4,4096]{2,1,0:T(4,128)(2,1)S(1)}, u32[]{:S(2)}, u32[]{:S(2)}) %collective-permute-start.10) | collective-permute-done | bytes 98336 | tf_op jit(solution)/shard_map/ppermute | solution.py:407
  91.7 0.7 fusion
  (19 shorter events, 0.0 us)
Async XLA Ops:
  0.0 12.1 %collective-permute-start.2 = (bf16[3,4,4096]{2,1,0:T(4,128)(2,1)}, bf16[3,4,4096]{2,1,0:T(4,128)(2,1)S(1)}, u32[]{:S(2)}, u32[]{:S(2)}) collective-permute-start(bf16[3,4,4096]{2,1,0:T(4,128)(2,1)} %bitcast.19), channel_id=1, source_target_pairs={{0,12},{4,0},{8,4},{12,8},{1,13},{5,1},{9,5},{13,9},{2,14},{6,2},{... | collective-permute-start | bytes 294920 | tf_op jit(solution)/shard_map/ppermute | solution.py:407
  5.0 9.0 %collective-permute-start.1 = (bf16[3,4,4096]{2,1,0:T(4,128)(2,1)}, bf16[3,4,4096]{2,1,0:T(4,128)(2,1)S(1)}, u32[]{:S(2)}, u32[]{:S(2)}) collective-permute-start(bf16[3,4,4096]{2,1,0:T(4,128)(2,1)} %bitcast.20), channel_id=1, source_target_pairs={{0,8},{4,12},{8,0},{12,4},{1,9},{5,13},{9,1},{13,5},{2,10},{6,14},... | collective-permute-start | bytes 294920 | tf_op jit(solution)/shard_map/ppermute | solution.py:407
  5.1 9.0 %collective-permute-start = (bf16[3,4,4096]{2,1,0:T(4,128)(2,1)}, bf16[3,4,4096]{2,1,0:T(4,128)(2,1)S(1)}, u32[]{:S(2)}, u32[]{:S(2)}) collective-permute-start(bf16[3,4,4096]{2,1,0:T(4,128)(2,1)} %bitcast.21), channel_id=1, source_target_pairs={{0,4},{4,8},{8,12},{12,0},{1,5},{5,9},{9,13},{13,1},{2,6},{6,10},{... | collective-permute-start | bytes 294920 | tf_op jit(solution)/shard_map/ppermute | solution.py:407
  6.7 1.0 %copy-start.6 = (bf16[1,4,512,128]{3,2,1,0:T(8,128)(2,1)S(1)}, bf16[1,4,512,128]{3,2,1,0:T(8,128)(2,1)}, u32[]{:S(2)}) copy-start(bf16[1,4,512,128]{3,2,1,0:T(8,128)(2,1)} %keys_ref.1) | copy-start | bytes 1572868
  7.8 1.0 %copy-start.7 = (bf16[1,4,512,128]{3,2,1,0:T(8,128)(2,1)S(1)}, bf16[1,4,512,128]{3,2,1,0:T(8,128)(2,1)}, u32[]{:S(2)}) copy-start(bf16[1,4,512,128]{3,2,1,0:T(8,128)(2,1)} %values_ref.1) | copy-start | bytes 1572868
  8.8 0.7 copy-start.12
  9.5 0.7 copy-start.13
  14.0 1.9 %copy-start.1 = (bf16[4,4096,96]{1,2,0:T(8,128)(2,1)S(1)}, bf16[4,4096,96]{1,2,0:T(8,128)(2,1)}, u32[]{:S(2)}) copy-start(bf16[4,4096,96]{1,2,0:T(8,128)(2,1)} %param.21) | copy-start | bytes 9437188
  15.9 0.9 copy-start.9
  18.7 17.6 %all-to-all-start = ((bf16[16,48,128]{2,1,0:T(8,128)(2,1)}), bf16[16,48,128]{2,1,0:T(8,128)(2,1)S(1)}, u32[]{:S(2)}, u32[]{:S(2)}) async-start(bf16[16,48,128]{2,1,0:T(8,128)(2,1)} %get-tuple-element.28), calls=%async_computation | async-start | bytes 393216 | tf_op jit(solution)/shard_map/all_to_all | solution.py:414
  23.3 17.5 %collective-permute-start.6 = (bf16[1040,128]{1,0:T(8,128)(2,1)}, bf16[1040,128]{1,0:T(8,128)(2,1)}, u32[]{:S(2)}, u32[]{:S(2)}) collective-permute-start(bf16[1040,128]{1,0:T(8,128)(2,1)} %get-tuple-element.34), channel_id=1, source_target_pairs={{0,4},{4,8},{8,12},{12,0},{1,5},{5,9},{9,13},{13,1},{2,6},{6,10},{... | collective-permute-start | bytes 798728 | tf_op jit(solution)/shard_map/ppermute | solution.py:407
  25.3 16.4 %collective-permute-start.8 = (bf16[1040,128]{1,0:T(8,128)(2,1)}, bf16[1040,128]{1,0:T(8,128)(2,1)}, u32[]{:S(2)}, u32[]{:S(2)}) collective-permute-start(bf16[1040,128]{1,0:T(8,128)(2,1)} %get-tuple-element.36), channel_id=1, source_target_pairs={{0,12},{4,0},{8,4},{12,8},{1,13},{5,1},{9,5},{13,9},{2,14},{6,2},{... | collective-permute-start | bytes 798728 | tf_op jit(solution)/shard_map/ppermute | solution.py:407
  27.2 9.2 %copy-start.2 = (bf16[4096,128]{1,0:T(8,128)(2,1)S(1)}, bf16[4096,128]{1,0:T(8,128)(2,1)}, u32[]{:S(2)}) copy-start(bf16[4096,128]{1,0:T(8,128)(2,1)} %key_ref.1) | copy-start | bytes 3145732
  27.2 9.2 %copy-start.3 = (bf16[4096,128]{1,0:T(8,128)(2,1)S(1)}, bf16[4096,128]{1,0:T(8,128)(2,1)}, u32[]{:S(2)}) copy-start(bf16[4096,128]{1,0:T(8,128)(2,1)} %value_ref.1) | copy-start | bytes 3145732
  27.2 9.2 %copy-start.10 = (bf16[4,32,128]{2,1,0:T(8,128)(2,1)S(1)}, bf16[4,32,128]{2,1,0:T(8,128)(2,1)}, u32[]{:S(2)}) copy-start(bf16[4,32,128]{2,1,0:T(8,128)(2,1)} %param.23) | copy-start | bytes 98308
  27.2 9.2 %copy-start.11 = (bf16[4,32,128]{2,1,0:T(8,128)(2,1)S(1)}, bf16[4,32,128]{2,1,0:T(8,128)(2,1)}, u32[]{:S(2)}) copy-start(bf16[4,32,128]{2,1,0:T(8,128)(2,1)} %param.24) | copy-start | bytes 98308
  31.4 23.1 %collective-permute-start.7 = (bf16[1040,128]{1,0:T(8,128)(2,1)}, bf16[1040,128]{1,0:T(8,128)(2,1)}, u32[]{:S(2)}, u32[]{:S(2)}) collective-permute-start(bf16[1040,128]{1,0:T(8,128)(2,1)} %get-tuple-element.35), channel_id=1, source_target_pairs={{0,8},{4,12},{8,0},{12,4},{1,9},{5,13},{9,1},{13,5},{2,10},{6,14},... | collective-permute-start | bytes 798728 | tf_op jit(solution)/shard_map/ppermute | solution.py:407
  36.4 1.0 %copy-start.5 = (bf16[4,32,2048]{2,1,0:T(8,128)(2,1)S(1)}, bf16[4,32,2048]{2,1,0:T(8,128)(2,1)}, u32[]{:S(2)}) copy-start(bf16[4,32,2048]{2,1,0:T(8,128)(2,1)} %param.22) | copy-start | bytes 1572868
  38.7 39.4 %copy-start.4 = (bf16[4,32,4096]{2,1,0:T(8,128)(2,1)S(1)}, bf16[4,32,4096]{2,1,0:T(8,128)(2,1)}, u32[]{:S(2)}) copy-start(bf16[4,32,4096]{2,1,0:T(8,128)(2,1)} %param.26) | copy-start | bytes 3145732
  38.7 15.8 %collective-permute-start.3 = (bf16[4,3,2304]{2,1,0:T(4,128)(2,1)S(1)}, bf16[4,3,2304]{2,1,0:T(4,128)(2,1)S(1)}, u32[]{:S(2)}, u32[]{:S(2)}) collective-permute-start(bf16[4,3,2304]{2,1,0:T(4,128)(2,1)S(1)} %get-tuple-element.30), channel_id=1, source_target_pairs={{0,1},{1,2},{2,3},{3,0},{4,5},{5,6},{6,7},{7,4},{8,9},{9,10},{10,1... | collective-permute-start | bytes 165896 | tf_op jit(solution)/shard_map/ppermute | solution.py:411
  38.8 15.7 %collective-permute-start.4 = (bf16[4,3,2304]{2,1,0:T(4,128)(2,1)S(1)}, bf16[4,3,2304]{2,1,0:T(4,128)(2,1)S(1)}, u32[]{:S(2)}, u32[]{:S(2)}) collective-permute-start(bf16[4,3,2304]{2,1,0:T(4,128)(2,1)S(1)} %get-tuple-element.31), channel_id=1, source_target_pairs={{0,2},{1,3},{2,0},{3,1},{4,6},{5,7},{6,4},{7,5},{8,10},{9,11},{10,... | collective-permute-start | bytes 165896 | tf_op jit(solution)/shard_map/ppermute | solution.py:411
  40.9 13.6 %collective-permute-start.5 = (bf16[4,3,2304]{2,1,0:T(4,128)(2,1)S(1)}, bf16[4,3,2304]{2,1,0:T(4,128)(2,1)S(1)}, u32[]{:S(2)}, u32[]{:S(2)}) collective-permute-start(bf16[4,3,2304]{2,1,0:T(4,128)(2,1)S(1)} %get-tuple-element.32), channel_id=1, source_target_pairs={{0,3},{1,0},{2,1},{3,2},{4,7},{5,4},{6,5},{7,6},{8,11},{9,8},{10,9... | collective-permute-start | bytes 165896 | tf_op jit(solution)/shard_map/ppermute | solution.py:411
  63.2 1.0 %copy-start.8 = (bf16[4,2048,32]{1,2,0:T(8,128)(2,1)S(1)}, bf16[4,2048,32]{1,2,0:T(8,128)(2,1)}, u32[]{:S(2)}) copy-start(bf16[4,2048,32]{1,2,0:T(8,128)(2,1)} %param.25) | copy-start | bytes 1572868
  65.4 12.7 %all-to-all-start.1 = ((bf16[16,48,128]{2,1,0:T(8,128)(2,1)}), bf16[16,48,128]{2,1,0:T(8,128)(2,1)S(1)}, u32[]{:S(2)}, u32[]{:S(2)}) async-start(bf16[16,48,128]{2,1,0:T(8,128)(2,1)} %get-tuple-element.38), calls=%async_computation.1 | async-start | bytes 393216 | tf_op jit(solution)/shard_map/all_to_all | solution.py:414
  69.1 5.8 %copy-start = (bf16[2048,4096]{1,0:T(8,128)(2,1)S(1)}, bf16[2048,4096]{1,0:T(8,128)(2,1)}, u32[]{:S(2)}) copy-start(bf16[2048,4096]{1,0:T(8,128)(2,1)} %weight_ref.5) | copy-start | bytes 50331652
  78.8 6.8 %collective-permute-start.9 = (bf16[3,4,4096]{2,1,0:T(4,128)(2,1)S(1)}, bf16[3,4,4096]{2,1,0:T(4,128)(2,1)S(1)}, u32[]{:S(2)}, u32[]{:S(2)}) collective-permute-start(bf16[3,4,4096]{2,1,0:T(4,128)(2,1)S(1)} %get-tuple-element.40), channel_id=1, source_target_pairs={{0,12},{4,0},{8,4},{12,8},{1,13},{5,1},{9,5},{13,9},{2,14},{6,2},{... | collective-permute-start | bytes 294920 | tf_op jit(solution)/shard_map/ppermute | solution.py:407
  82.4 9.3 %collective-permute-start.10 = (bf16[3,4,4096]{2,1,0:T(4,128)(2,1)S(1)}, bf16[3,4,4096]{2,1,0:T(4,128)(2,1)S(1)}, u32[]{:S(2)}, u32[]{:S(2)}) collective-permute-start(bf16[3,4,4096]{2,1,0:T(4,128)(2,1)S(1)} %get-tuple-element.41), channel_id=1, source_target_pairs={{0,8},{4,12},{8,0},{12,4},{1,9},{5,13},{9,1},{13,5},{2,10},{6,14},... | collective-permute-start | bytes 294920 | tf_op jit(solution)/shard_map/ppermute | solution.py:407
  82.4 9.3 %collective-permute-start.11 = (bf16[3,4,4096]{2,1,0:T(4,128)(2,1)S(1)}, bf16[3,4,4096]{2,1,0:T(4,128)(2,1)S(1)}, u32[]{:S(2)}, u32[]{:S(2)}) collective-permute-start(bf16[3,4,4096]{2,1,0:T(4,128)(2,1)S(1)} %get-tuple-element.42), channel_id=1, source_target_pairs={{0,4},{4,8},{8,12},{12,0},{1,5},{5,9},{9,13},{13,1},{2,6},{6,10},{... | collective-permute-start | bytes 294920 | tf_op jit(solution)/shard_map/ppermute | solution.py:407

commit v5 on v4

--- a/solution.py
+++ b/solution.py
@@ -127,59 +127,31 @@
     return jnp.where(slot == place, wide, 0.0).astype(jnp.bfloat16)
 
 
-def stream_kernel(first, chunks, depth, rows_ref, weight_ref, *refs):
-    *sums, total_ref, buffer, sems = refs
-
-    def copy(chunk):
-        return pltpu.make_async_copy(
-            weight_ref.at[pl.ds(first + chunk * depth, depth)],
-            buffer.at[pl.ds(chunk * depth, depth)],
-            sems.at[chunk],
-        )
-
-    for chunk in range(chunks):
-        copy(chunk).start()
-    for chunk in range(chunks):
-        start = first + chunk * depth
-        copy(chunk).wait()
-        product = dot(
-            rows_ref[:, start : start + depth], buffer[chunk * depth : (chunk + 1) * depth, :]
-        )
-        if chunk:
-            total_ref[...] += product
-        elif sums:
-            total_ref[...] = sums[0][...] + product
-        else:
-            total_ref[...] = product
-
-
-def stream(rows, weight, chunks, first, size, *sums):
-    width = weight.shape[1]
-    return call(
-        functools.partial(stream_kernel, first, chunks, size // chunks),
-        shape((rows.shape[0], width), jnp.float32),
-        [VMEM, HBM] + [VMEM] * len(sums),
-        [pltpu.VMEM((size, width), jnp.bfloat16), pltpu.SemaphoreType.DMA((chunks,))],
-        limit=50 * MIB,
-    )(rows, weight, *sums)
-
-
-def product_kernel(rows_ref, weight_ref, total_ref):
+def product_kernel(first, depth, rows_ref, weight_ref, *refs):
+    *sums, total_ref = refs
     width = total_ref.shape[1]
     step = width if width % 1024 else 1024
     for start in range(0, width, step):
-        total_ref[:, start : start + step] = dot(
-            rows_ref[...], weight_ref[:, start : start + step]
+        part = dot(
+            rows_ref[:, first : first + depth],
+            weight_ref[first : first + depth, start : start + step],
         )
-
-
-def product(rows, weight):
+        if sums:
+            part = sums[0][:, start : start + step] + part
+        total_ref[:, start : start + step] = part
+
+
+def product(rows, weight, first, depth, *sums):
+    width = weight.shape[1]
     return call(
-        product_kernel, shape((rows.shape[0], weight.shape[1]), jnp.float32), [VMEM] * 2
-    )(rows, weight)
+        functools.partial(product_kernel, first, depth),
+        shape((rows.shape[0], width), jnp.float32),
+        [VMEM] * (2 + len(sums)),
+    )(rows, weight, *sums)
 
 
 def pack_kernel(sizes, ids_ref, pool_ref, length_ref, keys_ref, values_ref, *refs):
+    refs = refs[2:]
     groups, blocks, drafts = sizes
     outs = refs[:blocks]
     slots_ref, extra_f32, extra_ref, sems = refs[blocks:]
@@ -236,7 +208,7 @@
         copy.wait()
 
 
-def pack(sizes, ids, pool, lengths, keys, values):
+def pack(sizes, ids, pool, lengths, keys, values, later):
     groups, blocks, drafts = sizes
     head_size = keys.shape[3]
     used = -(-(4 * drafts + 2) // 16) * 16
@@ -245,7 +217,7 @@
     return pl.pallas_call(
         functools.partial(pack_kernel, sizes),
         out_shape=outs + [shape((groups * blocks * drafts, 128), jnp.int32)],
-        in_specs=[smem, smem, smem, VMEM, VMEM],
+        in_specs=[smem, smem, smem, VMEM, VMEM] + [HBM] * 2,
         out_specs=[HBM] * blocks + [VMEM],
         scratch_shapes=[
             pltpu.VMEM((used, head_size), jnp.float32),
@@ -253,8 +225,8 @@
             pltpu.SemaphoreType.DMA((blocks, 3)),
         ],
         cost_estimate=pl.CostEstimate(flops=0, bytes_accessed=320 * keys.size, transcendentals=0),
-        compiler_params=pltpu.CompilerParams(vmem_limit_bytes=24 * MIB),
-    )(ids, pool, lengths, keys, values)
+        compiler_params=pltpu.CompilerParams(vmem_limit_bytes=40 * MIB),
+    )(ids, pool, lengths, keys, values, *[later] * 2)
 
 
 def grow_kernel(sizes, width, total_ref, rows_ref, key_ref, value_ref, slots_ref, ranks_ref, *rest):
@@ -287,7 +259,7 @@
 def attend_kernel(blocks, drafts, groups, cache_size, *refs):
     parts = refs[:groups]
     caches = refs[groups : groups + blocks]
-    mixed_ref, query_s, fresh_s, out_s = refs[groups + blocks :]
+    _, mixed_ref, query_s, fresh_s, out_s = refs[groups + blocks :]
     head_size = caches[0].shape[1]
     cols = parts[0].shape[2]
     heads = cols // head_size - 2
@@ -417,7 +389,7 @@
     pieces = [mine] + [over_tensor(mine, shift) for shift in range(1, blocks)]
 
     *messages, slots = pack(
-        sizes, adapter_ids, adapter_slots, cache_lengths, cache_keys, cache_values
+        sizes, adapter_ids, adapter_slots, cache_lengths, cache_keys, cache_values, w_out
     )
     caches = {shift: over_tensor(messages[shift], shift) for shift in range(1, blocks) if shift != 2}
 
@@ -430,11 +402,11 @@
     )(*pieces, shrink_in, slots)
     ranks = exchange(rank_part)
     half = features // 2
-    total = stream(rows, w_query, 4, 0, half)
+    total = product(rows, w_query, 0, half)
     total, *late = lax.optimization_barrier((total, *messages[2:3]))
     for message in late:
         caches[2] = over_tensor(message, 2)
-    total = stream(rows, w_query, 4, half, features - half, total)
+    total = product(rows, w_query, half, features - half, total)
     caches = [messages[0]] + [caches[shift] for shift in range(1, blocks)]
     cols = total.shape[1] + w_key.shape[1] + w_value.shape[1]
     sent = call(
@@ -456,7 +428,7 @@
     mixed = call(
         functools.partial(attend_kernel, blocks, drafts, groups, cache_size),
         shape((span, head_cols)),
-        [VMEM] * (groups + blocks),
+        [VMEM] * (groups + blocks) + [HBM],
         [
             pltpu.VMEM((blocks, head_cols // head_size * drafts, head_size), jnp.float32),
             pltpu.VMEM((2 * blocks, 128, head_size), jnp.float32),
@@ -464,7 +436,8 @@
         ],
         4 * span * head_cols * cache_size,
         320 * blocks * cache_size * head_size,
-    )(*parts, *caches)
+        40 * MIB,
+    )(*parts, *caches, w_query)
     gathered = lax.all_gather(mixed, GROUP, axis=0, tiled=False)
     out_rows, out_part = call(
         functools.partial(out_rank_kernel, owned),
@@ -476,7 +449,7 @@
     )(gathered, jnp.transpose(shrink_out, (0, 2, 1)).reshape(-1, head_cols), slots)
     out_ranks = exchange(out_part)
     out_cols = w_out.shape[1]
-    out_total = product(out_rows, w_out)
+    out_total = product(out_rows, w_out, 0, head_cols)
     leaving = call(
         functools.partial(out_grow_kernel, sizes, width),
         [shape((drafts, groups, out_cols))] * blocks,

time: 93.1 us -> 89.3 us (0.959)
  Pallas kernels: 20.9 us -> 16 us
  local copies, waits for them, and re-layouts: 14 us -> 16 us
    pallas_call x3, Pallas kernels: 11.1 us -> 6.08 us  [product(): call(functools.partial(product_kernel, first, depth), shape((rows.shape[0...]
    unnamed x28 -> x30, local copies, waits for them, and re-layouts: 14 us -> 16 us
  transfers between devices with their start and end apart: 14 -> 14, of which waited for: 5 -> 5; matrix products, arithmetic and copies ran while one was open for 0% -> 0% of each run, Pallas kernels for 15% -> 10%
where the time goes in v5:
time: 89.3 us; the launch traced here: 88.7 us
  starting transfers between devices  26.9 us (30%)
  waiting for transfers between devices  22.5 us (25%)
  local copies, waits for them, and re-layouts  16 us (18%)
  Pallas kernels  16 us (18%)
  blocking collectives  5.79 us (6%)
    ppermute x9, waiting for transfers between devices, over_tensor(): return lax.ppermute(value, 'tensor', route)  22.2 us
    unnamed x30, local copies, waits for them, and re-layouts  16 us
    ppermute x9, starting transfers between devices, over_tensor(): return lax.ppermute(value, 'tensor', route)  15.6 us
    all_to_all x2, starting transfers between devices, exchange(): return lax.all_to_all(value, EVERY, split_axis=0, concat_axis=0, tiled=True)  8.32 us
    pallas_call x3, Pallas kernels, product(): call(functools.partial(product_kernel, first, depth), shape((rows.shape[0...  6.08 us
    all_gather x1, blocking collectives, by_head(): gathered = lax.all_gather(mixed, GROUP, axis=0, tiled=False)  5.79 us
    pallas_call x1, Pallas kernels, by_head(): call(functools.partial(attend_kernel, blocks, drafts, groups, cache_size)...  2.99 us
    ppermute x3, starting transfers between devices, over_group(): return lax.ppermute(value, GROUP, route)  2.97 us
  transfers between devices with their start and end apart: 14, of which 5 were waited for; matrix products, arithmetic and copies ran while one was open for 0% of the time, Pallas kernels for 10%

profile of v5, /device:TPU:0, one launch (start us, length us, event | category | flops | bytes accessed | tf_op | source)
XLA Modules:
  0.0 88.7 jit_solution(17543481625000195119)
XLA Ops:
  0.0 5.0 %collective-permute-start.2 = (bf16[3,4,4096]{2,1,0:T(4,128)(2,1)}, bf16[3,4,4096]{2,1,0:T(4,128)(2,1)S(1)}, u32[]{:S(2)}, u32[]{:S(2)}) collective-permute-start(bf16[3,4,4096]{2,1,0:T(4,128)(2,1)} %bitcast.19), channel_id=1, source_target_pairs={{0,12},{4,0},{8,4},{12,8},{1,13},{5,1},{9,5},{13,9},{2,14},{6,2},{... | collective-permute-start | bytes 294920 | tf_op jit(solution)/shard_map/ppermute | solution.py:379
  5.0 0.0 collective-permute-start.1
  5.1 1.0 %collective-permute-start = (bf16[3,4,4096]{2,1,0:T(4,128)(2,1)}, bf16[3,4,4096]{2,1,0:T(4,128)(2,1)S(1)}, u32[]{:S(2)}, u32[]{:S(2)}) collective-permute-start(bf16[3,4,4096]{2,1,0:T(4,128)(2,1)} %bitcast.21), channel_id=1, source_target_pairs={{0,4},{4,8},{8,12},{12,0},{1,5},{5,9},{9,13},{13,1},{2,6},{6,10},{... | collective-permute-start | bytes 294920 | tf_op jit(solution)/shard_map/ppermute | solution.py:379
  6.7 1.0 %copy-done.6 = bf16[1,4,512,128]{3,2,1,0:T(8,128)(2,1)S(1)} copy-done((bf16[1,4,512,128]{3,2,1,0:T(8,128)(2,1)S(1)}, bf16[1,4,512,128]{3,2,1,0:T(8,128)(2,1)}, u32[]{:S(2)}) %copy-start.6) | copy-done | bytes 524312
  7.8 1.0 %copy-done.7 = bf16[1,4,512,128]{3,2,1,0:T(8,128)(2,1)S(1)} copy-done((bf16[1,4,512,128]{3,2,1,0:T(8,128)(2,1)S(1)}, bf16[1,4,512,128]{3,2,1,0:T(8,128)(2,1)}, u32[]{:S(2)}) %copy-start.7) | copy-done | bytes 524312
  8.8 0.7 copy-done.13
  9.5 0.7 copy-done.14
  10.1 1.9 %shard_map.154 = (bf16[1040,128]{1,0:T(8,128)(2,1)S(1)}, bf16[1040,128]{1,0:T(8,128)(2,1)}, bf16[1040,128]{1,0:T(8,128)(2,1)}, bf16[1040,128]{1,0:T(8,128)(2,1)}, s32[48,128]{1,0:T(8,128)S(1)}) custom-call(s32[16]{0:T(128)S(1)} %copy-done.13, s32[16]{0:T(128)S(1)} %copy-done.14, s32[1]{0:T(128)S(6)} %copy.17.length_ref, ...), custom_call_target="tpu_custom_call" | custom-call | bytes 83886080 | tf_op jit(solution)/shard_map/pallas_call | solution.py:217
  12.1 0.0 collective-permute-done.2.refs_3_
  12.1 1.9 %collective-permute-done.1.refs_2_ = bf16[3,4,4096]{2,1,0:T(4,128)(2,1)S(1)} collective-permute-done((bf16[3,4,4096]{2,1,0:T(4,128)(2,1)}, bf16[3,4,4096]{2,1,0:T(4,128)(2,1)S(1)}, u32[]{:S(2)}, u32[]{:S(2)}) %collective-permute-start.1) | collective-permute-done | bytes 98336 | tf_op jit(solution)/shard_map/ppermute | solution.py:379
  14.0 0.0 collective-permute-done.refs_1_
  14.0 1.9 %shard_map.155 = (bf16[48,4096]{1,0:T(8,128)(2,1)S(1)}, bf16[16,48,128]{2,1,0:T(8,128)(2,1)}) custom-call(bf16[3,4,4096]{2,1,0:T(4,128)(2,1)S(1)} %bitcast.22, bf16[3,4,4096]{2,1,0:T(4,128)(2,1)S(1)} %collective-permute-done.refs_1_, bf16[3,4,4096]{2,1,0:T(4,128)(2,1)S(1)} %collective-permute-done.1.refs_2_, ...), custom_call_target="tpu_custom_call" | custom-call | tf_op jit(solution)/shard_map/pallas_call | solution.py:397
  16.0 4.6 %all-to-all-start = ((bf16[16,48,128]{2,1,0:T(8,128)(2,1)}), bf16[16,48,128]{2,1,0:T(8,128)(2,1)S(1)}, u32[]{:S(2)}, u32[]{:S(2)}) async-start(bf16[16,48,128]{2,1,0:T(8,128)(2,1)} %get-tuple-element.28), calls=%async_computation | async-start | bytes 393216 | tf_op jit(solution)/shard_map/all_to_all | solution.py:386
  20.5 1.9 %collective-permute-start.6 = (bf16[1040,128]{1,0:T(8,128)(2,1)}, bf16[1040,128]{1,0:T(8,128)(2,1)}, u32[]{:S(2)}, u32[]{:S(2)}) collective-permute-start(bf16[1040,128]{1,0:T(8,128)(2,1)} %get-tuple-element.34), channel_id=1, source_target_pairs={{0,4},{4,8},{8,12},{12,0},{1,5},{5,9},{9,13},{13,1},{2,6},{6,10},{... | collective-permute-start | bytes 798728 | tf_op jit(solution)/shard_map/ppermute | solution.py:379
  22.5 2.0 %collective-permute-start.8 = (bf16[1040,128]{1,0:T(8,128)(2,1)}, bf16[1040,128]{1,0:T(8,128)(2,1)}, u32[]{:S(2)}, u32[]{:S(2)}) collective-permute-start(bf16[1040,128]{1,0:T(8,128)(2,1)} %get-tuple-element.36), channel_id=1, source_target_pairs={{0,12},{4,0},{8,4},{12,8},{1,13},{5,1},{9,5},{13,9},{2,14},{6,2},{... | collective-permute-start | bytes 798728 | tf_op jit(solution)/shard_map/ppermute | solution.py:379
  24.4 5.8 %copy-done = bf16[4096,2048]{1,0:T(8,128)(2,1)S(1)} copy-done((bf16[4096,2048]{1,0:T(8,128)(2,1)S(1)}, bf16[4096,2048]{1,0:T(8,128)(2,1)}, u32[]{:S(2)}) %copy-start) | copy-done | bytes 16777240
  30.2 1.5 %shard_map.156.refs_0_ = f32[48,2048]{1,0:T(8,128)S(1)} custom-call(bf16[48,4096]{1,0:T(8,128)(2,1)S(1)} %get-tuple-element.25.rows_ref, bf16[4096,2048]{1,0:T(8,128)(2,1)S(1)} %copy-done), custom_call_target="tpu_custom_call" | custom-call | tf_op jit(solution)/shard_map/pallas_call | solution.py:146
  31.8 1.0 %collective-permute-start.7 = (bf16[1040,128]{1,0:T(8,128)(2,1)}, bf16[1040,128]{1,0:T(8,128)(2,1)}, u32[]{:S(2)}, u32[]{:S(2)}) collective-permute-start(bf16[1040,128]{1,0:T(8,128)(2,1)} %get-tuple-element.35), channel_id=1, source_target_pairs={{0,8},{4,12},{8,0},{12,4},{1,9},{5,13},{9,1},{13,5},{2,10},{6,14},... | collective-permute-start | bytes 798728 | tf_op jit(solution)/shard_map/ppermute | solution.py:379
  32.7 1.6 %shard_map.157.total_ref = f32[48,2048]{1,0:T(8,128)S(1)} custom-call(bf16[48,4096]{1,0:T(8,128)(2,1)S(1)} %get-tuple-element.25.rows_ref, bf16[4096,2048]{1,0:T(8,128)(2,1)S(1)} %copy-done, f32[48,2048]{1,0:T(8,128)S(1)} %shard_map.156.refs_0_), custom_call_target="tpu_custom_call" | custom-call | tf_op jit(solution)/shard_map/pallas_call | solution.py:146
  34.3 0.0 all-to-all-done.ranks_ref
  34.4 0.0 copy-start.8
  34.4 1.0 %copy-done.8 = bf16[4,32,2048]{2,1,0:T(8,128)(2,1)S(1)} copy-done((bf16[4,32,2048]{2,1,0:T(8,128)(2,1)S(1)}, bf16[4,32,2048]{2,1,0:T(8,128)(2,1)}, u32[]{:S(2)}) %copy-start.8) | copy-done | bytes 524312
  35.4 1.2 %shard_map.158 = (bf16[4,3,2304]{2,1,0:T(4,128)(2,1)S(1)}, bf16[4,3,2304]{2,1,0:T(4,128)(2,1)S(1)}, bf16[4,3,2304]{2,1,0:T(4,128)(2,1)S(1)}, bf16[4,3,2304]{2,1,0:T(4,128)(2,1)S(1)}) custom-call(f32[48,2048]{1,0:T(8,128)S(1)} %shard_map.157.total_ref, bf16[48,4096]{1,0:T(8,128)(2,1)S(1)} %get-tuple-element.25.rows_ref, bf16[4096,128]{1,0:T(8,128)(2,1)S(1)} %copy-done.3, ...), custom_call_target="tpu_custom_call" | custom-call | tf_op jit(solution)/shard_map/pallas_call | solution.py:412
  36.6 0.1 collective-permute-start.3
  36.7 1.5 %collective-permute-start.4 = (bf16[4,3,2304]{2,1,0:T(4,128)(2,1)S(1)}, bf16[4,3,2304]{2,1,0:T(4,128)(2,1)S(1)}, u32[]{:S(2)}, u32[]{:S(2)}) collective-permute-start(bf16[4,3,2304]{2,1,0:T(4,128)(2,1)S(1)} %get-tuple-element.31), channel_id=1, source_target_pairs={{0,2},{1,3},{2,0},{3,1},{4,6},{5,7},{6,4},{7,5},{8,10},{9,11},{10,... | collective-permute-start | bytes 165896 | tf_op jit(solution)/shard_map/ppermute | solution.py:383
  38.2 0.0 collective-permute-done.6.refs_5_
  38.2 1.4 %collective-permute-start.5 = (bf16[4,3,2304]{2,1,0:T(4,128)(2,1)S(1)}, bf16[4,3,2304]{2,1,0:T(4,128)(2,1)S(1)}, u32[]{:S(2)}, u32[]{:S(2)}) collective-permute-start(bf16[4,3,2304]{2,1,0:T(4,128)(2,1)S(1)} %get-tuple-element.32), channel_id=1, source_target_pairs={{0,3},{1,0},{2,1},{3,2},{4,7},{5,4},{6,5},{7,6},{8,11},{9,8},{10,9... | collective-permute-start | bytes 165896 | tf_op jit(solution)/shard_map/ppermute | solution.py:383
  39.6 0.0 collective-permute-done.8.refs_7_
  39.6 12.1 %collective-permute-done.7.refs_6_ = bf16[1040,128]{1,0:T(8,128)(2,1)} collective-permute-done((bf16[1040,128]{1,0:T(8,128)(2,1)}, bf16[1040,128]{1,0:T(8,128)(2,1)}, u32[]{:S(2)}, u32[]{:S(2)}) %collective-permute-start.7) | collective-permute-done | bytes 266272 | tf_op jit(solution)/shard_map/ppermute | solution.py:379
  51.7 0.0 collective-permute-done.3.refs_1_
  51.7 0.0 collective-permute-done.4.refs_2_
  51.7 0.0 collective-permute-done.5.refs_3_
  51.7 0.0 copy-start.5
  51.7 3.0 %shard_map.159 = bf16[12,2048]{1,0:T(8,128)(2,1)S(1)} custom-call(bf16[4,3,2304]{2,1,0:T(4,128)(2,1)S(1)} %get-tuple-element.29.refs_0_, bf16[4,3,2304]{2,1,0:T(4,128)(2,1)S(1)} %collective-permute-done.3.refs_1_, bf16[4,3,2304]{2,1,0:T(4,128)(2,1)S(1)} %collective-permute-done.4.refs_2_, bf16[4,3,2304]{2,1,0:T(4,128)(2,1)S(1)} %collective-permute-done.5.refs_3_, ...), custom_call_target="tpu_custom_call" | custom-call | flops 50331648 | bytes 83886080 | tf_op jit(solution)/shard_map/pallas_call | solution.py:428
  54.7 5.8 %all-gather.1.got_ref = bf16[4,12,2048]{2,1,0:T(8,128)(2,1)S(1)} all-gather(bf16[1,12,2048]{2,1,0:T(8,128)(2,1)S(1)} %bitcast.18), channel_id=2, replica_groups=mesh['parts'=2,'tensor'=4,'dp'=2,'pipe'=2] {'dp','pipe'}, dimensions={0}, use_global_device_ids=true | all-gather | bytes 245760 | tf_op jit(solution)/shard_map/all_gather | solution.py:441
  60.5 1.1 %shard_map.160 = (bf16[48,2048]{1,0:T(8,128)(2,1)S(1)}, bf16[16,48,128]{2,1,0:T(8,128)(2,1)}) custom-call(bf16[4,12,2048]{2,1,0:T(8,128)(2,1)S(1)} %all-gather.1.got_ref, bf16[128,2048]{1,0:T(8,128)(2,1)S(1)} %bitcast.17, s32[48,128]{1,0:T(8,128)S(1)} %get-tuple-element.24.refs_5_.slots_ref), custom_call_target="tpu_custom_call" | custom-call | flops 25165824 | bytes 917504 | tf_op jit(solution)/shard_map/pallas_call | solution.py:442
  61.6 3.7 %all-to-all-start.1 = ((bf16[16,48,128]{2,1,0:T(8,128)(2,1)}), bf16[16,48,128]{2,1,0:T(8,128)(2,1)S(1)}, u32[]{:S(2)}, u32[]{:S(2)}) async-start(bf16[16,48,128]{2,1,0:T(8,128)(2,1)} %get-tuple-element.38), calls=%async_computation.1 | async-start | bytes 393216 | tf_op jit(solution)/shard_map/all_to_all | solution.py:386
  65.4 0.0 copy-start.1
  65.4 5.8 %copy-done.1 = bf16[2048,4096]{1,0:T(8,128)(2,1)S(1)} copy-done((bf16[2048,4096]{1,0:T(8,128)(2,1)S(1)}, bf16[2048,4096]{1,0:T(8,128)(2,1)}, u32[]{:S(2)}) %copy-start.1) | copy-done | bytes 16777240
  71.2 3.0 %shard_map.161.total_ref = f32[48,4096]{1,0:T(8,128)S(1)} custom-call(bf16[48,2048]{1,0:T(8,128)(2,1)S(1)} %get-tuple-element.37.rows_ref, bf16[2048,4096]{1,0:T(8,128)(2,1)S(1)} %copy-done.1), custom_call_target="tpu_custom_call" | custom-call | tf_op jit(solution)/shard_map/pallas_call | solution.py:146
  74.1 0.2 all-to-all-done.1.ranks_ref
  74.4 0.7 shard_map.162
  75.1 3.6 %collective-permute-start.9 = (bf16[3,4,4096]{2,1,0:T(4,128)(2,1)S(1)}, bf16[3,4,4096]{2,1,0:T(4,128)(2,1)S(1)}, u32[]{:S(2)}, u32[]{:S(2)}) collective-permute-start(bf16[3,4,4096]{2,1,0:T(4,128)(2,1)S(1)} %get-tuple-element.40), channel_id=1, source_target_pairs={{0,12},{4,0},{8,4},{12,8},{1,13},{5,1},{9,5},{13,9},{2,14},{6,2},{... | collective-permute-start | bytes 294920 | tf_op jit(solution)/shard_map/ppermute | solution.py:379
  78.7 0.0 collective-permute-start.10
  78.7 1.1 %collective-permute-start.11 = (bf16[3,4,4096]{2,1,0:T(4,128)(2,1)S(1)}, bf16[3,4,4096]{2,1,0:T(4,128)(2,1)S(1)}, u32[]{:S(2)}, u32[]{:S(2)}) collective-permute-start(bf16[3,4,4096]{2,1,0:T(4,128)(2,1)S(1)} %get-tuple-element.42), channel_id=1, source_target_pairs={{0,4},{4,8},{8,12},{12,0},{1,5},{5,9},{9,13},{13,1},{2,6},{6,10},{... | collective-permute-start | bytes 294920 | tf_op jit(solution)/shard_map/ppermute | solution.py:379
  79.8 2.1 %collective-permute-done.9 = bf16[3,4,4096]{2,1,0:T(4,128)(2,1)S(1)} collective-permute-done((bf16[3,4,4096]{2,1,0:T(4,128)(2,1)S(1)}, bf16[3,4,4096]{2,1,0:T(4,128)(2,1)S(1)}, u32[]{:S(2)}, u32[]{:S(2)}) %collective-permute-start.9) | collective-permute-done | bytes 98336 | tf_op jit(solution)/shard_map/ppermute | solution.py:379
  81.9 6.1 %collective-permute-done.10 = bf16[3,4,4096]{2,1,0:T(4,128)(2,1)S(1)} collective-permute-done((bf16[3,4,4096]{2,1,0:T(4,128)(2,1)S(1)}, bf16[3,4,4096]{2,1,0:T(4,128)(2,1)S(1)}, u32[]{:S(2)}, u32[]{:S(2)}) %collective-permute-start.10) | collective-permute-done | bytes 98336 | tf_op jit(solution)/shard_map/ppermute | solution.py:379
  88.0 0.7 fusion
  (21 shorter events, 0.0 us)
Async XLA Ops:
  0.0 12.1 %collective-permute-start.2 = (bf16[3,4,4096]{2,1,0:T(4,128)(2,1)}, bf16[3,4,4096]{2,1,0:T(4,128)(2,1)S(1)}, u32[]{:S(2)}, u32[]{:S(2)}) collective-permute-start(bf16[3,4,4096]{2,1,0:T(4,128)(2,1)} %bitcast.19), channel_id=1, source_target_pairs={{0,12},{4,0},{8,4},{12,8},{1,13},{5,1},{9,5},{13,9},{2,14},{6,2},{... | collective-permute-start | bytes 294920 | tf_op jit(solution)/shard_map/ppermute | solution.py:379
  5.0 9.0 %collective-permute-start.1 = (bf16[3,4,4096]{2,1,0:T(4,128)(2,1)}, bf16[3,4,4096]{2,1,0:T(4,128)(2,1)S(1)}, u32[]{:S(2)}, u32[]{:S(2)}) collective-permute-start(bf16[3,4,4096]{2,1,0:T(4,128)(2,1)} %bitcast.20), channel_id=1, source_target_pairs={{0,8},{4,12},{8,0},{12,4},{1,9},{5,13},{9,1},{13,5},{2,10},{6,14},... | collective-permute-start | bytes 294920 | tf_op jit(solution)/shard_map/ppermute | solution.py:379
  5.1 9.0 %collective-permute-start = (bf16[3,4,4096]{2,1,0:T(4,128)(2,1)}, bf16[3,4,4096]{2,1,0:T(4,128)(2,1)S(1)}, u32[]{:S(2)}, u32[]{:S(2)}) collective-permute-start(bf16[3,4,4096]{2,1,0:T(4,128)(2,1)} %bitcast.21), channel_id=1, source_target_pairs={{0,4},{4,8},{8,12},{12,0},{1,5},{5,9},{9,13},{13,1},{2,6},{6,10},{... | collective-permute-start | bytes 294920 | tf_op jit(solution)/shard_map/ppermute | solution.py:379
  6.7 1.0 %copy-start.6 = (bf16[1,4,512,128]{3,2,1,0:T(8,128)(2,1)S(1)}, bf16[1,4,512,128]{3,2,1,0:T(8,128)(2,1)}, u32[]{:S(2)}) copy-start(bf16[1,4,512,128]{3,2,1,0:T(8,128)(2,1)} %keys_ref.1) | copy-start | bytes 1572868
  7.8 1.0 %copy-start.7 = (bf16[1,4,512,128]{3,2,1,0:T(8,128)(2,1)S(1)}, bf16[1,4,512,128]{3,2,1,0:T(8,128)(2,1)}, u32[]{:S(2)}) copy-start(bf16[1,4,512,128]{3,2,1,0:T(8,128)(2,1)} %values_ref.1) | copy-start | bytes 1572868
  8.8 0.7 copy-start.13
  9.5 0.7 copy-start.14
  10.1 3.9 %copy-start.2 = (bf16[4,4096,96]{1,2,0:T(8,128)(2,1)S(1)}, bf16[4,4096,96]{1,2,0:T(8,128)(2,1)}, u32[]{:S(2)}) copy-start(bf16[4,4096,96]{1,2,0:T(8,128)(2,1)} %param.21) | copy-start | bytes 9437188
  10.1 3.9 %copy-start.10 = (bf16[4,3,4096]{2,0,1:T(4,128)(2,1)S(1)}, bf16[4,3,4096]{2,0,1:T(4,128)(2,1)}, u32[]{:S(2)}) copy-start(bf16[4,3,4096]{2,0,1:T(4,128)(2,1)} %param.16) | copy-start | bytes 294916
  16.0 18.3 %all-to-all-start = ((bf16[16,48,128]{2,1,0:T(8,128)(2,1)}), bf16[16,48,128]{2,1,0:T(8,128)(2,1)S(1)}, u32[]{:S(2)}, u32[]{:S(2)}) async-start(bf16[16,48,128]{2,1,0:T(8,128)(2,1)} %get-tuple-element.28), calls=%async_computation | async-start | bytes 393216 | tf_op jit(solution)/shard_map/all_to_all | solution.py:386
  20.5 17.7 %collective-permute-start.6 = (bf16[1040,128]{1,0:T(8,128)(2,1)}, bf16[1040,128]{1,0:T(8,128)(2,1)}, u32[]{:S(2)}, u32[]{:S(2)}) collective-permute-start(bf16[1040,128]{1,0:T(8,128)(2,1)} %get-tuple-element.34), channel_id=1, source_target_pairs={{0,4},{4,8},{8,12},{12,0},{1,5},{5,9},{9,13},{13,1},{2,6},{6,10},{... | collective-permute-start | bytes 798728 | tf_op jit(solution)/shard_map/ppermute | solution.py:379
  22.5 17.1 %collective-permute-start.8 = (bf16[1040,128]{1,0:T(8,128)(2,1)}, bf16[1040,128]{1,0:T(8,128)(2,1)}, u32[]{:S(2)}, u32[]{:S(2)}) collective-permute-start(bf16[1040,128]{1,0:T(8,128)(2,1)} %get-tuple-element.36), channel_id=1, source_target_pairs={{0,12},{4,0},{8,4},{12,8},{1,13},{5,1},{9,5},{13,9},{2,14},{6,2},{... | collective-permute-start | bytes 798728 | tf_op jit(solution)/shard_map/ppermute | solution.py:379
  24.4 5.8 %copy-start = (bf16[4096,2048]{1,0:T(8,128)(2,1)S(1)}, bf16[4096,2048]{1,0:T(8,128)(2,1)}, u32[]{:S(2)}) copy-start(bf16[4096,2048]{1,0:T(8,128)(2,1)} %refs_8_.1) | copy-start | bytes 50331652
  30.2 4.1 %copy-start.3 = (bf16[4096,128]{1,0:T(8,128)(2,1)S(1)}, bf16[4096,128]{1,0:T(8,128)(2,1)}, u32[]{:S(2)}) copy-start(bf16[4096,128]{1,0:T(8,128)(2,1)} %key_ref.1) | copy-start | bytes 3145732
  30.2 4.1 %copy-start.4 = (bf16[4096,128]{1,0:T(8,128)(2,1)S(1)}, bf16[4096,128]{1,0:T(8,128)(2,1)}, u32[]{:S(2)}) copy-start(bf16[4096,128]{1,0:T(8,128)(2,1)} %value_ref.1) | copy-start | bytes 3145732
  30.2 4.1 %copy-start.11 = (bf16[4,32,128]{2,1,0:T(8,128)(2,1)S(1)}, bf16[4,32,128]{2,1,0:T(8,128)(2,1)}, u32[]{:S(2)}) copy-start(bf16[4,32,128]{2,1,0:T(8,128)(2,1)} %param.23) | copy-start | bytes 98308
  30.2 4.1 %copy-start.12 = (bf16[4,32,128]{2,1,0:T(8,128)(2,1)S(1)}, bf16[4,32,128]{2,1,0:T(8,128)(2,1)}, u32[]{:S(2)}) copy-start(bf16[4,32,128]{2,1,0:T(8,128)(2,1)} %param.24) | copy-start | bytes 98308
  31.8 20.0 %collective-permute-start.7 = (bf16[1040,128]{1,0:T(8,128)(2,1)}, bf16[1040,128]{1,0:T(8,128)(2,1)}, u32[]{:S(2)}, u32[]{:S(2)}) collective-permute-start(bf16[1040,128]{1,0:T(8,128)(2,1)} %get-tuple-element.35), channel_id=1, source_target_pairs={{0,8},{4,12},{8,0},{12,4},{1,9},{5,13},{9,1},{13,5},{2,10},{6,14},... | collective-permute-start | bytes 798728 | tf_op jit(solution)/shard_map/ppermute | solution.py:379
  34.4 1.0 %copy-start.8 = (bf16[4,32,2048]{2,1,0:T(8,128)(2,1)S(1)}, bf16[4,32,2048]{2,1,0:T(8,128)(2,1)}, u32[]{:S(2)}) copy-start(bf16[4,32,2048]{2,1,0:T(8,128)(2,1)} %param.22) | copy-start | bytes 1572868
  35.4 25.1 %copy-start.9 = (bf16[4,2048,32]{1,2,0:T(8,128)(2,1)S(1)}, bf16[4,2048,32]{1,2,0:T(8,128)(2,1)}, u32[]{:S(2)}) copy-start(bf16[4,2048,32]{1,2,0:T(8,128)(2,1)} %param.25) | copy-start | bytes 1572868
  36.6 15.1 %collective-permute-start.3 = (bf16[4,3,2304]{2,1,0:T(4,128)(2,1)S(1)}, bf16[4,3,2304]{2,1,0:T(4,128)(2,1)S(1)}, u32[]{:S(2)}, u32[]{:S(2)}) collective-permute-start(bf16[4,3,2304]{2,1,0:T(4,128)(2,1)S(1)} %get-tuple-element.30), channel_id=1, source_target_pairs={{0,1},{1,2},{2,3},{3,0},{4,5},{5,6},{6,7},{7,4},{8,9},{9,10},{10,1... | collective-permute-start | bytes 165896 | tf_op jit(solution)/shard_map/ppermute | solution.py:383
  36.7 15.1 %collective-permute-start.4 = (bf16[4,3,2304]{2,1,0:T(4,128)(2,1)S(1)}, bf16[4,3,2304]{2,1,0:T(4,128)(2,1)S(1)}, u32[]{:S(2)}, u32[]{:S(2)}) collective-permute-start(bf16[4,3,2304]{2,1,0:T(4,128)(2,1)S(1)} %get-tuple-element.31), channel_id=1, source_target_pairs={{0,2},{1,3},{2,0},{3,1},{4,6},{5,7},{6,4},{7,5},{8,10},{9,11},{10,... | collective-permute-start | bytes 165896 | tf_op jit(solution)/shard_map/ppermute | solution.py:383
  38.2 13.5 %collective-permute-start.5 = (bf16[4,3,2304]{2,1,0:T(4,128)(2,1)S(1)}, bf16[4,3,2304]{2,1,0:T(4,128)(2,1)S(1)}, u32[]{:S(2)}, u32[]{:S(2)}) collective-permute-start(bf16[4,3,2304]{2,1,0:T(4,128)(2,1)S(1)} %get-tuple-element.32), channel_id=1, source_target_pairs={{0,3},{1,0},{2,1},{3,2},{4,7},{5,4},{6,5},{7,6},{8,11},{9,8},{10,9... | collective-permute-start | bytes 165896 | tf_op jit(solution)/shard_map/ppermute | solution.py:383
  51.7 22.7 %copy-start.5 = (bf16[4,32,4096]{2,1,0:T(8,128)(2,1)S(1)}, bf16[4,32,4096]{2,1,0:T(8,128)(2,1)}, u32[]{:S(2)}) copy-start(bf16[4,32,4096]{2,1,0:T(8,128)(2,1)} %param.26) | copy-start | bytes 3145732
  61.6 12.7 %all-to-all-start.1 = ((bf16[16,48,128]{2,1,0:T(8,128)(2,1)}), bf16[16,48,128]{2,1,0:T(8,128)(2,1)S(1)}, u32[]{:S(2)}, u32[]{:S(2)}) async-start(bf16[16,48,128]{2,1,0:T(8,128)(2,1)} %get-tuple-element.38), calls=%async_computation.1 | async-start | bytes 393216 | tf_op jit(solution)/shard_map/all_to_all | solution.py:386
  65.4 5.8 %copy-start.1 = (bf16[2048,4096]{1,0:T(8,128)(2,1)S(1)}, bf16[2048,4096]{1,0:T(8,128)(2,1)}, u32[]{:S(2)}) copy-start(bf16[2048,4096]{1,0:T(8,128)(2,1)} %weight_ref.5) | copy-start | bytes 50331652
  75.1 6.8 %collective-permute-start.9 = (bf16[3,4,4096]{2,1,0:T(4,128)(2,1)S(1)}, bf16[3,4,4096]{2,1,0:T(4,128)(2,1)S(1)}, u32[]{:S(2)}, u32[]{:S(2)}) collective-permute-start(bf16[3,4,4096]{2,1,0:T(4,128)(2,1)S(1)} %get-tuple-element.40), channel_id=1, source_target_pairs={{0,12},{4,0},{8,4},{12,8},{1,13},{5,1},{9,5},{13,9},{2,14},{6,2},{... | collective-permute-start | bytes 294920 | tf_op jit(solution)/shard_map/ppermute | solution.py:379
  78.7 9.3 %collective-permute-start.10 = (bf16[3,4,4096]{2,1,0:T(4,128)(2,1)S(1)}, bf16[3,4,4096]{2,1,0:T(4,128)(2,1)S(1)}, u32[]{:S(2)}, u32[]{:S(2)}) collective-permute-start(bf16[3,4,4096]{2,1,0:T(4,128)(2,1)S(1)} %get-tuple-element.41), channel_id=1, source_target_pairs={{0,8},{4,12},{8,0},{12,4},{1,9},{5,13},{9,1},{13,5},{2,10},{6,14},... | collective-permute-start | bytes 294920 | tf_op jit(solution)/shard_map/ppermute | solution.py:379
  78.7 9.3 %collective-permute-start.11 = (bf16[3,4,4096]{2,1,0:T(4,128)(2,1)S(1)}, bf16[3,4,4096]{2,1,0:T(4,128)(2,1)S(1)}, u32[]{:S(2)}, u32[]{:S(2)}) collective-permute-start(bf16[3,4,4096]{2,1,0:T(4,128)(2,1)S(1)} %get-tuple-element.42), channel_id=1, source_target_pairs={{0,4},{4,8},{8,12},{12,0},{1,5},{5,9},{9,13},{13,1},{2,6},{6,10},{... | collective-permute-start | bytes 294920 | tf_op jit(solution)/shard_map/ppermute | solution.py:379

commit v6 on v5

--- a/solution.py
+++ b/solution.py
@@ -127,8 +127,8 @@
     return jnp.where(slot == place, wide, 0.0).astype(jnp.bfloat16)
 
 
-def product_kernel(first, depth, rows_ref, weight_ref, *refs):
-    *sums, total_ref = refs
+def product_kernel(first, depth, added, rows_ref, weight_ref, *refs):
+    sums, total_ref = refs[:added], refs[-1]
     width = total_ref.shape[1]
     step = width if width % 1024 else 1024
     for start in range(0, width, step):
@@ -141,17 +141,17 @@
         total_ref[:, start : start + step] = part
 
 
-def product(rows, weight, first, depth, *sums):
+def product(rows, weight, first, depth, sums=(), after=()):
     width = weight.shape[1]
     return call(
-        functools.partial(product_kernel, first, depth),
+        functools.partial(product_kernel, first, depth, len(sums)),
         shape((rows.shape[0], width), jnp.float32),
-        [VMEM] * (2 + len(sums)),
-    )(rows, weight, *sums)
+        [VMEM] * (2 + len(sums)) + [HBM] * len(after),
+    )(rows, weight, *sums, *after)
 
 
 def pack_kernel(sizes, ids_ref, pool_ref, length_ref, keys_ref, values_ref, *refs):
-    refs = refs[2:]
+    refs = refs[6:]
     groups, blocks, drafts = sizes
     outs = refs[:blocks]
     slots_ref, extra_f32, extra_ref, sems = refs[blocks:]
@@ -217,7 +217,7 @@
     return pl.pallas_call(
         functools.partial(pack_kernel, sizes),
         out_shape=outs + [shape((groups * blocks * drafts, 128), jnp.int32)],
-        in_specs=[smem, smem, smem, VMEM, VMEM] + [HBM] * 2,
+        in_specs=[smem, smem, smem, VMEM, VMEM] + [HBM] * 6,
         out_specs=[HBM] * blocks + [VMEM],
         scratch_shapes=[
             pltpu.VMEM((used, head_size), jnp.float32),
@@ -226,7 +226,7 @@
         ],
         cost_estimate=pl.CostEstimate(flops=0, bytes_accessed=320 * keys.size, transcendentals=0),
         compiler_params=pltpu.CompilerParams(vmem_limit_bytes=40 * MIB),
-    )(ids, pool, lengths, keys, values, *[later] * 2)
+    )(ids, pool, lengths, keys, values, *[later] * 6)
 
 
 def grow_kernel(sizes, width, total_ref, rows_ref, key_ref, value_ref, slots_ref, ranks_ref, *rest):
@@ -259,7 +259,7 @@
 def attend_kernel(blocks, drafts, groups, cache_size, *refs):
     parts = refs[:groups]
     caches = refs[groups : groups + blocks]
-    _, mixed_ref, query_s, fresh_s, out_s = refs[groups + blocks :]
+    mixed_ref, query_s, fresh_s, out_s = refs[-4:]
     head_size = caches[0].shape[1]
     cols = parts[0].shape[2]
     heads = cols // head_size - 2
@@ -402,11 +402,12 @@
     )(*pieces, shrink_in, slots)
     ranks = exchange(rank_part)
     half = features // 2
+    early = [caches[shift] for shift in sorted(caches)]
     total = product(rows, w_query, 0, half)
     total, *late = lax.optimization_barrier((total, *messages[2:3]))
     for message in late:
         caches[2] = over_tensor(message, 2)
-    total = product(rows, w_query, half, features - half, total)
+    total = product(rows, w_query, half, features - half, [total], early)
     caches = [messages[0]] + [caches[shift] for shift in range(1, blocks)]
     cols = total.shape[1] + w_key.shape[1] + w_value.shape[1]
     sent = call(
@@ -428,7 +429,7 @@
     mixed = call(
         functools.partial(attend_kernel, blocks, drafts, groups, cache_size),
         shape((span, head_cols)),
-        [VMEM] * (groups + blocks) + [HBM],
+        [VMEM] * (groups + blocks) + [HBM] * 5,
         [
             pltpu.VMEM((blocks, head_cols // head_size * drafts, head_size), jnp.float32),
             pltpu.VMEM((2 * blocks, 128, head_size), jnp.float32),
@@ -437,7 +438,7 @@
         4 * span * head_cols * cache_size,
         320 * blocks * cache_size * head_size,
         40 * MIB,
-    )(*parts, *caches, w_query)
+    )(*parts, *caches, *[w_query] * 5)
     gathered = lax.all_gather(mixed, GROUP, axis=0, tiled=False)
     out_rows, out_part = call(
         functools.partial(out_rank_kernel, owned),

time: 89.3 us -> 94.5 us (1.058)
  starting transfers between devices: 26.9 us -> 31.2 us
  waiting for transfers between devices: 22.5 us -> 21.5 us
    all_to_all x2, starting transfers between devices: 8.32 us -> 12.7 us  [exchange(): return lax.all_to_all(value, EVERY, split_axis=0, concat_axis=0, tiled=True)]
    unnamed x30 -> x34, local copies, waits for them, and re-layouts: 16 us -> 16.9 us
  transfers between devices with their start and end apart: 14 -> 14, of which waited for: 5 -> 7; matrix products, arithmetic and copies ran while one was open for 0% -> 0% of each run, Pallas kernels for 10% -> 11%
where the time goes in v6:
time: 94.5 us; the launch traced here: 93.9 us
  starting transfers between devices  31.2 us (33%)
  waiting for transfers between devices  21.5 us (23%)
  local copies, waits for them, and re-layouts  16.9 us (18%)
  Pallas kernels  16.7 us (18%)
  blocking collectives  5.92 us (6%)
    ppermute x9, waiting for transfers between devices, over_tensor(): return lax.ppermute(value, 'tensor', route)  21.3 us
    unnamed x34, local copies, waits for them, and re-layouts  16.9 us
    ppermute x9, starting transfers between devices, over_tensor(): return lax.ppermute(value, 'tensor', route)  15.6 us
    all_to_all x2, starting transfers between devices, exchange(): return lax.all_to_all(value, EVERY, split_axis=0, concat_axis=0, tiled=True)  12.7 us
    pallas_call x3, Pallas kernels, product(): call(functools.partial(product_kernel, first, depth, len(sums)), shape((r...  6.08 us
    all_gather x1, blocking collectives, by_head(): gathered = lax.all_gather(mixed, GROUP, axis=0, tiled=False)  5.92 us
    ppermute x3, starting transfers between devices, over_group(): return lax.ppermute(value, GROUP, route)  2.97 us
    pallas_call x1, Pallas kernels, by_head(): call(functools.partial(attend_kernel, blocks, drafts, groups, cache_size)...  2.8 us
  transfers between devices with their start and end apart: 14, of which 7 were waited for; matrix products, arithmetic and copies ran while one was open for 0% of the time, Pallas kernels for 11%

profile of v6, /device:TPU:0, one launch (start us, length us, event | category | flops | bytes accessed | tf_op | source)
XLA Modules:
  0.0 93.9 jit_solution(773403630488149205)
XLA Ops:
  0.0 5.0 %collective-permute-start.2 = (bf16[3,4,4096]{2,1,0:T(4,128)(2,1)}, bf16[3,4,4096]{2,1,0:T(4,128)(2,1)S(1)}, u32[]{:S(2)}, u32[]{:S(2)}) collective-permute-start(bf16[3,4,4096]{2,1,0:T(4,128)(2,1)} %bitcast.19), channel_id=1, source_target_pairs={{0,12},{4,0},{8,4},{12,8},{1,13},{5,1},{9,5},{13,9},{2,14},{6,2},{... | collective-permute-start | bytes 294920 | tf_op jit(solution)/shard_map/ppermute | solution.py:379
  5.0 0.0 collective-permute-start.1
  5.1 1.0 %collective-permute-start = (bf16[3,4,4096]{2,1,0:T(4,128)(2,1)}, bf16[3,4,4096]{2,1,0:T(4,128)(2,1)S(1)}, u32[]{:S(2)}, u32[]{:S(2)}) collective-permute-start(bf16[3,4,4096]{2,1,0:T(4,128)(2,1)} %bitcast.21), channel_id=1, source_target_pairs={{0,4},{4,8},{8,12},{12,0},{1,5},{5,9},{9,13},{13,1},{2,6},{6,10},{... | collective-permute-start | bytes 294920 | tf_op jit(solution)/shard_map/ppermute | solution.py:379
  6.7 1.0 %copy-done.6 = bf16[1,4,512,128]{3,2,1,0:T(8,128)(2,1)S(1)} copy-done((bf16[1,4,512,128]{3,2,1,0:T(8,128)(2,1)S(1)}, bf16[1,4,512,128]{3,2,1,0:T(8,128)(2,1)}, u32[]{:S(2)}) %copy-start.6) | copy-done | bytes 524312
  7.8 1.0 %copy-done.7 = bf16[1,4,512,128]{3,2,1,0:T(8,128)(2,1)S(1)} copy-done((bf16[1,4,512,128]{3,2,1,0:T(8,128)(2,1)S(1)}, bf16[1,4,512,128]{3,2,1,0:T(8,128)(2,1)}, u32[]{:S(2)}) %copy-start.7) | copy-done | bytes 524312
  8.8 0.7 copy-done.15
  9.5 0.7 copy-done.16
  10.1 1.9 %shard_map.154 = (bf16[1040,128]{1,0:T(8,128)(2,1)S(1)}, bf16[1040,128]{1,0:T(8,128)(2,1)}, bf16[1040,128]{1,0:T(8,128)(2,1)}, bf16[1040,128]{1,0:T(8,128)(2,1)}, s32[48,128]{1,0:T(8,128)S(1)}) custom-call(s32[16]{0:T(128)S(1)} %copy-done.15, s32[16]{0:T(128)S(1)} %copy-done.16, s32[1]{0:T(128)S(6)} %copy.17.length_ref, ...), custom_call_target="tpu_custom_call" | custom-call | bytes 83886080 | tf_op jit(solution)/shard_map/pallas_call | solution.py:217
  12.1 0.0 collective-permute-done.2.refs_3_
  12.1 1.9 %collective-permute-done.1.refs_2_ = bf16[3,4,4096]{2,1,0:T(4,128)(2,1)S(1)} collective-permute-done((bf16[3,4,4096]{2,1,0:T(4,128)(2,1)}, bf16[3,4,4096]{2,1,0:T(4,128)(2,1)S(1)}, u32[]{:S(2)}, u32[]{:S(2)}) %collective-permute-start.1) | collective-permute-done | bytes 98336 | tf_op jit(solution)/shard_map/ppermute | solution.py:379
  14.0 1.9 %shard_map.155 = (bf16[48,4096]{1,0:T(8,128)(2,1)S(1)}, bf16[16,48,128]{2,1,0:T(8,128)(2,1)}) custom-call(bf16[3,4,4096]{2,1,0:T(4,128)(2,1)S(1)} %bitcast.22, bf16[3,4,4096]{2,1,0:T(4,128)(2,1)S(1)} %collective-permute-done.refs_1_, bf16[3,4,4096]{2,1,0:T(4,128)(2,1)S(1)} %collective-permute-done.1.refs_2_, ...), custom_call_target="tpu_custom_call" | custom-call | tf_op jit(solution)/shard_map/pallas_call | solution.py:397
  16.0 4.6 %all-to-all-start = ((bf16[16,48,128]{2,1,0:T(8,128)(2,1)}), bf16[16,48,128]{2,1,0:T(8,128)(2,1)}, u32[]{:S(2)}, u32[]{:S(2)}) async-start(bf16[16,48,128]{2,1,0:T(8,128)(2,1)} %get-tuple-element.30), calls=%async_computation | async-start | bytes 393216 | tf_op jit(solution)/shard_map/all_to_all | solution.py:386
  20.6 1.9 %collective-permute-start.3 = (bf16[1040,128]{1,0:T(8,128)(2,1)}, bf16[1040,128]{1,0:T(8,128)(2,1)S(1)}, u32[]{:S(2)}, u32[]{:S(2)}) collective-permute-start(bf16[1040,128]{1,0:T(8,128)(2,1)} %get-tuple-element.28), channel_id=1, source_target_pairs={{0,4},{4,8},{8,12},{12,0},{1,5},{5,9},{9,13},{13,1},{2,6},{6,10},{... | collective-permute-start | bytes 798728 | tf_op jit(solution)/shard_map/ppermute | solution.py:379
  22.5 2.0 %collective-permute-start.4 = (bf16[1040,128]{1,0:T(8,128)(2,1)}, bf16[1040,128]{1,0:T(8,128)(2,1)S(1)}, u32[]{:S(2)}, u32[]{:S(2)}) collective-permute-start(bf16[1040,128]{1,0:T(8,128)(2,1)} %get-tuple-element.29), channel_id=1, source_target_pairs={{0,12},{4,0},{8,4},{12,8},{1,13},{5,1},{9,5},{13,9},{2,14},{6,2},{... | collective-permute-start | bytes 798728 | tf_op jit(solution)/shard_map/ppermute | solution.py:379
  24.5 5.8 %copy-done = bf16[4096,2048]{1,0:T(8,128)(2,1)S(1)} copy-done((bf16[4096,2048]{1,0:T(8,128)(2,1)S(1)}, bf16[4096,2048]{1,0:T(8,128)(2,1)}, u32[]{:S(2)}) %copy-start) | copy-done | bytes 16777240
  30.3 1.5 %shard_map.156.refs_0_ = f32[48,2048]{1,0:T(8,128)S(1)} custom-call(bf16[48,4096]{1,0:T(8,128)(2,1)S(1)} %get-tuple-element.25.rows_ref, bf16[4096,2048]{1,0:T(8,128)(2,1)S(1)} %copy-done), custom_call_target="tpu_custom_call" | custom-call | tf_op jit(solution)/shard_map/pallas_call | solution.py:146
  31.8 1.0 %collective-permute-start.8 = (bf16[1040,128]{1,0:T(8,128)(2,1)}, bf16[1040,128]{1,0:T(8,128)(2,1)}, u32[]{:S(2)}, u32[]{:S(2)}) collective-permute-start(bf16[1040,128]{1,0:T(8,128)(2,1)} %get-tuple-element.36), channel_id=1, source_target_pairs={{0,8},{4,12},{8,0},{12,4},{1,9},{5,13},{9,1},{13,5},{2,10},{6,14},... | collective-permute-start | bytes 798728 | tf_op jit(solution)/shard_map/ppermute | solution.py:379
  32.7 2.1 %collective-permute-done.3.refs_1_.refs_5_ = bf16[1040,128]{1,0:T(8,128)(2,1)S(1)} collective-permute-done((bf16[1040,128]{1,0:T(8,128)(2,1)}, bf16[1040,128]{1,0:T(8,128)(2,1)S(1)}, u32[]{:S(2)}, u32[]{:S(2)}) %collective-permute-start.3) | collective-permute-done | bytes 266272 | tf_op jit(solution)/shard_map/ppermute | solution.py:379
  34.8 3.5 %collective-permute-done.4.refs_2_.refs_7_ = bf16[1040,128]{1,0:T(8,128)(2,1)S(1)} collective-permute-done((bf16[1040,128]{1,0:T(8,128)(2,1)}, bf16[1040,128]{1,0:T(8,128)(2,1)S(1)}, u32[]{:S(2)}, u32[]{:S(2)}) %collective-permute-start.4) | collective-permute-done | bytes 266272 | tf_op jit(solution)/shard_map/ppermute | solution.py:379
  38.4 1.6 %shard_map.157.total_ref = f32[48,2048]{1,0:T(8,128)S(1)} custom-call(bf16[48,4096]{1,0:T(8,128)(2,1)S(1)} %get-tuple-element.25.rows_ref, bf16[4096,2048]{1,0:T(8,128)(2,1)S(1)} %copy-done, f32[48,2048]{1,0:T(8,128)S(1)} %shard_map.156.refs_0_, bf16[1040,128]{1,0:T(8,128)(2,1)S(1)} %collective-permute-done.3.refs_1_.refs_5_, ...), custom_call_target="tpu_custom_call" | custom-call | tf_op jit(solution)/shard_map/pallas_call | solution.py:146
  39.9 0.0 all-to-all-done.ranks_ref
  40.0 0.0 copy-start.8
  40.0 1.0 %copy-done.8 = bf16[4,32,2048]{2,1,0:T(8,128)(2,1)S(1)} copy-done((bf16[4,32,2048]{2,1,0:T(8,128)(2,1)S(1)}, bf16[4,32,2048]{2,1,0:T(8,128)(2,1)}, u32[]{:S(2)}) %copy-start.8) | copy-done | bytes 524312
  41.0 2.1 %shard_map.158 = (bf16[4,3,2304]{2,1,0:T(4,128)(2,1)S(1)}, bf16[4,3,2304]{2,1,0:T(4,128)(2,1)S(1)}, bf16[4,3,2304]{2,1,0:T(4,128)(2,1)S(1)}, bf16[4,3,2304]{2,1,0:T(4,128)(2,1)S(1)}) custom-call(f32[48,2048]{1,0:T(8,128)S(1)} %shard_map.157.total_ref, bf16[48,4096]{1,0:T(8,128)(2,1)S(1)} %get-tuple-element.25.rows_ref, bf16[4096,128]{1,0:T(8,128)(2,1)S(1)} %copy-done.3, ...), custom_call_target="tpu_custom_call" | custom-call | tf_op jit(solution)/shard_map/pallas_call | solution.py:413
  43.2 0.1 collective-permute-start.5
  43.2 1.5 %collective-permute-start.6 = (bf16[4,3,2304]{2,1,0:T(4,128)(2,1)S(1)}, bf16[4,3,2304]{2,1,0:T(4,128)(2,1)S(1)}, u32[]{:S(2)}, u32[]{:S(2)}) collective-permute-start(bf16[4,3,2304]{2,1,0:T(4,128)(2,1)S(1)} %get-tuple-element.33), channel_id=1, source_target_pairs={{0,2},{1,3},{2,0},{3,1},{4,6},{5,7},{6,4},{7,5},{8,10},{9,11},{10,... | collective-permute-start | bytes 165896 | tf_op jit(solution)/shard_map/ppermute | solution.py:383
  44.7 1.4 %collective-permute-start.7 = (bf16[4,3,2304]{2,1,0:T(4,128)(2,1)S(1)}, bf16[4,3,2304]{2,1,0:T(4,128)(2,1)S(1)}, u32[]{:S(2)}, u32[]{:S(2)}) collective-permute-start(bf16[4,3,2304]{2,1,0:T(4,128)(2,1)S(1)} %get-tuple-element.34), channel_id=1, source_target_pairs={{0,3},{1,0},{2,1},{3,2},{4,7},{5,4},{6,5},{7,6},{8,11},{9,8},{10,9... | collective-permute-start | bytes 165896 | tf_op jit(solution)/shard_map/ppermute | solution.py:383
  46.1 5.6 %collective-permute-done.8.refs_6_ = bf16[1040,128]{1,0:T(8,128)(2,1)} collective-permute-done((bf16[1040,128]{1,0:T(8,128)(2,1)}, bf16[1040,128]{1,0:T(8,128)(2,1)}, u32[]{:S(2)}, u32[]{:S(2)}) %collective-permute-start.8) | collective-permute-done | bytes 266272 | tf_op jit(solution)/shard_map/ppermute | solution.py:379
  51.7 0.0 collective-permute-done.6.refs_2_
  51.7 0.0 collective-permute-done.7.refs_3_
  51.7 0.9 %copy-done.11 = bf16[1040,128]{1,0:T(8,128)(2,1)S(1)} copy-done((bf16[1040,128]{1,0:T(8,128)(2,1)S(1)}, bf16[1040,128]{1,0:T(8,128)(2,1)}, u32[]{:S(2)}) %copy-start.11) | copy-done | bytes 266264
  52.7 2.8 %shard_map.159 = bf16[12,2048]{1,0:T(8,128)(2,1)S(1)} custom-call(bf16[4,3,2304]{2,1,0:T(4,128)(2,1)S(1)} %get-tuple-element.31.refs_0_, bf16[4,3,2304]{2,1,0:T(4,128)(2,1)S(1)} %collective-permute-done.5.refs_1_, bf16[4,3,2304]{2,1,0:T(4,128)(2,1)S(1)} %collective-permute-done.6.refs_2_, bf16[4,3,2304]{2,1,0:T(4,128)(2,1)S(1)} %collective-permute-done.7.refs_3_, ...), custom_call_target="tpu_custom_call" | custom-call | flops 50331648 | bytes 83886080 | tf_op jit(solution)/shard_map/pallas_call | solution.py:429
  55.5 0.0 copy-start.5
  55.5 5.9 %all-gather.1.got_ref = bf16[4,12,2048]{2,1,0:T(8,128)(2,1)S(1)} all-gather(bf16[1,12,2048]{2,1,0:T(8,128)(2,1)S(1)} %bitcast.18), channel_id=2, replica_groups=mesh['parts'=2,'tensor'=4,'dp'=2,'pipe'=2] {'dp','pipe'}, dimensions={0}, use_global_device_ids=true | all-gather | bytes 245760 | tf_op jit(solution)/shard_map/all_gather | solution.py:442
  61.4 1.1 %shard_map.160 = (bf16[48,2048]{1,0:T(8,128)(2,1)S(1)}, bf16[16,48,128]{2,1,0:T(8,128)(2,1)}) custom-call(bf16[4,12,2048]{2,1,0:T(8,128)(2,1)S(1)} %all-gather.1.got_ref, bf16[128,2048]{1,0:T(8,128)(2,1)S(1)} %bitcast.17, s32[48,128]{1,0:T(8,128)S(1)} %get-tuple-element.24.refs_5_.slots_ref), custom_call_target="tpu_custom_call" | custom-call | flops 25165824 | bytes 917504 | tf_op jit(solution)/shard_map/pallas_call | solution.py:443
  62.5 8.0 %all-to-all-start.1 = ((bf16[16,48,128]{2,1,0:T(8,128)(2,1)}), bf16[16,48,128]{2,1,0:T(8,128)(2,1)S(1)}, u32[]{:S(2)}, u32[]{:S(2)}) async-start(bf16[16,48,128]{2,1,0:T(8,128)(2,1)} %get-tuple-element.38), calls=%async_computation.1 | async-start | bytes 393216 | tf_op jit(solution)/shard_map/all_to_all | solution.py:386
  70.6 0.0 copy-start.1
  70.6 5.8 %copy-done.1 = bf16[2048,4096]{1,0:T(8,128)(2,1)S(1)} copy-done((bf16[2048,4096]{1,0:T(8,128)(2,1)S(1)}, bf16[2048,4096]{1,0:T(8,128)(2,1)}, u32[]{:S(2)}) %copy-start.1) | copy-done | bytes 16777240
  76.4 3.0 %shard_map.161.total_ref = f32[48,4096]{1,0:T(8,128)S(1)} custom-call(bf16[48,2048]{1,0:T(8,128)(2,1)S(1)} %get-tuple-element.37.rows_ref, bf16[2048,4096]{1,0:T(8,128)(2,1)S(1)} %copy-done.1), custom_call_target="tpu_custom_call" | custom-call | tf_op jit(solution)/shard_map/pallas_call | solution.py:146
  79.3 0.2 all-to-all-done.1.ranks_ref
  79.6 0.7 shard_map.162
  80.3 3.6 %collective-permute-start.9 = (bf16[3,4,4096]{2,1,0:T(4,128)(2,1)S(1)}, bf16[3,4,4096]{2,1,0:T(4,128)(2,1)S(1)}, u32[]{:S(2)}, u32[]{:S(2)}) collective-permute-start(bf16[3,4,4096]{2,1,0:T(4,128)(2,1)S(1)} %get-tuple-element.40), channel_id=1, source_target_pairs={{0,12},{4,0},{8,4},{12,8},{1,13},{5,1},{9,5},{13,9},{2,14},{6,2},{... | collective-permute-start | bytes 294920 | tf_op jit(solution)/shard_map/ppermute | solution.py:379
  83.9 0.0 collective-permute-start.10
  83.9 1.1 %collective-permute-start.11 = (bf16[3,4,4096]{2,1,0:T(4,128)(2,1)S(1)}, bf16[3,4,4096]{2,1,0:T(4,128)(2,1)S(1)}, u32[]{:S(2)}, u32[]{:S(2)}) collective-permute-start(bf16[3,4,4096]{2,1,0:T(4,128)(2,1)S(1)} %get-tuple-element.42), channel_id=1, source_target_pairs={{0,4},{4,8},{8,12},{12,0},{1,5},{5,9},{9,13},{13,1},{2,6},{6,10},{... | collective-permute-start | bytes 294920 | tf_op jit(solution)/shard_map/ppermute | solution.py:379
  85.0 2.1 %collective-permute-done.9 = bf16[3,4,4096]{2,1,0:T(4,128)(2,1)S(1)} collective-permute-done((bf16[3,4,4096]{2,1,0:T(4,128)(2,1)S(1)}, bf16[3,4,4096]{2,1,0:T(4,128)(2,1)S(1)}, u32[]{:S(2)}, u32[]{:S(2)}) %collective-permute-start.9) | collective-permute-done | bytes 98336 | tf_op jit(solution)/shard_map/ppermute | solution.py:379
  87.1 6.1 %collective-permute-done.10 = bf16[3,4,4096]{2,1,0:T(4,128)(2,1)S(1)} collective-permute-done((bf16[3,4,4096]{2,1,0:T(4,128)(2,1)S(1)}, bf16[3,4,4096]{2,1,0:T(4,128)(2,1)S(1)}, u32[]{:S(2)}, u32[]{:S(2)}) %collective-permute-start.10) | collective-permute-done | bytes 98336 | tf_op jit(solution)/shard_map/ppermute | solution.py:379
  93.2 0.0 collective-permute-done.11
  93.2 0.7 fusion
  (25 shorter events, 0.0 us)
Async XLA Ops:
  0.0 12.1 %collective-permute-start.2 = (bf16[3,4,4096]{2,1,0:T(4,128)(2,1)}, bf16[3,4,4096]{2,1,0:T(4,128)(2,1)S(1)}, u32[]{:S(2)}, u32[]{:S(2)}) collective-permute-start(bf16[3,4,4096]{2,1,0:T(4,128)(2,1)} %bitcast.19), channel_id=1, source_target_pairs={{0,12},{4,0},{8,4},{12,8},{1,13},{5,1},{9,5},{13,9},{2,14},{6,2},{... | collective-permute-start | bytes 294920 | tf_op jit(solution)/shard_map/ppermute | solution.py:379
  5.0 9.0 %collective-permute-start.1 = (bf16[3,4,4096]{2,1,0:T(4,128)(2,1)}, bf16[3,4,4096]{2,1,0:T(4,128)(2,1)S(1)}, u32[]{:S(2)}, u32[]{:S(2)}) collective-permute-start(bf16[3,4,4096]{2,1,0:T(4,128)(2,1)} %bitcast.20), channel_id=1, source_target_pairs={{0,8},{4,12},{8,0},{12,4},{1,9},{5,13},{9,1},{13,5},{2,10},{6,14},... | collective-permute-start | bytes 294920 | tf_op jit(solution)/shard_map/ppermute | solution.py:379
  5.1 9.0 %collective-permute-start = (bf16[3,4,4096]{2,1,0:T(4,128)(2,1)}, bf16[3,4,4096]{2,1,0:T(4,128)(2,1)S(1)}, u32[]{:S(2)}, u32[]{:S(2)}) collective-permute-start(bf16[3,4,4096]{2,1,0:T(4,128)(2,1)} %bitcast.21), channel_id=1, source_target_pairs={{0,4},{4,8},{8,12},{12,0},{1,5},{5,9},{9,13},{13,1},{2,6},{6,10},{... | collective-permute-start | bytes 294920 | tf_op jit(solution)/shard_map/ppermute | solution.py:379
  6.7 1.0 %copy-start.6 = (bf16[1,4,512,128]{3,2,1,0:T(8,128)(2,1)S(1)}, bf16[1,4,512,128]{3,2,1,0:T(8,128)(2,1)}, u32[]{:S(2)}) copy-start(bf16[1,4,512,128]{3,2,1,0:T(8,128)(2,1)} %keys_ref.1) | copy-start | bytes 1572868
  7.8 1.0 %copy-start.7 = (bf16[1,4,512,128]{3,2,1,0:T(8,128)(2,1)S(1)}, bf16[1,4,512,128]{3,2,1,0:T(8,128)(2,1)}, u32[]{:S(2)}) copy-start(bf16[1,4,512,128]{3,2,1,0:T(8,128)(2,1)} %values_ref.1) | copy-start | bytes 1572868
  8.8 0.7 copy-start.15
  9.5 0.7 copy-start.16
  10.1 3.9 %copy-start.2 = (bf16[4,4096,96]{1,2,0:T(8,128)(2,1)S(1)}, bf16[4,4096,96]{1,2,0:T(8,128)(2,1)}, u32[]{:S(2)}) copy-start(bf16[4,4096,96]{1,2,0:T(8,128)(2,1)} %param.21) | copy-start | bytes 9437188
  10.1 3.9 %copy-start.12 = (bf16[4,3,4096]{2,0,1:T(4,128)(2,1)S(1)}, bf16[4,3,4096]{2,0,1:T(4,128)(2,1)}, u32[]{:S(2)}) copy-start(bf16[4,3,4096]{2,0,1:T(4,128)(2,1)} %param.16) | copy-start | bytes 294916
  12.1 3.9 %copy-start.10 = (bf16[1040,128]{1,0:T(8,128)(2,1)}, bf16[1040,128]{1,0:T(8,128)(2,1)S(1)}, u32[]{:S(2)}) copy-start(bf16[1040,128]{1,0:T(8,128)(2,1)S(1)} %get-tuple-element.35.refs_4_) | copy-start | bytes 798724
  16.0 24.0 %all-to-all-start = ((bf16[16,48,128]{2,1,0:T(8,128)(2,1)}), bf16[16,48,128]{2,1,0:T(8,128)(2,1)}, u32[]{:S(2)}, u32[]{:S(2)}) async-start(bf16[16,48,128]{2,1,0:T(8,128)(2,1)} %get-tuple-element.30), calls=%async_computation | async-start | bytes 393216 | tf_op jit(solution)/shard_map/all_to_all | solution.py:386
  20.6 14.2 %collective-permute-start.3 = (bf16[1040,128]{1,0:T(8,128)(2,1)}, bf16[1040,128]{1,0:T(8,128)(2,1)S(1)}, u32[]{:S(2)}, u32[]{:S(2)}) collective-permute-start(bf16[1040,128]{1,0:T(8,128)(2,1)} %get-tuple-element.28), channel_id=1, source_target_pairs={{0,4},{4,8},{8,12},{12,0},{1,5},{5,9},{9,13},{13,1},{2,6},{6,10},{... | collective-permute-start | bytes 798728 | tf_op jit(solution)/shard_map/ppermute | solution.py:379
  22.5 15.9 %collective-permute-start.4 = (bf16[1040,128]{1,0:T(8,128)(2,1)}, bf16[1040,128]{1,0:T(8,128)(2,1)S(1)}, u32[]{:S(2)}, u32[]{:S(2)}) collective-permute-start(bf16[1040,128]{1,0:T(8,128)(2,1)} %get-tuple-element.29), channel_id=1, source_target_pairs={{0,12},{4,0},{8,4},{12,8},{1,13},{5,1},{9,5},{13,9},{2,14},{6,2},{... | collective-permute-start | bytes 798728 | tf_op jit(solution)/shard_map/ppermute | solution.py:379
  24.5 5.8 %copy-start = (bf16[4096,2048]{1,0:T(8,128)(2,1)S(1)}, bf16[4096,2048]{1,0:T(8,128)(2,1)}, u32[]{:S(2)}) copy-start(bf16[4096,2048]{1,0:T(8,128)(2,1)} %refs_12_.1) | copy-start | bytes 50331652
  30.2 9.7 %copy-start.3 = (bf16[4096,128]{1,0:T(8,128)(2,1)S(1)}, bf16[4096,128]{1,0:T(8,128)(2,1)}, u32[]{:S(2)}) copy-start(bf16[4096,128]{1,0:T(8,128)(2,1)} %key_ref.1) | copy-start | bytes 3145732
  30.2 9.7 %copy-start.4 = (bf16[4096,128]{1,0:T(8,128)(2,1)S(1)}, bf16[4096,128]{1,0:T(8,128)(2,1)}, u32[]{:S(2)}) copy-start(bf16[4096,128]{1,0:T(8,128)(2,1)} %value_ref.1) | copy-start | bytes 3145732
  30.2 9.7 %copy-start.13 = (bf16[4,32,128]{2,1,0:T(8,128)(2,1)S(1)}, bf16[4,32,128]{2,1,0:T(8,128)(2,1)}, u32[]{:S(2)}) copy-start(bf16[4,32,128]{2,1,0:T(8,128)(2,1)} %param.23) | copy-start | bytes 98308
  30.2 9.7 %copy-start.14 = (bf16[4,32,128]{2,1,0:T(8,128)(2,1)S(1)}, bf16[4,32,128]{2,1,0:T(8,128)(2,1)}, u32[]{:S(2)}) copy-start(bf16[4,32,128]{2,1,0:T(8,128)(2,1)} %param.24) | copy-start | bytes 98308
  31.8 19.9 %collective-permute-start.8 = (bf16[1040,128]{1,0:T(8,128)(2,1)}, bf16[1040,128]{1,0:T(8,128)(2,1)}, u32[]{:S(2)}, u32[]{:S(2)}) collective-permute-start(bf16[1040,128]{1,0:T(8,128)(2,1)} %get-tuple-element.36), channel_id=1, source_target_pairs={{0,8},{4,12},{8,0},{12,4},{1,9},{5,13},{9,1},{13,5},{2,10},{6,14},... | collective-permute-start | bytes 798728 | tf_op jit(solution)/shard_map/ppermute | solution.py:379
  40.0 1.0 %copy-start.8 = (bf16[4,32,2048]{2,1,0:T(8,128)(2,1)S(1)}, bf16[4,32,2048]{2,1,0:T(8,128)(2,1)}, u32[]{:S(2)}) copy-start(bf16[4,32,2048]{2,1,0:T(8,128)(2,1)} %param.22) | copy-start | bytes 1572868
  43.2 8.6 %collective-permute-start.5 = (bf16[4,3,2304]{2,1,0:T(4,128)(2,1)S(1)}, bf16[4,3,2304]{2,1,0:T(4,128)(2,1)S(1)}, u32[]{:S(2)}, u32[]{:S(2)}) collective-permute-start(bf16[4,3,2304]{2,1,0:T(4,128)(2,1)S(1)} %get-tuple-element.32), channel_id=1, source_target_pairs={{0,1},{1,2},{2,3},{3,0},{4,5},{5,6},{6,7},{7,4},{8,9},{9,10},{10,1... | collective-permute-start | bytes 165896 | tf_op jit(solution)/shard_map/ppermute | solution.py:383
  43.2 8.5 %collective-permute-start.6 = (bf16[4,3,2304]{2,1,0:T(4,128)(2,1)S(1)}, bf16[4,3,2304]{2,1,0:T(4,128)(2,1)S(1)}, u32[]{:S(2)}, u32[]{:S(2)}) collective-permute-start(bf16[4,3,2304]{2,1,0:T(4,128)(2,1)S(1)} %get-tuple-element.33), channel_id=1, source_target_pairs={{0,2},{1,3},{2,0},{3,1},{4,6},{5,7},{6,4},{7,5},{8,10},{9,11},{10,... | collective-permute-start | bytes 165896 | tf_op jit(solution)/shard_map/ppermute | solution.py:383
  44.7 7.0 %collective-permute-start.7 = (bf16[4,3,2304]{2,1,0:T(4,128)(2,1)S(1)}, bf16[4,3,2304]{2,1,0:T(4,128)(2,1)S(1)}, u32[]{:S(2)}, u32[]{:S(2)}) collective-permute-start(bf16[4,3,2304]{2,1,0:T(4,128)(2,1)S(1)} %get-tuple-element.34), channel_id=1, source_target_pairs={{0,3},{1,0},{2,1},{3,2},{4,7},{5,4},{6,5},{7,6},{8,11},{9,8},{10,9... | collective-permute-start | bytes 165896 | tf_op jit(solution)/shard_map/ppermute | solution.py:383
  51.7 1.0 %copy-start.11 = (bf16[1040,128]{1,0:T(8,128)(2,1)S(1)}, bf16[1040,128]{1,0:T(8,128)(2,1)}, u32[]{:S(2)}) copy-start(bf16[1040,128]{1,0:T(8,128)(2,1)} %copy-done.10) | copy-start | bytes 798724
  52.7 8.7 %copy-start.9 = (bf16[4,2048,32]{1,2,0:T(8,128)(2,1)S(1)}, bf16[4,2048,32]{1,2,0:T(8,128)(2,1)}, u32[]{:S(2)}) copy-start(bf16[4,2048,32]{1,2,0:T(8,128)(2,1)} %param.25) | copy-start | bytes 1572868
  55.5 24.1 %copy-start.5 = (bf16[4,32,4096]{2,1,0:T(8,128)(2,1)S(1)}, bf16[4,32,4096]{2,1,0:T(8,128)(2,1)}, u32[]{:S(2)}) copy-start(bf16[4,32,4096]{2,1,0:T(8,128)(2,1)} %param.26) | copy-start | bytes 3145732
  62.5 17.0 %all-to-all-start.1 = ((bf16[16,48,128]{2,1,0:T(8,128)(2,1)}), bf16[16,48,128]{2,1,0:T(8,128)(2,1)S(1)}, u32[]{:S(2)}, u32[]{:S(2)}) async-start(bf16[16,48,128]{2,1,0:T(8,128)(2,1)} %get-tuple-element.38), calls=%async_computation.1 | async-start | bytes 393216 | tf_op jit(solution)/shard_map/all_to_all | solution.py:386
  70.6 5.8 %copy-start.1 = (bf16[2048,4096]{1,0:T(8,128)(2,1)S(1)}, bf16[2048,4096]{1,0:T(8,128)(2,1)}, u32[]{:S(2)}) copy-start(bf16[2048,4096]{1,0:T(8,128)(2,1)} %weight_ref.5) | copy-start | bytes 50331652
  80.3 6.8 %collective-permute-start.9 = (bf16[3,4,4096]{2,1,0:T(4,128)(2,1)S(1)}, bf16[3,4,4096]{2,1,0:T(4,128)(2,1)S(1)}, u32[]{:S(2)}, u32[]{:S(2)}) collective-permute-start(bf16[3,4,4096]{2,1,0:T(4,128)(2,1)S(1)} %get-tuple-element.40), channel_id=1, source_target_pairs={{0,12},{4,0},{8,4},{12,8},{1,13},{5,1},{9,5},{13,9},{2,14},{6,2},{... | collective-permute-start | bytes 294920 | tf_op jit(solution)/shard_map/ppermute | solution.py:379
  83.9 9.3 %collective-permute-start.10 = (bf16[3,4,4096]{2,1,0:T(4,128)(2,1)S(1)}, bf16[3,4,4096]{2,1,0:T(4,128)(2,1)S(1)}, u32[]{:S(2)}, u32[]{:S(2)}) collective-permute-start(bf16[3,4,4096]{2,1,0:T(4,128)(2,1)S(1)} %get-tuple-element.41), channel_id=1, source_target_pairs={{0,8},{4,12},{8,0},{12,4},{1,9},{5,13},{9,1},{13,5},{2,10},{6,14},... | collective-permute-start | bytes 294920 | tf_op jit(solution)/shard_map/ppermute | solution.py:379
  83.9 9.3 %collective-permute-start.11 = (bf16[3,4,4096]{2,1,0:T(4,128)(2,1)S(1)}, bf16[3,4,4096]{2,1,0:T(4,128)(2,1)S(1)}, u32[]{:S(2)}, u32[]{:S(2)}) collective-permute-start(bf16[3,4,4096]{2,1,0:T(4,128)(2,1)S(1)} %get-tuple-element.42), channel_id=1, source_target_pairs={{0,4},{4,8},{8,12},{12,0},{1,5},{5,9},{9,13},{13,1},{2,6},{6,10},{... | collective-permute-start | bytes 294920 | tf_op jit(solution)/shard_map/ppermute | solution.py:379

commit v7 on v3

--- a/solution.py
+++ b/solution.py
@@ -55,34 +55,33 @@
     return value & (size - 1) if size & (size - 1) == 0 else lax.rem(value, size)
 
 
-def block_first(sizes, group, block, draft):
+def as_gathered(sizes, group, block, draft):
     groups, blocks, drafts = sizes
     return (block * drafts + draft) * groups + group
 
 
-def group_first(sizes, group, block, draft):
-    groups, blocks, drafts = sizes
-    return (group * blocks + block) * drafts + draft
+def by_request(sizes, group, block, draft):
+    groups, blocks, drafts = sizes
+    return (block * groups + group) * drafts + draft
 
 
 def parts_of(order, sizes, index):
     groups, blocks, drafts = sizes
-    if order is block_first:
-        return (
-            rest_of(index, groups),
-            over(index, groups * drafts),
-            rest_of(over(index, groups), drafts),
-        )
-    return over(index, blocks * drafts), rest_of(over(index, drafts), blocks), rest_of(index, drafts)
-
-
-def reorder(sizes, after, before, turn_block, turn_group=0):
+    block = over(index, groups * drafts)
+    if order is as_gathered:
+        return rest_of(index, groups), block, rest_of(over(index, groups), drafts)
+    return rest_of(over(index, drafts), groups), block, rest_of(index, drafts)
+
+
+def turned(block, blocks):
+    return rest_of(lax.axis_index("tensor") - block + blocks, blocks)
+
+
+def reorder(sizes, after, before):
     groups, blocks, drafts = sizes
     rows = groups * blocks * drafts
     group, block, draft = parts_of(after, sizes, iota((rows, rows), 0))
-    wanted = before(
-        sizes, rest_of(group + turn_group, groups), rest_of(block + turn_block, blocks), draft
-    )
+    wanted = before(sizes, group, turned(block, blocks), draft)
     return jnp.where(wanted == iota((rows, rows), 1), 1.0, 0.0).astype(jnp.bfloat16)
 
 
@@ -104,6 +103,7 @@
     ranks = owned_ranks(
         rows, shrink_ref[...], place, shrink_ref.shape[0] // owned, rank_ref.shape[2]
     )
+    ranks = dot(reorder(sizes, by_request, as_gathered), ranks).astype(jnp.bfloat16)
     for target in range(rank_ref.shape[0]):
         rank_ref[target] = ranks
 
@@ -128,173 +128,117 @@
     return jnp.where(slot == place, wide, 0.0).astype(jnp.bfloat16)
 
 
-def stream_kernel(first, chunks, depth, rows_ref, weight_ref, *refs):
-    *sums, total_ref, buffer, sems = refs
+def stream_kernel(chunks, rows_ref, weight_ref, total_ref, buffer, sems):
+    depth = rows_ref.shape[1] // chunks
 
     def copy(chunk):
-        return pltpu.make_async_copy(
-            weight_ref.at[pl.ds(first + chunk * depth, depth)],
-            buffer.at[pl.ds(chunk * depth, depth)],
-            sems.at[chunk],
-        )
+        part = pl.ds(chunk * depth, depth)
+        return pltpu.make_async_copy(weight_ref.at[part], buffer.at[part], sems.at[chunk])
 
     for chunk in range(chunks):
         copy(chunk).start()
     for chunk in range(chunks):
-        start = first + chunk * depth
         copy(chunk).wait()
         product = dot(
-            rows_ref[:, start : start + depth], buffer[chunk * depth : (chunk + 1) * depth, :]
+            rows_ref[:, chunk * depth : (chunk + 1) * depth],
+            buffer[chunk * depth : (chunk + 1) * depth, :],
         )
         if chunk:
             total_ref[...] += product
-        elif sums:
-            total_ref[...] = sums[0][...] + product
         else:
             total_ref[...] = product
 
 
-def stream(rows, weight, chunks, first, size, *sums):
-    width = weight.shape[1]
+def stream(rows, weight, chunks):
     return call(
-        functools.partial(stream_kernel, first, chunks, size // chunks),
-        shape((rows.shape[0], width), jnp.float32),
-        [VMEM, HBM] + [VMEM] * len(sums),
-        [pltpu.VMEM((size, width), jnp.bfloat16), pltpu.SemaphoreType.DMA((chunks,))],
-        2 * rows.shape[0] * size * width,
-        2 * size * width,
+        functools.partial(stream_kernel, chunks),
+        shape((rows.shape[0], weight.shape[1]), jnp.float32),
+        [VMEM, HBM],
+        [pltpu.VMEM(weight.shape, weight.dtype), pltpu.SemaphoreType.DMA((chunks,))],
+        2 * rows.shape[0] * weight.size,
+        2 * weight.size,
         40 * MIB,
-    )(rows, weight, *sums)
-
-
-def pack_kernel(sizes, ids_ref, pool_ref, length_ref, keys_ref, values_ref, turns_ref, *refs):
-    groups, blocks, drafts = sizes
-    outs = refs[:blocks]
-    slots_ref, extra_f32, extra_ref, sems = refs[blocks:]
-    size, head_size = keys_ref.shape[2:]
-    me = lax.axis_index("tensor")
-    length = length_ref[0]
-    positions = (iota((drafts, head_size), 0) + length).astype(jnp.float32)
-    angles = positions * turns_ref[0:1, :]
-    extra_f32[...] = jnp.zeros(extra_f32.shape, jnp.float32)
-    for index, value in enumerate((jnp.cos(angles), jnp.sin(angles) * turns_ref[1:2, :])):
-        high = value.astype(jnp.bfloat16).astype(jnp.float32)
-        start = 2 * index * drafts
-        extra_f32[start : start + drafts, :] = high
-        extra_f32[start + drafts : start + 2 * drafts, :] = value - high
-    ones = jnp.ones((1, head_size), jnp.float32)
-    extra_f32[4 * drafts : 4 * drafts + 1, :] = ones * (length >> 4).astype(jnp.float32)
-    extra_f32[4 * drafts + 1 : 4 * drafts + 2, :] = ones * (length & 15).astype(jnp.float32)
-    extra_ref[...] = extra_f32[...].astype(jnp.bfloat16)
-    copies = []
-    for shift in range(blocks):
-        head = lax.rem(me + shift, blocks)
-        copies += [
-            pltpu.make_async_copy(
-                keys_ref.at[0, head], outs[shift].at[pl.ds(0, size)], sems.at[shift, 0]
-            ),
-            pltpu.make_async_copy(
-                values_ref.at[0, head], outs[shift].at[pl.ds(size, size)], sems.at[shift, 1]
-            ),
-            pltpu.make_async_copy(
-                extra_ref,
-                outs[shift].at[pl.ds(2 * size, extra_ref.shape[0])],
-                sems.at[shift, 2],
-            ),
-        ]
-    for copy in copies:
-        copy.start()
+    )(rows, weight)
+
+
+def prepare_kernel(sizes, ids_ref, pool_ref, length_ref, _, slots_ref, cosine_ref, sine_ref):
+    groups, blocks, drafts = sizes
+    width = cosine_ref.shape[1]
+    lane = iota(cosine_ref.shape, 1)
+    half = (lane & (width // 2 - 1)).astype(jnp.float32)
+    positions = (iota(cosine_ref.shape, 0) + length_ref[0]).astype(jnp.float32)
+    angles = positions * jnp.exp(half * (-2.0 * math.log(rope_base) / width))
+    cosine_ref[...] = jnp.cos(angles)
+    sine_ref[...] = jnp.sin(angles) * jnp.where(lane < width // 2, -1.0, 1.0)
     index = iota(slots_ref.shape, 0)
     column = iota(slots_ref.shape, 1)
-    near = parts_of(block_first, sizes, index)
-    far = parts_of(group_first, sizes, index)
+    near = parts_of(as_gathered, sizes, index)
+    far = parts_of(by_request, sizes, index)
     row_group = jnp.where(column == 0, near[0], far[0])
-    row_block = jnp.where(column == 0, near[1], far[1])
+    row_block = jnp.where(column == 0, turned(near[1], blocks), far[1])
     place = row_block * groups + row_group
     slots = jnp.zeros(slots_ref.shape, jnp.int32)
-    for block in range(blocks):
-        for group in range(groups):
-            row = lax.rem(me - block + blocks, blocks) * groups + group
-            slots = jnp.where(place == block * groups + group, pool_ref[ids_ref[row]], slots)
+    for row in range(blocks * groups):
+        slots = jnp.where(place == row, pool_ref[ids_ref[row]], slots)
     slots_ref[...] = slots
-    for copy in copies:
-        copy.wait()
-
-
-def pack(sizes, ids, pool, lengths, keys, values):
-    groups, blocks, drafts = sizes
-    head_size = keys.shape[3]
-    half = np.arange(head_size // 2)
-    frequency = (rope_base ** (-2.0 * half / head_size)).astype(np.float32)
-    signs = np.ones(half.size, np.float32)
-    turns = np.stack([np.tile(frequency, 2), np.concatenate([-signs, signs])])
-    used = -(-(4 * drafts + 2) // 16) * 16
-    outs = [shape((2 * keys.shape[2] + used, head_size))] * blocks
+
+
+def prepare(sizes, ids, pool, lengths, head_size, later):
+    groups, blocks, drafts = sizes
     smem = pl.BlockSpec(memory_space=pltpu.SMEM)
-    return pl.pallas_call(
-        functools.partial(pack_kernel, sizes),
-        out_shape=outs + [shape((groups * blocks * drafts, 128), jnp.int32)],
-        in_specs=[smem, smem, smem, VMEM, VMEM, VMEM],
-        out_specs=[HBM] * blocks + [VMEM],
-        scratch_shapes=[
-            pltpu.VMEM((used, head_size), jnp.float32),
-            pltpu.VMEM((used, head_size), jnp.bfloat16),
-            pltpu.SemaphoreType.DMA((blocks, 3)),
-        ],
-        cost_estimate=pl.CostEstimate(flops=0, bytes_accessed=8 * keys.size, transcendentals=0),
-        compiler_params=pltpu.CompilerParams(vmem_limit_bytes=24 * MIB),
-    )(ids, pool, lengths, keys, values, jnp.asarray(turns))
-
-
-def grow_kernel(sizes, width, total_ref, rows_ref, key_ref, value_ref, slots_ref, ranks_ref, *rest):
-    groups, blocks, drafts = sizes
-    grows = rest[:3]
-    outs = rest[3:]
+    table = shape((8 * -(-drafts // 8), head_size), jnp.float32)
+    return call(
+        functools.partial(prepare_kernel, sizes),
+        [shape((groups * blocks * drafts, 128), jnp.int32), table, table],
+        [smem, smem, smem, HBM],
+        limit=40 * MIB,
+    )(ids, pool, lengths, later)
+
+
+def grow_kernel(
+    sizes, width, total_ref, rows_ref, key_ref, value_ref, slots_ref, ranks_ref, *refs
+):
+    groups, blocks, drafts = sizes
+    *grows, out_ref = refs
     group = group_of()
     owned = grows[0].shape[0] // width
     ranks = ranks_ref[group * groups].astype(jnp.float32)
     for other in range(1, groups):
         ranks = ranks + ranks_ref[group * groups + other].astype(jnp.float32)
-    turn = rest_of(group - lax.axis_index("tensor") + blocks, blocks)
-    ranks = dot(reorder(sizes, block_first, block_first, turn), ranks.astype(jnp.bfloat16))
+    ranks = dot(reorder(sizes, as_gathered, by_request), ranks.astype(jnp.bfloat16))
     place = slots_ref[:, 0:1] - group * owned
     wide = spread_ranks(ranks.astype(jnp.bfloat16), place, width, owned, len(grows))
-    by_group = reorder(sizes, group_first, block_first, 0, group)
+    arranged = reorder(sizes, by_request, as_gathered)
     start = 0
     for index, grow in enumerate(grows):
         deep, cols = grow.shape
-        base = total_ref[...] if index == 0 else dot(rows_ref[...], (key_ref, value_ref)[index - 1][...])
-        full = base + dot(wide[:, index * deep : (index + 1) * deep], grow[...])
-        full = dot(by_group, full.astype(jnp.bfloat16)).astype(jnp.bfloat16)
-        for step in range(groups):
-            for block in range(blocks):
-                row = (step * blocks + block) * drafts
-                outs[step][block, :, start : start + cols] = full[row : row + drafts]
+        if index == 0:
+            full = total_ref[...]
+        else:
+            full = dot(rows_ref[...], (key_ref, value_ref)[index - 1][...])
+        full = full + dot(wide[:, index * deep : (index + 1) * deep], grow[...])
+        full = dot(arranged, full.astype(jnp.bfloat16)).astype(jnp.bfloat16)
+        for row in range(groups * blocks):
+            out_ref[row, :, start : start + cols] = full[row * drafts : (row + 1) * drafts]
         start += cols
 
 
-def attend_kernel(blocks, drafts, groups, cache_size, *refs):
-    parts = refs[:groups]
-    caches = refs[groups : groups + blocks]
-    mixed_ref, query_s, fresh_s, out_s = refs[groups + blocks :]
-    head_size = caches[0].shape[1]
-    cols = parts[0].shape[2]
-    heads = cols // head_size - 2
-    count = heads * drafts
+def attend_kernel(
+    sizes, arrived_ref, keys_ref, values_ref, length_ref, cosine_ref, sine_ref, out_ref, *scratch
+):
+    groups, blocks, drafts = sizes
+    query_s, fresh_s, out_s = scratch
+    cache_size, head_size = keys_ref.shape[2:]
+    heads = arrived_ref.shape[2] // head_size - 2
     scale = 1.0 / math.sqrt(head_size)
     fresh_s[...] = jnp.zeros(fresh_s.shape, jnp.float32)
-    pad = fresh_s.shape[1]
+    cosine = cosine_ref[0:drafts, :]
+    sine = sine_ref[0:drafts, :]
     for block in range(blocks):
-        joined = parts[0][block].astype(jnp.float32)
-        for other in parts[1:]:
-            joined = joined + other[block].astype(jnp.float32)
+        joined = arrived_ref[block * groups].astype(jnp.float32)
+        for other in range(1, groups):
+            joined = joined + arrived_ref[block * groups + other].astype(jnp.float32)
         joined = joined.astype(jnp.bfloat16).astype(jnp.float32)
-        extra = caches[block][2 * cache_size :, :].astype(jnp.float32)
-        cosine = extra[0:drafts] + extra[drafts : 2 * drafts]
-        sine = extra[2 * drafts : 3 * drafts] + extra[3 * drafts : 4 * drafts]
-        length = extra[4 * drafts : 4 * drafts + 1, 0:1] * 16.0 + extra[
-            4 * drafts + 1 : 4 * drafts + 2, 0:1
-        ]
 
         def rotated(head):
             value = joined[:, head * head_size : (head + 1) * head_size]
@@ -305,32 +249,31 @@
         fresh_s[2 * block, 0:drafts, :] = rotated(heads)
         fresh_s[2 * block + 1, 0:drafts, :] = joined[:, (heads + 1) * head_size :]
         query = query_s[block].astype(jnp.bfloat16)
-        old = dot_nt(query, caches[block][0:cache_size, :]) * scale
+        old = dot_nt(query, keys_ref[0, block]) * scale
         new = dot_nt(query, fresh_s[2 * block].astype(jnp.bfloat16)) * scale
-        old_seen = iota(old.shape, 1).astype(jnp.float32) < length
-        new_seen = iota(new.shape, 1) <= lax.rem(iota(new.shape, 0), drafts)
-        old = jnp.where(old_seen, old, -jnp.inf)
-        new = jnp.where(new_seen, new, -jnp.inf)
-        peak = jnp.maximum(
-            jnp.max(old, 1, keepdims=True), jnp.max(new, 1, keepdims=True)
-        )
+        old = jnp.where(iota(old.shape, 1) < length_ref[0], old, -jnp.inf)
+        seen = iota(new.shape, 1) <= lax.rem(iota(new.shape, 0), drafts)
+        new = jnp.where(seen, new, -jnp.inf)
+        peak = jnp.maximum(jnp.max(old, 1, keepdims=True), jnp.max(new, 1, keepdims=True))
         old = jnp.exp(old - peak)
         new = jnp.exp(new - peak)
         below = jnp.sum(old, 1, keepdims=True) + jnp.sum(new, 1, keepdims=True)
-        mixed = dot(
-            (old / below).astype(jnp.bfloat16), caches[block][cache_size : 2 * cache_size, :]
-        ) + dot((new / below).astype(jnp.bfloat16), fresh_s[2 * block + 1].astype(jnp.bfloat16))
+        mixed = dot((old / below).astype(jnp.bfloat16), values_ref[0, block]) + dot(
+            (new / below).astype(jnp.bfloat16), fresh_s[2 * block + 1].astype(jnp.bfloat16)
+        )
         for head in range(heads):
-            out_s[
-                block * drafts : (block + 1) * drafts, head * head_size : (head + 1) * head_size
-            ] = mixed[head * drafts : (head + 1) * drafts]
-    mixed_ref[...] = out_s[...].astype(jnp.bfloat16)
+            out_s[block, 0:drafts, head * head_size : (head + 1) * head_size] = mixed[
+                head * drafts : (head + 1) * drafts
+            ]
+        result = out_s[block, 0:drafts, :].astype(jnp.bfloat16)
+        for target in range(groups):
+            out_ref[block * groups + target] = result
 
 
 def out_rank_kernel(owned, got_ref, shrink_ref, slots_ref, rows_ref, rank_ref, wide):
-    span = got_ref.shape[1]
-    for group in range(got_ref.shape[0]):
-        wide[group * span : (group + 1) * span, :] = got_ref[group].astype(jnp.float32)
+    drafts = got_ref.shape[1]
+    for row in range(got_ref.shape[0]):
+        wide[row * drafts : (row + 1) * drafts, :] = got_ref[row].astype(jnp.float32)
     rows = wide[...].astype(jnp.bfloat16)
     rows_ref[...] = rows
     place = slots_ref[:, 1:2] - group_of() * owned
@@ -345,24 +288,20 @@
     groups, blocks, drafts = sizes
     owned = grow_ref.shape[0] // width
     me = lax.axis_index("tensor")
-    ranks = None
-    for source in range(blocks):
-        turn = rest_of(source - me + blocks, blocks)
-        moved = dot(
-            reorder(sizes, group_first, group_first, turn), ranks_ref[source * groups + me]
-        )
-        ranks = moved if ranks is None else ranks + moved
+    ranks = ranks_ref[me].astype(jnp.float32)
+    for source in range(1, blocks):
+        ranks = ranks + ranks_ref[source * groups + me].astype(jnp.float32)
     place = slots_ref[:, 1:2] - me * owned
     wide = spread_ranks(ranks.astype(jnp.bfloat16), place, width, owned, 1)
     full = (total_ref[...] + dot(wide, grow_ref[...])).astype(jnp.bfloat16)
-    full = dot(reorder(sizes, block_first, group_first, 0), full).astype(jnp.bfloat16)
+    full = dot(reorder(sizes, as_gathered, by_request), full).astype(jnp.bfloat16)
     for block in range(blocks):
         for draft in range(drafts):
             start = (block * drafts + draft) * groups
             outs[block][draft] = full[start : start + groups]
 
 
-def by_head(
+def by_kernels(
     tokens,
     w_query,
     w_key,
@@ -386,7 +325,7 @@
     sizes = (groups, blocks, drafts)
     owned = shrink_qkv.shape[0]
     width = grow_out.shape[1]
-    cache_size, head_size = cache_keys.shape[2:]
+    head_size = cache_keys.shape[3]
     span = blocks * drafts
     count = groups * span
     lanes = -(-shrink_qkv.shape[2] // 128) * 128
@@ -395,21 +334,15 @@
         route = [(t, (t + shift) % blocks) for t in range(blocks)]
         return lax.ppermute(value, "tensor", route)
 
-    def over_group(value, shift):
-        route = [(g, (g + shift) % groups) for g in range(groups)]
-        return lax.ppermute(value, GROUP, route)
-
     def exchange(value):
         return lax.all_to_all(value, EVERY, split_axis=0, concat_axis=0, tiled=True)
 
     mine = jnp.transpose(tokens, (1, 0, 2))
     pieces = [mine] + [over_tensor(mine, shift) for shift in range(1, blocks)]
 
-    *messages, slots = pack(
-        sizes, adapter_ids, adapter_slots, cache_lengths, cache_keys, cache_values
-    )
-    caches = {shift: over_tensor(messages[shift], shift) for shift in range(1, blocks) if shift != 2}
-
+    slots, cosine, sine = prepare(
+        sizes, adapter_ids, adapter_slots, cache_lengths, head_size, w_out
+    )
     shrink_in = jnp.transpose(shrink_qkv, (0, 2, 1)).reshape(-1, features)
     rows, rank_part = call(
         functools.partial(rank_kernel, sizes, owned),
@@ -420,17 +353,11 @@
         2 * shrink_qkv.size + 4 * count * features,
     )(*pieces, shrink_in, slots)
     ranks = exchange(rank_part)
-    half = features // 2
-    total = stream(rows, w_query, 4, 0, half)
-    total, *late = lax.optimization_barrier((total, *messages[2:3]))
-    for message in late:
-        caches[2] = over_tensor(message, 2)
-    total = stream(rows, w_query, 4, half, features - half, total)
-    caches = [messages[0]] + [caches[shift] for shift in range(1, blocks)]
+    total = stream(rows, w_query, 8)
     cols = total.shape[1] + w_key.shape[1] + w_value.shape[1]
     sent = call(
         functools.partial(grow_kernel, sizes, width),
-        [shape((blocks, drafts, cols))] * groups,
+        shape((blocks * groups, drafts, cols)),
         [VMEM] * 9,
         [],
         2 * count * owned * width * cols,
@@ -444,31 +371,27 @@
         ranks,
         *[grow.reshape(owned * width, -1) for grow in (grow_query, grow_key, grow_value)],
     )
-    parts = [sent[0]] + [over_group(sent[shift], shift) for shift in range(1, groups)]
     head_cols = cols - 2 * head_size
+    heads = head_cols // head_size
     mixed = call(
-        functools.partial(attend_kernel, blocks, drafts, groups, cache_size),
-        shape((span, head_cols)),
-        [VMEM] * (groups + blocks),
+        functools.partial(attend_kernel, sizes),
+        shape((blocks * groups, drafts, head_cols)),
+        [VMEM] * 3 + [pl.BlockSpec(memory_space=pltpu.SMEM)] + [VMEM] * 2,
         [
-            pltpu.VMEM((blocks, head_cols // head_size * drafts, head_size), jnp.float32),
+            pltpu.VMEM((blocks, heads * drafts, head_size), jnp.float32),
             pltpu.VMEM((2 * blocks, 128, head_size), jnp.float32),
-            pltpu.VMEM((span, head_cols), jnp.float32),
+            pltpu.VMEM((blocks, drafts, head_cols), jnp.float32),
         ],
-        4 * span * head_cols * cache_size,
-        4 * blocks * cache_size * head_size,
-    )(*parts, *caches)
-    gathered = lax.all_gather(mixed, GROUP, axis=0, tiled=False)
+    )(exchange(sent), cache_keys, cache_values, cache_lengths, cosine, sine)
+    gathered = exchange(mixed)
     out_rows, out_part = call(
         functools.partial(out_rank_kernel, owned),
         [shape((count, head_cols)), shape((blocks * groups, count, lanes))],
         [VMEM] * 3,
         [pltpu.VMEM((count, head_cols), jnp.float32)],
-        2 * count * shrink_out.size,
-        2 * shrink_out.size + 4 * count * head_cols,
     )(gathered, jnp.transpose(shrink_out, (0, 2, 1)).reshape(-1, head_cols), slots)
     out_ranks = exchange(out_part)
-    out_total = stream(out_rows, w_out, 8, 0, head_cols)
+    out_total = stream(out_rows, w_out, 8)
     out_cols = out_total.shape[1]
     leaving = call(
         functools.partial(out_grow_kernel, sizes, width),
@@ -672,7 +595,7 @@
 def local(*arrays):
     heads = arrays[11].shape[1]
     if heads == lax.axis_size("tensor") == lax.axis_size(GROUP):
-        return by_head(*arrays)
+        return by_kernels(*arrays)
     return by_row(*arrays)
 
 

time: 91 us -> 91.3 us (level)
  blocking collectives: 5.79 us -> 26.9 us
  starting transfers between devices: 25.1 us -> 16.9 us
  waiting for transfers between devices: 24.7 us -> 18.5 us
  Pallas kernels: 24.3 us -> 20.2 us
  local copies, waits for them, and re-layouts: 8.95 us -> 6.71 us
    all_to_all x0 -> x2, blocking collectives: none -> 26.9 us  [exchange(): return lax.all_to_all(value, EVERY, split_axis=0, concat_axis=0, tiled=True)]
    ppermute x9 -> x6, waiting for transfers between devices: 22.1 us -> 13.4 us  [over_tensor(): return lax.ppermute(value, 'tensor', route)]
    all_gather x1 -> x0, blocking collectives: 5.79 us -> none  [by_head(): gathered = lax.all_gather(mixed, GROUP, axis=0, tiled=False)]
    ppermute x9 -> x6, starting transfers between devices: 13.8 us -> 8.79 us  [over_tensor(): return lax.ppermute(value, 'tensor', route)]
    pallas_call x9 -> x8, Pallas kernels: 24.3 us -> 20.2 us  [the longest x2 12.8 us: stream(): call(functools.partial(stream_kernel, chunks), shape((rows.shape[0], weig...]
    ppermute x3 -> x0, starting transfers between devices: 2.97 us -> none  [over_group(): return lax.ppermute(value, GROUP, route)]
    all_to_all x2, waiting for transfers between devices: 2.58 us -> 5.12 us  [exchange(): return lax.all_to_all(value, EVERY, split_axis=0, concat_axis=0, tiled=True)]
    unnamed x28 -> x26, local copies, waits for them, and re-layouts: 8.95 us -> 6.71 us
  transfers between devices with their start and end apart: 14 -> 8, of which waited for: 5 -> 5; matrix products, arithmetic and copies ran while one was open for 0% -> 0% of each run, Pallas kernels for 20% -> 15%
where the time goes in v7:
time: 91.3 us; the launch traced here: 90.7 us
  blocking collectives  26.9 us (29%)
  Pallas kernels  20.2 us (22%)
  waiting for transfers between devices  18.5 us (20%)
  starting transfers between devices  16.9 us (19%)
  local copies, waits for them, and re-layouts  6.71 us (7%)
    all_to_all x2, blocking collectives, exchange(): return lax.all_to_all(value, EVERY, split_axis=0, concat_axis=0, tiled=True)  26.9 us
    ppermute x6, waiting for transfers between devices, over_tensor(): return lax.ppermute(value, 'tensor', route)  13.4 us
    pallas_call x2, Pallas kernels, stream(): call(functools.partial(stream_kernel, chunks), shape((rows.shape[0], weig...  12.8 us
    ppermute x6, starting transfers between devices, over_tensor(): return lax.ppermute(value, 'tensor', route)  8.79 us
    all_to_all x2, starting transfers between devices, exchange(): return lax.all_to_all(value, EVERY, split_axis=0, concat_axis=0, tiled=True)  8.1 us
    unnamed x26, local copies, waits for them, and re-layouts  6.71 us
    all_to_all x2, waiting for transfers between devices, exchange(): return lax.all_to_all(value, EVERY, split_axis=0, concat_axis=0, tiled=True)  5.12 us
    pallas_call x1, Pallas kernels, by_kernels(): call(functools.partial(rank_kernel, sizes, owned), [shape((count, feature...  2.11 us
  transfers between devices with their start and end apart: 8, of which 5 were waited for; matrix products, arithmetic and copies ran while one was open for 0% of the time, Pallas kernels for 15%

profile of v7, /device:TPU:0, one launch (start us, length us, event | category | flops | bytes accessed | tf_op | source)
XLA Modules:
  0.0 90.7 jit_solution(5516682702033432686)
XLA Ops:
  0.0 0.0 copy-start.8
  0.0 0.0 copy-start
  0.0 5.0 %collective-permute-start.2 = (bf16[3,4,4096]{2,1,0:T(4,128)(2,1)}, bf16[3,4,4096]{2,1,0:T(4,128)(2,1)S(1)}, u32[]{:S(2)}, u32[]{:S(2)}) collective-permute-start(bf16[3,4,4096]{2,1,0:T(4,128)(2,1)} %bitcast.17), channel_id=1, source_target_pairs={{0,12},{4,0},{8,4},{12,8},{1,13},{5,1},{9,5},{13,9},{2,14},{6,2},{... | collective-permute-start | bytes 294920 | tf_op jit(solution)/shard_map/ppermute | solution.py:335
  5.1 0.0 collective-permute-start.1
  5.1 1.0 %collective-permute-start = (bf16[3,4,4096]{2,1,0:T(4,128)(2,1)}, bf16[3,4,4096]{2,1,0:T(4,128)(2,1)S(1)}, u32[]{:S(2)}, u32[]{:S(2)}) collective-permute-start(bf16[3,4,4096]{2,1,0:T(4,128)(2,1)} %bitcast.19), channel_id=1, source_target_pairs={{0,4},{4,8},{8,12},{12,0},{1,5},{5,9},{9,13},{13,1},{2,6},{6,10},{... | collective-permute-start | bytes 294920 | tf_op jit(solution)/shard_map/ppermute | solution.py:335
  6.7 0.0 copy-start.11
  6.7 0.6 copy-done.11
  7.4 0.0 copy-start.12
  7.4 0.7 copy-done.12
  8.0 0.0 copy-start.2
  8.0 0.0 copy-start.9
  8.0 0.6 shard_map.154
  8.6 0.0 collective-permute-done.2.refs_3_
  8.7 5.4 %collective-permute-done.1.refs_2_ = bf16[3,4,4096]{2,1,0:T(4,128)(2,1)S(1)} collective-permute-done((bf16[3,4,4096]{2,1,0:T(4,128)(2,1)}, bf16[3,4,4096]{2,1,0:T(4,128)(2,1)S(1)}, u32[]{:S(2)}, u32[]{:S(2)}) %collective-permute-start.1) | collective-permute-done | bytes 98336 | tf_op jit(solution)/shard_map/ppermute | solution.py:335
  14.0 0.0 collective-permute-done.refs_1_
  14.0 0.0 copy-done.8
  14.0 0.0 copy-done
  14.0 2.1 %shard_map.155 = (bf16[48,4096]{1,0:T(8,128)(2,1)S(1)}, bf16[16,48,128]{2,1,0:T(8,128)(2,1)}) custom-call(bf16[3,4,4096]{2,1,0:T(4,128)(2,1)S(1)} %bitcast.20, bf16[3,4,4096]{2,1,0:T(4,128)(2,1)S(1)} %collective-permute-done.refs_1_, bf16[3,4,4096]{2,1,0:T(4,128)(2,1)S(1)} %collective-permute-done.1.refs_2_, ...), custom_call_target="tpu_custom_call" | custom-call | flops 150994944 | bytes 3932160 | tf_op jit(solution)/shard_map/pallas_call | solution.py:347
  16.1 4.6 %all-to-all-start = ((bf16[16,48,128]{2,1,0:T(8,128)(2,1)}), bf16[16,48,128]{2,1,0:T(8,128)(2,1)S(1)}, u32[]{:S(2)}, u32[]{:S(2)}) async-start(bf16[16,48,128]{2,1,0:T(8,128)(2,1)} %get-tuple-element.18), calls=%async_computation | async-start | bytes 393216 | tf_op jit(solution)/shard_map/all_to_all | solution.py:338
  20.7 6.4 %shard_map.156.total_ref = f32[48,2048]{1,0:T(8,128)S(1)} custom-call(bf16[48,4096]{1,0:T(8,128)(2,1)S(1)} %get-tuple-element.17.rows_ref, bf16[4096,2048]{1,0:T(8,128)(2,1)} %weight_ref.2), custom_call_target="tpu_custom_call" | custom-call | flops 805306368 | bytes 16777216 | tf_op jit(solution)/shard_map/pallas_call | solution.py:153
  27.1 0.0 copy-start.1
  27.1 2.6 %all-to-all-done.ranks_ref = bf16[16,48,128]{2,1,0:T(8,128)(2,1)S(1)} async-done(((bf16[16,48,128]{2,1,0:T(8,128)(2,1)}), bf16[16,48,128]{2,1,0:T(8,128)(2,1)S(1)}, u32[]{:S(2)}, u32[]{:S(2)}) %all-to-all-start) | async-done | bytes 196640 | tf_op jit(solution)/shard_map/all_to_all | solution.py:338
  29.7 0.0 copy-done.2
  29.7 0.0 copy-done.9
  29.7 0.0 copy-done.10
  29.7 0.0 copy-start.3
  29.7 1.2 %copy-done.3 = bf16[4096,128]{1,0:T(8,128)(2,1)S(1)} copy-done((bf16[4096,128]{1,0:T(8,128)(2,1)S(1)}, bf16[4096,128]{1,0:T(8,128)(2,1)}, u32[]{:S(2)}) %copy-start.3) | copy-done | bytes 1048600
  31.0 1.0 %copy-done.4 = bf16[4,32,2048]{2,1,0:T(8,128)(2,1)S(1)} copy-done((bf16[4,32,2048]{2,1,0:T(8,128)(2,1)S(1)}, bf16[4,32,2048]{2,1,0:T(8,128)(2,1)}, u32[]{:S(2)}) %copy-start.4) | copy-done | bytes 524312
  32.0 1.2 %shard_map.157 = bf16[16,3,2304]{2,1,0:T(4,128)(2,1)S(1)} custom-call(f32[48,2048]{1,0:T(8,128)S(1)} %shard_map.156.total_ref, bf16[48,4096]{1,0:T(8,128)(2,1)S(1)} %get-tuple-element.17.rows_ref, bf16[4096,128]{1,0:T(8,128)(2,1)S(1)} %copy-done.2, bf16[4096,128]{1,0:T(8,128)(2,1)S(1)} %copy-done.3, s32[48,128]{1,0:T(8,128)S(1)} %get-tuple-element.16.refs_5_.slots_ref, ...), custom_call_target="tpu_custom_call" | custom-call | flops 28311552 | bytes 1474560 | tf_op jit(solution)/shard_map/pallas_call | solution.py:358
  33.2 13.9 %all_to_all.20.arrived_ref = bf16[16,3,2304]{2,1,0:T(4,128)(2,1)S(1)} all-to-all(bf16[16,3,2304]{2,1,0:T(4,128)(2,1)S(1)} %shard_map.157), channel_id=1, replica_groups=mesh['parts'=2,'tensor'=4,'dp'=2,'pipe'=2] {'tensor','dp','pipe'}, dimensions={0} | all-to-all | bytes 442368 | tf_op jit(solution)/shard_map/all_to_all | solution.py:338
  47.1 1.0 %copy-done.5 = bf16[1,4,512,128]{3,2,1,0:T(8,128)(2,1)S(1)} copy-done((bf16[1,4,512,128]{3,2,1,0:T(8,128)(2,1)S(1)}, bf16[1,4,512,128]{3,2,1,0:T(8,128)(2,1)}, u32[]{:S(2)}) %copy-start.5) | copy-done | bytes 524312
  48.2 1.0 %copy-done.6 = bf16[1,4,512,128]{3,2,1,0:T(8,128)(2,1)S(1)} copy-done((bf16[1,4,512,128]{3,2,1,0:T(8,128)(2,1)S(1)}, bf16[1,4,512,128]{3,2,1,0:T(8,128)(2,1)}, u32[]{:S(2)}) %copy-start.6) | copy-done | bytes 524312
  49.2 1.8 %shard_map.158 = bf16[16,3,2048]{2,1,0:T(4,128)(2,1)S(1)} custom-call(bf16[16,3,2304]{2,1,0:T(4,128)(2,1)S(1)} %all_to_all.20.arrived_ref, bf16[1,4,512,128]{3,2,1,0:T(8,128)(2,1)S(1)} %copy-done.5, bf16[1,4,512,128]{3,2,1,0:T(8,128)(2,1)S(1)} %copy-done.6, s32[1]{0:T(128)S(6)} %copy.17.length_ref, f32[8,128]{1,0:T(8,128)S(1)} %get-tuple-element.19.cosine_ref, ...), custom_call_target="tpu_custom_call" | custom-call | tf_op jit(solution)/shard_map/pallas_call | solution.py:376
  51.0 13.0 %all_to_all.21.got_ref = bf16[16,3,2048]{2,1,0:T(4,128)(2,1)S(1)} all-to-all(bf16[16,3,2048]{2,1,0:T(4,128)(2,1)S(1)} %shard_map.158), channel_id=1, replica_groups=mesh['parts'=2,'tensor'=4,'dp'=2,'pipe'=2] {'tensor','dp','pipe'}, dimensions={0} | all-to-all | bytes 393216 | tf_op jit(solution)/shard_map/all_to_all | solution.py:338
  63.9 1.0 %copy-done.7 = bf16[4,2048,32]{1,2,0:T(8,128)(2,1)S(1)} copy-done((bf16[4,2048,32]{1,2,0:T(8,128)(2,1)S(1)}, bf16[4,2048,32]{1,2,0:T(8,128)(2,1)}, u32[]{:S(2)}) %copy-start.7) | copy-done | bytes 524312
  65.0 1.1 %shard_map.159 = (bf16[48,2048]{1,0:T(8,128)(2,1)S(1)}, bf16[16,48,128]{2,1,0:T(8,128)(2,1)}) custom-call(bf16[16,3,2048]{2,1,0:T(4,128)(2,1)S(1)} %all_to_all.21.got_ref, bf16[128,2048]{1,0:T(8,128)(2,1)S(1)} %bitcast.16, s32[48,128]{1,0:T(8,128)S(1)} %get-tuple-element.16.refs_5_.slots_ref), custom_call_target="tpu_custom_call" | custom-call | tf_op jit(solution)/shard_map/pallas_call | solution.py:387
  66.1 3.5 %all-to-all-start.3 = ((bf16[16,48,128]{2,1,0:T(8,128)(2,1)}), bf16[16,48,128]{2,1,0:T(8,128)(2,1)S(1)}, u32[]{:S(2)}, u32[]{:S(2)}) async-start(bf16[16,48,128]{2,1,0:T(8,128)(2,1)} %get-tuple-element.22), calls=%async_computation.3 | async-start | bytes 393216 | tf_op jit(solution)/shard_map/all_to_all | solution.py:338
  69.7 6.4 %shard_map.160.total_ref = f32[48,4096]{1,0:T(8,128)S(1)} custom-call(bf16[48,2048]{1,0:T(8,128)(2,1)S(1)} %get-tuple-element.21.rows_ref, bf16[2048,4096]{1,0:T(8,128)(2,1)} %weight_ref.3), custom_call_target="tpu_custom_call" | custom-call | flops 805306368 | bytes 16777216 | tf_op jit(solution)/shard_map/pallas_call | solution.py:153
  76.1 2.6 %all-to-all-done.3.ranks_ref = bf16[16,48,128]{2,1,0:T(8,128)(2,1)S(1)} async-done(((bf16[16,48,128]{2,1,0:T(8,128)(2,1)}), bf16[16,48,128]{2,1,0:T(8,128)(2,1)S(1)}, u32[]{:S(2)}, u32[]{:S(2)}) %all-to-all-start.3) | async-done | bytes 196640 | tf_op jit(solution)/shard_map/all_to_all | solution.py:338
  78.6 0.0 copy-done.1
  78.6 0.5 shard_map.161
  79.2 1.2 %collective-permute-start.3 = (bf16[3,4,4096]{2,1,0:T(4,128)(2,1)S(1)}, bf16[3,4,4096]{2,1,0:T(4,128)(2,1)S(1)}, u32[]{:S(2)}, u32[]{:S(2)}) collective-permute-start(bf16[3,4,4096]{2,1,0:T(4,128)(2,1)S(1)} %get-tuple-element.24), channel_id=1, source_target_pairs={{0,12},{4,0},{8,4},{12,8},{1,13},{5,1},{9,5},{13,9},{2,14},{6,2},{... | collective-permute-start | bytes 294920 | tf_op jit(solution)/shard_map/ppermute | solution.py:335
  80.4 0.0 collective-permute-start.4
  80.4 1.5 %collective-permute-start.5 = (bf16[3,4,4096]{2,1,0:T(4,128)(2,1)S(1)}, bf16[3,4,4096]{2,1,0:T(4,128)(2,1)S(1)}, u32[]{:S(2)}, u32[]{:S(2)}) collective-permute-start(bf16[3,4,4096]{2,1,0:T(4,128)(2,1)S(1)} %get-tuple-element.26), channel_id=1, source_target_pairs={{0,4},{4,8},{8,12},{12,0},{1,5},{5,9},{9,13},{13,1},{2,6},{6,10},{... | collective-permute-start | bytes 294920 | tf_op jit(solution)/shard_map/ppermute | solution.py:335
  81.9 1.9 %collective-permute-done.3 = bf16[3,4,4096]{2,1,0:T(4,128)(2,1)S(1)} collective-permute-done((bf16[3,4,4096]{2,1,0:T(4,128)(2,1)S(1)}, bf16[3,4,4096]{2,1,0:T(4,128)(2,1)S(1)}, u32[]{:S(2)}, u32[]{:S(2)}) %collective-permute-start.3) | collective-permute-done | bytes 98336 | tf_op jit(solution)/shard_map/ppermute | solution.py:335
  83.8 6.1 %collective-permute-done.4 = bf16[3,4,4096]{2,1,0:T(4,128)(2,1)S(1)} collective-permute-done((bf16[3,4,4096]{2,1,0:T(4,128)(2,1)S(1)}, bf16[3,4,4096]{2,1,0:T(4,128)(2,1)S(1)}, u32[]{:S(2)}, u32[]{:S(2)}) %collective-permute-start.4) | collective-permute-done | bytes 98336 | tf_op jit(solution)/shard_map/ppermute | solution.py:335
  89.9 0.0 collective-permute-done.5
  89.9 0.7 fusion
  (5 shorter events, 0.0 us)
Async XLA Ops:
  0.0 14.0 %copy-start.8 = (bf16[4,3,4096]{2,0,1:T(4,128)(2,1)S(1)}, bf16[4,3,4096]{2,0,1:T(4,128)(2,1)}, u32[]{:S(2)}) copy-start(bf16[4,3,4096]{2,0,1:T(4,128)(2,1)} %param.16) | copy-start | bytes 294916
  0.0 14.0 %copy-start = (bf16[4,4096,96]{1,2,0:T(8,128)(2,1)S(1)}, bf16[4,4096,96]{1,2,0:T(8,128)(2,1)}, u32[]{:S(2)}) copy-start(bf16[4,4096,96]{1,2,0:T(8,128)(2,1)} %param.21) | copy-start | bytes 9437188
  0.0 8.6 %collective-permute-start.2 = (bf16[3,4,4096]{2,1,0:T(4,128)(2,1)}, bf16[3,4,4096]{2,1,0:T(4,128)(2,1)S(1)}, u32[]{:S(2)}, u32[]{:S(2)}) collective-permute-start(bf16[3,4,4096]{2,1,0:T(4,128)(2,1)} %bitcast.17), channel_id=1, source_target_pairs={{0,12},{4,0},{8,4},{12,8},{1,13},{5,1},{9,5},{13,9},{2,14},{6,2},{... | collective-permute-start | bytes 294920 | tf_op jit(solution)/shard_map/ppermute | solution.py:335
  5.1 9.0 %collective-permute-start.1 = (bf16[3,4,4096]{2,1,0:T(4,128)(2,1)}, bf16[3,4,4096]{2,1,0:T(4,128)(2,1)S(1)}, u32[]{:S(2)}, u32[]{:S(2)}) collective-permute-start(bf16[3,4,4096]{2,1,0:T(4,128)(2,1)} %bitcast.18), channel_id=1, source_target_pairs={{0,8},{4,12},{8,0},{12,4},{1,9},{5,13},{9,1},{13,5},{2,10},{6,14},... | collective-permute-start | bytes 294920 | tf_op jit(solution)/shard_map/ppermute | solution.py:335
  5.1 9.0 %collective-permute-start = (bf16[3,4,4096]{2,1,0:T(4,128)(2,1)}, bf16[3,4,4096]{2,1,0:T(4,128)(2,1)S(1)}, u32[]{:S(2)}, u32[]{:S(2)}) collective-permute-start(bf16[3,4,4096]{2,1,0:T(4,128)(2,1)} %bitcast.19), channel_id=1, source_target_pairs={{0,4},{4,8},{8,12},{12,0},{1,5},{5,9},{9,13},{13,1},{2,6},{6,10},{... | collective-permute-start | bytes 294920 | tf_op jit(solution)/shard_map/ppermute | solution.py:335
  6.7 0.7 copy-start.11
  7.4 0.7 copy-start.12
  8.0 21.7 %copy-start.2 = (bf16[4096,128]{1,0:T(8,128)(2,1)S(1)}, bf16[4096,128]{1,0:T(8,128)(2,1)}, u32[]{:S(2)}) copy-start(bf16[4096,128]{1,0:T(8,128)(2,1)} %key_ref.1) | copy-start | bytes 3145732
  8.0 21.7 %copy-start.9 = (bf16[4,32,128]{2,1,0:T(8,128)(2,1)S(1)}, bf16[4,32,128]{2,1,0:T(8,128)(2,1)}, u32[]{:S(2)}) copy-start(bf16[4,32,128]{2,1,0:T(8,128)(2,1)} %param.23) | copy-start | bytes 98308
  8.0 21.7 %copy-start.10 = (bf16[4,32,128]{2,1,0:T(8,128)(2,1)S(1)}, bf16[4,32,128]{2,1,0:T(8,128)(2,1)}, u32[]{:S(2)}) copy-start(bf16[4,32,128]{2,1,0:T(8,128)(2,1)} %param.24) | copy-start | bytes 98308
  16.1 13.6 %all-to-all-start = ((bf16[16,48,128]{2,1,0:T(8,128)(2,1)}), bf16[16,48,128]{2,1,0:T(8,128)(2,1)S(1)}, u32[]{:S(2)}, u32[]{:S(2)}) async-start(bf16[16,48,128]{2,1,0:T(8,128)(2,1)} %get-tuple-element.18), calls=%async_computation | async-start | bytes 393216 | tf_op jit(solution)/shard_map/all_to_all | solution.py:338
  27.1 51.5 %copy-start.1 = (bf16[4,32,4096]{2,1,0:T(8,128)(2,1)S(1)}, bf16[4,32,4096]{2,1,0:T(8,128)(2,1)}, u32[]{:S(2)}) copy-start(bf16[4,32,4096]{2,1,0:T(8,128)(2,1)} %param.26) | copy-start | bytes 3145732
  29.7 1.2 %copy-start.3 = (bf16[4096,128]{1,0:T(8,128)(2,1)S(1)}, bf16[4096,128]{1,0:T(8,128)(2,1)}, u32[]{:S(2)}) copy-start(bf16[4096,128]{1,0:T(8,128)(2,1)} %value_ref.1) | copy-start | bytes 3145732
  31.0 1.0 %copy-start.4 = (bf16[4,32,2048]{2,1,0:T(8,128)(2,1)S(1)}, bf16[4,32,2048]{2,1,0:T(8,128)(2,1)}, u32[]{:S(2)}) copy-start(bf16[4,32,2048]{2,1,0:T(8,128)(2,1)} %param.22) | copy-start | bytes 1572868
  47.1 1.0 %copy-start.5 = (bf16[1,4,512,128]{3,2,1,0:T(8,128)(2,1)S(1)}, bf16[1,4,512,128]{3,2,1,0:T(8,128)(2,1)}, u32[]{:S(2)}) copy-start(bf16[1,4,512,128]{3,2,1,0:T(8,128)(2,1)} %keys_ref.1) | copy-start | bytes 1572868
  48.2 1.0 %copy-start.6 = (bf16[1,4,512,128]{3,2,1,0:T(8,128)(2,1)S(1)}, bf16[1,4,512,128]{3,2,1,0:T(8,128)(2,1)}, u32[]{:S(2)}) copy-start(bf16[1,4,512,128]{3,2,1,0:T(8,128)(2,1)} %values_ref.1) | copy-start | bytes 1572868
  63.9 1.0 %copy-start.7 = (bf16[4,2048,32]{1,2,0:T(8,128)(2,1)S(1)}, bf16[4,2048,32]{1,2,0:T(8,128)(2,1)}, u32[]{:S(2)}) copy-start(bf16[4,2048,32]{1,2,0:T(8,128)(2,1)} %param.25) | copy-start | bytes 1572868
  66.1 12.5 %all-to-all-start.3 = ((bf16[16,48,128]{2,1,0:T(8,128)(2,1)}), bf16[16,48,128]{2,1,0:T(8,128)(2,1)S(1)}, u32[]{:S(2)}, u32[]{:S(2)}) async-start(bf16[16,48,128]{2,1,0:T(8,128)(2,1)} %get-tuple-element.22), calls=%async_computation.3 | async-start | bytes 393216 | tf_op jit(solution)/shard_map/all_to_all | solution.py:338
  79.2 4.7 %collective-permute-start.3 = (bf16[3,4,4096]{2,1,0:T(4,128)(2,1)S(1)}, bf16[3,4,4096]{2,1,0:T(4,128)(2,1)S(1)}, u32[]{:S(2)}, u32[]{:S(2)}) collective-permute-start(bf16[3,4,4096]{2,1,0:T(4,128)(2,1)S(1)} %get-tuple-element.24), channel_id=1, source_target_pairs={{0,12},{4,0},{8,4},{12,8},{1,13},{5,1},{9,5},{13,9},{2,14},{6,2},{... | collective-permute-start | bytes 294920 | tf_op jit(solution)/shard_map/ppermute | solution.py:335
  80.4 9.6 %collective-permute-start.4 = (bf16[3,4,4096]{2,1,0:T(4,128)(2,1)S(1)}, bf16[3,4,4096]{2,1,0:T(4,128)(2,1)S(1)}, u32[]{:S(2)}, u32[]{:S(2)}) collective-permute-start(bf16[3,4,4096]{2,1,0:T(4,128)(2,1)S(1)} %get-tuple-element.25), channel_id=1, source_target_pairs={{0,8},{4,12},{8,0},{12,4},{1,9},{5,13},{9,1},{13,5},{2,10},{6,14},... | collective-permute-start | bytes 294920 | tf_op jit(solution)/shard_map/ppermute | solution.py:335
  80.4 9.6 %collective-permute-start.5 = (bf16[3,4,4096]{2,1,0:T(4,128)(2,1)S(1)}, bf16[3,4,4096]{2,1,0:T(4,128)(2,1)S(1)}, u32[]{:S(2)}, u32[]{:S(2)}) collective-permute-start(bf16[3,4,4096]{2,1,0:T(4,128)(2,1)S(1)} %get-tuple-element.26), channel_id=1, source_target_pairs={{0,4},{4,8},{8,12},{12,0},{1,5},{5,9},{9,13},{13,1},{2,6},{6,10},{... | collective-permute-start | bytes 294920 | tf_op jit(solution)/shard_map/ppermute | solution.py:335

commit v8 on v7

--- a/solution.py
+++ b/solution.py
@@ -60,17 +60,17 @@
     return (block * drafts + draft) * groups + group
 
 
-def by_request(sizes, group, block, draft):
-    groups, blocks, drafts = sizes
-    return (block * groups + group) * drafts + draft
+def by_draft(sizes, group, block, draft):
+    groups, blocks, drafts = sizes
+    return (draft * blocks + block) * groups + group
 
 
 def parts_of(order, sizes, index):
     groups, blocks, drafts = sizes
-    block = over(index, groups * drafts)
+    group, left = rest_of(index, groups), over(index, groups)
     if order is as_gathered:
-        return rest_of(index, groups), block, rest_of(over(index, groups), drafts)
-    return rest_of(over(index, drafts), groups), block, rest_of(index, drafts)
+        return group, over(left, drafts), rest_of(left, drafts)
+    return group, rest_of(left, blocks), over(left, blocks)
 
 
 def turned(block, blocks):
@@ -103,7 +103,7 @@
     ranks = owned_ranks(
         rows, shrink_ref[...], place, shrink_ref.shape[0] // owned, rank_ref.shape[2]
     )
-    ranks = dot(reorder(sizes, by_request, as_gathered), ranks).astype(jnp.bfloat16)
+    ranks = dot(reorder(sizes, by_draft, as_gathered), ranks).astype(jnp.bfloat16)
     for target in range(rank_ref.shape[0]):
         rank_ref[target] = ranks
 
@@ -128,7 +128,8 @@
     return jnp.where(slot == place, wide, 0.0).astype(jnp.bfloat16)
 
 
-def stream_kernel(chunks, rows_ref, weight_ref, total_ref, buffer, sems):
+def stream_kernel(chunks, rows_ref, weight_ref, *refs):
+    total_ref, buffer, sems = refs[-3:]
     depth = rows_ref.shape[1] // chunks
 
     def copy(chunk):
@@ -149,16 +150,16 @@
             total_ref[...] = product
 
 
-def stream(rows, weight, chunks):
+def stream(rows, weight, chunks, later=()):
     return call(
         functools.partial(stream_kernel, chunks),
         shape((rows.shape[0], weight.shape[1]), jnp.float32),
-        [VMEM, HBM],
+        [VMEM, HBM] + [HBM] * len(later),
         [pltpu.VMEM(weight.shape, weight.dtype), pltpu.SemaphoreType.DMA((chunks,))],
         2 * rows.shape[0] * weight.size,
         2 * weight.size,
         40 * MIB,
-    )(rows, weight)
+    )(rows, weight, *later)
 
 
 def prepare_kernel(sizes, ids_ref, pool_ref, length_ref, _, slots_ref, cosine_ref, sine_ref):
@@ -166,14 +167,14 @@
     width = cosine_ref.shape[1]
     lane = iota(cosine_ref.shape, 1)
     half = (lane & (width // 2 - 1)).astype(jnp.float32)
-    positions = (iota(cosine_ref.shape, 0) + length_ref[0]).astype(jnp.float32)
+    positions = (lax.rem(iota(cosine_ref.shape, 0), drafts) + length_ref[0]).astype(jnp.float32)
     angles = positions * jnp.exp(half * (-2.0 * math.log(rope_base) / width))
     cosine_ref[...] = jnp.cos(angles)
     sine_ref[...] = jnp.sin(angles) * jnp.where(lane < width // 2, -1.0, 1.0)
     index = iota(slots_ref.shape, 0)
     column = iota(slots_ref.shape, 1)
     near = parts_of(as_gathered, sizes, index)
-    far = parts_of(by_request, sizes, index)
+    far = parts_of(by_draft, sizes, index)
     row_group = jnp.where(column == 0, near[0], far[0])
     row_block = jnp.where(column == 0, turned(near[1], blocks), far[1])
     place = row_block * groups + row_group
@@ -183,10 +184,10 @@
     slots_ref[...] = slots
 
 
-def prepare(sizes, ids, pool, lengths, head_size, later):
+def prepare(sizes, ids, pool, lengths, table, later):
     groups, blocks, drafts = sizes
     smem = pl.BlockSpec(memory_space=pltpu.SMEM)
-    table = shape((8 * -(-drafts // 8), head_size), jnp.float32)
+    table = shape(table, jnp.float32)
     return call(
         functools.partial(prepare_kernel, sizes),
         [shape((groups * blocks * drafts, 128), jnp.int32), table, table],
@@ -199,16 +200,19 @@
     sizes, width, total_ref, rows_ref, key_ref, value_ref, slots_ref, ranks_ref, *refs
 ):
     groups, blocks, drafts = sizes
-    *grows, out_ref = refs
+    *grows, out_ref, held = refs
     group = group_of()
+    requests = groups * blocks
+    lines = out_ref.shape[1]
+    held[...] = jnp.zeros(held.shape, jnp.float32)
     owned = grows[0].shape[0] // width
     ranks = ranks_ref[group * groups].astype(jnp.float32)
     for other in range(1, groups):
         ranks = ranks + ranks_ref[group * groups + other].astype(jnp.float32)
-    ranks = dot(reorder(sizes, as_gathered, by_request), ranks.astype(jnp.bfloat16))
+    ranks = dot(reorder(sizes, as_gathered, by_draft), ranks.astype(jnp.bfloat16))
     place = slots_ref[:, 0:1] - group * owned
     wide = spread_ranks(ranks.astype(jnp.bfloat16), place, width, owned, len(grows))
-    arranged = reorder(sizes, by_request, as_gathered)
+    arranged = reorder(sizes, by_draft, as_gathered)
     start = 0
     for index, grow in enumerate(grows):
         deep, cols = grow.shape
@@ -217,38 +221,35 @@
         else:
             full = dot(rows_ref[...], (key_ref, value_ref)[index - 1][...])
         full = full + dot(wide[:, index * deep : (index + 1) * deep], grow[...])
-        full = dot(arranged, full.astype(jnp.bfloat16)).astype(jnp.bfloat16)
-        for row in range(groups * blocks):
-            out_ref[row, :, start : start + cols] = full[row * drafts : (row + 1) * drafts]
-        start += cols
+        full = dot(arranged, full.astype(jnp.bfloat16))
+        for head in range(cols // 128):
+            for draft in range(drafts):
+                held[pl.ds(start + draft, requests, stride=lines), :] = full[
+                    draft * requests : (draft + 1) * requests, head * 128 : (head + 1) * 128
+                ]
+            start += drafts
+    for row in range(requests):
+        out_ref[row] = held[row * lines : (row + 1) * lines, :].astype(jnp.bfloat16)
 
 
 def attend_kernel(
     sizes, arrived_ref, keys_ref, values_ref, length_ref, cosine_ref, sine_ref, out_ref, *scratch
 ):
     groups, blocks, drafts = sizes
-    query_s, fresh_s, out_s = scratch
+    (fresh_s,) = scratch
     cache_size, head_size = keys_ref.shape[2:]
-    heads = arrived_ref.shape[2] // head_size - 2
+    count = out_ref.shape[1]
     scale = 1.0 / math.sqrt(head_size)
     fresh_s[...] = jnp.zeros(fresh_s.shape, jnp.float32)
-    cosine = cosine_ref[0:drafts, :]
-    sine = sine_ref[0:drafts, :]
     for block in range(blocks):
         joined = arrived_ref[block * groups].astype(jnp.float32)
         for other in range(1, groups):
             joined = joined + arrived_ref[block * groups + other].astype(jnp.float32)
         joined = joined.astype(jnp.bfloat16).astype(jnp.float32)
-
-        def rotated(head):
-            value = joined[:, head * head_size : (head + 1) * head_size]
-            return value * cosine + pltpu.roll(value, head_size // 2, 1) * sine
-
-        for head in range(heads):
-            query_s[block, head * drafts : (head + 1) * drafts, :] = rotated(head)
-        fresh_s[2 * block, 0:drafts, :] = rotated(heads)
-        fresh_s[2 * block + 1, 0:drafts, :] = joined[:, (heads + 1) * head_size :]
-        query = query_s[block].astype(jnp.bfloat16)
+        rotated = joined * cosine_ref[...] + pltpu.roll(joined, head_size // 2, 1) * sine_ref[...]
+        fresh_s[2 * block, 0:drafts, :] = rotated[count : count + drafts]
+        fresh_s[2 * block + 1, 0:drafts, :] = joined[count + drafts : count + 2 * drafts]
+        query = rotated[0:count].astype(jnp.bfloat16)
         old = dot_nt(query, keys_ref[0, block]) * scale
         new = dot_nt(query, fresh_s[2 * block].astype(jnp.bfloat16)) * scale
         old = jnp.where(iota(old.shape, 1) < length_ref[0], old, -jnp.inf)
@@ -261,25 +262,42 @@
         mixed = dot((old / below).astype(jnp.bfloat16), values_ref[0, block]) + dot(
             (new / below).astype(jnp.bfloat16), fresh_s[2 * block + 1].astype(jnp.bfloat16)
         )
-        for head in range(heads):
-            out_s[block, 0:drafts, head * head_size : (head + 1) * head_size] = mixed[
-                head * drafts : (head + 1) * drafts
-            ]
-        result = out_s[block, 0:drafts, :].astype(jnp.bfloat16)
+        mixed = mixed.astype(jnp.bfloat16)
         for target in range(groups):
-            out_ref[block * groups + target] = result
-
-
-def out_rank_kernel(owned, got_ref, shrink_ref, slots_ref, rows_ref, rank_ref, wide):
-    drafts = got_ref.shape[1]
-    for row in range(got_ref.shape[0]):
-        wide[row * drafts : (row + 1) * drafts, :] = got_ref[row].astype(jnp.float32)
-    rows = wide[...].astype(jnp.bfloat16)
-    rows_ref[...] = rows
+            out_ref[block * groups + target] = mixed
+
+
+def packing(rows, width, lanes):
+    parts = lanes // width
+    return parts, rows // parts
+
+
+def out_rank_kernel(sizes, owned, got_ref, shrink_ref, slots_ref, rows_ref, rank_ref, wide):
+    drafts = sizes[2]
+    requests, lines, head_size = got_ref.shape
+    for row in range(requests):
+        wide[row * lines : (row + 1) * lines, :] = got_ref[row].astype(jnp.float32)
+    for head in range(lines // drafts):
+        for draft in range(drafts):
+            rows_ref[
+                draft * requests : (draft + 1) * requests,
+                head * head_size : (head + 1) * head_size,
+            ] = wide[pl.ds(head * drafts + draft, requests, stride=lines), :].astype(jnp.bfloat16)
+    rows = rows_ref[...]
     place = slots_ref[:, 1:2] - group_of() * owned
-    ranks = owned_ranks(
-        rows, shrink_ref[...], place, shrink_ref.shape[0] // owned, rank_ref.shape[2]
-    )
+    width = shrink_ref.shape[0] // owned
+    _, held, lanes = rank_ref.shape
+    parts, span = packing(rows.shape[0], width, lanes)
+    ranks = dot_nt(rows, shrink_ref[...])
+    kept = jnp.where(over(iota(ranks.shape, 1), width) == place, ranks, 0.0).astype(jnp.bfloat16)
+    fold = (ranks.shape[1], lanes)
+    fold = rest_of(iota(fold, 0), width) == rest_of(iota(fold, 1), width)
+    ranks = dot(kept, jnp.where(fold, 1.0, 0.0).astype(jnp.bfloat16))
+    mine = over(iota(ranks.shape, 1), width) == over(iota(ranks.shape, 0), span)
+    ranks = jnp.where(mine, ranks, 0.0).astype(jnp.bfloat16)
+    put = (held, rows.shape[0])
+    put = iota(put, 0) == rest_of(iota(put, 1), span)
+    ranks = dot(jnp.where(put, 1.0, 0.0).astype(jnp.bfloat16), ranks).astype(jnp.bfloat16)
     for target in range(rank_ref.shape[0]):
         rank_ref[target] = ranks
 
@@ -291,10 +309,20 @@
     ranks = ranks_ref[me].astype(jnp.float32)
     for source in range(1, blocks):
         ranks = ranks + ranks_ref[source * groups + me].astype(jnp.float32)
+    count = total_ref.shape[0]
+    held, lanes = ranks.shape
+    parts, span = packing(count, width, lanes)
+    put = rest_of(iota((count, held), 0), span) == iota((count, held), 1)
+    ranks = dot(jnp.where(put, 1.0, 0.0).astype(jnp.bfloat16), ranks.astype(jnp.bfloat16))
+    mine = over(iota(ranks.shape, 1), width) == over(iota(ranks.shape, 0), span)
+    ranks = jnp.where(mine, ranks, 0.0).astype(jnp.bfloat16)
+    tile = (lanes, owned * width)
+    tile = rest_of(iota(tile, 0), width) == rest_of(iota(tile, 1), width)
+    ranks = dot(ranks, jnp.where(tile, 1.0, 0.0).astype(jnp.bfloat16))
     place = slots_ref[:, 1:2] - me * owned
-    wide = spread_ranks(ranks.astype(jnp.bfloat16), place, width, owned, 1)
+    wide = jnp.where(over(iota(ranks.shape, 1), width) == place, ranks, 0.0).astype(jnp.bfloat16)
     full = (total_ref[...] + dot(wide, grow_ref[...])).astype(jnp.bfloat16)
-    full = dot(reorder(sizes, as_gathered, by_request), full).astype(jnp.bfloat16)
+    full = dot(reorder(sizes, as_gathered, by_draft), full).astype(jnp.bfloat16)
     for block in range(blocks):
         for draft in range(drafts):
             start = (block * drafts + draft) * groups
@@ -340,8 +368,10 @@
     mine = jnp.transpose(tokens, (1, 0, 2))
     pieces = [mine] + [over_tensor(mine, shift) for shift in range(1, blocks)]
 
+    lines = (w_query.shape[1] // head_size + 2) * drafts
+    lines = -(-lines // 8) * 8
     slots, cosine, sine = prepare(
-        sizes, adapter_ids, adapter_slots, cache_lengths, head_size, w_out
+        sizes, adapter_ids, adapter_slots, cache_lengths, (lines, head_size), w_out
     )
     shrink_in = jnp.transpose(shrink_qkv, (0, 2, 1)).reshape(-1, features)
     rows, rank_part = call(
@@ -353,13 +383,15 @@
         2 * shrink_qkv.size + 4 * count * features,
     )(*pieces, shrink_in, slots)
     ranks = exchange(rank_part)
-    total = stream(rows, w_query, 8)
+    total = stream(rows, w_query, 8, [w_out] * 3)
     cols = total.shape[1] + w_key.shape[1] + w_value.shape[1]
+    head_cols = total.shape[1]
+    query_lines = head_cols // head_size * drafts
     sent = call(
         functools.partial(grow_kernel, sizes, width),
-        shape((blocks * groups, drafts, cols)),
+        shape((blocks * groups, lines, head_size)),
         [VMEM] * 9,
-        [],
+        [pltpu.VMEM((blocks * groups * lines, head_size), jnp.float32)],
         2 * count * owned * width * cols,
         8 * count * cols + 2 * owned * width * cols,
     )(
@@ -371,24 +403,19 @@
         ranks,
         *[grow.reshape(owned * width, -1) for grow in (grow_query, grow_key, grow_value)],
     )
-    head_cols = cols - 2 * head_size
-    heads = head_cols // head_size
     mixed = call(
         functools.partial(attend_kernel, sizes),
-        shape((blocks * groups, drafts, head_cols)),
+        shape((blocks * groups, query_lines, head_size)),
         [VMEM] * 3 + [pl.BlockSpec(memory_space=pltpu.SMEM)] + [VMEM] * 2,
-        [
-            pltpu.VMEM((blocks, heads * drafts, head_size), jnp.float32),
-            pltpu.VMEM((2 * blocks, 128, head_size), jnp.float32),
-            pltpu.VMEM((blocks, drafts, head_cols), jnp.float32),
-        ],
+        [pltpu.VMEM((2 * blocks, 128, head_size), jnp.float32)],
     )(exchange(sent), cache_keys, cache_values, cache_lengths, cosine, sine)
     gathered = exchange(mixed)
+    held = -(-packing(count, width, 128)[1] // 16) * 16
     out_rows, out_part = call(
-        functools.partial(out_rank_kernel, owned),
-        [shape((count, head_cols)), shape((blocks * groups, count, lanes))],
+        functools.partial(out_rank_kernel, sizes, owned),
+        [shape((count, head_cols)), shape((blocks * groups, held, 128))],
         [VMEM] * 3,
-        [pltpu.VMEM((count, head_cols), jnp.float32)],
+        [pltpu.VMEM((blocks * groups * query_lines, head_size), jnp.float32)],
     )(gathered, jnp.transpose(shrink_out, (0, 2, 1)).reshape(-1, head_cols), slots)
     out_ranks = exchange(out_part)
     out_total = stream(out_rows, w_out, 8)

time: 91.3 us -> 88.8 us (0.973)
  blocking collectives: 26.9 us -> 24.6 us
  waiting for transfers between devices: 18.5 us -> 16.4 us
  starting transfers between devices: 16.9 us -> 18.5 us
    all_to_all x2, blocking collectives: 26.9 us -> 24.6 us  [exchange(): return lax.all_to_all(value, EVERY, split_axis=0, concat_axis=0, tiled=True)]
    all_to_all x2, waiting for transfers between devices: 5.12 us -> 2.91 us  [exchange(): return lax.all_to_all(value, EVERY, split_axis=0, concat_axis=0, tiled=True)]
    ppermute x6, starting transfers between devices: 8.79 us -> 10.5 us  [over_tensor(): return lax.ppermute(value, 'tensor', route)]
where the time goes in v8:
time: 88.8 us; the launch traced here: 88.2 us
  blocking collectives  24.6 us (28%)
  Pallas kernels  20.5 us (23%)
  starting transfers between devices  18.5 us (21%)
  waiting for transfers between devices  16.4 us (18%)
  local copies, waits for them, and re-layouts  6.72 us (8%)
    all_to_all x2, blocking collectives, exchange(): return lax.all_to_all(value, EVERY, split_axis=0, concat_axis=0, tiled=True)  24.6 us
    ppermute x6, waiting for transfers between devices, over_tensor(): return lax.ppermute(value, 'tensor', route)  13.4 us
    pallas_call x2, Pallas kernels, stream(): call(functools.partial(stream_kernel, chunks), shape((rows.shape[0], weig...  12.9 us
    ppermute x6, starting transfers between devices, over_tensor(): return lax.ppermute(value, 'tensor', route)  10.5 us
    all_to_all x2, starting transfers between devices, exchange(): return lax.all_to_all(value, EVERY, split_axis=0, concat_axis=0, tiled=True)  8.08 us
    unnamed x26, local copies, waits for them, and re-layouts  6.72 us
    all_to_all x2, waiting for transfers between devices, exchange(): return lax.all_to_all(value, EVERY, split_axis=0, concat_axis=0, tiled=True)  2.91 us
    pallas_call x1, Pallas kernels, by_kernels(): call(functools.partial(rank_kernel, sizes, owned), [shape((count, feature...  2.11 us
  transfers between devices with their start and end apart: 8, of which 5 were waited for; matrix products, arithmetic and copies ran while one was open for 0% of the time, Pallas kernels for 15%

profile of v8, /device:TPU:0, one launch (start us, length us, event | category | flops | bytes accessed | tf_op | source)
XLA Modules:
  0.0 88.2 jit_solution(4905801221605407795)
XLA Ops:
  0.0 0.0 copy-start.8
  0.0 0.0 copy-start
  0.0 5.0 %collective-permute-start.2 = (bf16[3,4,4096]{2,1,0:T(4,128)(2,1)}, bf16[3,4,4096]{2,1,0:T(4,128)(2,1)S(1)}, u32[]{:S(2)}, u32[]{:S(2)}) collective-permute-start(bf16[3,4,4096]{2,1,0:T(4,128)(2,1)} %bitcast.17), channel_id=1, source_target_pairs={{0,12},{4,0},{8,4},{12,8},{1,13},{5,1},{9,5},{13,9},{2,14},{6,2},{... | collective-permute-start | bytes 294920 | tf_op jit(solution)/shard_map/ppermute | solution.py:363
  5.1 0.0 collective-permute-start.1
  5.1 1.0 %collective-permute-start = (bf16[3,4,4096]{2,1,0:T(4,128)(2,1)}, bf16[3,4,4096]{2,1,0:T(4,128)(2,1)S(1)}, u32[]{:S(2)}, u32[]{:S(2)}) collective-permute-start(bf16[3,4,4096]{2,1,0:T(4,128)(2,1)} %bitcast.19), channel_id=1, source_target_pairs={{0,4},{4,8},{8,12},{12,0},{1,5},{5,9},{9,13},{13,1},{2,6},{6,10},{... | collective-permute-start | bytes 294920 | tf_op jit(solution)/shard_map/ppermute | solution.py:363
  6.7 0.0 copy-start.11
  6.7 0.6 copy-done.11
  7.4 0.7 copy-done.12
  8.0 0.7 shard_map.154
  8.7 0.0 collective-permute-done.2.refs_3_
  8.8 5.3 %collective-permute-done.1.refs_2_ = bf16[3,4,4096]{2,1,0:T(4,128)(2,1)S(1)} collective-permute-done((bf16[3,4,4096]{2,1,0:T(4,128)(2,1)}, bf16[3,4,4096]{2,1,0:T(4,128)(2,1)S(1)}, u32[]{:S(2)}, u32[]{:S(2)}) %collective-permute-start.1) | collective-permute-done | bytes 98336 | tf_op jit(solution)/shard_map/ppermute | solution.py:363
  14.0 0.0 collective-permute-done.refs_1_
  14.0 0.0 copy-done.8
  14.0 0.0 copy-done
  14.0 2.1 %shard_map.155 = (bf16[48,4096]{1,0:T(8,128)(2,1)S(1)}, bf16[16,48,128]{2,1,0:T(8,128)(2,1)}) custom-call(bf16[3,4,4096]{2,1,0:T(4,128)(2,1)S(1)} %bitcast.20, bf16[3,4,4096]{2,1,0:T(4,128)(2,1)S(1)} %collective-permute-done.refs_1_, bf16[3,4,4096]{2,1,0:T(4,128)(2,1)S(1)} %collective-permute-done.1.refs_2_, ...), custom_call_target="tpu_custom_call" | custom-call | flops 150994944 | bytes 3932160 | tf_op jit(solution)/shard_map/pallas_call | solution.py:377
  16.1 4.6 %all-to-all-start = ((bf16[16,48,128]{2,1,0:T(8,128)(2,1)}), bf16[16,48,128]{2,1,0:T(8,128)(2,1)S(1)}, u32[]{:S(2)}, u32[]{:S(2)}) async-start(bf16[16,48,128]{2,1,0:T(8,128)(2,1)} %get-tuple-element.18), calls=%async_computation | async-start | bytes 393216 | tf_op jit(solution)/shard_map/all_to_all | solution.py:366
  20.7 0.0 copy-start.2
  20.7 0.0 copy-start.9
  20.7 0.0 copy-start.10
  20.8 6.5 %shard_map.156.total_ref = f32[48,2048]{1,0:T(8,128)S(1)} custom-call(bf16[48,4096]{1,0:T(8,128)(2,1)S(1)} %get-tuple-element.17.rows_ref, bf16[4096,2048]{1,0:T(8,128)(2,1)} %weight_ref.2, bf16[2048,4096]{1,0:T(8,128)(2,1)} %weight_ref.3, bf16[2048,4096]{1,0:T(8,128)(2,1)} %weight_ref.3, bf16[2048,4096]{1,0:T(8,128)(2,1)} %weight_ref.3), custom_call_target="tpu_custom_call" | custom-call | flops 805306368 | bytes 16777216 | tf_op jit(solution)/shard_map/pallas_call | solution.py:154
  27.2 0.0 copy-start.1
  27.3 2.5 %all-to-all-done.ranks_ref = bf16[16,48,128]{2,1,0:T(8,128)(2,1)S(1)} async-done(((bf16[16,48,128]{2,1,0:T(8,128)(2,1)}), bf16[16,48,128]{2,1,0:T(8,128)(2,1)S(1)}, u32[]{:S(2)}, u32[]{:S(2)}) %all-to-all-start) | async-done | bytes 196640 | tf_op jit(solution)/shard_map/all_to_all | solution.py:366
  29.7 0.0 copy-done.2
  29.7 0.0 copy-done.9
  29.7 0.0 copy-done.10
  29.7 0.0 copy-start.3
  29.7 1.2 %copy-done.3 = bf16[4096,128]{1,0:T(8,128)(2,1)S(1)} copy-done((bf16[4096,128]{1,0:T(8,128)(2,1)S(1)}, bf16[4096,128]{1,0:T(8,128)(2,1)}, u32[]{:S(2)}) %copy-start.3) | copy-done | bytes 1048600
  31.0 1.0 %copy-done.7 = bf16[4,32,2048]{2,1,0:T(8,128)(2,1)S(1)} copy-done((bf16[4,32,2048]{2,1,0:T(8,128)(2,1)S(1)}, bf16[4,32,2048]{2,1,0:T(8,128)(2,1)}, u32[]{:S(2)}) %copy-start.7) | copy-done | bytes 524312
  32.0 1.2 %shard_map.157 = bf16[16,56,128]{2,1,0:T(8,128)(2,1)S(1)} custom-call(f32[48,2048]{1,0:T(8,128)S(1)} %shard_map.156.total_ref, bf16[48,4096]{1,0:T(8,128)(2,1)S(1)} %get-tuple-element.17.rows_ref, bf16[4096,128]{1,0:T(8,128)(2,1)S(1)} %copy-done.2, bf16[4096,128]{1,0:T(8,128)(2,1)S(1)} %copy-done.3, s32[48,128]{1,0:T(8,128)S(1)} %get-tuple-element.16.refs_5_.slots_ref, ...), custom_call_target="tpu_custom_call" | custom-call | flops 28311552 | bytes 1474560 | tf_op jit(solution)/shard_map/pallas_call | solution.py:390
  33.2 13.0 %all_to_all.20.arrived_ref = bf16[16,56,128]{2,1,0:T(8,128)(2,1)S(1)} all-to-all(bf16[16,56,128]{2,1,0:T(8,128)(2,1)S(1)} %shard_map.157), channel_id=1, replica_groups=mesh['parts'=2,'tensor'=4,'dp'=2,'pipe'=2] {'tensor','dp','pipe'}, dimensions={0} | all-to-all | bytes 458752 | tf_op jit(solution)/shard_map/all_to_all | solution.py:366
  46.2 1.0 %copy-done.4 = bf16[1,4,512,128]{3,2,1,0:T(8,128)(2,1)S(1)} copy-done((bf16[1,4,512,128]{3,2,1,0:T(8,128)(2,1)S(1)}, bf16[1,4,512,128]{3,2,1,0:T(8,128)(2,1)}, u32[]{:S(2)}) %copy-start.4) | copy-done | bytes 524312
  47.2 1.0 %copy-done.5 = bf16[1,4,512,128]{3,2,1,0:T(8,128)(2,1)S(1)} copy-done((bf16[1,4,512,128]{3,2,1,0:T(8,128)(2,1)S(1)}, bf16[1,4,512,128]{3,2,1,0:T(8,128)(2,1)}, u32[]{:S(2)}) %copy-start.5) | copy-done | bytes 524312
  48.3 1.7 %shard_map.158 = bf16[16,48,128]{2,1,0:T(8,128)(2,1)S(1)} custom-call(bf16[16,56,128]{2,1,0:T(8,128)(2,1)S(1)} %all_to_all.20.arrived_ref, bf16[1,4,512,128]{3,2,1,0:T(8,128)(2,1)S(1)} %copy-done.4, bf16[1,4,512,128]{3,2,1,0:T(8,128)(2,1)S(1)} %copy-done.5, s32[1]{0:T(128)S(6)} %copy.17.length_ref, f32[56,128]{1,0:T(8,128)S(1)} %get-tuple-element.19.cosine_ref, ...), custom_call_target="tpu_custom_call" | custom-call | tf_op jit(solution)/shard_map/pallas_call | solution.py:406
  50.0 11.6 %all_to_all.21.got_ref = bf16[16,48,128]{2,1,0:T(8,128)(2,1)S(1)} all-to-all(bf16[16,48,128]{2,1,0:T(8,128)(2,1)S(1)} %shard_map.158), channel_id=1, replica_groups=mesh['parts'=2,'tensor'=4,'dp'=2,'pipe'=2] {'tensor','dp','pipe'}, dimensions={0} | all-to-all | bytes 393216 | tf_op jit(solution)/shard_map/all_to_all | solution.py:366
  61.7 1.0 %copy-done.6 = bf16[4,2048,32]{1,2,0:T(8,128)(2,1)S(1)} copy-done((bf16[4,2048,32]{1,2,0:T(8,128)(2,1)S(1)}, bf16[4,2048,32]{1,2,0:T(8,128)(2,1)}, u32[]{:S(2)}) %copy-start.6) | copy-done | bytes 524312
  62.7 1.2 %shard_map.159 = (bf16[48,2048]{1,0:T(8,128)(2,1)S(1)}, bf16[16,16,128]{2,1,0:T(8,128)(2,1)}) custom-call(bf16[16,48,128]{2,1,0:T(8,128)(2,1)S(1)} %all_to_all.21.got_ref, bf16[128,2048]{1,0:T(8,128)(2,1)S(1)} %bitcast.15, s32[48,128]{1,0:T(8,128)S(1)} %get-tuple-element.16.refs_5_.slots_ref), custom_call_target="tpu_custom_call" | custom-call | tf_op jit(solution)/shard_map/pallas_call | solution.py:414
  63.9 3.5 %all-to-all-start.3 = ((bf16[16,16,128]{2,1,0:T(8,128)(2,1)}), bf16[16,16,128]{2,1,0:T(8,128)(2,1)S(1)}, u32[]{:S(2)}, u32[]{:S(2)}) async-start(bf16[16,16,128]{2,1,0:T(8,128)(2,1)} %get-tuple-element.22), calls=%async_computation.3 | async-start | bytes 131072 | tf_op jit(solution)/shard_map/all_to_all | solution.py:366
  67.4 6.4 %shard_map.160.total_ref = f32[48,4096]{1,0:T(8,128)S(1)} custom-call(bf16[48,2048]{1,0:T(8,128)(2,1)S(1)} %get-tuple-element.21.rows_ref, bf16[2048,4096]{1,0:T(8,128)(2,1)} %weight_ref.3), custom_call_target="tpu_custom_call" | custom-call | flops 805306368 | bytes 16777216 | tf_op jit(solution)/shard_map/pallas_call | solution.py:154
  73.8 0.4 all-to-all-done.3.ranks_ref
  74.3 0.0 copy-done.1
  74.3 0.6 shard_map.161
  74.9 3.3 %collective-permute-start.3 = (bf16[3,4,4096]{2,1,0:T(4,128)(2,1)S(1)}, bf16[3,4,4096]{2,1,0:T(4,128)(2,1)S(1)}, u32[]{:S(2)}, u32[]{:S(2)}) collective-permute-start(bf16[3,4,4096]{2,1,0:T(4,128)(2,1)S(1)} %get-tuple-element.24), channel_id=1, source_target_pairs={{0,12},{4,0},{8,4},{12,8},{1,13},{5,1},{9,5},{13,9},{2,14},{6,2},{... | collective-permute-start | bytes 294920 | tf_op jit(solution)/shard_map/ppermute | solution.py:363
  78.2 0.0 collective-permute-start.4
  78.2 1.1 %collective-permute-start.5 = (bf16[3,4,4096]{2,1,0:T(4,128)(2,1)S(1)}, bf16[3,4,4096]{2,1,0:T(4,128)(2,1)S(1)}, u32[]{:S(2)}, u32[]{:S(2)}) collective-permute-start(bf16[3,4,4096]{2,1,0:T(4,128)(2,1)S(1)} %get-tuple-element.26), channel_id=1, source_target_pairs={{0,4},{4,8},{8,12},{12,0},{1,5},{5,9},{9,13},{13,1},{2,6},{6,10},{... | collective-permute-start | bytes 294920 | tf_op jit(solution)/shard_map/ppermute | solution.py:363
  79.3 2.1 %collective-permute-done.3 = bf16[3,4,4096]{2,1,0:T(4,128)(2,1)S(1)} collective-permute-done((bf16[3,4,4096]{2,1,0:T(4,128)(2,1)S(1)}, bf16[3,4,4096]{2,1,0:T(4,128)(2,1)S(1)}, u32[]{:S(2)}, u32[]{:S(2)}) %collective-permute-start.3) | collective-permute-done | bytes 98336 | tf_op jit(solution)/shard_map/ppermute | solution.py:363
  81.4 6.1 %collective-permute-done.4 = bf16[3,4,4096]{2,1,0:T(4,128)(2,1)S(1)} collective-permute-done((bf16[3,4,4096]{2,1,0:T(4,128)(2,1)S(1)}, bf16[3,4,4096]{2,1,0:T(4,128)(2,1)S(1)}, u32[]{:S(2)}, u32[]{:S(2)}) %collective-permute-start.4) | collective-permute-done | bytes 98336 | tf_op jit(solution)/shard_map/ppermute | solution.py:363
  87.5 0.0 collective-permute-done.5
  87.5 0.7 fusion
  (5 shorter events, 0.0 us)
Async XLA Ops:
  0.0 14.0 %copy-start.8 = (bf16[4,3,4096]{2,0,1:T(4,128)(2,1)S(1)}, bf16[4,3,4096]{2,0,1:T(4,128)(2,1)}, u32[]{:S(2)}) copy-start(bf16[4,3,4096]{2,0,1:T(4,128)(2,1)} %param.16) | copy-start | bytes 294916
  0.0 14.0 %copy-start = (bf16[4,4096,96]{1,2,0:T(8,128)(2,1)S(1)}, bf16[4,4096,96]{1,2,0:T(8,128)(2,1)}, u32[]{:S(2)}) copy-start(bf16[4,4096,96]{1,2,0:T(8,128)(2,1)} %param.21) | copy-start | bytes 9437188
  0.0 8.7 %collective-permute-start.2 = (bf16[3,4,4096]{2,1,0:T(4,128)(2,1)}, bf16[3,4,4096]{2,1,0:T(4,128)(2,1)S(1)}, u32[]{:S(2)}, u32[]{:S(2)}) collective-permute-start(bf16[3,4,4096]{2,1,0:T(4,128)(2,1)} %bitcast.17), channel_id=1, source_target_pairs={{0,12},{4,0},{8,4},{12,8},{1,13},{5,1},{9,5},{13,9},{2,14},{6,2},{... | collective-permute-start | bytes 294920 | tf_op jit(solution)/shard_map/ppermute | solution.py:363
  5.1 9.0 %collective-permute-start.1 = (bf16[3,4,4096]{2,1,0:T(4,128)(2,1)}, bf16[3,4,4096]{2,1,0:T(4,128)(2,1)S(1)}, u32[]{:S(2)}, u32[]{:S(2)}) collective-permute-start(bf16[3,4,4096]{2,1,0:T(4,128)(2,1)} %bitcast.18), channel_id=1, source_target_pairs={{0,8},{4,12},{8,0},{12,4},{1,9},{5,13},{9,1},{13,5},{2,10},{6,14},... | collective-permute-start | bytes 294920 | tf_op jit(solution)/shard_map/ppermute | solution.py:363
  5.1 9.0 %collective-permute-start = (bf16[3,4,4096]{2,1,0:T(4,128)(2,1)}, bf16[3,4,4096]{2,1,0:T(4,128)(2,1)S(1)}, u32[]{:S(2)}, u32[]{:S(2)}) collective-permute-start(bf16[3,4,4096]{2,1,0:T(4,128)(2,1)} %bitcast.19), channel_id=1, source_target_pairs={{0,4},{4,8},{8,12},{12,0},{1,5},{5,9},{9,13},{13,1},{2,6},{6,10},{... | collective-permute-start | bytes 294920 | tf_op jit(solution)/shard_map/ppermute | solution.py:363
  6.7 0.7 copy-start.11
  7.4 0.7 copy-start.12
  16.1 13.6 %all-to-all-start = ((bf16[16,48,128]{2,1,0:T(8,128)(2,1)}), bf16[16,48,128]{2,1,0:T(8,128)(2,1)S(1)}, u32[]{:S(2)}, u32[]{:S(2)}) async-start(bf16[16,48,128]{2,1,0:T(8,128)(2,1)} %get-tuple-element.18), calls=%async_computation | async-start | bytes 393216 | tf_op jit(solution)/shard_map/all_to_all | solution.py:366
  20.7 9.0 %copy-start.2 = (bf16[4096,128]{1,0:T(8,128)(2,1)S(1)}, bf16[4096,128]{1,0:T(8,128)(2,1)}, u32[]{:S(2)}) copy-start(bf16[4096,128]{1,0:T(8,128)(2,1)} %key_ref.1) | copy-start | bytes 3145732
  20.7 9.0 %copy-start.9 = (bf16[4,32,128]{2,1,0:T(8,128)(2,1)S(1)}, bf16[4,32,128]{2,1,0:T(8,128)(2,1)}, u32[]{:S(2)}) copy-start(bf16[4,32,128]{2,1,0:T(8,128)(2,1)} %param.23) | copy-start | bytes 98308
  20.7 9.0 %copy-start.10 = (bf16[4,32,128]{2,1,0:T(8,128)(2,1)S(1)}, bf16[4,32,128]{2,1,0:T(8,128)(2,1)}, u32[]{:S(2)}) copy-start(bf16[4,32,128]{2,1,0:T(8,128)(2,1)} %param.24) | copy-start | bytes 98308
  27.2 47.0 %copy-start.1 = (bf16[4,32,4096]{2,1,0:T(8,128)(2,1)S(1)}, bf16[4,32,4096]{2,1,0:T(8,128)(2,1)}, u32[]{:S(2)}) copy-start(bf16[4,32,4096]{2,1,0:T(8,128)(2,1)} %param.26) | copy-start | bytes 3145732
  29.7 1.2 %copy-start.3 = (bf16[4096,128]{1,0:T(8,128)(2,1)S(1)}, bf16[4096,128]{1,0:T(8,128)(2,1)}, u32[]{:S(2)}) copy-start(bf16[4096,128]{1,0:T(8,128)(2,1)} %value_ref.1) | copy-start | bytes 3145732
  31.0 1.0 %copy-start.7 = (bf16[4,32,2048]{2,1,0:T(8,128)(2,1)S(1)}, bf16[4,32,2048]{2,1,0:T(8,128)(2,1)}, u32[]{:S(2)}) copy-start(bf16[4,32,2048]{2,1,0:T(8,128)(2,1)} %param.22) | copy-start | bytes 1572868
  46.2 1.0 %copy-start.4 = (bf16[1,4,512,128]{3,2,1,0:T(8,128)(2,1)S(1)}, bf16[1,4,512,128]{3,2,1,0:T(8,128)(2,1)}, u32[]{:S(2)}) copy-start(bf16[1,4,512,128]{3,2,1,0:T(8,128)(2,1)} %keys_ref.1) | copy-start | bytes 1572868
  47.2 1.0 %copy-start.5 = (bf16[1,4,512,128]{3,2,1,0:T(8,128)(2,1)S(1)}, bf16[1,4,512,128]{3,2,1,0:T(8,128)(2,1)}, u32[]{:S(2)}) copy-start(bf16[1,4,512,128]{3,2,1,0:T(8,128)(2,1)} %values_ref.1) | copy-start | bytes 1572868
  61.7 1.0 %copy-start.6 = (bf16[4,2048,32]{1,2,0:T(8,128)(2,1)S(1)}, bf16[4,2048,32]{1,2,0:T(8,128)(2,1)}, u32[]{:S(2)}) copy-start(bf16[4,2048,32]{1,2,0:T(8,128)(2,1)} %param.25) | copy-start | bytes 1572868
  63.9 10.4 %all-to-all-start.3 = ((bf16[16,16,128]{2,1,0:T(8,128)(2,1)}), bf16[16,16,128]{2,1,0:T(8,128)(2,1)S(1)}, u32[]{:S(2)}, u32[]{:S(2)}) async-start(bf16[16,16,128]{2,1,0:T(8,128)(2,1)} %get-tuple-element.22), calls=%async_computation.3 | async-start | bytes 131072 | tf_op jit(solution)/shard_map/all_to_all | solution.py:366
  74.9 6.5 %collective-permute-start.3 = (bf16[3,4,4096]{2,1,0:T(4,128)(2,1)S(1)}, bf16[3,4,4096]{2,1,0:T(4,128)(2,1)S(1)}, u32[]{:S(2)}, u32[]{:S(2)}) collective-permute-start(bf16[3,4,4096]{2,1,0:T(4,128)(2,1)S(1)} %get-tuple-element.24), channel_id=1, source_target_pairs={{0,12},{4,0},{8,4},{12,8},{1,13},{5,1},{9,5},{13,9},{2,14},{6,2},{... | collective-permute-start | bytes 294920 | tf_op jit(solution)/shard_map/ppermute | solution.py:363
  78.2 9.3 %collective-permute-start.4 = (bf16[3,4,4096]{2,1,0:T(4,128)(2,1)S(1)}, bf16[3,4,4096]{2,1,0:T(4,128)(2,1)S(1)}, u32[]{:S(2)}, u32[]{:S(2)}) collective-permute-start(bf16[3,4,4096]{2,1,0:T(4,128)(2,1)S(1)} %get-tuple-element.25), channel_id=1, source_target_pairs={{0,8},{4,12},{8,0},{12,4},{1,9},{5,13},{9,1},{13,5},{2,10},{6,14},... | collective-permute-start | bytes 294920 | tf_op jit(solution)/shard_map/ppermute | solution.py:363
  78.2 9.3 %collective-permute-start.5 = (bf16[3,4,4096]{2,1,0:T(4,128)(2,1)S(1)}, bf16[3,4,4096]{2,1,0:T(4,128)(2,1)S(1)}, u32[]{:S(2)}, u32[]{:S(2)}) collective-permute-start(bf16[3,4,4096]{2,1,0:T(4,128)(2,1)S(1)} %get-tuple-element.26), channel_id=1, source_target_pairs={{0,4},{4,8},{8,12},{12,0},{1,5},{5,9},{9,13},{13,1},{2,6},{6,10},{... | collective-permute-start | bytes 294920 | tf_op jit(solution)/shard_map/ppermute | solution.py:363

commit v9 on v8

--- a/solution.py
+++ b/solution.py
@@ -92,7 +92,8 @@
 def rank_kernel(sizes, owned, *refs):
     groups, blocks, drafts = sizes
     pieces = refs[:blocks]
-    shrink_ref, slots_ref, rows_ref, rank_ref, wide = refs[blocks:]
+    shrink_ref, slots_ref = refs[blocks : blocks + 2]
+    rows_ref, rank_ref, wide = refs[-3:]
     for block in range(blocks):
         for draft in range(drafts):
             start = (block * drafts + draft) * groups
@@ -103,7 +104,13 @@
     ranks = owned_ranks(
         rows, shrink_ref[...], place, shrink_ref.shape[0] // owned, rank_ref.shape[2]
     )
-    ranks = dot(reorder(sizes, by_draft, as_gathered), ranks).astype(jnp.bfloat16)
+    put = (rank_ref.shape[1], rows.shape[0])
+    draft = parts_of(as_gathered, sizes, iota((rows.shape[0], put[0]), 0))[2]
+    line = slots_ref[:, 2:3] * drafts + draft
+    put = jnp.where(line == iota((rows.shape[0], put[0]), 1), 1.0, 0.0).astype(jnp.bfloat16)
+    ranks = lax.dot_general(
+        put, ranks, (((0,), (0,)), ((), ())), preferred_element_type=jnp.float32
+    ).astype(jnp.bfloat16)
     for target in range(rank_ref.shape[0]):
         rank_ref[target] = ranks
 
@@ -156,13 +163,12 @@
         shape((rows.shape[0], weight.shape[1]), jnp.float32),
         [VMEM, HBM] + [HBM] * len(later),
         [pltpu.VMEM(weight.shape, weight.dtype), pltpu.SemaphoreType.DMA((chunks,))],
-        2 * rows.shape[0] * weight.size,
-        2 * weight.size,
-        40 * MIB,
+        limit=40 * MIB,
     )(rows, weight, *later)
 
 
-def prepare_kernel(sizes, ids_ref, pool_ref, length_ref, _, slots_ref, cosine_ref, sine_ref):
+def prepare_kernel(sizes, owned, ids_ref, pool_ref, length_ref, _, *outs):
+    slots_ref, cosine_ref, sine_ref = outs
     groups, blocks, drafts = sizes
     width = cosine_ref.shape[1]
     lane = iota(cosine_ref.shape, 1)
@@ -175,21 +181,28 @@
     column = iota(slots_ref.shape, 1)
     near = parts_of(as_gathered, sizes, index)
     far = parts_of(by_draft, sizes, index)
-    row_group = jnp.where(column == 0, near[0], far[0])
-    row_block = jnp.where(column == 0, turned(near[1], blocks), far[1])
+    row_group = jnp.where(column == 1, far[0], near[0])
+    row_block = jnp.where(column == 1, far[1], turned(near[1], blocks))
     place = row_block * groups + row_group
     slots = jnp.zeros(slots_ref.shape, jnp.int32)
+    sent, taken = 0, 0
     for row in range(blocks * groups):
-        slots = jnp.where(place == row, pool_ref[ids_ref[row]], slots)
+        slot = pool_ref[ids_ref[row]]
+        owner = over(slot, owned)
+        sends = jnp.where(owner == lax.axis_index("tensor"), 1, 0)
+        takes = jnp.where(owner == group_of(), 1, 0)
+        line = jnp.where(column == 2, sent - 64 * (1 - sends), taken - 64 * (1 - takes))
+        slots = jnp.where(place == row, jnp.where(column < 2, slot, line), slots)
+        sent, taken = sent + sends, taken + takes
     slots_ref[...] = slots
 
 
-def prepare(sizes, ids, pool, lengths, table, later):
+def prepare(sizes, owned, ids, pool, lengths, table, later):
     groups, blocks, drafts = sizes
     smem = pl.BlockSpec(memory_space=pltpu.SMEM)
     table = shape(table, jnp.float32)
     return call(
-        functools.partial(prepare_kernel, sizes),
+        functools.partial(prepare_kernel, sizes, owned),
         [shape((groups * blocks * drafts, 128), jnp.int32), table, table],
         [smem, smem, smem, HBM],
         limit=40 * MIB,
@@ -200,7 +213,7 @@
     sizes, width, total_ref, rows_ref, key_ref, value_ref, slots_ref, ranks_ref, *refs
 ):
     groups, blocks, drafts = sizes
-    *grows, out_ref, held = refs
+    grows, (out_ref, held) = refs[:3], refs[-2:]
     group = group_of()
     requests = groups * blocks
     lines = out_ref.shape[1]
@@ -209,7 +222,10 @@
     ranks = ranks_ref[group * groups].astype(jnp.float32)
     for other in range(1, groups):
         ranks = ranks + ranks_ref[group * groups + other].astype(jnp.float32)
-    ranks = dot(reorder(sizes, as_gathered, by_draft), ranks.astype(jnp.bfloat16))
+    get = (rows_ref.shape[0], ranks.shape[0])
+    draft = parts_of(as_gathered, sizes, iota(get, 0))[2]
+    get = slots_ref[:, 3:4] * drafts + draft == iota(get, 1)
+    ranks = dot(jnp.where(get, 1.0, 0.0).astype(jnp.bfloat16), ranks.astype(jnp.bfloat16))
     place = slots_ref[:, 0:1] - group * owned
     wide = spread_ranks(ranks.astype(jnp.bfloat16), place, width, owned, len(grows))
     arranged = reorder(sizes, by_draft, as_gathered)
@@ -371,12 +387,13 @@
     lines = (w_query.shape[1] // head_size + 2) * drafts
     lines = -(-lines // 8) * 8
     slots, cosine, sine = prepare(
-        sizes, adapter_ids, adapter_slots, cache_lengths, (lines, head_size), w_out
-    )
+        sizes, owned, adapter_ids, adapter_slots, cache_lengths, (lines, head_size), w_out
+    )
+    packed = -(-2 * blocks * drafts // 16) * 16
     shrink_in = jnp.transpose(shrink_qkv, (0, 2, 1)).reshape(-1, features)
     rows, rank_part = call(
         functools.partial(rank_kernel, sizes, owned),
-        [shape((count, features)), shape((blocks * groups, count, lanes))],
+        [shape((count, features)), shape((blocks * groups, packed, lanes))],
         [VMEM] * (blocks + 2),
         [pltpu.VMEM((count, features), jnp.float32)],
         2 * count * shrink_qkv.size,
@@ -390,10 +407,9 @@
     sent = call(
         functools.partial(grow_kernel, sizes, width),
         shape((blocks * groups, lines, head_size)),
-        [VMEM] * 9,
+        [VMEM] * 9 + [HBM] * 2,
         [pltpu.VMEM((blocks * groups * lines, head_size), jnp.float32)],
-        2 * count * owned * width * cols,
-        8 * count * cols + 2 * owned * width * cols,
+        limit=40 * MIB,
     )(
         total,
         rows,
@@ -402,6 +418,7 @@
         slots,
         ranks,
         *[grow.reshape(owned * width, -1) for grow in (grow_query, grow_key, grow_value)],
+        *[w_out] * 2,
     )
     mixed = call(
         functools.partial(attend_kernel, sizes),

time: 88.8 us -> 85.8 us (0.966)
  local copies, waits for them, and re-layouts: 6.72 us -> 3.62 us
  blocking collectives: 24.6 us -> 25.8 us
  waiting for transfers between devices: 16.4 us -> 15.2 us
    unnamed x26 -> x40, local copies, waits for them, and re-layouts: 6.72 us -> 3.62 us
    all_to_all x2, blocking collectives: 24.6 us -> 25.8 us  [exchange(): return lax.all_to_all(value, EVERY, split_axis=0, concat_axis=0, tiled=True)]
    all_to_all x2, waiting for transfers between devices: 2.91 us -> 1.79 us  [exchange(): return lax.all_to_all(value, EVERY, split_axis=0, concat_axis=0, tiled=True)]
  transfers between devices with their start and end apart: 8 -> 8, of which waited for: 5 -> 5; matrix products, arithmetic and copies ran while one was open for 0% -> 0% of each run, Pallas kernels for 15% -> 16%
where the time goes in v9:
time: 85.8 us; the launch traced here: 85.3 us
  blocking collectives  25.8 us (30%)
  Pallas kernels  20.5 us (24%)
  starting transfers between devices  18.6 us (22%)
  waiting for transfers between devices  15.2 us (18%)
  local copies, waits for them, and re-layouts  3.62 us (4%)
    all_to_all x2, blocking collectives, exchange(): return lax.all_to_all(value, EVERY, split_axis=0, concat_axis=0, tiled=True)  25.8 us
    ppermute x6, waiting for transfers between devices, over_tensor(): return lax.ppermute(value, 'tensor', route)  13.4 us
    pallas_call x2, Pallas kernels, stream(): call(functools.partial(stream_kernel, chunks), shape((rows.shape[0], weig...  13 us
    ppermute x6, starting transfers between devices, over_tensor(): return lax.ppermute(value, 'tensor', route)  10.5 us
    all_to_all x2, starting transfers between devices, exchange(): return lax.all_to_all(value, EVERY, split_axis=0, concat_axis=0, tiled=True)  8.09 us
    unnamed x40, local copies, waits for them, and re-layouts  3.62 us
    pallas_call x1, Pallas kernels, by_kernels(): call(functools.partial(rank_kernel, sizes, owned), [shape((count, feature...  2.05 us
    all_to_all x2, waiting for transfers between devices, exchange(): return lax.all_to_all(value, EVERY, split_axis=0, concat_axis=0, tiled=True)  1.79 us
  transfers between devices with their start and end apart: 8, of which 5 were waited for; matrix products, arithmetic and copies ran while one was open for 0% of the time, Pallas kernels for 16%

profile of v9, /device:TPU:0, one launch (start us, length us, event | category | flops | bytes accessed | tf_op | source)
XLA Modules:
  0.0 85.3 jit_solution(561026588687336385)
XLA Ops:
  0.0 5.0 %collective-permute-start.2 = (bf16[3,4,4096]{2,1,0:T(4,128)(2,1)}, bf16[3,4,4096]{2,1,0:T(4,128)(2,1)S(1)}, u32[]{:S(2)}, u32[]{:S(2)}) collective-permute-start(bf16[3,4,4096]{2,1,0:T(4,128)(2,1)} %bitcast.17), channel_id=1, source_target_pairs={{0,12},{4,0},{8,4},{12,8},{1,13},{5,1},{9,5},{13,9},{2,14},{6,2},{... | collective-permute-start | bytes 294920 | tf_op jit(solution)/shard_map/ppermute | solution.py:379
  5.1 0.0 collective-permute-start.1
  5.1 1.0 %collective-permute-start = (bf16[3,4,4096]{2,1,0:T(4,128)(2,1)}, bf16[3,4,4096]{2,1,0:T(4,128)(2,1)S(1)}, u32[]{:S(2)}, u32[]{:S(2)}) collective-permute-start(bf16[3,4,4096]{2,1,0:T(4,128)(2,1)} %bitcast.19), channel_id=1, source_target_pairs={{0,4},{4,8},{8,12},{12,0},{1,5},{5,9},{9,13},{13,1},{2,6},{6,10},{... | collective-permute-start | bytes 294920 | tf_op jit(solution)/shard_map/ppermute | solution.py:379
  6.7 0.0 copy-start.18
  6.7 0.6 copy-done.18
  7.4 0.7 copy-done.19
  8.0 0.7 shard_map.154
  8.8 0.0 copy-start.8
  8.8 0.0 copy-start.14
  8.8 0.0 copy-start.16
  8.8 0.0 collective-permute-done.2.refs_3_
  8.8 5.2 %collective-permute-done.1.refs_2_ = bf16[3,4,4096]{2,1,0:T(4,128)(2,1)S(1)} collective-permute-done((bf16[3,4,4096]{2,1,0:T(4,128)(2,1)}, bf16[3,4,4096]{2,1,0:T(4,128)(2,1)S(1)}, u32[]{:S(2)}, u32[]{:S(2)}) %collective-permute-start.1) | collective-permute-done | bytes 98336 | tf_op jit(solution)/shard_map/ppermute | solution.py:379
  14.0 0.0 collective-permute-done.refs_1_
  14.0 0.0 copy-done.11
  14.0 0.0 copy-done
  14.0 2.1 %shard_map.155 = (bf16[48,4096]{1,0:T(8,128)(2,1)S(1)}, bf16[16,32,128]{2,1,0:T(8,128)(2,1)}) custom-call(bf16[3,4,4096]{2,1,0:T(4,128)(2,1)S(1)} %bitcast.20, bf16[3,4,4096]{2,1,0:T(4,128)(2,1)S(1)} %collective-permute-done.refs_1_, bf16[3,4,4096]{2,1,0:T(4,128)(2,1)S(1)} %collective-permute-done.1.refs_2_, ...), custom_call_target="tpu_custom_call" | custom-call | flops 150994944 | bytes 3932160 | tf_op jit(solution)/shard_map/pallas_call | solution.py:394
  16.1 4.6 %all-to-all-start = ((bf16[16,32,128]{2,1,0:T(8,128)(2,1)}), bf16[16,32,128]{2,1,0:T(8,128)(2,1)S(1)}, u32[]{:S(2)}, u32[]{:S(2)}) async-start(bf16[16,32,128]{2,1,0:T(8,128)(2,1)} %get-tuple-element.18), calls=%async_computation | async-start | bytes 262144 | tf_op jit(solution)/shard_map/all_to_all | solution.py:382
  20.7 0.0 copy-start.1
  20.7 0.0 copy-start.2
  20.7 0.0 copy-start.4
  20.7 6.5 %shard_map.156.total_ref = f32[48,2048]{1,0:T(8,128)S(1)} custom-call(bf16[48,4096]{1,0:T(8,128)(2,1)S(1)} %get-tuple-element.17.rows_ref, bf16[4096,2048]{1,0:T(8,128)(2,1)} %weight_ref.2, bf16[2048,4096]{1,0:T(8,128)(2,1)} %weight_ref.3, bf16[2048,4096]{1,0:T(8,128)(2,1)} %weight_ref.3, bf16[2048,4096]{1,0:T(8,128)(2,1)} %weight_ref.3), custom_call_target="tpu_custom_call" | custom-call | tf_op jit(solution)/shard_map/pallas_call | solution.py:161
  27.3 1.3 %all-to-all-done.ranks_ref = bf16[16,32,128]{2,1,0:T(8,128)(2,1)S(1)} async-done(((bf16[16,32,128]{2,1,0:T(8,128)(2,1)}), bf16[16,32,128]{2,1,0:T(8,128)(2,1)S(1)}, u32[]{:S(2)}, u32[]{:S(2)}) %all-to-all-start) | async-done | bytes 131104 | tf_op jit(solution)/shard_map/all_to_all | solution.py:382
  28.6 0.0 copy-done.1
  28.6 0.7 copy-done.9
  29.4 0.8 copy-done.12
  30.1 0.8 copy-done.13
  30.9 0.0 copy-start.7
  30.9 1.3 %shard_map.157 = bf16[16,56,128]{2,1,0:T(8,128)(2,1)S(1)} custom-call(f32[48,2048]{1,0:T(8,128)S(1)} %shard_map.156.total_ref, bf16[48,4096]{1,0:T(8,128)(2,1)S(1)} %get-tuple-element.17.rows_ref, bf16[4096,128]{1,0:T(8,128)(2,1)S(1)} %copy-done.1, bf16[4096,128]{1,0:T(8,128)(2,1)S(1)} %copy-done.2, s32[48,128]{1,0:T(8,128)S(1)} %copy-done.9, ...), custom_call_target="tpu_custom_call" | custom-call | tf_op jit(solution)/shard_map/pallas_call | solution.py:407
  32.2 0.0 copy-start.3
  32.2 0.0 copy-start.10
  32.2 14.1 %all_to_all.20.arrived_ref = bf16[16,56,128]{2,1,0:T(8,128)(2,1)S(1)} all-to-all(bf16[16,56,128]{2,1,0:T(8,128)(2,1)S(1)} %shard_map.157), channel_id=1, replica_groups=mesh['parts'=2,'tensor'=4,'dp'=2,'pipe'=2] {'tensor','dp','pipe'}, dimensions={0} | all-to-all | bytes 458752 | tf_op jit(solution)/shard_map/all_to_all | solution.py:382
  46.3 0.0 copy-done.15
  46.3 0.0 copy-done.17
  46.3 1.7 %shard_map.158 = bf16[16,48,128]{2,1,0:T(8,128)(2,1)S(1)} custom-call(bf16[16,56,128]{2,1,0:T(8,128)(2,1)S(1)} %all_to_all.20.arrived_ref, bf16[1,4,512,128]{3,2,1,0:T(8,128)(2,1)S(1)} %copy-done.5, bf16[1,4,512,128]{3,2,1,0:T(8,128)(2,1)S(1)} %copy-done.6, s32[1]{0:T(128)S(6)} %copy.17.length_ref, f32[56,128]{1,0:T(8,128)S(1)} %copy-done.15, ...), custom_call_target="tpu_custom_call" | custom-call | tf_op jit(solution)/shard_map/pallas_call | solution.py:423
  48.1 11.6 %all_to_all.21.got_ref = bf16[16,48,128]{2,1,0:T(8,128)(2,1)S(1)} all-to-all(bf16[16,48,128]{2,1,0:T(8,128)(2,1)S(1)} %shard_map.158), channel_id=1, replica_groups=mesh['parts'=2,'tensor'=4,'dp'=2,'pipe'=2] {'tensor','dp','pipe'}, dimensions={0} | all-to-all | bytes 393216 | tf_op jit(solution)/shard_map/all_to_all | solution.py:382
  59.7 0.0 copy-done.7
  59.7 1.2 %shard_map.159 = (bf16[48,2048]{1,0:T(8,128)(2,1)S(1)}, bf16[16,16,128]{2,1,0:T(8,128)(2,1)}) custom-call(bf16[16,48,128]{2,1,0:T(8,128)(2,1)S(1)} %all_to_all.21.got_ref, bf16[128,2048]{1,0:T(8,128)(2,1)S(1)} %bitcast.16, s32[48,128]{1,0:T(8,128)S(1)} %copy-done.9), custom_call_target="tpu_custom_call" | custom-call | tf_op jit(solution)/shard_map/pallas_call | solution.py:431
  60.9 3.5 %all-to-all-start.3 = ((bf16[16,16,128]{2,1,0:T(8,128)(2,1)}), bf16[16,16,128]{2,1,0:T(8,128)(2,1)S(1)}, u32[]{:S(2)}, u32[]{:S(2)}) async-start(bf16[16,16,128]{2,1,0:T(8,128)(2,1)} %get-tuple-element.22), calls=%async_computation.3 | async-start | bytes 131072 | tf_op jit(solution)/shard_map/all_to_all | solution.py:382
  64.4 6.4 %shard_map.160.total_ref = f32[48,4096]{1,0:T(8,128)S(1)} custom-call(bf16[48,2048]{1,0:T(8,128)(2,1)S(1)} %get-tuple-element.21.rows_ref, bf16[2048,4096]{1,0:T(8,128)(2,1)} %weight_ref.3), custom_call_target="tpu_custom_call" | custom-call | tf_op jit(solution)/shard_map/pallas_call | solution.py:161
  70.9 0.4 all-to-all-done.3.ranks_ref
  71.3 0.6 shard_map.161
  71.9 3.3 %collective-permute-start.3 = (bf16[3,4,4096]{2,1,0:T(4,128)(2,1)S(1)}, bf16[3,4,4096]{2,1,0:T(4,128)(2,1)S(1)}, u32[]{:S(2)}, u32[]{:S(2)}) collective-permute-start(bf16[3,4,4096]{2,1,0:T(4,128)(2,1)S(1)} %get-tuple-element.24), channel_id=1, source_target_pairs={{0,12},{4,0},{8,4},{12,8},{1,13},{5,1},{9,5},{13,9},{2,14},{6,2},{... | collective-permute-start | bytes 294920 | tf_op jit(solution)/shard_map/ppermute | solution.py:379
  75.3 0.0 collective-permute-start.4
  75.3 1.1 %collective-permute-start.5 = (bf16[3,4,4096]{2,1,0:T(4,128)(2,1)S(1)}, bf16[3,4,4096]{2,1,0:T(4,128)(2,1)S(1)}, u32[]{:S(2)}, u32[]{:S(2)}) collective-permute-start(bf16[3,4,4096]{2,1,0:T(4,128)(2,1)S(1)} %get-tuple-element.26), channel_id=1, source_target_pairs={{0,4},{4,8},{8,12},{12,0},{1,5},{5,9},{9,13},{13,1},{2,6},{6,10},{... | collective-permute-start | bytes 294920 | tf_op jit(solution)/shard_map/ppermute | solution.py:379
  76.4 2.1 %collective-permute-done.3 = bf16[3,4,4096]{2,1,0:T(4,128)(2,1)S(1)} collective-permute-done((bf16[3,4,4096]{2,1,0:T(4,128)(2,1)S(1)}, bf16[3,4,4096]{2,1,0:T(4,128)(2,1)S(1)}, u32[]{:S(2)}, u32[]{:S(2)}) %collective-permute-start.3) | collective-permute-done | bytes 98336 | tf_op jit(solution)/shard_map/ppermute | solution.py:379
  78.5 6.1 %collective-permute-done.4 = bf16[3,4,4096]{2,1,0:T(4,128)(2,1)S(1)} collective-permute-done((bf16[3,4,4096]{2,1,0:T(4,128)(2,1)S(1)}, bf16[3,4,4096]{2,1,0:T(4,128)(2,1)S(1)}, u32[]{:S(2)}, u32[]{:S(2)}) %collective-permute-start.4) | collective-permute-done | bytes 98336 | tf_op jit(solution)/shard_map/ppermute | solution.py:379
  84.5 0.0 collective-permute-done.5
  84.5 0.7 fusion
  (19 shorter events, 0.0 us)
Async XLA Ops:
  0.0 14.0 %copy-start.11 = (bf16[4,3,4096]{2,0,1:T(4,128)(2,1)S(1)}, bf16[4,3,4096]{2,0,1:T(4,128)(2,1)}, u32[]{:S(2)}) copy-start(bf16[4,3,4096]{2,0,1:T(4,128)(2,1)} %param.16) | copy-start | bytes 294916
  0.0 14.0 %copy-start = (bf16[4,4096,96]{1,2,0:T(8,128)(2,1)S(1)}, bf16[4,4096,96]{1,2,0:T(8,128)(2,1)}, u32[]{:S(2)}) copy-start(bf16[4,4096,96]{1,2,0:T(8,128)(2,1)} %param.21) | copy-start | bytes 9437188
  0.0 8.8 %collective-permute-start.2 = (bf16[3,4,4096]{2,1,0:T(4,128)(2,1)}, bf16[3,4,4096]{2,1,0:T(4,128)(2,1)S(1)}, u32[]{:S(2)}, u32[]{:S(2)}) collective-permute-start(bf16[3,4,4096]{2,1,0:T(4,128)(2,1)} %bitcast.17), channel_id=1, source_target_pairs={{0,12},{4,0},{8,4},{12,8},{1,13},{5,1},{9,5},{13,9},{2,14},{6,2},{... | collective-permute-start | bytes 294920 | tf_op jit(solution)/shard_map/ppermute | solution.py:379
  5.1 9.0 %collective-permute-start.1 = (bf16[3,4,4096]{2,1,0:T(4,128)(2,1)}, bf16[3,4,4096]{2,1,0:T(4,128)(2,1)S(1)}, u32[]{:S(2)}, u32[]{:S(2)}) collective-permute-start(bf16[3,4,4096]{2,1,0:T(4,128)(2,1)} %bitcast.18), channel_id=1, source_target_pairs={{0,8},{4,12},{8,0},{12,4},{1,9},{5,13},{9,1},{13,5},{2,10},{6,14},... | collective-permute-start | bytes 294920 | tf_op jit(solution)/shard_map/ppermute | solution.py:379
  5.1 9.0 %collective-permute-start = (bf16[3,4,4096]{2,1,0:T(4,128)(2,1)}, bf16[3,4,4096]{2,1,0:T(4,128)(2,1)S(1)}, u32[]{:S(2)}, u32[]{:S(2)}) collective-permute-start(bf16[3,4,4096]{2,1,0:T(4,128)(2,1)} %bitcast.19), channel_id=1, source_target_pairs={{0,4},{4,8},{8,12},{12,0},{1,5},{5,9},{9,13},{13,1},{2,6},{6,10},{... | collective-permute-start | bytes 294920 | tf_op jit(solution)/shard_map/ppermute | solution.py:379
  6.7 0.7 copy-start.18
  7.4 0.7 copy-start.19
  8.8 7.3 %copy-start.8 = (s32[48,128]{1,0:T(8,128)}, s32[48,128]{1,0:T(8,128)S(1)}, u32[]{:S(2)}) copy-start(s32[48,128]{1,0:T(8,128)S(1)} %get-tuple-element.16.refs_5_.slots_ref) | copy-start | bytes 73732
  8.8 7.3 %copy-start.14 = (f32[56,128]{1,0:T(8,128)}, f32[56,128]{1,0:T(8,128)S(1)}, u32[]{:S(2)}) copy-start(f32[56,128]{1,0:T(8,128)S(1)} %get-tuple-element.19.cosine_ref) | copy-start | bytes 86020
  8.8 7.3 %copy-start.16 = (f32[56,128]{1,0:T(8,128)}, f32[56,128]{1,0:T(8,128)S(1)}, u32[]{:S(2)}) copy-start(f32[56,128]{1,0:T(8,128)S(1)} %get-tuple-element.20.sine_ref) | copy-start | bytes 86020
  16.1 12.5 %all-to-all-start = ((bf16[16,32,128]{2,1,0:T(8,128)(2,1)}), bf16[16,32,128]{2,1,0:T(8,128)(2,1)S(1)}, u32[]{:S(2)}, u32[]{:S(2)}) async-start(bf16[16,32,128]{2,1,0:T(8,128)(2,1)} %get-tuple-element.18), calls=%async_computation | async-start | bytes 262144 | tf_op jit(solution)/shard_map/all_to_all | solution.py:382
  20.7 7.9 %copy-start.1 = (bf16[4096,128]{1,0:T(8,128)(2,1)S(1)}, bf16[4096,128]{1,0:T(8,128)(2,1)}, u32[]{:S(2)}) copy-start(bf16[4096,128]{1,0:T(8,128)(2,1)} %key_ref.1) | copy-start | bytes 3145732
  20.7 7.9 %copy-start.2 = (bf16[4096,128]{1,0:T(8,128)(2,1)S(1)}, bf16[4096,128]{1,0:T(8,128)(2,1)}, u32[]{:S(2)}) copy-start(bf16[4096,128]{1,0:T(8,128)(2,1)} %value_ref.1) | copy-start | bytes 3145732
  20.7 7.9 %copy-start.4 = (bf16[4,32,2048]{2,1,0:T(8,128)(2,1)S(1)}, bf16[4,32,2048]{2,1,0:T(8,128)(2,1)}, u32[]{:S(2)}) copy-start(bf16[4,32,2048]{2,1,0:T(8,128)(2,1)} %param.22) | copy-start | bytes 1572868
  28.6 0.7 copy-start.9
  29.4 0.8 copy-start.12
  30.1 0.8 copy-start.13
  30.9 15.4 %copy-start.5 = (bf16[1,4,512,128]{3,2,1,0:T(8,128)(2,1)S(1)}, bf16[1,4,512,128]{3,2,1,0:T(8,128)(2,1)}, u32[]{:S(2)}) copy-start(bf16[1,4,512,128]{3,2,1,0:T(8,128)(2,1)} %keys_ref.1) | copy-start | bytes 1572868
  30.9 15.4 %copy-start.6 = (bf16[1,4,512,128]{3,2,1,0:T(8,128)(2,1)S(1)}, bf16[1,4,512,128]{3,2,1,0:T(8,128)(2,1)}, u32[]{:S(2)}) copy-start(bf16[1,4,512,128]{3,2,1,0:T(8,128)(2,1)} %values_ref.1) | copy-start | bytes 1572868
  30.9 15.4 %copy-start.15 = (f32[56,128]{1,0:T(8,128)S(1)}, f32[56,128]{1,0:T(8,128)}, u32[]{:S(2)}) copy-start(f32[56,128]{1,0:T(8,128)} %copy-done.14) | copy-start | bytes 86020
  30.9 15.4 %copy-start.17 = (f32[56,128]{1,0:T(8,128)S(1)}, f32[56,128]{1,0:T(8,128)}, u32[]{:S(2)}) copy-start(f32[56,128]{1,0:T(8,128)} %copy-done.16) | copy-start | bytes 86020
  30.9 28.8 %copy-start.7 = (bf16[4,2048,32]{1,2,0:T(8,128)(2,1)S(1)}, bf16[4,2048,32]{1,2,0:T(8,128)(2,1)}, u32[]{:S(2)}) copy-start(bf16[4,2048,32]{1,2,0:T(8,128)(2,1)} %param.25) | copy-start | bytes 1572868
  32.2 39.1 %copy-start.3 = (bf16[4,32,4096]{2,1,0:T(8,128)(2,1)S(1)}, bf16[4,32,4096]{2,1,0:T(8,128)(2,1)}, u32[]{:S(2)}) copy-start(bf16[4,32,4096]{2,1,0:T(8,128)(2,1)} %param.26) | copy-start | bytes 3145732
  32.2 39.1 %copy-start.10 = (s32[48,128]{1,0:T(8,128)S(1)}, s32[48,128]{1,0:T(8,128)}, u32[]{:S(2)}) copy-start(s32[48,128]{1,0:T(8,128)} %copy-done.8) | copy-start | bytes 73732
  60.9 10.4 %all-to-all-start.3 = ((bf16[16,16,128]{2,1,0:T(8,128)(2,1)}), bf16[16,16,128]{2,1,0:T(8,128)(2,1)S(1)}, u32[]{:S(2)}, u32[]{:S(2)}) async-start(bf16[16,16,128]{2,1,0:T(8,128)(2,1)} %get-tuple-element.22), calls=%async_computation.3 | async-start | bytes 131072 | tf_op jit(solution)/shard_map/all_to_all | solution.py:382
  71.9 6.5 %collective-permute-start.3 = (bf16[3,4,4096]{2,1,0:T(4,128)(2,1)S(1)}, bf16[3,4,4096]{2,1,0:T(4,128)(2,1)S(1)}, u32[]{:S(2)}, u32[]{:S(2)}) collective-permute-start(bf16[3,4,4096]{2,1,0:T(4,128)(2,1)S(1)} %get-tuple-element.24), channel_id=1, source_target_pairs={{0,12},{4,0},{8,4},{12,8},{1,13},{5,1},{9,5},{13,9},{2,14},{6,2},{... | collective-permute-start | bytes 294920 | tf_op jit(solution)/shard_map/ppermute | solution.py:379
  75.3 9.3 %collective-permute-start.4 = (bf16[3,4,4096]{2,1,0:T(4,128)(2,1)S(1)}, bf16[3,4,4096]{2,1,0:T(4,128)(2,1)S(1)}, u32[]{:S(2)}, u32[]{:S(2)}) collective-permute-start(bf16[3,4,4096]{2,1,0:T(4,128)(2,1)S(1)} %get-tuple-element.25), channel_id=1, source_target_pairs={{0,8},{4,12},{8,0},{12,4},{1,9},{5,13},{9,1},{13,5},{2,10},{6,14},... | collective-permute-start | bytes 294920 | tf_op jit(solution)/shard_map/ppermute | solution.py:379
  75.3 9.3 %collective-permute-start.5 = (bf16[3,4,4096]{2,1,0:T(4,128)(2,1)S(1)}, bf16[3,4,4096]{2,1,0:T(4,128)(2,1)S(1)}, u32[]{:S(2)}, u32[]{:S(2)}) collective-permute-start(bf16[3,4,4096]{2,1,0:T(4,128)(2,1)S(1)} %get-tuple-element.26), channel_id=1, source_target_pairs={{0,4},{4,8},{8,12},{12,0},{1,5},{5,9},{9,13},{13,1},{2,6},{6,10},{... | collective-permute-start | bytes 294920 | tf_op jit(solution)/shard_map/ppermute | solution.py:379

commit v10 on v9

--- a/solution.py
+++ b/solution.py
@@ -135,9 +135,10 @@
     return jnp.where(slot == place, wide, 0.0).astype(jnp.bfloat16)
 
 
-def stream_kernel(chunks, rows_ref, weight_ref, *refs):
+def stream_kernel(chunks, small, rows_ref, weight_ref, *refs):
     total_ref, buffer, sems = refs[-3:]
     depth = rows_ref.shape[1] // chunks
+    width = weight_ref.shape[1]
 
     def copy(chunk):
         part = pl.ds(chunk * depth, depth)
@@ -145,6 +146,10 @@
 
     for chunk in range(chunks):
         copy(chunk).start()
+    start = width
+    for other in refs[:small]:
+        total_ref[:, start : start + other.shape[1]] = dot(rows_ref[...], other[...])
+        start += other.shape[1]
     for chunk in range(chunks):
         copy(chunk).wait()
         product = dot(
@@ -152,19 +157,20 @@
             buffer[chunk * depth : (chunk + 1) * depth, :],
         )
         if chunk:
-            total_ref[...] += product
+            total_ref[:, 0:width] += product
         else:
-            total_ref[...] = product
-
-
-def stream(rows, weight, chunks, later=()):
+            total_ref[:, 0:width] = product
+
+
+def stream(rows, weight, chunks, small=(), later=()):
+    width = weight.shape[1] + sum(other.shape[1] for other in small)
     return call(
-        functools.partial(stream_kernel, chunks),
-        shape((rows.shape[0], weight.shape[1]), jnp.float32),
-        [VMEM, HBM] + [HBM] * len(later),
+        functools.partial(stream_kernel, chunks, len(small)),
+        shape((rows.shape[0], width), jnp.float32),
+        [VMEM, HBM] + [VMEM] * len(small) + [HBM] * len(later),
         [pltpu.VMEM(weight.shape, weight.dtype), pltpu.SemaphoreType.DMA((chunks,))],
         limit=40 * MIB,
-    )(rows, weight, *later)
+    )(rows, weight, *small, *later)
 
 
 def prepare_kernel(sizes, owned, ids_ref, pool_ref, length_ref, _, *outs):
@@ -209,9 +215,7 @@
     )(ids, pool, lengths, later)
 
 
-def grow_kernel(
-    sizes, width, total_ref, rows_ref, key_ref, value_ref, slots_ref, ranks_ref, *refs
-):
+def grow_kernel(sizes, width, total_ref, slots_ref, ranks_ref, *refs):
     groups, blocks, drafts = sizes
     grows, (out_ref, held) = refs[:3], refs[-2:]
     group = group_of()
@@ -222,21 +226,20 @@
     ranks = ranks_ref[group * groups].astype(jnp.float32)
     for other in range(1, groups):
         ranks = ranks + ranks_ref[group * groups + other].astype(jnp.float32)
-    get = (rows_ref.shape[0], ranks.shape[0])
+    get = (total_ref.shape[0], ranks.shape[0])
     draft = parts_of(as_gathered, sizes, iota(get, 0))[2]
     get = slots_ref[:, 3:4] * drafts + draft == iota(get, 1)
     ranks = dot(jnp.where(get, 1.0, 0.0).astype(jnp.bfloat16), ranks.astype(jnp.bfloat16))
     place = slots_ref[:, 0:1] - group * owned
     wide = spread_ranks(ranks.astype(jnp.bfloat16), place, width, owned, len(grows))
     arranged = reorder(sizes, by_draft, as_gathered)
-    start = 0
+    start, column = 0, 0
     for index, grow in enumerate(grows):
         deep, cols = grow.shape
-        if index == 0:
-            full = total_ref[...]
-        else:
-            full = dot(rows_ref[...], (key_ref, value_ref)[index - 1][...])
-        full = full + dot(wide[:, index * deep : (index + 1) * deep], grow[...])
+        full = total_ref[:, column : column + cols] + dot(
+            wide[:, index * deep : (index + 1) * deep], grow[...]
+        )
+        column += cols
         full = dot(arranged, full.astype(jnp.bfloat16))
         for head in range(cols // 128):
             for draft in range(drafts):
@@ -400,21 +403,18 @@
         2 * shrink_qkv.size + 4 * count * features,
     )(*pieces, shrink_in, slots)
     ranks = exchange(rank_part)
-    total = stream(rows, w_query, 8, [w_out] * 3)
-    cols = total.shape[1] + w_key.shape[1] + w_value.shape[1]
-    head_cols = total.shape[1]
+    total = stream(rows, w_query, 8, [w_key, w_value], [w_out] * 3)
+    cols = total.shape[1]
+    head_cols = w_query.shape[1]
     query_lines = head_cols // head_size * drafts
     sent = call(
         functools.partial(grow_kernel, sizes, width),
         shape((blocks * groups, lines, head_size)),
-        [VMEM] * 9 + [HBM] * 2,
+        [VMEM] * 6 + [HBM] * 2,
         [pltpu.VMEM((blocks * groups * lines, head_size), jnp.float32)],
         limit=40 * MIB,
     )(
         total,
-        rows,
-        w_key,
-        w_value,
         slots,
         ranks,
         *[grow.reshape(owned * width, -1) for grow in (grow_query, grow_key, grow_value)],

time: 85.8 us -> 84.9 us (0.990)
  blocking collectives: 25.8 us -> 26.7 us
  waiting for transfers between devices: 15.2 us -> 14.3 us
    all_to_all x2, blocking collectives: 25.8 us -> 26.7 us  [exchange(): return lax.all_to_all(value, EVERY, split_axis=0, concat_axis=0, tiled=True)]
    all_to_all x2, waiting for transfers between devices: 1.79 us -> 0.84 us  [exchange(): return lax.all_to_all(value, EVERY, split_axis=0, concat_axis=0, tiled=True)]
    unnamed x40 -> x30, local copies, waits for them, and re-layouts: 3.62 us -> 3.1 us
where the time goes in v10:
time: 84.9 us; the launch traced here: 84.5 us
  blocking collectives  26.7 us (31%)
  Pallas kernels  20.2 us (24%)
  starting transfers between devices  18.6 us (22%)
  waiting for transfers between devices  14.3 us (17%)
  local copies, waits for them, and re-layouts  3.1 us (4%)
    all_to_all x2, blocking collectives, exchange(): return lax.all_to_all(value, EVERY, split_axis=0, concat_axis=0, tiled=True)  26.7 us
    ppermute x6, waiting for transfers between devices, over_tensor(): return lax.ppermute(value, 'tensor', route)  13.4 us
    pallas_call x2, Pallas kernels, stream(): call(functools.partial(stream_kernel, chunks, len(small)), shape((rows.sh...  12.9 us
    ppermute x6, starting transfers between devices, over_tensor(): return lax.ppermute(value, 'tensor', route)  10.5 us
    all_to_all x2, starting transfers between devices, exchange(): return lax.all_to_all(value, EVERY, split_axis=0, concat_axis=0, tiled=True)  8.08 us
    unnamed x30, local copies, waits for them, and re-layouts  3.1 us
    pallas_call x1, Pallas kernels, by_kernels(): call(functools.partial(rank_kernel, sizes, owned), [shape((count, feature...  2.06 us
    pallas_call x1, Pallas kernels, by_kernels(): call(functools.partial(attend_kernel, sizes), shape((blocks * groups, que...  1.75 us
  transfers between devices with their start and end apart: 8, of which 5 were waited for; matrix products, arithmetic and copies ran while one was open for 0% of the time, Pallas kernels for 16%

profile of v10, /device:TPU:0, one launch (start us, length us, event | category | flops | bytes accessed | tf_op | source)
XLA Modules:
  0.0 84.5 jit_solution(12016232611847788079)
XLA Ops:
  0.0 5.1 %collective-permute-start.2 = (bf16[3,4,4096]{2,1,0:T(4,128)(2,1)}, bf16[3,4,4096]{2,1,0:T(4,128)(2,1)S(1)}, u32[]{:S(2)}, u32[]{:S(2)}) collective-permute-start(bf16[3,4,4096]{2,1,0:T(4,128)(2,1)} %bitcast.17), channel_id=1, source_target_pairs={{0,12},{4,0},{8,4},{12,8},{1,13},{5,1},{9,5},{13,9},{2,14},{6,2},{... | collective-permute-start | bytes 294920 | tf_op jit(solution)/shard_map/ppermute | solution.py:382
  5.1 0.0 collective-permute-start.1
  5.1 1.0 %collective-permute-start = (bf16[3,4,4096]{2,1,0:T(4,128)(2,1)}, bf16[3,4,4096]{2,1,0:T(4,128)(2,1)S(1)}, u32[]{:S(2)}, u32[]{:S(2)}) collective-permute-start(bf16[3,4,4096]{2,1,0:T(4,128)(2,1)} %bitcast.19), channel_id=1, source_target_pairs={{0,4},{4,8},{8,12},{12,0},{1,5},{5,9},{9,13},{13,1},{2,6},{6,10},{... | collective-permute-start | bytes 294920 | tf_op jit(solution)/shard_map/ppermute | solution.py:382
  6.8 0.0 copy-start.13
  6.8 0.6 copy-done.13
  7.4 0.7 copy-done.14
  8.1 0.7 shard_map.154
  8.8 0.0 collective-permute-done.2.refs_3_
  8.8 5.2 %collective-permute-done.1.refs_2_ = bf16[3,4,4096]{2,1,0:T(4,128)(2,1)S(1)} collective-permute-done((bf16[3,4,4096]{2,1,0:T(4,128)(2,1)}, bf16[3,4,4096]{2,1,0:T(4,128)(2,1)S(1)}, u32[]{:S(2)}, u32[]{:S(2)}) %collective-permute-start.1) | collective-permute-done | bytes 98336 | tf_op jit(solution)/shard_map/ppermute | solution.py:382
  14.1 0.0 collective-permute-done.refs_1_
  14.1 0.0 copy-done.10
  14.1 0.0 copy-done
  14.1 2.1 %shard_map.155 = (bf16[48,4096]{1,0:T(8,128)(2,1)S(1)}, bf16[16,32,128]{2,1,0:T(8,128)(2,1)}) custom-call(bf16[3,4,4096]{2,1,0:T(4,128)(2,1)S(1)} %bitcast.20, bf16[3,4,4096]{2,1,0:T(4,128)(2,1)S(1)} %collective-permute-done.refs_1_, bf16[3,4,4096]{2,1,0:T(4,128)(2,1)S(1)} %collective-permute-done.1.refs_2_, ...), custom_call_target="tpu_custom_call" | custom-call | flops 150994944 | bytes 3932160 | tf_op jit(solution)/shard_map/pallas_call | solution.py:397
  16.2 0.8 copy-done.8
  16.9 4.6 %all-to-all-start = ((bf16[16,32,128]{2,1,0:T(8,128)(2,1)}), bf16[16,32,128]{2,1,0:T(8,128)(2,1)S(1)}, u32[]{:S(2)}, u32[]{:S(2)}) async-start(bf16[16,32,128]{2,1,0:T(8,128)(2,1)} %get-tuple-element.18), calls=%async_computation | async-start | bytes 262144 | tf_op jit(solution)/shard_map/all_to_all | solution.py:385
  21.5 0.0 copy-done.2
  21.5 0.0 copy-done.1
  21.5 0.0 copy-start.9
  21.5 1.0 %copy-done.9 = bf16[48,4096]{1,0:T(8,128)(2,1)S(1)} copy-done((bf16[48,4096]{1,0:T(8,128)(2,1)S(1)}, bf16[48,4096]{1,0:T(8,128)(2,1)}, u32[]{:S(2)}) %copy-start.9) | copy-done | bytes 393240
  22.5 6.5 %shard_map.156.total_ref = f32[48,2304]{1,0:T(8,128)S(1)} custom-call(bf16[48,4096]{1,0:T(8,128)(2,1)S(1)} %copy-done.9, bf16[4096,2048]{1,0:T(8,128)(2,1)} %weight_ref.2, bf16[4096,128]{1,0:T(8,128)(2,1)S(1)} %copy-done.1, bf16[4096,128]{1,0:T(8,128)(2,1)S(1)} %copy-done.2, bf16[2048,4096]{1,0:T(8,128)(2,1)} %weight_ref.3, bf16[2048,4096]{1,0:T(8,128)(2,1)} %weight_ref.3, ...), custom_call_target="tpu_custom_call" | custom-call | tf_op jit(solution)/shard_map/pallas_call | solution.py:167
  29.0 0.4 all-to-all-done.ranks_ref
  29.4 0.0 copy-done.4
  29.4 0.0 copy-done.11
  29.4 0.0 copy-done.12
  29.4 0.0 copy-start.5
  29.4 0.0 copy-start.6
  29.5 0.0 copy-start.7
  29.5 0.9 %shard_map.157 = bf16[16,56,128]{2,1,0:T(8,128)(2,1)S(1)} custom-call(f32[48,2304]{1,0:T(8,128)S(1)} %shard_map.156.total_ref, s32[48,128]{1,0:T(8,128)S(1)} %get-tuple-element.16.refs_5_.slots_ref, bf16[16,32,128]{2,1,0:T(8,128)(2,1)S(1)} %all-to-all-done.ranks_ref, bf16[128,2048]{1,0:T(8,128)(2,1)S(1)} %bitcast.15, bf16[128,128]{1,0:T(8,128)(2,1)S(1)} %bitcast.21, ...), custom_call_target="tpu_custom_call" | custom-call | tf_op jit(solution)/shard_map/pallas_call | solution.py:410
  30.4 0.0 copy-start.3
  30.4 15.1 %all_to_all.20.arrived_ref = bf16[16,56,128]{2,1,0:T(8,128)(2,1)S(1)} all-to-all(bf16[16,56,128]{2,1,0:T(8,128)(2,1)S(1)} %shard_map.157), channel_id=1, replica_groups=mesh['parts'=2,'tensor'=4,'dp'=2,'pipe'=2] {'tensor','dp','pipe'}, dimensions={0} | all-to-all | bytes 458752 | tf_op jit(solution)/shard_map/all_to_all | solution.py:385
  45.5 0.0 copy-done.5
  45.5 0.0 copy-done.6
  45.5 1.8 %shard_map.158 = bf16[16,48,128]{2,1,0:T(8,128)(2,1)S(1)} custom-call(bf16[16,56,128]{2,1,0:T(8,128)(2,1)S(1)} %all_to_all.20.arrived_ref, bf16[1,4,512,128]{3,2,1,0:T(8,128)(2,1)S(1)} %copy-done.5, bf16[1,4,512,128]{3,2,1,0:T(8,128)(2,1)S(1)} %copy-done.6, s32[1]{0:T(128)S(6)} %copy.17.length_ref, f32[56,128]{1,0:T(8,128)S(1)} %get-tuple-element.19.cosine_ref, ...), custom_call_target="tpu_custom_call" | custom-call | tf_op jit(solution)/shard_map/pallas_call | solution.py:423
  47.3 11.6 %all_to_all.21.got_ref = bf16[16,48,128]{2,1,0:T(8,128)(2,1)S(1)} all-to-all(bf16[16,48,128]{2,1,0:T(8,128)(2,1)S(1)} %shard_map.158), channel_id=1, replica_groups=mesh['parts'=2,'tensor'=4,'dp'=2,'pipe'=2] {'tensor','dp','pipe'}, dimensions={0} | all-to-all | bytes 393216 | tf_op jit(solution)/shard_map/all_to_all | solution.py:385
  58.9 0.0 copy-done.7
  58.9 1.2 %shard_map.159 = (bf16[48,2048]{1,0:T(8,128)(2,1)S(1)}, bf16[16,16,128]{2,1,0:T(8,128)(2,1)}) custom-call(bf16[16,48,128]{2,1,0:T(8,128)(2,1)S(1)} %all_to_all.21.got_ref, bf16[128,2048]{1,0:T(8,128)(2,1)S(1)} %bitcast.16, s32[48,128]{1,0:T(8,128)S(1)} %get-tuple-element.16.refs_5_.slots_ref), custom_call_target="tpu_custom_call" | custom-call | tf_op jit(solution)/shard_map/pallas_call | solution.py:431
  60.1 3.5 %all-to-all-start.3 = ((bf16[16,16,128]{2,1,0:T(8,128)(2,1)}), bf16[16,16,128]{2,1,0:T(8,128)(2,1)S(1)}, u32[]{:S(2)}, u32[]{:S(2)}) async-start(bf16[16,16,128]{2,1,0:T(8,128)(2,1)} %get-tuple-element.22), calls=%async_computation.3 | async-start | bytes 131072 | tf_op jit(solution)/shard_map/all_to_all | solution.py:385
  63.6 6.4 %shard_map.160.total_ref = f32[48,4096]{1,0:T(8,128)S(1)} custom-call(bf16[48,2048]{1,0:T(8,128)(2,1)S(1)} %get-tuple-element.21.rows_ref, bf16[2048,4096]{1,0:T(8,128)(2,1)} %weight_ref.3), custom_call_target="tpu_custom_call" | custom-call | tf_op jit(solution)/shard_map/pallas_call | solution.py:167
  70.0 0.4 all-to-all-done.3.ranks_ref
  70.5 0.0 copy-done.3
  70.5 0.6 shard_map.161
  71.1 3.3 %collective-permute-start.3 = (bf16[3,4,4096]{2,1,0:T(4,128)(2,1)S(1)}, bf16[3,4,4096]{2,1,0:T(4,128)(2,1)S(1)}, u32[]{:S(2)}, u32[]{:S(2)}) collective-permute-start(bf16[3,4,4096]{2,1,0:T(4,128)(2,1)S(1)} %get-tuple-element.24), channel_id=1, source_target_pairs={{0,12},{4,0},{8,4},{12,8},{1,13},{5,1},{9,5},{13,9},{2,14},{6,2},{... | collective-permute-start | bytes 294920 | tf_op jit(solution)/shard_map/ppermute | solution.py:382
  74.4 0.0 collective-permute-start.4
  74.4 1.1 %collective-permute-start.5 = (bf16[3,4,4096]{2,1,0:T(4,128)(2,1)S(1)}, bf16[3,4,4096]{2,1,0:T(4,128)(2,1)S(1)}, u32[]{:S(2)}, u32[]{:S(2)}) collective-permute-start(bf16[3,4,4096]{2,1,0:T(4,128)(2,1)S(1)} %get-tuple-element.26), channel_id=1, source_target_pairs={{0,4},{4,8},{8,12},{12,0},{1,5},{5,9},{9,13},{13,1},{2,6},{6,10},{... | collective-permute-start | bytes 294920 | tf_op jit(solution)/shard_map/ppermute | solution.py:382
  75.5 2.1 %collective-permute-done.3 = bf16[3,4,4096]{2,1,0:T(4,128)(2,1)S(1)} collective-permute-done((bf16[3,4,4096]{2,1,0:T(4,128)(2,1)S(1)}, bf16[3,4,4096]{2,1,0:T(4,128)(2,1)S(1)}, u32[]{:S(2)}, u32[]{:S(2)}) %collective-permute-start.3) | collective-permute-done | bytes 98336 | tf_op jit(solution)/shard_map/ppermute | solution.py:382
  77.6 6.1 %collective-permute-done.4 = bf16[3,4,4096]{2,1,0:T(4,128)(2,1)S(1)} collective-permute-done((bf16[3,4,4096]{2,1,0:T(4,128)(2,1)S(1)}, bf16[3,4,4096]{2,1,0:T(4,128)(2,1)S(1)}, u32[]{:S(2)}, u32[]{:S(2)}) %collective-permute-start.4) | collective-permute-done | bytes 98336 | tf_op jit(solution)/shard_map/ppermute | solution.py:382
  83.7 0.0 collective-permute-done.5
  83.7 0.7 fusion
  (9 shorter events, 0.0 us)
Async XLA Ops:
  0.0 14.1 %copy-start.10 = (bf16[4,3,4096]{2,0,1:T(4,128)(2,1)S(1)}, bf16[4,3,4096]{2,0,1:T(4,128)(2,1)}, u32[]{:S(2)}) copy-start(bf16[4,3,4096]{2,0,1:T(4,128)(2,1)} %param.16) | copy-start | bytes 294916
  0.0 14.1 %copy-start = (bf16[4,4096,96]{1,2,0:T(8,128)(2,1)S(1)}, bf16[4,4096,96]{1,2,0:T(8,128)(2,1)}, u32[]{:S(2)}) copy-start(bf16[4,4096,96]{1,2,0:T(8,128)(2,1)} %param.21) | copy-start | bytes 9437188
  0.0 21.5 %copy-start.2 = (bf16[4096,128]{1,0:T(8,128)(2,1)S(1)}, bf16[4096,128]{1,0:T(8,128)(2,1)}, u32[]{:S(2)}) copy-start(bf16[4096,128]{1,0:T(8,128)(2,1)} %refs_1_.1) | copy-start | bytes 3145732
  0.0 21.5 %copy-start.1 = (bf16[4096,128]{1,0:T(8,128)(2,1)S(1)}, bf16[4096,128]{1,0:T(8,128)(2,1)}, u32[]{:S(2)}) copy-start(bf16[4096,128]{1,0:T(8,128)(2,1)} %refs_0_.1) | copy-start | bytes 3145732
  0.0 8.8 %collective-permute-start.2 = (bf16[3,4,4096]{2,1,0:T(4,128)(2,1)}, bf16[3,4,4096]{2,1,0:T(4,128)(2,1)S(1)}, u32[]{:S(2)}, u32[]{:S(2)}) collective-permute-start(bf16[3,4,4096]{2,1,0:T(4,128)(2,1)} %bitcast.17), channel_id=1, source_target_pairs={{0,12},{4,0},{8,4},{12,8},{1,13},{5,1},{9,5},{13,9},{2,14},{6,2},{... | collective-permute-start | bytes 294920 | tf_op jit(solution)/shard_map/ppermute | solution.py:382
  5.1 9.0 %collective-permute-start.1 = (bf16[3,4,4096]{2,1,0:T(4,128)(2,1)}, bf16[3,4,4096]{2,1,0:T(4,128)(2,1)S(1)}, u32[]{:S(2)}, u32[]{:S(2)}) collective-permute-start(bf16[3,4,4096]{2,1,0:T(4,128)(2,1)} %bitcast.18), channel_id=1, source_target_pairs={{0,8},{4,12},{8,0},{12,4},{1,9},{5,13},{9,1},{13,5},{2,10},{6,14},... | collective-permute-start | bytes 294920 | tf_op jit(solution)/shard_map/ppermute | solution.py:382
  5.1 9.0 %collective-permute-start = (bf16[3,4,4096]{2,1,0:T(4,128)(2,1)}, bf16[3,4,4096]{2,1,0:T(4,128)(2,1)S(1)}, u32[]{:S(2)}, u32[]{:S(2)}) collective-permute-start(bf16[3,4,4096]{2,1,0:T(4,128)(2,1)} %bitcast.19), channel_id=1, source_target_pairs={{0,4},{4,8},{8,12},{12,0},{1,5},{5,9},{9,13},{13,1},{2,6},{6,10},{... | collective-permute-start | bytes 294920 | tf_op jit(solution)/shard_map/ppermute | solution.py:382
  6.8 0.7 copy-start.13
  7.4 0.7 copy-start.14
  16.1 0.8 copy-start.8
  16.9 12.5 %all-to-all-start = ((bf16[16,32,128]{2,1,0:T(8,128)(2,1)}), bf16[16,32,128]{2,1,0:T(8,128)(2,1)S(1)}, u32[]{:S(2)}, u32[]{:S(2)}) async-start(bf16[16,32,128]{2,1,0:T(8,128)(2,1)} %get-tuple-element.18), calls=%async_computation | async-start | bytes 262144 | tf_op jit(solution)/shard_map/all_to_all | solution.py:385
  21.5 1.0 %copy-start.9 = (bf16[48,4096]{1,0:T(8,128)(2,1)S(1)}, bf16[48,4096]{1,0:T(8,128)(2,1)}, u32[]{:S(2)}) copy-start(bf16[48,4096]{1,0:T(8,128)(2,1)} %copy-done.8) | copy-start | bytes 1179652
  22.5 6.9 %copy-start.4 = (bf16[4,32,2048]{2,1,0:T(8,128)(2,1)S(1)}, bf16[4,32,2048]{2,1,0:T(8,128)(2,1)}, u32[]{:S(2)}) copy-start(bf16[4,32,2048]{2,1,0:T(8,128)(2,1)} %param.22) | copy-start | bytes 1572868
  22.5 6.9 %copy-start.11 = (bf16[4,32,128]{2,1,0:T(8,128)(2,1)S(1)}, bf16[4,32,128]{2,1,0:T(8,128)(2,1)}, u32[]{:S(2)}) copy-start(bf16[4,32,128]{2,1,0:T(8,128)(2,1)} %param.23) | copy-start | bytes 98308
  22.5 6.9 %copy-start.12 = (bf16[4,32,128]{2,1,0:T(8,128)(2,1)S(1)}, bf16[4,32,128]{2,1,0:T(8,128)(2,1)}, u32[]{:S(2)}) copy-start(bf16[4,32,128]{2,1,0:T(8,128)(2,1)} %param.24) | copy-start | bytes 98308
  29.4 16.1 %copy-start.5 = (bf16[1,4,512,128]{3,2,1,0:T(8,128)(2,1)S(1)}, bf16[1,4,512,128]{3,2,1,0:T(8,128)(2,1)}, u32[]{:S(2)}) copy-start(bf16[1,4,512,128]{3,2,1,0:T(8,128)(2,1)} %keys_ref.1) | copy-start | bytes 1572868
  29.4 16.1 %copy-start.6 = (bf16[1,4,512,128]{3,2,1,0:T(8,128)(2,1)S(1)}, bf16[1,4,512,128]{3,2,1,0:T(8,128)(2,1)}, u32[]{:S(2)}) copy-start(bf16[1,4,512,128]{3,2,1,0:T(8,128)(2,1)} %values_ref.1) | copy-start | bytes 1572868
  29.5 29.5 %copy-start.7 = (bf16[4,2048,32]{1,2,0:T(8,128)(2,1)S(1)}, bf16[4,2048,32]{1,2,0:T(8,128)(2,1)}, u32[]{:S(2)}) copy-start(bf16[4,2048,32]{1,2,0:T(8,128)(2,1)} %param.25) | copy-start | bytes 1572868
  30.4 40.1 %copy-start.3 = (bf16[4,32,4096]{2,1,0:T(8,128)(2,1)S(1)}, bf16[4,32,4096]{2,1,0:T(8,128)(2,1)}, u32[]{:S(2)}) copy-start(bf16[4,32,4096]{2,1,0:T(8,128)(2,1)} %param.26) | copy-start | bytes 3145732
  60.1 10.4 %all-to-all-start.3 = ((bf16[16,16,128]{2,1,0:T(8,128)(2,1)}), bf16[16,16,128]{2,1,0:T(8,128)(2,1)S(1)}, u32[]{:S(2)}, u32[]{:S(2)}) async-start(bf16[16,16,128]{2,1,0:T(8,128)(2,1)} %get-tuple-element.22), calls=%async_computation.3 | async-start | bytes 131072 | tf_op jit(solution)/shard_map/all_to_all | solution.py:385
  71.1 6.5 %collective-permute-start.3 = (bf16[3,4,4096]{2,1,0:T(4,128)(2,1)S(1)}, bf16[3,4,4096]{2,1,0:T(4,128)(2,1)S(1)}, u32[]{:S(2)}, u32[]{:S(2)}) collective-permute-start(bf16[3,4,4096]{2,1,0:T(4,128)(2,1)S(1)} %get-tuple-element.24), channel_id=1, source_target_pairs={{0,12},{4,0},{8,4},{12,8},{1,13},{5,1},{9,5},{13,9},{2,14},{6,2},{... | collective-permute-start | bytes 294920 | tf_op jit(solution)/shard_map/ppermute | solution.py:382
  74.4 9.3 %collective-permute-start.4 = (bf16[3,4,4096]{2,1,0:T(4,128)(2,1)S(1)}, bf16[3,4,4096]{2,1,0:T(4,128)(2,1)S(1)}, u32[]{:S(2)}, u32[]{:S(2)}) collective-permute-start(bf16[3,4,4096]{2,1,0:T(4,128)(2,1)S(1)} %get-tuple-element.25), channel_id=1, source_target_pairs={{0,8},{4,12},{8,0},{12,4},{1,9},{5,13},{9,1},{13,5},{2,10},{6,14},... | collective-permute-start | bytes 294920 | tf_op jit(solution)/shard_map/ppermute | solution.py:382
  74.4 9.3 %collective-permute-start.5 = (bf16[3,4,4096]{2,1,0:T(4,128)(2,1)S(1)}, bf16[3,4,4096]{2,1,0:T(4,128)(2,1)S(1)}, u32[]{:S(2)}, u32[]{:S(2)}) collective-permute-start(bf16[3,4,4096]{2,1,0:T(4,128)(2,1)S(1)} %get-tuple-element.26), channel_id=1, source_target_pairs={{0,4},{4,8},{8,12},{12,0},{1,5},{5,9},{9,13},{13,1},{2,6},{6,10},{... | collective-permute-start | bytes 294920 | tf_op jit(solution)/shard_map/ppermute | solution.py:382

commit v11 on v10

--- a/solution.py
+++ b/solution.py
@@ -215,7 +215,7 @@
     )(ids, pool, lengths, later)
 
 
-def grow_kernel(sizes, width, total_ref, slots_ref, ranks_ref, *refs):
+def grow_kernel(sizes, width, total_ref, rows_ref, value_ref, slots_ref, ranks_ref, *refs):
     groups, blocks, drafts = sizes
     grows, (out_ref, held) = refs[:3], refs[-2:]
     group = group_of()
@@ -236,9 +236,11 @@
     start, column = 0, 0
     for index, grow in enumerate(grows):
         deep, cols = grow.shape
-        full = total_ref[:, column : column + cols] + dot(
-            wide[:, index * deep : (index + 1) * deep], grow[...]
-        )
+        if column < total_ref.shape[1]:
+            full = total_ref[:, column : column + cols]
+        else:
+            full = dot(rows_ref[...], value_ref[...])
+        full = full + dot(wide[:, index * deep : (index + 1) * deep], grow[...])
         column += cols
         full = dot(arranged, full.astype(jnp.bfloat16))
         for head in range(cols // 128):
@@ -403,18 +405,20 @@
         2 * shrink_qkv.size + 4 * count * features,
     )(*pieces, shrink_in, slots)
     ranks = exchange(rank_part)
-    total = stream(rows, w_query, 8, [w_key, w_value], [w_out] * 3)
-    cols = total.shape[1]
+    total = stream(rows, w_query, 8, [w_key], [w_out] * 3)
+    cols = total.shape[1] + w_value.shape[1]
     head_cols = w_query.shape[1]
     query_lines = head_cols // head_size * drafts
     sent = call(
         functools.partial(grow_kernel, sizes, width),
         shape((blocks * groups, lines, head_size)),
-        [VMEM] * 6 + [HBM] * 2,
+        [VMEM] * 8 + [HBM] * 2,
         [pltpu.VMEM((blocks * groups * lines, head_size), jnp.float32)],
         limit=40 * MIB,
     )(
         total,
+        rows,
+        w_value,
         slots,
         ranks,
         *[grow.reshape(owned * width, -1) for grow in (grow_query, grow_key, grow_value)],

time: 84.9 us -> 84.3 us (level)
  local copies, waits for them, and re-layouts: 3.1 us -> 1.38 us
  Pallas kernels: 20.2 us -> 21.4 us
  blocking collectives: 26.7 us -> 25.7 us
  waiting for transfers between devices: 14.3 us -> 15.2 us
    unnamed x30, local copies, waits for them, and re-layouts: 3.1 us -> 1.38 us
    pallas_call x1, Pallas kernels: 0.92 us -> 2.1 us  [by_kernels(): call(functools.partial(grow_kernel, sizes, width), shape((blocks * groups...]
    all_to_all x2, blocking collectives: 26.7 us -> 25.7 us  [exchange(): return lax.all_to_all(value, EVERY, split_axis=0, concat_axis=0, tiled=True)]
    all_to_all x2, waiting for transfers between devices: 0.84 us -> 1.83 us  [exchange(): return lax.all_to_all(value, EVERY, split_axis=0, concat_axis=0, tiled=True)]
where the time goes in v11:
time: 84.3 us; the launch traced here: 83.9 us
  blocking collectives  25.7 us (30%)
  Pallas kernels  21.4 us (25%)
  starting transfers between devices  18.6 us (22%)
  waiting for transfers between devices  15.2 us (18%)
  local copies, waits for them, and re-layouts  1.38 us (2%)
  between operations  0.86 us (1%)
    all_to_all x2, blocking collectives, exchange(): return lax.all_to_all(value, EVERY, split_axis=0, concat_axis=0, tiled=True)  25.7 us
    ppermute x6, waiting for transfers between devices, over_tensor(): return lax.ppermute(value, 'tensor', route)  13.4 us
    pallas_call x2, Pallas kernels, stream(): call(functools.partial(stream_kernel, chunks, len(small)), shape((rows.sh...  12.9 us
    ppermute x6, starting transfers between devices, over_tensor(): return lax.ppermute(value, 'tensor', route)  10.5 us
    all_to_all x2, starting transfers between devices, exchange(): return lax.all_to_all(value, EVERY, split_axis=0, concat_axis=0, tiled=True)  8.13 us
    pallas_call x1, Pallas kernels, by_kernels(): call(functools.partial(grow_kernel, sizes, width), shape((blocks * groups...  2.1 us
    pallas_call x1, Pallas kernels, by_kernels(): call(functools.partial(rank_kernel, sizes, owned), [shape((count, feature...  2.05 us
    all_to_all x2, waiting for transfers between devices, exchange(): return lax.all_to_all(value, EVERY, split_axis=0, concat_axis=0, tiled=True)  1.83 us
  transfers between devices with their start and end apart: 8, of which 5 were waited for; matrix products, arithmetic and copies ran while one was open for 0% of the time, Pallas kernels for 16%

profile of v11, /device:TPU:0, one launch (start us, length us, event | category | flops | bytes accessed | tf_op | source)
XLA Modules:
  0.0 83.9 jit_solution(9542258035921565767)
XLA Ops:
  0.0 5.1 %collective-permute-start.2 = (bf16[3,4,4096]{2,1,0:T(4,128)(2,1)}, bf16[3,4,4096]{2,1,0:T(4,128)(2,1)S(1)}, u32[]{:S(2)}, u32[]{:S(2)}) collective-permute-start(bf16[3,4,4096]{2,1,0:T(4,128)(2,1)} %bitcast.17), channel_id=1, source_target_pairs={{0,12},{4,0},{8,4},{12,8},{1,13},{5,1},{9,5},{13,9},{2,14},{6,2},{... | collective-permute-start | bytes 294920 | tf_op jit(solution)/shard_map/ppermute | solution.py:384
  5.1 0.0 collective-permute-start.1
  5.1 1.0 %collective-permute-start = (bf16[3,4,4096]{2,1,0:T(4,128)(2,1)}, bf16[3,4,4096]{2,1,0:T(4,128)(2,1)S(1)}, u32[]{:S(2)}, u32[]{:S(2)}) collective-permute-start(bf16[3,4,4096]{2,1,0:T(4,128)(2,1)} %bitcast.19), channel_id=1, source_target_pairs={{0,4},{4,8},{8,12},{12,0},{1,5},{5,9},{9,13},{13,1},{2,6},{6,10},{... | collective-permute-start | bytes 294920 | tf_op jit(solution)/shard_map/ppermute | solution.py:384
  6.8 0.0 copy-start.13
  6.8 0.6 copy-done.13
  7.4 0.7 copy-done.14
  8.1 0.7 shard_map.154
  8.8 0.0 copy-start.11
  8.8 0.0 collective-permute-done.2.refs_3_
  8.8 5.2 %collective-permute-done.1.refs_2_ = bf16[3,4,4096]{2,1,0:T(4,128)(2,1)S(1)} collective-permute-done((bf16[3,4,4096]{2,1,0:T(4,128)(2,1)}, bf16[3,4,4096]{2,1,0:T(4,128)(2,1)S(1)}, u32[]{:S(2)}, u32[]{:S(2)}) %collective-permute-start.1) | collective-permute-done | bytes 98336 | tf_op jit(solution)/shard_map/ppermute | solution.py:384
  14.1 0.0 collective-permute-done.refs_1_
  14.1 0.0 copy-done.8
  14.1 0.0 copy-done
  14.1 2.0 %shard_map.155 = (bf16[48,4096]{1,0:T(8,128)(2,1)S(1)}, bf16[16,32,128]{2,1,0:T(8,128)(2,1)}) custom-call(bf16[3,4,4096]{2,1,0:T(4,128)(2,1)S(1)} %bitcast.20, bf16[3,4,4096]{2,1,0:T(4,128)(2,1)S(1)} %collective-permute-done.refs_1_, bf16[3,4,4096]{2,1,0:T(4,128)(2,1)S(1)} %collective-permute-done.1.refs_2_, ...), custom_call_target="tpu_custom_call" | custom-call | flops 150994944 | bytes 3932160 | tf_op jit(solution)/shard_map/pallas_call | solution.py:399
  16.1 4.6 %all-to-all-start = ((bf16[16,32,128]{2,1,0:T(8,128)(2,1)}), bf16[16,32,128]{2,1,0:T(8,128)(2,1)}, u32[]{:S(2)}, u32[]{:S(2)}) async-start(bf16[16,32,128]{2,1,0:T(8,128)(2,1)} %get-tuple-element.18), calls=%async_computation | async-start | bytes 262144 | tf_op jit(solution)/shard_map/all_to_all | solution.py:387
  20.8 0.0 copy-done.11
  20.8 0.0 copy-done.1
  20.8 0.0 copy-start.2
  20.8 0.0 copy-start.4
  20.8 0.0 copy-start.9
  20.8 0.0 copy-start.10
  20.8 6.5 %shard_map.156.total_ref = f32[48,2176]{1,0:T(8,128)S(1)} custom-call(bf16[48,4096]{1,0:T(8,128)(2,1)S(1)} %get-tuple-element.17.rows_ref, bf16[4096,2048]{1,0:T(8,128)(2,1)} %weight_ref.2, bf16[4096,128]{1,0:T(8,128)(2,1)S(1)} %copy-done.1, bf16[2048,4096]{1,0:T(8,128)(2,1)} %weight_ref.3, bf16[2048,4096]{1,0:T(8,128)(2,1)} %weight_ref.3, ...), custom_call_target="tpu_custom_call" | custom-call | tf_op jit(solution)/shard_map/pallas_call | solution.py:167
  27.4 1.4 %all-to-all-done.ranks_ref = bf16[16,32,128]{2,1,0:T(8,128)(2,1)} async-done(((bf16[16,32,128]{2,1,0:T(8,128)(2,1)}), bf16[16,32,128]{2,1,0:T(8,128)(2,1)}, u32[]{:S(2)}, u32[]{:S(2)}) %all-to-all-start) | async-done | bytes 131104 | tf_op jit(solution)/shard_map/all_to_all | solution.py:387
  28.8 0.0 copy-done.2
  28.8 0.0 copy-done.4
  28.8 0.0 copy-done.9
  28.8 0.0 copy-start.5
  28.8 0.0 copy-start.6
  28.8 0.0 copy-start.12
  28.8 0.0 copy-start.7
  28.8 2.1 %shard_map.157 = bf16[16,56,128]{2,1,0:T(8,128)(2,1)S(1)} custom-call(f32[48,2176]{1,0:T(8,128)S(1)} %shard_map.156.total_ref, bf16[48,4096]{1,0:T(8,128)(2,1)S(1)} %get-tuple-element.17.rows_ref, bf16[4096,128]{1,0:T(8,128)(2,1)S(1)} %copy-done.2, s32[48,128]{1,0:T(8,128)S(1)} %get-tuple-element.16.refs_5_.slots_ref, ...), custom_call_target="tpu_custom_call" | custom-call | tf_op jit(solution)/shard_map/pallas_call | solution.py:412
  30.9 0.0 copy-start.3
  30.9 14.1 %all_to_all.20.arrived_ref = bf16[16,56,128]{2,1,0:T(8,128)(2,1)S(1)} all-to-all(bf16[16,56,128]{2,1,0:T(8,128)(2,1)S(1)} %shard_map.157), channel_id=1, replica_groups=mesh['parts'=2,'tensor'=4,'dp'=2,'pipe'=2] {'tensor','dp','pipe'}, dimensions={0} | all-to-all | bytes 458752 | tf_op jit(solution)/shard_map/all_to_all | solution.py:387
  45.0 0.0 copy-done.6
  45.0 1.8 %shard_map.158 = bf16[16,48,128]{2,1,0:T(8,128)(2,1)S(1)} custom-call(bf16[16,56,128]{2,1,0:T(8,128)(2,1)S(1)} %all_to_all.20.arrived_ref, bf16[1,4,512,128]{3,2,1,0:T(8,128)(2,1)S(1)} %copy-done.5, bf16[1,4,512,128]{3,2,1,0:T(8,128)(2,1)S(1)} %copy-done.6, s32[1]{0:T(128)S(6)} %copy.17.length_ref, f32[56,128]{1,0:T(8,128)S(1)} %get-tuple-element.19.cosine_ref, ...), custom_call_target="tpu_custom_call" | custom-call | tf_op jit(solution)/shard_map/pallas_call | solution.py:427
  46.8 11.6 %all_to_all.21.got_ref = bf16[16,48,128]{2,1,0:T(8,128)(2,1)S(1)} all-to-all(bf16[16,48,128]{2,1,0:T(8,128)(2,1)S(1)} %shard_map.158), channel_id=1, replica_groups=mesh['parts'=2,'tensor'=4,'dp'=2,'pipe'=2] {'tensor','dp','pipe'}, dimensions={0} | all-to-all | bytes 393216 | tf_op jit(solution)/shard_map/all_to_all | solution.py:387
  58.4 1.2 %shard_map.159 = (bf16[48,2048]{1,0:T(8,128)(2,1)S(1)}, bf16[16,16,128]{2,1,0:T(8,128)(2,1)}) custom-call(bf16[16,48,128]{2,1,0:T(8,128)(2,1)S(1)} %all_to_all.21.got_ref, bf16[128,2048]{1,0:T(8,128)(2,1)S(1)} %bitcast.16, s32[48,128]{1,0:T(8,128)S(1)} %get-tuple-element.16.refs_5_.slots_ref), custom_call_target="tpu_custom_call" | custom-call | tf_op jit(solution)/shard_map/pallas_call | solution.py:435
  59.6 3.5 %all-to-all-start.3 = ((bf16[16,16,128]{2,1,0:T(8,128)(2,1)}), bf16[16,16,128]{2,1,0:T(8,128)(2,1)S(1)}, u32[]{:S(2)}, u32[]{:S(2)}) async-start(bf16[16,16,128]{2,1,0:T(8,128)(2,1)} %get-tuple-element.22), calls=%async_computation.3 | async-start | bytes 131072 | tf_op jit(solution)/shard_map/all_to_all | solution.py:387
  63.1 6.4 %shard_map.160.total_ref = f32[48,4096]{1,0:T(8,128)S(1)} custom-call(bf16[48,2048]{1,0:T(8,128)(2,1)S(1)} %get-tuple-element.21.rows_ref, bf16[2048,4096]{1,0:T(8,128)(2,1)} %weight_ref.3), custom_call_target="tpu_custom_call" | custom-call | tf_op jit(solution)/shard_map/pallas_call | solution.py:167
  69.5 0.4 all-to-all-done.3.ranks_ref
  70.0 0.6 shard_map.161
  70.6 3.3 %collective-permute-start.3 = (bf16[3,4,4096]{2,1,0:T(4,128)(2,1)S(1)}, bf16[3,4,4096]{2,1,0:T(4,128)(2,1)S(1)}, u32[]{:S(2)}, u32[]{:S(2)}) collective-permute-start(bf16[3,4,4096]{2,1,0:T(4,128)(2,1)S(1)} %get-tuple-element.24), channel_id=1, source_target_pairs={{0,12},{4,0},{8,4},{12,8},{1,13},{5,1},{9,5},{13,9},{2,14},{6,2},{... | collective-permute-start | bytes 294920 | tf_op jit(solution)/shard_map/ppermute | solution.py:384
  73.9 0.0 collective-permute-start.4
  73.9 1.1 %collective-permute-start.5 = (bf16[3,4,4096]{2,1,0:T(4,128)(2,1)S(1)}, bf16[3,4,4096]{2,1,0:T(4,128)(2,1)S(1)}, u32[]{:S(2)}, u32[]{:S(2)}) collective-permute-start(bf16[3,4,4096]{2,1,0:T(4,128)(2,1)S(1)} %get-tuple-element.26), channel_id=1, source_target_pairs={{0,4},{4,8},{8,12},{12,0},{1,5},{5,9},{9,13},{13,1},{2,6},{6,10},{... | collective-permute-start | bytes 294920 | tf_op jit(solution)/shard_map/ppermute | solution.py:384
  75.0 2.1 %collective-permute-done.3 = bf16[3,4,4096]{2,1,0:T(4,128)(2,1)S(1)} collective-permute-done((bf16[3,4,4096]{2,1,0:T(4,128)(2,1)S(1)}, bf16[3,4,4096]{2,1,0:T(4,128)(2,1)S(1)}, u32[]{:S(2)}, u32[]{:S(2)}) %collective-permute-start.3) | collective-permute-done | bytes 98336 | tf_op jit(solution)/shard_map/ppermute | solution.py:384
  77.1 6.1 %collective-permute-done.4 = bf16[3,4,4096]{2,1,0:T(4,128)(2,1)S(1)} collective-permute-done((bf16[3,4,4096]{2,1,0:T(4,128)(2,1)S(1)}, bf16[3,4,4096]{2,1,0:T(4,128)(2,1)S(1)}, u32[]{:S(2)}, u32[]{:S(2)}) %collective-permute-start.4) | collective-permute-done | bytes 98336 | tf_op jit(solution)/shard_map/ppermute | solution.py:384
  83.2 0.0 collective-permute-done.5
  83.2 0.7 fusion
  (9 shorter events, 0.0 us)
Async XLA Ops:
  0.0 14.1 %copy-start.8 = (bf16[4,3,4096]{2,0,1:T(4,128)(2,1)S(1)}, bf16[4,3,4096]{2,0,1:T(4,128)(2,1)}, u32[]{:S(2)}) copy-start(bf16[4,3,4096]{2,0,1:T(4,128)(2,1)} %param.16) | copy-start | bytes 294916
  0.0 14.1 %copy-start = (bf16[4,4096,96]{1,2,0:T(8,128)(2,1)S(1)}, bf16[4,4096,96]{1,2,0:T(8,128)(2,1)}, u32[]{:S(2)}) copy-start(bf16[4,4096,96]{1,2,0:T(8,128)(2,1)} %param.21) | copy-start | bytes 9437188
  0.0 20.8 %copy-start.1 = (bf16[4096,128]{1,0:T(8,128)(2,1)S(1)}, bf16[4096,128]{1,0:T(8,128)(2,1)}, u32[]{:S(2)}) copy-start(bf16[4096,128]{1,0:T(8,128)(2,1)} %refs_0_.1) | copy-start | bytes 3145732
  0.0 8.8 %collective-permute-start.2 = (bf16[3,4,4096]{2,1,0:T(4,128)(2,1)}, bf16[3,4,4096]{2,1,0:T(4,128)(2,1)S(1)}, u32[]{:S(2)}, u32[]{:S(2)}) collective-permute-start(bf16[3,4,4096]{2,1,0:T(4,128)(2,1)} %bitcast.17), channel_id=1, source_target_pairs={{0,12},{4,0},{8,4},{12,8},{1,13},{5,1},{9,5},{13,9},{2,14},{6,2},{... | collective-permute-start | bytes 294920 | tf_op jit(solution)/shard_map/ppermute | solution.py:384
  5.1 9.0 %collective-permute-start.1 = (bf16[3,4,4096]{2,1,0:T(4,128)(2,1)}, bf16[3,4,4096]{2,1,0:T(4,128)(2,1)S(1)}, u32[]{:S(2)}, u32[]{:S(2)}) collective-permute-start(bf16[3,4,4096]{2,1,0:T(4,128)(2,1)} %bitcast.18), channel_id=1, source_target_pairs={{0,8},{4,12},{8,0},{12,4},{1,9},{5,13},{9,1},{13,5},{2,10},{6,14},... | collective-permute-start | bytes 294920 | tf_op jit(solution)/shard_map/ppermute | solution.py:384
  5.1 9.0 %collective-permute-start = (bf16[3,4,4096]{2,1,0:T(4,128)(2,1)}, bf16[3,4,4096]{2,1,0:T(4,128)(2,1)S(1)}, u32[]{:S(2)}, u32[]{:S(2)}) collective-permute-start(bf16[3,4,4096]{2,1,0:T(4,128)(2,1)} %bitcast.19), channel_id=1, source_target_pairs={{0,4},{4,8},{8,12},{12,0},{1,5},{5,9},{9,13},{13,1},{2,6},{6,10},{... | collective-permute-start | bytes 294920 | tf_op jit(solution)/shard_map/ppermute | solution.py:384
  6.8 0.7 copy-start.13
  7.4 0.7 copy-start.14
  8.8 11.9 %copy-start.11 = (f32[56,128]{1,0:T(8,128)}, f32[56,128]{1,0:T(8,128)S(1)}, u32[]{:S(2)}) copy-start(f32[56,128]{1,0:T(8,128)S(1)} %get-tuple-element.20.sine_ref) | copy-start | bytes 86020
  16.1 12.6 %all-to-all-start = ((bf16[16,32,128]{2,1,0:T(8,128)(2,1)}), bf16[16,32,128]{2,1,0:T(8,128)(2,1)}, u32[]{:S(2)}, u32[]{:S(2)}) async-start(bf16[16,32,128]{2,1,0:T(8,128)(2,1)} %get-tuple-element.18), calls=%async_computation | async-start | bytes 262144 | tf_op jit(solution)/shard_map/all_to_all | solution.py:387
  20.8 8.0 %copy-start.2 = (bf16[4096,128]{1,0:T(8,128)(2,1)S(1)}, bf16[4096,128]{1,0:T(8,128)(2,1)}, u32[]{:S(2)}) copy-start(bf16[4096,128]{1,0:T(8,128)(2,1)} %value_ref.1) | copy-start | bytes 3145732
  20.8 8.0 %copy-start.4 = (bf16[4,32,2048]{2,1,0:T(8,128)(2,1)S(1)}, bf16[4,32,2048]{2,1,0:T(8,128)(2,1)}, u32[]{:S(2)}) copy-start(bf16[4,32,2048]{2,1,0:T(8,128)(2,1)} %param.22) | copy-start | bytes 1572868
  20.8 8.0 %copy-start.9 = (bf16[4,32,128]{2,1,0:T(8,128)(2,1)S(1)}, bf16[4,32,128]{2,1,0:T(8,128)(2,1)}, u32[]{:S(2)}) copy-start(bf16[4,32,128]{2,1,0:T(8,128)(2,1)} %param.23) | copy-start | bytes 98308
  20.8 7.9 %copy-start.10 = (bf16[4,32,128]{2,1,0:T(8,128)(2,1)S(1)}, bf16[4,32,128]{2,1,0:T(8,128)(2,1)}, u32[]{:S(2)}) copy-start(bf16[4,32,128]{2,1,0:T(8,128)(2,1)} %param.24) | copy-start | bytes 98308
  28.8 16.2 %copy-start.5 = (bf16[1,4,512,128]{3,2,1,0:T(8,128)(2,1)S(1)}, bf16[1,4,512,128]{3,2,1,0:T(8,128)(2,1)}, u32[]{:S(2)}) copy-start(bf16[1,4,512,128]{3,2,1,0:T(8,128)(2,1)} %keys_ref.1) | copy-start | bytes 1572868
  28.8 16.2 %copy-start.6 = (bf16[1,4,512,128]{3,2,1,0:T(8,128)(2,1)S(1)}, bf16[1,4,512,128]{3,2,1,0:T(8,128)(2,1)}, u32[]{:S(2)}) copy-start(bf16[1,4,512,128]{3,2,1,0:T(8,128)(2,1)} %values_ref.1) | copy-start | bytes 1572868
  28.8 16.2 %copy-start.12 = (f32[56,128]{1,0:T(8,128)S(1)}, f32[56,128]{1,0:T(8,128)}, u32[]{:S(2)}) copy-start(f32[56,128]{1,0:T(8,128)} %copy-done.11) | copy-start | bytes 86020
  28.8 29.6 %copy-start.7 = (bf16[4,2048,32]{1,2,0:T(8,128)(2,1)S(1)}, bf16[4,2048,32]{1,2,0:T(8,128)(2,1)}, u32[]{:S(2)}) copy-start(bf16[4,2048,32]{1,2,0:T(8,128)(2,1)} %param.25) | copy-start | bytes 1572868
  30.9 39.0 %copy-start.3 = (bf16[4,32,4096]{2,1,0:T(8,128)(2,1)S(1)}, bf16[4,32,4096]{2,1,0:T(8,128)(2,1)}, u32[]{:S(2)}) copy-start(bf16[4,32,4096]{2,1,0:T(8,128)(2,1)} %param.26) | copy-start | bytes 3145732
  59.6 10.4 %all-to-all-start.3 = ((bf16[16,16,128]{2,1,0:T(8,128)(2,1)}), bf16[16,16,128]{2,1,0:T(8,128)(2,1)S(1)}, u32[]{:S(2)}, u32[]{:S(2)}) async-start(bf16[16,16,128]{2,1,0:T(8,128)(2,1)} %get-tuple-element.22), calls=%async_computation.3 | async-start | bytes 131072 | tf_op jit(solution)/shard_map/all_to_all | solution.py:387
  70.6 6.5 %collective-permute-start.3 = (bf16[3,4,4096]{2,1,0:T(4,128)(2,1)S(1)}, bf16[3,4,4096]{2,1,0:T(4,128)(2,1)S(1)}, u32[]{:S(2)}, u32[]{:S(2)}) collective-permute-start(bf16[3,4,4096]{2,1,0:T(4,128)(2,1)S(1)} %get-tuple-element.24), channel_id=1, source_target_pairs={{0,12},{4,0},{8,4},{12,8},{1,13},{5,1},{9,5},{13,9},{2,14},{6,2},{... | collective-permute-start | bytes 294920 | tf_op jit(solution)/shard_map/ppermute | solution.py:384
  73.9 9.3 %collective-permute-start.4 = (bf16[3,4,4096]{2,1,0:T(4,128)(2,1)S(1)}, bf16[3,4,4096]{2,1,0:T(4,128)(2,1)S(1)}, u32[]{:S(2)}, u32[]{:S(2)}) collective-permute-start(bf16[3,4,4096]{2,1,0:T(4,128)(2,1)S(1)} %get-tuple-element.25), channel_id=1, source_target_pairs={{0,8},{4,12},{8,0},{12,4},{1,9},{5,13},{9,1},{13,5},{2,10},{6,14},... | collective-permute-start | bytes 294920 | tf_op jit(solution)/shard_map/ppermute | solution.py:384
  73.9 9.3 %collective-permute-start.5 = (bf16[3,4,4096]{2,1,0:T(4,128)(2,1)S(1)}, bf16[3,4,4096]{2,1,0:T(4,128)(2,1)S(1)}, u32[]{:S(2)}, u32[]{:S(2)}) collective-permute-start(bf16[3,4,4096]{2,1,0:T(4,128)(2,1)S(1)} %get-tuple-element.26), channel_id=1, source_target_pairs={{0,4},{4,8},{8,12},{12,0},{1,5},{5,9},{9,13},{13,1},{2,6},{6,10},{... | collective-permute-start | bytes 294920 | tf_op jit(solution)/shard_map/ppermute | solution.py:384

commit v12 on v10

--- a/solution.py
+++ b/solution.py
@@ -102,17 +102,16 @@
     rows_ref[...] = rows
     place = slots_ref[:, 0:1] - lax.axis_index("tensor") * owned
     ranks = owned_ranks(
-        rows, shrink_ref[...], place, shrink_ref.shape[0] // owned, rank_ref.shape[2]
-    )
-    put = (rank_ref.shape[1], rows.shape[0])
+        rows, shrink_ref[...], place, shrink_ref.shape[0] // owned, rank_ref.shape[1]
+    )
+    put = (rank_ref.shape[0], rows.shape[0])
     draft = parts_of(as_gathered, sizes, iota((rows.shape[0], put[0]), 0))[2]
     line = slots_ref[:, 2:3] * drafts + draft
     put = jnp.where(line == iota((rows.shape[0], put[0]), 1), 1.0, 0.0).astype(jnp.bfloat16)
     ranks = lax.dot_general(
         put, ranks, (((0,), (0,)), ((), ())), preferred_element_type=jnp.float32
-    ).astype(jnp.bfloat16)
-    for target in range(rank_ref.shape[0]):
-        rank_ref[target] = ranks
+    )
+    rank_ref[...] = ranks.astype(jnp.bfloat16)
 
 
 def owned_ranks(rows, shrink, place, width, lanes):
@@ -135,46 +134,30 @@
     return jnp.where(slot == place, wide, 0.0).astype(jnp.bfloat16)
 
 
-def stream_kernel(chunks, small, rows_ref, weight_ref, *refs):
-    total_ref, buffer, sems = refs[-3:]
-    depth = rows_ref.shape[1] // chunks
-    width = weight_ref.shape[1]
-
-    def copy(chunk):
-        part = pl.ds(chunk * depth, depth)
-        return pltpu.make_async_copy(weight_ref.at[part], buffer.at[part], sems.at[chunk])
-
-    for chunk in range(chunks):
-        copy(chunk).start()
-    start = width
-    for other in refs[:small]:
-        total_ref[:, start : start + other.shape[1]] = dot(rows_ref[...], other[...])
-        start += other.shape[1]
-    for chunk in range(chunks):
-        copy(chunk).wait()
-        product = dot(
-            rows_ref[:, chunk * depth : (chunk + 1) * depth],
-            buffer[chunk * depth : (chunk + 1) * depth, :],
-        )
-        if chunk:
-            total_ref[:, 0:width] += product
-        else:
-            total_ref[:, 0:width] = product
-
-
-def stream(rows, weight, chunks, small=(), later=()):
-    width = weight.shape[1] + sum(other.shape[1] for other in small)
+def product_kernel(rows_ref, *refs):
+    *weights, total_ref = refs
+    start = 0
+    for weight in weights:
+        width = weight.shape[1]
+        step = width if width % 1024 else 1024
+        for first in range(0, width, step):
+            total_ref[:, start : start + step] = dot(
+                rows_ref[...], weight[:, first : first + step]
+            )
+            start += step
+
+
+def product(rows, *weights):
+    width = sum(weight.shape[1] for weight in weights)
     return call(
-        functools.partial(stream_kernel, chunks, len(small)),
+        product_kernel,
         shape((rows.shape[0], width), jnp.float32),
-        [VMEM, HBM] + [VMEM] * len(small) + [HBM] * len(later),
-        [pltpu.VMEM(weight.shape, weight.dtype), pltpu.SemaphoreType.DMA((chunks,))],
-        limit=40 * MIB,
-    )(rows, weight, *small, *later)
-
-
-def prepare_kernel(sizes, owned, ids_ref, pool_ref, length_ref, _, *outs):
-    slots_ref, cosine_ref, sine_ref = outs
+        [VMEM] * (1 + len(weights)),
+    )(rows, *weights)
+
+
+def prepare_kernel(sizes, owned, ids_ref, pool_ref, length_ref, *refs):
+    slots_ref, cosine_ref, sine_ref = refs[-3:]
     groups, blocks, drafts = sizes
     width = cosine_ref.shape[1]
     lane = iota(cosine_ref.shape, 1)
@@ -210,22 +193,22 @@
     return call(
         functools.partial(prepare_kernel, sizes, owned),
         [shape((groups * blocks * drafts, 128), jnp.int32), table, table],
-        [smem, smem, smem, HBM],
+        [smem, smem, smem] + [HBM] * 3,
         limit=40 * MIB,
-    )(ids, pool, lengths, later)
-
-
-def grow_kernel(sizes, width, total_ref, slots_ref, ranks_ref, *refs):
-    groups, blocks, drafts = sizes
-    grows, (out_ref, held) = refs[:3], refs[-2:]
+    )(ids, pool, lengths, *[later] * 3)
+
+
+def grow_kernel(sizes, width, total_ref, slots_ref, *refs):
+    groups, blocks, drafts = sizes
+    ranks_in, grows, (out_ref, held) = refs[:groups], refs[groups : groups + 3], refs[-2:]
     group = group_of()
     requests = groups * blocks
     lines = out_ref.shape[1]
     held[...] = jnp.zeros(held.shape, jnp.float32)
     owned = grows[0].shape[0] // width
-    ranks = ranks_ref[group * groups].astype(jnp.float32)
-    for other in range(1, groups):
-        ranks = ranks + ranks_ref[group * groups + other].astype(jnp.float32)
+    ranks = ranks_in[0][...].astype(jnp.float32)
+    for other in ranks_in[1:]:
+        ranks = ranks + other[...].astype(jnp.float32)
     get = (total_ref.shape[0], ranks.shape[0])
     draft = parts_of(as_gathered, sizes, iota(get, 0))[2]
     get = slots_ref[:, 3:4] * drafts + draft == iota(get, 1)
@@ -291,7 +274,8 @@
     return parts, rows // parts
 
 
-def out_rank_kernel(sizes, owned, got_ref, shrink_ref, slots_ref, rows_ref, rank_ref, wide):
+def out_rank_kernel(sizes, owned, got_ref, shrink_ref, slots_ref, *refs):
+    rows_ref, rank_ref, wide = refs[-3:]
     drafts = sizes[2]
     requests, lines, head_size = got_ref.shape
     for row in range(requests):
@@ -305,7 +289,7 @@
     rows = rows_ref[...]
     place = slots_ref[:, 1:2] - group_of() * owned
     width = shrink_ref.shape[0] // owned
-    _, held, lanes = rank_ref.shape
+    held, lanes = rank_ref.shape
     parts, span = packing(rows.shape[0], width, lanes)
     ranks = dot_nt(rows, shrink_ref[...])
     kept = jnp.where(over(iota(ranks.shape, 1), width) == place, ranks, 0.0).astype(jnp.bfloat16)
@@ -316,18 +300,18 @@
     ranks = jnp.where(mine, ranks, 0.0).astype(jnp.bfloat16)
     put = (held, rows.shape[0])
     put = iota(put, 0) == rest_of(iota(put, 1), span)
-    ranks = dot(jnp.where(put, 1.0, 0.0).astype(jnp.bfloat16), ranks).astype(jnp.bfloat16)
-    for target in range(rank_ref.shape[0]):
-        rank_ref[target] = ranks
-
-
-def out_grow_kernel(sizes, width, total_ref, slots_ref, ranks_ref, grow_ref, *outs):
-    groups, blocks, drafts = sizes
+    ranks = dot(jnp.where(put, 1.0, 0.0).astype(jnp.bfloat16), ranks)
+    rank_ref[...] = ranks.astype(jnp.bfloat16)
+
+
+def out_grow_kernel(sizes, width, total_ref, slots_ref, grow_ref, *refs):
+    groups, blocks, drafts = sizes
+    ranks_in, outs = refs[:blocks], refs[blocks:]
     owned = grow_ref.shape[0] // width
     me = lax.axis_index("tensor")
-    ranks = ranks_ref[me].astype(jnp.float32)
-    for source in range(1, blocks):
-        ranks = ranks + ranks_ref[source * groups + me].astype(jnp.float32)
+    ranks = ranks_in[0][...].astype(jnp.float32)
+    for other in ranks_in[1:]:
+        ranks = ranks + other[...].astype(jnp.float32)
     count = total_ref.shape[0]
     held, lanes = ranks.shape
     parts, span = packing(count, width, lanes)
@@ -381,6 +365,22 @@
         route = [(t, (t + shift) % blocks) for t in range(blocks)]
         return lax.ppermute(value, "tensor", route)
 
+    def to_growers(value, shift):
+        route = [
+            (t * groups + g, ((g + shift) % blocks) * groups + t)
+            for t in range(blocks)
+            for g in range(groups)
+        ]
+        return lax.ppermute(value, EVERY, route)
+
+    def to_out_growers(value, shift):
+        route = [
+            (t * groups + g, g * groups + (t + shift) % groups)
+            for t in range(blocks)
+            for g in range(groups)
+        ]
+        return lax.ppermute(value, EVERY, route)
+
     def exchange(value):
         return lax.all_to_all(value, EVERY, split_axis=0, concat_axis=0, tiled=True)
 
@@ -396,27 +396,27 @@
     shrink_in = jnp.transpose(shrink_qkv, (0, 2, 1)).reshape(-1, features)
     rows, rank_part = call(
         functools.partial(rank_kernel, sizes, owned),
-        [shape((count, features)), shape((blocks * groups, packed, lanes))],
+        [shape((count, features)), shape((packed, lanes))],
         [VMEM] * (blocks + 2),
         [pltpu.VMEM((count, features), jnp.float32)],
         2 * count * shrink_qkv.size,
         2 * shrink_qkv.size + 4 * count * features,
     )(*pieces, shrink_in, slots)
-    ranks = exchange(rank_part)
-    total = stream(rows, w_query, 8, [w_key, w_value], [w_out] * 3)
+    ranks = [to_growers(rank_part, shift) for shift in range(blocks)]
+    total = product(rows, w_query, w_key, w_value)
     cols = total.shape[1]
     head_cols = w_query.shape[1]
     query_lines = head_cols // head_size * drafts
     sent = call(
         functools.partial(grow_kernel, sizes, width),
         shape((blocks * groups, lines, head_size)),
-        [VMEM] * 6 + [HBM] * 2,
+        [VMEM] * (5 + groups) + [HBM] * 2,
         [pltpu.VMEM((blocks * groups * lines, head_size), jnp.float32)],
         limit=40 * MIB,
     )(
         total,
         slots,
-        ranks,
+        *ranks,
         *[grow.reshape(owned * width, -1) for grow in (grow_query, grow_key, grow_value)],
         *[w_out] * 2,
     )
@@ -430,21 +430,22 @@
     held = -(-packing(count, width, 128)[1] // 16) * 16
     out_rows, out_part = call(
         functools.partial(out_rank_kernel, sizes, owned),
-        [shape((count, head_cols)), shape((blocks * groups, held, 128))],
-        [VMEM] * 3,
+        [shape((count, head_cols)), shape((held, 128))],
+        [VMEM] * 3 + [HBM] * 4,
         [pltpu.VMEM((blocks * groups * query_lines, head_size), jnp.float32)],
-    )(gathered, jnp.transpose(shrink_out, (0, 2, 1)).reshape(-1, head_cols), slots)
-    out_ranks = exchange(out_part)
-    out_total = stream(out_rows, w_out, 8)
+        limit=40 * MIB,
+    )(gathered, jnp.transpose(shrink_out, (0, 2, 1)).reshape(-1, head_cols), slots, *[w_query] * 4)
+    out_ranks = [to_out_growers(out_part, shift) for shift in range(blocks)]
+    out_total = product(out_rows, w_out)
     out_cols = out_total.shape[1]
     leaving = call(
         functools.partial(out_grow_kernel, sizes, width),
         [shape((drafts, groups, out_cols))] * blocks,
-        [VMEM] * 4,
+        [VMEM] * (3 + blocks),
         [],
         2 * count * owned * width * out_cols,
         8 * count * out_cols + 2 * owned * width * out_cols,
-    )(out_total, slots, out_ranks, grow_out.reshape(owned * width, -1))
+    )(out_total, slots, grow_out.reshape(owned * width, -1), *out_ranks)
     result = leaving[0].astype(jnp.float32)
     for shift in range(1, blocks):
         result = result + over_tensor(leaving[shift], -shift).astype(jnp.float32)

time: 84.9 us -> 77.6 us (0.914)
  Pallas kernels: 20.2 us -> 12.3 us
  starting transfers between devices: 18.6 us -> 20.9 us
  waiting for transfers between devices: 14.3 us -> 12.1 us
  blocking collectives: 26.7 us -> 28.1 us
    all_to_all x2 -> x0, starting transfers between devices: 8.08 us -> none  [exchange(): return lax.all_to_all(value, EVERY, split_axis=0, concat_axis=0, tiled=True)]
    ppermute x0 -> x8, starting transfers between devices: none -> 7.89 us  [the longest x4 4.8 us: to_growers(): return lax.ppermute(value, EVERY, route)]
    pallas_call x2, Pallas kernels: 12.9 us -> 6.31 us  [product(): call(product_kernel, shape((rows.shape[0], width), jnp.float32), [VMEM] *...]
    ppermute x6, starting transfers between devices: 10.5 us -> 13 us  [over_tensor(): return lax.ppermute(value, 'tensor', route)]
    ppermute x6, waiting for transfers between devices: 13.4 us -> 12.1 us  [over_tensor(): return lax.ppermute(value, 'tensor', route)]
    all_to_all x2, blocking collectives: 26.7 us -> 28.1 us  [exchange(): return lax.all_to_all(value, EVERY, split_axis=0, concat_axis=0, tiled=True)]
    unnamed x30 -> x36, local copies, waits for them, and re-layouts: 3.1 us -> 2.35 us
  transfers between devices with their start and end apart: 8 -> 14, of which waited for: 5 -> 3; matrix products, arithmetic and copies ran while one was open for 0% -> 0% of each run, Pallas kernels for 16% -> 9%
where the time goes in v12:
time: 77.6 us; the launch traced here: 77.4 us
  blocking collectives  28.1 us (36%)
  starting transfers between devices  20.9 us (27%)
  Pallas kernels  12.3 us (16%)
  waiting for transfers between devices  12.1 us (16%)
  local copies, waits for them, and re-layouts  2.35 us (3%)
  between operations  0.95 us (1%)
    all_to_all x2, blocking collectives, exchange(): return lax.all_to_all(value, EVERY, split_axis=0, concat_axis=0, tiled=True)  28.1 us
    ppermute x6, starting transfers between devices, over_tensor(): return lax.ppermute(value, 'tensor', route)  13 us
    ppermute x6, waiting for transfers between devices, over_tensor(): return lax.ppermute(value, 'tensor', route)  12.1 us
    pallas_call x2, Pallas kernels, product(): call(product_kernel, shape((rows.shape[0], width), jnp.float32), [VMEM] *...  6.31 us
    ppermute x4, starting transfers between devices, to_growers(): return lax.ppermute(value, EVERY, route)  4.8 us
    ppermute x4, starting transfers between devices, to_out_growers(): return lax.ppermute(value, EVERY, route)  3.09 us
    unnamed x36, local copies, waits for them, and re-layouts  2.35 us
    pallas_call x1, Pallas kernels, by_kernels(): call(functools.partial(attend_kernel, sizes), shape((blocks * groups, que...  1.75 us
  transfers between devices with their start and end apart: 14, of which 3 were waited for; matrix products, arithmetic and copies ran while one was open for 0% of the time, Pallas kernels for 9%

profile of v12, /device:TPU:0, one launch (start us, length us, event | category | flops | bytes accessed | tf_op | source)
XLA Modules:
  0.0 77.4 jit_solution(11157387076109190076)
XLA Ops:
  0.0 5.0 %collective-permute-start.2 = (bf16[3,4,4096]{2,1,0:T(4,128)(2,1)}, bf16[3,4,4096]{2,1,0:T(4,128)(2,1)S(1)}, u32[]{:S(2)}, u32[]{:S(2)}) collective-permute-start(bf16[3,4,4096]{2,1,0:T(4,128)(2,1)} %bitcast.19), channel_id=1, source_target_pairs={{0,12},{4,0},{8,4},{12,8},{1,13},{5,1},{9,5},{13,9},{2,14},{6,2},{... | collective-permute-start | bytes 294920 | tf_op jit(solution)/shard_map/ppermute | solution.py:366
  5.0 0.0 collective-permute-start.1
  5.1 1.0 %collective-permute-start = (bf16[3,4,4096]{2,1,0:T(4,128)(2,1)}, bf16[3,4,4096]{2,1,0:T(4,128)(2,1)S(1)}, u32[]{:S(2)}, u32[]{:S(2)}) collective-permute-start(bf16[3,4,4096]{2,1,0:T(4,128)(2,1)} %bitcast.21), channel_id=1, source_target_pairs={{0,4},{4,8},{8,12},{12,0},{1,5},{5,9},{9,13},{13,1},{2,6},{6,10},{... | collective-permute-start | bytes 294920 | tf_op jit(solution)/shard_map/ppermute | solution.py:366
  6.7 0.6 copy-done.12
  7.4 0.7 copy-done.13
  8.0 0.7 shard_map.154
  8.8 0.0 copy-start.5
  8.8 0.0 copy-start.10
  8.8 0.0 copy-start.11
  8.8 0.0 collective-permute-done.2.refs_3_
  8.8 5.2 %collective-permute-done.1.refs_2_ = bf16[3,4,4096]{2,1,0:T(4,128)(2,1)S(1)} collective-permute-done((bf16[3,4,4096]{2,1,0:T(4,128)(2,1)}, bf16[3,4,4096]{2,1,0:T(4,128)(2,1)S(1)}, u32[]{:S(2)}, u32[]{:S(2)}) %collective-permute-start.1) | collective-permute-done | bytes 98336 | tf_op jit(solution)/shard_map/ppermute | solution.py:366
  14.0 0.0 collective-permute-done.refs_1_
  14.0 1.4 %shard_map.155 = (bf16[48,4096]{1,0:T(8,128)(2,1)S(1)}, bf16[32,128]{1,0:T(8,128)(2,1)S(1)}) custom-call(bf16[3,4,4096]{2,1,0:T(4,128)(2,1)S(1)} %bitcast.22, bf16[3,4,4096]{2,1,0:T(4,128)(2,1)S(1)} %collective-permute-done.refs_1_, bf16[3,4,4096]{2,1,0:T(4,128)(2,1)S(1)} %collective-permute-done.1.refs_2_, ...), custom_call_target="tpu_custom_call" | custom-call | flops 150994944 | bytes 3932160 | tf_op jit(solution)/shard_map/pallas_call | solution.py:397
  15.4 2.0 %collective-permute-start.6 = (bf16[32,128]{1,0:T(8,128)(2,1)S(1)}, bf16[32,128]{1,0:T(8,128)(2,1)S(1)}, u32[]{:S(2)}, u32[]{:S(2)}) collective-permute-start(bf16[32,128]{1,0:T(8,128)(2,1)S(1)} %get-tuple-element.18), channel_id=1, source_target_pairs={{0,12},{1,0},{2,4},{3,8},{4,13},{5,1},{6,5},{7,9},{8,14},{9,2},{10... | collective-permute-start | bytes 24584 | tf_op jit(solution)/shard_map/ppermute | solution.py:374
  17.4 1.5 %collective-permute-start.5 = (bf16[32,128]{1,0:T(8,128)(2,1)S(1)}, bf16[32,128]{1,0:T(8,128)(2,1)S(1)}, u32[]{:S(2)}, u32[]{:S(2)}) collective-permute-start(bf16[32,128]{1,0:T(8,128)(2,1)S(1)} %get-tuple-element.18), channel_id=1, source_target_pairs={{0,8},{1,12},{2,0},{3,4},{4,9},{5,13},{6,1},{7,5},{8,10},{9,14},{1... | collective-permute-start | bytes 24584 | tf_op jit(solution)/shard_map/ppermute | solution.py:374
  18.9 0.7 collective-permute-start.4
  19.6 0.6 collective-permute-start.3
  20.2 0.0 copy-done
  20.2 3.3 %shard_map.156.total_ref = f32[48,2304]{1,0:T(8,128)S(1)} custom-call(bf16[48,4096]{1,0:T(8,128)(2,1)S(1)} %get-tuple-element.17.rows_ref, bf16[4096,2048]{1,0:T(8,128)(2,1)S(1)} %copy-done, bf16[4096,128]{1,0:T(8,128)(2,1)S(1)} %copy-done.2, bf16[4096,128]{1,0:T(8,128)(2,1)S(1)} %copy-done.3), custom_call_target="tpu_custom_call" | custom-call | tf_op jit(solution)/shard_map/pallas_call | solution.py:152
  23.6 0.0 collective-permute-done.6.refs_3_
  23.6 0.0 collective-permute-done.5.refs_2_
  23.6 0.0 collective-permute-done.4.refs_1_
  23.6 0.0 collective-permute-done.3.refs_0_
  23.6 0.0 copy-start.7
  23.6 0.0 copy-start.8
  23.7 0.0 copy-start.6
  23.7 0.9 %shard_map.157 = bf16[16,56,128]{2,1,0:T(8,128)(2,1)S(1)} custom-call(f32[48,2304]{1,0:T(8,128)S(1)} %shard_map.156.total_ref, s32[48,128]{1,0:T(8,128)S(1)} %get-tuple-element.16.refs_5_.slots_ref, bf16[32,128]{1,0:T(8,128)(2,1)S(1)} %collective-permute-done.3.refs_0_, bf16[32,128]{1,0:T(8,128)(2,1)S(1)} %collective-permute-done.4.refs_1_, ...), custom_call_target="tpu_custom_call" | custom-call | tf_op jit(solution)/shard_map/pallas_call | solution.py:410
  24.6 16.4 %all_to_all.10.arrived_ref = bf16[16,56,128]{2,1,0:T(8,128)(2,1)S(1)} all-to-all(bf16[16,56,128]{2,1,0:T(8,128)(2,1)S(1)} %shard_map.157), channel_id=1, replica_groups=mesh['parts'=2,'tensor'=4,'dp'=2,'pipe'=2] {'tensor','dp','pipe'}, dimensions={0} | all-to-all | bytes 458752 | tf_op jit(solution)/shard_map/all_to_all | solution.py:385
  41.0 1.8 %shard_map.158 = bf16[16,48,128]{2,1,0:T(8,128)(2,1)S(1)} custom-call(bf16[16,56,128]{2,1,0:T(8,128)(2,1)S(1)} %all_to_all.10.arrived_ref, bf16[1,4,512,128]{3,2,1,0:T(8,128)(2,1)S(1)} %copy-done.7, bf16[1,4,512,128]{3,2,1,0:T(8,128)(2,1)S(1)} %copy-done.8, s32[1]{0:T(128)S(6)} %copy.17.length_ref, f32[56,128]{1,0:T(8,128)S(1)} %get-tuple-element.19.cosine_ref, ...), custom_call_target="tpu_custom_call" | custom-call | tf_op jit(solution)/shard_map/pallas_call | solution.py:423
  42.8 11.6 %all_to_all.11.got_ref = bf16[16,48,128]{2,1,0:T(8,128)(2,1)S(1)} all-to-all(bf16[16,48,128]{2,1,0:T(8,128)(2,1)S(1)} %shard_map.158), channel_id=1, replica_groups=mesh['parts'=2,'tensor'=4,'dp'=2,'pipe'=2] {'tensor','dp','pipe'}, dimensions={0} | all-to-all | bytes 393216 | tf_op jit(solution)/shard_map/all_to_all | solution.py:385
  54.4 0.6 shard_map.159
  55.0 0.0 collective-permute-start.10
  55.0 0.6 collective-permute-start.9
  55.6 1.7 %collective-permute-start.8 = (bf16[16,128]{1,0:T(8,128)(2,1)S(1)}, bf16[16,128]{1,0:T(8,128)(2,1)S(1)}, u32[]{:S(2)}, u32[]{:S(2)}) collective-permute-start(bf16[16,128]{1,0:T(8,128)(2,1)S(1)} %get-tuple-element.22), channel_id=1, source_target_pairs={{0,1},{1,5},{2,9},{3,13},{4,2},{5,6},{6,10},{7,14},{8,3},{9,7},{10... | collective-permute-start | bytes 12296 | tf_op jit(solution)/shard_map/ppermute | solution.py:382
  57.3 0.8 %collective-permute-start.7 = (bf16[16,128]{1,0:T(8,128)(2,1)S(1)}, bf16[16,128]{1,0:T(8,128)(2,1)S(1)}, u32[]{:S(2)}, u32[]{:S(2)}) collective-permute-start(bf16[16,128]{1,0:T(8,128)(2,1)S(1)} %get-tuple-element.22), channel_id=1, source_target_pairs={{0,0},{1,4},{2,8},{3,12},{4,1},{5,5},{6,9},{7,13},{8,2},{9,6},{10,... | collective-permute-start | bytes 12296 | tf_op jit(solution)/shard_map/ppermute | solution.py:382
  58.1 1.0 %slice-done.3 = s8[4194304]{0:T(1024)(128)(4,1)S(1)} async-done(((s8[16777216]{0:T(1024)(128)(4,1)}), s8[4194304]{0:T(1024)(128)(4,1)S(1)}, s32[]{:S(2)}) %slice-start.3) | async-done | bytes 4194328
  59.1 3.0 %shard_map.160.total_ref = f32[48,4096]{1,0:T(8,128)S(1)} custom-call(bf16[48,2048]{1,0:T(8,128)(2,1)S(1)} %get-tuple-element.21.rows_ref, bf16[2048,4096]{1,0:T(8,128)(2,1)S(1)} %bitcast.14), custom_call_target="tpu_custom_call" | custom-call | tf_op jit(solution)/shard_map/pallas_call | solution.py:152
  62.1 0.0 collective-permute-done.10.refs_3_
  62.1 0.0 collective-permute-done.9.refs_2_
  62.1 0.0 collective-permute-done.8.refs_1_
  62.1 0.0 collective-permute-done.7.refs_0_
  62.2 0.6 shard_map.161
  62.8 4.9 %collective-permute-start.11 = (bf16[3,4,4096]{2,1,0:T(4,128)(2,1)S(1)}, bf16[3,4,4096]{2,1,0:T(4,128)(2,1)S(1)}, u32[]{:S(2)}, u32[]{:S(2)}) collective-permute-start(bf16[3,4,4096]{2,1,0:T(4,128)(2,1)S(1)} %get-tuple-element.24), channel_id=1, source_target_pairs={{0,12},{4,0},{8,4},{12,8},{1,13},{5,1},{9,5},{13,9},{2,14},{6,2},{... | collective-permute-start | bytes 294920 | tf_op jit(solution)/shard_map/ppermute | solution.py:366
  67.7 0.1 collective-permute-start.12
  67.8 1.9 %collective-permute-start.13 = (bf16[3,4,4096]{2,1,0:T(4,128)(2,1)S(1)}, bf16[3,4,4096]{2,1,0:T(4,128)(2,1)S(1)}, u32[]{:S(2)}, u32[]{:S(2)}) collective-permute-start(bf16[3,4,4096]{2,1,0:T(4,128)(2,1)S(1)} %get-tuple-element.26), channel_id=1, source_target_pairs={{0,4},{4,8},{8,12},{12,0},{1,5},{5,9},{9,13},{13,1},{2,6},{6,10},{... | collective-permute-start | bytes 294920 | tf_op jit(solution)/shard_map/ppermute | solution.py:366
  69.8 1.2 %collective-permute-done.11 = bf16[3,4,4096]{2,1,0:T(4,128)(2,1)S(1)} collective-permute-done((bf16[3,4,4096]{2,1,0:T(4,128)(2,1)S(1)}, bf16[3,4,4096]{2,1,0:T(4,128)(2,1)S(1)}, u32[]{:S(2)}, u32[]{:S(2)}) %collective-permute-start.11) | collective-permute-done | bytes 98336 | tf_op jit(solution)/shard_map/ppermute | solution.py:366
  70.9 5.7 %collective-permute-done.12 = bf16[3,4,4096]{2,1,0:T(4,128)(2,1)S(1)} collective-permute-done((bf16[3,4,4096]{2,1,0:T(4,128)(2,1)S(1)}, bf16[3,4,4096]{2,1,0:T(4,128)(2,1)S(1)}, u32[]{:S(2)}, u32[]{:S(2)}) %collective-permute-start.12) | collective-permute-done | bytes 98336 | tf_op jit(solution)/shard_map/ppermute | solution.py:366
  76.7 0.7 fusion
  (28 shorter events, 0.1 us)
Async XLA Ops:
  0.0 8.8 %collective-permute-start.2 = (bf16[3,4,4096]{2,1,0:T(4,128)(2,1)}, bf16[3,4,4096]{2,1,0:T(4,128)(2,1)S(1)}, u32[]{:S(2)}, u32[]{:S(2)}) collective-permute-start(bf16[3,4,4096]{2,1,0:T(4,128)(2,1)} %bitcast.19), channel_id=1, source_target_pairs={{0,12},{4,0},{8,4},{12,8},{1,13},{5,1},{9,5},{13,9},{2,14},{6,2},{... | collective-permute-start | bytes 294920 | tf_op jit(solution)/shard_map/ppermute | solution.py:366
  5.0 9.0 %collective-permute-start.1 = (bf16[3,4,4096]{2,1,0:T(4,128)(2,1)}, bf16[3,4,4096]{2,1,0:T(4,128)(2,1)S(1)}, u32[]{:S(2)}, u32[]{:S(2)}) collective-permute-start(bf16[3,4,4096]{2,1,0:T(4,128)(2,1)} %bitcast.20), channel_id=1, source_target_pairs={{0,8},{4,12},{8,0},{12,4},{1,9},{5,13},{9,1},{13,5},{2,10},{6,14},... | collective-permute-start | bytes 294920 | tf_op jit(solution)/shard_map/ppermute | solution.py:366
  5.1 9.0 %collective-permute-start = (bf16[3,4,4096]{2,1,0:T(4,128)(2,1)}, bf16[3,4,4096]{2,1,0:T(4,128)(2,1)S(1)}, u32[]{:S(2)}, u32[]{:S(2)}) collective-permute-start(bf16[3,4,4096]{2,1,0:T(4,128)(2,1)} %bitcast.21), channel_id=1, source_target_pairs={{0,4},{4,8},{8,12},{12,0},{1,5},{5,9},{9,13},{13,1},{2,6},{6,10},{... | collective-permute-start | bytes 294920 | tf_op jit(solution)/shard_map/ppermute | solution.py:366
  6.7 0.7 copy-start.12
  7.4 0.7 copy-start.13
  8.0 6.0 %copy-start.1 = (bf16[4,4096,96]{1,2,0:T(8,128)(2,1)S(1)}, bf16[4,4096,96]{1,2,0:T(8,128)(2,1)}, u32[]{:S(2)}) copy-start(bf16[4,4096,96]{1,2,0:T(8,128)(2,1)} %param.21) | copy-start | bytes 9437188
  8.0 6.0 %copy-start.9 = (bf16[4,3,4096]{2,0,1:T(4,128)(2,1)S(1)}, bf16[4,3,4096]{2,0,1:T(4,128)(2,1)}, u32[]{:S(2)}) copy-start(bf16[4,3,4096]{2,0,1:T(4,128)(2,1)} %param.16) | copy-start | bytes 294916
  8.0 12.2 %copy-start = (bf16[4096,2048]{1,0:T(8,128)(2,1)S(1)}, bf16[4096,2048]{1,0:T(8,128)(2,1)}, u32[]{:S(2)}) copy-start(bf16[4096,2048]{1,0:T(8,128)(2,1)} %refs_3_.1) | copy-start | bytes 50331652
  8.0 12.2 %copy-start.2 = (bf16[4096,128]{1,0:T(8,128)(2,1)S(1)}, bf16[4096,128]{1,0:T(8,128)(2,1)}, u32[]{:S(2)}) copy-start(bf16[4096,128]{1,0:T(8,128)(2,1)} %refs_1_.4) | copy-start | bytes 3145732
  8.0 12.2 %copy-start.3 = (bf16[4096,128]{1,0:T(8,128)(2,1)S(1)}, bf16[4096,128]{1,0:T(8,128)(2,1)}, u32[]{:S(2)}) copy-start(bf16[4096,128]{1,0:T(8,128)(2,1)} %refs_2_.4) | copy-start | bytes 3145732
  8.8 14.8 %copy-start.5 = (bf16[4,32,2048]{2,1,0:T(8,128)(2,1)S(1)}, bf16[4,32,2048]{2,1,0:T(8,128)(2,1)}, u32[]{:S(2)}) copy-start(bf16[4,32,2048]{2,1,0:T(8,128)(2,1)} %param.22) | copy-start | bytes 1572868
  8.8 14.8 %copy-start.10 = (bf16[4,32,128]{2,1,0:T(8,128)(2,1)S(1)}, bf16[4,32,128]{2,1,0:T(8,128)(2,1)}, u32[]{:S(2)}) copy-start(bf16[4,32,128]{2,1,0:T(8,128)(2,1)} %param.23) | copy-start | bytes 98308
  8.8 14.8 %copy-start.11 = (bf16[4,32,128]{2,1,0:T(8,128)(2,1)S(1)}, bf16[4,32,128]{2,1,0:T(8,128)(2,1)}, u32[]{:S(2)}) copy-start(bf16[4,32,128]{2,1,0:T(8,128)(2,1)} %param.24) | copy-start | bytes 98308
  15.4 8.2 %collective-permute-start.6 = (bf16[32,128]{1,0:T(8,128)(2,1)S(1)}, bf16[32,128]{1,0:T(8,128)(2,1)S(1)}, u32[]{:S(2)}, u32[]{:S(2)}) collective-permute-start(bf16[32,128]{1,0:T(8,128)(2,1)S(1)} %get-tuple-element.18), channel_id=1, source_target_pairs={{0,12},{1,0},{2,4},{3,8},{4,13},{5,1},{6,5},{7,9},{8,14},{9,2},{10... | collective-permute-start | bytes 24584 | tf_op jit(solution)/shard_map/ppermute | solution.py:374
  17.4 6.2 %collective-permute-start.5 = (bf16[32,128]{1,0:T(8,128)(2,1)S(1)}, bf16[32,128]{1,0:T(8,128)(2,1)S(1)}, u32[]{:S(2)}, u32[]{:S(2)}) collective-permute-start(bf16[32,128]{1,0:T(8,128)(2,1)S(1)} %get-tuple-element.18), channel_id=1, source_target_pairs={{0,8},{1,12},{2,0},{3,4},{4,9},{5,13},{6,1},{7,5},{8,10},{9,14},{1... | collective-permute-start | bytes 24584 | tf_op jit(solution)/shard_map/ppermute | solution.py:374
  18.9 4.7 %collective-permute-start.4 = (bf16[32,128]{1,0:T(8,128)(2,1)S(1)}, bf16[32,128]{1,0:T(8,128)(2,1)S(1)}, u32[]{:S(2)}, u32[]{:S(2)}) collective-permute-start(bf16[32,128]{1,0:T(8,128)(2,1)S(1)} %get-tuple-element.18), channel_id=1, source_target_pairs={{0,4},{1,8},{2,12},{3,0},{4,5},{5,9},{6,13},{7,1},{8,6},{9,10},{10... | collective-permute-start | bytes 24584 | tf_op jit(solution)/shard_map/ppermute | solution.py:374
  19.6 4.0 %collective-permute-start.3 = (bf16[32,128]{1,0:T(8,128)(2,1)S(1)}, bf16[32,128]{1,0:T(8,128)(2,1)S(1)}, u32[]{:S(2)}, u32[]{:S(2)}) collective-permute-start(bf16[32,128]{1,0:T(8,128)(2,1)S(1)} %get-tuple-element.18), channel_id=1, source_target_pairs={{0,0},{1,4},{2,8},{3,12},{4,1},{5,5},{6,9},{7,13},{8,2},{9,6},{10,... | collective-permute-start | bytes 24584 | tf_op jit(solution)/shard_map/ppermute | solution.py:374
  23.6 17.4 %copy-start.7 = (bf16[1,4,512,128]{3,2,1,0:T(8,128)(2,1)S(1)}, bf16[1,4,512,128]{3,2,1,0:T(8,128)(2,1)}, u32[]{:S(2)}) copy-start(bf16[1,4,512,128]{3,2,1,0:T(8,128)(2,1)} %keys_ref.1) | copy-start | bytes 1572868
  23.6 17.4 %copy-start.8 = (bf16[1,4,512,128]{3,2,1,0:T(8,128)(2,1)S(1)}, bf16[1,4,512,128]{3,2,1,0:T(8,128)(2,1)}, u32[]{:S(2)}) copy-start(bf16[1,4,512,128]{3,2,1,0:T(8,128)(2,1)} %values_ref.1) | copy-start | bytes 1572868
  23.7 30.8 %copy-start.6 = (bf16[4,2048,32]{1,2,0:T(8,128)(2,1)S(1)}, bf16[4,2048,32]{1,2,0:T(8,128)(2,1)}, u32[]{:S(2)}) copy-start(bf16[4,2048,32]{1,2,0:T(8,128)(2,1)} %param.25) | copy-start | bytes 1572868
  41.0 17.1 %slice-start = ((s8[16777216]{0:T(1024)(128)(4,1)}), s8[4194304]{0:T(1024)(128)(4,1)S(1)}, s32[]{:S(2)}) async-start(s8[16777216]{0:T(1024)(128)(4,1)} %bitcast.13), calls=%async_computation.2 | async-start | bytes 8388608
  54.4 3.7 %slice-start.1 = ((s8[16777216]{0:T(1024)(128)(4,1)}), s8[4194304]{0:T(1024)(128)(4,1)S(1)}, s32[]{:S(2)}) async-start(s8[16777216]{0:T(1024)(128)(4,1)} %bitcast.13), calls=%async_computation.3 | async-start | bytes 8388608
  54.4 3.7 %slice-start.2 = ((s8[16777216]{0:T(1024)(128)(4,1)}), s8[4194304]{0:T(1024)(128)(4,1)S(1)}, s32[]{:S(2)}) async-start(s8[16777216]{0:T(1024)(128)(4,1)} %bitcast.13), calls=%async_computation.4 | async-start | bytes 8388608
  54.4 4.7 %slice-start.3 = ((s8[16777216]{0:T(1024)(128)(4,1)}), s8[4194304]{0:T(1024)(128)(4,1)S(1)}, s32[]{:S(2)}) async-start(s8[16777216]{0:T(1024)(128)(4,1)} %bitcast.13), calls=%async_computation.5 | async-start | bytes 8388608
  55.0 7.2 %copy-start.4 = (bf16[4,32,4096]{2,1,0:T(8,128)(2,1)S(1)}, bf16[4,32,4096]{2,1,0:T(8,128)(2,1)}, u32[]{:S(2)}) copy-start(bf16[4,32,4096]{2,1,0:T(8,128)(2,1)} %param.26) | copy-start | bytes 3145732
  55.0 7.1 %collective-permute-start.10 = (bf16[16,128]{1,0:T(8,128)(2,1)S(1)}, bf16[16,128]{1,0:T(8,128)(2,1)S(1)}, u32[]{:S(2)}, u32[]{:S(2)}) collective-permute-start(bf16[16,128]{1,0:T(8,128)(2,1)S(1)} %get-tuple-element.22), channel_id=1, source_target_pairs={{0,3},{1,7},{2,11},{3,15},{4,0},{5,4},{6,8},{7,12},{8,1},{9,5},{10... | collective-permute-start | bytes 12296 | tf_op jit(solution)/shard_map/ppermute | solution.py:382
  55.0 7.1 %collective-permute-start.9 = (bf16[16,128]{1,0:T(8,128)(2,1)S(1)}, bf16[16,128]{1,0:T(8,128)(2,1)S(1)}, u32[]{:S(2)}, u32[]{:S(2)}) collective-permute-start(bf16[16,128]{1,0:T(8,128)(2,1)S(1)} %get-tuple-element.22), channel_id=1, source_target_pairs={{0,2},{1,6},{2,10},{3,14},{4,3},{5,7},{6,11},{7,15},{8,0},{9,4},{1... | collective-permute-start | bytes 12296 | tf_op jit(solution)/shard_map/ppermute | solution.py:382
  55.6 6.5 %collective-permute-start.8 = (bf16[16,128]{1,0:T(8,128)(2,1)S(1)}, bf16[16,128]{1,0:T(8,128)(2,1)S(1)}, u32[]{:S(2)}, u32[]{:S(2)}) collective-permute-start(bf16[16,128]{1,0:T(8,128)(2,1)S(1)} %get-tuple-element.22), channel_id=1, source_target_pairs={{0,1},{1,5},{2,9},{3,13},{4,2},{5,6},{6,10},{7,14},{8,3},{9,7},{10... | collective-permute-start | bytes 12296 | tf_op jit(solution)/shard_map/ppermute | solution.py:382
  57.3 4.8 %collective-permute-start.7 = (bf16[16,128]{1,0:T(8,128)(2,1)S(1)}, bf16[16,128]{1,0:T(8,128)(2,1)S(1)}, u32[]{:S(2)}, u32[]{:S(2)}) collective-permute-start(bf16[16,128]{1,0:T(8,128)(2,1)S(1)} %get-tuple-element.22), channel_id=1, source_target_pairs={{0,0},{1,4},{2,8},{3,12},{4,1},{5,5},{6,9},{7,13},{8,2},{9,6},{10,... | collective-permute-start | bytes 12296 | tf_op jit(solution)/shard_map/ppermute | solution.py:382
  62.8 8.1 %collective-permute-start.11 = (bf16[3,4,4096]{2,1,0:T(4,128)(2,1)S(1)}, bf16[3,4,4096]{2,1,0:T(4,128)(2,1)S(1)}, u32[]{:S(2)}, u32[]{:S(2)}) collective-permute-start(bf16[3,4,4096]{2,1,0:T(4,128)(2,1)S(1)} %get-tuple-element.24), channel_id=1, source_target_pairs={{0,12},{4,0},{8,4},{12,8},{1,13},{5,1},{9,5},{13,9},{2,14},{6,2},{... | collective-permute-start | bytes 294920 | tf_op jit(solution)/shard_map/ppermute | solution.py:366
  67.7 9.0 %collective-permute-start.12 = (bf16[3,4,4096]{2,1,0:T(4,128)(2,1)S(1)}, bf16[3,4,4096]{2,1,0:T(4,128)(2,1)S(1)}, u32[]{:S(2)}, u32[]{:S(2)}) collective-permute-start(bf16[3,4,4096]{2,1,0:T(4,128)(2,1)S(1)} %get-tuple-element.25), channel_id=1, source_target_pairs={{0,8},{4,12},{8,0},{12,4},{1,9},{5,13},{9,1},{13,5},{2,10},{6,14},... | collective-permute-start | bytes 294920 | tf_op jit(solution)/shard_map/ppermute | solution.py:366
  67.8 8.8 %collective-permute-start.13 = (bf16[3,4,4096]{2,1,0:T(4,128)(2,1)S(1)}, bf16[3,4,4096]{2,1,0:T(4,128)(2,1)S(1)}, u32[]{:S(2)}, u32[]{:S(2)}) collective-permute-start(bf16[3,4,4096]{2,1,0:T(4,128)(2,1)S(1)} %get-tuple-element.26), channel_id=1, source_target_pairs={{0,4},{4,8},{8,12},{12,0},{1,5},{5,9},{9,13},{13,1},{2,6},{6,10},{... | collective-permute-start | bytes 294920 | tf_op jit(solution)/shard_map/ppermute | solution.py:366

commit v13 on v12

--- a/solution.py
+++ b/solution.py
@@ -73,15 +73,15 @@
     return group, rest_of(left, blocks), over(left, blocks)
 
 
-def turned(block, blocks):
-    return rest_of(lax.axis_index("tensor") - block + blocks, blocks)
+def turned(block):
+    return lax.axis_index("tensor") ^ block
 
 
 def reorder(sizes, after, before):
     groups, blocks, drafts = sizes
     rows = groups * blocks * drafts
     group, block, draft = parts_of(after, sizes, iota((rows, rows), 0))
-    wanted = before(sizes, group, turned(block, blocks), draft)
+    wanted = before(sizes, group, turned(block), draft)
     return jnp.where(wanted == iota((rows, rows), 1), 1.0, 0.0).astype(jnp.bfloat16)
 
 
@@ -171,7 +171,7 @@
     near = parts_of(as_gathered, sizes, index)
     far = parts_of(by_draft, sizes, index)
     row_group = jnp.where(column == 1, far[0], near[0])
-    row_block = jnp.where(column == 1, far[1], turned(near[1], blocks))
+    row_block = jnp.where(column == 1, far[1], turned(near[1]))
     place = row_block * groups + row_group
     slots = jnp.zeros(slots_ref.shape, jnp.int32)
     sent, taken = 0, 0
@@ -362,7 +362,7 @@
     lanes = -(-shrink_qkv.shape[2] // 128) * 128
 
     def over_tensor(value, shift):
-        route = [(t, (t + shift) % blocks) for t in range(blocks)]
+        route = [(t, t ^ shift) for t in range(blocks)]
         return lax.ppermute(value, "tensor", route)
 
     def to_growers(value, shift):
@@ -448,7 +448,7 @@
     )(out_total, slots, grow_out.reshape(owned * width, -1), *out_ranks)
     result = leaving[0].astype(jnp.float32)
     for shift in range(1, blocks):
-        result = result + over_tensor(leaving[shift], -shift).astype(jnp.float32)
+        result = result + over_tensor(leaving[shift], shift).astype(jnp.float32)
     return jnp.transpose(result.astype(jnp.bfloat16), (1, 0, 2))
 
 
@@ -639,7 +639,8 @@
 
 def local(*arrays):
     heads = arrays[11].shape[1]
-    if heads == lax.axis_size("tensor") == lax.axis_size(GROUP):
+    paired = heads & (heads - 1) == 0
+    if paired and heads == lax.axis_size("tensor") == lax.axis_size(GROUP):
         return by_kernels(*arrays)
     return by_row(*arrays)
 

time: 77.6 us -> 76.9 us (level)
  starting transfers between devices: 20.9 us -> 19.9 us
    ppermute x6, starting transfers between devices: 13 us -> 12.1 us  [over_tensor(): return lax.ppermute(value, 'tensor', route)]
where the time goes in v13:
time: 76.9 us; the launch traced here: 76.6 us
  blocking collectives  28.4 us (37%)
  starting transfers between devices  19.9 us (26%)
  Pallas kernels  12.3 us (16%)
  waiting for transfers between devices  11.9 us (15%)
  local copies, waits for them, and re-layouts  2.35 us (3%)
  between operations  0.94 us (1%)
    all_to_all x2, blocking collectives, exchange(): return lax.all_to_all(value, EVERY, split_axis=0, concat_axis=0, tiled=True)  28.4 us
    ppermute x6, starting transfers between devices, over_tensor(): return lax.ppermute(value, 'tensor', route)  12.1 us
    ppermute x6, waiting for transfers between devices, over_tensor(): return lax.ppermute(value, 'tensor', route)  11.9 us
    pallas_call x2, Pallas kernels, product(): call(product_kernel, shape((rows.shape[0], width), jnp.float32), [VMEM] *...  6.31 us
    ppermute x4, starting transfers between devices, to_growers(): return lax.ppermute(value, EVERY, route)  4.8 us
    ppermute x4, starting transfers between devices, to_out_growers(): return lax.ppermute(value, EVERY, route)  3.09 us
    unnamed x36, local copies, waits for them, and re-layouts  2.35 us
    pallas_call x1, Pallas kernels, by_kernels(): call(functools.partial(attend_kernel, sizes), shape((blocks * groups, que...  1.75 us
  transfers between devices with their start and end apart: 14, of which 3 were waited for; matrix products, arithmetic and copies ran while one was open for 0% of the time, Pallas kernels for 9%

profile of v13, /device:TPU:0, one launch (start us, length us, event | category | flops | bytes accessed | tf_op | source)
XLA Modules:
  0.0 76.6 jit_solution(15852619164309870818)
XLA Ops:
  0.0 5.0 %collective-permute-start.2 = (bf16[3,4,4096]{2,1,0:T(4,128)(2,1)}, bf16[3,4,4096]{2,1,0:T(4,128)(2,1)S(1)}, u32[]{:S(2)}, u32[]{:S(2)}) collective-permute-start(bf16[3,4,4096]{2,1,0:T(4,128)(2,1)} %bitcast.19), channel_id=1, source_target_pairs={{0,12},{4,8},{8,4},{12,0},{1,13},{5,9},{9,5},{13,1},{2,14},{6,10},... | collective-permute-start | bytes 294920 | tf_op jit(solution)/shard_map/ppermute | solution.py:366
  5.0 0.0 collective-permute-start.1
  5.1 0.6 collective-permute-start
  6.3 0.6 copy-done.12
  6.9 0.7 copy-done.13
  7.6 0.7 shard_map.154
  8.3 0.0 copy-start.5
  8.4 0.0 copy-start.10
  8.4 0.0 copy-start.11
  8.4 0.6 collective-permute-done.2.refs_3_
  9.0 4.6 %collective-permute-done.1.refs_2_ = bf16[3,4,4096]{2,1,0:T(4,128)(2,1)S(1)} collective-permute-done((bf16[3,4,4096]{2,1,0:T(4,128)(2,1)}, bf16[3,4,4096]{2,1,0:T(4,128)(2,1)S(1)}, u32[]{:S(2)}, u32[]{:S(2)}) %collective-permute-start.1) | collective-permute-done | bytes 98336 | tf_op jit(solution)/shard_map/ppermute | solution.py:366
  13.5 0.0 collective-permute-done.refs_1_
  13.5 1.4 %shard_map.155 = (bf16[48,4096]{1,0:T(8,128)(2,1)S(1)}, bf16[32,128]{1,0:T(8,128)(2,1)S(1)}) custom-call(bf16[3,4,4096]{2,1,0:T(4,128)(2,1)S(1)} %bitcast.22, bf16[3,4,4096]{2,1,0:T(4,128)(2,1)S(1)} %collective-permute-done.refs_1_, bf16[3,4,4096]{2,1,0:T(4,128)(2,1)S(1)} %collective-permute-done.1.refs_2_, ...), custom_call_target="tpu_custom_call" | custom-call | flops 150994944 | bytes 3932160 | tf_op jit(solution)/shard_map/pallas_call | solution.py:397
  14.9 2.5 %collective-permute-start.6 = (bf16[32,128]{1,0:T(8,128)(2,1)S(1)}, bf16[32,128]{1,0:T(8,128)(2,1)S(1)}, u32[]{:S(2)}, u32[]{:S(2)}) collective-permute-start(bf16[32,128]{1,0:T(8,128)(2,1)S(1)} %get-tuple-element.18), channel_id=1, source_target_pairs={{0,12},{1,0},{2,4},{3,8},{4,13},{5,1},{6,5},{7,9},{8,14},{9,2},{10... | collective-permute-start | bytes 24584 | tf_op jit(solution)/shard_map/ppermute | solution.py:374
  17.4 1.5 %collective-permute-start.5 = (bf16[32,128]{1,0:T(8,128)(2,1)S(1)}, bf16[32,128]{1,0:T(8,128)(2,1)S(1)}, u32[]{:S(2)}, u32[]{:S(2)}) collective-permute-start(bf16[32,128]{1,0:T(8,128)(2,1)S(1)} %get-tuple-element.18), channel_id=1, source_target_pairs={{0,8},{1,12},{2,0},{3,4},{4,9},{5,13},{6,1},{7,5},{8,10},{9,14},{1... | collective-permute-start | bytes 24584 | tf_op jit(solution)/shard_map/ppermute | solution.py:374
  18.9 0.2 collective-permute-start.4
  19.1 0.6 collective-permute-start.3
  19.7 0.0 copy-done
  19.8 3.3 %shard_map.156.total_ref = f32[48,2304]{1,0:T(8,128)S(1)} custom-call(bf16[48,4096]{1,0:T(8,128)(2,1)S(1)} %get-tuple-element.17.rows_ref, bf16[4096,2048]{1,0:T(8,128)(2,1)S(1)} %copy-done, bf16[4096,128]{1,0:T(8,128)(2,1)S(1)} %copy-done.2, bf16[4096,128]{1,0:T(8,128)(2,1)S(1)} %copy-done.3), custom_call_target="tpu_custom_call" | custom-call | tf_op jit(solution)/shard_map/pallas_call | solution.py:152
  23.1 0.0 collective-permute-done.6.refs_3_
  23.1 0.0 collective-permute-done.5.refs_2_
  23.1 0.0 collective-permute-done.4.refs_1_
  23.1 0.0 collective-permute-done.3.refs_0_
  23.2 0.0 copy-start.7
  23.2 0.0 copy-start.8
  23.2 0.0 copy-start.6
  23.2 0.9 %shard_map.157 = bf16[16,56,128]{2,1,0:T(8,128)(2,1)S(1)} custom-call(f32[48,2304]{1,0:T(8,128)S(1)} %shard_map.156.total_ref, s32[48,128]{1,0:T(8,128)S(1)} %get-tuple-element.16.refs_5_.slots_ref, bf16[32,128]{1,0:T(8,128)(2,1)S(1)} %collective-permute-done.3.refs_0_, bf16[32,128]{1,0:T(8,128)(2,1)S(1)} %collective-permute-done.4.refs_1_, ...), custom_call_target="tpu_custom_call" | custom-call | tf_op jit(solution)/shard_map/pallas_call | solution.py:410
  24.1 16.8 %all_to_all.10.arrived_ref = bf16[16,56,128]{2,1,0:T(8,128)(2,1)S(1)} all-to-all(bf16[16,56,128]{2,1,0:T(8,128)(2,1)S(1)} %shard_map.157), channel_id=1, replica_groups=mesh['parts'=2,'tensor'=4,'dp'=2,'pipe'=2] {'tensor','dp','pipe'}, dimensions={0} | all-to-all | bytes 458752 | tf_op jit(solution)/shard_map/all_to_all | solution.py:385
  40.9 1.8 %shard_map.158 = bf16[16,48,128]{2,1,0:T(8,128)(2,1)S(1)} custom-call(bf16[16,56,128]{2,1,0:T(8,128)(2,1)S(1)} %all_to_all.10.arrived_ref, bf16[1,4,512,128]{3,2,1,0:T(8,128)(2,1)S(1)} %copy-done.7, bf16[1,4,512,128]{3,2,1,0:T(8,128)(2,1)S(1)} %copy-done.8, s32[1]{0:T(128)S(6)} %copy.17.length_ref, f32[56,128]{1,0:T(8,128)S(1)} %get-tuple-element.19.cosine_ref, ...), custom_call_target="tpu_custom_call" | custom-call | tf_op jit(solution)/shard_map/pallas_call | solution.py:423
  42.7 11.6 %all_to_all.11.got_ref = bf16[16,48,128]{2,1,0:T(8,128)(2,1)S(1)} all-to-all(bf16[16,48,128]{2,1,0:T(8,128)(2,1)S(1)} %shard_map.158), channel_id=1, replica_groups=mesh['parts'=2,'tensor'=4,'dp'=2,'pipe'=2] {'tensor','dp','pipe'}, dimensions={0} | all-to-all | bytes 393216 | tf_op jit(solution)/shard_map/all_to_all | solution.py:385
  54.3 0.6 shard_map.159
  54.9 0.0 collective-permute-start.10
  54.9 0.6 collective-permute-start.9
  55.5 1.7 %collective-permute-start.8 = (bf16[16,128]{1,0:T(8,128)(2,1)S(1)}, bf16[16,128]{1,0:T(8,128)(2,1)S(1)}, u32[]{:S(2)}, u32[]{:S(2)}) collective-permute-start(bf16[16,128]{1,0:T(8,128)(2,1)S(1)} %get-tuple-element.22), channel_id=1, source_target_pairs={{0,1},{1,5},{2,9},{3,13},{4,2},{5,6},{6,10},{7,14},{8,3},{9,7},{10... | collective-permute-start | bytes 12296 | tf_op jit(solution)/shard_map/ppermute | solution.py:382
  57.2 0.8 %collective-permute-start.7 = (bf16[16,128]{1,0:T(8,128)(2,1)S(1)}, bf16[16,128]{1,0:T(8,128)(2,1)S(1)}, u32[]{:S(2)}, u32[]{:S(2)}) collective-permute-start(bf16[16,128]{1,0:T(8,128)(2,1)S(1)} %get-tuple-element.22), channel_id=1, source_target_pairs={{0,0},{1,4},{2,8},{3,12},{4,1},{5,5},{6,9},{7,13},{8,2},{9,6},{10,... | collective-permute-start | bytes 12296 | tf_op jit(solution)/shard_map/ppermute | solution.py:382
  58.0 1.0 %slice-done.3 = s8[4194304]{0:T(1024)(128)(4,1)S(1)} async-done(((s8[16777216]{0:T(1024)(128)(4,1)}), s8[4194304]{0:T(1024)(128)(4,1)S(1)}, s32[]{:S(2)}) %slice-start.3) | async-done | bytes 4194328
  59.0 3.0 %shard_map.160.total_ref = f32[48,4096]{1,0:T(8,128)S(1)} custom-call(bf16[48,2048]{1,0:T(8,128)(2,1)S(1)} %get-tuple-element.21.rows_ref, bf16[2048,4096]{1,0:T(8,128)(2,1)S(1)} %bitcast.14), custom_call_target="tpu_custom_call" | custom-call | tf_op jit(solution)/shard_map/pallas_call | solution.py:152
  62.0 0.0 collective-permute-done.10.refs_3_
  62.0 0.0 collective-permute-done.9.refs_2_
  62.0 0.0 collective-permute-done.8.refs_1_
  62.0 0.0 collective-permute-done.7.refs_0_
  62.0 0.6 shard_map.161
  62.7 2.1 %collective-permute-start.11 = (bf16[3,4,4096]{2,1,0:T(4,128)(2,1)S(1)}, bf16[3,4,4096]{2,1,0:T(4,128)(2,1)S(1)}, u32[]{:S(2)}, u32[]{:S(2)}) collective-permute-start(bf16[3,4,4096]{2,1,0:T(4,128)(2,1)S(1)} %get-tuple-element.24), channel_id=1, source_target_pairs={{0,4},{4,0},{8,12},{12,8},{1,5},{5,1},{9,13},{13,9},{2,6},{6,2},{1... | collective-permute-start | bytes 294920 | tf_op jit(solution)/shard_map/ppermute | solution.py:366
  64.8 3.4 %collective-permute-start.12 = (bf16[3,4,4096]{2,1,0:T(4,128)(2,1)S(1)}, bf16[3,4,4096]{2,1,0:T(4,128)(2,1)S(1)}, u32[]{:S(2)}, u32[]{:S(2)}) collective-permute-start(bf16[3,4,4096]{2,1,0:T(4,128)(2,1)S(1)} %get-tuple-element.25), channel_id=1, source_target_pairs={{0,8},{4,12},{8,0},{12,4},{1,9},{5,13},{9,1},{13,5},{2,10},{6,14},... | collective-permute-start | bytes 294920 | tf_op jit(solution)/shard_map/ppermute | solution.py:366
  68.2 0.9 %collective-permute-start.13 = (bf16[3,4,4096]{2,1,0:T(4,128)(2,1)S(1)}, bf16[3,4,4096]{2,1,0:T(4,128)(2,1)S(1)}, u32[]{:S(2)}, u32[]{:S(2)}) collective-permute-start(bf16[3,4,4096]{2,1,0:T(4,128)(2,1)S(1)} %get-tuple-element.26), channel_id=1, source_target_pairs={{0,12},{4,8},{8,4},{12,0},{1,13},{5,9},{9,5},{13,1},{2,14},{6,10},... | collective-permute-start | bytes 294920 | tf_op jit(solution)/shard_map/ppermute | solution.py:366
  69.1 0.0 collective-permute-done.11
  69.1 6.8 %collective-permute-done.12 = bf16[3,4,4096]{2,1,0:T(4,128)(2,1)S(1)} collective-permute-done((bf16[3,4,4096]{2,1,0:T(4,128)(2,1)S(1)}, bf16[3,4,4096]{2,1,0:T(4,128)(2,1)S(1)}, u32[]{:S(2)}, u32[]{:S(2)}) %collective-permute-start.12) | collective-permute-done | bytes 98336 | tf_op jit(solution)/shard_map/ppermute | solution.py:366
  75.9 0.7 fusion
  (28 shorter events, 0.1 us)
Async XLA Ops:
  0.0 9.0 %collective-permute-start.2 = (bf16[3,4,4096]{2,1,0:T(4,128)(2,1)}, bf16[3,4,4096]{2,1,0:T(4,128)(2,1)S(1)}, u32[]{:S(2)}, u32[]{:S(2)}) collective-permute-start(bf16[3,4,4096]{2,1,0:T(4,128)(2,1)} %bitcast.19), channel_id=1, source_target_pairs={{0,12},{4,8},{8,4},{12,0},{1,13},{5,9},{9,5},{13,1},{2,14},{6,10},... | collective-permute-start | bytes 294920 | tf_op jit(solution)/shard_map/ppermute | solution.py:366
  5.0 8.5 %collective-permute-start.1 = (bf16[3,4,4096]{2,1,0:T(4,128)(2,1)}, bf16[3,4,4096]{2,1,0:T(4,128)(2,1)S(1)}, u32[]{:S(2)}, u32[]{:S(2)}) collective-permute-start(bf16[3,4,4096]{2,1,0:T(4,128)(2,1)} %bitcast.20), channel_id=1, source_target_pairs={{0,8},{4,12},{8,0},{12,4},{1,9},{5,13},{9,1},{13,5},{2,10},{6,14},... | collective-permute-start | bytes 294920 | tf_op jit(solution)/shard_map/ppermute | solution.py:366
  5.1 8.5 %collective-permute-start = (bf16[3,4,4096]{2,1,0:T(4,128)(2,1)}, bf16[3,4,4096]{2,1,0:T(4,128)(2,1)S(1)}, u32[]{:S(2)}, u32[]{:S(2)}) collective-permute-start(bf16[3,4,4096]{2,1,0:T(4,128)(2,1)} %bitcast.21), channel_id=1, source_target_pairs={{0,4},{4,0},{8,12},{12,8},{1,5},{5,1},{9,13},{13,9},{2,6},{6,2},{1... | collective-permute-start | bytes 294920 | tf_op jit(solution)/shard_map/ppermute | solution.py:366
  6.3 0.7 copy-start.12
  6.9 0.7 copy-start.13
  7.6 6.0 %copy-start.1 = (bf16[4,4096,96]{1,2,0:T(8,128)(2,1)S(1)}, bf16[4,4096,96]{1,2,0:T(8,128)(2,1)}, u32[]{:S(2)}) copy-start(bf16[4,4096,96]{1,2,0:T(8,128)(2,1)} %param.21) | copy-start | bytes 9437188
  7.6 6.0 %copy-start.9 = (bf16[4,3,4096]{2,0,1:T(4,128)(2,1)S(1)}, bf16[4,3,4096]{2,0,1:T(4,128)(2,1)}, u32[]{:S(2)}) copy-start(bf16[4,3,4096]{2,0,1:T(4,128)(2,1)} %param.16) | copy-start | bytes 294916
  7.6 12.1 %copy-start = (bf16[4096,2048]{1,0:T(8,128)(2,1)S(1)}, bf16[4096,2048]{1,0:T(8,128)(2,1)}, u32[]{:S(2)}) copy-start(bf16[4096,2048]{1,0:T(8,128)(2,1)} %refs_3_.1) | copy-start | bytes 50331652
  7.6 12.2 %copy-start.2 = (bf16[4096,128]{1,0:T(8,128)(2,1)S(1)}, bf16[4096,128]{1,0:T(8,128)(2,1)}, u32[]{:S(2)}) copy-start(bf16[4096,128]{1,0:T(8,128)(2,1)} %refs_1_.4) | copy-start | bytes 3145732
  7.6 12.2 %copy-start.3 = (bf16[4096,128]{1,0:T(8,128)(2,1)S(1)}, bf16[4096,128]{1,0:T(8,128)(2,1)}, u32[]{:S(2)}) copy-start(bf16[4096,128]{1,0:T(8,128)(2,1)} %refs_2_.4) | copy-start | bytes 3145732
  8.3 14.8 %copy-start.5 = (bf16[4,32,2048]{2,1,0:T(8,128)(2,1)S(1)}, bf16[4,32,2048]{2,1,0:T(8,128)(2,1)}, u32[]{:S(2)}) copy-start(bf16[4,32,2048]{2,1,0:T(8,128)(2,1)} %param.22) | copy-start | bytes 1572868
  8.4 14.8 %copy-start.10 = (bf16[4,32,128]{2,1,0:T(8,128)(2,1)S(1)}, bf16[4,32,128]{2,1,0:T(8,128)(2,1)}, u32[]{:S(2)}) copy-start(bf16[4,32,128]{2,1,0:T(8,128)(2,1)} %param.23) | copy-start | bytes 98308
  8.4 14.8 %copy-start.11 = (bf16[4,32,128]{2,1,0:T(8,128)(2,1)S(1)}, bf16[4,32,128]{2,1,0:T(8,128)(2,1)}, u32[]{:S(2)}) copy-start(bf16[4,32,128]{2,1,0:T(8,128)(2,1)} %param.24) | copy-start | bytes 98308
  14.9 8.2 %collective-permute-start.6 = (bf16[32,128]{1,0:T(8,128)(2,1)S(1)}, bf16[32,128]{1,0:T(8,128)(2,1)S(1)}, u32[]{:S(2)}, u32[]{:S(2)}) collective-permute-start(bf16[32,128]{1,0:T(8,128)(2,1)S(1)} %get-tuple-element.18), channel_id=1, source_target_pairs={{0,12},{1,0},{2,4},{3,8},{4,13},{5,1},{6,5},{7,9},{8,14},{9,2},{10... | collective-permute-start | bytes 24584 | tf_op jit(solution)/shard_map/ppermute | solution.py:374
  17.4 5.7 %collective-permute-start.5 = (bf16[32,128]{1,0:T(8,128)(2,1)S(1)}, bf16[32,128]{1,0:T(8,128)(2,1)S(1)}, u32[]{:S(2)}, u32[]{:S(2)}) collective-permute-start(bf16[32,128]{1,0:T(8,128)(2,1)S(1)} %get-tuple-element.18), channel_id=1, source_target_pairs={{0,8},{1,12},{2,0},{3,4},{4,9},{5,13},{6,1},{7,5},{8,10},{9,14},{1... | collective-permute-start | bytes 24584 | tf_op jit(solution)/shard_map/ppermute | solution.py:374
  18.9 4.2 %collective-permute-start.4 = (bf16[32,128]{1,0:T(8,128)(2,1)S(1)}, bf16[32,128]{1,0:T(8,128)(2,1)S(1)}, u32[]{:S(2)}, u32[]{:S(2)}) collective-permute-start(bf16[32,128]{1,0:T(8,128)(2,1)S(1)} %get-tuple-element.18), channel_id=1, source_target_pairs={{0,4},{1,8},{2,12},{3,0},{4,5},{5,9},{6,13},{7,1},{8,6},{9,10},{10... | collective-permute-start | bytes 24584 | tf_op jit(solution)/shard_map/ppermute | solution.py:374
  19.1 4.0 %collective-permute-start.3 = (bf16[32,128]{1,0:T(8,128)(2,1)S(1)}, bf16[32,128]{1,0:T(8,128)(2,1)S(1)}, u32[]{:S(2)}, u32[]{:S(2)}) collective-permute-start(bf16[32,128]{1,0:T(8,128)(2,1)S(1)} %get-tuple-element.18), channel_id=1, source_target_pairs={{0,0},{1,4},{2,8},{3,12},{4,1},{5,5},{6,9},{7,13},{8,2},{9,6},{10,... | collective-permute-start | bytes 24584 | tf_op jit(solution)/shard_map/ppermute | solution.py:374
  23.2 17.8 %copy-start.7 = (bf16[1,4,512,128]{3,2,1,0:T(8,128)(2,1)S(1)}, bf16[1,4,512,128]{3,2,1,0:T(8,128)(2,1)}, u32[]{:S(2)}) copy-start(bf16[1,4,512,128]{3,2,1,0:T(8,128)(2,1)} %keys_ref.1) | copy-start | bytes 1572868
  23.2 17.8 %copy-start.8 = (bf16[1,4,512,128]{3,2,1,0:T(8,128)(2,1)S(1)}, bf16[1,4,512,128]{3,2,1,0:T(8,128)(2,1)}, u32[]{:S(2)}) copy-start(bf16[1,4,512,128]{3,2,1,0:T(8,128)(2,1)} %values_ref.1) | copy-start | bytes 1572868
  23.2 31.1 %copy-start.6 = (bf16[4,2048,32]{1,2,0:T(8,128)(2,1)S(1)}, bf16[4,2048,32]{1,2,0:T(8,128)(2,1)}, u32[]{:S(2)}) copy-start(bf16[4,2048,32]{1,2,0:T(8,128)(2,1)} %param.25) | copy-start | bytes 1572868
  40.9 17.1 %slice-start = ((s8[16777216]{0:T(1024)(128)(4,1)}), s8[4194304]{0:T(1024)(128)(4,1)S(1)}, s32[]{:S(2)}) async-start(s8[16777216]{0:T(1024)(128)(4,1)} %bitcast.13), calls=%async_computation.2 | async-start | bytes 8388608
  54.3 3.7 %slice-start.1 = ((s8[16777216]{0:T(1024)(128)(4,1)}), s8[4194304]{0:T(1024)(128)(4,1)S(1)}, s32[]{:S(2)}) async-start(s8[16777216]{0:T(1024)(128)(4,1)} %bitcast.13), calls=%async_computation.3 | async-start | bytes 8388608
  54.3 3.7 %slice-start.2 = ((s8[16777216]{0:T(1024)(128)(4,1)}), s8[4194304]{0:T(1024)(128)(4,1)S(1)}, s32[]{:S(2)}) async-start(s8[16777216]{0:T(1024)(128)(4,1)} %bitcast.13), calls=%async_computation.4 | async-start | bytes 8388608
  54.3 4.7 %slice-start.3 = ((s8[16777216]{0:T(1024)(128)(4,1)}), s8[4194304]{0:T(1024)(128)(4,1)S(1)}, s32[]{:S(2)}) async-start(s8[16777216]{0:T(1024)(128)(4,1)} %bitcast.13), calls=%async_computation.5 | async-start | bytes 8388608
  54.9 7.2 %copy-start.4 = (bf16[4,32,4096]{2,1,0:T(8,128)(2,1)S(1)}, bf16[4,32,4096]{2,1,0:T(8,128)(2,1)}, u32[]{:S(2)}) copy-start(bf16[4,32,4096]{2,1,0:T(8,128)(2,1)} %param.26) | copy-start | bytes 3145732
  54.9 7.1 %collective-permute-start.10 = (bf16[16,128]{1,0:T(8,128)(2,1)S(1)}, bf16[16,128]{1,0:T(8,128)(2,1)S(1)}, u32[]{:S(2)}, u32[]{:S(2)}) collective-permute-start(bf16[16,128]{1,0:T(8,128)(2,1)S(1)} %get-tuple-element.22), channel_id=1, source_target_pairs={{0,3},{1,7},{2,11},{3,15},{4,0},{5,4},{6,8},{7,12},{8,1},{9,5},{10... | collective-permute-start | bytes 12296 | tf_op jit(solution)/shard_map/ppermute | solution.py:382
  54.9 7.1 %collective-permute-start.9 = (bf16[16,128]{1,0:T(8,128)(2,1)S(1)}, bf16[16,128]{1,0:T(8,128)(2,1)S(1)}, u32[]{:S(2)}, u32[]{:S(2)}) collective-permute-start(bf16[16,128]{1,0:T(8,128)(2,1)S(1)} %get-tuple-element.22), channel_id=1, source_target_pairs={{0,2},{1,6},{2,10},{3,14},{4,3},{5,7},{6,11},{7,15},{8,0},{9,4},{1... | collective-permute-start | bytes 12296 | tf_op jit(solution)/shard_map/ppermute | solution.py:382
  55.5 6.5 %collective-permute-start.8 = (bf16[16,128]{1,0:T(8,128)(2,1)S(1)}, bf16[16,128]{1,0:T(8,128)(2,1)S(1)}, u32[]{:S(2)}, u32[]{:S(2)}) collective-permute-start(bf16[16,128]{1,0:T(8,128)(2,1)S(1)} %get-tuple-element.22), channel_id=1, source_target_pairs={{0,1},{1,5},{2,9},{3,13},{4,2},{5,6},{6,10},{7,14},{8,3},{9,7},{10... | collective-permute-start | bytes 12296 | tf_op jit(solution)/shard_map/ppermute | solution.py:382
  57.2 4.8 %collective-permute-start.7 = (bf16[16,128]{1,0:T(8,128)(2,1)S(1)}, bf16[16,128]{1,0:T(8,128)(2,1)S(1)}, u32[]{:S(2)}, u32[]{:S(2)}) collective-permute-start(bf16[16,128]{1,0:T(8,128)(2,1)S(1)} %get-tuple-element.22), channel_id=1, source_target_pairs={{0,0},{1,4},{2,8},{3,12},{4,1},{5,5},{6,9},{7,13},{8,2},{9,6},{10,... | collective-permute-start | bytes 12296 | tf_op jit(solution)/shard_map/ppermute | solution.py:382
  62.7 6.4 %collective-permute-start.11 = (bf16[3,4,4096]{2,1,0:T(4,128)(2,1)S(1)}, bf16[3,4,4096]{2,1,0:T(4,128)(2,1)S(1)}, u32[]{:S(2)}, u32[]{:S(2)}) collective-permute-start(bf16[3,4,4096]{2,1,0:T(4,128)(2,1)S(1)} %get-tuple-element.24), channel_id=1, source_target_pairs={{0,4},{4,0},{8,12},{12,8},{1,5},{5,1},{9,13},{13,9},{2,6},{6,2},{1... | collective-permute-start | bytes 294920 | tf_op jit(solution)/shard_map/ppermute | solution.py:366
  64.8 11.1 %collective-permute-start.12 = (bf16[3,4,4096]{2,1,0:T(4,128)(2,1)S(1)}, bf16[3,4,4096]{2,1,0:T(4,128)(2,1)S(1)}, u32[]{:S(2)}, u32[]{:S(2)}) collective-permute-start(bf16[3,4,4096]{2,1,0:T(4,128)(2,1)S(1)} %get-tuple-element.25), channel_id=1, source_target_pairs={{0,8},{4,12},{8,0},{12,4},{1,9},{5,13},{9,1},{13,5},{2,10},{6,14},... | collective-permute-start | bytes 294920 | tf_op jit(solution)/shard_map/ppermute | solution.py:366
  68.2 7.7 %collective-permute-start.13 = (bf16[3,4,4096]{2,1,0:T(4,128)(2,1)S(1)}, bf16[3,4,4096]{2,1,0:T(4,128)(2,1)S(1)}, u32[]{:S(2)}, u32[]{:S(2)}) collective-permute-start(bf16[3,4,4096]{2,1,0:T(4,128)(2,1)S(1)} %get-tuple-element.26), channel_id=1, source_target_pairs={{0,12},{4,8},{8,4},{12,0},{1,13},{5,9},{9,5},{13,1},{2,14},{6,10},... | collective-permute-start | bytes 294920 | tf_op jit(solution)/shard_map/ppermute | solution.py:366

commit v14 on v13

--- a/solution.py
+++ b/solution.py
@@ -200,7 +200,7 @@
 
 def grow_kernel(sizes, width, total_ref, slots_ref, *refs):
     groups, blocks, drafts = sizes
-    ranks_in, grows, (out_ref, held) = refs[:groups], refs[groups : groups + 3], refs[-2:]
+    ranks_in, grows, (out_ref, held) = refs[:2], refs[2:5], refs[-2:]
     group = group_of()
     requests = groups * blocks
     lines = out_ref.shape[1]
@@ -269,6 +269,11 @@
             out_ref[block * groups + target] = mixed
 
 
+def add_kernel(left_ref, right_ref, out_ref):
+    total = left_ref[...].astype(jnp.float32) + right_ref[...].astype(jnp.float32)
+    out_ref[...] = total.astype(jnp.bfloat16)
+
+
 def packing(rows, width, lanes):
     parts = lanes // width
     return parts, rows // parts
@@ -306,7 +311,7 @@
 
 def out_grow_kernel(sizes, width, total_ref, slots_ref, grow_ref, *refs):
     groups, blocks, drafts = sizes
-    ranks_in, outs = refs[:blocks], refs[blocks:]
+    ranks_in, outs = refs[:2], refs[2:]
     owned = grow_ref.shape[0] // width
     me = lax.axis_index("tensor")
     ranks = ranks_in[0][...].astype(jnp.float32)
@@ -365,21 +370,28 @@
         route = [(t, t ^ shift) for t in range(blocks)]
         return lax.ppermute(value, "tensor", route)
 
-    def to_growers(value, shift):
+    def over_core(value):
+        return lax.ppermute(value, "pipe", [(0, 1), (1, 0)])
+
+    def to_growers(value, flip):
         route = [
-            (t * groups + g, ((g + shift) % blocks) * groups + t)
+            (t * groups + 2 * x + c, (2 * c + (x ^ flip)) * groups + t)
+            for t in range(blocks)
+            for x in range(2)
+            for c in range(2)
+        ]
+        return lax.ppermute(value, EVERY, route)
+
+    def to_out_growers(value, flip):
+        route = [
+            (t * groups + g, g * groups + 2 * ((t // 2) ^ flip) + t % 2)
             for t in range(blocks)
             for g in range(groups)
         ]
         return lax.ppermute(value, EVERY, route)
 
-    def to_out_growers(value, shift):
-        route = [
-            (t * groups + g, g * groups + (t + shift) % groups)
-            for t in range(blocks)
-            for g in range(groups)
-        ]
-        return lax.ppermute(value, EVERY, route)
+    def added(left, right):
+        return call(add_kernel, shape(left.shape), [VMEM] * 2)(left, right)
 
     def exchange(value):
         return lax.all_to_all(value, EVERY, split_axis=0, concat_axis=0, tiled=True)
@@ -402,7 +414,8 @@
         2 * count * shrink_qkv.size,
         2 * shrink_qkv.size + 4 * count * features,
     )(*pieces, shrink_in, slots)
-    ranks = [to_growers(rank_part, shift) for shift in range(blocks)]
+    rank_part = added(rank_part, over_core(rank_part))
+    ranks = [to_growers(rank_part, flip) for flip in range(2)]
     total = product(rows, w_query, w_key, w_value)
     cols = total.shape[1]
     head_cols = w_query.shape[1]
@@ -410,7 +423,7 @@
     sent = call(
         functools.partial(grow_kernel, sizes, width),
         shape((blocks * groups, lines, head_size)),
-        [VMEM] * (5 + groups) + [HBM] * 2,
+        [VMEM] * 7 + [HBM] * 2,
         [pltpu.VMEM((blocks * groups * lines, head_size), jnp.float32)],
         limit=40 * MIB,
     )(
@@ -435,13 +448,14 @@
         [pltpu.VMEM((blocks * groups * query_lines, head_size), jnp.float32)],
         limit=40 * MIB,
     )(gathered, jnp.transpose(shrink_out, (0, 2, 1)).reshape(-1, head_cols), slots, *[w_query] * 4)
-    out_ranks = [to_out_growers(out_part, shift) for shift in range(blocks)]
+    out_part = added(*[to_out_growers(out_part, flip) for flip in range(2)])
+    out_ranks = [out_part, over_core(out_part)]
     out_total = product(out_rows, w_out)
     out_cols = out_total.shape[1]
     leaving = call(
         functools.partial(out_grow_kernel, sizes, width),
         [shape((drafts, groups, out_cols))] * blocks,
-        [VMEM] * (3 + blocks),
+        [VMEM] * 5,
         [],
         2 * count * owned * width * out_cols,
         8 * count * out_cols + 2 * owned * width * out_cols,
@@ -639,8 +653,8 @@
 
 def local(*arrays):
     heads = arrays[11].shape[1]
-    paired = heads & (heads - 1) == 0
-    if paired and heads == lax.axis_size("tensor") == lax.axis_size(GROUP):
+    sizes = [lax.axis_size(name) for name in EVERY]
+    if heads == 4 and sizes == [4, 2, 2]:
         return by_kernels(*arrays)
     return by_row(*arrays)
 

time: 76.9 us -> 77.2 us (level)
  waiting for transfers between devices: 11.9 us -> 17.5 us
  starting transfers between devices: 19.9 us -> 15.1 us
  local copies, waits for them, and re-layouts: 2.35 us -> 1.38 us
    ppermute x4 -> x2, waiting for transfers between devices: 0.02 us -> 3.72 us  [to_out_growers(): return lax.ppermute(value, EVERY, route)]
    ppermute x4 -> x2, starting transfers between devices: 4.8 us -> 1.17 us  [to_growers(): return lax.ppermute(value, EVERY, route)]
    ppermute x4 -> x2, starting transfers between devices: 3.09 us -> 0.81 us  [to_out_growers(): return lax.ppermute(value, EVERY, route)]
    ppermute x0 -> x2, waiting for transfers between devices: none -> 1.19 us  [over_core(): return lax.ppermute(value, 'pipe', [(0, 1), (1, 0)])]
    unnamed x36, local copies, waits for them, and re-layouts: 2.35 us -> 1.38 us
  transfers between devices with their start and end apart: 14 -> 12, of which waited for: 3 -> 6; matrix products, arithmetic and copies ran while one was open for 0% -> 0% of each run, Pallas kernels for 9% -> 9%
where the time goes in v14:
time: 77.2 us; the launch traced here: 77 us
  blocking collectives  29 us (38%)
  waiting for transfers between devices  17.5 us (23%)
  starting transfers between devices  15.1 us (20%)
  Pallas kernels  12.3 us (16%)
  local copies, waits for them, and re-layouts  1.38 us (2%)
  between operations  0.89 us (1%)
    all_to_all x2, blocking collectives, exchange(): return lax.all_to_all(value, EVERY, split_axis=0, concat_axis=0, tiled=True)  29 us
    ppermute x6, waiting for transfers between devices, over_tensor(): return lax.ppermute(value, 'tensor', route)  12.6 us
    ppermute x6, starting transfers between devices, over_tensor(): return lax.ppermute(value, 'tensor', route)  12.4 us
    pallas_call x2, Pallas kernels, product(): call(product_kernel, shape((rows.shape[0], width), jnp.float32), [VMEM] *...  6.31 us
    ppermute x2, waiting for transfers between devices, to_out_growers(): return lax.ppermute(value, EVERY, route)  3.72 us
    pallas_call x1, Pallas kernels, by_kernels(): call(functools.partial(attend_kernel, sizes), shape((blocks * groups, que...  1.76 us
  transfers between devices with their start and end apart: 12, of which 6 were waited for; matrix products, arithmetic and copies ran while one was open for 0% of the time, Pallas kernels for 9%

profile of v14, /device:TPU:0, one launch (start us, length us, event | category | flops | bytes accessed | tf_op | source)
XLA Modules:
  0.0 77.0 jit_solution(15871709899884928077)
XLA Ops:
  0.0 5.0 %collective-permute-start.2 = (bf16[3,4,4096]{2,1,0:T(4,128)(2,1)}, bf16[3,4,4096]{2,1,0:T(4,128)(2,1)S(1)}, u32[]{:S(2)}, u32[]{:S(2)}) collective-permute-start(bf16[3,4,4096]{2,1,0:T(4,128)(2,1)} %bitcast.19), channel_id=1, source_target_pairs={{0,12},{4,8},{8,4},{12,0},{1,13},{5,9},{9,5},{13,1},{2,14},{6,10},... | collective-permute-start | bytes 294920 | tf_op jit(solution)/shard_map/ppermute | solution.py:371
  5.0 0.0 collective-permute-start.1
  5.1 0.6 collective-permute-start
  6.3 0.6 copy-done.12
  6.9 0.7 copy-done.13
  7.6 0.7 shard_map.154
  8.3 0.0 copy-start.8
  8.4 0.0 copy-start.10
  8.4 0.0 copy-start.11
  8.4 0.6 collective-permute-done.2.refs_3_
  9.0 4.6 %collective-permute-done.1.refs_2_ = bf16[3,4,4096]{2,1,0:T(4,128)(2,1)S(1)} collective-permute-done((bf16[3,4,4096]{2,1,0:T(4,128)(2,1)}, bf16[3,4,4096]{2,1,0:T(4,128)(2,1)S(1)}, u32[]{:S(2)}, u32[]{:S(2)}) %collective-permute-start.1) | collective-permute-done | bytes 98336 | tf_op jit(solution)/shard_map/ppermute | solution.py:371
  13.5 0.0 collective-permute-done.refs_1_
  13.5 0.0 copy-done.1
  13.5 1.4 %shard_map.155 = (bf16[48,4096]{1,0:T(8,128)(2,1)S(1)}, bf16[32,128]{1,0:T(8,128)(2,1)S(1)}) custom-call(bf16[3,4,4096]{2,1,0:T(4,128)(2,1)S(1)} %bitcast.22, bf16[3,4,4096]{2,1,0:T(4,128)(2,1)S(1)} %collective-permute-done.refs_1_, bf16[3,4,4096]{2,1,0:T(4,128)(2,1)S(1)} %collective-permute-done.1.refs_2_, ...), custom_call_target="tpu_custom_call" | custom-call | flops 150994944 | bytes 3932160 | tf_op jit(solution)/shard_map/pallas_call | solution.py:409
  14.9 0.0 collective-permute-start.3
  14.9 1.2 %collective-permute-done.3.right_ref = bf16[32,128]{1,0:T(8,128)(2,1)S(1)} collective-permute-done((bf16[32,128]{1,0:T(8,128)(2,1)S(1)}, bf16[32,128]{1,0:T(8,128)(2,1)S(1)}, u32[]{:S(2)}, u32[]{:S(2)}) %collective-permute-start.3) | collective-permute-done | bytes 8224 | tf_op jit(solution)/shard_map/ppermute | solution.py:374
  16.1 0.5 collective-permute-start.5
  16.6 0.6 collective-permute-start.4
  17.3 0.0 copy-done
  17.3 0.0 copy-done.2
  17.3 0.0 copy-done.3
  17.3 3.3 %shard_map.156.total_ref = f32[48,2304]{1,0:T(8,128)S(1)} custom-call(bf16[48,4096]{1,0:T(8,128)(2,1)S(1)} %get-tuple-element.17.rows_ref, bf16[4096,2048]{1,0:T(8,128)(2,1)S(1)} %copy-done, bf16[4096,128]{1,0:T(8,128)(2,1)S(1)} %copy-done.2, bf16[4096,128]{1,0:T(8,128)(2,1)S(1)} %copy-done.3), custom_call_target="tpu_custom_call" | custom-call | tf_op jit(solution)/shard_map/pallas_call | solution.py:152
  20.6 0.0 collective-permute-done.5.refs_1_
  20.7 0.0 collective-permute-done.4.refs_0_
  20.7 0.0 copy-start.6
  20.7 0.0 copy-start.7
  20.7 0.0 copy-start.5
  20.7 0.9 %shard_map.158 = bf16[16,56,128]{2,1,0:T(8,128)(2,1)S(1)} custom-call(f32[48,2304]{1,0:T(8,128)S(1)} %shard_map.156.total_ref, s32[48,128]{1,0:T(8,128)S(1)} %get-tuple-element.16.refs_5_.slots_ref, bf16[32,128]{1,0:T(8,128)(2,1)S(1)} %collective-permute-done.4.refs_0_, bf16[32,128]{1,0:T(8,128)(2,1)S(1)} %collective-permute-done.5.refs_1_, ...), custom_call_target="tpu_custom_call" | custom-call | tf_op jit(solution)/shard_map/pallas_call | solution.py:423
  21.7 17.4 %all_to_all.10.arrived_ref = bf16[16,56,128]{2,1,0:T(8,128)(2,1)S(1)} all-to-all(bf16[16,56,128]{2,1,0:T(8,128)(2,1)S(1)} %shard_map.158), channel_id=1, replica_groups=mesh['parts'=2,'tensor'=4,'dp'=2,'pipe'=2] {'tensor','dp','pipe'}, dimensions={0} | all-to-all | bytes 458752 | tf_op jit(solution)/shard_map/all_to_all | solution.py:397
  39.0 1.8 %shard_map.159 = bf16[16,48,128]{2,1,0:T(8,128)(2,1)S(1)} custom-call(bf16[16,56,128]{2,1,0:T(8,128)(2,1)S(1)} %all_to_all.10.arrived_ref, bf16[1,4,512,128]{3,2,1,0:T(8,128)(2,1)S(1)} %copy-done.6, bf16[1,4,512,128]{3,2,1,0:T(8,128)(2,1)S(1)} %copy-done.7, s32[1]{0:T(128)S(6)} %copy.17.length_ref, f32[56,128]{1,0:T(8,128)S(1)} %get-tuple-element.19.cosine_ref, ...), custom_call_target="tpu_custom_call" | custom-call | tf_op jit(solution)/shard_map/pallas_call | solution.py:436
  40.8 11.6 %all_to_all.11.got_ref = bf16[16,48,128]{2,1,0:T(8,128)(2,1)S(1)} all-to-all(bf16[16,48,128]{2,1,0:T(8,128)(2,1)S(1)} %shard_map.159), channel_id=1, replica_groups=mesh['parts'=2,'tensor'=4,'dp'=2,'pipe'=2] {'tensor','dp','pipe'}, dimensions={0} | all-to-all | bytes 393216 | tf_op jit(solution)/shard_map/all_to_all | solution.py:397
  52.4 0.0 copy-done.5
  52.5 0.6 shard_map.160
  53.0 0.0 collective-permute-start.7
  53.0 0.8 %collective-permute-start.6 = (bf16[16,128]{1,0:T(8,128)(2,1)S(1)}, bf16[16,128]{1,0:T(8,128)(2,1)S(1)}, u32[]{:S(2)}, u32[]{:S(2)}) collective-permute-start(bf16[16,128]{1,0:T(8,128)(2,1)S(1)} %get-tuple-element.22), channel_id=1, source_target_pairs={{0,0},{1,4},{2,8},{3,12},{4,1},{5,5},{6,9},{7,13},{8,2},{9,6},{10,... | collective-permute-start | bytes 12296 | tf_op jit(solution)/shard_map/ppermute | solution.py:391
  53.8 3.7 %collective-permute-done.7.right_ref = bf16[16,128]{1,0:T(8,128)(2,1)S(1)} collective-permute-done((bf16[16,128]{1,0:T(8,128)(2,1)S(1)}, bf16[16,128]{1,0:T(8,128)(2,1)S(1)}, u32[]{:S(2)}, u32[]{:S(2)}) %collective-permute-start.7) | collective-permute-done | bytes 4128 | tf_op jit(solution)/shard_map/ppermute | solution.py:391
  57.5 0.0 collective-permute-done.6.left_ref
  57.5 0.7 collective-permute-start.8
  58.3 3.0 %shard_map.161.total_ref = f32[48,4096]{1,0:T(8,128)S(1)} custom-call(bf16[48,2048]{1,0:T(8,128)(2,1)S(1)} %get-tuple-element.21.rows_ref, bf16[2048,4096]{1,0:T(8,128)(2,1)S(1)} %bitcast.14), custom_call_target="tpu_custom_call" | custom-call | tf_op jit(solution)/shard_map/pallas_call | solution.py:152
  61.3 0.0 collective-permute-done.8.refs_1_
  61.3 0.6 shard_map.163
  62.0 1.5 %collective-permute-start.9 = (bf16[3,4,4096]{2,1,0:T(4,128)(2,1)S(1)}, bf16[3,4,4096]{2,1,0:T(4,128)(2,1)S(1)}, u32[]{:S(2)}, u32[]{:S(2)}) collective-permute-start(bf16[3,4,4096]{2,1,0:T(4,128)(2,1)S(1)} %get-tuple-element.24), channel_id=1, source_target_pairs={{0,4},{4,0},{8,12},{12,8},{1,5},{5,1},{9,13},{13,9},{2,6},{6,2},{1... | collective-permute-start | bytes 294920 | tf_op jit(solution)/shard_map/ppermute | solution.py:371
  63.5 5.0 %collective-permute-start.10 = (bf16[3,4,4096]{2,1,0:T(4,128)(2,1)S(1)}, bf16[3,4,4096]{2,1,0:T(4,128)(2,1)S(1)}, u32[]{:S(2)}, u32[]{:S(2)}) collective-permute-start(bf16[3,4,4096]{2,1,0:T(4,128)(2,1)S(1)} %get-tuple-element.25), channel_id=1, source_target_pairs={{0,8},{4,12},{8,0},{12,4},{1,9},{5,13},{9,1},{13,5},{2,10},{6,14},... | collective-permute-start | bytes 294920 | tf_op jit(solution)/shard_map/ppermute | solution.py:371
  68.4 0.3 collective-permute-start.11
  68.8 0.0 collective-permute-done.9
  68.8 3.4 %collective-permute-done.10 = bf16[3,4,4096]{2,1,0:T(4,128)(2,1)S(1)} collective-permute-done((bf16[3,4,4096]{2,1,0:T(4,128)(2,1)S(1)}, bf16[3,4,4096]{2,1,0:T(4,128)(2,1)S(1)}, u32[]{:S(2)}, u32[]{:S(2)}) %collective-permute-start.10) | collective-permute-done | bytes 98336 | tf_op jit(solution)/shard_map/ppermute | solution.py:371
  72.2 4.1 %collective-permute-done.11 = bf16[3,4,4096]{2,1,0:T(4,128)(2,1)S(1)} collective-permute-done((bf16[3,4,4096]{2,1,0:T(4,128)(2,1)S(1)}, bf16[3,4,4096]{2,1,0:T(4,128)(2,1)S(1)}, u32[]{:S(2)}, u32[]{:S(2)}) %collective-permute-start.11) | collective-permute-done | bytes 98336 | tf_op jit(solution)/shard_map/ppermute | solution.py:371
  76.2 0.7 fusion
  (26 shorter events, 0.1 us)
Async XLA Ops:
  0.0 9.0 %collective-permute-start.2 = (bf16[3,4,4096]{2,1,0:T(4,128)(2,1)}, bf16[3,4,4096]{2,1,0:T(4,128)(2,1)S(1)}, u32[]{:S(2)}, u32[]{:S(2)}) collective-permute-start(bf16[3,4,4096]{2,1,0:T(4,128)(2,1)} %bitcast.19), channel_id=1, source_target_pairs={{0,12},{4,8},{8,4},{12,0},{1,13},{5,9},{9,5},{13,1},{2,14},{6,10},... | collective-permute-start | bytes 294920 | tf_op jit(solution)/shard_map/ppermute | solution.py:371
  5.0 8.5 %collective-permute-start.1 = (bf16[3,4,4096]{2,1,0:T(4,128)(2,1)}, bf16[3,4,4096]{2,1,0:T(4,128)(2,1)S(1)}, u32[]{:S(2)}, u32[]{:S(2)}) collective-permute-start(bf16[3,4,4096]{2,1,0:T(4,128)(2,1)} %bitcast.20), channel_id=1, source_target_pairs={{0,8},{4,12},{8,0},{12,4},{1,9},{5,13},{9,1},{13,5},{2,10},{6,14},... | collective-permute-start | bytes 294920 | tf_op jit(solution)/shard_map/ppermute | solution.py:371
  5.1 8.5 %collective-permute-start = (bf16[3,4,4096]{2,1,0:T(4,128)(2,1)}, bf16[3,4,4096]{2,1,0:T(4,128)(2,1)S(1)}, u32[]{:S(2)}, u32[]{:S(2)}) collective-permute-start(bf16[3,4,4096]{2,1,0:T(4,128)(2,1)} %bitcast.21), channel_id=1, source_target_pairs={{0,4},{4,0},{8,12},{12,8},{1,5},{5,1},{9,13},{13,9},{2,6},{6,2},{1... | collective-permute-start | bytes 294920 | tf_op jit(solution)/shard_map/ppermute | solution.py:371
  6.3 0.7 copy-start.12
  6.9 0.7 copy-start.13
  7.6 6.0 %copy-start.1 = (bf16[4,4096,96]{1,2,0:T(8,128)(2,1)S(1)}, bf16[4,4096,96]{1,2,0:T(8,128)(2,1)}, u32[]{:S(2)}) copy-start(bf16[4,4096,96]{1,2,0:T(8,128)(2,1)} %param.21) | copy-start | bytes 9437188
  7.6 6.0 %copy-start.9 = (bf16[4,3,4096]{2,0,1:T(4,128)(2,1)S(1)}, bf16[4,3,4096]{2,0,1:T(4,128)(2,1)}, u32[]{:S(2)}) copy-start(bf16[4,3,4096]{2,0,1:T(4,128)(2,1)} %param.16) | copy-start | bytes 294916
  7.6 9.7 %copy-start = (bf16[4096,2048]{1,0:T(8,128)(2,1)S(1)}, bf16[4096,2048]{1,0:T(8,128)(2,1)}, u32[]{:S(2)}) copy-start(bf16[4096,2048]{1,0:T(8,128)(2,1)} %refs_3_.1) | copy-start | bytes 50331652
  7.6 9.7 %copy-start.2 = (bf16[4096,128]{1,0:T(8,128)(2,1)S(1)}, bf16[4096,128]{1,0:T(8,128)(2,1)}, u32[]{:S(2)}) copy-start(bf16[4096,128]{1,0:T(8,128)(2,1)} %refs_1_.4) | copy-start | bytes 3145732
  7.6 9.7 %copy-start.3 = (bf16[4096,128]{1,0:T(8,128)(2,1)S(1)}, bf16[4096,128]{1,0:T(8,128)(2,1)}, u32[]{:S(2)}) copy-start(bf16[4096,128]{1,0:T(8,128)(2,1)} %refs_2_.4) | copy-start | bytes 3145732
  8.3 12.3 %copy-start.8 = (bf16[4,32,2048]{2,1,0:T(8,128)(2,1)S(1)}, bf16[4,32,2048]{2,1,0:T(8,128)(2,1)}, u32[]{:S(2)}) copy-start(bf16[4,32,2048]{2,1,0:T(8,128)(2,1)} %param.22) | copy-start | bytes 1572868
  8.4 12.3 %copy-start.10 = (bf16[4,32,128]{2,1,0:T(8,128)(2,1)S(1)}, bf16[4,32,128]{2,1,0:T(8,128)(2,1)}, u32[]{:S(2)}) copy-start(bf16[4,32,128]{2,1,0:T(8,128)(2,1)} %param.23) | copy-start | bytes 98308
  8.4 12.3 %copy-start.11 = (bf16[4,32,128]{2,1,0:T(8,128)(2,1)S(1)}, bf16[4,32,128]{2,1,0:T(8,128)(2,1)}, u32[]{:S(2)}) copy-start(bf16[4,32,128]{2,1,0:T(8,128)(2,1)} %param.24) | copy-start | bytes 98308
  14.9 1.2 %collective-permute-start.3 = (bf16[32,128]{1,0:T(8,128)(2,1)S(1)}, bf16[32,128]{1,0:T(8,128)(2,1)S(1)}, u32[]{:S(2)}, u32[]{:S(2)}) collective-permute-start(bf16[32,128]{1,0:T(8,128)(2,1)S(1)} %get-tuple-element.18.left_ref), channel_id=1, source_target_pairs={{0,1},{1,0},{2,3},{3,2},{4,5},{5,4},{6,7},{7,6},{8,9},{9,8},{10,11... | collective-permute-start | bytes 24584 | tf_op jit(solution)/shard_map/ppermute | solution.py:374
  16.1 4.5 %collective-permute-start.5 = (bf16[32,128]{1,0:T(8,128)(2,1)S(1)}, bf16[32,128]{1,0:T(8,128)(2,1)S(1)}, u32[]{:S(2)}, u32[]{:S(2)}) collective-permute-start(bf16[32,128]{1,0:T(8,128)(2,1)S(1)} %shard_map.157), channel_id=1, source_target_pairs={{0,4},{1,12},{2,0},{3,8},{4,5},{5,13},{6,1},{7,9},{8,6},{9,14},{10... | collective-permute-start | bytes 24584 | tf_op jit(solution)/shard_map/ppermute | solution.py:383
  16.6 4.0 %collective-permute-start.4 = (bf16[32,128]{1,0:T(8,128)(2,1)S(1)}, bf16[32,128]{1,0:T(8,128)(2,1)S(1)}, u32[]{:S(2)}, u32[]{:S(2)}) collective-permute-start(bf16[32,128]{1,0:T(8,128)(2,1)S(1)} %shard_map.157), channel_id=1, source_target_pairs={{0,0},{1,8},{2,4},{3,12},{4,1},{5,9},{6,5},{7,13},{8,2},{9,10},{10... | collective-permute-start | bytes 24584 | tf_op jit(solution)/shard_map/ppermute | solution.py:383
  20.7 18.3 %copy-start.6 = (bf16[1,4,512,128]{3,2,1,0:T(8,128)(2,1)S(1)}, bf16[1,4,512,128]{3,2,1,0:T(8,128)(2,1)}, u32[]{:S(2)}) copy-start(bf16[1,4,512,128]{3,2,1,0:T(8,128)(2,1)} %keys_ref.1) | copy-start | bytes 1572868
  20.7 18.3 %copy-start.7 = (bf16[1,4,512,128]{3,2,1,0:T(8,128)(2,1)S(1)}, bf16[1,4,512,128]{3,2,1,0:T(8,128)(2,1)}, u32[]{:S(2)}) copy-start(bf16[1,4,512,128]{3,2,1,0:T(8,128)(2,1)} %values_ref.1) | copy-start | bytes 1572868
  20.7 31.7 %copy-start.5 = (bf16[4,2048,32]{1,2,0:T(8,128)(2,1)S(1)}, bf16[4,2048,32]{1,2,0:T(8,128)(2,1)}, u32[]{:S(2)}) copy-start(bf16[4,2048,32]{1,2,0:T(8,128)(2,1)} %param.25) | copy-start | bytes 1572868
  39.0 19.2 %slice-start = ((s8[16777216]{0:T(1024)(128)(4,1)}), s8[4194304]{0:T(1024)(128)(4,1)S(1)}, s32[]{:S(2)}) async-start(s8[16777216]{0:T(1024)(128)(4,1)} %bitcast.13), calls=%async_computation.2 | async-start | bytes 8388608
  52.4 5.8 %slice-start.1 = ((s8[16777216]{0:T(1024)(128)(4,1)}), s8[4194304]{0:T(1024)(128)(4,1)S(1)}, s32[]{:S(2)}) async-start(s8[16777216]{0:T(1024)(128)(4,1)} %bitcast.13), calls=%async_computation.3 | async-start | bytes 8388608
  52.4 5.8 %slice-start.2 = ((s8[16777216]{0:T(1024)(128)(4,1)}), s8[4194304]{0:T(1024)(128)(4,1)S(1)}, s32[]{:S(2)}) async-start(s8[16777216]{0:T(1024)(128)(4,1)} %bitcast.13), calls=%async_computation.4 | async-start | bytes 8388608
  52.4 5.8 %slice-start.3 = ((s8[16777216]{0:T(1024)(128)(4,1)}), s8[4194304]{0:T(1024)(128)(4,1)S(1)}, s32[]{:S(2)}) async-start(s8[16777216]{0:T(1024)(128)(4,1)} %bitcast.13), calls=%async_computation.5 | async-start | bytes 8388608
  53.0 8.3 %copy-start.4 = (bf16[4,32,4096]{2,1,0:T(8,128)(2,1)S(1)}, bf16[4,32,4096]{2,1,0:T(8,128)(2,1)}, u32[]{:S(2)}) copy-start(bf16[4,32,4096]{2,1,0:T(8,128)(2,1)} %param.26) | copy-start | bytes 3145732
  53.0 4.5 %collective-permute-start.7 = (bf16[16,128]{1,0:T(8,128)(2,1)S(1)}, bf16[16,128]{1,0:T(8,128)(2,1)S(1)}, u32[]{:S(2)}, u32[]{:S(2)}) collective-permute-start(bf16[16,128]{1,0:T(8,128)(2,1)S(1)} %get-tuple-element.22), channel_id=1, source_target_pairs={{0,2},{1,6},{2,10},{3,14},{4,3},{5,7},{6,11},{7,15},{8,0},{9,4},{1... | collective-permute-start | bytes 12296 | tf_op jit(solution)/shard_map/ppermute | solution.py:391
  53.0 4.5 %collective-permute-start.6 = (bf16[16,128]{1,0:T(8,128)(2,1)S(1)}, bf16[16,128]{1,0:T(8,128)(2,1)S(1)}, u32[]{:S(2)}, u32[]{:S(2)}) collective-permute-start(bf16[16,128]{1,0:T(8,128)(2,1)S(1)} %get-tuple-element.22), channel_id=1, source_target_pairs={{0,0},{1,4},{2,8},{3,12},{4,1},{5,5},{6,9},{7,13},{8,2},{9,6},{10,... | collective-permute-start | bytes 12296 | tf_op jit(solution)/shard_map/ppermute | solution.py:391
  57.5 3.8 %collective-permute-start.8 = (bf16[16,128]{1,0:T(8,128)(2,1)S(1)}, bf16[16,128]{1,0:T(8,128)(2,1)S(1)}, u32[]{:S(2)}, u32[]{:S(2)}) collective-permute-start(bf16[16,128]{1,0:T(8,128)(2,1)S(1)} %shard_map.162.refs_0_), channel_id=1, source_target_pairs={{0,1},{1,0},{2,3},{3,2},{4,5},{5,4},{6,7},{7,6},{8,9},{9,8},{10,11... | collective-permute-start | bytes 12296 | tf_op jit(solution)/shard_map/ppermute | solution.py:374
  62.0 6.8 %collective-permute-start.9 = (bf16[3,4,4096]{2,1,0:T(4,128)(2,1)S(1)}, bf16[3,4,4096]{2,1,0:T(4,128)(2,1)S(1)}, u32[]{:S(2)}, u32[]{:S(2)}) collective-permute-start(bf16[3,4,4096]{2,1,0:T(4,128)(2,1)S(1)} %get-tuple-element.24), channel_id=1, source_target_pairs={{0,4},{4,0},{8,12},{12,8},{1,5},{5,1},{9,13},{13,9},{2,6},{6,2},{1... | collective-permute-start | bytes 294920 | tf_op jit(solution)/shard_map/ppermute | solution.py:371
  63.5 8.7 %collective-permute-start.10 = (bf16[3,4,4096]{2,1,0:T(4,128)(2,1)S(1)}, bf16[3,4,4096]{2,1,0:T(4,128)(2,1)S(1)}, u32[]{:S(2)}, u32[]{:S(2)}) collective-permute-start(bf16[3,4,4096]{2,1,0:T(4,128)(2,1)S(1)} %get-tuple-element.25), channel_id=1, source_target_pairs={{0,8},{4,12},{8,0},{12,4},{1,9},{5,13},{9,1},{13,5},{2,10},{6,14},... | collective-permute-start | bytes 294920 | tf_op jit(solution)/shard_map/ppermute | solution.py:371
  68.4 7.8 %collective-permute-start.11 = (bf16[3,4,4096]{2,1,0:T(4,128)(2,1)S(1)}, bf16[3,4,4096]{2,1,0:T(4,128)(2,1)S(1)}, u32[]{:S(2)}, u32[]{:S(2)}) collective-permute-start(bf16[3,4,4096]{2,1,0:T(4,128)(2,1)S(1)} %get-tuple-element.26), channel_id=1, source_target_pairs={{0,12},{4,8},{8,4},{12,0},{1,13},{5,9},{9,5},{13,1},{2,14},{6,10},... | collective-permute-start | bytes 294920 | tf_op jit(solution)/shard_map/ppermute | solution.py:371

commit v15 on v14

--- a/solution.py
+++ b/solution.py
@@ -311,7 +311,7 @@
 
 def out_grow_kernel(sizes, width, total_ref, slots_ref, grow_ref, *refs):
     groups, blocks, drafts = sizes
-    ranks_in, outs = refs[:2], refs[2:]
+    ranks_in, outs = refs[:blocks], refs[blocks:]
     owned = grow_ref.shape[0] // width
     me = lax.axis_index("tensor")
     ranks = ranks_in[0][...].astype(jnp.float32)
@@ -382,9 +382,9 @@
         ]
         return lax.ppermute(value, EVERY, route)
 
-    def to_out_growers(value, flip):
+    def to_out_growers(value, shift):
         route = [
-            (t * groups + g, g * groups + 2 * ((t // 2) ^ flip) + t % 2)
+            (t * groups + g, g * groups + (t + shift) % groups)
             for t in range(blocks)
             for g in range(groups)
         ]
@@ -448,14 +448,13 @@
         [pltpu.VMEM((blocks * groups * query_lines, head_size), jnp.float32)],
         limit=40 * MIB,
     )(gathered, jnp.transpose(shrink_out, (0, 2, 1)).reshape(-1, head_cols), slots, *[w_query] * 4)
-    out_part = added(*[to_out_growers(out_part, flip) for flip in range(2)])
-    out_ranks = [out_part, over_core(out_part)]
+    out_ranks = [to_out_growers(out_part, shift) for shift in range(blocks)]
     out_total = product(out_rows, w_out)
     out_cols = out_total.shape[1]
     leaving = call(
         functools.partial(out_grow_kernel, sizes, width),
         [shape((drafts, groups, out_cols))] * blocks,
-        [VMEM] * 5,
+        [VMEM] * (3 + blocks),
         [],
         2 * count * owned * width * out_cols,
         8 * count * out_cols + 2 * owned * width * out_cols,

time: 77.2 us -> 75 us (0.972)
  waiting for transfers between devices: 17.5 us -> 13.1 us
  starting transfers between devices: 15.1 us -> 16.3 us
  local copies, waits for them, and re-layouts: 1.38 us -> 2.35 us
    ppermute x2 -> x4, waiting for transfers between devices: 3.72 us -> 0.02 us  [to_out_growers(): return lax.ppermute(value, EVERY, route)]
    ppermute x2 -> x4, starting transfers between devices: 0.81 us -> 3.09 us  [to_out_growers(): return lax.ppermute(value, EVERY, route)]
    unnamed x36, local copies, waits for them, and re-layouts: 1.38 us -> 2.35 us
  transfers between devices with their start and end apart: 12 -> 13, of which waited for: 6 -> 4; matrix products, arithmetic and copies ran while one was open for 0% -> 0% of each run, Pallas kernels for 9% -> 9%
where the time goes in v15:
time: 75 us; the launch traced here: 74.7 us
  blocking collectives  29 us (39%)
  starting transfers between devices  16.3 us (22%)
  waiting for transfers between devices  13.1 us (17%)
  Pallas kernels  12.3 us (16%)
  local copies, waits for them, and re-layouts  2.35 us (3%)
  between operations  0.93 us (1%)
  other arithmetic  0.75 us (1%)
    all_to_all x2, blocking collectives, exchange(): return lax.all_to_all(value, EVERY, split_axis=0, concat_axis=0, tiled=True)  29 us
    ppermute x6, starting transfers between devices, over_tensor(): return lax.ppermute(value, 'tensor', route)  12.1 us
    ppermute x6, waiting for transfers between devices, over_tensor(): return lax.ppermute(value, 'tensor', route)  11.9 us
    pallas_call x2, Pallas kernels, product(): call(product_kernel, shape((rows.shape[0], width), jnp.float32), [VMEM] *...  6.31 us
    ppermute x4, starting transfers between devices, to_out_growers(): return lax.ppermute(value, EVERY, route)  3.09 us
    unnamed x36, local copies, waits for them, and re-layouts  2.35 us
    pallas_call x1, Pallas kernels, by_kernels(): call(functools.partial(attend_kernel, sizes), shape((blocks * groups, que...  1.76 us
  transfers between devices with their start and end apart: 13, of which 4 were waited for; matrix products, arithmetic and copies ran while one was open for 0% of the time, Pallas kernels for 9%

profile of v15, /device:TPU:0, one launch (start us, length us, event | category | flops | bytes accessed | tf_op | source)
XLA Modules:
  0.0 74.7 jit_solution(9338050682415821995)
XLA Ops:
  0.0 5.0 %collective-permute-start.2 = (bf16[3,4,4096]{2,1,0:T(4,128)(2,1)}, bf16[3,4,4096]{2,1,0:T(4,128)(2,1)S(1)}, u32[]{:S(2)}, u32[]{:S(2)}) collective-permute-start(bf16[3,4,4096]{2,1,0:T(4,128)(2,1)} %bitcast.19), channel_id=1, source_target_pairs={{0,12},{4,8},{8,4},{12,0},{1,13},{5,9},{9,5},{13,1},{2,14},{6,10},... | collective-permute-start | bytes 294920 | tf_op jit(solution)/shard_map/ppermute | solution.py:371
  5.0 0.0 collective-permute-start.1
  5.1 0.6 collective-permute-start
  6.3 0.6 copy-done.12
  6.9 0.7 copy-done.13
  7.6 0.7 shard_map.154
  8.3 0.0 copy-start.8
  8.4 0.0 copy-start.10
  8.4 0.0 copy-start.11
  8.4 0.6 collective-permute-done.2.refs_3_
  9.0 4.6 %collective-permute-done.1.refs_2_ = bf16[3,4,4096]{2,1,0:T(4,128)(2,1)S(1)} collective-permute-done((bf16[3,4,4096]{2,1,0:T(4,128)(2,1)}, bf16[3,4,4096]{2,1,0:T(4,128)(2,1)S(1)}, u32[]{:S(2)}, u32[]{:S(2)}) %collective-permute-start.1) | collective-permute-done | bytes 98336 | tf_op jit(solution)/shard_map/ppermute | solution.py:371
  13.5 0.0 collective-permute-done.refs_1_
  13.5 0.0 copy-done.1
  13.5 1.4 %shard_map.155 = (bf16[48,4096]{1,0:T(8,128)(2,1)S(1)}, bf16[32,128]{1,0:T(8,128)(2,1)S(1)}) custom-call(bf16[3,4,4096]{2,1,0:T(4,128)(2,1)S(1)} %bitcast.22, bf16[3,4,4096]{2,1,0:T(4,128)(2,1)S(1)} %collective-permute-done.refs_1_, bf16[3,4,4096]{2,1,0:T(4,128)(2,1)S(1)} %collective-permute-done.1.refs_2_, ...), custom_call_target="tpu_custom_call" | custom-call | flops 150994944 | bytes 3932160 | tf_op jit(solution)/shard_map/pallas_call | solution.py:409
  14.9 0.0 collective-permute-start.3
  14.9 1.2 %collective-permute-done.3.right_ref = bf16[32,128]{1,0:T(8,128)(2,1)S(1)} collective-permute-done((bf16[32,128]{1,0:T(8,128)(2,1)S(1)}, bf16[32,128]{1,0:T(8,128)(2,1)S(1)}, u32[]{:S(2)}, u32[]{:S(2)}) %collective-permute-start.3) | collective-permute-done | bytes 8224 | tf_op jit(solution)/shard_map/ppermute | solution.py:374
  16.1 0.5 collective-permute-start.5
  16.6 0.6 collective-permute-start.4
  17.3 0.0 copy-done
  17.3 3.3 %shard_map.156.total_ref = f32[48,2304]{1,0:T(8,128)S(1)} custom-call(bf16[48,4096]{1,0:T(8,128)(2,1)S(1)} %get-tuple-element.17.rows_ref, bf16[4096,2048]{1,0:T(8,128)(2,1)S(1)} %copy-done, bf16[4096,128]{1,0:T(8,128)(2,1)S(1)} %copy-done.2, bf16[4096,128]{1,0:T(8,128)(2,1)S(1)} %copy-done.3), custom_call_target="tpu_custom_call" | custom-call | tf_op jit(solution)/shard_map/pallas_call | solution.py:152
  20.6 0.0 collective-permute-done.5.refs_1_
  20.7 0.0 collective-permute-done.4.refs_0_
  20.7 0.0 copy-start.6
  20.7 0.0 copy-start.7
  20.7 0.0 copy-start.5
  20.7 0.9 %shard_map.158 = bf16[16,56,128]{2,1,0:T(8,128)(2,1)S(1)} custom-call(f32[48,2304]{1,0:T(8,128)S(1)} %shard_map.156.total_ref, s32[48,128]{1,0:T(8,128)S(1)} %get-tuple-element.16.refs_5_.slots_ref, bf16[32,128]{1,0:T(8,128)(2,1)S(1)} %collective-permute-done.4.refs_0_, bf16[32,128]{1,0:T(8,128)(2,1)S(1)} %collective-permute-done.5.refs_1_, ...), custom_call_target="tpu_custom_call" | custom-call | tf_op jit(solution)/shard_map/pallas_call | solution.py:423
  21.7 17.4 %all_to_all.10.arrived_ref = bf16[16,56,128]{2,1,0:T(8,128)(2,1)S(1)} all-to-all(bf16[16,56,128]{2,1,0:T(8,128)(2,1)S(1)} %shard_map.158), channel_id=1, replica_groups=mesh['parts'=2,'tensor'=4,'dp'=2,'pipe'=2] {'tensor','dp','pipe'}, dimensions={0} | all-to-all | bytes 458752 | tf_op jit(solution)/shard_map/all_to_all | solution.py:397
  39.0 1.8 %shard_map.159 = bf16[16,48,128]{2,1,0:T(8,128)(2,1)S(1)} custom-call(bf16[16,56,128]{2,1,0:T(8,128)(2,1)S(1)} %all_to_all.10.arrived_ref, bf16[1,4,512,128]{3,2,1,0:T(8,128)(2,1)S(1)} %copy-done.6, bf16[1,4,512,128]{3,2,1,0:T(8,128)(2,1)S(1)} %copy-done.7, s32[1]{0:T(128)S(6)} %copy.17.length_ref, f32[56,128]{1,0:T(8,128)S(1)} %get-tuple-element.19.cosine_ref, ...), custom_call_target="tpu_custom_call" | custom-call | tf_op jit(solution)/shard_map/pallas_call | solution.py:436
  40.8 11.6 %all_to_all.11.got_ref = bf16[16,48,128]{2,1,0:T(8,128)(2,1)S(1)} all-to-all(bf16[16,48,128]{2,1,0:T(8,128)(2,1)S(1)} %shard_map.159), channel_id=1, replica_groups=mesh['parts'=2,'tensor'=4,'dp'=2,'pipe'=2] {'tensor','dp','pipe'}, dimensions={0} | all-to-all | bytes 393216 | tf_op jit(solution)/shard_map/all_to_all | solution.py:397
  52.5 0.6 shard_map.160
  53.0 0.0 collective-permute-start.9
  53.0 0.6 collective-permute-start.8
  53.6 1.7 %collective-permute-start.7 = (bf16[16,128]{1,0:T(8,128)(2,1)S(1)}, bf16[16,128]{1,0:T(8,128)(2,1)S(1)}, u32[]{:S(2)}, u32[]{:S(2)}) collective-permute-start(bf16[16,128]{1,0:T(8,128)(2,1)S(1)} %get-tuple-element.22), channel_id=1, source_target_pairs={{0,1},{1,5},{2,9},{3,13},{4,2},{5,6},{6,10},{7,14},{8,3},{9,7},{10... | collective-permute-start | bytes 12296 | tf_op jit(solution)/shard_map/ppermute | solution.py:391
  55.3 0.8 %collective-permute-start.6 = (bf16[16,128]{1,0:T(8,128)(2,1)S(1)}, bf16[16,128]{1,0:T(8,128)(2,1)S(1)}, u32[]{:S(2)}, u32[]{:S(2)}) collective-permute-start(bf16[16,128]{1,0:T(8,128)(2,1)S(1)} %get-tuple-element.22), channel_id=1, source_target_pairs={{0,0},{1,4},{2,8},{3,12},{4,1},{5,5},{6,9},{7,13},{8,2},{9,6},{10,... | collective-permute-start | bytes 12296 | tf_op jit(solution)/shard_map/ppermute | solution.py:391
  56.1 1.0 %slice-done.3 = s8[4194304]{0:T(1024)(128)(4,1)S(1)} async-done(((s8[16777216]{0:T(1024)(128)(4,1)}), s8[4194304]{0:T(1024)(128)(4,1)S(1)}, s32[]{:S(2)}) %slice-start.3) | async-done | bytes 4194328
  57.1 3.0 %shard_map.161.total_ref = f32[48,4096]{1,0:T(8,128)S(1)} custom-call(bf16[48,2048]{1,0:T(8,128)(2,1)S(1)} %get-tuple-element.21.rows_ref, bf16[2048,4096]{1,0:T(8,128)(2,1)S(1)} %bitcast.14), custom_call_target="tpu_custom_call" | custom-call | tf_op jit(solution)/shard_map/pallas_call | solution.py:152
  60.1 0.0 collective-permute-done.9.refs_3_
  60.1 0.0 collective-permute-done.8.refs_2_
  60.1 0.0 collective-permute-done.7.refs_1_
  60.1 0.0 collective-permute-done.6.refs_0_
  60.2 0.6 shard_map.162
  60.8 2.1 %collective-permute-start.10 = (bf16[3,4,4096]{2,1,0:T(4,128)(2,1)S(1)}, bf16[3,4,4096]{2,1,0:T(4,128)(2,1)S(1)}, u32[]{:S(2)}, u32[]{:S(2)}) collective-permute-start(bf16[3,4,4096]{2,1,0:T(4,128)(2,1)S(1)} %get-tuple-element.24), channel_id=1, source_target_pairs={{0,4},{4,0},{8,12},{12,8},{1,5},{5,1},{9,13},{13,9},{2,6},{6,2},{1... | collective-permute-start | bytes 294920 | tf_op jit(solution)/shard_map/ppermute | solution.py:371
  62.9 3.4 %collective-permute-start.11 = (bf16[3,4,4096]{2,1,0:T(4,128)(2,1)S(1)}, bf16[3,4,4096]{2,1,0:T(4,128)(2,1)S(1)}, u32[]{:S(2)}, u32[]{:S(2)}) collective-permute-start(bf16[3,4,4096]{2,1,0:T(4,128)(2,1)S(1)} %get-tuple-element.25), channel_id=1, source_target_pairs={{0,8},{4,12},{8,0},{12,4},{1,9},{5,13},{9,1},{13,5},{2,10},{6,14},... | collective-permute-start | bytes 294920 | tf_op jit(solution)/shard_map/ppermute | solution.py:371
  66.3 0.9 %collective-permute-start.12 = (bf16[3,4,4096]{2,1,0:T(4,128)(2,1)S(1)}, bf16[3,4,4096]{2,1,0:T(4,128)(2,1)S(1)}, u32[]{:S(2)}, u32[]{:S(2)}) collective-permute-start(bf16[3,4,4096]{2,1,0:T(4,128)(2,1)S(1)} %get-tuple-element.26), channel_id=1, source_target_pairs={{0,12},{4,8},{8,4},{12,0},{1,13},{5,9},{9,5},{13,1},{2,14},{6,10},... | collective-permute-start | bytes 294920 | tf_op jit(solution)/shard_map/ppermute | solution.py:371
  67.2 0.0 collective-permute-done.10
  67.2 6.8 %collective-permute-done.11 = bf16[3,4,4096]{2,1,0:T(4,128)(2,1)S(1)} collective-permute-done((bf16[3,4,4096]{2,1,0:T(4,128)(2,1)S(1)}, bf16[3,4,4096]{2,1,0:T(4,128)(2,1)S(1)}, u32[]{:S(2)}, u32[]{:S(2)}) %collective-permute-start.11) | collective-permute-done | bytes 98336 | tf_op jit(solution)/shard_map/ppermute | solution.py:371
  74.0 0.0 collective-permute-done.12
  74.0 0.7 %fusion = bf16[4,3,4096]{2,0,1:T(4,128)(2,1)} fusion(bf16[3,4,4096]{2,1,0:T(4,128)(2,1)S(1)} %collective-permute-done.12, bf16[3,4,4096]{2,1,0:T(4,128)(2,1)S(1)} %collective-permute-done.11, bf16[3,4,4096]{2,1,0:T(4,128)(2,1)S(1)} %collective-permute-done.10, bf16[3,4,4096]{2,1,0:T(4,128)(2,1)S(1)} %get-tuple-element.23), kind=kLoop, calls=%fused_computation.1 | loop fusion | flops 393216 | bytes 491520 | tf_op jit(solution)/shard_map/transpose | solution.py:465
  (27 shorter events, 0.1 us)
Async XLA Ops:
  0.0 9.0 %collective-permute-start.2 = (bf16[3,4,4096]{2,1,0:T(4,128)(2,1)}, bf16[3,4,4096]{2,1,0:T(4,128)(2,1)S(1)}, u32[]{:S(2)}, u32[]{:S(2)}) collective-permute-start(bf16[3,4,4096]{2,1,0:T(4,128)(2,1)} %bitcast.19), channel_id=1, source_target_pairs={{0,12},{4,8},{8,4},{12,0},{1,13},{5,9},{9,5},{13,1},{2,14},{6,10},... | collective-permute-start | bytes 294920 | tf_op jit(solution)/shard_map/ppermute | solution.py:371
  5.0 8.5 %collective-permute-start.1 = (bf16[3,4,4096]{2,1,0:T(4,128)(2,1)}, bf16[3,4,4096]{2,1,0:T(4,128)(2,1)S(1)}, u32[]{:S(2)}, u32[]{:S(2)}) collective-permute-start(bf16[3,4,4096]{2,1,0:T(4,128)(2,1)} %bitcast.20), channel_id=1, source_target_pairs={{0,8},{4,12},{8,0},{12,4},{1,9},{5,13},{9,1},{13,5},{2,10},{6,14},... | collective-permute-start | bytes 294920 | tf_op jit(solution)/shard_map/ppermute | solution.py:371
  5.1 8.5 %collective-permute-start = (bf16[3,4,4096]{2,1,0:T(4,128)(2,1)}, bf16[3,4,4096]{2,1,0:T(4,128)(2,1)S(1)}, u32[]{:S(2)}, u32[]{:S(2)}) collective-permute-start(bf16[3,4,4096]{2,1,0:T(4,128)(2,1)} %bitcast.21), channel_id=1, source_target_pairs={{0,4},{4,0},{8,12},{12,8},{1,5},{5,1},{9,13},{13,9},{2,6},{6,2},{1... | collective-permute-start | bytes 294920 | tf_op jit(solution)/shard_map/ppermute | solution.py:371
  6.3 0.7 copy-start.12
  6.9 0.7 copy-start.13
  7.6 6.0 %copy-start.1 = (bf16[4,4096,96]{1,2,0:T(8,128)(2,1)S(1)}, bf16[4,4096,96]{1,2,0:T(8,128)(2,1)}, u32[]{:S(2)}) copy-start(bf16[4,4096,96]{1,2,0:T(8,128)(2,1)} %param.21) | copy-start | bytes 9437188
  7.6 6.0 %copy-start.9 = (bf16[4,3,4096]{2,0,1:T(4,128)(2,1)S(1)}, bf16[4,3,4096]{2,0,1:T(4,128)(2,1)}, u32[]{:S(2)}) copy-start(bf16[4,3,4096]{2,0,1:T(4,128)(2,1)} %param.16) | copy-start | bytes 294916
  7.6 9.7 %copy-start = (bf16[4096,2048]{1,0:T(8,128)(2,1)S(1)}, bf16[4096,2048]{1,0:T(8,128)(2,1)}, u32[]{:S(2)}) copy-start(bf16[4096,2048]{1,0:T(8,128)(2,1)} %refs_3_.1) | copy-start | bytes 50331652
  7.6 9.7 %copy-start.2 = (bf16[4096,128]{1,0:T(8,128)(2,1)S(1)}, bf16[4096,128]{1,0:T(8,128)(2,1)}, u32[]{:S(2)}) copy-start(bf16[4096,128]{1,0:T(8,128)(2,1)} %refs_1_.4) | copy-start | bytes 3145732
  7.6 9.7 %copy-start.3 = (bf16[4096,128]{1,0:T(8,128)(2,1)S(1)}, bf16[4096,128]{1,0:T(8,128)(2,1)}, u32[]{:S(2)}) copy-start(bf16[4096,128]{1,0:T(8,128)(2,1)} %refs_2_.4) | copy-start | bytes 3145732
  8.3 12.3 %copy-start.8 = (bf16[4,32,2048]{2,1,0:T(8,128)(2,1)S(1)}, bf16[4,32,2048]{2,1,0:T(8,128)(2,1)}, u32[]{:S(2)}) copy-start(bf16[4,32,2048]{2,1,0:T(8,128)(2,1)} %param.22) | copy-start | bytes 1572868
  8.4 12.3 %copy-start.10 = (bf16[4,32,128]{2,1,0:T(8,128)(2,1)S(1)}, bf16[4,32,128]{2,1,0:T(8,128)(2,1)}, u32[]{:S(2)}) copy-start(bf16[4,32,128]{2,1,0:T(8,128)(2,1)} %param.23) | copy-start | bytes 98308
  8.4 12.3 %copy-start.11 = (bf16[4,32,128]{2,1,0:T(8,128)(2,1)S(1)}, bf16[4,32,128]{2,1,0:T(8,128)(2,1)}, u32[]{:S(2)}) copy-start(bf16[4,32,128]{2,1,0:T(8,128)(2,1)} %param.24) | copy-start | bytes 98308
  14.9 1.2 %collective-permute-start.3 = (bf16[32,128]{1,0:T(8,128)(2,1)S(1)}, bf16[32,128]{1,0:T(8,128)(2,1)S(1)}, u32[]{:S(2)}, u32[]{:S(2)}) collective-permute-start(bf16[32,128]{1,0:T(8,128)(2,1)S(1)} %get-tuple-element.18.left_ref), channel_id=1, source_target_pairs={{0,1},{1,0},{2,3},{3,2},{4,5},{5,4},{6,7},{7,6},{8,9},{9,8},{10,11... | collective-permute-start | bytes 24584 | tf_op jit(solution)/shard_map/ppermute | solution.py:374
  16.1 4.5 %collective-permute-start.5 = (bf16[32,128]{1,0:T(8,128)(2,1)S(1)}, bf16[32,128]{1,0:T(8,128)(2,1)S(1)}, u32[]{:S(2)}, u32[]{:S(2)}) collective-permute-start(bf16[32,128]{1,0:T(8,128)(2,1)S(1)} %shard_map.157), channel_id=1, source_target_pairs={{0,4},{1,12},{2,0},{3,8},{4,5},{5,13},{6,1},{7,9},{8,6},{9,14},{10... | collective-permute-start | bytes 24584 | tf_op jit(solution)/shard_map/ppermute | solution.py:383
  16.6 4.0 %collective-permute-start.4 = (bf16[32,128]{1,0:T(8,128)(2,1)S(1)}, bf16[32,128]{1,0:T(8,128)(2,1)S(1)}, u32[]{:S(2)}, u32[]{:S(2)}) collective-permute-start(bf16[32,128]{1,0:T(8,128)(2,1)S(1)} %shard_map.157), channel_id=1, source_target_pairs={{0,0},{1,8},{2,4},{3,12},{4,1},{5,9},{6,5},{7,13},{8,2},{9,10},{10... | collective-permute-start | bytes 24584 | tf_op jit(solution)/shard_map/ppermute | solution.py:383
  20.7 18.3 %copy-start.6 = (bf16[1,4,512,128]{3,2,1,0:T(8,128)(2,1)S(1)}, bf16[1,4,512,128]{3,2,1,0:T(8,128)(2,1)}, u32[]{:S(2)}) copy-start(bf16[1,4,512,128]{3,2,1,0:T(8,128)(2,1)} %keys_ref.1) | copy-start | bytes 1572868
  20.7 18.3 %copy-start.7 = (bf16[1,4,512,128]{3,2,1,0:T(8,128)(2,1)S(1)}, bf16[1,4,512,128]{3,2,1,0:T(8,128)(2,1)}, u32[]{:S(2)}) copy-start(bf16[1,4,512,128]{3,2,1,0:T(8,128)(2,1)} %values_ref.1) | copy-start | bytes 1572868
  20.7 31.7 %copy-start.5 = (bf16[4,2048,32]{1,2,0:T(8,128)(2,1)S(1)}, bf16[4,2048,32]{1,2,0:T(8,128)(2,1)}, u32[]{:S(2)}) copy-start(bf16[4,2048,32]{1,2,0:T(8,128)(2,1)} %param.25) | copy-start | bytes 1572868
  39.0 17.1 %slice-start = ((s8[16777216]{0:T(1024)(128)(4,1)}), s8[4194304]{0:T(1024)(128)(4,1)S(1)}, s32[]{:S(2)}) async-start(s8[16777216]{0:T(1024)(128)(4,1)} %bitcast.13), calls=%async_computation.2 | async-start | bytes 8388608
  52.4 3.7 %slice-start.1 = ((s8[16777216]{0:T(1024)(128)(4,1)}), s8[4194304]{0:T(1024)(128)(4,1)S(1)}, s32[]{:S(2)}) async-start(s8[16777216]{0:T(1024)(128)(4,1)} %bitcast.13), calls=%async_computation.3 | async-start | bytes 8388608
  52.4 3.7 %slice-start.2 = ((s8[16777216]{0:T(1024)(128)(4,1)}), s8[4194304]{0:T(1024)(128)(4,1)S(1)}, s32[]{:S(2)}) async-start(s8[16777216]{0:T(1024)(128)(4,1)} %bitcast.13), calls=%async_computation.4 | async-start | bytes 8388608
  52.4 4.7 %slice-start.3 = ((s8[16777216]{0:T(1024)(128)(4,1)}), s8[4194304]{0:T(1024)(128)(4,1)S(1)}, s32[]{:S(2)}) async-start(s8[16777216]{0:T(1024)(128)(4,1)} %bitcast.13), calls=%async_computation.5 | async-start | bytes 8388608
  53.0 7.1 %copy-start.4 = (bf16[4,32,4096]{2,1,0:T(8,128)(2,1)S(1)}, bf16[4,32,4096]{2,1,0:T(8,128)(2,1)}, u32[]{:S(2)}) copy-start(bf16[4,32,4096]{2,1,0:T(8,128)(2,1)} %param.26) | copy-start | bytes 3145732
  53.0 7.1 %collective-permute-start.9 = (bf16[16,128]{1,0:T(8,128)(2,1)S(1)}, bf16[16,128]{1,0:T(8,128)(2,1)S(1)}, u32[]{:S(2)}, u32[]{:S(2)}) collective-permute-start(bf16[16,128]{1,0:T(8,128)(2,1)S(1)} %get-tuple-element.22), channel_id=1, source_target_pairs={{0,3},{1,7},{2,11},{3,15},{4,0},{5,4},{6,8},{7,12},{8,1},{9,5},{10... | collective-permute-start | bytes 12296 | tf_op jit(solution)/shard_map/ppermute | solution.py:391
  53.0 7.1 %collective-permute-start.8 = (bf16[16,128]{1,0:T(8,128)(2,1)S(1)}, bf16[16,128]{1,0:T(8,128)(2,1)S(1)}, u32[]{:S(2)}, u32[]{:S(2)}) collective-permute-start(bf16[16,128]{1,0:T(8,128)(2,1)S(1)} %get-tuple-element.22), channel_id=1, source_target_pairs={{0,2},{1,6},{2,10},{3,14},{4,3},{5,7},{6,11},{7,15},{8,0},{9,4},{1... | collective-permute-start | bytes 12296 | tf_op jit(solution)/shard_map/ppermute | solution.py:391
  53.6 6.5 %collective-permute-start.7 = (bf16[16,128]{1,0:T(8,128)(2,1)S(1)}, bf16[16,128]{1,0:T(8,128)(2,1)S(1)}, u32[]{:S(2)}, u32[]{:S(2)}) collective-permute-start(bf16[16,128]{1,0:T(8,128)(2,1)S(1)} %get-tuple-element.22), channel_id=1, source_target_pairs={{0,1},{1,5},{2,9},{3,13},{4,2},{5,6},{6,10},{7,14},{8,3},{9,7},{10... | collective-permute-start | bytes 12296 | tf_op jit(solution)/shard_map/ppermute | solution.py:391
  55.3 4.8 %collective-permute-start.6 = (bf16[16,128]{1,0:T(8,128)(2,1)S(1)}, bf16[16,128]{1,0:T(8,128)(2,1)S(1)}, u32[]{:S(2)}, u32[]{:S(2)}) collective-permute-start(bf16[16,128]{1,0:T(8,128)(2,1)S(1)} %get-tuple-element.22), channel_id=1, source_target_pairs={{0,0},{1,4},{2,8},{3,12},{4,1},{5,5},{6,9},{7,13},{8,2},{9,6},{10,... | collective-permute-start | bytes 12296 | tf_op jit(solution)/shard_map/ppermute | solution.py:391
  60.8 6.4 %collective-permute-start.10 = (bf16[3,4,4096]{2,1,0:T(4,128)(2,1)S(1)}, bf16[3,4,4096]{2,1,0:T(4,128)(2,1)S(1)}, u32[]{:S(2)}, u32[]{:S(2)}) collective-permute-start(bf16[3,4,4096]{2,1,0:T(4,128)(2,1)S(1)} %get-tuple-element.24), channel_id=1, source_target_pairs={{0,4},{4,0},{8,12},{12,8},{1,5},{5,1},{9,13},{13,9},{2,6},{6,2},{1... | collective-permute-start | bytes 294920 | tf_op jit(solution)/shard_map/ppermute | solution.py:371
  62.9 11.1 %collective-permute-start.11 = (bf16[3,4,4096]{2,1,0:T(4,128)(2,1)S(1)}, bf16[3,4,4096]{2,1,0:T(4,128)(2,1)S(1)}, u32[]{:S(2)}, u32[]{:S(2)}) collective-permute-start(bf16[3,4,4096]{2,1,0:T(4,128)(2,1)S(1)} %get-tuple-element.25), channel_id=1, source_target_pairs={{0,8},{4,12},{8,0},{12,4},{1,9},{5,13},{9,1},{13,5},{2,10},{6,14},... | collective-permute-start | bytes 294920 | tf_op jit(solution)/shard_map/ppermute | solution.py:371
  66.3 7.7 %collective-permute-start.12 = (bf16[3,4,4096]{2,1,0:T(4,128)(2,1)S(1)}, bf16[3,4,4096]{2,1,0:T(4,128)(2,1)S(1)}, u32[]{:S(2)}, u32[]{:S(2)}) collective-permute-start(bf16[3,4,4096]{2,1,0:T(4,128)(2,1)S(1)} %get-tuple-element.26), channel_id=1, source_target_pairs={{0,12},{4,8},{8,4},{12,0},{1,13},{5,9},{9,5},{13,1},{2,14},{6,10},... | collective-permute-start | bytes 294920 | tf_op jit(solution)/shard_map/ppermute | solution.py:371

commit v16 on v15

--- a/solution.py
+++ b/solution.py
@@ -170,8 +170,8 @@
     column = iota(slots_ref.shape, 1)
     near = parts_of(as_gathered, sizes, index)
     far = parts_of(by_draft, sizes, index)
-    row_group = jnp.where(column == 1, far[0], near[0])
-    row_block = jnp.where(column == 1, far[1], turned(near[1]))
+    row_group = jnp.where(column == 1, far[0] ^ group_of(), near[0])
+    row_block = jnp.where(column == 1, turned(far[1]), turned(near[1]))
     place = row_block * groups + row_group
     slots = jnp.zeros(slots_ref.shape, jnp.int32)
     sent, taken = 0, 0
@@ -235,24 +235,25 @@
 
 
 def attend_kernel(
-    sizes, arrived_ref, keys_ref, values_ref, length_ref, cosine_ref, sine_ref, out_ref, *scratch
+    sizes, arrived_ref, keys_ref, values_ref, length_ref, cosine_ref, sine_ref, *refs
 ):
     groups, blocks, drafts = sizes
-    (fresh_s,) = scratch
+    outs, fresh_s = refs[:blocks], refs[blocks]
     cache_size, head_size = keys_ref.shape[2:]
-    count = out_ref.shape[1]
+    count = outs[0].shape[0]
     scale = 1.0 / math.sqrt(head_size)
     fresh_s[...] = jnp.zeros(fresh_s.shape, jnp.float32)
     for block in range(blocks):
-        joined = arrived_ref[block * groups].astype(jnp.float32)
+        head = turned(block)
+        joined = arrived_ref[head * groups].astype(jnp.float32)
         for other in range(1, groups):
-            joined = joined + arrived_ref[block * groups + other].astype(jnp.float32)
+            joined = joined + arrived_ref[head * groups + other].astype(jnp.float32)
         joined = joined.astype(jnp.bfloat16).astype(jnp.float32)
         rotated = joined * cosine_ref[...] + pltpu.roll(joined, head_size // 2, 1) * sine_ref[...]
         fresh_s[2 * block, 0:drafts, :] = rotated[count : count + drafts]
         fresh_s[2 * block + 1, 0:drafts, :] = joined[count + drafts : count + 2 * drafts]
         query = rotated[0:count].astype(jnp.bfloat16)
-        old = dot_nt(query, keys_ref[0, block]) * scale
+        old = dot_nt(query, keys_ref[0, head]) * scale
         new = dot_nt(query, fresh_s[2 * block].astype(jnp.bfloat16)) * scale
         old = jnp.where(iota(old.shape, 1) < length_ref[0], old, -jnp.inf)
         seen = iota(new.shape, 1) <= lax.rem(iota(new.shape, 0), drafts)
@@ -261,12 +262,10 @@
         old = jnp.exp(old - peak)
         new = jnp.exp(new - peak)
         below = jnp.sum(old, 1, keepdims=True) + jnp.sum(new, 1, keepdims=True)
-        mixed = dot((old / below).astype(jnp.bfloat16), values_ref[0, block]) + dot(
+        mixed = dot((old / below).astype(jnp.bfloat16), values_ref[0, head]) + dot(
             (new / below).astype(jnp.bfloat16), fresh_s[2 * block + 1].astype(jnp.bfloat16)
         )
-        mixed = mixed.astype(jnp.bfloat16)
-        for target in range(groups):
-            out_ref[block * groups + target] = mixed
+        outs[block][...] = mixed.astype(jnp.bfloat16)
 
 
 def add_kernel(left_ref, right_ref, out_ref):
@@ -274,17 +273,31 @@
     out_ref[...] = total.astype(jnp.bfloat16)
 
 
+def absolute(sizes, index):
+    group, block, draft = parts_of(by_draft, sizes, index)
+    return by_draft(sizes, group ^ group_of(), turned(block), draft)
+
+
+def stack_kernel(*refs):
+    for index, ref in enumerate(refs[:-1]):
+        refs[-1][index] = ref[...]
+
+
 def packing(rows, width, lanes):
     parts = lanes // width
     return parts, rows // parts
 
 
-def out_rank_kernel(sizes, owned, got_ref, shrink_ref, slots_ref, *refs):
+def out_rank_kernel(sizes, owned, *refs):
+    groups, blocks, drafts = sizes
+    shrink_ref, slots_ref = refs[groups : groups + 2]
     rows_ref, rank_ref, wide = refs[-3:]
-    drafts = sizes[2]
-    requests, lines, head_size = got_ref.shape
-    for row in range(requests):
-        wide[row * lines : (row + 1) * lines, :] = got_ref[row].astype(jnp.float32)
+    lines, head_size = refs[0].shape[1:]
+    requests = blocks * groups
+    for block in range(blocks):
+        for group in range(groups):
+            start = (block * groups + group) * lines
+            wide[start : start + lines, :] = refs[group][block].astype(jnp.float32)
     for head in range(lines // drafts):
         for draft in range(drafts):
             rows_ref[
@@ -301,10 +314,10 @@
     fold = (ranks.shape[1], lanes)
     fold = rest_of(iota(fold, 0), width) == rest_of(iota(fold, 1), width)
     ranks = dot(kept, jnp.where(fold, 1.0, 0.0).astype(jnp.bfloat16))
-    mine = over(iota(ranks.shape, 1), width) == over(iota(ranks.shape, 0), span)
+    mine = over(iota(ranks.shape, 1), width) == over(absolute(sizes, iota(ranks.shape, 0)), span)
     ranks = jnp.where(mine, ranks, 0.0).astype(jnp.bfloat16)
     put = (held, rows.shape[0])
-    put = iota(put, 0) == rest_of(iota(put, 1), span)
+    put = iota(put, 0) == rest_of(absolute(sizes, iota(put, 1)), span)
     ranks = dot(jnp.where(put, 1.0, 0.0).astype(jnp.bfloat16), ranks)
     rank_ref[...] = ranks.astype(jnp.bfloat16)
 
@@ -320,9 +333,9 @@
     count = total_ref.shape[0]
     held, lanes = ranks.shape
     parts, span = packing(count, width, lanes)
-    put = rest_of(iota((count, held), 0), span) == iota((count, held), 1)
+    put = rest_of(absolute(sizes, iota((count, held), 0)), span) == iota((count, held), 1)
     ranks = dot(jnp.where(put, 1.0, 0.0).astype(jnp.bfloat16), ranks.astype(jnp.bfloat16))
-    mine = over(iota(ranks.shape, 1), width) == over(iota(ranks.shape, 0), span)
+    mine = over(iota(ranks.shape, 1), width) == over(absolute(sizes, iota(ranks.shape, 0)), span)
     ranks = jnp.where(mine, ranks, 0.0).astype(jnp.bfloat16)
     tile = (lanes, owned * width)
     tile = rest_of(iota(tile, 0), width) == rest_of(iota(tile, 1), width)
@@ -330,7 +343,9 @@
     place = slots_ref[:, 1:2] - me * owned
     wide = jnp.where(over(iota(ranks.shape, 1), width) == place, ranks, 0.0).astype(jnp.bfloat16)
     full = (total_ref[...] + dot(wide, grow_ref[...])).astype(jnp.bfloat16)
-    full = dot(reorder(sizes, as_gathered, by_draft), full).astype(jnp.bfloat16)
+    group, block, draft = parts_of(as_gathered, sizes, iota((count, count), 0))
+    wanted = by_draft(sizes, group ^ group_of(), block, draft) == iota((count, count), 1)
+    full = dot(jnp.where(wanted, 1.0, 0.0).astype(jnp.bfloat16), full).astype(jnp.bfloat16)
     for block in range(blocks):
         for draft in range(drafts):
             start = (block * drafts + draft) * groups
@@ -370,6 +385,9 @@
         route = [(t, t ^ shift) for t in range(blocks)]
         return lax.ppermute(value, "tensor", route)
 
+    def over_group(value, shift):
+        return lax.ppermute(value, GROUP, [(g, g ^ shift) for g in range(groups)])
+
     def over_core(value):
         return lax.ppermute(value, "pipe", [(0, 1), (1, 0)])
 
@@ -384,7 +402,7 @@
 
     def to_out_growers(value, shift):
         route = [
-            (t * groups + g, g * groups + (t + shift) % groups)
+            (t * groups + g, g * groups + (t ^ shift))
             for t in range(blocks)
             for g in range(groups)
         ]
@@ -435,19 +453,22 @@
     )
     mixed = call(
         functools.partial(attend_kernel, sizes),
-        shape((blocks * groups, query_lines, head_size)),
+        [shape((query_lines, head_size))] * blocks,
         [VMEM] * 3 + [pl.BlockSpec(memory_space=pltpu.SMEM)] + [VMEM] * 2,
         [pltpu.VMEM((2 * blocks, 128, head_size), jnp.float32)],
     )(exchange(sent), cache_keys, cache_values, cache_lengths, cosine, sine)
-    gathered = exchange(mixed)
+    stacked = call(
+        stack_kernel, shape((blocks, query_lines, head_size)), [VMEM] * blocks
+    )(mixed[0], *[over_tensor(mixed[shift], shift) for shift in range(1, blocks)])
+    gathered = [stacked] + [over_group(stacked, shift) for shift in range(1, groups)]
     held = -(-packing(count, width, 128)[1] // 16) * 16
     out_rows, out_part = call(
         functools.partial(out_rank_kernel, sizes, owned),
         [shape((count, head_cols)), shape((held, 128))],
-        [VMEM] * 3 + [HBM] * 4,
+        [VMEM] * (groups + 2) + [HBM] * 4,
         [pltpu.VMEM((blocks * groups * query_lines, head_size), jnp.float32)],
         limit=40 * MIB,
-    )(gathered, jnp.transpose(shrink_out, (0, 2, 1)).reshape(-1, head_cols), slots, *[w_query] * 4)
+    )(*gathered, jnp.transpose(shrink_out, (0, 2, 1)).reshape(-1, head_cols), slots, *[w_query] * 4)
     out_ranks = [to_out_growers(out_part, shift) for shift in range(blocks)]
     out_total = product(out_rows, w_out)
     out_cols = out_total.shape[1]

time: 75 us -> 76.3 us (1.017)
  blocking collectives: 29 us -> 17.6 us
  starting transfers between devices: 16.3 us -> 22.1 us
  waiting for transfers between devices: 13.1 us -> 18.6 us
  local copies, waits for them, and re-layouts: 2.35 us -> 3.46 us
    all_to_all x2 -> x1, blocking collectives: 29 us -> 17.6 us  [exchange(): return lax.all_to_all(value, EVERY, split_axis=0, concat_axis=0, tiled=True)]
    ppermute x6 -> x9, starting transfers between devices: 12.1 us -> 17.1 us  [over_tensor(): return lax.ppermute(value, 'tensor', route)]
    ppermute x0 -> x3, waiting for transfers between devices: none -> 2.77 us  [over_group(): return lax.ppermute(value, GROUP, [(g, g ^ shift) for g in range(groups)])]
    ppermute x6 -> x9, waiting for transfers between devices: 11.9 us -> 14.6 us  [over_tensor(): return lax.ppermute(value, 'tensor', route)]
    ppermute x0 -> x3, starting transfers between devices: none -> 1.86 us  [over_group(): return lax.ppermute(value, GROUP, [(g, g ^ shift) for g in range(groups)])]
    ppermute x4, starting transfers between devices: 3.09 us -> 1.97 us  [to_out_growers(): return lax.ppermute(value, EVERY, route)]
    unnamed x36, local copies, waits for them, and re-layouts: 2.35 us -> 3.46 us
    pallas_call x1 -> x2, Pallas kernels: 1.76 us -> 1.76 us  [the longest x1 1.75 us: by_kernels(): call(functools.partial(attend_kernel, sizes), [shape((query_lines, head_s...]
  transfers between devices with their start and end apart: 13 -> 19, of which waited for: 4 -> 8; matrix products, arithmetic and copies ran while one was open for 0% -> 0% of each run, Pallas kernels for 9% -> 9%
where the time goes in v16:
time: 76.3 us; the launch traced here: 75.8 us
  starting transfers between devices  22.1 us (29%)
  waiting for transfers between devices  18.6 us (24%)
  blocking collectives  17.6 us (23%)
  Pallas kernels  12.3 us (16%)
  local copies, waits for them, and re-layouts  3.46 us (5%)
  between operations  0.96 us (1%)
    all_to_all x1, blocking collectives, exchange(): return lax.all_to_all(value, EVERY, split_axis=0, concat_axis=0, tiled=True)  17.6 us
    ppermute x9, starting transfers between devices, over_tensor(): return lax.ppermute(value, 'tensor', route)  17.1 us
    ppermute x9, waiting for transfers between devices, over_tensor(): return lax.ppermute(value, 'tensor', route)  14.6 us
    pallas_call x2, Pallas kernels, product(): call(product_kernel, shape((rows.shape[0], width), jnp.float32), [VMEM] *...  6.31 us
    unnamed x36, local copies, waits for them, and re-layouts  3.46 us
    ppermute x3, waiting for transfers between devices, over_group(): return lax.ppermute(value, GROUP, [(g, g ^ shift) for g in range(groups)])  2.77 us
    ppermute x4, starting transfers between devices, to_out_growers(): return lax.ppermute(value, EVERY, route)  1.97 us
    ppermute x3, starting transfers between devices, over_group(): return lax.ppermute(value, GROUP, [(g, g ^ shift) for g in range(groups)])  1.86 us
  transfers between devices with their start and end apart: 19, of which 8 were waited for; matrix products, arithmetic and copies ran while one was open for 0% of the time, Pallas kernels for 9%

profile of v16, /device:TPU:0, one launch (start us, length us, event | category | flops | bytes accessed | tf_op | source)
XLA Modules:
  0.0 75.8 jit_solution(4364762062983005482)
XLA Ops:
  0.0 5.0 %collective-permute-start.2 = (bf16[3,4,4096]{2,1,0:T(4,128)(2,1)}, bf16[3,4,4096]{2,1,0:T(4,128)(2,1)S(1)}, u32[]{:S(2)}, u32[]{:S(2)}) collective-permute-start(bf16[3,4,4096]{2,1,0:T(4,128)(2,1)} %bitcast.19), channel_id=1, source_target_pairs={{0,12},{4,8},{8,4},{12,0},{1,13},{5,9},{9,5},{13,1},{2,14},{6,10},... | collective-permute-start | bytes 294920 | tf_op jit(solution)/shard_map/ppermute | solution.py:386
  5.1 0.6 collective-permute-start
  6.3 0.6 copy-done.12
  6.9 0.7 copy-done.13
  7.6 0.7 shard_map.154
  8.3 0.0 copy-start.8
  8.4 0.0 copy-start.10
  8.4 0.0 copy-start.11
  8.4 0.6 collective-permute-done.2.refs_3_
  9.0 4.6 %collective-permute-done.1.refs_2_ = bf16[3,4,4096]{2,1,0:T(4,128)(2,1)S(1)} collective-permute-done((bf16[3,4,4096]{2,1,0:T(4,128)(2,1)}, bf16[3,4,4096]{2,1,0:T(4,128)(2,1)S(1)}, u32[]{:S(2)}, u32[]{:S(2)}) %collective-permute-start.1) | collective-permute-done | bytes 98336 | tf_op jit(solution)/shard_map/ppermute | solution.py:386
  13.5 0.0 collective-permute-done.refs_1_
  13.5 1.4 %shard_map.155 = (bf16[48,4096]{1,0:T(8,128)(2,1)S(1)}, bf16[32,128]{1,0:T(8,128)(2,1)S(1)}) custom-call(bf16[3,4,4096]{2,1,0:T(4,128)(2,1)S(1)} %bitcast.22, bf16[3,4,4096]{2,1,0:T(4,128)(2,1)S(1)} %collective-permute-done.refs_1_, bf16[3,4,4096]{2,1,0:T(4,128)(2,1)S(1)} %collective-permute-done.1.refs_2_, ...), custom_call_target="tpu_custom_call" | custom-call | flops 150994944 | bytes 3932160 | tf_op jit(solution)/shard_map/pallas_call | solution.py:427
  14.9 1.2 %collective-permute-done.3.right_ref = bf16[32,128]{1,0:T(8,128)(2,1)S(1)} collective-permute-done((bf16[32,128]{1,0:T(8,128)(2,1)S(1)}, bf16[32,128]{1,0:T(8,128)(2,1)S(1)}, u32[]{:S(2)}, u32[]{:S(2)}) %collective-permute-start.3) | collective-permute-done | bytes 8224 | tf_op jit(solution)/shard_map/ppermute | solution.py:392
  16.1 0.5 collective-permute-start.5
  16.6 0.6 collective-permute-start.4
  17.3 3.3 %shard_map.156.total_ref = f32[48,2304]{1,0:T(8,128)S(1)} custom-call(bf16[48,4096]{1,0:T(8,128)(2,1)S(1)} %get-tuple-element.21.rows_ref, bf16[4096,2048]{1,0:T(8,128)(2,1)S(1)} %copy-done, bf16[4096,128]{1,0:T(8,128)(2,1)S(1)} %copy-done.2, bf16[4096,128]{1,0:T(8,128)(2,1)S(1)} %copy-done.3), custom_call_target="tpu_custom_call" | custom-call | tf_op jit(solution)/shard_map/pallas_call | solution.py:152
  20.6 0.0 collective-permute-done.5.refs_1_
  20.7 0.0 copy-start.6
  20.7 0.0 copy-start.7
  20.7 0.0 copy-start.5
  20.7 0.9 %shard_map.158 = bf16[16,56,128]{2,1,0:T(8,128)(2,1)S(1)} custom-call(f32[48,2304]{1,0:T(8,128)S(1)} %shard_map.156.total_ref, s32[48,128]{1,0:T(8,128)S(1)} %get-tuple-element.20.refs_5_.slots_ref, bf16[32,128]{1,0:T(8,128)(2,1)S(1)} %collective-permute-done.4.refs_0_, bf16[32,128]{1,0:T(8,128)(2,1)S(1)} %collective-permute-done.5.refs_1_, ...), custom_call_target="tpu_custom_call" | custom-call | tf_op jit(solution)/shard_map/pallas_call | solution.py:441
  21.7 0.0 slice-start
  21.7 17.6 %all_to_all.5.arrived_ref = bf16[16,56,128]{2,1,0:T(8,128)(2,1)S(1)} all-to-all(bf16[16,56,128]{2,1,0:T(8,128)(2,1)S(1)} %shard_map.158), channel_id=1, replica_groups=mesh['parts'=2,'tensor'=4,'dp'=2,'pipe'=2] {'tensor','dp','pipe'}, dimensions={0} | all-to-all | bytes 458752 | tf_op jit(solution)/shard_map/all_to_all | solution.py:415
  39.3 1.8 %shard_map.159 = (bf16[48,128]{1,0:T(8,128)(2,1)S(1)}, bf16[48,128]{1,0:T(8,128)(2,1)S(1)}, bf16[48,128]{1,0:T(8,128)(2,1)S(1)}, bf16[48,128]{1,0:T(8,128)(2,1)S(1)}) custom-call(bf16[16,56,128]{2,1,0:T(8,128)(2,1)S(1)} %all_to_all.5.arrived_ref, bf16[1,4,512,128]{3,2,1,0:T(8,128)(2,1)S(1)} %copy-done.6, bf16[1,4,512,128]{3,2,1,0:T(8,128)(2,1)S(1)} %copy-done.7, ...), custom_call_target="tpu_custom_call" | custom-call | tf_op jit(solution)/shard_map/pallas_call | solution.py:454
  41.1 0.1 collective-permute-start.6
  41.2 1.5 %collective-permute-start.7 = (bf16[48,128]{1,0:T(8,128)(2,1)S(1)}, bf16[48,128]{1,0:T(8,128)(2,1)S(1)}, u32[]{:S(2)}, u32[]{:S(2)}) collective-permute-start(bf16[48,128]{1,0:T(8,128)(2,1)S(1)} %get-tuple-element.27), channel_id=1, source_target_pairs={{0,8},{4,12},{8,0},{12,4},{1,9},{5,13},{9,1},{13,5},{2,10},{6,14},... | collective-permute-start | bytes 36872 | tf_op jit(solution)/shard_map/ppermute | solution.py:386
  42.6 2.9 %collective-permute-start.8 = (bf16[48,128]{1,0:T(8,128)(2,1)S(1)}, bf16[48,128]{1,0:T(8,128)(2,1)S(1)}, u32[]{:S(2)}, u32[]{:S(2)}) collective-permute-start(bf16[48,128]{1,0:T(8,128)(2,1)S(1)} %get-tuple-element.28), channel_id=1, source_target_pairs={{0,12},{4,8},{8,4},{12,0},{1,13},{5,9},{9,5},{13,1},{2,14},{6,10},... | collective-permute-start | bytes 36872 | tf_op jit(solution)/shard_map/ppermute | solution.py:386
  45.5 0.4 collective-permute-done.7.refs_2_
  45.9 2.2 %collective-permute-done.8.refs_3_ = bf16[48,128]{1,0:T(8,128)(2,1)S(1)} collective-permute-done((bf16[48,128]{1,0:T(8,128)(2,1)S(1)}, bf16[48,128]{1,0:T(8,128)(2,1)S(1)}, u32[]{:S(2)}, u32[]{:S(2)}) %collective-permute-start.8) | collective-permute-done | bytes 12320 | tf_op jit(solution)/shard_map/ppermute | solution.py:386
  48.1 0.0 collective-permute-start.11
  48.1 1.2 %collective-permute-start.10 = (bf16[4,48,128]{2,1,0:T(8,128)(2,1)S(1)}, bf16[4,48,128]{2,1,0:T(8,128)(2,1)S(1)}, u32[]{:S(2)}, u32[]{:S(2)}) collective-permute-start(bf16[4,48,128]{2,1,0:T(8,128)(2,1)S(1)} %shard_map.160.refs_0_), channel_id=1, source_target_pairs={{0,2},{1,3},{2,0},{3,1},{4,6},{5,7},{6,4},{7,5},{8,10},{9,11},{10,... | collective-permute-start | bytes 147464 | tf_op jit(solution)/shard_map/ppermute | solution.py:389
  49.3 0.7 collective-permute-start.9
  50.0 2.0 %collective-permute-done.11.refs_3_ = bf16[4,48,128]{2,1,0:T(8,128)(2,1)S(1)} collective-permute-done((bf16[4,48,128]{2,1,0:T(8,128)(2,1)S(1)}, bf16[4,48,128]{2,1,0:T(8,128)(2,1)S(1)}, u32[]{:S(2)}, u32[]{:S(2)}) %collective-permute-start.11) | collective-permute-done | bytes 49184 | tf_op jit(solution)/shard_map/ppermute | solution.py:389
  51.9 0.8 %collective-permute-done.10.refs_2_ = bf16[4,48,128]{2,1,0:T(8,128)(2,1)S(1)} collective-permute-done((bf16[4,48,128]{2,1,0:T(8,128)(2,1)S(1)}, bf16[4,48,128]{2,1,0:T(8,128)(2,1)S(1)}, u32[]{:S(2)}, u32[]{:S(2)}) %collective-permute-start.10) | collective-permute-done | bytes 49184 | tf_op jit(solution)/shard_map/ppermute | solution.py:389
  52.8 0.6 shard_map.161
  53.3 0.9 %collective-permute-start.15 = (bf16[16,128]{1,0:T(8,128)(2,1)S(1)}, bf16[16,128]{1,0:T(8,128)(2,1)S(1)}, u32[]{:S(2)}, u32[]{:S(2)}) collective-permute-start(bf16[16,128]{1,0:T(8,128)(2,1)S(1)} %get-tuple-element.30), channel_id=1, source_target_pairs={{0,3},{1,7},{2,11},{3,15},{4,2},{5,6},{6,10},{7,14},{8,1},{9,5},{1... | collective-permute-start | bytes 12296 | tf_op jit(solution)/shard_map/ppermute | solution.py:409
  54.2 0.3 collective-permute-start.14
  54.5 0.8 %collective-permute-start.12 = (bf16[16,128]{1,0:T(8,128)(2,1)S(1)}, bf16[16,128]{1,0:T(8,128)(2,1)S(1)}, u32[]{:S(2)}, u32[]{:S(2)}) collective-permute-start(bf16[16,128]{1,0:T(8,128)(2,1)S(1)} %get-tuple-element.30), channel_id=1, source_target_pairs={{0,0},{1,4},{2,8},{3,12},{4,1},{5,5},{6,9},{7,13},{8,2},{9,6},{10,... | collective-permute-start | bytes 12296 | tf_op jit(solution)/shard_map/ppermute | solution.py:409
  55.3 0.9 %slice-done.2 = s8[4194304]{0:T(1024)(128)(4,1)S(1)} async-done(((s8[16777216]{0:T(1024)(128)(4,1)}), s8[4194304]{0:T(1024)(128)(4,1)S(1)}, s32[]{:S(2)}) %slice-start.2) | async-done | bytes 4194328
  56.2 1.2 %slice-done.3 = s8[4194304]{0:T(1024)(128)(4,1)S(1)} async-done(((s8[16777216]{0:T(1024)(128)(4,1)}), s8[4194304]{0:T(1024)(128)(4,1)S(1)}, s32[]{:S(2)}) %slice-start.3) | async-done | bytes 4194328
  57.4 3.0 %shard_map.162.total_ref = f32[48,4096]{1,0:T(8,128)S(1)} custom-call(bf16[48,2048]{1,0:T(8,128)(2,1)S(1)} %get-tuple-element.29.rows_ref, bf16[2048,4096]{1,0:T(8,128)(2,1)S(1)} %bitcast.14), custom_call_target="tpu_custom_call" | custom-call | tf_op jit(solution)/shard_map/pallas_call | solution.py:152
  60.4 0.0 collective-permute-done.15.refs_3_
  60.5 0.7 shard_map.163
  61.1 2.7 %collective-permute-start.16 = (bf16[3,4,4096]{2,1,0:T(4,128)(2,1)S(1)}, bf16[3,4,4096]{2,1,0:T(4,128)(2,1)S(1)}, u32[]{:S(2)}, u32[]{:S(2)}) collective-permute-start(bf16[3,4,4096]{2,1,0:T(4,128)(2,1)S(1)} %get-tuple-element.32), channel_id=1, source_target_pairs={{0,4},{4,0},{8,12},{12,8},{1,5},{5,1},{9,13},{13,9},{2,6},{6,2},{1... | collective-permute-start | bytes 294920 | tf_op jit(solution)/shard_map/ppermute | solution.py:386
  63.9 3.4 %collective-permute-start.17 = (bf16[3,4,4096]{2,1,0:T(4,128)(2,1)S(1)}, bf16[3,4,4096]{2,1,0:T(4,128)(2,1)S(1)}, u32[]{:S(2)}, u32[]{:S(2)}) collective-permute-start(bf16[3,4,4096]{2,1,0:T(4,128)(2,1)S(1)} %get-tuple-element.33), channel_id=1, source_target_pairs={{0,8},{4,12},{8,0},{12,4},{1,9},{5,13},{9,1},{13,5},{2,10},{6,14},... | collective-permute-start | bytes 294920 | tf_op jit(solution)/shard_map/ppermute | solution.py:386
  67.2 0.9 %collective-permute-start.18 = (bf16[3,4,4096]{2,1,0:T(4,128)(2,1)S(1)}, bf16[3,4,4096]{2,1,0:T(4,128)(2,1)S(1)}, u32[]{:S(2)}, u32[]{:S(2)}) collective-permute-start(bf16[3,4,4096]{2,1,0:T(4,128)(2,1)S(1)} %get-tuple-element.34), channel_id=1, source_target_pairs={{0,12},{4,8},{8,4},{12,0},{1,13},{5,9},{9,5},{13,1},{2,14},{6,10},... | collective-permute-start | bytes 294920 | tf_op jit(solution)/shard_map/ppermute | solution.py:386
  68.2 6.9 %collective-permute-done.17 = bf16[3,4,4096]{2,1,0:T(4,128)(2,1)S(1)} collective-permute-done((bf16[3,4,4096]{2,1,0:T(4,128)(2,1)S(1)}, bf16[3,4,4096]{2,1,0:T(4,128)(2,1)S(1)}, u32[]{:S(2)}, u32[]{:S(2)}) %collective-permute-start.17) | collective-permute-done | bytes 98336 | tf_op jit(solution)/shard_map/ppermute | solution.py:386
  75.1 0.7 fusion
  (39 shorter events, 0.1 us)
Async XLA Ops:
  0.0 9.0 %collective-permute-start.2 = (bf16[3,4,4096]{2,1,0:T(4,128)(2,1)}, bf16[3,4,4096]{2,1,0:T(4,128)(2,1)S(1)}, u32[]{:S(2)}, u32[]{:S(2)}) collective-permute-start(bf16[3,4,4096]{2,1,0:T(4,128)(2,1)} %bitcast.19), channel_id=1, source_target_pairs={{0,12},{4,8},{8,4},{12,0},{1,13},{5,9},{9,5},{13,1},{2,14},{6,10},... | collective-permute-start | bytes 294920 | tf_op jit(solution)/shard_map/ppermute | solution.py:386
  5.0 8.5 %collective-permute-start.1 = (bf16[3,4,4096]{2,1,0:T(4,128)(2,1)}, bf16[3,4,4096]{2,1,0:T(4,128)(2,1)S(1)}, u32[]{:S(2)}, u32[]{:S(2)}) collective-permute-start(bf16[3,4,4096]{2,1,0:T(4,128)(2,1)} %bitcast.20), channel_id=1, source_target_pairs={{0,8},{4,12},{8,0},{12,4},{1,9},{5,13},{9,1},{13,5},{2,10},{6,14},... | collective-permute-start | bytes 294920 | tf_op jit(solution)/shard_map/ppermute | solution.py:386
  5.1 8.5 %collective-permute-start = (bf16[3,4,4096]{2,1,0:T(4,128)(2,1)}, bf16[3,4,4096]{2,1,0:T(4,128)(2,1)S(1)}, u32[]{:S(2)}, u32[]{:S(2)}) collective-permute-start(bf16[3,4,4096]{2,1,0:T(4,128)(2,1)} %bitcast.21), channel_id=1, source_target_pairs={{0,4},{4,0},{8,12},{12,8},{1,5},{5,1},{9,13},{13,9},{2,6},{6,2},{1... | collective-permute-start | bytes 294920 | tf_op jit(solution)/shard_map/ppermute | solution.py:386
  6.3 0.7 copy-start.12
  6.9 0.7 copy-start.13
  7.6 6.0 %copy-start.1 = (bf16[4,4096,96]{1,2,0:T(8,128)(2,1)S(1)}, bf16[4,4096,96]{1,2,0:T(8,128)(2,1)}, u32[]{:S(2)}) copy-start(bf16[4,4096,96]{1,2,0:T(8,128)(2,1)} %param.21) | copy-start | bytes 9437188
  7.6 6.0 %copy-start.9 = (bf16[4,3,4096]{2,0,1:T(4,128)(2,1)S(1)}, bf16[4,3,4096]{2,0,1:T(4,128)(2,1)}, u32[]{:S(2)}) copy-start(bf16[4,3,4096]{2,0,1:T(4,128)(2,1)} %param.16) | copy-start | bytes 294916
  7.6 9.7 %copy-start = (bf16[4096,2048]{1,0:T(8,128)(2,1)S(1)}, bf16[4096,2048]{1,0:T(8,128)(2,1)}, u32[]{:S(2)}) copy-start(bf16[4096,2048]{1,0:T(8,128)(2,1)} %refs_9_.1) | copy-start | bytes 50331652
  7.6 9.7 %copy-start.2 = (bf16[4096,128]{1,0:T(8,128)(2,1)S(1)}, bf16[4096,128]{1,0:T(8,128)(2,1)}, u32[]{:S(2)}) copy-start(bf16[4096,128]{1,0:T(8,128)(2,1)} %refs_1_.3) | copy-start | bytes 3145732
  7.6 9.7 %copy-start.3 = (bf16[4096,128]{1,0:T(8,128)(2,1)S(1)}, bf16[4096,128]{1,0:T(8,128)(2,1)}, u32[]{:S(2)}) copy-start(bf16[4096,128]{1,0:T(8,128)(2,1)} %refs_2_.3) | copy-start | bytes 3145732
  8.3 12.3 %copy-start.8 = (bf16[4,32,2048]{2,1,0:T(8,128)(2,1)S(1)}, bf16[4,32,2048]{2,1,0:T(8,128)(2,1)}, u32[]{:S(2)}) copy-start(bf16[4,32,2048]{2,1,0:T(8,128)(2,1)} %param.22) | copy-start | bytes 1572868
  8.4 12.3 %copy-start.10 = (bf16[4,32,128]{2,1,0:T(8,128)(2,1)S(1)}, bf16[4,32,128]{2,1,0:T(8,128)(2,1)}, u32[]{:S(2)}) copy-start(bf16[4,32,128]{2,1,0:T(8,128)(2,1)} %param.23) | copy-start | bytes 98308
  8.4 12.3 %copy-start.11 = (bf16[4,32,128]{2,1,0:T(8,128)(2,1)S(1)}, bf16[4,32,128]{2,1,0:T(8,128)(2,1)}, u32[]{:S(2)}) copy-start(bf16[4,32,128]{2,1,0:T(8,128)(2,1)} %param.24) | copy-start | bytes 98308
  14.9 1.2 %collective-permute-start.3 = (bf16[32,128]{1,0:T(8,128)(2,1)S(1)}, bf16[32,128]{1,0:T(8,128)(2,1)S(1)}, u32[]{:S(2)}, u32[]{:S(2)}) collective-permute-start(bf16[32,128]{1,0:T(8,128)(2,1)S(1)} %get-tuple-element.22.left_ref), channel_id=1, source_target_pairs={{0,1},{1,0},{2,3},{3,2},{4,5},{5,4},{6,7},{7,6},{8,9},{9,8},{10,11... | collective-permute-start | bytes 24584 | tf_op jit(solution)/shard_map/ppermute | solution.py:392
  16.1 4.5 %collective-permute-start.5 = (bf16[32,128]{1,0:T(8,128)(2,1)S(1)}, bf16[32,128]{1,0:T(8,128)(2,1)S(1)}, u32[]{:S(2)}, u32[]{:S(2)}) collective-permute-start(bf16[32,128]{1,0:T(8,128)(2,1)S(1)} %shard_map.157), channel_id=1, source_target_pairs={{0,4},{1,12},{2,0},{3,8},{4,5},{5,13},{6,1},{7,9},{8,6},{9,14},{10... | collective-permute-start | bytes 24584 | tf_op jit(solution)/shard_map/ppermute | solution.py:401
  16.6 4.0 %collective-permute-start.4 = (bf16[32,128]{1,0:T(8,128)(2,1)S(1)}, bf16[32,128]{1,0:T(8,128)(2,1)S(1)}, u32[]{:S(2)}, u32[]{:S(2)}) collective-permute-start(bf16[32,128]{1,0:T(8,128)(2,1)S(1)} %shard_map.157), channel_id=1, source_target_pairs={{0,0},{1,8},{2,4},{3,12},{4,1},{5,9},{6,5},{7,13},{8,2},{9,10},{10... | collective-permute-start | bytes 24584 | tf_op jit(solution)/shard_map/ppermute | solution.py:401
  20.7 18.6 %copy-start.6 = (bf16[1,4,512,128]{3,2,1,0:T(8,128)(2,1)S(1)}, bf16[1,4,512,128]{3,2,1,0:T(8,128)(2,1)}, u32[]{:S(2)}) copy-start(bf16[1,4,512,128]{3,2,1,0:T(8,128)(2,1)} %keys_ref.1) | copy-start | bytes 1572868
  20.7 18.6 %copy-start.7 = (bf16[1,4,512,128]{3,2,1,0:T(8,128)(2,1)S(1)}, bf16[1,4,512,128]{3,2,1,0:T(8,128)(2,1)}, u32[]{:S(2)}) copy-start(bf16[1,4,512,128]{3,2,1,0:T(8,128)(2,1)} %values_ref.1) | copy-start | bytes 1572868
  20.7 32.0 %copy-start.5 = (bf16[4,2048,32]{1,2,0:T(8,128)(2,1)S(1)}, bf16[4,2048,32]{1,2,0:T(8,128)(2,1)}, u32[]{:S(2)}) copy-start(bf16[4,2048,32]{1,2,0:T(8,128)(2,1)} %param.25) | copy-start | bytes 1572868
  21.7 33.6 %slice-start = ((s8[16777216]{0:T(1024)(128)(4,1)}), s8[4194304]{0:T(1024)(128)(4,1)S(1)}, s32[]{:S(2)}) async-start(s8[16777216]{0:T(1024)(128)(4,1)} %bitcast.13), calls=%async_computation.1 | async-start | bytes 8388608
  41.1 4.5 %collective-permute-start.6 = (bf16[48,128]{1,0:T(8,128)(2,1)S(1)}, bf16[48,128]{1,0:T(8,128)(2,1)S(1)}, u32[]{:S(2)}, u32[]{:S(2)}) collective-permute-start(bf16[48,128]{1,0:T(8,128)(2,1)S(1)} %get-tuple-element.26), channel_id=1, source_target_pairs={{0,4},{4,0},{8,12},{12,8},{1,5},{5,1},{9,13},{13,9},{2,6},{6,2},{1... | collective-permute-start | bytes 36872 | tf_op jit(solution)/shard_map/ppermute | solution.py:386
  41.2 4.7 %collective-permute-start.7 = (bf16[48,128]{1,0:T(8,128)(2,1)S(1)}, bf16[48,128]{1,0:T(8,128)(2,1)S(1)}, u32[]{:S(2)}, u32[]{:S(2)}) collective-permute-start(bf16[48,128]{1,0:T(8,128)(2,1)S(1)} %get-tuple-element.27), channel_id=1, source_target_pairs={{0,8},{4,12},{8,0},{12,4},{1,9},{5,13},{9,1},{13,5},{2,10},{6,14},... | collective-permute-start | bytes 36872 | tf_op jit(solution)/shard_map/ppermute | solution.py:386
  42.6 5.5 %collective-permute-start.8 = (bf16[48,128]{1,0:T(8,128)(2,1)S(1)}, bf16[48,128]{1,0:T(8,128)(2,1)S(1)}, u32[]{:S(2)}, u32[]{:S(2)}) collective-permute-start(bf16[48,128]{1,0:T(8,128)(2,1)S(1)} %get-tuple-element.28), channel_id=1, source_target_pairs={{0,12},{4,8},{8,4},{12,0},{1,13},{5,9},{9,5},{13,1},{2,14},{6,10},... | collective-permute-start | bytes 36872 | tf_op jit(solution)/shard_map/ppermute | solution.py:386
  48.1 3.8 %collective-permute-start.11 = (bf16[4,48,128]{2,1,0:T(8,128)(2,1)S(1)}, bf16[4,48,128]{2,1,0:T(8,128)(2,1)S(1)}, u32[]{:S(2)}, u32[]{:S(2)}) collective-permute-start(bf16[4,48,128]{2,1,0:T(8,128)(2,1)S(1)} %shard_map.160.refs_0_), channel_id=1, source_target_pairs={{0,3},{1,2},{2,1},{3,0},{4,7},{5,6},{6,5},{7,4},{8,11},{9,10},{10,... | collective-permute-start | bytes 147464 | tf_op jit(solution)/shard_map/ppermute | solution.py:389
  48.1 4.6 %collective-permute-start.10 = (bf16[4,48,128]{2,1,0:T(8,128)(2,1)S(1)}, bf16[4,48,128]{2,1,0:T(8,128)(2,1)S(1)}, u32[]{:S(2)}, u32[]{:S(2)}) collective-permute-start(bf16[4,48,128]{2,1,0:T(8,128)(2,1)S(1)} %shard_map.160.refs_0_), channel_id=1, source_target_pairs={{0,2},{1,3},{2,0},{3,1},{4,6},{5,7},{6,4},{7,5},{8,10},{9,11},{10,... | collective-permute-start | bytes 147464 | tf_op jit(solution)/shard_map/ppermute | solution.py:389
  49.3 3.5 %collective-permute-start.9 = (bf16[4,48,128]{2,1,0:T(8,128)(2,1)S(1)}, bf16[4,48,128]{2,1,0:T(8,128)(2,1)S(1)}, u32[]{:S(2)}, u32[]{:S(2)}) collective-permute-start(bf16[4,48,128]{2,1,0:T(8,128)(2,1)S(1)} %shard_map.160.refs_0_), channel_id=1, source_target_pairs={{0,1},{1,0},{2,3},{3,2},{4,5},{5,4},{6,7},{7,6},{8,9},{9,8},{10,11... | collective-permute-start | bytes 147464 | tf_op jit(solution)/shard_map/ppermute | solution.py:389
  52.8 2.6 %slice-start.1 = ((s8[16777216]{0:T(1024)(128)(4,1)}), s8[4194304]{0:T(1024)(128)(4,1)S(1)}, s32[]{:S(2)}) async-start(s8[16777216]{0:T(1024)(128)(4,1)} %bitcast.13), calls=%async_computation.2 | async-start | bytes 8388608
  52.8 3.5 %slice-start.2 = ((s8[16777216]{0:T(1024)(128)(4,1)}), s8[4194304]{0:T(1024)(128)(4,1)S(1)}, s32[]{:S(2)}) async-start(s8[16777216]{0:T(1024)(128)(4,1)} %bitcast.13), calls=%async_computation.3 | async-start | bytes 8388608
  52.8 4.6 %slice-start.3 = ((s8[16777216]{0:T(1024)(128)(4,1)}), s8[4194304]{0:T(1024)(128)(4,1)S(1)}, s32[]{:S(2)}) async-start(s8[16777216]{0:T(1024)(128)(4,1)} %bitcast.13), calls=%async_computation.4 | async-start | bytes 8388608
  53.3 7.1 %copy-start.4 = (bf16[4,32,4096]{2,1,0:T(8,128)(2,1)S(1)}, bf16[4,32,4096]{2,1,0:T(8,128)(2,1)}, u32[]{:S(2)}) copy-start(bf16[4,32,4096]{2,1,0:T(8,128)(2,1)} %param.26) | copy-start | bytes 3145732
  53.3 7.1 %collective-permute-start.15 = (bf16[16,128]{1,0:T(8,128)(2,1)S(1)}, bf16[16,128]{1,0:T(8,128)(2,1)S(1)}, u32[]{:S(2)}, u32[]{:S(2)}) collective-permute-start(bf16[16,128]{1,0:T(8,128)(2,1)S(1)} %get-tuple-element.30), channel_id=1, source_target_pairs={{0,3},{1,7},{2,11},{3,15},{4,2},{5,6},{6,10},{7,14},{8,1},{9,5},{1... | collective-permute-start | bytes 12296 | tf_op jit(solution)/shard_map/ppermute | solution.py:409
  54.2 6.2 %collective-permute-start.14 = (bf16[16,128]{1,0:T(8,128)(2,1)S(1)}, bf16[16,128]{1,0:T(8,128)(2,1)S(1)}, u32[]{:S(2)}, u32[]{:S(2)}) collective-permute-start(bf16[16,128]{1,0:T(8,128)(2,1)S(1)} %get-tuple-element.30), channel_id=1, source_target_pairs={{0,2},{1,6},{2,10},{3,14},{4,3},{5,7},{6,11},{7,15},{8,0},{9,4},{1... | collective-permute-start | bytes 12296 | tf_op jit(solution)/shard_map/ppermute | solution.py:409
  54.5 5.9 %collective-permute-start.13 = (bf16[16,128]{1,0:T(8,128)(2,1)S(1)}, bf16[16,128]{1,0:T(8,128)(2,1)S(1)}, u32[]{:S(2)}, u32[]{:S(2)}) collective-permute-start(bf16[16,128]{1,0:T(8,128)(2,1)S(1)} %get-tuple-element.30), channel_id=1, source_target_pairs={{0,1},{1,5},{2,9},{3,13},{4,0},{5,4},{6,8},{7,12},{8,3},{9,7},{10,... | collective-permute-start | bytes 12296 | tf_op jit(solution)/shard_map/ppermute | solution.py:409
  54.5 5.9 %collective-permute-start.12 = (bf16[16,128]{1,0:T(8,128)(2,1)S(1)}, bf16[16,128]{1,0:T(8,128)(2,1)S(1)}, u32[]{:S(2)}, u32[]{:S(2)}) collective-permute-start(bf16[16,128]{1,0:T(8,128)(2,1)S(1)} %get-tuple-element.30), channel_id=1, source_target_pairs={{0,0},{1,4},{2,8},{3,12},{4,1},{5,5},{6,9},{7,13},{8,2},{9,6},{10,... | collective-permute-start | bytes 12296 | tf_op jit(solution)/shard_map/ppermute | solution.py:409
  61.1 7.0 %collective-permute-start.16 = (bf16[3,4,4096]{2,1,0:T(4,128)(2,1)S(1)}, bf16[3,4,4096]{2,1,0:T(4,128)(2,1)S(1)}, u32[]{:S(2)}, u32[]{:S(2)}) collective-permute-start(bf16[3,4,4096]{2,1,0:T(4,128)(2,1)S(1)} %get-tuple-element.32), channel_id=1, source_target_pairs={{0,4},{4,0},{8,12},{12,8},{1,5},{5,1},{9,13},{13,9},{2,6},{6,2},{1... | collective-permute-start | bytes 294920 | tf_op jit(solution)/shard_map/ppermute | solution.py:386
  63.9 11.2 %collective-permute-start.17 = (bf16[3,4,4096]{2,1,0:T(4,128)(2,1)S(1)}, bf16[3,4,4096]{2,1,0:T(4,128)(2,1)S(1)}, u32[]{:S(2)}, u32[]{:S(2)}) collective-permute-start(bf16[3,4,4096]{2,1,0:T(4,128)(2,1)S(1)} %get-tuple-element.33), channel_id=1, source_target_pairs={{0,8},{4,12},{8,0},{12,4},{1,9},{5,13},{9,1},{13,5},{2,10},{6,14},... | collective-permute-start | bytes 294920 | tf_op jit(solution)/shard_map/ppermute | solution.py:386
  67.2 7.8 %collective-permute-start.18 = (bf16[3,4,4096]{2,1,0:T(4,128)(2,1)S(1)}, bf16[3,4,4096]{2,1,0:T(4,128)(2,1)S(1)}, u32[]{:S(2)}, u32[]{:S(2)}) collective-permute-start(bf16[3,4,4096]{2,1,0:T(4,128)(2,1)S(1)} %get-tuple-element.34), channel_id=1, source_target_pairs={{0,12},{4,8},{8,4},{12,0},{1,13},{5,9},{9,5},{13,1},{2,14},{6,10},... | collective-permute-start | bytes 294920 | tf_op jit(solution)/shard_map/ppermute | solution.py:386

commit v17 on v15

--- a/solution.py
+++ b/solution.py
@@ -243,6 +243,7 @@
     count = out_ref.shape[1]
     scale = 1.0 / math.sqrt(head_size)
     fresh_s[...] = jnp.zeros(fresh_s.shape, jnp.float32)
+    scores = []
     for block in range(blocks):
         joined = arrived_ref[block * groups].astype(jnp.float32)
         for other in range(1, groups):
@@ -252,17 +253,21 @@
         fresh_s[2 * block, 0:drafts, :] = rotated[count : count + drafts]
         fresh_s[2 * block + 1, 0:drafts, :] = joined[count + drafts : count + 2 * drafts]
         query = rotated[0:count].astype(jnp.bfloat16)
-        old = dot_nt(query, keys_ref[0, block]) * scale
-        new = dot_nt(query, fresh_s[2 * block].astype(jnp.bfloat16)) * scale
-        old = jnp.where(iota(old.shape, 1) < length_ref[0], old, -jnp.inf)
-        seen = iota(new.shape, 1) <= lax.rem(iota(new.shape, 0), drafts)
-        new = jnp.where(seen, new, -jnp.inf)
-        peak = jnp.maximum(jnp.max(old, 1, keepdims=True), jnp.max(new, 1, keepdims=True))
-        old = jnp.exp(old - peak)
-        new = jnp.exp(new - peak)
-        below = jnp.sum(old, 1, keepdims=True) + jnp.sum(new, 1, keepdims=True)
-        mixed = dot((old / below).astype(jnp.bfloat16), values_ref[0, block]) + dot(
-            (new / below).astype(jnp.bfloat16), fresh_s[2 * block + 1].astype(jnp.bfloat16)
+        old = dot_nt(query, keys_ref[0, block])
+        new = dot_nt(query, fresh_s[2 * block].astype(jnp.bfloat16))
+        scores.append(jnp.concatenate([old, new], 1))
+    scores = jnp.concatenate(scores, 0) * scale
+    column = iota(scores.shape, 1)
+    limit = cache_size + lax.rem(iota((scores.shape[0], 1), 0), drafts)
+    seen = (column < length_ref[0]) | ((column >= cache_size) & (column <= limit))
+    scores = jnp.where(seen, scores, -jnp.inf)
+    scores = jnp.exp(scores - jnp.max(scores, 1, keepdims=True))
+    below = 1.0 / jnp.sum(scores, 1, keepdims=True)
+    probs = (scores * below).astype(jnp.bfloat16)
+    for block in range(blocks):
+        mine = probs[block * count : (block + 1) * count]
+        mixed = dot(mine[:, :cache_size], values_ref[0, block]) + dot(
+            mine[:, cache_size:], fresh_s[2 * block + 1].astype(jnp.bfloat16)
         )
         mixed = mixed.astype(jnp.bfloat16)
         for target in range(groups):
@@ -384,7 +389,7 @@
 
     def to_out_growers(value, shift):
         route = [
-            (t * groups + g, g * groups + (t + shift) % groups)
+            (t * groups + g, g * groups + (t ^ shift))
             for t in range(blocks)
             for g in range(groups)
         ]
@@ -460,7 +465,7 @@
         8 * count * out_cols + 2 * owned * width * out_cols,
     )(out_total, slots, grow_out.reshape(owned * width, -1), *out_ranks)
     result = leaving[0].astype(jnp.float32)
-    for shift in range(1, blocks):
+    for shift in sorted(range(1, blocks), key=lambda shift: shift < blocks // 2):
         result = result + over_tensor(leaving[shift], shift).astype(jnp.float32)
     return jnp.transpose(result.astype(jnp.bfloat16), (1, 0, 2))
 

time: 75 us -> 74 us (0.987)
  local copies, waits for them, and re-layouts: 2.35 us -> 3.89 us
  starting transfers between devices: 16.3 us -> 14.9 us
  Pallas kernels: 12.3 us -> 11.3 us
    unnamed x36, local copies, waits for them, and re-layouts: 2.35 us -> 3.89 us
    ppermute x4, starting transfers between devices: 3.09 us -> 1.56 us  [to_out_growers(): return lax.ppermute(value, EVERY, route)]
    pallas_call x1, Pallas kernels: 1.76 us -> 0.76 us  [by_kernels(): call(functools.partial(attend_kernel, sizes), shape((blocks * groups, que...]
  transfers between devices with their start and end apart: 13 -> 13, of which waited for: 4 -> 5; matrix products, arithmetic and copies ran while one was open for 0% -> 0% of each run, Pallas kernels for 9% -> 10%
where the time goes in v17:
time: 74 us; the launch traced here: 73.7 us
  blocking collectives  29.1 us (39%)
  starting transfers between devices  14.9 us (20%)
  waiting for transfers between devices  12.8 us (17%)
  Pallas kernels  11.3 us (15%)
  local copies, waits for them, and re-layouts  3.89 us (5%)
  between operations  0.91 us (1%)
  other arithmetic  0.75 us (1%)
    all_to_all x2, blocking collectives, exchange(): return lax.all_to_all(value, EVERY, split_axis=0, concat_axis=0, tiled=True)  29.1 us
    ppermute x6, starting transfers between devices, over_tensor(): return lax.ppermute(value, 'tensor', route)  12.2 us
    ppermute x6, waiting for transfers between devices, over_tensor(): return lax.ppermute(value, 'tensor', route)  11.6 us
    pallas_call x2, Pallas kernels, product(): call(product_kernel, shape((rows.shape[0], width), jnp.float32), [VMEM] *...  6.31 us
    unnamed x36, local copies, waits for them, and re-layouts  3.89 us
    ppermute x4, starting transfers between devices, to_out_growers(): return lax.ppermute(value, EVERY, route)  1.56 us
  transfers between devices with their start and end apart: 13, of which 5 were waited for; matrix products, arithmetic and copies ran while one was open for 0% of the time, Pallas kernels for 10%

profile of v17, /device:TPU:0, one launch (start us, length us, event | category | flops | bytes accessed | tf_op | source)
XLA Modules:
  0.0 73.7 jit_solution(7490605621944291246)
XLA Ops:
  0.0 5.0 %collective-permute-start.2 = (bf16[3,4,4096]{2,1,0:T(4,128)(2,1)}, bf16[3,4,4096]{2,1,0:T(4,128)(2,1)S(1)}, u32[]{:S(2)}, u32[]{:S(2)}) collective-permute-start(bf16[3,4,4096]{2,1,0:T(4,128)(2,1)} %bitcast.19), channel_id=1, source_target_pairs={{0,12},{4,8},{8,4},{12,0},{1,13},{5,9},{9,5},{13,1},{2,14},{6,10},... | collective-permute-start | bytes 294920 | tf_op jit(solution)/shard_map/ppermute | solution.py:376
  5.0 0.0 collective-permute-start.1
  5.1 0.6 collective-permute-start
  6.3 0.6 copy-done.12
  6.9 0.7 copy-done.13
  7.6 0.7 shard_map.154
  8.3 0.0 copy-start.8
  8.4 0.0 copy-start.10
  8.4 0.0 copy-start.11
  8.4 0.6 collective-permute-done.2.refs_3_
  9.0 4.6 %collective-permute-done.1.refs_2_ = bf16[3,4,4096]{2,1,0:T(4,128)(2,1)S(1)} collective-permute-done((bf16[3,4,4096]{2,1,0:T(4,128)(2,1)}, bf16[3,4,4096]{2,1,0:T(4,128)(2,1)S(1)}, u32[]{:S(2)}, u32[]{:S(2)}) %collective-permute-start.1) | collective-permute-done | bytes 98336 | tf_op jit(solution)/shard_map/ppermute | solution.py:376
  13.5 0.0 collective-permute-done.refs_1_
  13.5 1.4 %shard_map.155 = (bf16[48,4096]{1,0:T(8,128)(2,1)S(1)}, bf16[32,128]{1,0:T(8,128)(2,1)S(1)}) custom-call(bf16[3,4,4096]{2,1,0:T(4,128)(2,1)S(1)} %bitcast.22, bf16[3,4,4096]{2,1,0:T(4,128)(2,1)S(1)} %collective-permute-done.refs_1_, bf16[3,4,4096]{2,1,0:T(4,128)(2,1)S(1)} %collective-permute-done.1.refs_2_, ...), custom_call_target="tpu_custom_call" | custom-call | flops 150994944 | bytes 3932160 | tf_op jit(solution)/shard_map/pallas_call | solution.py:414
  14.9 0.0 collective-permute-start.3
  14.9 1.2 %collective-permute-done.3.right_ref = bf16[32,128]{1,0:T(8,128)(2,1)S(1)} collective-permute-done((bf16[32,128]{1,0:T(8,128)(2,1)S(1)}, bf16[32,128]{1,0:T(8,128)(2,1)S(1)}, u32[]{:S(2)}, u32[]{:S(2)}) %collective-permute-start.3) | collective-permute-done | bytes 8224 | tf_op jit(solution)/shard_map/ppermute | solution.py:379
  16.1 0.5 collective-permute-start.5
  16.6 0.6 collective-permute-start.4
  17.3 0.0 copy-done
  17.3 3.3 %shard_map.156.total_ref = f32[48,2304]{1,0:T(8,128)S(1)} custom-call(bf16[48,4096]{1,0:T(8,128)(2,1)S(1)} %get-tuple-element.17.rows_ref, bf16[4096,2048]{1,0:T(8,128)(2,1)S(1)} %copy-done, bf16[4096,128]{1,0:T(8,128)(2,1)S(1)} %copy-done.2, bf16[4096,128]{1,0:T(8,128)(2,1)S(1)} %copy-done.3), custom_call_target="tpu_custom_call" | custom-call | tf_op jit(solution)/shard_map/pallas_call | solution.py:152
  20.6 0.0 collective-permute-done.5.refs_1_
  20.7 0.0 collective-permute-done.4.refs_0_
  20.7 0.0 copy-start.6
  20.7 0.0 copy-start.7
  20.7 0.0 copy-start.5
  20.7 0.9 %shard_map.158 = bf16[16,56,128]{2,1,0:T(8,128)(2,1)S(1)} custom-call(f32[48,2304]{1,0:T(8,128)S(1)} %shard_map.156.total_ref, s32[48,128]{1,0:T(8,128)S(1)} %get-tuple-element.16.refs_5_.slots_ref, bf16[32,128]{1,0:T(8,128)(2,1)S(1)} %collective-permute-done.4.refs_0_, bf16[32,128]{1,0:T(8,128)(2,1)S(1)} %collective-permute-done.5.refs_1_, ...), custom_call_target="tpu_custom_call" | custom-call | tf_op jit(solution)/shard_map/pallas_call | solution.py:428
  21.7 17.4 %all_to_all.10.arrived_ref = bf16[16,56,128]{2,1,0:T(8,128)(2,1)S(1)} all-to-all(bf16[16,56,128]{2,1,0:T(8,128)(2,1)S(1)} %shard_map.158), channel_id=1, replica_groups=mesh['parts'=2,'tensor'=4,'dp'=2,'pipe'=2] {'tensor','dp','pipe'}, dimensions={0} | all-to-all | bytes 458752 | tf_op jit(solution)/shard_map/all_to_all | solution.py:402
  39.0 0.8 %shard_map.159 = bf16[16,48,128]{2,1,0:T(8,128)(2,1)S(1)} custom-call(bf16[16,56,128]{2,1,0:T(8,128)(2,1)S(1)} %all_to_all.10.arrived_ref, bf16[1,4,512,128]{3,2,1,0:T(8,128)(2,1)S(1)} %copy-done.6, bf16[1,4,512,128]{3,2,1,0:T(8,128)(2,1)S(1)} %copy-done.7, s32[1]{0:T(128)S(6)} %copy.17.length_ref, f32[56,128]{1,0:T(8,128)S(1)} %get-tuple-element.19.cosine_ref, ...), custom_call_target="tpu_custom_call" | custom-call | tf_op jit(solution)/shard_map/pallas_call | solution.py:441
  39.8 11.8 %all_to_all.11.got_ref = bf16[16,48,128]{2,1,0:T(8,128)(2,1)S(1)} all-to-all(bf16[16,48,128]{2,1,0:T(8,128)(2,1)S(1)} %shard_map.159), channel_id=1, replica_groups=mesh['parts'=2,'tensor'=4,'dp'=2,'pipe'=2] {'tensor','dp','pipe'}, dimensions={0} | all-to-all | bytes 393216 | tf_op jit(solution)/shard_map/all_to_all | solution.py:402
  51.6 0.6 shard_map.160
  52.1 0.0 collective-permute-start.9
  52.1 0.6 collective-permute-start.8
  52.7 0.2 collective-permute-start.7
  52.9 0.8 %collective-permute-start.6 = (bf16[16,128]{1,0:T(8,128)(2,1)S(1)}, bf16[16,128]{1,0:T(8,128)(2,1)S(1)}, u32[]{:S(2)}, u32[]{:S(2)}) collective-permute-start(bf16[16,128]{1,0:T(8,128)(2,1)S(1)} %get-tuple-element.22), channel_id=1, source_target_pairs={{0,0},{1,4},{2,8},{3,12},{4,1},{5,5},{6,9},{7,13},{8,2},{9,6},{10,... | collective-permute-start | bytes 12296 | tf_op jit(solution)/shard_map/ppermute | solution.py:396
  53.7 0.0 slice-done.1
  53.8 1.3 %slice-done.2 = s8[4194304]{0:T(1024)(128)(4,1)S(1)} async-done(((s8[16777216]{0:T(1024)(128)(4,1)}), s8[4194304]{0:T(1024)(128)(4,1)S(1)}, s32[]{:S(2)}) %slice-start.2) | async-done | bytes 4194328
  55.0 1.2 %slice-done.3 = s8[4194304]{0:T(1024)(128)(4,1)S(1)} async-done(((s8[16777216]{0:T(1024)(128)(4,1)}), s8[4194304]{0:T(1024)(128)(4,1)S(1)}, s32[]{:S(2)}) %slice-start.3) | async-done | bytes 4194328
  56.2 3.0 %shard_map.161.total_ref = f32[48,4096]{1,0:T(8,128)S(1)} custom-call(bf16[48,2048]{1,0:T(8,128)(2,1)S(1)} %get-tuple-element.21.rows_ref, bf16[2048,4096]{1,0:T(8,128)(2,1)S(1)} %bitcast.14), custom_call_target="tpu_custom_call" | custom-call | tf_op jit(solution)/shard_map/pallas_call | solution.py:152
  59.2 0.0 collective-permute-done.9.refs_3_
  59.3 0.0 collective-permute-done.8.refs_2_
  59.3 0.0 collective-permute-done.7.refs_1_
  59.3 0.0 collective-permute-done.6.refs_0_
  59.3 0.6 shard_map.162
  59.9 5.9 %collective-permute-start.10 = (bf16[3,4,4096]{2,1,0:T(4,128)(2,1)S(1)}, bf16[3,4,4096]{2,1,0:T(4,128)(2,1)S(1)}, u32[]{:S(2)}, u32[]{:S(2)}) collective-permute-start(bf16[3,4,4096]{2,1,0:T(4,128)(2,1)S(1)} %get-tuple-element.24), channel_id=1, source_target_pairs={{0,8},{4,12},{8,0},{12,4},{1,9},{5,13},{9,1},{13,5},{2,10},{6,14},... | collective-permute-start | bytes 294920 | tf_op jit(solution)/shard_map/ppermute | solution.py:376
  65.9 0.0 collective-permute-start.11
  65.9 0.6 collective-permute-start.12
  66.5 6.0 %collective-permute-done.10 = bf16[3,4,4096]{2,1,0:T(4,128)(2,1)S(1)} collective-permute-done((bf16[3,4,4096]{2,1,0:T(4,128)(2,1)S(1)}, bf16[3,4,4096]{2,1,0:T(4,128)(2,1)S(1)}, u32[]{:S(2)}, u32[]{:S(2)}) %collective-permute-start.10) | collective-permute-done | bytes 98336 | tf_op jit(solution)/shard_map/ppermute | solution.py:376
  72.5 0.5 collective-permute-done.12
  73.0 0.7 %fusion = bf16[4,3,4096]{2,0,1:T(4,128)(2,1)} fusion(bf16[3,4,4096]{2,1,0:T(4,128)(2,1)S(1)} %collective-permute-done.12, bf16[3,4,4096]{2,1,0:T(4,128)(2,1)S(1)} %collective-permute-done.11, bf16[3,4,4096]{2,1,0:T(4,128)(2,1)S(1)} %collective-permute-done.10, bf16[3,4,4096]{2,1,0:T(4,128)(2,1)S(1)} %get-tuple-element.23), kind=kLoop, calls=%fused_computation.1 | loop fusion | flops 393216 | bytes 491520 | tf_op jit(solution)/shard_map/transpose | solution.py:470
  (27 shorter events, 0.1 us)
Async XLA Ops:
  0.0 9.0 %collective-permute-start.2 = (bf16[3,4,4096]{2,1,0:T(4,128)(2,1)}, bf16[3,4,4096]{2,1,0:T(4,128)(2,1)S(1)}, u32[]{:S(2)}, u32[]{:S(2)}) collective-permute-start(bf16[3,4,4096]{2,1,0:T(4,128)(2,1)} %bitcast.19), channel_id=1, source_target_pairs={{0,12},{4,8},{8,4},{12,0},{1,13},{5,9},{9,5},{13,1},{2,14},{6,10},... | collective-permute-start | bytes 294920 | tf_op jit(solution)/shard_map/ppermute | solution.py:376
  5.0 8.5 %collective-permute-start.1 = (bf16[3,4,4096]{2,1,0:T(4,128)(2,1)}, bf16[3,4,4096]{2,1,0:T(4,128)(2,1)S(1)}, u32[]{:S(2)}, u32[]{:S(2)}) collective-permute-start(bf16[3,4,4096]{2,1,0:T(4,128)(2,1)} %bitcast.20), channel_id=1, source_target_pairs={{0,8},{4,12},{8,0},{12,4},{1,9},{5,13},{9,1},{13,5},{2,10},{6,14},... | collective-permute-start | bytes 294920 | tf_op jit(solution)/shard_map/ppermute | solution.py:376
  5.1 8.5 %collective-permute-start = (bf16[3,4,4096]{2,1,0:T(4,128)(2,1)}, bf16[3,4,4096]{2,1,0:T(4,128)(2,1)S(1)}, u32[]{:S(2)}, u32[]{:S(2)}) collective-permute-start(bf16[3,4,4096]{2,1,0:T(4,128)(2,1)} %bitcast.21), channel_id=1, source_target_pairs={{0,4},{4,0},{8,12},{12,8},{1,5},{5,1},{9,13},{13,9},{2,6},{6,2},{1... | collective-permute-start | bytes 294920 | tf_op jit(solution)/shard_map/ppermute | solution.py:376
  6.3 0.7 copy-start.12
  6.9 0.7 copy-start.13
  7.6 6.0 %copy-start.1 = (bf16[4,4096,96]{1,2,0:T(8,128)(2,1)S(1)}, bf16[4,4096,96]{1,2,0:T(8,128)(2,1)}, u32[]{:S(2)}) copy-start(bf16[4,4096,96]{1,2,0:T(8,128)(2,1)} %param.21) | copy-start | bytes 9437188
  7.6 6.0 %copy-start.9 = (bf16[4,3,4096]{2,0,1:T(4,128)(2,1)S(1)}, bf16[4,3,4096]{2,0,1:T(4,128)(2,1)}, u32[]{:S(2)}) copy-start(bf16[4,3,4096]{2,0,1:T(4,128)(2,1)} %param.16) | copy-start | bytes 294916
  7.6 9.7 %copy-start = (bf16[4096,2048]{1,0:T(8,128)(2,1)S(1)}, bf16[4096,2048]{1,0:T(8,128)(2,1)}, u32[]{:S(2)}) copy-start(bf16[4096,2048]{1,0:T(8,128)(2,1)} %refs_3_.1) | copy-start | bytes 50331652
  7.6 9.7 %copy-start.2 = (bf16[4096,128]{1,0:T(8,128)(2,1)S(1)}, bf16[4096,128]{1,0:T(8,128)(2,1)}, u32[]{:S(2)}) copy-start(bf16[4096,128]{1,0:T(8,128)(2,1)} %refs_1_.4) | copy-start | bytes 3145732
  7.6 9.7 %copy-start.3 = (bf16[4096,128]{1,0:T(8,128)(2,1)S(1)}, bf16[4096,128]{1,0:T(8,128)(2,1)}, u32[]{:S(2)}) copy-start(bf16[4096,128]{1,0:T(8,128)(2,1)} %refs_2_.4) | copy-start | bytes 3145732
  8.3 12.3 %copy-start.8 = (bf16[4,32,2048]{2,1,0:T(8,128)(2,1)S(1)}, bf16[4,32,2048]{2,1,0:T(8,128)(2,1)}, u32[]{:S(2)}) copy-start(bf16[4,32,2048]{2,1,0:T(8,128)(2,1)} %param.22) | copy-start | bytes 1572868
  8.4 12.3 %copy-start.10 = (bf16[4,32,128]{2,1,0:T(8,128)(2,1)S(1)}, bf16[4,32,128]{2,1,0:T(8,128)(2,1)}, u32[]{:S(2)}) copy-start(bf16[4,32,128]{2,1,0:T(8,128)(2,1)} %param.23) | copy-start | bytes 98308
  8.4 12.3 %copy-start.11 = (bf16[4,32,128]{2,1,0:T(8,128)(2,1)S(1)}, bf16[4,32,128]{2,1,0:T(8,128)(2,1)}, u32[]{:S(2)}) copy-start(bf16[4,32,128]{2,1,0:T(8,128)(2,1)} %param.24) | copy-start | bytes 98308
  14.9 1.2 %collective-permute-start.3 = (bf16[32,128]{1,0:T(8,128)(2,1)S(1)}, bf16[32,128]{1,0:T(8,128)(2,1)S(1)}, u32[]{:S(2)}, u32[]{:S(2)}) collective-permute-start(bf16[32,128]{1,0:T(8,128)(2,1)S(1)} %get-tuple-element.18.left_ref), channel_id=1, source_target_pairs={{0,1},{1,0},{2,3},{3,2},{4,5},{5,4},{6,7},{7,6},{8,9},{9,8},{10,11... | collective-permute-start | bytes 24584 | tf_op jit(solution)/shard_map/ppermute | solution.py:379
  16.1 4.5 %collective-permute-start.5 = (bf16[32,128]{1,0:T(8,128)(2,1)S(1)}, bf16[32,128]{1,0:T(8,128)(2,1)S(1)}, u32[]{:S(2)}, u32[]{:S(2)}) collective-permute-start(bf16[32,128]{1,0:T(8,128)(2,1)S(1)} %shard_map.157), channel_id=1, source_target_pairs={{0,4},{1,12},{2,0},{3,8},{4,5},{5,13},{6,1},{7,9},{8,6},{9,14},{10... | collective-permute-start | bytes 24584 | tf_op jit(solution)/shard_map/ppermute | solution.py:388
  16.6 4.0 %collective-permute-start.4 = (bf16[32,128]{1,0:T(8,128)(2,1)S(1)}, bf16[32,128]{1,0:T(8,128)(2,1)S(1)}, u32[]{:S(2)}, u32[]{:S(2)}) collective-permute-start(bf16[32,128]{1,0:T(8,128)(2,1)S(1)} %shard_map.157), channel_id=1, source_target_pairs={{0,0},{1,8},{2,4},{3,12},{4,1},{5,9},{6,5},{7,13},{8,2},{9,10},{10... | collective-permute-start | bytes 24584 | tf_op jit(solution)/shard_map/ppermute | solution.py:388
  20.7 18.3 %copy-start.6 = (bf16[1,4,512,128]{3,2,1,0:T(8,128)(2,1)S(1)}, bf16[1,4,512,128]{3,2,1,0:T(8,128)(2,1)}, u32[]{:S(2)}) copy-start(bf16[1,4,512,128]{3,2,1,0:T(8,128)(2,1)} %keys_ref.1) | copy-start | bytes 1572868
  20.7 18.3 %copy-start.7 = (bf16[1,4,512,128]{3,2,1,0:T(8,128)(2,1)S(1)}, bf16[1,4,512,128]{3,2,1,0:T(8,128)(2,1)}, u32[]{:S(2)}) copy-start(bf16[1,4,512,128]{3,2,1,0:T(8,128)(2,1)} %values_ref.1) | copy-start | bytes 1572868
  20.7 30.9 %copy-start.5 = (bf16[4,2048,32]{1,2,0:T(8,128)(2,1)S(1)}, bf16[4,2048,32]{1,2,0:T(8,128)(2,1)}, u32[]{:S(2)}) copy-start(bf16[4,2048,32]{1,2,0:T(8,128)(2,1)} %param.25) | copy-start | bytes 1572868
  39.0 14.7 %slice-start = ((s8[16777216]{0:T(1024)(128)(4,1)}), s8[4194304]{0:T(1024)(128)(4,1)S(1)}, s32[]{:S(2)}) async-start(s8[16777216]{0:T(1024)(128)(4,1)} %bitcast.13), calls=%async_computation.2 | async-start | bytes 8388608
  51.6 2.2 %slice-start.1 = ((s8[16777216]{0:T(1024)(128)(4,1)}), s8[4194304]{0:T(1024)(128)(4,1)S(1)}, s32[]{:S(2)}) async-start(s8[16777216]{0:T(1024)(128)(4,1)} %bitcast.13), calls=%async_computation.3 | async-start | bytes 8388608
  51.6 3.5 %slice-start.2 = ((s8[16777216]{0:T(1024)(128)(4,1)}), s8[4194304]{0:T(1024)(128)(4,1)S(1)}, s32[]{:S(2)}) async-start(s8[16777216]{0:T(1024)(128)(4,1)} %bitcast.13), calls=%async_computation.4 | async-start | bytes 8388608
  51.6 4.7 %slice-start.3 = ((s8[16777216]{0:T(1024)(128)(4,1)}), s8[4194304]{0:T(1024)(128)(4,1)S(1)}, s32[]{:S(2)}) async-start(s8[16777216]{0:T(1024)(128)(4,1)} %bitcast.13), calls=%async_computation.5 | async-start | bytes 8388608
  52.1 7.2 %copy-start.4 = (bf16[4,32,4096]{2,1,0:T(8,128)(2,1)S(1)}, bf16[4,32,4096]{2,1,0:T(8,128)(2,1)}, u32[]{:S(2)}) copy-start(bf16[4,32,4096]{2,1,0:T(8,128)(2,1)} %param.26) | copy-start | bytes 3145732
  52.1 7.1 %collective-permute-start.9 = (bf16[16,128]{1,0:T(8,128)(2,1)S(1)}, bf16[16,128]{1,0:T(8,128)(2,1)S(1)}, u32[]{:S(2)}, u32[]{:S(2)}) collective-permute-start(bf16[16,128]{1,0:T(8,128)(2,1)S(1)} %get-tuple-element.22), channel_id=1, source_target_pairs={{0,3},{1,7},{2,11},{3,15},{4,2},{5,6},{6,10},{7,14},{8,1},{9,5},{1... | collective-permute-start | bytes 12296 | tf_op jit(solution)/shard_map/ppermute | solution.py:396
  52.1 7.1 %collective-permute-start.8 = (bf16[16,128]{1,0:T(8,128)(2,1)S(1)}, bf16[16,128]{1,0:T(8,128)(2,1)S(1)}, u32[]{:S(2)}, u32[]{:S(2)}) collective-permute-start(bf16[16,128]{1,0:T(8,128)(2,1)S(1)} %get-tuple-element.22), channel_id=1, source_target_pairs={{0,2},{1,6},{2,10},{3,14},{4,3},{5,7},{6,11},{7,15},{8,0},{9,4},{1... | collective-permute-start | bytes 12296 | tf_op jit(solution)/shard_map/ppermute | solution.py:396
  52.7 6.5 %collective-permute-start.7 = (bf16[16,128]{1,0:T(8,128)(2,1)S(1)}, bf16[16,128]{1,0:T(8,128)(2,1)S(1)}, u32[]{:S(2)}, u32[]{:S(2)}) collective-permute-start(bf16[16,128]{1,0:T(8,128)(2,1)S(1)} %get-tuple-element.22), channel_id=1, source_target_pairs={{0,1},{1,5},{2,9},{3,13},{4,0},{5,4},{6,8},{7,12},{8,3},{9,7},{10,... | collective-permute-start | bytes 12296 | tf_op jit(solution)/shard_map/ppermute | solution.py:396
  52.9 6.4 %collective-permute-start.6 = (bf16[16,128]{1,0:T(8,128)(2,1)S(1)}, bf16[16,128]{1,0:T(8,128)(2,1)S(1)}, u32[]{:S(2)}, u32[]{:S(2)}) collective-permute-start(bf16[16,128]{1,0:T(8,128)(2,1)S(1)} %get-tuple-element.22), channel_id=1, source_target_pairs={{0,0},{1,4},{2,8},{3,12},{4,1},{5,5},{6,9},{7,13},{8,2},{9,6},{10,... | collective-permute-start | bytes 12296 | tf_op jit(solution)/shard_map/ppermute | solution.py:396
  59.9 12.6 %collective-permute-start.10 = (bf16[3,4,4096]{2,1,0:T(4,128)(2,1)S(1)}, bf16[3,4,4096]{2,1,0:T(4,128)(2,1)S(1)}, u32[]{:S(2)}, u32[]{:S(2)}) collective-permute-start(bf16[3,4,4096]{2,1,0:T(4,128)(2,1)S(1)} %get-tuple-element.24), channel_id=1, source_target_pairs={{0,8},{4,12},{8,0},{12,4},{1,9},{5,13},{9,1},{13,5},{2,10},{6,14},... | collective-permute-start | bytes 294920 | tf_op jit(solution)/shard_map/ppermute | solution.py:376
  65.9 6.6 %collective-permute-start.11 = (bf16[3,4,4096]{2,1,0:T(4,128)(2,1)S(1)}, bf16[3,4,4096]{2,1,0:T(4,128)(2,1)S(1)}, u32[]{:S(2)}, u32[]{:S(2)}) collective-permute-start(bf16[3,4,4096]{2,1,0:T(4,128)(2,1)S(1)} %get-tuple-element.25), channel_id=1, source_target_pairs={{0,12},{4,8},{8,4},{12,0},{1,13},{5,9},{9,5},{13,1},{2,14},{6,10},... | collective-permute-start | bytes 294920 | tf_op jit(solution)/shard_map/ppermute | solution.py:376
  65.9 7.1 %collective-permute-start.12 = (bf16[3,4,4096]{2,1,0:T(4,128)(2,1)S(1)}, bf16[3,4,4096]{2,1,0:T(4,128)(2,1)S(1)}, u32[]{:S(2)}, u32[]{:S(2)}) collective-permute-start(bf16[3,4,4096]{2,1,0:T(4,128)(2,1)S(1)} %get-tuple-element.26), channel_id=1, source_target_pairs={{0,4},{4,0},{8,12},{12,8},{1,5},{5,1},{9,13},{13,9},{2,6},{6,2},{1... | collective-permute-start | bytes 294920 | tf_op jit(solution)/shard_map/ppermute | solution.py:376

commit v18 on v17

--- a/solution.py
+++ b/solution.py
@@ -316,7 +316,7 @@
 
 def out_grow_kernel(sizes, width, total_ref, slots_ref, grow_ref, *refs):
     groups, blocks, drafts = sizes
-    ranks_in, outs = refs[:blocks], refs[blocks:]
+    ranks_in, outs = refs[:2], refs[2:]
     owned = grow_ref.shape[0] // width
     me = lax.axis_index("tensor")
     ranks = ranks_in[0][...].astype(jnp.float32)
@@ -387,9 +387,9 @@
         ]
         return lax.ppermute(value, EVERY, route)
 
-    def to_out_growers(value, shift):
+    def to_out_growers(value, flip):
         route = [
-            (t * groups + g, g * groups + (t ^ shift))
+            (t * groups + g, g * groups + 2 * (t % 2) + ((t // 2) ^ flip))
             for t in range(blocks)
             for g in range(groups)
         ]
@@ -453,13 +453,14 @@
         [pltpu.VMEM((blocks * groups * query_lines, head_size), jnp.float32)],
         limit=40 * MIB,
     )(gathered, jnp.transpose(shrink_out, (0, 2, 1)).reshape(-1, head_cols), slots, *[w_query] * 4)
-    out_ranks = [to_out_growers(out_part, shift) for shift in range(blocks)]
+    out_part = added(out_part, over_tensor(out_part, 1))
+    out_ranks = [to_out_growers(out_part, flip) for flip in range(2)]
     out_total = product(out_rows, w_out)
     out_cols = out_total.shape[1]
     leaving = call(
         functools.partial(out_grow_kernel, sizes, width),
         [shape((drafts, groups, out_cols))] * blocks,
-        [VMEM] * (3 + blocks),
+        [VMEM] * 5,
         [],
         2 * count * owned * width * out_cols,
         8 * count * out_cols + 2 * owned * width * out_cols,

time: 74 us -> 74.2 us (level)
  waiting for transfers between devices: 12.8 us -> 16.7 us
  local copies, waits for them, and re-layouts: 3.89 us -> 1.38 us
  starting transfers between devices: 14.9 us -> 13.9 us
    ppermute x6 -> x7, waiting for transfers between devices: 11.6 us -> 14.7 us  [over_tensor(): return lax.ppermute(value, 'tensor', route)]
    unnamed x36, local copies, waits for them, and re-layouts: 3.89 us -> 1.38 us
    ppermute x4 -> x2, starting transfers between devices: 1.56 us -> 0.66 us  [to_out_growers(): return lax.ppermute(value, EVERY, route)]
    ppermute x4 -> x2, waiting for transfers between devices: 0.02 us -> 0.81 us  [to_out_growers(): return lax.ppermute(value, EVERY, route)]
    ppermute x6 -> x7, starting transfers between devices: 12.2 us -> 12 us  [over_tensor(): return lax.ppermute(value, 'tensor', route)]
  transfers between devices with their start and end apart: 13 -> 12, of which waited for: 5 -> 7; matrix products, arithmetic and copies ran while one was open for 0% -> 0% of each run, Pallas kernels for 10% -> 10%
where the time goes in v18:
time: 74.2 us; the launch traced here: 74 us
  blocking collectives  29.1 us (39%)
  waiting for transfers between devices  16.7 us (23%)
  starting transfers between devices  13.9 us (19%)
  Pallas kernels  11.3 us (15%)
  local copies, waits for them, and re-layouts  1.38 us (2%)
  between operations  0.91 us (1%)
  other arithmetic  0.75 us (1%)
    all_to_all x2, blocking collectives, exchange(): return lax.all_to_all(value, EVERY, split_axis=0, concat_axis=0, tiled=True)  29.1 us
    ppermute x7, waiting for transfers between devices, over_tensor(): return lax.ppermute(value, 'tensor', route)  14.7 us
    ppermute x7, starting transfers between devices, over_tensor(): return lax.ppermute(value, 'tensor', route)  12 us
    pallas_call x2, Pallas kernels, product(): call(product_kernel, shape((rows.shape[0], width), jnp.float32), [VMEM] *...  6.31 us
  transfers between devices with their start and end apart: 12, of which 7 were waited for; matrix products, arithmetic and copies ran while one was open for 0% of the time, Pallas kernels for 10%

profile of v18, /device:TPU:0, one launch (start us, length us, event | category | flops | bytes accessed | tf_op | source)
XLA Modules:
  0.0 74.0 jit_solution(7143449578403433677)
XLA Ops:
  0.0 5.0 %collective-permute-start.2 = (bf16[3,4,4096]{2,1,0:T(4,128)(2,1)}, bf16[3,4,4096]{2,1,0:T(4,128)(2,1)S(1)}, u32[]{:S(2)}, u32[]{:S(2)}) collective-permute-start(bf16[3,4,4096]{2,1,0:T(4,128)(2,1)} %bitcast.19), channel_id=1, source_target_pairs={{0,12},{4,8},{8,4},{12,0},{1,13},{5,9},{9,5},{13,1},{2,14},{6,10},... | collective-permute-start | bytes 294920 | tf_op jit(solution)/shard_map/ppermute | solution.py:376
  5.0 0.0 collective-permute-start.1
  5.1 0.6 collective-permute-start
  6.3 0.6 copy-done.12
  6.9 0.7 copy-done.13
  7.6 0.7 shard_map.154
  8.3 0.0 copy-start.8
  8.4 0.0 copy-start.10
  8.4 0.0 copy-start.11
  8.4 0.6 collective-permute-done.2.refs_3_
  9.0 4.6 %collective-permute-done.1.refs_2_ = bf16[3,4,4096]{2,1,0:T(4,128)(2,1)S(1)} collective-permute-done((bf16[3,4,4096]{2,1,0:T(4,128)(2,1)}, bf16[3,4,4096]{2,1,0:T(4,128)(2,1)S(1)}, u32[]{:S(2)}, u32[]{:S(2)}) %collective-permute-start.1) | collective-permute-done | bytes 98336 | tf_op jit(solution)/shard_map/ppermute | solution.py:376
  13.5 0.0 collective-permute-done.refs_1_
  13.5 0.0 copy-done.9
  13.5 1.4 %shard_map.155 = (bf16[48,4096]{1,0:T(8,128)(2,1)S(1)}, bf16[32,128]{1,0:T(8,128)(2,1)S(1)}) custom-call(bf16[3,4,4096]{2,1,0:T(4,128)(2,1)S(1)} %bitcast.22, bf16[3,4,4096]{2,1,0:T(4,128)(2,1)S(1)} %collective-permute-done.refs_1_, bf16[3,4,4096]{2,1,0:T(4,128)(2,1)S(1)} %collective-permute-done.1.refs_2_, ...), custom_call_target="tpu_custom_call" | custom-call | flops 150994944 | bytes 3932160 | tf_op jit(solution)/shard_map/pallas_call | solution.py:414
  14.9 0.0 collective-permute-start.3
  14.9 1.2 %collective-permute-done.3.right_ref = bf16[32,128]{1,0:T(8,128)(2,1)S(1)} collective-permute-done((bf16[32,128]{1,0:T(8,128)(2,1)S(1)}, bf16[32,128]{1,0:T(8,128)(2,1)S(1)}, u32[]{:S(2)}, u32[]{:S(2)}) %collective-permute-start.3) | collective-permute-done | bytes 8224 | tf_op jit(solution)/shard_map/ppermute | solution.py:379
  16.1 0.5 collective-permute-start.5
  16.6 0.6 collective-permute-start.4
  17.3 0.0 copy-done
  17.3 3.3 %shard_map.156.total_ref = f32[48,2304]{1,0:T(8,128)S(1)} custom-call(bf16[48,4096]{1,0:T(8,128)(2,1)S(1)} %get-tuple-element.17.rows_ref, bf16[4096,2048]{1,0:T(8,128)(2,1)S(1)} %copy-done, bf16[4096,128]{1,0:T(8,128)(2,1)S(1)} %copy-done.2, bf16[4096,128]{1,0:T(8,128)(2,1)S(1)} %copy-done.3), custom_call_target="tpu_custom_call" | custom-call | tf_op jit(solution)/shard_map/pallas_call | solution.py:152
  20.6 0.0 collective-permute-done.5.refs_1_
  20.7 0.0 collective-permute-done.4.refs_0_
  20.7 0.0 copy-start.6
  20.7 0.0 copy-start.7
  20.7 0.0 copy-start.5
  20.7 0.9 %shard_map.158 = bf16[16,56,128]{2,1,0:T(8,128)(2,1)S(1)} custom-call(f32[48,2304]{1,0:T(8,128)S(1)} %shard_map.156.total_ref, s32[48,128]{1,0:T(8,128)S(1)} %get-tuple-element.16.refs_5_.slots_ref, bf16[32,128]{1,0:T(8,128)(2,1)S(1)} %collective-permute-done.4.refs_0_, bf16[32,128]{1,0:T(8,128)(2,1)S(1)} %collective-permute-done.5.refs_1_, ...), custom_call_target="tpu_custom_call" | custom-call | tf_op jit(solution)/shard_map/pallas_call | solution.py:428
  21.7 17.4 %all_to_all.10.arrived_ref = bf16[16,56,128]{2,1,0:T(8,128)(2,1)S(1)} all-to-all(bf16[16,56,128]{2,1,0:T(8,128)(2,1)S(1)} %shard_map.158), channel_id=1, replica_groups=mesh['parts'=2,'tensor'=4,'dp'=2,'pipe'=2] {'tensor','dp','pipe'}, dimensions={0} | all-to-all | bytes 458752 | tf_op jit(solution)/shard_map/all_to_all | solution.py:402
  39.0 0.8 %shard_map.159 = bf16[16,48,128]{2,1,0:T(8,128)(2,1)S(1)} custom-call(bf16[16,56,128]{2,1,0:T(8,128)(2,1)S(1)} %all_to_all.10.arrived_ref, bf16[1,4,512,128]{3,2,1,0:T(8,128)(2,1)S(1)} %copy-done.6, bf16[1,4,512,128]{3,2,1,0:T(8,128)(2,1)S(1)} %copy-done.7, s32[1]{0:T(128)S(6)} %copy.17.length_ref, f32[56,128]{1,0:T(8,128)S(1)} %get-tuple-element.19.cosine_ref, ...), custom_call_target="tpu_custom_call" | custom-call | tf_op jit(solution)/shard_map/pallas_call | solution.py:441
  39.8 11.8 %all_to_all.11.got_ref = bf16[16,48,128]{2,1,0:T(8,128)(2,1)S(1)} all-to-all(bf16[16,48,128]{2,1,0:T(8,128)(2,1)S(1)} %shard_map.159), channel_id=1, replica_groups=mesh['parts'=2,'tensor'=4,'dp'=2,'pipe'=2] {'tensor','dp','pipe'}, dimensions={0} | all-to-all | bytes 393216 | tf_op jit(solution)/shard_map/all_to_all | solution.py:402
  51.6 0.6 shard_map.160
  52.1 0.0 collective-permute-start.6
  52.1 3.6 %collective-permute-done.6.right_ref = bf16[16,128]{1,0:T(8,128)(2,1)S(1)} collective-permute-done((bf16[16,128]{1,0:T(8,128)(2,1)S(1)}, bf16[16,128]{1,0:T(8,128)(2,1)S(1)}, u32[]{:S(2)}, u32[]{:S(2)}) %collective-permute-start.6) | collective-permute-done | bytes 4128 | tf_op jit(solution)/shard_map/ppermute | solution.py:376
  55.8 0.0 collective-permute-start.8
  55.8 0.7 collective-permute-start.7
  56.4 0.0 slice-done
  56.5 0.0 slice-done.1
  56.5 0.0 slice-done.2
  56.5 3.0 %shard_map.161.total_ref = f32[48,4096]{1,0:T(8,128)S(1)} custom-call(bf16[48,2048]{1,0:T(8,128)(2,1)S(1)} %get-tuple-element.21.rows_ref, bf16[2048,4096]{1,0:T(8,128)(2,1)S(1)} %bitcast.14), custom_call_target="tpu_custom_call" | custom-call | tf_op jit(solution)/shard_map/pallas_call | solution.py:152
  59.5 0.8 %collective-permute-done.8.refs_1_ = bf16[16,128]{1,0:T(8,128)(2,1)S(1)} collective-permute-done((bf16[16,128]{1,0:T(8,128)(2,1)S(1)}, bf16[16,128]{1,0:T(8,128)(2,1)S(1)}, u32[]{:S(2)}, u32[]{:S(2)}) %collective-permute-start.8) | collective-permute-done | bytes 4128 | tf_op jit(solution)/shard_map/ppermute | solution.py:396
  60.3 0.0 collective-permute-done.7.refs_0_
  60.3 0.6 shard_map.163
  60.9 5.8 %collective-permute-start.9 = (bf16[3,4,4096]{2,1,0:T(4,128)(2,1)S(1)}, bf16[3,4,4096]{2,1,0:T(4,128)(2,1)S(1)}, u32[]{:S(2)}, u32[]{:S(2)}) collective-permute-start(bf16[3,4,4096]{2,1,0:T(4,128)(2,1)S(1)} %get-tuple-element.24), channel_id=1, source_target_pairs={{0,8},{4,12},{8,0},{12,4},{1,9},{5,13},{9,1},{13,5},{2,10},{6,14},... | collective-permute-start | bytes 294920 | tf_op jit(solution)/shard_map/ppermute | solution.py:376
  66.7 0.0 collective-permute-start.10
  66.7 0.6 collective-permute-start.11
  67.4 4.1 %collective-permute-done.9 = bf16[3,4,4096]{2,1,0:T(4,128)(2,1)S(1)} collective-permute-done((bf16[3,4,4096]{2,1,0:T(4,128)(2,1)S(1)}, bf16[3,4,4096]{2,1,0:T(4,128)(2,1)S(1)}, u32[]{:S(2)}, u32[]{:S(2)}) %collective-permute-start.9) | collective-permute-done | bytes 98336 | tf_op jit(solution)/shard_map/ppermute | solution.py:376
  71.5 1.8 %collective-permute-done.10 = bf16[3,4,4096]{2,1,0:T(4,128)(2,1)S(1)} collective-permute-done((bf16[3,4,4096]{2,1,0:T(4,128)(2,1)S(1)}, bf16[3,4,4096]{2,1,0:T(4,128)(2,1)S(1)}, u32[]{:S(2)}, u32[]{:S(2)}) %collective-permute-start.10) | collective-permute-done | bytes 98336 | tf_op jit(solution)/shard_map/ppermute | solution.py:376
  73.2 0.0 collective-permute-done.11
  73.2 0.7 %fusion = bf16[4,3,4096]{2,0,1:T(4,128)(2,1)} fusion(bf16[3,4,4096]{2,1,0:T(4,128)(2,1)S(1)} %collective-permute-done.11, bf16[3,4,4096]{2,1,0:T(4,128)(2,1)S(1)} %collective-permute-done.10, bf16[3,4,4096]{2,1,0:T(4,128)(2,1)S(1)} %collective-permute-done.9, bf16[3,4,4096]{2,1,0:T(4,128)(2,1)S(1)} %get-tuple-element.23), kind=kLoop, calls=%fused_computation.1 | loop fusion | flops 393216 | bytes 491520 | tf_op jit(solution)/shard_map/transpose | solution.py:471
  (26 shorter events, 0.1 us)
Async XLA Ops:
  0.0 9.0 %collective-permute-start.2 = (bf16[3,4,4096]{2,1,0:T(4,128)(2,1)}, bf16[3,4,4096]{2,1,0:T(4,128)(2,1)S(1)}, u32[]{:S(2)}, u32[]{:S(2)}) collective-permute-start(bf16[3,4,4096]{2,1,0:T(4,128)(2,1)} %bitcast.19), channel_id=1, source_target_pairs={{0,12},{4,8},{8,4},{12,0},{1,13},{5,9},{9,5},{13,1},{2,14},{6,10},... | collective-permute-start | bytes 294920 | tf_op jit(solution)/shard_map/ppermute | solution.py:376
  5.0 8.5 %collective-permute-start.1 = (bf16[3,4,4096]{2,1,0:T(4,128)(2,1)}, bf16[3,4,4096]{2,1,0:T(4,128)(2,1)S(1)}, u32[]{:S(2)}, u32[]{:S(2)}) collective-permute-start(bf16[3,4,4096]{2,1,0:T(4,128)(2,1)} %bitcast.20), channel_id=1, source_target_pairs={{0,8},{4,12},{8,0},{12,4},{1,9},{5,13},{9,1},{13,5},{2,10},{6,14},... | collective-permute-start | bytes 294920 | tf_op jit(solution)/shard_map/ppermute | solution.py:376
  5.1 8.5 %collective-permute-start = (bf16[3,4,4096]{2,1,0:T(4,128)(2,1)}, bf16[3,4,4096]{2,1,0:T(4,128)(2,1)S(1)}, u32[]{:S(2)}, u32[]{:S(2)}) collective-permute-start(bf16[3,4,4096]{2,1,0:T(4,128)(2,1)} %bitcast.21), channel_id=1, source_target_pairs={{0,4},{4,0},{8,12},{12,8},{1,5},{5,1},{9,13},{13,9},{2,6},{6,2},{1... | collective-permute-start | bytes 294920 | tf_op jit(solution)/shard_map/ppermute | solution.py:376
  6.3 0.7 copy-start.12
  6.9 0.7 copy-start.13
  7.6 6.0 %copy-start.1 = (bf16[4,4096,96]{1,2,0:T(8,128)(2,1)S(1)}, bf16[4,4096,96]{1,2,0:T(8,128)(2,1)}, u32[]{:S(2)}) copy-start(bf16[4,4096,96]{1,2,0:T(8,128)(2,1)} %param.21) | copy-start | bytes 9437188
  7.6 6.0 %copy-start.9 = (bf16[4,3,4096]{2,0,1:T(4,128)(2,1)S(1)}, bf16[4,3,4096]{2,0,1:T(4,128)(2,1)}, u32[]{:S(2)}) copy-start(bf16[4,3,4096]{2,0,1:T(4,128)(2,1)} %param.16) | copy-start | bytes 294916
  7.6 9.7 %copy-start = (bf16[4096,2048]{1,0:T(8,128)(2,1)S(1)}, bf16[4096,2048]{1,0:T(8,128)(2,1)}, u32[]{:S(2)}) copy-start(bf16[4096,2048]{1,0:T(8,128)(2,1)} %refs_3_.1) | copy-start | bytes 50331652
  7.6 9.7 %copy-start.2 = (bf16[4096,128]{1,0:T(8,128)(2,1)S(1)}, bf16[4096,128]{1,0:T(8,128)(2,1)}, u32[]{:S(2)}) copy-start(bf16[4096,128]{1,0:T(8,128)(2,1)} %refs_1_.4) | copy-start | bytes 3145732
  7.6 9.7 %copy-start.3 = (bf16[4096,128]{1,0:T(8,128)(2,1)S(1)}, bf16[4096,128]{1,0:T(8,128)(2,1)}, u32[]{:S(2)}) copy-start(bf16[4096,128]{1,0:T(8,128)(2,1)} %refs_2_.4) | copy-start | bytes 3145732
  8.3 12.3 %copy-start.8 = (bf16[4,32,2048]{2,1,0:T(8,128)(2,1)S(1)}, bf16[4,32,2048]{2,1,0:T(8,128)(2,1)}, u32[]{:S(2)}) copy-start(bf16[4,32,2048]{2,1,0:T(8,128)(2,1)} %param.22) | copy-start | bytes 1572868
  8.4 12.3 %copy-start.10 = (bf16[4,32,128]{2,1,0:T(8,128)(2,1)S(1)}, bf16[4,32,128]{2,1,0:T(8,128)(2,1)}, u32[]{:S(2)}) copy-start(bf16[4,32,128]{2,1,0:T(8,128)(2,1)} %param.23) | copy-start | bytes 98308
  8.4 12.3 %copy-start.11 = (bf16[4,32,128]{2,1,0:T(8,128)(2,1)S(1)}, bf16[4,32,128]{2,1,0:T(8,128)(2,1)}, u32[]{:S(2)}) copy-start(bf16[4,32,128]{2,1,0:T(8,128)(2,1)} %param.24) | copy-start | bytes 98308
  14.9 1.2 %collective-permute-start.3 = (bf16[32,128]{1,0:T(8,128)(2,1)S(1)}, bf16[32,128]{1,0:T(8,128)(2,1)S(1)}, u32[]{:S(2)}, u32[]{:S(2)}) collective-permute-start(bf16[32,128]{1,0:T(8,128)(2,1)S(1)} %get-tuple-element.18.left_ref), channel_id=1, source_target_pairs={{0,1},{1,0},{2,3},{3,2},{4,5},{5,4},{6,7},{7,6},{8,9},{9,8},{10,11... | collective-permute-start | bytes 24584 | tf_op jit(solution)/shard_map/ppermute | solution.py:379
  16.1 4.5 %collective-permute-start.5 = (bf16[32,128]{1,0:T(8,128)(2,1)S(1)}, bf16[32,128]{1,0:T(8,128)(2,1)S(1)}, u32[]{:S(2)}, u32[]{:S(2)}) collective-permute-start(bf16[32,128]{1,0:T(8,128)(2,1)S(1)} %shard_map.157), channel_id=1, source_target_pairs={{0,4},{1,12},{2,0},{3,8},{4,5},{5,13},{6,1},{7,9},{8,6},{9,14},{10... | collective-permute-start | bytes 24584 | tf_op jit(solution)/shard_map/ppermute | solution.py:388
  16.6 4.0 %collective-permute-start.4 = (bf16[32,128]{1,0:T(8,128)(2,1)S(1)}, bf16[32,128]{1,0:T(8,128)(2,1)S(1)}, u32[]{:S(2)}, u32[]{:S(2)}) collective-permute-start(bf16[32,128]{1,0:T(8,128)(2,1)S(1)} %shard_map.157), channel_id=1, source_target_pairs={{0,0},{1,8},{2,4},{3,12},{4,1},{5,9},{6,5},{7,13},{8,2},{9,10},{10... | collective-permute-start | bytes 24584 | tf_op jit(solution)/shard_map/ppermute | solution.py:388
  20.7 18.3 %copy-start.6 = (bf16[1,4,512,128]{3,2,1,0:T(8,128)(2,1)S(1)}, bf16[1,4,512,128]{3,2,1,0:T(8,128)(2,1)}, u32[]{:S(2)}) copy-start(bf16[1,4,512,128]{3,2,1,0:T(8,128)(2,1)} %keys_ref.1) | copy-start | bytes 1572868
  20.7 18.3 %copy-start.7 = (bf16[1,4,512,128]{3,2,1,0:T(8,128)(2,1)S(1)}, bf16[1,4,512,128]{3,2,1,0:T(8,128)(2,1)}, u32[]{:S(2)}) copy-start(bf16[1,4,512,128]{3,2,1,0:T(8,128)(2,1)} %values_ref.1) | copy-start | bytes 1572868
  20.7 30.9 %copy-start.5 = (bf16[4,2048,32]{1,2,0:T(8,128)(2,1)S(1)}, bf16[4,2048,32]{1,2,0:T(8,128)(2,1)}, u32[]{:S(2)}) copy-start(bf16[4,2048,32]{1,2,0:T(8,128)(2,1)} %param.25) | copy-start | bytes 1572868
  39.0 17.4 %slice-start = ((s8[16777216]{0:T(1024)(128)(4,1)}), s8[4194304]{0:T(1024)(128)(4,1)S(1)}, s32[]{:S(2)}) async-start(s8[16777216]{0:T(1024)(128)(4,1)} %bitcast.13), calls=%async_computation.2 | async-start | bytes 8388608
  51.6 4.9 %slice-start.1 = ((s8[16777216]{0:T(1024)(128)(4,1)}), s8[4194304]{0:T(1024)(128)(4,1)S(1)}, s32[]{:S(2)}) async-start(s8[16777216]{0:T(1024)(128)(4,1)} %bitcast.13), calls=%async_computation.3 | async-start | bytes 8388608
  51.6 4.9 %slice-start.2 = ((s8[16777216]{0:T(1024)(128)(4,1)}), s8[4194304]{0:T(1024)(128)(4,1)S(1)}, s32[]{:S(2)}) async-start(s8[16777216]{0:T(1024)(128)(4,1)} %bitcast.13), calls=%async_computation.4 | async-start | bytes 8388608
  51.6 4.9 %slice-start.3 = ((s8[16777216]{0:T(1024)(128)(4,1)}), s8[4194304]{0:T(1024)(128)(4,1)S(1)}, s32[]{:S(2)}) async-start(s8[16777216]{0:T(1024)(128)(4,1)} %bitcast.13), calls=%async_computation.5 | async-start | bytes 8388608
  52.1 8.2 %copy-start.4 = (bf16[4,32,4096]{2,1,0:T(8,128)(2,1)S(1)}, bf16[4,32,4096]{2,1,0:T(8,128)(2,1)}, u32[]{:S(2)}) copy-start(bf16[4,32,4096]{2,1,0:T(8,128)(2,1)} %param.26) | copy-start | bytes 3145732
  52.1 3.6 %collective-permute-start.6 = (bf16[16,128]{1,0:T(8,128)(2,1)S(1)}, bf16[16,128]{1,0:T(8,128)(2,1)S(1)}, u32[]{:S(2)}, u32[]{:S(2)}) collective-permute-start(bf16[16,128]{1,0:T(8,128)(2,1)S(1)} %get-tuple-element.22.left_ref), channel_id=1, source_target_pairs={{0,4},{4,0},{8,12},{12,8},{1,5},{5,1},{9,13},{13,9},{2,6},{6,2},{1... | collective-permute-start | bytes 12296 | tf_op jit(solution)/shard_map/ppermute | solution.py:376
  55.8 4.5 %collective-permute-start.8 = (bf16[16,128]{1,0:T(8,128)(2,1)S(1)}, bf16[16,128]{1,0:T(8,128)(2,1)S(1)}, u32[]{:S(2)}, u32[]{:S(2)}) collective-permute-start(bf16[16,128]{1,0:T(8,128)(2,1)S(1)} %shard_map.162), channel_id=1, source_target_pairs={{0,1},{1,5},{2,9},{3,13},{4,3},{5,7},{6,11},{7,15},{8,0},{9,4},{10... | collective-permute-start | bytes 12296 | tf_op jit(solution)/shard_map/ppermute | solution.py:396
  55.8 4.5 %collective-permute-start.7 = (bf16[16,128]{1,0:T(8,128)(2,1)S(1)}, bf16[16,128]{1,0:T(8,128)(2,1)S(1)}, u32[]{:S(2)}, u32[]{:S(2)}) collective-permute-start(bf16[16,128]{1,0:T(8,128)(2,1)S(1)} %shard_map.162), channel_id=1, source_target_pairs={{0,0},{1,4},{2,8},{3,12},{4,2},{5,6},{6,10},{7,14},{8,1},{9,5},{10... | collective-permute-start | bytes 12296 | tf_op jit(solution)/shard_map/ppermute | solution.py:396
  60.9 10.5 %collective-permute-start.9 = (bf16[3,4,4096]{2,1,0:T(4,128)(2,1)S(1)}, bf16[3,4,4096]{2,1,0:T(4,128)(2,1)S(1)}, u32[]{:S(2)}, u32[]{:S(2)}) collective-permute-start(bf16[3,4,4096]{2,1,0:T(4,128)(2,1)S(1)} %get-tuple-element.24), channel_id=1, source_target_pairs={{0,8},{4,12},{8,0},{12,4},{1,9},{5,13},{9,1},{13,5},{2,10},{6,14},... | collective-permute-start | bytes 294920 | tf_op jit(solution)/shard_map/ppermute | solution.py:376
  66.7 6.5 %collective-permute-start.10 = (bf16[3,4,4096]{2,1,0:T(4,128)(2,1)S(1)}, bf16[3,4,4096]{2,1,0:T(4,128)(2,1)S(1)}, u32[]{:S(2)}, u32[]{:S(2)}) collective-permute-start(bf16[3,4,4096]{2,1,0:T(4,128)(2,1)S(1)} %get-tuple-element.25), channel_id=1, source_target_pairs={{0,12},{4,8},{8,4},{12,0},{1,13},{5,9},{9,5},{13,1},{2,14},{6,10},... | collective-permute-start | bytes 294920 | tf_op jit(solution)/shard_map/ppermute | solution.py:376
  66.7 6.5 %collective-permute-start.11 = (bf16[3,4,4096]{2,1,0:T(4,128)(2,1)S(1)}, bf16[3,4,4096]{2,1,0:T(4,128)(2,1)S(1)}, u32[]{:S(2)}, u32[]{:S(2)}) collective-permute-start(bf16[3,4,4096]{2,1,0:T(4,128)(2,1)S(1)} %get-tuple-element.26), channel_id=1, source_target_pairs={{0,4},{4,0},{8,12},{12,8},{1,5},{5,1},{9,13},{13,9},{2,6},{6,2},{1... | collective-permute-start | bytes 294920 | tf_op jit(solution)/shard_map/ppermute | solution.py:376

commit v19 on v17

--- a/solution.py
+++ b/solution.py
@@ -380,7 +380,7 @@
 
     def to_growers(value, flip):
         route = [
-            (t * groups + 2 * x + c, (2 * c + (x ^ flip)) * groups + t)
+            (t * groups + 2 * x + c, (3 - c if x ^ flip else c) * groups + t)
             for t in range(blocks)
             for x in range(2)
             for c in range(2)

time: 74 us -> 74.7 us (level)
  starting transfers between devices: 14.9 us -> 16.9 us
  blocking collectives: 29.1 us -> 27.9 us
    ppermute x2, starting transfers between devices: 1.17 us -> 3.12 us  [to_growers(): return lax.ppermute(value, EVERY, route)]
    all_to_all x2, blocking collectives: 29.1 us -> 27.9 us  [exchange(): return lax.all_to_all(value, EVERY, split_axis=0, concat_axis=0, tiled=True)]
  transfers between devices with their start and end apart: 13 -> 13, of which waited for: 5 -> 5; matrix products, arithmetic and copies ran while one was open for 0% -> 0% of each run, Pallas kernels for 10% -> 9%
where the time goes in v19:
time: 74.7 us; the launch traced here: 74.5 us
  blocking collectives  27.9 us (37%)
  starting transfers between devices  16.9 us (23%)
  waiting for transfers between devices  12.8 us (17%)
  Pallas kernels  11.3 us (15%)
  local copies, waits for them, and re-layouts  3.89 us (5%)
  between operations  0.91 us (1%)
  other arithmetic  0.75 us (1%)
    all_to_all x2, blocking collectives, exchange(): return lax.all_to_all(value, EVERY, split_axis=0, concat_axis=0, tiled=True)  27.9 us
    ppermute x6, starting transfers between devices, over_tensor(): return lax.ppermute(value, 'tensor', route)  12.2 us
    ppermute x6, waiting for transfers between devices, over_tensor(): return lax.ppermute(value, 'tensor', route)  11.6 us
    pallas_call x2, Pallas kernels, product(): call(product_kernel, shape((rows.shape[0], width), jnp.float32), [VMEM] *...  6.31 us
    unnamed x36, local copies, waits for them, and re-layouts  3.89 us
    ppermute x2, starting transfers between devices, to_growers(): return lax.ppermute(value, EVERY, route)  3.12 us
    ppermute x4, starting transfers between devices, to_out_growers(): return lax.ppermute(value, EVERY, route)  1.56 us
  transfers between devices with their start and end apart: 13, of which 5 were waited for; matrix products, arithmetic and copies ran while one was open for 0% of the time, Pallas kernels for 9%

profile of v19, /device:TPU:0, one launch (start us, length us, event | category | flops | bytes accessed | tf_op | source)
XLA Modules:
  0.0 74.5 jit_solution(17351310210062562337)
XLA Ops:
  0.0 5.0 %collective-permute-start.2 = (bf16[3,4,4096]{2,1,0:T(4,128)(2,1)}, bf16[3,4,4096]{2,1,0:T(4,128)(2,1)S(1)}, u32[]{:S(2)}, u32[]{:S(2)}) collective-permute-start(bf16[3,4,4096]{2,1,0:T(4,128)(2,1)} %bitcast.19), channel_id=1, source_target_pairs={{0,12},{4,8},{8,4},{12,0},{1,13},{5,9},{9,5},{13,1},{2,14},{6,10},... | collective-permute-start | bytes 294920 | tf_op jit(solution)/shard_map/ppermute | solution.py:376
  5.0 0.0 collective-permute-start.1
  5.1 0.6 collective-permute-start
  6.3 0.6 copy-done.12
  6.9 0.7 copy-done.13
  7.6 0.7 shard_map.154
  8.3 0.0 copy-start.8
  8.4 0.0 copy-start.10
  8.4 0.0 copy-start.11
  8.4 0.6 collective-permute-done.2.refs_3_
  9.0 4.6 %collective-permute-done.1.refs_2_ = bf16[3,4,4096]{2,1,0:T(4,128)(2,1)S(1)} collective-permute-done((bf16[3,4,4096]{2,1,0:T(4,128)(2,1)}, bf16[3,4,4096]{2,1,0:T(4,128)(2,1)S(1)}, u32[]{:S(2)}, u32[]{:S(2)}) %collective-permute-start.1) | collective-permute-done | bytes 98336 | tf_op jit(solution)/shard_map/ppermute | solution.py:376
  13.5 0.0 collective-permute-done.refs_1_
  13.5 1.4 %shard_map.155 = (bf16[48,4096]{1,0:T(8,128)(2,1)S(1)}, bf16[32,128]{1,0:T(8,128)(2,1)S(1)}) custom-call(bf16[3,4,4096]{2,1,0:T(4,128)(2,1)S(1)} %bitcast.22, bf16[3,4,4096]{2,1,0:T(4,128)(2,1)S(1)} %collective-permute-done.refs_1_, bf16[3,4,4096]{2,1,0:T(4,128)(2,1)S(1)} %collective-permute-done.1.refs_2_, ...), custom_call_target="tpu_custom_call" | custom-call | flops 150994944 | bytes 3932160 | tf_op jit(solution)/shard_map/pallas_call | solution.py:414
  14.9 0.0 collective-permute-start.3
  14.9 1.2 %collective-permute-done.3.right_ref = bf16[32,128]{1,0:T(8,128)(2,1)S(1)} collective-permute-done((bf16[32,128]{1,0:T(8,128)(2,1)S(1)}, bf16[32,128]{1,0:T(8,128)(2,1)S(1)}, u32[]{:S(2)}, u32[]{:S(2)}) %collective-permute-start.3) | collective-permute-done | bytes 8224 | tf_op jit(solution)/shard_map/ppermute | solution.py:379
  16.1 2.5 %collective-permute-start.5 = (bf16[32,128]{1,0:T(8,128)(2,1)S(1)}, bf16[32,128]{1,0:T(8,128)(2,1)S(1)}, u32[]{:S(2)}, u32[]{:S(2)}) collective-permute-start(bf16[32,128]{1,0:T(8,128)(2,1)S(1)} %shard_map.157), channel_id=1, source_target_pairs={{0,12},{1,8},{2,0},{3,4},{4,13},{5,9},{6,1},{7,5},{8,14},{9,10},{1... | collective-permute-start | bytes 24584 | tf_op jit(solution)/shard_map/ppermute | solution.py:388
  18.6 0.6 collective-permute-start.4
  19.2 0.0 copy-done
  19.3 3.3 %shard_map.156.total_ref = f32[48,2304]{1,0:T(8,128)S(1)} custom-call(bf16[48,4096]{1,0:T(8,128)(2,1)S(1)} %get-tuple-element.17.rows_ref, bf16[4096,2048]{1,0:T(8,128)(2,1)S(1)} %copy-done, bf16[4096,128]{1,0:T(8,128)(2,1)S(1)} %copy-done.2, bf16[4096,128]{1,0:T(8,128)(2,1)S(1)} %copy-done.3), custom_call_target="tpu_custom_call" | custom-call | tf_op jit(solution)/shard_map/pallas_call | solution.py:152
  22.6 0.0 collective-permute-done.5.refs_1_
  22.6 0.0 collective-permute-done.4.refs_0_
  22.6 0.0 copy-start.6
  22.7 0.0 copy-start.7
  22.7 0.0 copy-start.5
  22.7 0.9 %shard_map.158 = bf16[16,56,128]{2,1,0:T(8,128)(2,1)S(1)} custom-call(f32[48,2304]{1,0:T(8,128)S(1)} %shard_map.156.total_ref, s32[48,128]{1,0:T(8,128)S(1)} %get-tuple-element.16.refs_5_.slots_ref, bf16[32,128]{1,0:T(8,128)(2,1)S(1)} %collective-permute-done.4.refs_0_, bf16[32,128]{1,0:T(8,128)(2,1)S(1)} %collective-permute-done.5.refs_1_, ...), custom_call_target="tpu_custom_call" | custom-call | tf_op jit(solution)/shard_map/pallas_call | solution.py:428
  23.6 16.1 %all_to_all.10.arrived_ref = bf16[16,56,128]{2,1,0:T(8,128)(2,1)S(1)} all-to-all(bf16[16,56,128]{2,1,0:T(8,128)(2,1)S(1)} %shard_map.158), channel_id=1, replica_groups=mesh['parts'=2,'tensor'=4,'dp'=2,'pipe'=2] {'tensor','dp','pipe'}, dimensions={0} | all-to-all | bytes 458752 | tf_op jit(solution)/shard_map/all_to_all | solution.py:402
  39.8 0.8 %shard_map.159 = bf16[16,48,128]{2,1,0:T(8,128)(2,1)S(1)} custom-call(bf16[16,56,128]{2,1,0:T(8,128)(2,1)S(1)} %all_to_all.10.arrived_ref, bf16[1,4,512,128]{3,2,1,0:T(8,128)(2,1)S(1)} %copy-done.6, bf16[1,4,512,128]{3,2,1,0:T(8,128)(2,1)S(1)} %copy-done.7, s32[1]{0:T(128)S(6)} %copy.17.length_ref, f32[56,128]{1,0:T(8,128)S(1)} %get-tuple-element.19.cosine_ref, ...), custom_call_target="tpu_custom_call" | custom-call | tf_op jit(solution)/shard_map/pallas_call | solution.py:441
  40.5 11.8 %all_to_all.11.got_ref = bf16[16,48,128]{2,1,0:T(8,128)(2,1)S(1)} all-to-all(bf16[16,48,128]{2,1,0:T(8,128)(2,1)S(1)} %shard_map.159), channel_id=1, replica_groups=mesh['parts'=2,'tensor'=4,'dp'=2,'pipe'=2] {'tensor','dp','pipe'}, dimensions={0} | all-to-all | bytes 393216 | tf_op jit(solution)/shard_map/all_to_all | solution.py:402
  52.3 0.6 shard_map.160
  52.9 0.0 collective-permute-start.9
  52.9 0.6 collective-permute-start.8
  53.5 0.2 collective-permute-start.7
  53.7 0.8 %collective-permute-start.6 = (bf16[16,128]{1,0:T(8,128)(2,1)S(1)}, bf16[16,128]{1,0:T(8,128)(2,1)S(1)}, u32[]{:S(2)}, u32[]{:S(2)}) collective-permute-start(bf16[16,128]{1,0:T(8,128)(2,1)S(1)} %get-tuple-element.22), channel_id=1, source_target_pairs={{0,0},{1,4},{2,8},{3,12},{4,1},{5,5},{6,9},{7,13},{8,2},{9,6},{10,... | collective-permute-start | bytes 12296 | tf_op jit(solution)/shard_map/ppermute | solution.py:396
  54.5 0.0 slice-done.1
  54.5 1.3 %slice-done.2 = s8[4194304]{0:T(1024)(128)(4,1)S(1)} async-done(((s8[16777216]{0:T(1024)(128)(4,1)}), s8[4194304]{0:T(1024)(128)(4,1)S(1)}, s32[]{:S(2)}) %slice-start.2) | async-done | bytes 4194328
  55.8 1.2 %slice-done.3 = s8[4194304]{0:T(1024)(128)(4,1)S(1)} async-done(((s8[16777216]{0:T(1024)(128)(4,1)}), s8[4194304]{0:T(1024)(128)(4,1)S(1)}, s32[]{:S(2)}) %slice-start.3) | async-done | bytes 4194328
  57.0 3.0 %shard_map.161.total_ref = f32[48,4096]{1,0:T(8,128)S(1)} custom-call(bf16[48,2048]{1,0:T(8,128)(2,1)S(1)} %get-tuple-element.21.rows_ref, bf16[2048,4096]{1,0:T(8,128)(2,1)S(1)} %bitcast.14), custom_call_target="tpu_custom_call" | custom-call | tf_op jit(solution)/shard_map/pallas_call | solution.py:152
  60.0 0.0 collective-permute-done.9.refs_3_
  60.0 0.0 collective-permute-done.8.refs_2_
  60.0 0.0 collective-permute-done.7.refs_1_
  60.0 0.0 collective-permute-done.6.refs_0_
  60.0 0.6 shard_map.162
  60.7 5.9 %collective-permute-start.10 = (bf16[3,4,4096]{2,1,0:T(4,128)(2,1)S(1)}, bf16[3,4,4096]{2,1,0:T(4,128)(2,1)S(1)}, u32[]{:S(2)}, u32[]{:S(2)}) collective-permute-start(bf16[3,4,4096]{2,1,0:T(4,128)(2,1)S(1)} %get-tuple-element.24), channel_id=1, source_target_pairs={{0,8},{4,12},{8,0},{12,4},{1,9},{5,13},{9,1},{13,5},{2,10},{6,14},... | collective-permute-start | bytes 294920 | tf_op jit(solution)/shard_map/ppermute | solution.py:376
  66.6 0.6 collective-permute-start.12
  67.2 6.0 %collective-permute-done.10 = bf16[3,4,4096]{2,1,0:T(4,128)(2,1)S(1)} collective-permute-done((bf16[3,4,4096]{2,1,0:T(4,128)(2,1)S(1)}, bf16[3,4,4096]{2,1,0:T(4,128)(2,1)S(1)}, u32[]{:S(2)}, u32[]{:S(2)}) %collective-permute-start.10) | collective-permute-done | bytes 98336 | tf_op jit(solution)/shard_map/ppermute | solution.py:376
  73.3 0.0 collective-permute-done.11
  73.3 0.5 collective-permute-done.12
  73.7 0.7 %fusion = bf16[4,3,4096]{2,0,1:T(4,128)(2,1)} fusion(bf16[3,4,4096]{2,1,0:T(4,128)(2,1)S(1)} %collective-permute-done.12, bf16[3,4,4096]{2,1,0:T(4,128)(2,1)S(1)} %collective-permute-done.11, bf16[3,4,4096]{2,1,0:T(4,128)(2,1)S(1)} %collective-permute-done.10, bf16[3,4,4096]{2,1,0:T(4,128)(2,1)S(1)} %get-tuple-element.23), kind=kLoop, calls=%fused_computation.1 | loop fusion | flops 393216 | bytes 491520 | tf_op jit(solution)/shard_map/transpose | solution.py:470
  (27 shorter events, 0.1 us)
Async XLA Ops:
  0.0 9.0 %collective-permute-start.2 = (bf16[3,4,4096]{2,1,0:T(4,128)(2,1)}, bf16[3,4,4096]{2,1,0:T(4,128)(2,1)S(1)}, u32[]{:S(2)}, u32[]{:S(2)}) collective-permute-start(bf16[3,4,4096]{2,1,0:T(4,128)(2,1)} %bitcast.19), channel_id=1, source_target_pairs={{0,12},{4,8},{8,4},{12,0},{1,13},{5,9},{9,5},{13,1},{2,14},{6,10},... | collective-permute-start | bytes 294920 | tf_op jit(solution)/shard_map/ppermute | solution.py:376
  5.0 8.5 %collective-permute-start.1 = (bf16[3,4,4096]{2,1,0:T(4,128)(2,1)}, bf16[3,4,4096]{2,1,0:T(4,128)(2,1)S(1)}, u32[]{:S(2)}, u32[]{:S(2)}) collective-permute-start(bf16[3,4,4096]{2,1,0:T(4,128)(2,1)} %bitcast.20), channel_id=1, source_target_pairs={{0,8},{4,12},{8,0},{12,4},{1,9},{5,13},{9,1},{13,5},{2,10},{6,14},... | collective-permute-start | bytes 294920 | tf_op jit(solution)/shard_map/ppermute | solution.py:376
  5.1 8.5 %collective-permute-start = (bf16[3,4,4096]{2,1,0:T(4,128)(2,1)}, bf16[3,4,4096]{2,1,0:T(4,128)(2,1)S(1)}, u32[]{:S(2)}, u32[]{:S(2)}) collective-permute-start(bf16[3,4,4096]{2,1,0:T(4,128)(2,1)} %bitcast.21), channel_id=1, source_target_pairs={{0,4},{4,0},{8,12},{12,8},{1,5},{5,1},{9,13},{13,9},{2,6},{6,2},{1... | collective-permute-start | bytes 294920 | tf_op jit(solution)/shard_map/ppermute | solution.py:376
  6.3 0.7 copy-start.12
  6.9 0.7 copy-start.13
  7.6 6.0 %copy-start.1 = (bf16[4,4096,96]{1,2,0:T(8,128)(2,1)S(1)}, bf16[4,4096,96]{1,2,0:T(8,128)(2,1)}, u32[]{:S(2)}) copy-start(bf16[4,4096,96]{1,2,0:T(8,128)(2,1)} %param.21) | copy-start | bytes 9437188
  7.6 6.0 %copy-start.9 = (bf16[4,3,4096]{2,0,1:T(4,128)(2,1)S(1)}, bf16[4,3,4096]{2,0,1:T(4,128)(2,1)}, u32[]{:S(2)}) copy-start(bf16[4,3,4096]{2,0,1:T(4,128)(2,1)} %param.16) | copy-start | bytes 294916
  7.6 11.7 %copy-start = (bf16[4096,2048]{1,0:T(8,128)(2,1)S(1)}, bf16[4096,2048]{1,0:T(8,128)(2,1)}, u32[]{:S(2)}) copy-start(bf16[4096,2048]{1,0:T(8,128)(2,1)} %refs_3_.1) | copy-start | bytes 50331652
  7.6 11.7 %copy-start.2 = (bf16[4096,128]{1,0:T(8,128)(2,1)S(1)}, bf16[4096,128]{1,0:T(8,128)(2,1)}, u32[]{:S(2)}) copy-start(bf16[4096,128]{1,0:T(8,128)(2,1)} %refs_1_.4) | copy-start | bytes 3145732
  7.6 11.7 %copy-start.3 = (bf16[4096,128]{1,0:T(8,128)(2,1)S(1)}, bf16[4096,128]{1,0:T(8,128)(2,1)}, u32[]{:S(2)}) copy-start(bf16[4096,128]{1,0:T(8,128)(2,1)} %refs_2_.4) | copy-start | bytes 3145732
  8.3 14.3 %copy-start.8 = (bf16[4,32,2048]{2,1,0:T(8,128)(2,1)S(1)}, bf16[4,32,2048]{2,1,0:T(8,128)(2,1)}, u32[]{:S(2)}) copy-start(bf16[4,32,2048]{2,1,0:T(8,128)(2,1)} %param.22) | copy-start | bytes 1572868
  8.4 14.3 %copy-start.10 = (bf16[4,32,128]{2,1,0:T(8,128)(2,1)S(1)}, bf16[4,32,128]{2,1,0:T(8,128)(2,1)}, u32[]{:S(2)}) copy-start(bf16[4,32,128]{2,1,0:T(8,128)(2,1)} %param.23) | copy-start | bytes 98308
  8.4 14.3 %copy-start.11 = (bf16[4,32,128]{2,1,0:T(8,128)(2,1)S(1)}, bf16[4,32,128]{2,1,0:T(8,128)(2,1)}, u32[]{:S(2)}) copy-start(bf16[4,32,128]{2,1,0:T(8,128)(2,1)} %param.24) | copy-start | bytes 98308
  14.9 1.2 %collective-permute-start.3 = (bf16[32,128]{1,0:T(8,128)(2,1)S(1)}, bf16[32,128]{1,0:T(8,128)(2,1)S(1)}, u32[]{:S(2)}, u32[]{:S(2)}) collective-permute-start(bf16[32,128]{1,0:T(8,128)(2,1)S(1)} %get-tuple-element.18.left_ref), channel_id=1, source_target_pairs={{0,1},{1,0},{2,3},{3,2},{4,5},{5,4},{6,7},{7,6},{8,9},{9,8},{10,11... | collective-permute-start | bytes 24584 | tf_op jit(solution)/shard_map/ppermute | solution.py:379
  16.1 6.5 %collective-permute-start.5 = (bf16[32,128]{1,0:T(8,128)(2,1)S(1)}, bf16[32,128]{1,0:T(8,128)(2,1)S(1)}, u32[]{:S(2)}, u32[]{:S(2)}) collective-permute-start(bf16[32,128]{1,0:T(8,128)(2,1)S(1)} %shard_map.157), channel_id=1, source_target_pairs={{0,12},{1,8},{2,0},{3,4},{4,13},{5,9},{6,1},{7,5},{8,14},{9,10},{1... | collective-permute-start | bytes 24584 | tf_op jit(solution)/shard_map/ppermute | solution.py:388
  18.6 4.0 %collective-permute-start.4 = (bf16[32,128]{1,0:T(8,128)(2,1)S(1)}, bf16[32,128]{1,0:T(8,128)(2,1)S(1)}, u32[]{:S(2)}, u32[]{:S(2)}) collective-permute-start(bf16[32,128]{1,0:T(8,128)(2,1)S(1)} %shard_map.157), channel_id=1, source_target_pairs={{0,0},{1,4},{2,12},{3,8},{4,1},{5,5},{6,13},{7,9},{8,2},{9,6},{10,... | collective-permute-start | bytes 24584 | tf_op jit(solution)/shard_map/ppermute | solution.py:388
  22.6 17.1 %copy-start.6 = (bf16[1,4,512,128]{3,2,1,0:T(8,128)(2,1)S(1)}, bf16[1,4,512,128]{3,2,1,0:T(8,128)(2,1)}, u32[]{:S(2)}) copy-start(bf16[1,4,512,128]{3,2,1,0:T(8,128)(2,1)} %keys_ref.1) | copy-start | bytes 1572868
  22.7 17.1 %copy-start.7 = (bf16[1,4,512,128]{3,2,1,0:T(8,128)(2,1)S(1)}, bf16[1,4,512,128]{3,2,1,0:T(8,128)(2,1)}, u32[]{:S(2)}) copy-start(bf16[1,4,512,128]{3,2,1,0:T(8,128)(2,1)} %values_ref.1) | copy-start | bytes 1572868
  22.7 29.6 %copy-start.5 = (bf16[4,2048,32]{1,2,0:T(8,128)(2,1)S(1)}, bf16[4,2048,32]{1,2,0:T(8,128)(2,1)}, u32[]{:S(2)}) copy-start(bf16[4,2048,32]{1,2,0:T(8,128)(2,1)} %param.25) | copy-start | bytes 1572868
  39.8 14.7 %slice-start = ((s8[16777216]{0:T(1024)(128)(4,1)}), s8[4194304]{0:T(1024)(128)(4,1)S(1)}, s32[]{:S(2)}) async-start(s8[16777216]{0:T(1024)(128)(4,1)} %bitcast.13), calls=%async_computation.2 | async-start | bytes 8388608
  52.3 2.2 %slice-start.1 = ((s8[16777216]{0:T(1024)(128)(4,1)}), s8[4194304]{0:T(1024)(128)(4,1)S(1)}, s32[]{:S(2)}) async-start(s8[16777216]{0:T(1024)(128)(4,1)} %bitcast.13), calls=%async_computation.3 | async-start | bytes 8388608
  52.3 3.5 %slice-start.2 = ((s8[16777216]{0:T(1024)(128)(4,1)}), s8[4194304]{0:T(1024)(128)(4,1)S(1)}, s32[]{:S(2)}) async-start(s8[16777216]{0:T(1024)(128)(4,1)} %bitcast.13), calls=%async_computation.4 | async-start | bytes 8388608
  52.3 4.7 %slice-start.3 = ((s8[16777216]{0:T(1024)(128)(4,1)}), s8[4194304]{0:T(1024)(128)(4,1)S(1)}, s32[]{:S(2)}) async-start(s8[16777216]{0:T(1024)(128)(4,1)} %bitcast.13), calls=%async_computation.5 | async-start | bytes 8388608
  52.9 7.1 %copy-start.4 = (bf16[4,32,4096]{2,1,0:T(8,128)(2,1)S(1)}, bf16[4,32,4096]{2,1,0:T(8,128)(2,1)}, u32[]{:S(2)}) copy-start(bf16[4,32,4096]{2,1,0:T(8,128)(2,1)} %param.26) | copy-start | bytes 3145732
  52.9 7.1 %collective-permute-start.9 = (bf16[16,128]{1,0:T(8,128)(2,1)S(1)}, bf16[16,128]{1,0:T(8,128)(2,1)S(1)}, u32[]{:S(2)}, u32[]{:S(2)}) collective-permute-start(bf16[16,128]{1,0:T(8,128)(2,1)S(1)} %get-tuple-element.22), channel_id=1, source_target_pairs={{0,3},{1,7},{2,11},{3,15},{4,2},{5,6},{6,10},{7,14},{8,1},{9,5},{1... | collective-permute-start | bytes 12296 | tf_op jit(solution)/shard_map/ppermute | solution.py:396
  52.9 7.1 %collective-permute-start.8 = (bf16[16,128]{1,0:T(8,128)(2,1)S(1)}, bf16[16,128]{1,0:T(8,128)(2,1)S(1)}, u32[]{:S(2)}, u32[]{:S(2)}) collective-permute-start(bf16[16,128]{1,0:T(8,128)(2,1)S(1)} %get-tuple-element.22), channel_id=1, source_target_pairs={{0,2},{1,6},{2,10},{3,14},{4,3},{5,7},{6,11},{7,15},{8,0},{9,4},{1... | collective-permute-start | bytes 12296 | tf_op jit(solution)/shard_map/ppermute | solution.py:396
  53.5 6.5 %collective-permute-start.7 = (bf16[16,128]{1,0:T(8,128)(2,1)S(1)}, bf16[16,128]{1,0:T(8,128)(2,1)S(1)}, u32[]{:S(2)}, u32[]{:S(2)}) collective-permute-start(bf16[16,128]{1,0:T(8,128)(2,1)S(1)} %get-tuple-element.22), channel_id=1, source_target_pairs={{0,1},{1,5},{2,9},{3,13},{4,0},{5,4},{6,8},{7,12},{8,3},{9,7},{10,... | collective-permute-start | bytes 12296 | tf_op jit(solution)/shard_map/ppermute | solution.py:396
  53.7 6.4 %collective-permute-start.6 = (bf16[16,128]{1,0:T(8,128)(2,1)S(1)}, bf16[16,128]{1,0:T(8,128)(2,1)S(1)}, u32[]{:S(2)}, u32[]{:S(2)}) collective-permute-start(bf16[16,128]{1,0:T(8,128)(2,1)S(1)} %get-tuple-element.22), channel_id=1, source_target_pairs={{0,0},{1,4},{2,8},{3,12},{4,1},{5,5},{6,9},{7,13},{8,2},{9,6},{10,... | collective-permute-start | bytes 12296 | tf_op jit(solution)/shard_map/ppermute | solution.py:396
  60.7 12.6 %collective-permute-start.10 = (bf16[3,4,4096]{2,1,0:T(4,128)(2,1)S(1)}, bf16[3,4,4096]{2,1,0:T(4,128)(2,1)S(1)}, u32[]{:S(2)}, u32[]{:S(2)}) collective-permute-start(bf16[3,4,4096]{2,1,0:T(4,128)(2,1)S(1)} %get-tuple-element.24), channel_id=1, source_target_pairs={{0,8},{4,12},{8,0},{12,4},{1,9},{5,13},{9,1},{13,5},{2,10},{6,14},... | collective-permute-start | bytes 294920 | tf_op jit(solution)/shard_map/ppermute | solution.py:376
  66.6 6.7 %collective-permute-start.11 = (bf16[3,4,4096]{2,1,0:T(4,128)(2,1)S(1)}, bf16[3,4,4096]{2,1,0:T(4,128)(2,1)S(1)}, u32[]{:S(2)}, u32[]{:S(2)}) collective-permute-start(bf16[3,4,4096]{2,1,0:T(4,128)(2,1)S(1)} %get-tuple-element.25), channel_id=1, source_target_pairs={{0,12},{4,8},{8,4},{12,0},{1,13},{5,9},{9,5},{13,1},{2,14},{6,10},... | collective-permute-start | bytes 294920 | tf_op jit(solution)/shard_map/ppermute | solution.py:376
  66.6 7.1 %collective-permute-start.12 = (bf16[3,4,4096]{2,1,0:T(4,128)(2,1)S(1)}, bf16[3,4,4096]{2,1,0:T(4,128)(2,1)S(1)}, u32[]{:S(2)}, u32[]{:S(2)}) collective-permute-start(bf16[3,4,4096]{2,1,0:T(4,128)(2,1)S(1)} %get-tuple-element.26), channel_id=1, source_target_pairs={{0,4},{4,0},{8,12},{12,8},{1,5},{5,1},{9,13},{13,9},{2,6},{6,2},{1... | collective-permute-start | bytes 294920 | tf_op jit(solution)/shard_map/ppermute | solution.py:376

commit v20 on v17

--- a/solution.py
+++ b/solution.py
@@ -465,7 +465,7 @@
         8 * count * out_cols + 2 * owned * width * out_cols,
     )(out_total, slots, grow_out.reshape(owned * width, -1), *out_ranks)
     result = leaving[0].astype(jnp.float32)
-    for shift in sorted(range(1, blocks), key=lambda shift: shift < blocks // 2):
+    for shift in range(1, blocks):
         result = result + over_tensor(leaving[shift], shift).astype(jnp.float32)
     return jnp.transpose(result.astype(jnp.bfloat16), (1, 0, 2))
 

time: 74 us -> 74.7 us (level)
  starting transfers between devices: 14.9 us -> 15.8 us
    ppermute x6, starting transfers between devices: 12.2 us -> 13 us  [over_tensor(): return lax.ppermute(value, 'tensor', route)]
  transfers between devices with their start and end apart: 13 -> 13, of which waited for: 5 -> 4; matrix products, arithmetic and copies ran while one was open for 0% -> 0% of each run, Pallas kernels for 10% -> 9%
where the time goes in v20:
time: 74.7 us; the launch traced here: 74.5 us
  blocking collectives  29.1 us (39%)
  starting transfers between devices  15.8 us (21%)
  waiting for transfers between devices  12.7 us (17%)
  Pallas kernels  11.3 us (15%)
  local copies, waits for them, and re-layouts  3.89 us (5%)
  between operations  0.91 us (1%)
  other arithmetic  0.75 us (1%)
    all_to_all x2, blocking collectives, exchange(): return lax.all_to_all(value, EVERY, split_axis=0, concat_axis=0, tiled=True)  29.1 us
    ppermute x6, starting transfers between devices, over_tensor(): return lax.ppermute(value, 'tensor', route)  13 us
    ppermute x6, waiting for transfers between devices, over_tensor(): return lax.ppermute(value, 'tensor', route)  11.5 us
    pallas_call x2, Pallas kernels, product(): call(product_kernel, shape((rows.shape[0], width), jnp.float32), [VMEM] *...  6.31 us
    unnamed x36, local copies, waits for them, and re-layouts  3.89 us
    ppermute x4, starting transfers between devices, to_out_growers(): return lax.ppermute(value, EVERY, route)  1.56 us
  transfers between devices with their start and end apart: 13, of which 4 were waited for; matrix products, arithmetic and copies ran while one was open for 0% of the time, Pallas kernels for 9%

profile of v20, /device:TPU:0, one launch (start us, length us, event | category | flops | bytes accessed | tf_op | source)
XLA Modules:
  0.0 74.5 jit_solution(9194524534468967892)
XLA Ops:
  0.0 5.0 %collective-permute-start.2 = (bf16[3,4,4096]{2,1,0:T(4,128)(2,1)}, bf16[3,4,4096]{2,1,0:T(4,128)(2,1)S(1)}, u32[]{:S(2)}, u32[]{:S(2)}) collective-permute-start(bf16[3,4,4096]{2,1,0:T(4,128)(2,1)} %bitcast.19), channel_id=1, source_target_pairs={{0,12},{4,8},{8,4},{12,0},{1,13},{5,9},{9,5},{13,1},{2,14},{6,10},... | collective-permute-start | bytes 294920 | tf_op jit(solution)/shard_map/ppermute | solution.py:376
  5.0 0.0 collective-permute-start.1
  5.1 0.6 collective-permute-start
  6.3 0.6 copy-done.12
  6.9 0.7 copy-done.13
  7.6 0.7 shard_map.154
  8.3 0.0 copy-start.8
  8.4 0.0 copy-start.10
  8.4 0.0 copy-start.11
  8.4 0.6 collective-permute-done.2.refs_3_
  9.0 4.6 %collective-permute-done.1.refs_2_ = bf16[3,4,4096]{2,1,0:T(4,128)(2,1)S(1)} collective-permute-done((bf16[3,4,4096]{2,1,0:T(4,128)(2,1)}, bf16[3,4,4096]{2,1,0:T(4,128)(2,1)S(1)}, u32[]{:S(2)}, u32[]{:S(2)}) %collective-permute-start.1) | collective-permute-done | bytes 98336 | tf_op jit(solution)/shard_map/ppermute | solution.py:376
  13.5 0.0 collective-permute-done.refs_1_
  13.5 1.4 %shard_map.155 = (bf16[48,4096]{1,0:T(8,128)(2,1)S(1)}, bf16[32,128]{1,0:T(8,128)(2,1)S(1)}) custom-call(bf16[3,4,4096]{2,1,0:T(4,128)(2,1)S(1)} %bitcast.22, bf16[3,4,4096]{2,1,0:T(4,128)(2,1)S(1)} %collective-permute-done.refs_1_, bf16[3,4,4096]{2,1,0:T(4,128)(2,1)S(1)} %collective-permute-done.1.refs_2_, ...), custom_call_target="tpu_custom_call" | custom-call | flops 150994944 | bytes 3932160 | tf_op jit(solution)/shard_map/pallas_call | solution.py:414
  14.9 0.0 collective-permute-start.3
  14.9 1.2 %collective-permute-done.3.right_ref = bf16[32,128]{1,0:T(8,128)(2,1)S(1)} collective-permute-done((bf16[32,128]{1,0:T(8,128)(2,1)S(1)}, bf16[32,128]{1,0:T(8,128)(2,1)S(1)}, u32[]{:S(2)}, u32[]{:S(2)}) %collective-permute-start.3) | collective-permute-done | bytes 8224 | tf_op jit(solution)/shard_map/ppermute | solution.py:379
  16.1 0.5 collective-permute-start.5
  16.6 0.6 collective-permute-start.4
  17.3 0.0 copy-done
  17.3 3.3 %shard_map.156.total_ref = f32[48,2304]{1,0:T(8,128)S(1)} custom-call(bf16[48,4096]{1,0:T(8,128)(2,1)S(1)} %get-tuple-element.17.rows_ref, bf16[4096,2048]{1,0:T(8,128)(2,1)S(1)} %copy-done, bf16[4096,128]{1,0:T(8,128)(2,1)S(1)} %copy-done.2, bf16[4096,128]{1,0:T(8,128)(2,1)S(1)} %copy-done.3), custom_call_target="tpu_custom_call" | custom-call | tf_op jit(solution)/shard_map/pallas_call | solution.py:152
  20.6 0.0 collective-permute-done.5.refs_1_
  20.7 0.0 collective-permute-done.4.refs_0_
  20.7 0.0 copy-start.6
  20.7 0.0 copy-start.7
  20.7 0.0 copy-start.5
  20.7 0.9 %shard_map.158 = bf16[16,56,128]{2,1,0:T(8,128)(2,1)S(1)} custom-call(f32[48,2304]{1,0:T(8,128)S(1)} %shard_map.156.total_ref, s32[48,128]{1,0:T(8,128)S(1)} %get-tuple-element.16.refs_5_.slots_ref, bf16[32,128]{1,0:T(8,128)(2,1)S(1)} %collective-permute-done.4.refs_0_, bf16[32,128]{1,0:T(8,128)(2,1)S(1)} %collective-permute-done.5.refs_1_, ...), custom_call_target="tpu_custom_call" | custom-call | tf_op jit(solution)/shard_map/pallas_call | solution.py:428
  21.7 17.4 %all_to_all.10.arrived_ref = bf16[16,56,128]{2,1,0:T(8,128)(2,1)S(1)} all-to-all(bf16[16,56,128]{2,1,0:T(8,128)(2,1)S(1)} %shard_map.158), channel_id=1, replica_groups=mesh['parts'=2,'tensor'=4,'dp'=2,'pipe'=2] {'tensor','dp','pipe'}, dimensions={0} | all-to-all | bytes 458752 | tf_op jit(solution)/shard_map/all_to_all | solution.py:402
  39.0 0.8 %shard_map.159 = bf16[16,48,128]{2,1,0:T(8,128)(2,1)S(1)} custom-call(bf16[16,56,128]{2,1,0:T(8,128)(2,1)S(1)} %all_to_all.10.arrived_ref, bf16[1,4,512,128]{3,2,1,0:T(8,128)(2,1)S(1)} %copy-done.6, bf16[1,4,512,128]{3,2,1,0:T(8,128)(2,1)S(1)} %copy-done.7, s32[1]{0:T(128)S(6)} %copy.17.length_ref, f32[56,128]{1,0:T(8,128)S(1)} %get-tuple-element.19.cosine_ref, ...), custom_call_target="tpu_custom_call" | custom-call | tf_op jit(solution)/shard_map/pallas_call | solution.py:441
  39.8 11.8 %all_to_all.11.got_ref = bf16[16,48,128]{2,1,0:T(8,128)(2,1)S(1)} all-to-all(bf16[16,48,128]{2,1,0:T(8,128)(2,1)S(1)} %shard_map.159), channel_id=1, replica_groups=mesh['parts'=2,'tensor'=4,'dp'=2,'pipe'=2] {'tensor','dp','pipe'}, dimensions={0} | all-to-all | bytes 393216 | tf_op jit(solution)/shard_map/all_to_all | solution.py:402
  51.6 0.6 shard_map.160
  52.1 0.0 collective-permute-start.9
  52.1 0.6 collective-permute-start.8
  52.7 0.2 collective-permute-start.7
  52.9 0.8 %collective-permute-start.6 = (bf16[16,128]{1,0:T(8,128)(2,1)S(1)}, bf16[16,128]{1,0:T(8,128)(2,1)S(1)}, u32[]{:S(2)}, u32[]{:S(2)}) collective-permute-start(bf16[16,128]{1,0:T(8,128)(2,1)S(1)} %get-tuple-element.22), channel_id=1, source_target_pairs={{0,0},{1,4},{2,8},{3,12},{4,1},{5,5},{6,9},{7,13},{8,2},{9,6},{10,... | collective-permute-start | bytes 12296 | tf_op jit(solution)/shard_map/ppermute | solution.py:396
  53.7 0.0 slice-done.1
  53.8 1.3 %slice-done.2 = s8[4194304]{0:T(1024)(128)(4,1)S(1)} async-done(((s8[16777216]{0:T(1024)(128)(4,1)}), s8[4194304]{0:T(1024)(128)(4,1)S(1)}, s32[]{:S(2)}) %slice-start.2) | async-done | bytes 4194328
  55.0 1.2 %slice-done.3 = s8[4194304]{0:T(1024)(128)(4,1)S(1)} async-done(((s8[16777216]{0:T(1024)(128)(4,1)}), s8[4194304]{0:T(1024)(128)(4,1)S(1)}, s32[]{:S(2)}) %slice-start.3) | async-done | bytes 4194328
  56.2 3.0 %shard_map.161.total_ref = f32[48,4096]{1,0:T(8,128)S(1)} custom-call(bf16[48,2048]{1,0:T(8,128)(2,1)S(1)} %get-tuple-element.21.rows_ref, bf16[2048,4096]{1,0:T(8,128)(2,1)S(1)} %bitcast.14), custom_call_target="tpu_custom_call" | custom-call | tf_op jit(solution)/shard_map/pallas_call | solution.py:152
  59.2 0.0 collective-permute-done.9.refs_3_
  59.3 0.0 collective-permute-done.8.refs_2_
  59.3 0.0 collective-permute-done.7.refs_1_
  59.3 0.0 collective-permute-done.6.refs_0_
  59.3 0.6 shard_map.162
  59.9 1.8 %collective-permute-start.10 = (bf16[3,4,4096]{2,1,0:T(4,128)(2,1)S(1)}, bf16[3,4,4096]{2,1,0:T(4,128)(2,1)S(1)}, u32[]{:S(2)}, u32[]{:S(2)}) collective-permute-start(bf16[3,4,4096]{2,1,0:T(4,128)(2,1)S(1)} %get-tuple-element.24), channel_id=1, source_target_pairs={{0,4},{4,0},{8,12},{12,8},{1,5},{5,1},{9,13},{13,9},{2,6},{6,2},{1... | collective-permute-start | bytes 294920 | tf_op jit(solution)/shard_map/ppermute | solution.py:376
  61.7 4.5 %collective-permute-start.11 = (bf16[3,4,4096]{2,1,0:T(4,128)(2,1)S(1)}, bf16[3,4,4096]{2,1,0:T(4,128)(2,1)S(1)}, u32[]{:S(2)}, u32[]{:S(2)}) collective-permute-start(bf16[3,4,4096]{2,1,0:T(4,128)(2,1)S(1)} %get-tuple-element.25), channel_id=1, source_target_pairs={{0,8},{4,12},{8,0},{12,4},{1,9},{5,13},{9,1},{13,5},{2,10},{6,14},... | collective-permute-start | bytes 294920 | tf_op jit(solution)/shard_map/ppermute | solution.py:376
  66.2 1.1 %collective-permute-start.12 = (bf16[3,4,4096]{2,1,0:T(4,128)(2,1)S(1)}, bf16[3,4,4096]{2,1,0:T(4,128)(2,1)S(1)}, u32[]{:S(2)}, u32[]{:S(2)}) collective-permute-start(bf16[3,4,4096]{2,1,0:T(4,128)(2,1)S(1)} %get-tuple-element.26), channel_id=1, source_target_pairs={{0,12},{4,8},{8,4},{12,0},{1,13},{5,9},{9,5},{13,1},{2,14},{6,10},... | collective-permute-start | bytes 294920 | tf_op jit(solution)/shard_map/ppermute | solution.py:376
  67.3 0.0 collective-permute-done.10
  67.3 6.4 %collective-permute-done.11 = bf16[3,4,4096]{2,1,0:T(4,128)(2,1)S(1)} collective-permute-done((bf16[3,4,4096]{2,1,0:T(4,128)(2,1)S(1)}, bf16[3,4,4096]{2,1,0:T(4,128)(2,1)S(1)}, u32[]{:S(2)}, u32[]{:S(2)}) %collective-permute-start.11) | collective-permute-done | bytes 98336 | tf_op jit(solution)/shard_map/ppermute | solution.py:376
  73.7 0.7 %fusion = bf16[4,3,4096]{2,0,1:T(4,128)(2,1)} fusion(bf16[3,4,4096]{2,1,0:T(4,128)(2,1)S(1)} %collective-permute-done.12, bf16[3,4,4096]{2,1,0:T(4,128)(2,1)S(1)} %collective-permute-done.11, bf16[3,4,4096]{2,1,0:T(4,128)(2,1)S(1)} %collective-permute-done.10, bf16[3,4,4096]{2,1,0:T(4,128)(2,1)S(1)} %get-tuple-element.23), kind=kLoop, calls=%fused_computation.1 | loop fusion | flops 393216 | bytes 491520 | tf_op jit(solution)/shard_map/transpose | solution.py:470
  (27 shorter events, 0.1 us)
Async XLA Ops:
  0.0 9.0 %collective-permute-start.2 = (bf16[3,4,4096]{2,1,0:T(4,128)(2,1)}, bf16[3,4,4096]{2,1,0:T(4,128)(2,1)S(1)}, u32[]{:S(2)}, u32[]{:S(2)}) collective-permute-start(bf16[3,4,4096]{2,1,0:T(4,128)(2,1)} %bitcast.19), channel_id=1, source_target_pairs={{0,12},{4,8},{8,4},{12,0},{1,13},{5,9},{9,5},{13,1},{2,14},{6,10},... | collective-permute-start | bytes 294920 | tf_op jit(solution)/shard_map/ppermute | solution.py:376
  5.0 8.5 %collective-permute-start.1 = (bf16[3,4,4096]{2,1,0:T(4,128)(2,1)}, bf16[3,4,4096]{2,1,0:T(4,128)(2,1)S(1)}, u32[]{:S(2)}, u32[]{:S(2)}) collective-permute-start(bf16[3,4,4096]{2,1,0:T(4,128)(2,1)} %bitcast.20), channel_id=1, source_target_pairs={{0,8},{4,12},{8,0},{12,4},{1,9},{5,13},{9,1},{13,5},{2,10},{6,14},... | collective-permute-start | bytes 294920 | tf_op jit(solution)/shard_map/ppermute | solution.py:376
  5.1 8.5 %collective-permute-start = (bf16[3,4,4096]{2,1,0:T(4,128)(2,1)}, bf16[3,4,4096]{2,1,0:T(4,128)(2,1)S(1)}, u32[]{:S(2)}, u32[]{:S(2)}) collective-permute-start(bf16[3,4,4096]{2,1,0:T(4,128)(2,1)} %bitcast.21), channel_id=1, source_target_pairs={{0,4},{4,0},{8,12},{12,8},{1,5},{5,1},{9,13},{13,9},{2,6},{6,2},{1... | collective-permute-start | bytes 294920 | tf_op jit(solution)/shard_map/ppermute | solution.py:376
  6.3 0.7 copy-start.12
  6.9 0.7 copy-start.13
  7.6 6.0 %copy-start.1 = (bf16[4,4096,96]{1,2,0:T(8,128)(2,1)S(1)}, bf16[4,4096,96]{1,2,0:T(8,128)(2,1)}, u32[]{:S(2)}) copy-start(bf16[4,4096,96]{1,2,0:T(8,128)(2,1)} %param.21) | copy-start | bytes 9437188
  7.6 6.0 %copy-start.9 = (bf16[4,3,4096]{2,0,1:T(4,128)(2,1)S(1)}, bf16[4,3,4096]{2,0,1:T(4,128)(2,1)}, u32[]{:S(2)}) copy-start(bf16[4,3,4096]{2,0,1:T(4,128)(2,1)} %param.16) | copy-start | bytes 294916
  7.6 9.7 %copy-start = (bf16[4096,2048]{1,0:T(8,128)(2,1)S(1)}, bf16[4096,2048]{1,0:T(8,128)(2,1)}, u32[]{:S(2)}) copy-start(bf16[4096,2048]{1,0:T(8,128)(2,1)} %refs_3_.1) | copy-start | bytes 50331652
  7.6 9.7 %copy-start.2 = (bf16[4096,128]{1,0:T(8,128)(2,1)S(1)}, bf16[4096,128]{1,0:T(8,128)(2,1)}, u32[]{:S(2)}) copy-start(bf16[4096,128]{1,0:T(8,128)(2,1)} %refs_1_.4) | copy-start | bytes 3145732
  7.6 9.7 %copy-start.3 = (bf16[4096,128]{1,0:T(8,128)(2,1)S(1)}, bf16[4096,128]{1,0:T(8,128)(2,1)}, u32[]{:S(2)}) copy-start(bf16[4096,128]{1,0:T(8,128)(2,1)} %refs_2_.4) | copy-start | bytes 3145732
  8.3 12.3 %copy-start.8 = (bf16[4,32,2048]{2,1,0:T(8,128)(2,1)S(1)}, bf16[4,32,2048]{2,1,0:T(8,128)(2,1)}, u32[]{:S(2)}) copy-start(bf16[4,32,2048]{2,1,0:T(8,128)(2,1)} %param.22) | copy-start | bytes 1572868
  8.4 12.3 %copy-start.10 = (bf16[4,32,128]{2,1,0:T(8,128)(2,1)S(1)}, bf16[4,32,128]{2,1,0:T(8,128)(2,1)}, u32[]{:S(2)}) copy-start(bf16[4,32,128]{2,1,0:T(8,128)(2,1)} %param.23) | copy-start | bytes 98308
  8.4 12.3 %copy-start.11 = (bf16[4,32,128]{2,1,0:T(8,128)(2,1)S(1)}, bf16[4,32,128]{2,1,0:T(8,128)(2,1)}, u32[]{:S(2)}) copy-start(bf16[4,32,128]{2,1,0:T(8,128)(2,1)} %param.24) | copy-start | bytes 98308
  14.9 1.2 %collective-permute-start.3 = (bf16[32,128]{1,0:T(8,128)(2,1)S(1)}, bf16[32,128]{1,0:T(8,128)(2,1)S(1)}, u32[]{:S(2)}, u32[]{:S(2)}) collective-permute-start(bf16[32,128]{1,0:T(8,128)(2,1)S(1)} %get-tuple-element.18.left_ref), channel_id=1, source_target_pairs={{0,1},{1,0},{2,3},{3,2},{4,5},{5,4},{6,7},{7,6},{8,9},{9,8},{10,11... | collective-permute-start | bytes 24584 | tf_op jit(solution)/shard_map/ppermute | solution.py:379
  16.1 4.5 %collective-permute-start.5 = (bf16[32,128]{1,0:T(8,128)(2,1)S(1)}, bf16[32,128]{1,0:T(8,128)(2,1)S(1)}, u32[]{:S(2)}, u32[]{:S(2)}) collective-permute-start(bf16[32,128]{1,0:T(8,128)(2,1)S(1)} %shard_map.157), channel_id=1, source_target_pairs={{0,4},{1,12},{2,0},{3,8},{4,5},{5,13},{6,1},{7,9},{8,6},{9,14},{10... | collective-permute-start | bytes 24584 | tf_op jit(solution)/shard_map/ppermute | solution.py:388
  16.6 4.0 %collective-permute-start.4 = (bf16[32,128]{1,0:T(8,128)(2,1)S(1)}, bf16[32,128]{1,0:T(8,128)(2,1)S(1)}, u32[]{:S(2)}, u32[]{:S(2)}) collective-permute-start(bf16[32,128]{1,0:T(8,128)(2,1)S(1)} %shard_map.157), channel_id=1, source_target_pairs={{0,0},{1,8},{2,4},{3,12},{4,1},{5,9},{6,5},{7,13},{8,2},{9,10},{10... | collective-permute-start | bytes 24584 | tf_op jit(solution)/shard_map/ppermute | solution.py:388
  20.7 18.3 %copy-start.6 = (bf16[1,4,512,128]{3,2,1,0:T(8,128)(2,1)S(1)}, bf16[1,4,512,128]{3,2,1,0:T(8,128)(2,1)}, u32[]{:S(2)}) copy-start(bf16[1,4,512,128]{3,2,1,0:T(8,128)(2,1)} %keys_ref.1) | copy-start | bytes 1572868
  20.7 18.3 %copy-start.7 = (bf16[1,4,512,128]{3,2,1,0:T(8,128)(2,1)S(1)}, bf16[1,4,512,128]{3,2,1,0:T(8,128)(2,1)}, u32[]{:S(2)}) copy-start(bf16[1,4,512,128]{3,2,1,0:T(8,128)(2,1)} %values_ref.1) | copy-start | bytes 1572868
  20.7 30.9 %copy-start.5 = (bf16[4,2048,32]{1,2,0:T(8,128)(2,1)S(1)}, bf16[4,2048,32]{1,2,0:T(8,128)(2,1)}, u32[]{:S(2)}) copy-start(bf16[4,2048,32]{1,2,0:T(8,128)(2,1)} %param.25) | copy-start | bytes 1572868
  39.0 14.7 %slice-start = ((s8[16777216]{0:T(1024)(128)(4,1)}), s8[4194304]{0:T(1024)(128)(4,1)S(1)}, s32[]{:S(2)}) async-start(s8[16777216]{0:T(1024)(128)(4,1)} %bitcast.13), calls=%async_computation.2 | async-start | bytes 8388608
  51.6 2.2 %slice-start.1 = ((s8[16777216]{0:T(1024)(128)(4,1)}), s8[4194304]{0:T(1024)(128)(4,1)S(1)}, s32[]{:S(2)}) async-start(s8[16777216]{0:T(1024)(128)(4,1)} %bitcast.13), calls=%async_computation.3 | async-start | bytes 8388608
  51.6 3.5 %slice-start.2 = ((s8[16777216]{0:T(1024)(128)(4,1)}), s8[4194304]{0:T(1024)(128)(4,1)S(1)}, s32[]{:S(2)}) async-start(s8[16777216]{0:T(1024)(128)(4,1)} %bitcast.13), calls=%async_computation.4 | async-start | bytes 8388608
  51.6 4.7 %slice-start.3 = ((s8[16777216]{0:T(1024)(128)(4,1)}), s8[4194304]{0:T(1024)(128)(4,1)S(1)}, s32[]{:S(2)}) async-start(s8[16777216]{0:T(1024)(128)(4,1)} %bitcast.13), calls=%async_computation.5 | async-start | bytes 8388608
  52.1 7.2 %copy-start.4 = (bf16[4,32,4096]{2,1,0:T(8,128)(2,1)S(1)}, bf16[4,32,4096]{2,1,0:T(8,128)(2,1)}, u32[]{:S(2)}) copy-start(bf16[4,32,4096]{2,1,0:T(8,128)(2,1)} %param.26) | copy-start | bytes 3145732
  52.1 7.1 %collective-permute-start.9 = (bf16[16,128]{1,0:T(8,128)(2,1)S(1)}, bf16[16,128]{1,0:T(8,128)(2,1)S(1)}, u32[]{:S(2)}, u32[]{:S(2)}) collective-permute-start(bf16[16,128]{1,0:T(8,128)(2,1)S(1)} %get-tuple-element.22), channel_id=1, source_target_pairs={{0,3},{1,7},{2,11},{3,15},{4,2},{5,6},{6,10},{7,14},{8,1},{9,5},{1... | collective-permute-start | bytes 12296 | tf_op jit(solution)/shard_map/ppermute | solution.py:396
  52.1 7.1 %collective-permute-start.8 = (bf16[16,128]{1,0:T(8,128)(2,1)S(1)}, bf16[16,128]{1,0:T(8,128)(2,1)S(1)}, u32[]{:S(2)}, u32[]{:S(2)}) collective-permute-start(bf16[16,128]{1,0:T(8,128)(2,1)S(1)} %get-tuple-element.22), channel_id=1, source_target_pairs={{0,2},{1,6},{2,10},{3,14},{4,3},{5,7},{6,11},{7,15},{8,0},{9,4},{1... | collective-permute-start | bytes 12296 | tf_op jit(solution)/shard_map/ppermute | solution.py:396
  52.7 6.5 %collective-permute-start.7 = (bf16[16,128]{1,0:T(8,128)(2,1)S(1)}, bf16[16,128]{1,0:T(8,128)(2,1)S(1)}, u32[]{:S(2)}, u32[]{:S(2)}) collective-permute-start(bf16[16,128]{1,0:T(8,128)(2,1)S(1)} %get-tuple-element.22), channel_id=1, source_target_pairs={{0,1},{1,5},{2,9},{3,13},{4,0},{5,4},{6,8},{7,12},{8,3},{9,7},{10,... | collective-permute-start | bytes 12296 | tf_op jit(solution)/shard_map/ppermute | solution.py:396
  52.9 6.4 %collective-permute-start.6 = (bf16[16,128]{1,0:T(8,128)(2,1)S(1)}, bf16[16,128]{1,0:T(8,128)(2,1)S(1)}, u32[]{:S(2)}, u32[]{:S(2)}) collective-permute-start(bf16[16,128]{1,0:T(8,128)(2,1)S(1)} %get-tuple-element.22), channel_id=1, source_target_pairs={{0,0},{1,4},{2,8},{3,12},{4,1},{5,5},{6,9},{7,13},{8,2},{9,6},{10,... | collective-permute-start | bytes 12296 | tf_op jit(solution)/shard_map/ppermute | solution.py:396
  59.9 7.4 %collective-permute-start.10 = (bf16[3,4,4096]{2,1,0:T(4,128)(2,1)S(1)}, bf16[3,4,4096]{2,1,0:T(4,128)(2,1)S(1)}, u32[]{:S(2)}, u32[]{:S(2)}) collective-permute-start(bf16[3,4,4096]{2,1,0:T(4,128)(2,1)S(1)} %get-tuple-element.24), channel_id=1, source_target_pairs={{0,4},{4,0},{8,12},{12,8},{1,5},{5,1},{9,13},{13,9},{2,6},{6,2},{1... | collective-permute-start | bytes 294920 | tf_op jit(solution)/shard_map/ppermute | solution.py:376
  61.7 12.0 %collective-permute-start.11 = (bf16[3,4,4096]{2,1,0:T(4,128)(2,1)S(1)}, bf16[3,4,4096]{2,1,0:T(4,128)(2,1)S(1)}, u32[]{:S(2)}, u32[]{:S(2)}) collective-permute-start(bf16[3,4,4096]{2,1,0:T(4,128)(2,1)S(1)} %get-tuple-element.25), channel_id=1, source_target_pairs={{0,8},{4,12},{8,0},{12,4},{1,9},{5,13},{9,1},{13,5},{2,10},{6,14},... | collective-permute-start | bytes 294920 | tf_op jit(solution)/shard_map/ppermute | solution.py:376
  66.2 7.5 %collective-permute-start.12 = (bf16[3,4,4096]{2,1,0:T(4,128)(2,1)S(1)}, bf16[3,4,4096]{2,1,0:T(4,128)(2,1)S(1)}, u32[]{:S(2)}, u32[]{:S(2)}) collective-permute-start(bf16[3,4,4096]{2,1,0:T(4,128)(2,1)S(1)} %get-tuple-element.26), channel_id=1, source_target_pairs={{0,12},{4,8},{8,4},{12,0},{1,13},{5,9},{9,5},{13,1},{2,14},{6,10},... | collective-permute-start | bytes 294920 | tf_op jit(solution)/shard_map/ppermute | solution.py:376

commit v21 on v20

--- a/solution.py
+++ b/solution.py
@@ -465,7 +465,7 @@
         8 * count * out_cols + 2 * owned * width * out_cols,
     )(out_total, slots, grow_out.reshape(owned * width, -1), *out_ranks)
     result = leaving[0].astype(jnp.float32)
-    for shift in range(1, blocks):
+    for shift in reversed(range(1, blocks)):
         result = result + over_tensor(leaving[shift], shift).astype(jnp.float32)
     return jnp.transpose(result.astype(jnp.bfloat16), (1, 0, 2))
 

time: 74.7 us -> 74.6 us (level)
  starting transfers between devices: 15.8 us -> 14.9 us
  waiting for transfers between devices: 12.7 us -> 13.5 us
    ppermute x6, starting transfers between devices: 13 us -> 12.1 us  [over_tensor(): return lax.ppermute(value, 'tensor', route)]
    ppermute x6, waiting for transfers between devices: 11.5 us -> 12.3 us  [over_tensor(): return lax.ppermute(value, 'tensor', route)]
  transfers between devices with their start and end apart: 13 -> 13, of which waited for: 4 -> 5; matrix products, arithmetic and copies ran while one was open for 0% -> 0% of each run, Pallas kernels for 9% -> 9%
where the time goes in v21:
time: 74.6 us; the launch traced here: 74.3 us
  blocking collectives  29.1 us (39%)
  starting transfers between devices  14.9 us (20%)
  waiting for transfers between devices  13.5 us (18%)
  Pallas kernels  11.3 us (15%)
  local copies, waits for them, and re-layouts  3.89 us (5%)
  between operations  0.91 us (1%)
  other arithmetic  0.75 us (1%)
    all_to_all x2, blocking collectives, exchange(): return lax.all_to_all(value, EVERY, split_axis=0, concat_axis=0, tiled=True)  29.1 us
    ppermute x6, waiting for transfers between devices, over_tensor(): return lax.ppermute(value, 'tensor', route)  12.3 us
    ppermute x6, starting transfers between devices, over_tensor(): return lax.ppermute(value, 'tensor', route)  12.1 us
    pallas_call x2, Pallas kernels, product(): call(product_kernel, shape((rows.shape[0], width), jnp.float32), [VMEM] *...  6.31 us
    unnamed x36, local copies, waits for them, and re-layouts  3.89 us
    ppermute x4, starting transfers between devices, to_out_growers(): return lax.ppermute(value, EVERY, route)  1.56 us
  transfers between devices with their start and end apart: 13, of which 5 were waited for; matrix products, arithmetic and copies ran while one was open for 0% of the time, Pallas kernels for 9%

profile of v21, /device:TPU:0, one launch (start us, length us, event | category | flops | bytes accessed | tf_op | source)
XLA Modules:
  0.0 74.3 jit_solution(15271715590179291005)
XLA Ops:
  0.0 5.0 %collective-permute-start.2 = (bf16[3,4,4096]{2,1,0:T(4,128)(2,1)}, bf16[3,4,4096]{2,1,0:T(4,128)(2,1)S(1)}, u32[]{:S(2)}, u32[]{:S(2)}) collective-permute-start(bf16[3,4,4096]{2,1,0:T(4,128)(2,1)} %bitcast.19), channel_id=1, source_target_pairs={{0,12},{4,8},{8,4},{12,0},{1,13},{5,9},{9,5},{13,1},{2,14},{6,10},... | collective-permute-start | bytes 294920 | tf_op jit(solution)/shard_map/ppermute | solution.py:376
  5.0 0.0 collective-permute-start.1
  5.1 0.6 collective-permute-start
  6.3 0.6 copy-done.12
  6.9 0.7 copy-done.13
  7.6 0.7 shard_map.154
  8.3 0.0 copy-start.8
  8.4 0.0 copy-start.10
  8.4 0.0 copy-start.11
  8.4 0.6 collective-permute-done.2.refs_3_
  9.0 4.6 %collective-permute-done.1.refs_2_ = bf16[3,4,4096]{2,1,0:T(4,128)(2,1)S(1)} collective-permute-done((bf16[3,4,4096]{2,1,0:T(4,128)(2,1)}, bf16[3,4,4096]{2,1,0:T(4,128)(2,1)S(1)}, u32[]{:S(2)}, u32[]{:S(2)}) %collective-permute-start.1) | collective-permute-done | bytes 98336 | tf_op jit(solution)/shard_map/ppermute | solution.py:376
  13.5 0.0 collective-permute-done.refs_1_
  13.5 1.4 %shard_map.155 = (bf16[48,4096]{1,0:T(8,128)(2,1)S(1)}, bf16[32,128]{1,0:T(8,128)(2,1)S(1)}) custom-call(bf16[3,4,4096]{2,1,0:T(4,128)(2,1)S(1)} %bitcast.22, bf16[3,4,4096]{2,1,0:T(4,128)(2,1)S(1)} %collective-permute-done.refs_1_, bf16[3,4,4096]{2,1,0:T(4,128)(2,1)S(1)} %collective-permute-done.1.refs_2_, ...), custom_call_target="tpu_custom_call" | custom-call | flops 150994944 | bytes 3932160 | tf_op jit(solution)/shard_map/pallas_call | solution.py:414
  14.9 0.0 collective-permute-start.3
  14.9 1.2 %collective-permute-done.3.right_ref = bf16[32,128]{1,0:T(8,128)(2,1)S(1)} collective-permute-done((bf16[32,128]{1,0:T(8,128)(2,1)S(1)}, bf16[32,128]{1,0:T(8,128)(2,1)S(1)}, u32[]{:S(2)}, u32[]{:S(2)}) %collective-permute-start.3) | collective-permute-done | bytes 8224 | tf_op jit(solution)/shard_map/ppermute | solution.py:379
  16.1 0.5 collective-permute-start.5
  16.6 0.6 collective-permute-start.4
  17.3 0.0 copy-done
  17.3 3.3 %shard_map.156.total_ref = f32[48,2304]{1,0:T(8,128)S(1)} custom-call(bf16[48,4096]{1,0:T(8,128)(2,1)S(1)} %get-tuple-element.17.rows_ref, bf16[4096,2048]{1,0:T(8,128)(2,1)S(1)} %copy-done, bf16[4096,128]{1,0:T(8,128)(2,1)S(1)} %copy-done.2, bf16[4096,128]{1,0:T(8,128)(2,1)S(1)} %copy-done.3), custom_call_target="tpu_custom_call" | custom-call | tf_op jit(solution)/shard_map/pallas_call | solution.py:152
  20.6 0.0 collective-permute-done.5.refs_1_
  20.7 0.0 collective-permute-done.4.refs_0_
  20.7 0.0 copy-start.6
  20.7 0.0 copy-start.7
  20.7 0.0 copy-start.5
  20.7 0.9 %shard_map.158 = bf16[16,56,128]{2,1,0:T(8,128)(2,1)S(1)} custom-call(f32[48,2304]{1,0:T(8,128)S(1)} %shard_map.156.total_ref, s32[48,128]{1,0:T(8,128)S(1)} %get-tuple-element.16.refs_5_.slots_ref, bf16[32,128]{1,0:T(8,128)(2,1)S(1)} %collective-permute-done.4.refs_0_, bf16[32,128]{1,0:T(8,128)(2,1)S(1)} %collective-permute-done.5.refs_1_, ...), custom_call_target="tpu_custom_call" | custom-call | tf_op jit(solution)/shard_map/pallas_call | solution.py:428
  21.7 17.4 %all_to_all.10.arrived_ref = bf16[16,56,128]{2,1,0:T(8,128)(2,1)S(1)} all-to-all(bf16[16,56,128]{2,1,0:T(8,128)(2,1)S(1)} %shard_map.158), channel_id=1, replica_groups=mesh['parts'=2,'tensor'=4,'dp'=2,'pipe'=2] {'tensor','dp','pipe'}, dimensions={0} | all-to-all | bytes 458752 | tf_op jit(solution)/shard_map/all_to_all | solution.py:402
  39.0 0.8 %shard_map.159 = bf16[16,48,128]{2,1,0:T(8,128)(2,1)S(1)} custom-call(bf16[16,56,128]{2,1,0:T(8,128)(2,1)S(1)} %all_to_all.10.arrived_ref, bf16[1,4,512,128]{3,2,1,0:T(8,128)(2,1)S(1)} %copy-done.6, bf16[1,4,512,128]{3,2,1,0:T(8,128)(2,1)S(1)} %copy-done.7, s32[1]{0:T(128)S(6)} %copy.17.length_ref, f32[56,128]{1,0:T(8,128)S(1)} %get-tuple-element.19.cosine_ref, ...), custom_call_target="tpu_custom_call" | custom-call | tf_op jit(solution)/shard_map/pallas_call | solution.py:441
  39.8 11.8 %all_to_all.11.got_ref = bf16[16,48,128]{2,1,0:T(8,128)(2,1)S(1)} all-to-all(bf16[16,48,128]{2,1,0:T(8,128)(2,1)S(1)} %shard_map.159), channel_id=1, replica_groups=mesh['parts'=2,'tensor'=4,'dp'=2,'pipe'=2] {'tensor','dp','pipe'}, dimensions={0} | all-to-all | bytes 393216 | tf_op jit(solution)/shard_map/all_to_all | solution.py:402
  51.6 0.6 shard_map.160
  52.1 0.0 collective-permute-start.9
  52.1 0.6 collective-permute-start.8
  52.7 0.2 collective-permute-start.7
  52.9 0.8 %collective-permute-start.6 = (bf16[16,128]{1,0:T(8,128)(2,1)S(1)}, bf16[16,128]{1,0:T(8,128)(2,1)S(1)}, u32[]{:S(2)}, u32[]{:S(2)}) collective-permute-start(bf16[16,128]{1,0:T(8,128)(2,1)S(1)} %get-tuple-element.22), channel_id=1, source_target_pairs={{0,0},{1,4},{2,8},{3,12},{4,1},{5,5},{6,9},{7,13},{8,2},{9,6},{10,... | collective-permute-start | bytes 12296 | tf_op jit(solution)/shard_map/ppermute | solution.py:396
  53.7 0.0 slice-done.1
  53.8 1.3 %slice-done.2 = s8[4194304]{0:T(1024)(128)(4,1)S(1)} async-done(((s8[16777216]{0:T(1024)(128)(4,1)}), s8[4194304]{0:T(1024)(128)(4,1)S(1)}, s32[]{:S(2)}) %slice-start.2) | async-done | bytes 4194328
  55.0 1.2 %slice-done.3 = s8[4194304]{0:T(1024)(128)(4,1)S(1)} async-done(((s8[16777216]{0:T(1024)(128)(4,1)}), s8[4194304]{0:T(1024)(128)(4,1)S(1)}, s32[]{:S(2)}) %slice-start.3) | async-done | bytes 4194328
  56.2 3.0 %shard_map.161.total_ref = f32[48,4096]{1,0:T(8,128)S(1)} custom-call(bf16[48,2048]{1,0:T(8,128)(2,1)S(1)} %get-tuple-element.21.rows_ref, bf16[2048,4096]{1,0:T(8,128)(2,1)S(1)} %bitcast.14), custom_call_target="tpu_custom_call" | custom-call | tf_op jit(solution)/shard_map/pallas_call | solution.py:152
  59.2 0.0 collective-permute-done.9.refs_3_
  59.3 0.0 collective-permute-done.7.refs_1_
  59.3 0.0 collective-permute-done.6.refs_0_
  59.3 0.6 shard_map.162
  59.9 5.7 %collective-permute-start.10 = (bf16[3,4,4096]{2,1,0:T(4,128)(2,1)S(1)}, bf16[3,4,4096]{2,1,0:T(4,128)(2,1)S(1)}, u32[]{:S(2)}, u32[]{:S(2)}) collective-permute-start(bf16[3,4,4096]{2,1,0:T(4,128)(2,1)S(1)} %get-tuple-element.24), channel_id=1, source_target_pairs={{0,12},{4,8},{8,4},{12,0},{1,13},{5,9},{9,5},{13,1},{2,14},{6,10},... | collective-permute-start | bytes 294920 | tf_op jit(solution)/shard_map/ppermute | solution.py:376
  65.7 0.3 collective-permute-start.11
  66.0 0.5 collective-permute-start.12
  66.4 3.0 %collective-permute-done.10 = bf16[3,4,4096]{2,1,0:T(4,128)(2,1)S(1)} collective-permute-done((bf16[3,4,4096]{2,1,0:T(4,128)(2,1)S(1)}, bf16[3,4,4096]{2,1,0:T(4,128)(2,1)S(1)}, u32[]{:S(2)}, u32[]{:S(2)}) %collective-permute-start.10) | collective-permute-done | bytes 98336 | tf_op jit(solution)/shard_map/ppermute | solution.py:376
  69.4 4.2 %collective-permute-done.11 = bf16[3,4,4096]{2,1,0:T(4,128)(2,1)S(1)} collective-permute-done((bf16[3,4,4096]{2,1,0:T(4,128)(2,1)S(1)}, bf16[3,4,4096]{2,1,0:T(4,128)(2,1)S(1)}, u32[]{:S(2)}, u32[]{:S(2)}) %collective-permute-start.11) | collective-permute-done | bytes 98336 | tf_op jit(solution)/shard_map/ppermute | solution.py:376
  73.6 0.0 collective-permute-done.12
  73.6 0.7 %fusion = bf16[4,3,4096]{2,0,1:T(4,128)(2,1)} fusion(bf16[3,4,4096]{2,1,0:T(4,128)(2,1)S(1)} %collective-permute-done.12, bf16[3,4,4096]{2,1,0:T(4,128)(2,1)S(1)} %collective-permute-done.11, bf16[3,4,4096]{2,1,0:T(4,128)(2,1)S(1)} %collective-permute-done.10, bf16[3,4,4096]{2,1,0:T(4,128)(2,1)S(1)} %get-tuple-element.23), kind=kLoop, calls=%fused_computation.1 | loop fusion | flops 393216 | bytes 491520 | tf_op jit(solution)/shard_map/transpose | solution.py:470
  (27 shorter events, 0.1 us)
Async XLA Ops:
  0.0 9.0 %collective-permute-start.2 = (bf16[3,4,4096]{2,1,0:T(4,128)(2,1)}, bf16[3,4,4096]{2,1,0:T(4,128)(2,1)S(1)}, u32[]{:S(2)}, u32[]{:S(2)}) collective-permute-start(bf16[3,4,4096]{2,1,0:T(4,128)(2,1)} %bitcast.19), channel_id=1, source_target_pairs={{0,12},{4,8},{8,4},{12,0},{1,13},{5,9},{9,5},{13,1},{2,14},{6,10},... | collective-permute-start | bytes 294920 | tf_op jit(solution)/shard_map/ppermute | solution.py:376
  5.0 8.5 %collective-permute-start.1 = (bf16[3,4,4096]{2,1,0:T(4,128)(2,1)}, bf16[3,4,4096]{2,1,0:T(4,128)(2,1)S(1)}, u32[]{:S(2)}, u32[]{:S(2)}) collective-permute-start(bf16[3,4,4096]{2,1,0:T(4,128)(2,1)} %bitcast.20), channel_id=1, source_target_pairs={{0,8},{4,12},{8,0},{12,4},{1,9},{5,13},{9,1},{13,5},{2,10},{6,14},... | collective-permute-start | bytes 294920 | tf_op jit(solution)/shard_map/ppermute | solution.py:376
  5.1 8.5 %collective-permute-start = (bf16[3,4,4096]{2,1,0:T(4,128)(2,1)}, bf16[3,4,4096]{2,1,0:T(4,128)(2,1)S(1)}, u32[]{:S(2)}, u32[]{:S(2)}) collective-permute-start(bf16[3,4,4096]{2,1,0:T(4,128)(2,1)} %bitcast.21), channel_id=1, source_target_pairs={{0,4},{4,0},{8,12},{12,8},{1,5},{5,1},{9,13},{13,9},{2,6},{6,2},{1... | collective-permute-start | bytes 294920 | tf_op jit(solution)/shard_map/ppermute | solution.py:376
  6.3 0.7 copy-start.12
  6.9 0.7 copy-start.13
  7.6 6.0 %copy-start.1 = (bf16[4,4096,96]{1,2,0:T(8,128)(2,1)S(1)}, bf16[4,4096,96]{1,2,0:T(8,128)(2,1)}, u32[]{:S(2)}) copy-start(bf16[4,4096,96]{1,2,0:T(8,128)(2,1)} %param.21) | copy-start | bytes 9437188
  7.6 6.0 %copy-start.9 = (bf16[4,3,4096]{2,0,1:T(4,128)(2,1)S(1)}, bf16[4,3,4096]{2,0,1:T(4,128)(2,1)}, u32[]{:S(2)}) copy-start(bf16[4,3,4096]{2,0,1:T(4,128)(2,1)} %param.16) | copy-start | bytes 294916
  7.6 9.7 %copy-start = (bf16[4096,2048]{1,0:T(8,128)(2,1)S(1)}, bf16[4096,2048]{1,0:T(8,128)(2,1)}, u32[]{:S(2)}) copy-start(bf16[4096,2048]{1,0:T(8,128)(2,1)} %refs_3_.1) | copy-start | bytes 50331652
  7.6 9.7 %copy-start.2 = (bf16[4096,128]{1,0:T(8,128)(2,1)S(1)}, bf16[4096,128]{1,0:T(8,128)(2,1)}, u32[]{:S(2)}) copy-start(bf16[4096,128]{1,0:T(8,128)(2,1)} %refs_1_.4) | copy-start | bytes 3145732
  7.6 9.7 %copy-start.3 = (bf16[4096,128]{1,0:T(8,128)(2,1)S(1)}, bf16[4096,128]{1,0:T(8,128)(2,1)}, u32[]{:S(2)}) copy-start(bf16[4096,128]{1,0:T(8,128)(2,1)} %refs_2_.4) | copy-start | bytes 3145732
  8.3 12.3 %copy-start.8 = (bf16[4,32,2048]{2,1,0:T(8,128)(2,1)S(1)}, bf16[4,32,2048]{2,1,0:T(8,128)(2,1)}, u32[]{:S(2)}) copy-start(bf16[4,32,2048]{2,1,0:T(8,128)(2,1)} %param.22) | copy-start | bytes 1572868
  8.4 12.3 %copy-start.10 = (bf16[4,32,128]{2,1,0:T(8,128)(2,1)S(1)}, bf16[4,32,128]{2,1,0:T(8,128)(2,1)}, u32[]{:S(2)}) copy-start(bf16[4,32,128]{2,1,0:T(8,128)(2,1)} %param.23) | copy-start | bytes 98308
  8.4 12.3 %copy-start.11 = (bf16[4,32,128]{2,1,0:T(8,128)(2,1)S(1)}, bf16[4,32,128]{2,1,0:T(8,128)(2,1)}, u32[]{:S(2)}) copy-start(bf16[4,32,128]{2,1,0:T(8,128)(2,1)} %param.24) | copy-start | bytes 98308
  14.9 1.2 %collective-permute-start.3 = (bf16[32,128]{1,0:T(8,128)(2,1)S(1)}, bf16[32,128]{1,0:T(8,128)(2,1)S(1)}, u32[]{:S(2)}, u32[]{:S(2)}) collective-permute-start(bf16[32,128]{1,0:T(8,128)(2,1)S(1)} %get-tuple-element.18.left_ref), channel_id=1, source_target_pairs={{0,1},{1,0},{2,3},{3,2},{4,5},{5,4},{6,7},{7,6},{8,9},{9,8},{10,11... | collective-permute-start | bytes 24584 | tf_op jit(solution)/shard_map/ppermute | solution.py:379
  16.1 4.5 %collective-permute-start.5 = (bf16[32,128]{1,0:T(8,128)(2,1)S(1)}, bf16[32,128]{1,0:T(8,128)(2,1)S(1)}, u32[]{:S(2)}, u32[]{:S(2)}) collective-permute-start(bf16[32,128]{1,0:T(8,128)(2,1)S(1)} %shard_map.157), channel_id=1, source_target_pairs={{0,4},{1,12},{2,0},{3,8},{4,5},{5,13},{6,1},{7,9},{8,6},{9,14},{10... | collective-permute-start | bytes 24584 | tf_op jit(solution)/shard_map/ppermute | solution.py:388
  16.6 4.0 %collective-permute-start.4 = (bf16[32,128]{1,0:T(8,128)(2,1)S(1)}, bf16[32,128]{1,0:T(8,128)(2,1)S(1)}, u32[]{:S(2)}, u32[]{:S(2)}) collective-permute-start(bf16[32,128]{1,0:T(8,128)(2,1)S(1)} %shard_map.157), channel_id=1, source_target_pairs={{0,0},{1,8},{2,4},{3,12},{4,1},{5,9},{6,5},{7,13},{8,2},{9,10},{10... | collective-permute-start | bytes 24584 | tf_op jit(solution)/shard_map/ppermute | solution.py:388
  20.7 18.3 %copy-start.6 = (bf16[1,4,512,128]{3,2,1,0:T(8,128)(2,1)S(1)}, bf16[1,4,512,128]{3,2,1,0:T(8,128)(2,1)}, u32[]{:S(2)}) copy-start(bf16[1,4,512,128]{3,2,1,0:T(8,128)(2,1)} %keys_ref.1) | copy-start | bytes 1572868
  20.7 18.3 %copy-start.7 = (bf16[1,4,512,128]{3,2,1,0:T(8,128)(2,1)S(1)}, bf16[1,4,512,128]{3,2,1,0:T(8,128)(2,1)}, u32[]{:S(2)}) copy-start(bf16[1,4,512,128]{3,2,1,0:T(8,128)(2,1)} %values_ref.1) | copy-start | bytes 1572868
  20.7 30.9 %copy-start.5 = (bf16[4,2048,32]{1,2,0:T(8,128)(2,1)S(1)}, bf16[4,2048,32]{1,2,0:T(8,128)(2,1)}, u32[]{:S(2)}) copy-start(bf16[4,2048,32]{1,2,0:T(8,128)(2,1)} %param.25) | copy-start | bytes 1572868
  39.0 14.7 %slice-start = ((s8[16777216]{0:T(1024)(128)(4,1)}), s8[4194304]{0:T(1024)(128)(4,1)S(1)}, s32[]{:S(2)}) async-start(s8[16777216]{0:T(1024)(128)(4,1)} %bitcast.13), calls=%async_computation.2 | async-start | bytes 8388608
  51.6 2.2 %slice-start.1 = ((s8[16777216]{0:T(1024)(128)(4,1)}), s8[4194304]{0:T(1024)(128)(4,1)S(1)}, s32[]{:S(2)}) async-start(s8[16777216]{0:T(1024)(128)(4,1)} %bitcast.13), calls=%async_computation.3 | async-start | bytes 8388608
  51.6 3.5 %slice-start.2 = ((s8[16777216]{0:T(1024)(128)(4,1)}), s8[4194304]{0:T(1024)(128)(4,1)S(1)}, s32[]{:S(2)}) async-start(s8[16777216]{0:T(1024)(128)(4,1)} %bitcast.13), calls=%async_computation.4 | async-start | bytes 8388608
  51.6 4.7 %slice-start.3 = ((s8[16777216]{0:T(1024)(128)(4,1)}), s8[4194304]{0:T(1024)(128)(4,1)S(1)}, s32[]{:S(2)}) async-start(s8[16777216]{0:T(1024)(128)(4,1)} %bitcast.13), calls=%async_computation.5 | async-start | bytes 8388608
  52.1 7.2 %copy-start.4 = (bf16[4,32,4096]{2,1,0:T(8,128)(2,1)S(1)}, bf16[4,32,4096]{2,1,0:T(8,128)(2,1)}, u32[]{:S(2)}) copy-start(bf16[4,32,4096]{2,1,0:T(8,128)(2,1)} %param.26) | copy-start | bytes 3145732
  52.1 7.1 %collective-permute-start.9 = (bf16[16,128]{1,0:T(8,128)(2,1)S(1)}, bf16[16,128]{1,0:T(8,128)(2,1)S(1)}, u32[]{:S(2)}, u32[]{:S(2)}) collective-permute-start(bf16[16,128]{1,0:T(8,128)(2,1)S(1)} %get-tuple-element.22), channel_id=1, source_target_pairs={{0,3},{1,7},{2,11},{3,15},{4,2},{5,6},{6,10},{7,14},{8,1},{9,5},{1... | collective-permute-start | bytes 12296 | tf_op jit(solution)/shard_map/ppermute | solution.py:396
  52.1 7.1 %collective-permute-start.8 = (bf16[16,128]{1,0:T(8,128)(2,1)S(1)}, bf16[16,128]{1,0:T(8,128)(2,1)S(1)}, u32[]{:S(2)}, u32[]{:S(2)}) collective-permute-start(bf16[16,128]{1,0:T(8,128)(2,1)S(1)} %get-tuple-element.22), channel_id=1, source_target_pairs={{0,2},{1,6},{2,10},{3,14},{4,3},{5,7},{6,11},{7,15},{8,0},{9,4},{1... | collective-permute-start | bytes 12296 | tf_op jit(solution)/shard_map/ppermute | solution.py:396
  52.7 6.5 %collective-permute-start.7 = (bf16[16,128]{1,0:T(8,128)(2,1)S(1)}, bf16[16,128]{1,0:T(8,128)(2,1)S(1)}, u32[]{:S(2)}, u32[]{:S(2)}) collective-permute-start(bf16[16,128]{1,0:T(8,128)(2,1)S(1)} %get-tuple-element.22), channel_id=1, source_target_pairs={{0,1},{1,5},{2,9},{3,13},{4,0},{5,4},{6,8},{7,12},{8,3},{9,7},{10,... | collective-permute-start | bytes 12296 | tf_op jit(solution)/shard_map/ppermute | solution.py:396
  52.9 6.4 %collective-permute-start.6 = (bf16[16,128]{1,0:T(8,128)(2,1)S(1)}, bf16[16,128]{1,0:T(8,128)(2,1)S(1)}, u32[]{:S(2)}, u32[]{:S(2)}) collective-permute-start(bf16[16,128]{1,0:T(8,128)(2,1)S(1)} %get-tuple-element.22), channel_id=1, source_target_pairs={{0,0},{1,4},{2,8},{3,12},{4,1},{5,5},{6,9},{7,13},{8,2},{9,6},{10,... | collective-permute-start | bytes 12296 | tf_op jit(solution)/shard_map/ppermute | solution.py:396
  59.9 9.5 %collective-permute-start.10 = (bf16[3,4,4096]{2,1,0:T(4,128)(2,1)S(1)}, bf16[3,4,4096]{2,1,0:T(4,128)(2,1)S(1)}, u32[]{:S(2)}, u32[]{:S(2)}) collective-permute-start(bf16[3,4,4096]{2,1,0:T(4,128)(2,1)S(1)} %get-tuple-element.24), channel_id=1, source_target_pairs={{0,12},{4,8},{8,4},{12,0},{1,13},{5,9},{9,5},{13,1},{2,14},{6,10},... | collective-permute-start | bytes 294920 | tf_op jit(solution)/shard_map/ppermute | solution.py:376
  65.7 7.9 %collective-permute-start.11 = (bf16[3,4,4096]{2,1,0:T(4,128)(2,1)S(1)}, bf16[3,4,4096]{2,1,0:T(4,128)(2,1)S(1)}, u32[]{:S(2)}, u32[]{:S(2)}) collective-permute-start(bf16[3,4,4096]{2,1,0:T(4,128)(2,1)S(1)} %get-tuple-element.25), channel_id=1, source_target_pairs={{0,8},{4,12},{8,0},{12,4},{1,9},{5,13},{9,1},{13,5},{2,10},{6,14},... | collective-permute-start | bytes 294920 | tf_op jit(solution)/shard_map/ppermute | solution.py:376
  66.0 7.6 %collective-permute-start.12 = (bf16[3,4,4096]{2,1,0:T(4,128)(2,1)S(1)}, bf16[3,4,4096]{2,1,0:T(4,128)(2,1)S(1)}, u32[]{:S(2)}, u32[]{:S(2)}) collective-permute-start(bf16[3,4,4096]{2,1,0:T(4,128)(2,1)S(1)} %get-tuple-element.26), channel_id=1, source_target_pairs={{0,4},{4,0},{8,12},{12,8},{1,5},{5,1},{9,13},{13,9},{2,6},{6,2},{1... | collective-permute-start | bytes 294920 | tf_op jit(solution)/shard_map/ppermute | solution.py:376

commit v22 on v21

--- a/solution.py
+++ b/solution.py
@@ -274,6 +274,13 @@
             out_ref[block * groups + target] = mixed
 
 
+def sum_kernel(*refs):
+    total = refs[0][...].astype(jnp.float32)
+    for ref in refs[1:-1]:
+        total = total + ref[...].astype(jnp.float32)
+    refs[-1][...] = total.astype(jnp.bfloat16)
+
+
 def add_kernel(left_ref, right_ref, out_ref):
     total = left_ref[...].astype(jnp.float32) + right_ref[...].astype(jnp.float32)
     out_ref[...] = total.astype(jnp.bfloat16)
@@ -464,10 +471,10 @@
         2 * count * owned * width * out_cols,
         8 * count * out_cols + 2 * owned * width * out_cols,
     )(out_total, slots, grow_out.reshape(owned * width, -1), *out_ranks)
-    result = leaving[0].astype(jnp.float32)
-    for shift in reversed(range(1, blocks)):
-        result = result + over_tensor(leaving[shift], shift).astype(jnp.float32)
-    return jnp.transpose(result.astype(jnp.bfloat16), (1, 0, 2))
+    order = sorted(range(1, blocks), key=lambda shift: shift < blocks // 2)
+    parts = [leaving[0]] + [over_tensor(leaving[shift], shift) for shift in order]
+    result = call(sum_kernel, shape(parts[0].shape), [VMEM] * blocks)(*parts)
+    return jnp.transpose(result, (1, 0, 2))
 
 
 def rotate(vectors, positions):

time: 74.6 us -> 73.9 us (level)
    transpose x1 -> x0, other arithmetic: 0.75 us -> none  [by_kernels(): return jnp.transpose(result.astype(jnp.bfloat16), (1, 0, 2))]
  transfers between devices with their start and end apart: 13 -> 13, of which waited for: 5 -> 5; matrix products, arithmetic and copies ran while one was open for 0% -> 0% of each run, Pallas kernels for 9% -> 10%
where the time goes in v22:
time: 73.9 us; the launch traced here: 73.7 us
  blocking collectives  29.1 us (39%)
  starting transfers between devices  14.9 us (20%)
  waiting for transfers between devices  12.8 us (17%)
  Pallas kernels  12 us (16%)
  local copies, waits for them, and re-layouts  3.89 us (5%)
  between operations  0.91 us (1%)
    all_to_all x2, blocking collectives, exchange(): return lax.all_to_all(value, EVERY, split_axis=0, concat_axis=0, tiled=True)  29.1 us
    ppermute x6, starting transfers between devices, over_tensor(): return lax.ppermute(value, 'tensor', route)  12.2 us
    ppermute x6, waiting for transfers between devices, over_tensor(): return lax.ppermute(value, 'tensor', route)  11.6 us
    pallas_call x2, Pallas kernels, product(): call(product_kernel, shape((rows.shape[0], width), jnp.float32), [VMEM] *...  6.31 us
    unnamed x36, local copies, waits for them, and re-layouts  3.89 us
    ppermute x4, starting transfers between devices, to_out_growers(): return lax.ppermute(value, EVERY, route)  1.56 us
  transfers between devices with their start and end apart: 13, of which 5 were waited for; matrix products, arithmetic and copies ran while one was open for 0% of the time, Pallas kernels for 10%

profile of v22, /device:TPU:0, one launch (start us, length us, event | category | flops | bytes accessed | tf_op | source)
XLA Modules:
  0.0 73.7 jit_solution(11671019431667713423)
XLA Ops:
  0.0 5.0 %collective-permute-start.2 = (bf16[3,4,4096]{2,1,0:T(4,128)(2,1)}, bf16[3,4,4096]{2,1,0:T(4,128)(2,1)S(1)}, u32[]{:S(2)}, u32[]{:S(2)}) collective-permute-start(bf16[3,4,4096]{2,1,0:T(4,128)(2,1)} %bitcast.18), channel_id=1, source_target_pairs={{0,12},{4,8},{8,4},{12,0},{1,13},{5,9},{9,5},{13,1},{2,14},{6,10},... | collective-permute-start | bytes 294920 | tf_op jit(solution)/shard_map/ppermute | solution.py:383
  5.0 0.0 collective-permute-start.1
  5.1 0.6 collective-permute-start
  6.3 0.6 copy-done.12
  6.9 0.7 copy-done.13
  7.6 0.7 shard_map.154
  8.3 0.0 copy-start.8
  8.4 0.0 copy-start.10
  8.4 0.0 copy-start.11
  8.4 0.6 collective-permute-done.2.refs_3_
  9.0 4.6 %collective-permute-done.1.refs_2_ = bf16[3,4,4096]{2,1,0:T(4,128)(2,1)S(1)} collective-permute-done((bf16[3,4,4096]{2,1,0:T(4,128)(2,1)}, bf16[3,4,4096]{2,1,0:T(4,128)(2,1)S(1)}, u32[]{:S(2)}, u32[]{:S(2)}) %collective-permute-start.1) | collective-permute-done | bytes 98336 | tf_op jit(solution)/shard_map/ppermute | solution.py:383
  13.5 0.0 collective-permute-done.refs_1_
  13.5 1.4 %shard_map.155 = (bf16[48,4096]{1,0:T(8,128)(2,1)S(1)}, bf16[32,128]{1,0:T(8,128)(2,1)S(1)}) custom-call(bf16[3,4,4096]{2,1,0:T(4,128)(2,1)S(1)} %bitcast.21, bf16[3,4,4096]{2,1,0:T(4,128)(2,1)S(1)} %collective-permute-done.refs_1_, bf16[3,4,4096]{2,1,0:T(4,128)(2,1)S(1)} %collective-permute-done.1.refs_2_, ...), custom_call_target="tpu_custom_call" | custom-call | flops 150994944 | bytes 3932160 | tf_op jit(solution)/shard_map/pallas_call | solution.py:421
  14.9 0.0 collective-permute-start.3
  14.9 1.2 %collective-permute-done.3.right_ref = bf16[32,128]{1,0:T(8,128)(2,1)S(1)} collective-permute-done((bf16[32,128]{1,0:T(8,128)(2,1)S(1)}, bf16[32,128]{1,0:T(8,128)(2,1)S(1)}, u32[]{:S(2)}, u32[]{:S(2)}) %collective-permute-start.3) | collective-permute-done | bytes 8224 | tf_op jit(solution)/shard_map/ppermute | solution.py:386
  16.1 0.5 collective-permute-start.5
  16.6 0.6 collective-permute-start.4
  17.3 0.0 copy-done
  17.3 3.3 %shard_map.156.total_ref = f32[48,2304]{1,0:T(8,128)S(1)} custom-call(bf16[48,4096]{1,0:T(8,128)(2,1)S(1)} %get-tuple-element.17.rows_ref, bf16[4096,2048]{1,0:T(8,128)(2,1)S(1)} %copy-done, bf16[4096,128]{1,0:T(8,128)(2,1)S(1)} %copy-done.2, bf16[4096,128]{1,0:T(8,128)(2,1)S(1)} %copy-done.3), custom_call_target="tpu_custom_call" | custom-call | tf_op jit(solution)/shard_map/pallas_call | solution.py:152
  20.6 0.0 collective-permute-done.5.refs_1_
  20.7 0.0 collective-permute-done.4.refs_0_
  20.7 0.0 copy-start.6
  20.7 0.0 copy-start.7
  20.7 0.0 copy-start.5
  20.7 0.9 %shard_map.158 = bf16[16,56,128]{2,1,0:T(8,128)(2,1)S(1)} custom-call(f32[48,2304]{1,0:T(8,128)S(1)} %shard_map.156.total_ref, s32[48,128]{1,0:T(8,128)S(1)} %get-tuple-element.16.refs_5_.slots_ref, bf16[32,128]{1,0:T(8,128)(2,1)S(1)} %collective-permute-done.4.refs_0_, bf16[32,128]{1,0:T(8,128)(2,1)S(1)} %collective-permute-done.5.refs_1_, ...), custom_call_target="tpu_custom_call" | custom-call | tf_op jit(solution)/shard_map/pallas_call | solution.py:435
  21.7 17.4 %all_to_all.10.arrived_ref = bf16[16,56,128]{2,1,0:T(8,128)(2,1)S(1)} all-to-all(bf16[16,56,128]{2,1,0:T(8,128)(2,1)S(1)} %shard_map.158), channel_id=1, replica_groups=mesh['parts'=2,'tensor'=4,'dp'=2,'pipe'=2] {'tensor','dp','pipe'}, dimensions={0} | all-to-all | bytes 458752 | tf_op jit(solution)/shard_map/all_to_all | solution.py:409
  39.0 0.8 %shard_map.159 = bf16[16,48,128]{2,1,0:T(8,128)(2,1)S(1)} custom-call(bf16[16,56,128]{2,1,0:T(8,128)(2,1)S(1)} %all_to_all.10.arrived_ref, bf16[1,4,512,128]{3,2,1,0:T(8,128)(2,1)S(1)} %copy-done.6, bf16[1,4,512,128]{3,2,1,0:T(8,128)(2,1)S(1)} %copy-done.7, s32[1]{0:T(128)S(6)} %copy.17.length_ref, f32[56,128]{1,0:T(8,128)S(1)} %get-tuple-element.19.cosine_ref, ...), custom_call_target="tpu_custom_call" | custom-call | tf_op jit(solution)/shard_map/pallas_call | solution.py:448
  39.8 11.8 %all_to_all.11.got_ref = bf16[16,48,128]{2,1,0:T(8,128)(2,1)S(1)} all-to-all(bf16[16,48,128]{2,1,0:T(8,128)(2,1)S(1)} %shard_map.159), channel_id=1, replica_groups=mesh['parts'=2,'tensor'=4,'dp'=2,'pipe'=2] {'tensor','dp','pipe'}, dimensions={0} | all-to-all | bytes 393216 | tf_op jit(solution)/shard_map/all_to_all | solution.py:409
  51.6 0.6 shard_map.160
  52.1 0.0 collective-permute-start.9
  52.1 0.6 collective-permute-start.8
  52.7 0.2 collective-permute-start.7
  52.9 0.8 %collective-permute-start.6 = (bf16[16,128]{1,0:T(8,128)(2,1)S(1)}, bf16[16,128]{1,0:T(8,128)(2,1)S(1)}, u32[]{:S(2)}, u32[]{:S(2)}) collective-permute-start(bf16[16,128]{1,0:T(8,128)(2,1)S(1)} %get-tuple-element.22), channel_id=1, source_target_pairs={{0,0},{1,4},{2,8},{3,12},{4,1},{5,5},{6,9},{7,13},{8,2},{9,6},{10,... | collective-permute-start | bytes 12296 | tf_op jit(solution)/shard_map/ppermute | solution.py:403
  53.7 0.0 slice-done.1
  53.8 1.3 %slice-done.2 = s8[4194304]{0:T(1024)(128)(4,1)S(1)} async-done(((s8[16777216]{0:T(1024)(128)(4,1)}), s8[4194304]{0:T(1024)(128)(4,1)S(1)}, s32[]{:S(2)}) %slice-start.2) | async-done | bytes 4194328
  55.0 1.2 %slice-done.3 = s8[4194304]{0:T(1024)(128)(4,1)S(1)} async-done(((s8[16777216]{0:T(1024)(128)(4,1)}), s8[4194304]{0:T(1024)(128)(4,1)S(1)}, s32[]{:S(2)}) %slice-start.3) | async-done | bytes 4194328
  56.2 3.0 %shard_map.161.total_ref = f32[48,4096]{1,0:T(8,128)S(1)} custom-call(bf16[48,2048]{1,0:T(8,128)(2,1)S(1)} %get-tuple-element.21.rows_ref, bf16[2048,4096]{1,0:T(8,128)(2,1)S(1)} %bitcast.13), custom_call_target="tpu_custom_call" | custom-call | tf_op jit(solution)/shard_map/pallas_call | solution.py:152
  59.2 0.0 collective-permute-done.9.refs_3_
  59.3 0.0 collective-permute-done.8.refs_2_
  59.3 0.0 collective-permute-done.7.refs_1_
  59.3 0.0 collective-permute-done.6.refs_0_
  59.3 0.6 shard_map.162
  59.9 5.9 %collective-permute-start.10 = (bf16[3,4,4096]{2,1,0:T(4,128)(2,1)S(1)}, bf16[3,4,4096]{2,1,0:T(4,128)(2,1)S(1)}, u32[]{:S(2)}, u32[]{:S(2)}) collective-permute-start(bf16[3,4,4096]{2,1,0:T(4,128)(2,1)S(1)} %get-tuple-element.24), channel_id=1, source_target_pairs={{0,8},{4,12},{8,0},{12,4},{1,9},{5,13},{9,1},{13,5},{2,10},{6,14},... | collective-permute-start | bytes 294920 | tf_op jit(solution)/shard_map/ppermute | solution.py:383
  65.9 0.0 collective-permute-start.11
  65.9 0.6 collective-permute-start.12
  66.5 6.0 %collective-permute-done.10.refs_1_ = bf16[3,4,4096]{2,1,0:T(4,128)(2,1)S(1)} collective-permute-done((bf16[3,4,4096]{2,1,0:T(4,128)(2,1)S(1)}, bf16[3,4,4096]{2,1,0:T(4,128)(2,1)S(1)}, u32[]{:S(2)}, u32[]{:S(2)}) %collective-permute-start.10) | collective-permute-done | bytes 98336 | tf_op jit(solution)/shard_map/ppermute | solution.py:383
  72.5 0.5 collective-permute-done.12.refs_3_
  73.0 0.7 shard_map.163
  (27 shorter events, 0.1 us)
Async XLA Ops:
  0.0 9.0 %collective-permute-start.2 = (bf16[3,4,4096]{2,1,0:T(4,128)(2,1)}, bf16[3,4,4096]{2,1,0:T(4,128)(2,1)S(1)}, u32[]{:S(2)}, u32[]{:S(2)}) collective-permute-start(bf16[3,4,4096]{2,1,0:T(4,128)(2,1)} %bitcast.18), channel_id=1, source_target_pairs={{0,12},{4,8},{8,4},{12,0},{1,13},{5,9},{9,5},{13,1},{2,14},{6,10},... | collective-permute-start | bytes 294920 | tf_op jit(solution)/shard_map/ppermute | solution.py:383
  5.0 8.5 %collective-permute-start.1 = (bf16[3,4,4096]{2,1,0:T(4,128)(2,1)}, bf16[3,4,4096]{2,1,0:T(4,128)(2,1)S(1)}, u32[]{:S(2)}, u32[]{:S(2)}) collective-permute-start(bf16[3,4,4096]{2,1,0:T(4,128)(2,1)} %bitcast.19), channel_id=1, source_target_pairs={{0,8},{4,12},{8,0},{12,4},{1,9},{5,13},{9,1},{13,5},{2,10},{6,14},... | collective-permute-start | bytes 294920 | tf_op jit(solution)/shard_map/ppermute | solution.py:383
  5.1 8.5 %collective-permute-start = (bf16[3,4,4096]{2,1,0:T(4,128)(2,1)}, bf16[3,4,4096]{2,1,0:T(4,128)(2,1)S(1)}, u32[]{:S(2)}, u32[]{:S(2)}) collective-permute-start(bf16[3,4,4096]{2,1,0:T(4,128)(2,1)} %bitcast.20), channel_id=1, source_target_pairs={{0,4},{4,0},{8,12},{12,8},{1,5},{5,1},{9,13},{13,9},{2,6},{6,2},{1... | collective-permute-start | bytes 294920 | tf_op jit(solution)/shard_map/ppermute | solution.py:383
  6.3 0.7 copy-start.12
  6.9 0.7 copy-start.13
  7.6 6.0 %copy-start.1 = (bf16[4,4096,96]{1,2,0:T(8,128)(2,1)S(1)}, bf16[4,4096,96]{1,2,0:T(8,128)(2,1)}, u32[]{:S(2)}) copy-start(bf16[4,4096,96]{1,2,0:T(8,128)(2,1)} %param.21) | copy-start | bytes 9437188
  7.6 6.0 %copy-start.9 = (bf16[4,3,4096]{2,0,1:T(4,128)(2,1)S(1)}, bf16[4,3,4096]{2,0,1:T(4,128)(2,1)}, u32[]{:S(2)}) copy-start(bf16[4,3,4096]{2,0,1:T(4,128)(2,1)} %param.16) | copy-start | bytes 294916
  7.6 9.7 %copy-start = (bf16[4096,2048]{1,0:T(8,128)(2,1)S(1)}, bf16[4096,2048]{1,0:T(8,128)(2,1)}, u32[]{:S(2)}) copy-start(bf16[4096,2048]{1,0:T(8,128)(2,1)} %refs_3_.1) | copy-start | bytes 50331652
  7.6 9.7 %copy-start.2 = (bf16[4096,128]{1,0:T(8,128)(2,1)S(1)}, bf16[4096,128]{1,0:T(8,128)(2,1)}, u32[]{:S(2)}) copy-start(bf16[4096,128]{1,0:T(8,128)(2,1)} %refs_1_.4) | copy-start | bytes 3145732
  7.6 9.7 %copy-start.3 = (bf16[4096,128]{1,0:T(8,128)(2,1)S(1)}, bf16[4096,128]{1,0:T(8,128)(2,1)}, u32[]{:S(2)}) copy-start(bf16[4096,128]{1,0:T(8,128)(2,1)} %refs_2_.4) | copy-start | bytes 3145732
  8.3 12.3 %copy-start.8 = (bf16[4,32,2048]{2,1,0:T(8,128)(2,1)S(1)}, bf16[4,32,2048]{2,1,0:T(8,128)(2,1)}, u32[]{:S(2)}) copy-start(bf16[4,32,2048]{2,1,0:T(8,128)(2,1)} %param.22) | copy-start | bytes 1572868
  8.4 12.3 %copy-start.10 = (bf16[4,32,128]{2,1,0:T(8,128)(2,1)S(1)}, bf16[4,32,128]{2,1,0:T(8,128)(2,1)}, u32[]{:S(2)}) copy-start(bf16[4,32,128]{2,1,0:T(8,128)(2,1)} %param.23) | copy-start | bytes 98308
  8.4 12.3 %copy-start.11 = (bf16[4,32,128]{2,1,0:T(8,128)(2,1)S(1)}, bf16[4,32,128]{2,1,0:T(8,128)(2,1)}, u32[]{:S(2)}) copy-start(bf16[4,32,128]{2,1,0:T(8,128)(2,1)} %param.24) | copy-start | bytes 98308
  14.9 1.2 %collective-permute-start.3 = (bf16[32,128]{1,0:T(8,128)(2,1)S(1)}, bf16[32,128]{1,0:T(8,128)(2,1)S(1)}, u32[]{:S(2)}, u32[]{:S(2)}) collective-permute-start(bf16[32,128]{1,0:T(8,128)(2,1)S(1)} %get-tuple-element.18.left_ref), channel_id=1, source_target_pairs={{0,1},{1,0},{2,3},{3,2},{4,5},{5,4},{6,7},{7,6},{8,9},{9,8},{10,11... | collective-permute-start | bytes 24584 | tf_op jit(solution)/shard_map/ppermute | solution.py:386
  16.1 4.5 %collective-permute-start.5 = (bf16[32,128]{1,0:T(8,128)(2,1)S(1)}, bf16[32,128]{1,0:T(8,128)(2,1)S(1)}, u32[]{:S(2)}, u32[]{:S(2)}) collective-permute-start(bf16[32,128]{1,0:T(8,128)(2,1)S(1)} %shard_map.157), channel_id=1, source_target_pairs={{0,4},{1,12},{2,0},{3,8},{4,5},{5,13},{6,1},{7,9},{8,6},{9,14},{10... | collective-permute-start | bytes 24584 | tf_op jit(solution)/shard_map/ppermute | solution.py:395
  16.6 4.0 %collective-permute-start.4 = (bf16[32,128]{1,0:T(8,128)(2,1)S(1)}, bf16[32,128]{1,0:T(8,128)(2,1)S(1)}, u32[]{:S(2)}, u32[]{:S(2)}) collective-permute-start(bf16[32,128]{1,0:T(8,128)(2,1)S(1)} %shard_map.157), channel_id=1, source_target_pairs={{0,0},{1,8},{2,4},{3,12},{4,1},{5,9},{6,5},{7,13},{8,2},{9,10},{10... | collective-permute-start | bytes 24584 | tf_op jit(solution)/shard_map/ppermute | solution.py:395
  20.7 18.3 %copy-start.6 = (bf16[1,4,512,128]{3,2,1,0:T(8,128)(2,1)S(1)}, bf16[1,4,512,128]{3,2,1,0:T(8,128)(2,1)}, u32[]{:S(2)}) copy-start(bf16[1,4,512,128]{3,2,1,0:T(8,128)(2,1)} %keys_ref.1) | copy-start | bytes 1572868
  20.7 18.3 %copy-start.7 = (bf16[1,4,512,128]{3,2,1,0:T(8,128)(2,1)S(1)}, bf16[1,4,512,128]{3,2,1,0:T(8,128)(2,1)}, u32[]{:S(2)}) copy-start(bf16[1,4,512,128]{3,2,1,0:T(8,128)(2,1)} %values_ref.1) | copy-start | bytes 1572868
  20.7 30.9 %copy-start.5 = (bf16[4,2048,32]{1,2,0:T(8,128)(2,1)S(1)}, bf16[4,2048,32]{1,2,0:T(8,128)(2,1)}, u32[]{:S(2)}) copy-start(bf16[4,2048,32]{1,2,0:T(8,128)(2,1)} %param.25) | copy-start | bytes 1572868
  39.0 14.7 %slice-start = ((s8[16777216]{0:T(1024)(128)(4,1)}), s8[4194304]{0:T(1024)(128)(4,1)S(1)}, s32[]{:S(2)}) async-start(s8[16777216]{0:T(1024)(128)(4,1)} %bitcast.12), calls=%async_computation.2 | async-start | bytes 8388608
  51.6 2.2 %slice-start.1 = ((s8[16777216]{0:T(1024)(128)(4,1)}), s8[4194304]{0:T(1024)(128)(4,1)S(1)}, s32[]{:S(2)}) async-start(s8[16777216]{0:T(1024)(128)(4,1)} %bitcast.12), calls=%async_computation.3 | async-start | bytes 8388608
  51.6 3.5 %slice-start.2 = ((s8[16777216]{0:T(1024)(128)(4,1)}), s8[4194304]{0:T(1024)(128)(4,1)S(1)}, s32[]{:S(2)}) async-start(s8[16777216]{0:T(1024)(128)(4,1)} %bitcast.12), calls=%async_computation.4 | async-start | bytes 8388608
  51.6 4.7 %slice-start.3 = ((s8[16777216]{0:T(1024)(128)(4,1)}), s8[4194304]{0:T(1024)(128)(4,1)S(1)}, s32[]{:S(2)}) async-start(s8[16777216]{0:T(1024)(128)(4,1)} %bitcast.12), calls=%async_computation.5 | async-start | bytes 8388608
  52.1 7.2 %copy-start.4 = (bf16[4,32,4096]{2,1,0:T(8,128)(2,1)S(1)}, bf16[4,32,4096]{2,1,0:T(8,128)(2,1)}, u32[]{:S(2)}) copy-start(bf16[4,32,4096]{2,1,0:T(8,128)(2,1)} %param.26) | copy-start | bytes 3145732
  52.1 7.1 %collective-permute-start.9 = (bf16[16,128]{1,0:T(8,128)(2,1)S(1)}, bf16[16,128]{1,0:T(8,128)(2,1)S(1)}, u32[]{:S(2)}, u32[]{:S(2)}) collective-permute-start(bf16[16,128]{1,0:T(8,128)(2,1)S(1)} %get-tuple-element.22), channel_id=1, source_target_pairs={{0,3},{1,7},{2,11},{3,15},{4,2},{5,6},{6,10},{7,14},{8,1},{9,5},{1... | collective-permute-start | bytes 12296 | tf_op jit(solution)/shard_map/ppermute | solution.py:403
  52.1 7.1 %collective-permute-start.8 = (bf16[16,128]{1,0:T(8,128)(2,1)S(1)}, bf16[16,128]{1,0:T(8,128)(2,1)S(1)}, u32[]{:S(2)}, u32[]{:S(2)}) collective-permute-start(bf16[16,128]{1,0:T(8,128)(2,1)S(1)} %get-tuple-element.22), channel_id=1, source_target_pairs={{0,2},{1,6},{2,10},{3,14},{4,3},{5,7},{6,11},{7,15},{8,0},{9,4},{1... | collective-permute-start | bytes 12296 | tf_op jit(solution)/shard_map/ppermute | solution.py:403
  52.7 6.5 %collective-permute-start.7 = (bf16[16,128]{1,0:T(8,128)(2,1)S(1)}, bf16[16,128]{1,0:T(8,128)(2,1)S(1)}, u32[]{:S(2)}, u32[]{:S(2)}) collective-permute-start(bf16[16,128]{1,0:T(8,128)(2,1)S(1)} %get-tuple-element.22), channel_id=1, source_target_pairs={{0,1},{1,5},{2,9},{3,13},{4,0},{5,4},{6,8},{7,12},{8,3},{9,7},{10,... | collective-permute-start | bytes 12296 | tf_op jit(solution)/shard_map/ppermute | solution.py:403
  52.9 6.4 %collective-permute-start.6 = (bf16[16,128]{1,0:T(8,128)(2,1)S(1)}, bf16[16,128]{1,0:T(8,128)(2,1)S(1)}, u32[]{:S(2)}, u32[]{:S(2)}) collective-permute-start(bf16[16,128]{1,0:T(8,128)(2,1)S(1)} %get-tuple-element.22), channel_id=1, source_target_pairs={{0,0},{1,4},{2,8},{3,12},{4,1},{5,5},{6,9},{7,13},{8,2},{9,6},{10,... | collective-permute-start | bytes 12296 | tf_op jit(solution)/shard_map/ppermute | solution.py:403
  59.9 12.6 %collective-permute-start.10 = (bf16[3,4,4096]{2,1,0:T(4,128)(2,1)S(1)}, bf16[3,4,4096]{2,1,0:T(4,128)(2,1)S(1)}, u32[]{:S(2)}, u32[]{:S(2)}) collective-permute-start(bf16[3,4,4096]{2,1,0:T(4,128)(2,1)S(1)} %get-tuple-element.24), channel_id=1, source_target_pairs={{0,8},{4,12},{8,0},{12,4},{1,9},{5,13},{9,1},{13,5},{2,10},{6,14},... | collective-permute-start | bytes 294920 | tf_op jit(solution)/shard_map/ppermute | solution.py:383
  65.9 6.6 %collective-permute-start.11 = (bf16[3,4,4096]{2,1,0:T(4,128)(2,1)S(1)}, bf16[3,4,4096]{2,1,0:T(4,128)(2,1)S(1)}, u32[]{:S(2)}, u32[]{:S(2)}) collective-permute-start(bf16[3,4,4096]{2,1,0:T(4,128)(2,1)S(1)} %get-tuple-element.25), channel_id=1, source_target_pairs={{0,12},{4,8},{8,4},{12,0},{1,13},{5,9},{9,5},{13,1},{2,14},{6,10},... | collective-permute-start | bytes 294920 | tf_op jit(solution)/shard_map/ppermute | solution.py:383
  65.9 7.1 %collective-permute-start.12 = (bf16[3,4,4096]{2,1,0:T(4,128)(2,1)S(1)}, bf16[3,4,4096]{2,1,0:T(4,128)(2,1)S(1)}, u32[]{:S(2)}, u32[]{:S(2)}) collective-permute-start(bf16[3,4,4096]{2,1,0:T(4,128)(2,1)S(1)} %get-tuple-element.26), channel_id=1, source_target_pairs={{0,4},{4,0},{8,12},{12,8},{1,5},{5,1},{9,13},{13,9},{2,6},{6,2},{1... | collective-permute-start | bytes 294920 | tf_op jit(solution)/shard_map/ppermute | solution.py:383
